TPU v7x, 32 devices: a whole 2x2x4 slice. The times are simulated.
32 devices in a mesh: grp: 2 (over y), ep: 4 (over z), et: 4 (over x, core).
Axes of the slice: x: 2, y: 2, z: 4, core: 2. Of those that a mesh axis runs over, the one named last changes fastest.
Arguments:
- tokens: bfloat16 [256, 4096], P(('grp', 'ep')), parts along dimension 0, may hold values from -6 to 6
- modulation: float32 [2, 2, 4096], replicated, may hold values from -3 to 3
- router: bfloat16 [4096, 4], replicated, may hold values from -0.25 to 0.25
- gate_weight: bfloat16 [4, 4096, 1536], P('ep', None, 'et'), may hold values from -0.09375 to 0.09375
- up_weight: bfloat16 [4, 4096, 1536], P('ep', None, 'et'), may hold values from -0.09375 to 0.09375
- down_weight: bfloat16 [4, 1536, 4096], P('ep', 'et'), may hold values from -0.15625 to 0.15625
- expert_ids: int32 [2, 256, 2], P(None, ('grp', 'ep')), parts along dimension 1, may hold values from 0 to 3, all different within a row; in each aligned block of 32 rows (0 to 31, 32 to 63, ..., all dimensions but the last counted through in order) at most 24 rows name the same one
Outputs:
- latents: bfloat16 [256, 4096], P(('grp', 'ep'), 'et'), parts along dimension 0
- velocity: bfloat16 [256, 4096], P(('grp', 'ep'), 'et'), parts along dimension 0
There are 2 independent parts, one for each index of `grp`. A program takes and returns all parts, laid end to end along the dimension named above; an argument that names none is the same for every part. Nothing has to cross between parts.
Inputs may be any that keep to these rules, and one draw needn't show every extreme that they name: `expert_ids`: each row names 2 different experts. In each section, among the 32 rows of one ep index, no expert is named by more than 24 rows, and in each section some expert is named by exactly 24 rows of some ep index.
All inputs are finite; a program needn't handle non-finite values.
Results may differ from a plain program's by a relative error of at most 0.017.
Values may be sent and summed in bfloat16 or wider, within the bound.
No kernel may reach another device: no remote copies, remote signals or barrier semaphores. Data moves between devices by JAX's collectives and lax.ppermute only.
A program may use at most 64 MiB of HBM per device.

v0:
```python
import jax
import jax.numpy as jnp
from jax import lax
from jax.sharding import PartitionSpec as P


def normalize(x, mod):
    xf = x.astype(jnp.float32)
    scaled = xf * lax.rsqrt(jnp.mean(xf * xf, axis=-1, keepdims=True) + 1e-06)
    return (scaled * (1.0 + mod[0]) + mod[1]).astype(jnp.bfloat16)


def one_section(x_full, x_cols, mod, ids, router, gate_weight, up_weight, down_weight):
    tok_rows = x_full.shape[0]
    width = x_full.shape[1]
    experts = router.shape[1]
    picks = ids.shape[1]
    n_peers = lax.axis_size("ep")
    quarter = width // lax.axis_size("et")
    slot_count = 3 * tok_rows * picks // (2 * experts)
    normed = normalize(x_full, mod)
    logits = jnp.dot(normed, router, preferred_element_type=jnp.float32)
    chosen = jax.nn.sigmoid(jnp.take_along_axis(logits, ids, axis=1))
    weight = chosen / jnp.sum(chosen, axis=1, keepdims=True)
    flat_e = ids.reshape(-1)
    onehot = (flat_e[:, None] == jnp.arange(experts, dtype=jnp.int32)).astype(jnp.int32)
    counted = jnp.cumsum(onehot, axis=0)
    slot = jnp.sum(onehot * (counted - 1), axis=1)
    repeated = jnp.repeat(normed, picks, axis=0)
    outbox = jnp.zeros((experts, slot_count, width), jnp.bfloat16).at[flat_e, slot].set(repeated)
    w_gate = gate_weight[0]
    w_up = up_weight[0]
    arrived = lax.all_to_all(outbox, "ep", split_axis=0, concat_axis=0, tiled=True)
    in_rows = arrived.reshape(n_peers * slot_count, width)
    gate = jnp.dot(in_rows, w_gate, preferred_element_type=jnp.float32)
    upper = jnp.dot(in_rows, w_up, preferred_element_type=jnp.float32)
    hidden = (jax.nn.silu(gate) * upper).astype(jnp.bfloat16)
    partial_out = jnp.dot(hidden, down_weight[0], preferred_element_type=jnp.float32)
    summed = lax.psum_scatter(
        partial_out.astype(jnp.bfloat16), "et", scatter_dimension=1, tiled=True
    )
    returned = lax.all_to_all(
        summed.reshape(n_peers, slot_count, quarter), "ep", split_axis=0, concat_axis=0, tiled=True
    )
    picked = returned[flat_e, slot].astype(jnp.float32).reshape(tok_rows, picks, quarter)
    velocity = jnp.sum(picked * weight[:, :, None], axis=1)
    moved = (x_cols.astype(jnp.float32) - 0.5 * velocity).astype(jnp.bfloat16)
    return (moved, velocity)


def body(tokens, modulation, router, gate_weight, up_weight, down_weight, expert_ids):
    quarter = tokens.shape[1] // lax.axis_size("et")
    column_start = lax.axis_index("et") * quarter
    first_cols = lax.dynamic_slice_in_dim(tokens, column_start, quarter, 1)
    first, _ = one_section(
        tokens,
        first_cols,
        modulation[0],
        expert_ids[0],
        router,
        gate_weight,
        up_weight,
        down_weight,
    )
    first_full = lax.all_gather(first, "et", axis=1, tiled=True)
    second, velocity = one_section(
        first_full, first, modulation[1], expert_ids[1], router, gate_weight, up_weight, down_weight
    )
    return (second, velocity.astype(jnp.bfloat16))


def solution(mesh):
    in_specs = (
        P(("grp", "ep"), None),
        P(),
        P(),
        P("ep", None, "et"),
        P("ep", None, "et"),
        P("ep", "et", None),
        P(None, ("grp", "ep"), None),
    )
    out_specs = (P(("grp", "ep"), "et"), P(("grp", "ep"), "et"))
    return jax.shard_map(body, mesh=mesh, in_specs=in_specs, out_specs=out_specs, check_vma=False)
```

profile of v0, /device:TPU:0, one launch (start us, length us, event | category | flops | bytes accessed | tf_op | source)
XLA Modules:
  0.0 212.8 jit_solution(9703639059760364445)
XLA Ops:
  8.4 1.1 fusion.26
  12.6 1.3 broadcast_in_dim.7
  13.9 2.0 reshape.199
  16.9 17.2 %scatter_fusion = bf16[4,24,4096]{2,1,0:T(8,128)(2,1)} fusion(bf16[4,24,4096]{2,1,0:T(8,128)(2,1)} %broadcast.134.clone, s32[64]{0:T(128)S(1)} %get-tuple-element.7, bf16[64,4096]{1,0:T(8,128)(2,1)} %reshape.199), kind=kCustom, calls=%fused_computation.4 | custom fusion | bytes 1573376 | tf_op jit(solution)/shard_map/scatter | solution.py:30
  34.1 26.5 %all_to_all.20 = bf16[4,24,4096]{2,1,0:T(8,128)(2,1)S(1)} all-to-all(bf16[4,24,4096]{2,1,0:T(8,128)(2,1)} %scatter_fusion), channel_id=1, replica_groups=mesh['grp'=2,'ep'=4,'et'=4] {'ep'}, dimensions={0} | all-to-all | bytes 1572864 | tf_op jit(solution)/shard_map/all_to_all | solution.py:33
  61.5 2.5 %fusion.8 = f32[96,384]{1,0:T(8,128)S(1)} fusion(bf16[96,4096]{1,0:T(8,128)(2,1)S(1)} %bitcast.87, bf16[1,4096,384]{2,1,0:T(8,128)(2,1)} %param.12), kind=kOutput, calls=%fused_computation.16 | convolution fusion | flops 301989888 | bytes 4079616 | tf_op jit(solution)/shard_map/dot_general | solution.py:35
  64.0 4.5 %convolution_convert_fusion.1 = bf16[96,4096]{1,0:T(8,128)(2,1)} fusion(bf16[1,384,4096]{2,1,0:T(8,128)(2,1)S(1)} %copy-done, bf16[96,4096]{1,0:T(8,128)(2,1)} %bitcast.88, bf16[1,4096,384]{2,1,0:T(8,128)(2,1)} %param.13, f32[96,384]{1,0:T(8,128)S(1)} %fusion.8), kind=kOutput, calls=%fused_computation.7 | convolution fusion | flops 604594176 | bytes 8011776 | tf_op jit(solution)/shard_map/dot_general | solution.py:38
  69.3 1.1 fusion.60
  71.6 19.6 %reduce-scatter.3.cloned.1.call-done = bf16[96,1024]{1,0:T(8,128)(2,1)} async-done(((bf16[96,4096]{1,0:T(8,128)(2,1)}), bf16[96,1024]{1,0:T(8,128)(2,1)}) %reduce-scatter.3.cloned.1.call-update) | async-done | bytes 196624 | tf_op jit(solution)/shard_map/reduce_scatter | solution.py:39
  91.2 4.6 %all-to-all-start.1 = ((bf16[4,24,1024]{2,1,0:T(8,128)(2,1)}), bf16[4,24,1024]{2,1,0:T(8,128)(2,1)S(1)}, u32[]{:S(2)}, u32[]{:S(2)}) async-start(bf16[4,24,1024]{2,1,0:T(8,128)(2,1)} %bitcast.93), calls=%async_computation.2 | async-start | bytes 393216 | tf_op jit(solution)/shard_map/all_to_all | solution.py:42
  96.0 7.3 %all-to-all-done.1 = bf16[4,24,1024]{2,1,0:T(8,128)(2,1)S(1)} async-done(((bf16[4,24,1024]{2,1,0:T(8,128)(2,1)}), bf16[4,24,1024]{2,1,0:T(8,128)(2,1)S(1)}, u32[]{:S(2)}, u32[]{:S(2)}) %all-to-all-start.1) | async-done | bytes 196640 | tf_op jit(solution)/shard_map/all_to_all | solution.py:42
  105.3 1.3 multiply_reduce_fusion.1
  107.5 5.8 %all_gather.3 = bf16[32,4096]{1,0:T(8,128)(2,1)S(1)} all-gather(bf16[32,1024]{1,0:T(8,128)(2,1)S(1)} %subtract_convert_fusion.1), channel_id=1, replica_groups=mesh['grp'=2,'ep'=4,'et'=4] {'et'}, dimensions={1}, use_global_device_ids=true | all-gather | bytes 327680 | tf_op jit(solution)/shard_map/all_gather | solution.py:65
  114.4 1.3 broadcast_in_dim.8
  115.6 2.0 reshape.205
  118.6 17.4 %scatter_fusion.1 = bf16[4,24,4096]{2,1,0:T(8,128)(2,1)} fusion(bf16[4,24,4096]{2,1,0:T(8,128)(2,1)} %broadcast.134, s32[64]{0:T(128)S(1)} %get-tuple-element.9, bf16[64,4096]{1,0:T(8,128)(2,1)} %reshape.205), kind=kCustom, calls=%fused_computation.5 | custom fusion | bytes 1573376 | tf_op jit(solution)/shard_map/scatter | solution.py:30
  136.0 24.4 %all_to_all.21 = bf16[4,24,4096]{2,1,0:T(8,128)(2,1)S(1)} all-to-all(bf16[4,24,4096]{2,1,0:T(8,128)(2,1)} %scatter_fusion.1), channel_id=1, replica_groups=mesh['grp'=2,'ep'=4,'et'=4] {'ep'}, dimensions={0} | all-to-all | bytes 1572864 | tf_op jit(solution)/shard_map/all_to_all | solution.py:33
  161.3 2.5 %fusion.6 = f32[96,384]{1,0:T(8,128)S(1)} fusion(bf16[96,4096]{1,0:T(8,128)(2,1)S(1)} %bitcast.89, bf16[1,4096,384]{2,1,0:T(8,128)(2,1)} %param.12), kind=kOutput, calls=%fused_computation.14 | convolution fusion | flops 301989888 | bytes 4079616 | tf_op jit(solution)/shard_map/dot_general | solution.py:35
  163.8 4.5 %convolution_convert_fusion = bf16[96,4096]{1,0:T(8,128)(2,1)} fusion(bf16[1,384,4096]{2,1,0:T(8,128)(2,1)S(1)} %copy-done, bf16[96,4096]{1,0:T(8,128)(2,1)} %bitcast.90, bf16[1,4096,384]{2,1,0:T(8,128)(2,1)} %param.13, f32[96,384]{1,0:T(8,128)S(1)} %fusion.6), kind=kOutput, calls=%fused_computation.6 | convolution fusion | flops 604594176 | bytes 8011776 | tf_op jit(solution)/shard_map/dot_general | solution.py:38
  168.5 1.1 fusion.61
  170.7 19.2 %reduce-scatter.5.cloned.1.call-done = bf16[96,1024]{1,0:T(8,128)(2,1)} async-done(((bf16[96,4096]{1,0:T(8,128)(2,1)}), bf16[96,1024]{1,0:T(8,128)(2,1)}) %reduce-scatter.5.cloned.1.call-update) | async-done | bytes 196624 | tf_op jit(solution)/shard_map/reduce_scatter | solution.py:39
  190.0 4.6 %all-to-all-start.3 = ((bf16[4,24,1024]{2,1,0:T(8,128)(2,1)}), bf16[4,24,1024]{2,1,0:T(8,128)(2,1)S(1)}, u32[]{:S(2)}, u32[]{:S(2)}) async-start(bf16[4,24,1024]{2,1,0:T(8,128)(2,1)} %bitcast.94), calls=%async_computation.5 | async-start | bytes 393216 | tf_op jit(solution)/shard_map/all_to_all | solution.py:42
  194.7 7.4 %all-to-all-done.3 = bf16[4,24,1024]{2,1,0:T(8,128)(2,1)S(1)} async-done(((bf16[4,24,1024]{2,1,0:T(8,128)(2,1)}), bf16[4,24,1024]{2,1,0:T(8,128)(2,1)S(1)}, u32[]{:S(2)}, u32[]{:S(2)}) %all-to-all-start.3) | async-done | bytes 196640 | tf_op jit(solution)/shard_map/all_to_all | solution.py:42
  202.1 1.7 gather_fusion.1
  (66 shorter events, 17.5 us)
Async XLA Ops:
  7.2 56.8 %copy-start = (bf16[1,384,4096]{2,1,0:T(8,128)(2,1)S(1)}, bf16[1,384,4096]{2,1,0:T(8,128)(2,1)}, u32[]{:S(2)}) copy-start(bf16[1,384,4096]{2,1,0:T(8,128)(2,1)} %param.14) | copy-start | bytes 9437188
  7.2 84.0 %reduce-scatter.3.cloned.1.call-start = ((), (), s32[]{:S(2)}) async-start(), calls=%async_computation.6 | async-start | bytes 983040 | tf_op jit(solution)/shard_map/reduce_scatter | solution.py:39
  11.9 0.7 copy-start.3
  60.6 0.9 copy-start.1
  64.0 4.8 %copy-start.5 = (s32[2,32,2]{1,2,0:T(2,128)S(1)}, s32[2,32,2]{1,2,0:T(2,128)}, u32[]{:S(2)}) copy-start(s32[2,32,2]{1,2,0:T(2,128)} %param.15) | copy-start | bytes 1540
  64.0 5.2 %copy-start.6 = (bf16[4096,4]{0,1:T(4,128)(2,1)S(1)}, bf16[4096,4]{0,1:T(4,128)(2,1)}, u32[]{:S(2)}) copy-start(bf16[4096,4]{0,1:T(4,128)(2,1)} %param.11) | copy-start | bytes 98308
  91.2 12.1 %all-to-all-start.1 = ((bf16[4,24,1024]{2,1,0:T(8,128)(2,1)}), bf16[4,24,1024]{2,1,0:T(8,128)(2,1)S(1)}, u32[]{:S(2)}, u32[]{:S(2)}) async-start(bf16[4,24,1024]{2,1,0:T(8,128)(2,1)} %bitcast.93), calls=%async_computation.2 | async-start | bytes 393216 | tf_op jit(solution)/shard_map/all_to_all | solution.py:42
  95.8 94.2 %reduce-scatter.5.cloned.1.call-start = ((), (), s32[]{:S(2)}) async-start(), calls=%async_computation.7 | async-start | bytes 983040 | tf_op jit(solution)/shard_map/reduce_scatter | solution.py:39
  113.7 0.7 copy-start.4
  160.4 0.9 copy-start.2
  163.8 4.7 %copy-start.7 = (bf16[4096,4]{0,1:T(4,128)(2,1)S(1)}, bf16[4096,4]{0,1:T(4,128)(2,1)}, u32[]{:S(2)}) copy-start(bf16[4096,4]{0,1:T(4,128)(2,1)} %param.11) | copy-start | bytes 98308
  190.0 12.1 %all-to-all-start.3 = ((bf16[4,24,1024]{2,1,0:T(8,128)(2,1)}), bf16[4,24,1024]{2,1,0:T(8,128)(2,1)S(1)}, u32[]{:S(2)}, u32[]{:S(2)}) async-start(bf16[4,24,1024]{2,1,0:T(8,128)(2,1)} %bitcast.94), calls=%async_computation.5 | async-start | bytes 393216 | tf_op jit(solution)/shard_map/all_to_all | solution.py:42
Sparse Core Ops, SparseCore 0:
  68.7 22.4 reduce-scatter.2
  168.4 21.4 reduce-scatter.4
where the time goes:
time: 214 us; the launch traced here: 213 us
  blocking collectives  56.6 us (26%)
  local copies, waits for them, and re-layouts  55.3 us (26%)
  waiting for transfers between devices  53.6 us (25%)
  matrix products  16.3 us (8%)
  between operations  14.3 us (7%)
  starting transfers between devices  9.24 us (4%)
  other arithmetic  7.53 us (4%)
    all_to_all x2, blocking collectives, one_section(): lax.all_to_all(outbox, 'ep', split_axis=0, concat_axis=0, tiled=True)  50.8 us
    reduce_scatter x2, waiting for transfers between devices, one_section(): lax.psum_scatter(partial_out.astype(jnp.bfloat16), 'et', scatter_dimensio...  38.8 us
    scatter x2, local copies, waits for them, and re-layouts, one_section(): jnp.zeros((experts, slot_count, width), jnp.bfloat16).at[flat_e, slot]  34.7 us
    all_to_all x2, waiting for transfers between devices, one_section(): lax.all_to_all(summed.reshape(n_peers, slot_count, quarter), 'ep', split_...  14.7 us
    all_to_all x2, starting transfers between devices, one_section(): lax.all_to_all(summed.reshape(n_peers, slot_count, quarter), 'ep', split_...  9.2 us
    dot_general x2, matrix products, one_section(): jnp.dot(hidden, down_weight[0], preferred_element_type=jnp.float32)  8.96 us
    all_gather x1, blocking collectives, body(): first_full = lax.all_gather(first, 'et', axis=1, tiled=True)  5.79 us
    dot_general x2, matrix products, one_section(): gate = jnp.dot(in_rows, w_gate, preferred_element_type=jnp.float32)  5.05 us
  transfers between devices with their start and end apart: 4, of which 4 were waited for; matrix products, arithmetic and copies ran while one was open for 3% of the time, Pallas kernels for 0%

commit v1 on v0

--- a/solution.py
+++ b/solution.py
@@ -10,7 +10,7 @@
     return (scaled * (1.0 + mod[0]) + mod[1]).astype(jnp.bfloat16)
 
 
-def one_section(x_full, x_cols, mod, ids, router, gate_weight, up_weight, down_weight):
+def routed_section(x_full, x_cols, mod, ids, router, gate_weight, up_weight, down_weight):
     tok_rows = x_full.shape[0]
     width = x_full.shape[1]
     experts = router.shape[1]
@@ -28,12 +28,10 @@
     slot = jnp.sum(onehot * (counted - 1), axis=1)
     repeated = jnp.repeat(normed, picks, axis=0)
     outbox = jnp.zeros((experts, slot_count, width), jnp.bfloat16).at[flat_e, slot].set(repeated)
-    w_gate = gate_weight[0]
-    w_up = up_weight[0]
     arrived = lax.all_to_all(outbox, "ep", split_axis=0, concat_axis=0, tiled=True)
     in_rows = arrived.reshape(n_peers * slot_count, width)
-    gate = jnp.dot(in_rows, w_gate, preferred_element_type=jnp.float32)
-    upper = jnp.dot(in_rows, w_up, preferred_element_type=jnp.float32)
+    gate = jnp.dot(in_rows, gate_weight[0], preferred_element_type=jnp.float32)
+    upper = jnp.dot(in_rows, up_weight[0], preferred_element_type=jnp.float32)
     hidden = (jax.nn.silu(gate) * upper).astype(jnp.bfloat16)
     partial_out = jnp.dot(hidden, down_weight[0], preferred_element_type=jnp.float32)
     summed = lax.psum_scatter(
@@ -48,25 +46,110 @@
     return (moved, velocity)
 
 
-def body(tokens, modulation, router, gate_weight, up_weight, down_weight, expert_ids):
+def routed_body(tokens, modulation, router, gate_weight, up_weight, down_weight, expert_ids):
     quarter = tokens.shape[1] // lax.axis_size("et")
     column_start = lax.axis_index("et") * quarter
-    first_cols = lax.dynamic_slice_in_dim(tokens, column_start, quarter, 1)
-    first, _ = one_section(
-        tokens,
-        first_cols,
-        modulation[0],
-        expert_ids[0],
-        router,
-        gate_weight,
-        up_weight,
-        down_weight,
-    )
-    first_full = lax.all_gather(first, "et", axis=1, tiled=True)
-    second, velocity = one_section(
-        first_full, first, modulation[1], expert_ids[1], router, gate_weight, up_weight, down_weight
-    )
+    cols = lax.dynamic_slice_in_dim(tokens, column_start, quarter, 1)
+    weights = (router, gate_weight, up_weight, down_weight)
+    first, _ = routed_section(tokens, cols, modulation[0], expert_ids[0], *weights)
+    full = lax.all_gather(first, "et", axis=1, tiled=True)
+    second, velocity = routed_section(full, first, modulation[1], expert_ids[1], *weights)
     return (second, velocity.astype(jnp.bfloat16))
+
+
+def swap(x, axis, bit):
+    size = lax.axis_size(axis)
+    return lax.ppermute(x, axis, [(i, i ^ bit) for i in range(size)])
+
+
+def both(mine, other, bit_set, axis):
+    low = jnp.where(bit_set, other, mine)
+    high = jnp.where(bit_set, mine, other)
+    return jnp.concatenate([low, high], axis=axis)
+
+
+def gather_ep(x):
+    return [x] + [swap(x, "ep", k) for k in range(1, lax.axis_size("ep"))]
+
+
+def take_half(x, bit_set, axis):
+    half = x.shape[axis] // 2
+    start = jnp.where(bit_set, half, 0)
+    return lax.dynamic_slice_in_dim(x, start, half, axis)
+
+
+def add_halves(x, y):
+    return (x.astype(jnp.float32) + y.astype(jnp.float32)).astype(jnp.bfloat16)
+
+
+def partial_sum(x, mod, ids, router, w_gate, w_up, w_down):
+    experts = router.shape[1]
+    normed = normalize(x, mod)
+    logits = jnp.dot(normed, router, preferred_element_type=jnp.float32)
+    numbers = jnp.arange(experts, dtype=jnp.int32)
+    named = jnp.any(ids[:, :, None] == numbers, axis=1)
+    chosen = jnp.where(named, jax.nn.sigmoid(logits), 0.0)
+    weight = chosen / jnp.sum(chosen, axis=1, keepdims=True)
+    mine = numbers == lax.axis_index("ep")
+    weight = jnp.sum(jnp.where(mine, weight, 0.0), axis=1, keepdims=True)
+    gate = jnp.dot(normed, w_gate, preferred_element_type=jnp.float32)
+    upper = jnp.dot(normed, w_up, preferred_element_type=jnp.float32)
+    hidden = (jax.nn.silu(gate) * upper * weight).astype(jnp.bfloat16)
+    return jnp.dot(hidden, w_down, preferred_element_type=jnp.float32).astype(jnp.bfloat16)
+
+
+def scatter_sum(part, core, side):
+    rows = part.shape[0] // lax.axis_size("ep")
+    width = part.shape[1]
+    part = part.reshape(part.shape[0], 2, 2, width // 4)
+    keep = jnp.where(core, part[:, :, 1], part[:, :, 0])
+    send = jnp.where(core, part[:, :, 0], part[:, :, 1])
+    part = add_halves(keep, swap(send, "et", 1))
+    keep = jnp.where(side, part[:, 1], part[:, 0])
+    send = jnp.where(side, part[:, 0], part[:, 1])
+    part = add_halves(keep, swap(send, "et", 2))
+    total = part[:rows].astype(jnp.float32)
+    for k in range(1, lax.axis_size("ep")):
+        total += swap(part[k * rows : (k + 1) * rows], "ep", k).astype(jnp.float32)
+    return total
+
+
+def dense_body(tokens, modulation, router, gate_weight, up_weight, down_weight, expert_ids):
+    rows, width = tokens.shape
+    quarter = width // lax.axis_size("et")
+    where_et = lax.axis_index("et")
+    core = where_et % 2 == 1
+    side = where_et // 2 == 1
+    weights = (router, gate_weight[0], up_weight[0], down_weight[0])
+    own = lax.dynamic_slice_in_dim(tokens, where_et * quarter, quarter, 1)
+
+    sections, _, picks = expert_ids.shape
+    flat_ids = expert_ids.transpose(1, 0, 2).reshape(rows, sections * picks)
+    half = take_half(tokens, core, 1)
+    flags = jnp.pad(flat_ids.astype(jnp.bfloat16), ((0, 0), (0, 128 - sections * picks)))
+    blocks = gather_ep(jnp.concatenate([half, flags], axis=1))
+    gathered = jnp.concatenate(blocks, axis=0)
+    ids = gathered[:, width // 2 : width // 2 + sections * picks].astype(jnp.int32)
+    ids = ids.reshape(-1, sections, picks)
+    mine = gathered[rows:, : width // 2]
+    others = both(mine, swap(mine, "et", 1), core, 1)
+    x = jnp.concatenate([tokens, others], axis=0)
+
+    part = partial_sum(x, modulation[0], ids[:, 0], *weights)
+    velocity = scatter_sum(part, core, side)
+    own = (own.astype(jnp.float32) - 0.5 * velocity).astype(jnp.bfloat16)
+
+    x = jnp.concatenate(gather_ep(own), axis=0)
+    far = swap(x, "et", 2)
+    x = jnp.stack([jnp.where(side, far, x), jnp.where(side, x, far)], axis=1)
+    near = swap(x, "et", 1)
+    x = jnp.stack([jnp.where(core, near, x), jnp.where(core, x, near)], axis=2)
+    x = x.reshape(-1, width)
+
+    part = partial_sum(x, modulation[1], ids[:, 1], *weights)
+    velocity = scatter_sum(part, core, side)
+    own = (own.astype(jnp.float32) - 0.5 * velocity).astype(jnp.bfloat16)
+    return (own, velocity.astype(jnp.bfloat16))
 
 
 def solution(mesh):
@@ -80,4 +163,10 @@
         P(None, ("grp", "ep"), None),
     )
     out_specs = (P(("grp", "ep"), "et"), P(("grp", "ep"), "et"))
+
+    def body(*args):
+        experts, picks = args[2].shape[1], args[6].shape[2]
+        chosen = dense_body if experts <= 2 * picks else routed_body
+        return chosen(*args)
+
     return jax.shard_map(body, mesh=mesh, in_specs=in_specs, out_specs=out_specs, check_vma=False)

time: 214 us -> 204 us (0.953)
  blocking collectives: 56.6 us -> 0 us
  waiting for transfers between devices: 53.6 us -> 86.1 us
  starting transfers between devices: 9.24 us -> 30.5 us
  other arithmetic: 7.53 us -> 24.2 us
  between operations: 14.3 us -> 1.03 us
  local copies, waits for them, and re-layouts: 55.3 us -> 47.3 us
  matrix products: 16.3 us -> 12.2 us
    ppermute x0 -> x19, waiting for transfers between devices: none -> 86.1 us  [swap(): return lax.ppermute(x, axis, [(i, i ^ bit) for i in range(size)])]
    all_to_all x2 -> x0, blocking collectives: 50.8 us -> none  [one_section(): lax.all_to_all(outbox, 'ep', split_axis=0, concat_axis=0, tiled=True)]
    reduce_scatter x2 -> x0, waiting for transfers between devices: 38.8 us -> none  [one_section(): lax.psum_scatter(partial_out.astype(jnp.bfloat16), 'et', scatter_dimensio...]
    scatter x2 -> x0, local copies, waits for them, and re-layouts: 34.7 us -> none  [one_section(): jnp.zeros((experts, slot_count, width), jnp.bfloat16).at[flat_e, slot]]
    ppermute x0 -> x19, starting transfers between devices: none -> 30.5 us  [swap(): return lax.ppermute(x, axis, [(i, i ^ bit) for i in range(size)])]
    unnamed x16 -> x62, local copies, waits for them, and re-layouts: 3.23 us -> 21.7 us
    all_to_all x2 -> x0, waiting for transfers between devices: 14.7 us -> none  [one_section(): lax.all_to_all(summed.reshape(n_peers, slot_count, quarter), 'ep', split_...]
    all_to_all x2 -> x0, starting transfers between devices: 9.2 us -> none  [one_section(): lax.all_to_all(summed.reshape(n_peers, slot_count, quarter), 'ep', split_...]
  transfers between devices with their start and end apart: 4 -> 19, of which waited for: 4 -> 14; matrix products, arithmetic and copies ran while one was open for 3% -> 5% of each run, Pallas kernels for 0% -> 0%
where the time goes in v1:
time: 204 us; the launch traced here: 201 us
  waiting for transfers between devices  86.1 us (42%)
  local copies, waits for them, and re-layouts  47.3 us (23%)
  starting transfers between devices  30.5 us (15%)
  other arithmetic  24.2 us (12%)
  matrix products  12.2 us (6%)
    ppermute x19, waiting for transfers between devices, swap(): return lax.ppermute(x, axis, [(i, i ^ bit) for i in range(size)])  86.1 us
    ppermute x19, starting transfers between devices, swap(): return lax.ppermute(x, axis, [(i, i ^ bit) for i in range(size)])  30.5 us
    unnamed x62, local copies, waits for them, and re-layouts  21.7 us
    dot_general x2, matrix products, partial_sum(): jnp.dot(hidden, w_down, preferred_element_type=jnp.float32)  9.23 us
    slice x2, local copies, waits for them, and re-layouts, scatter_sum(): keep = jnp.where(core, part[:, :, 1], part[:, :, 0])  8.55 us
    ppermute x3, local copies, waits for them, and re-layouts, swap(): return lax.ppermute(x, axis, [(i, i ^ bit) for i in range(size)])  5.92 us
    reshape x2, local copies, waits for them, and re-layouts, scatter_sum(): part = part.reshape(part.shape[0], 2, 2, width // 4)  5.22 us
  transfers between devices with their start and end apart: 19, of which 14 were waited for; matrix products, arithmetic and copies ran while one was open for 5% of the time, Pallas kernels for 0%

profile of v1, /device:TPU:0, one launch (start us, length us, event | category | flops | bytes accessed | tf_op | source)
XLA Modules:
  0.0 201.3 jit_solution(5458949997428411064)
XLA Ops:
  8.0 3.0 %collective-permute-start = (bf16[32,2176]{1,0:T(8,128)(2,1)}, bf16[32,2176]{1,0:T(8,128)(2,1)S(1)}, u32[]{:S(2)}, u32[]{:S(2)}) collective-permute-start(bf16[32,2176]{1,0:T(8,128)(2,1)} %copy.63), channel_id=1, source_target_pairs={{0,4},{4,0},{8,12},{12,8},{1,5},{5,1},{9,13},{13,9},{2,6},{6,2},{1... | collective-permute-start | bytes 417800 | tf_op jit(solution)/shard_map/ppermute | solution.py:62
  11.0 2.6 %collective-permute-start.1 = (bf16[32,2176]{1,0:T(8,128)(2,1)}, bf16[32,2176]{1,0:T(8,128)(2,1)S(1)}, u32[]{:S(2)}, u32[]{:S(2)}) collective-permute-start(bf16[32,2176]{1,0:T(8,128)(2,1)} %copy.63), channel_id=1, source_target_pairs={{0,8},{4,12},{8,0},{12,4},{1,9},{5,13},{9,1},{13,5},{2,10},{6,14},... | collective-permute-start | bytes 417800 | tf_op jit(solution)/shard_map/ppermute | solution.py:62
  16.7 8.0 %collective-permute-done.1 = bf16[32,2176]{1,0:T(8,128)(2,1)S(1)} collective-permute-done((bf16[32,2176]{1,0:T(8,128)(2,1)}, bf16[32,2176]{1,0:T(8,128)(2,1)S(1)}, u32[]{:S(2)}, u32[]{:S(2)}) %collective-permute-start.1) | collective-permute-done | bytes 139296 | tf_op jit(solution)/shard_map/ppermute | solution.py:62
  37.8 4.6 %convolution_convert_fusion.1 = bf16[128,4096]{1,0:T(8,128)(2,1)} fusion(bf16[1,384,4096]{2,1,0:T(8,128)(2,1)S(1)} %copy-done, bf16[1,4096,384]{2,1,0:T(8,128)(2,1)} %param.11, f32[128,384]{1,0:T(8,128)} %fusion.8, f32[128]{0:T(128)S(1)} %select_reduce_fusion.1, f32[4096]{0:T(1024)S(1)} %bitcast.94, f32[4096]{0:T(1024)S(1)} %bitcast.97, ...), kind=kOutput, calls=%fused_computation.1 | convolution fusion | flops 811417600 | bytes 8619008 | tf_op jit(solution)/shard_map/dot_general | solution.py:98
  42.4 2.6 %reshape.228 = bf16[128,2,2,1024]{3,2,1,0:T(2,128)(2,1)} reshape(bf16[128,4096]{1,0:T(8,128)(2,1)} %convolution_convert_fusion.1) | data formatting | bytes 2097152 | tf_op jit(solution)/shard_map/reshape | solution.py:104
  45.0 4.3 %fusion.76 = (bf16[128,2,1,1024]{3,2,1,0:T(2,128)(2,1)}, bf16[128,2,1,1024]{3,2,1,0:T(2,128)(2,1)}) fusion(bf16[128,2,2,1024]{3,2,1,0:T(2,128)(2,1)} %reshape.228), kind=kLoop, calls=%fused_computation.107 | loop fusion | bytes 2097152 | tf_op jit(solution)/shard_map/slice | solution.py:105
  49.3 3.5 %copy.78 = bf16[128,2,1,1024]{0,3,1,2:T(8,128)(2,1)} copy(bf16[128,2,1,1024]{3,2,1,0:T(2,128)(2,1)} %get-tuple-element.20) | data formatting | bytes 1048576
  52.8 3.5 %copy.79 = bf16[128,2,1,1024]{0,3,1,2:T(8,128)(2,1)} copy(bf16[128,2,1,1024]{3,2,1,0:T(2,128)(2,1)} %get-tuple-element.21) | data formatting | bytes 1048576
  64.4 7.2 %collective-permute-done.5 = bf16[128,1024]{0,1:T(8,128)(2,1)} collective-permute-done((bf16[128,1024]{0,1:T(8,128)(2,1)S(1)}, bf16[128,1024]{0,1:T(8,128)(2,1)}, u32[]{:S(2)}, u32[]{:S(2)}) %collective-permute-start.5) | collective-permute-done | bytes 262176 | tf_op jit(solution)/shard_map/ppermute | solution.py:62
  80.1 6.7 %collective-permute-done.6 = bf16[32,1024]{0,1:T(8,128)(2,1)} collective-permute-done((bf16[32,1024]{0,1:T(8,128)(2,1)}, bf16[32,1024]{0,1:T(8,128)(2,1)}, u32[]{:S(2)}, u32[]{:S(2)}) %collective-permute-start.6) | collective-permute-done | bytes 65568 | tf_op jit(solution)/shard_map/ppermute | solution.py:62
  86.7 10.5 %collective-permute-done.7 = bf16[32,1024]{0,1:T(8,128)(2,1)} collective-permute-done((bf16[32,1024]{0,1:T(8,128)(2,1)}, bf16[32,1024]{0,1:T(8,128)(2,1)}, u32[]{:S(2)}, u32[]{:S(2)}) %collective-permute-start.7) | collective-permute-done | bytes 65568 | tf_op jit(solution)/shard_map/ppermute | solution.py:62
  98.7 5.5 %collective-permute-start.10 = (bf16[32,1024]{0,1:T(8,128)(2,1)S(1)}, bf16[32,1024]{0,1:T(8,128)(2,1)S(1)}, u32[]{:S(2)}, u32[]{:S(2)}) collective-permute-start(bf16[32,1024]{0,1:T(8,128)(2,1)S(1)} %subtract_convert_fusion.1), channel_id=1, source_target_pairs={{0,8},{4,12},{8,0},{12,4},{1,9},{5,13},{9,1},{13,5},{2,10},{6,14},... | collective-permute-start | bytes 196616 | tf_op jit(solution)/shard_map/ppermute | solution.py:62
  105.6 16.0 %collective-permute-done.10 = bf16[32,1024]{0,1:T(8,128)(2,1)S(1)} collective-permute-done((bf16[32,1024]{0,1:T(8,128)(2,1)S(1)}, bf16[32,1024]{0,1:T(8,128)(2,1)S(1)}, u32[]{:S(2)}, u32[]{:S(2)}) %collective-permute-start.10) | collective-permute-done | bytes 65568 | tf_op jit(solution)/shard_map/ppermute | solution.py:62
  123.6 4.9 %collective-permute-done.12 = bf16[128,1024]{0,1:T(8,128)(2,1)S(1)} collective-permute-done((bf16[128,1024]{0,1:T(8,128)(2,1)S(1)}, bf16[128,1024]{0,1:T(8,128)(2,1)S(1)}, u32[]{:S(2)}, u32[]{:S(2)}) %collective-permute-start.12) | collective-permute-done | bytes 262176 | tf_op jit(solution)/shard_map/ppermute | solution.py:62
  139.2 4.6 %convolution_convert_fusion = bf16[128,4096]{1,0:T(8,128)(2,1)} fusion(bf16[1,384,4096]{2,1,0:T(8,128)(2,1)S(1)} %copy-done, bf16[128,4096]{0,1:T(8,128)(2,1)} %bitcast.89, bf16[1,4096,384]{2,1,0:T(8,128)(2,1)} %param.11, f32[128,384]{1,0:T(8,128)S(1)} %fusion.6, f32[128]{0:T(128)S(1)} %select_reduce_fusion), kind=kOutput, calls=%fused_computation | convolution fusion | flops 806174720 | bytes 8585728 | tf_op jit(solution)/shard_map/dot_general | solution.py:98
  143.8 2.6 %reshape.229 = bf16[128,2,2,1024]{3,2,1,0:T(2,128)(2,1)} reshape(bf16[128,4096]{1,0:T(8,128)(2,1)} %convolution_convert_fusion) | data formatting | bytes 2097152 | tf_op jit(solution)/shard_map/reshape | solution.py:104
  146.5 4.3 %fusion.75 = (bf16[128,2,1,1024]{3,2,1,0:T(2,128)(2,1)}, bf16[128,2,1,1024]{3,2,1,0:T(2,128)(2,1)}) fusion(bf16[128,2,2,1024]{3,2,1,0:T(2,128)(2,1)} %reshape.229), kind=kLoop, calls=%fused_computation.106 | loop fusion | bytes 2097152 | tf_op jit(solution)/shard_map/slice | solution.py:105
  150.7 3.5 %copy.80 = bf16[128,2,1,1024]{0,3,1,2:T(8,128)(2,1)} copy(bf16[128,2,1,1024]{3,2,1,0:T(2,128)(2,1)} %get-tuple-element.16) | data formatting | bytes 1048576
  154.2 3.5 %copy.81 = bf16[128,2,1,1024]{0,3,1,2:T(8,128)(2,1)} copy(bf16[128,2,1,1024]{3,2,1,0:T(2,128)(2,1)} %get-tuple-element.17) | data formatting | bytes 1048576
  163.7 6.8 %collective-permute-done.15 = bf16[128,1024]{0,1:T(8,128)(2,1)S(1)} collective-permute-done((bf16[128,1024]{0,1:T(8,128)(2,1)S(1)}, bf16[128,1024]{0,1:T(8,128)(2,1)S(1)}, u32[]{:S(2)}, u32[]{:S(2)}) %collective-permute-start.15) | collective-permute-done | bytes 262176 | tf_op jit(solution)/shard_map/ppermute | solution.py:62
  170.9 5.6 %collective-permute-start.16 = (bf16[32,1024]{0,1:T(8,128)(2,1)S(1)}, bf16[32,1024]{0,1:T(8,128)(2,1)S(1)}, u32[]{:S(2)}, u32[]{:S(2)}) collective-permute-start(bf16[32,1024]{0,1:T(8,128)(2,1)S(1)} %get-tuple-element.26), channel_id=1, source_target_pairs={{0,4},{4,0},{8,12},{12,8},{1,5},{5,1},{9,13},{13,9},{2,6},{6,2},{1... | collective-permute-start | bytes 196616 | tf_op jit(solution)/shard_map/ppermute | solution.py:62
  176.5 2.4 %collective-permute-start.18 = (bf16[32,1024]{0,1:T(8,128)(2,1)S(1)}, bf16[32,1024]{0,1:T(8,128)(2,1)S(1)}, u32[]{:S(2)}, u32[]{:S(2)}) collective-permute-start(bf16[32,1024]{0,1:T(8,128)(2,1)S(1)} %get-tuple-element.27), channel_id=1, source_target_pairs={{0,12},{4,8},{8,4},{12,0},{1,13},{5,9},{9,5},{13,1},{2,14},{6,10},... | collective-permute-start | bytes 196616 | tf_op jit(solution)/shard_map/ppermute | solution.py:62
  179.0 7.0 %collective-permute-done.16 = bf16[32,1024]{0,1:T(8,128)(2,1)S(1)} collective-permute-done((bf16[32,1024]{0,1:T(8,128)(2,1)S(1)}, bf16[32,1024]{0,1:T(8,128)(2,1)S(1)}, u32[]{:S(2)}, u32[]{:S(2)}) %collective-permute-start.16) | collective-permute-done | bytes 65568 | tf_op jit(solution)/shard_map/ppermute | solution.py:62
  186.0 11.9 %collective-permute-done.17 = bf16[32,1024]{0,1:T(8,128)(2,1)S(1)} collective-permute-done((bf16[32,1024]{0,1:T(8,128)(2,1)S(1)}, bf16[32,1024]{0,1:T(8,128)(2,1)S(1)}, u32[]{:S(2)}, u32[]{:S(2)}) %collective-permute-start.17) | collective-permute-done | bytes 65568 | tf_op jit(solution)/shard_map/ppermute | solution.py:62
  (131 shorter events, 65.0 us)
Async XLA Ops:
  0.6 37.0 %copy-start = (bf16[1,384,4096]{2,1,0:T(8,128)(2,1)S(1)}, bf16[1,384,4096]{2,1,0:T(8,128)(2,1)}, u32[]{:S(2)}) copy-start(bf16[1,384,4096]{2,1,0:T(8,128)(2,1)} %param.12) | copy-start | bytes 9437188
  8.0 8.7 %collective-permute-start = (bf16[32,2176]{1,0:T(8,128)(2,1)}, bf16[32,2176]{1,0:T(8,128)(2,1)S(1)}, u32[]{:S(2)}, u32[]{:S(2)}) collective-permute-start(bf16[32,2176]{1,0:T(8,128)(2,1)} %copy.63), channel_id=1, source_target_pairs={{0,4},{4,0},{8,12},{12,8},{1,5},{5,1},{9,13},{13,9},{2,6},{6,2},{1... | collective-permute-start | bytes 417800 | tf_op jit(solution)/shard_map/ppermute | solution.py:62
  11.0 13.7 %collective-permute-start.1 = (bf16[32,2176]{1,0:T(8,128)(2,1)}, bf16[32,2176]{1,0:T(8,128)(2,1)S(1)}, u32[]{:S(2)}, u32[]{:S(2)}) collective-permute-start(bf16[32,2176]{1,0:T(8,128)(2,1)} %copy.63), channel_id=1, source_target_pairs={{0,8},{4,12},{8,0},{12,4},{1,9},{5,13},{9,1},{13,5},{2,10},{6,14},... | collective-permute-start | bytes 417800 | tf_op jit(solution)/shard_map/ppermute | solution.py:62
  13.6 11.8 %collective-permute-start.2 = (bf16[32,2176]{1,0:T(8,128)(2,1)}, bf16[32,2176]{1,0:T(8,128)(2,1)}, u32[]{:S(2)}, u32[]{:S(2)}) collective-permute-start(bf16[32,2176]{1,0:T(8,128)(2,1)} %copy.63), channel_id=1, source_target_pairs={{0,12},{4,8},{8,4},{12,0},{1,13},{5,9},{9,5},{13,1},{2,14},{6,10},... | collective-permute-start | bytes 417800 | tf_op jit(solution)/shard_map/ppermute | solution.py:62
  26.4 7.5 %collective-permute-start.3 = (bf16[96,2048]{1,0:T(8,128)(2,1)S(1)}, bf16[96,2048]{1,0:T(8,128)(2,1)}, u32[]{:S(2)}, u32[]{:S(2)}) collective-permute-start(bf16[96,2048]{1,0:T(8,128)(2,1)S(1)} %pad_maximum_fusion.2), channel_id=1, source_target_pairs={{0,1},{1,0},{2,3},{3,2},{4,5},{5,4},{6,7},{7,6},{8,9},{9,8},{10,11... | collective-permute-start | bytes 1179656 | tf_op jit(solution)/shard_map/ppermute | solution.py:62
  58.2 2.4 %collective-permute-start.4 = (bf16[128,2,1024]{0,2,1:T(8,128)(2,1)}, bf16[128,2,1024]{0,2,1:T(8,128)(2,1)}, u32[]{:S(2)}, u32[]{:S(2)}) collective-permute-start(bf16[128,2,1024]{0,2,1:T(8,128)(2,1)} %select_bitcast_fusion.3), channel_id=1, source_target_pairs={{0,1},{1,0},{2,3},{3,2},{4,5},{5,4},{6,7},{7,6},{8,9},{9,8},{10,11... | collective-permute-start | bytes 1572872 | tf_op jit(solution)/shard_map/ppermute | solution.py:62
  62.8 8.8 %collective-permute-start.5 = (bf16[128,1024]{0,1:T(8,128)(2,1)S(1)}, bf16[128,1024]{0,1:T(8,128)(2,1)}, u32[]{:S(2)}, u32[]{:S(2)}) collective-permute-start(bf16[128,1024]{0,1:T(8,128)(2,1)S(1)} %select_bitcast_fusion.7), channel_id=1, source_target_pairs={{0,2},{1,3},{2,0},{3,1},{4,6},{5,7},{6,4},{7,5},{8,10},{9,11},{10,... | collective-permute-start | bytes 786440 | tf_op jit(solution)/shard_map/ppermute | solution.py:62
  74.0 12.8 %collective-permute-start.6 = (bf16[32,1024]{0,1:T(8,128)(2,1)}, bf16[32,1024]{0,1:T(8,128)(2,1)}, u32[]{:S(2)}, u32[]{:S(2)}) collective-permute-start(bf16[32,1024]{0,1:T(8,128)(2,1)} %get-tuple-element.29), channel_id=1, source_target_pairs={{0,4},{4,0},{8,12},{12,8},{1,5},{5,1},{9,13},{13,9},{2,6},{6,2},{1... | collective-permute-start | bytes 196616 | tf_op jit(solution)/shard_map/ppermute | solution.py:62
  75.5 21.7 %collective-permute-start.7 = (bf16[32,1024]{0,1:T(8,128)(2,1)}, bf16[32,1024]{0,1:T(8,128)(2,1)}, u32[]{:S(2)}, u32[]{:S(2)}) collective-permute-start(bf16[32,1024]{0,1:T(8,128)(2,1)} %get-tuple-element.31), channel_id=1, source_target_pairs={{0,8},{4,12},{8,0},{12,4},{1,9},{5,13},{9,1},{13,5},{2,10},{6,14},... | collective-permute-start | bytes 196616 | tf_op jit(solution)/shard_map/ppermute | solution.py:62
  76.8 20.4 %collective-permute-start.8 = (bf16[32,1024]{0,1:T(8,128)(2,1)}, bf16[32,1024]{0,1:T(8,128)(2,1)}, u32[]{:S(2)}, u32[]{:S(2)}) collective-permute-start(bf16[32,1024]{0,1:T(8,128)(2,1)} %get-tuple-element.30), channel_id=1, source_target_pairs={{0,12},{4,8},{8,4},{12,0},{1,13},{5,9},{9,5},{13,1},{2,14},{6,10},... | collective-permute-start | bytes 196616 | tf_op jit(solution)/shard_map/ppermute | solution.py:62
  98.6 31.4 %copy-start.17 = (f32[4096]{0:T(1024)S(1)}, f32[4096]{0:T(1024)}, u32[]{:S(2)}) copy-start(f32[4096]{0:T(1024)} %get-tuple-element.12) | copy-start | bytes 49156
  98.6 31.4 %copy-start.16 = (f32[4096]{0:T(1024)S(1)}, f32[4096]{0:T(1024)}, u32[]{:S(2)}) copy-start(f32[4096]{0:T(1024)} %get-tuple-element.13) | copy-start | bytes 49156
  98.7 31.5 %copy-start.26 = (s32[128,2]{0,1:T(2,128)S(1)}, s32[128,2]{0,1:T(2,128)}, u32[]{:S(2)}) copy-start(s32[128,2]{0,1:T(2,128)} %get-tuple-element.36) | copy-start | bytes 3076
  98.7 22.9 %collective-permute-start.10 = (bf16[32,1024]{0,1:T(8,128)(2,1)S(1)}, bf16[32,1024]{0,1:T(8,128)(2,1)S(1)}, u32[]{:S(2)}, u32[]{:S(2)}) collective-permute-start(bf16[32,1024]{0,1:T(8,128)(2,1)S(1)} %subtract_convert_fusion.1), channel_id=1, source_target_pairs={{0,8},{4,12},{8,0},{12,4},{1,9},{5,13},{9,1},{13,5},{2,10},{6,14},... | collective-permute-start | bytes 196616 | tf_op jit(solution)/shard_map/ppermute | solution.py:62
  104.2 17.4 %collective-permute-start.11 = (bf16[32,1024]{0,1:T(8,128)(2,1)S(1)}, bf16[32,1024]{0,1:T(8,128)(2,1)S(1)}, u32[]{:S(2)}, u32[]{:S(2)}) collective-permute-start(bf16[32,1024]{0,1:T(8,128)(2,1)S(1)} %subtract_convert_fusion.1), channel_id=1, source_target_pairs={{0,12},{4,8},{8,4},{12,0},{1,13},{5,9},{9,5},{13,1},{2,14},{6,10},... | collective-permute-start | bytes 196616 | tf_op jit(solution)/shard_map/ppermute | solution.py:62
  105.6 16.1 %collective-permute-start.9 = (bf16[32,1024]{0,1:T(8,128)(2,1)S(1)}, bf16[32,1024]{0,1:T(8,128)(2,1)S(1)}, u32[]{:S(2)}, u32[]{:S(2)}) collective-permute-start(bf16[32,1024]{0,1:T(8,128)(2,1)S(1)} %subtract_convert_fusion.1), channel_id=1, source_target_pairs={{0,4},{4,0},{8,12},{12,8},{1,5},{5,1},{9,13},{13,9},{2,6},{6,2},{1... | collective-permute-start | bytes 196616 | tf_op jit(solution)/shard_map/ppermute | solution.py:62
  122.0 6.4 %collective-permute-start.12 = (bf16[128,1024]{0,1:T(8,128)(2,1)S(1)}, bf16[128,1024]{0,1:T(8,128)(2,1)S(1)}, u32[]{:S(2)}, u32[]{:S(2)}) collective-permute-start(bf16[128,1024]{0,1:T(8,128)(2,1)S(1)} %pad_maximum_fusion.4), channel_id=1, source_target_pairs={{0,2},{1,3},{2,0},{3,1},{4,6},{5,7},{6,4},{7,5},{8,10},{9,11},{10,... | collective-permute-start | bytes 786440 | tf_op jit(solution)/shard_map/ppermute | solution.py:62
  130.1 2.3 %collective-permute-start.13 = (bf16[128,2,1024]{0,2,1:T(8,128)(2,1)}, bf16[128,2,1024]{0,2,1:T(8,128)(2,1)}, u32[]{:S(2)}, u32[]{:S(2)}) collective-permute-start(bf16[128,2,1024]{0,2,1:T(8,128)(2,1)} %pad_maximum_fusion.1), channel_id=1, source_target_pairs={{0,1},{1,0},{2,3},{3,2},{4,5},{5,4},{6,7},{7,6},{8,9},{9,8},{10,11... | collective-permute-start | bytes 1572872 | tf_op jit(solution)/shard_map/ppermute | solution.py:62
  158.8 2.0 collective-permute-start.14
  162.1 35.9 %copy-start.6 = (bf16[32,1024]{0,1:T(8,128)(2,1)S(1)}, bf16[32,1024]{0,1:T(8,128)(2,1)}, u32[]{:S(2)}) copy-start(bf16[32,1024]{0,1:T(8,128)(2,1)} %copy-done.5) | copy-start | bytes 196612
  162.1 8.4 %collective-permute-start.15 = (bf16[128,1024]{0,1:T(8,128)(2,1)S(1)}, bf16[128,1024]{0,1:T(8,128)(2,1)S(1)}, u32[]{:S(2)}, u32[]{:S(2)}) collective-permute-start(bf16[128,1024]{0,1:T(8,128)(2,1)S(1)} %select_bitcast_fusion.4), channel_id=1, source_target_pairs={{0,2},{1,3},{2,0},{3,1},{4,6},{5,7},{6,4},{7,5},{8,10},{9,11},{10,... | collective-permute-start | bytes 786440 | tf_op jit(solution)/shard_map/ppermute | solution.py:62
  170.9 15.1 %collective-permute-start.16 = (bf16[32,1024]{0,1:T(8,128)(2,1)S(1)}, bf16[32,1024]{0,1:T(8,128)(2,1)S(1)}, u32[]{:S(2)}, u32[]{:S(2)}) collective-permute-start(bf16[32,1024]{0,1:T(8,128)(2,1)S(1)} %get-tuple-element.26), channel_id=1, source_target_pairs={{0,4},{4,0},{8,12},{12,8},{1,5},{5,1},{9,13},{13,9},{2,6},{6,2},{1... | collective-permute-start | bytes 196616 | tf_op jit(solution)/shard_map/ppermute | solution.py:62
  176.5 21.4 %collective-permute-start.17 = (bf16[32,1024]{0,1:T(8,128)(2,1)S(1)}, bf16[32,1024]{0,1:T(8,128)(2,1)S(1)}, u32[]{:S(2)}, u32[]{:S(2)}) collective-permute-start(bf16[32,1024]{0,1:T(8,128)(2,1)S(1)} %get-tuple-element.28), channel_id=1, source_target_pairs={{0,8},{4,12},{8,0},{12,4},{1,9},{5,13},{9,1},{13,5},{2,10},{6,14},... | collective-permute-start | bytes 196616 | tf_op jit(solution)/shard_map/ppermute | solution.py:62
  176.5 21.4 %collective-permute-start.18 = (bf16[32,1024]{0,1:T(8,128)(2,1)S(1)}, bf16[32,1024]{0,1:T(8,128)(2,1)S(1)}, u32[]{:S(2)}, u32[]{:S(2)}) collective-permute-start(bf16[32,1024]{0,1:T(8,128)(2,1)S(1)} %get-tuple-element.27), channel_id=1, source_target_pairs={{0,12},{4,8},{8,4},{12,0},{1,13},{5,9},{9,5},{13,1},{2,14},{6,10},... | collective-permute-start | bytes 196616 | tf_op jit(solution)/shard_map/ppermute | solution.py:62
  (22 other events, 73.3 us)

commit v2 on v0

--- a/solution.py
+++ b/solution.py
@@ -1,6 +1,10 @@
+import functools
+
 import jax
 import jax.numpy as jnp
 from jax import lax
+from jax.experimental import pallas as pl
+from jax.experimental.pallas import tpu as pltpu
 from jax.sharding import PartitionSpec as P
 
 
@@ -10,7 +14,7 @@
     return (scaled * (1.0 + mod[0]) + mod[1]).astype(jnp.bfloat16)
 
 
-def one_section(x_full, x_cols, mod, ids, router, gate_weight, up_weight, down_weight):
+def routed_section(x_full, x_cols, mod, ids, router, gate_weight, up_weight, down_weight):
     tok_rows = x_full.shape[0]
     width = x_full.shape[1]
     experts = router.shape[1]
@@ -28,12 +32,10 @@
     slot = jnp.sum(onehot * (counted - 1), axis=1)
     repeated = jnp.repeat(normed, picks, axis=0)
     outbox = jnp.zeros((experts, slot_count, width), jnp.bfloat16).at[flat_e, slot].set(repeated)
-    w_gate = gate_weight[0]
-    w_up = up_weight[0]
     arrived = lax.all_to_all(outbox, "ep", split_axis=0, concat_axis=0, tiled=True)
     in_rows = arrived.reshape(n_peers * slot_count, width)
-    gate = jnp.dot(in_rows, w_gate, preferred_element_type=jnp.float32)
-    upper = jnp.dot(in_rows, w_up, preferred_element_type=jnp.float32)
+    gate = jnp.dot(in_rows, gate_weight[0], preferred_element_type=jnp.float32)
+    upper = jnp.dot(in_rows, up_weight[0], preferred_element_type=jnp.float32)
     hidden = (jax.nn.silu(gate) * upper).astype(jnp.bfloat16)
     partial_out = jnp.dot(hidden, down_weight[0], preferred_element_type=jnp.float32)
     summed = lax.psum_scatter(
@@ -48,25 +50,260 @@
     return (moved, velocity)
 
 
-def body(tokens, modulation, router, gate_weight, up_weight, down_weight, expert_ids):
+def routed_body(tokens, modulation, router, gate_weight, up_weight, down_weight, expert_ids):
     quarter = tokens.shape[1] // lax.axis_size("et")
     column_start = lax.axis_index("et") * quarter
-    first_cols = lax.dynamic_slice_in_dim(tokens, column_start, quarter, 1)
-    first, _ = one_section(
-        tokens,
-        first_cols,
-        modulation[0],
-        expert_ids[0],
-        router,
-        gate_weight,
-        up_weight,
-        down_weight,
-    )
-    first_full = lax.all_gather(first, "et", axis=1, tiled=True)
-    second, velocity = one_section(
-        first_full, first, modulation[1], expert_ids[1], router, gate_weight, up_weight, down_weight
-    )
+    cols = lax.dynamic_slice_in_dim(tokens, column_start, quarter, 1)
+    weights = (router, gate_weight, up_weight, down_weight)
+    first, _ = routed_section(tokens, cols, modulation[0], expert_ids[0], *weights)
+    full = lax.all_gather(first, "et", axis=1, tiled=True)
+    second, velocity = routed_section(full, first, modulation[1], expert_ids[1], *weights)
     return (second, velocity.astype(jnp.bfloat16))
+
+
+def swap(x, axis, bit):
+    size = lax.axis_size(axis)
+    return lax.ppermute(x, axis, [(i, i ^ bit) for i in range(size)])
+
+
+LANES = 128
+VMEM_LIMIT = 40 * 1024 * 1024
+
+
+def params():
+    return pltpu.CompilerParams(vmem_limit_bytes=VMEM_LIMIT)
+
+
+def whole(shape):
+    return pl.BlockSpec(shape, lambda *_: (0,) * len(shape))
+
+
+def aligned(index, size):
+    return pl.ds(pl.multiple_of(index * size, size), size)
+
+
+def pack_kernel(place, tokens_ref, ids_ref, out_ref, own_ref):
+    half = tokens_ref.shape[1] // 2
+    quarter = half // 2
+    out_ref[:, :half] = tokens_ref[:, aligned(place[0] & 1, half)]
+    own_ref[...] = tokens_ref[:, aligned(place[0], quarter)]
+    experts = place[2]
+    lane = lax.broadcasted_iota(jnp.int32, (tokens_ref.shape[0], LANES), 1)
+    flags = jnp.zeros(lane.shape, jnp.float32)
+    for s in range(ids_ref.shape[0]):
+        for k in range(ids_ref.shape[2]):
+            flags += jnp.where(ids_ref[s][:, k : k + 1] + s * experts == lane, 1.0, 0.0)
+    out_ref[:, half:] = flags.astype(jnp.bfloat16)
+
+
+def pack(place, tokens, ids):
+    rows, width = tokens.shape
+    shapes = [(rows, width // 2 + LANES), (rows, width // 4)]
+    return pl.pallas_call(
+        pack_kernel,
+        grid_spec=pltpu.PrefetchScalarGridSpec(
+            num_scalar_prefetch=1,
+            grid=(1,),
+            in_specs=[whole(tokens.shape), whole(ids.shape)],
+            out_specs=[whole(s) for s in shapes],
+        ),
+        out_shape=[jax.ShapeDtypeStruct(s, jnp.bfloat16) for s in shapes],
+        compiler_params=params(),
+        name="pack",
+    )(place, tokens, ids)
+
+
+def front_kernel(pieces, section, experts, n_flags, place, *refs):
+    n = len(pieces)
+    x_refs, flag_refs = refs[:n], refs[n : n + n_flags]
+    mod_ref, router_ref, gate_ref, up_ref, out_ref, normed_ref, gate_acc, up_acc, weight_ref = refs[n + n_flags :]
+    step = pl.program_id(0)
+    depth = gate_ref.shape[1]
+    width = normed_ref.shape[1]
+
+    @pl.when(step == 0)
+    def _():
+        groups = sorted({row for row, _, _, _ in pieces})
+        for row in groups:
+            members = [i for i in range(n) if pieces[i][0] == row]
+            rows = pieces[members[0]][1]
+            total = jnp.zeros((rows, 1), jnp.float32)
+            for i in members:
+                xf = x_refs[i][:, : pieces[i][2]].astype(jnp.float32)
+                total += jnp.sum(xf * xf, axis=1, keepdims=True)
+            scale = lax.rsqrt(total / width + 1e-06)
+            for i in members:
+                cols = pieces[i][2]
+                where = aligned(pieces[i][3](place[0]), cols)
+                xf = x_refs[i][:, :cols].astype(jnp.float32)
+                normed_ref[row : row + rows, where] = (
+                    xf * scale * (1.0 + mod_ref[0:1, where]) + mod_ref[1:2, where]
+                ).astype(jnp.bfloat16)
+        logits = lax.dot_general(
+            normed_ref[...], router_ref[...], (((1,), (1,)), ((), ())), preferred_element_type=jnp.float32
+        )
+        count = logits.shape[1]
+        lane = lax.broadcasted_iota(jnp.int32, logits.shape, 1)
+        flags = jnp.concatenate([f[:, :count] for f in flag_refs], axis=0).astype(jnp.float32)
+        here = (lane >= section * experts) & (lane < (section + 1) * experts) & (flags > 0.5)
+        chosen = jnp.where(here, jax.nn.sigmoid(logits), 0.0)
+        mine = jnp.where(lane == section * experts + place[1], chosen, 0.0)
+        weight_ref[...] = jnp.sum(mine, axis=1, keepdims=True) / jnp.sum(chosen, axis=1, keepdims=True)
+        gate_acc[...] = jnp.zeros_like(gate_acc)
+        up_acc[...] = jnp.zeros_like(up_acc)
+
+    block = normed_ref[:, aligned(step, depth)]
+    gate_acc[...] += jnp.dot(block, gate_ref[0], preferred_element_type=jnp.float32)
+    up_acc[...] += jnp.dot(block, up_ref[0], preferred_element_type=jnp.float32)
+
+    @pl.when(step == pl.num_programs(0) - 1)
+    def _():
+        gate = gate_acc[...]
+        out_ref[...] = (gate / (1.0 + jnp.exp(-gate)) * up_acc[...] * weight_ref[...]).astype(jnp.bfloat16)
+
+
+def front(place, xs, pieces, flags, half, section, experts, mod, routers, w_gate, w_up):
+    _, width, hidden = w_gate.shape
+    rows = sum(f.shape[0] for f in flags)
+    steps = 4
+    depth = width // steps
+    flag_spec = pl.BlockSpec((flags[0].shape[0], LANES), lambda k, p: (0, half // LANES))
+    weight_spec = pl.BlockSpec((1, depth, hidden), lambda k, p: (0, k, 0))
+    return pl.pallas_call(
+        functools.partial(front_kernel, pieces, section, experts, len(flags)),
+        grid_spec=pltpu.PrefetchScalarGridSpec(
+            num_scalar_prefetch=1,
+            grid=(steps,),
+            in_specs=[whole(x.shape) for x in xs]
+            + [flag_spec] * len(flags)
+            + [whole(mod.shape), whole(routers.shape), weight_spec, weight_spec],
+            out_specs=whole((rows, hidden)),
+            scratch_shapes=[
+                pltpu.VMEM((rows, width), jnp.bfloat16),
+                pltpu.VMEM((rows, hidden), jnp.float32),
+                pltpu.VMEM((rows, hidden), jnp.float32),
+                pltpu.VMEM((rows, 1), jnp.float32),
+            ],
+        ),
+        out_shape=jax.ShapeDtypeStruct((rows, hidden), jnp.bfloat16),
+        compiler_params=params(),
+        cost_estimate=pl.CostEstimate(
+            flops=4 * rows * width * hidden, bytes_accessed=4 * width * hidden, transcendentals=0
+        ),
+        name="front",
+    )(place, *xs, *flags, mod, routers, w_gate, w_up)
+
+
+def down_kernel(place, hidden_ref, down_ref, *refs):
+    product = jnp.dot(hidden_ref[...], down_ref[0], preferred_element_type=jnp.float32)
+    for ref in refs[:-1]:
+        product += ref[...].astype(jnp.float32)
+    refs[-1][...] = product.astype(refs[-1].dtype)
+
+
+def down(place, hidden, w_down, flip, adds=(), dtype=jnp.bfloat16):
+    _, units, width = w_down.shape
+    rows = hidden.shape[0]
+    quarter = width // 4
+    steps = 2
+    cols = quarter // steps
+    out_spec = pl.BlockSpec((rows, cols), lambda j, p: (0, j))
+    return pl.pallas_call(
+        down_kernel,
+        grid_spec=pltpu.PrefetchScalarGridSpec(
+            num_scalar_prefetch=1,
+            grid=(steps,),
+            in_specs=[
+                whole(hidden.shape),
+                pl.BlockSpec((1, units, cols), lambda j, p: (0, 0, (p[0] ^ flip) * steps + j)),
+            ]
+            + [out_spec] * len(adds),
+            out_specs=out_spec,
+        ),
+        out_shape=jax.ShapeDtypeStruct((rows, quarter), dtype),
+        compiler_params=params(),
+        cost_estimate=pl.CostEstimate(
+            flops=2 * rows * units * quarter, bytes_accessed=2 * units * quarter, transcendentals=0
+        ),
+        name="down",
+    )(place, hidden, w_down, *adds)
+
+
+def split_kernel(keep_ref, came_ref, *out_refs):
+    rows = out_refs[0].shape[0]
+    for k, out in enumerate(out_refs):
+        part = slice(k * rows, (k + 1) * rows)
+        out[...] = (keep_ref[part, :] + came_ref[part, :].astype(jnp.float32)).astype(out.dtype)
+
+
+def split(keep, came, blocks):
+    rows, cols = keep.shape
+    shape = (rows // blocks, cols)
+    dtypes = [jnp.float32] + [jnp.bfloat16] * (blocks - 1)
+    return pl.pallas_call(
+        split_kernel,
+        out_shape=[jax.ShapeDtypeStruct(shape, t) for t in dtypes],
+        compiler_params=params(),
+        name="split",
+    )(keep, came)
+
+
+def move_kernel(own_ref, total_ref, *refs):
+    came, (next_ref, velocity_ref) = refs[:-2], refs[-2:]
+    velocity = total_ref[...]
+    for ref in came:
+        velocity += ref[...].astype(jnp.float32)
+    next_ref[...] = (own_ref[...].astype(jnp.float32) - 0.5 * velocity).astype(jnp.bfloat16)
+    velocity_ref[...] = velocity.astype(jnp.bfloat16)
+
+
+def move(own, total, came):
+    return pl.pallas_call(
+        move_kernel,
+        out_shape=[jax.ShapeDtypeStruct(own.shape, jnp.bfloat16)] * 2,
+        compiler_params=params(),
+        name="move",
+    )(own, total, *came)
+
+
+def sum_back(place, hidden, w_down, own):
+    peers = lax.axis_size("ep")
+    far = swap(down(place, hidden, w_down, 3), "et", 1)
+    near = swap(down(place, hidden, w_down, 1), "et", 1)
+    came = swap(down(place, hidden, w_down, 2, (far,)), "et", 2)
+    keep = down(place, hidden, w_down, 0, (near,), jnp.float32)
+    total, *blocks = split(keep, came, peers)
+    return move(own, total, [swap(b, "ep", k + 1) for k, b in enumerate(blocks)])
+
+
+def dense_body(tokens, modulation, router, gate_weight, up_weight, down_weight, expert_ids):
+    rows, width = tokens.shape
+    half, quarter = width // 2, width // 4
+    experts = router.shape[1]
+    peers = range(1, lax.axis_size("ep"))
+    place = jnp.stack([lax.axis_index("et"), lax.axis_index("ep"), jnp.int32(experts)]).astype(jnp.int32)
+    routers = jnp.concatenate([router.T] * expert_ids.shape[0], axis=0)
+    expert = (routers, gate_weight, up_weight)
+
+    packed, own = pack(place, tokens, expert_ids)
+    flags = [packed] + [swap(packed, "ep", k) for k in peers]
+    xs, pieces = [tokens], [(0, rows, width, lambda et: 0)]
+    for k in peers:
+        xs += [flags[k], swap(flags[k], "et", 1)]
+        pieces += [
+            (k * rows, rows, half, lambda et: et & 1),
+            (k * rows, rows, half, lambda et: 1 - (et & 1)),
+        ]
+    hidden = front(place, xs, pieces, flags, half, 0, experts, modulation[0], *expert)
+    own, _ = sum_back(place, hidden, down_weight, own)
+
+    gathered = jnp.concatenate([own] + [swap(own, "ep", k) for k in peers], axis=0)
+    side = swap(gathered, "et", 2)
+    xs = [gathered, side, swap(gathered, "et", 1), swap(side, "et", 1)]
+    flips = [0, 2, 1, 3]
+    pieces = [(0, gathered.shape[0], quarter, functools.partial(lambda f, et: et ^ f, f)) for f in flips]
+    hidden = front(place, xs, pieces, flags, half, 1, experts, modulation[1], *expert)
+    return tuple(sum_back(place, hidden, down_weight, own))
 
 
 def solution(mesh):
@@ -80,4 +317,12 @@
         P(None, ("grp", "ep"), None),
     )
     out_specs = (P(("grp", "ep"), "et"), P(("grp", "ep"), "et"))
+
+    def body(*args):
+        experts, picks = args[2].shape[1], args[6].shape[2]
+        peers = lax.axis_size("ep")
+        fits = lax.axis_size("et") == 4 and peers & (peers - 1) == 0
+        chosen = dense_body if fits and experts <= 2 * picks else routed_body
+        return chosen(*args)
+
     return jax.shard_map(body, mesh=mesh, in_specs=in_specs, out_specs=out_specs, check_vma=False)

time: 214 us -> 93.7 us (0.44)
  blocking collectives: 56.6 us -> 0 us
  local copies, waits for them, and re-layouts: 55.3 us -> 6.32 us
  Pallas kernels: 0 us -> 18.7 us
  matrix products: 16.3 us -> 0 us
  starting transfers between devices: 9.24 us -> 25.1 us
  between operations: 14.3 us -> 0.81 us
  waiting for transfers between devices: 53.6 us -> 41.4 us
  other arithmetic: 7.53 us -> 0.94 us
    all_to_all x2 -> x0, blocking collectives: 50.8 us -> none  [one_section(): lax.all_to_all(outbox, 'ep', split_axis=0, concat_axis=0, tiled=True)]
    ppermute x0 -> x24, waiting for transfers between devices: none -> 41.4 us  [swap(): return lax.ppermute(x, axis, [(i, i ^ bit) for i in range(size)])]
    reduce_scatter x2 -> x0, waiting for transfers between devices: 38.8 us -> none  [one_section(): lax.psum_scatter(partial_out.astype(jnp.bfloat16), 'et', scatter_dimensio...]
    scatter x2 -> x0, local copies, waits for them, and re-layouts: 34.7 us -> none  [one_section(): jnp.zeros((experts, slot_count, width), jnp.bfloat16).at[flat_e, slot]]
    ppermute x0 -> x24, starting transfers between devices: none -> 25.1 us  [swap(): return lax.ppermute(x, axis, [(i, i ^ bit) for i in range(size)])]
    pallas_call x0 -> x15, Pallas kernels: none -> 18.7 us  [the longest x8 9.31 us: down(): pl.pallas_call(down_kernel, grid_spec=pltpu.PrefetchScalarGridSpec(num_sc...]
    dot_general x6 -> x0, matrix products: 16.3 us -> none  [the longest x2 8.96 us: one_section(): jnp.dot(hidden, down_weight[0], preferred_element_type=jnp.float32)]
    all_to_all x2 -> x0, waiting for transfers between devices: 14.7 us -> none  [one_section(): lax.all_to_all(summed.reshape(n_peers, slot_count, quarter), 'ep', split_...]
  transfers between devices with their start and end apart: 4 -> 24, of which waited for: 4 -> 14; matrix products, arithmetic and copies ran while one was open for 3% -> 2% of each run, Pallas kernels for 0% -> 8%
where the time goes in v2:
time: 93.7 us; the launch traced here: 93.3 us
  waiting for transfers between devices  41.4 us (44%)
  starting transfers between devices  25.1 us (27%)
  Pallas kernels  18.7 us (20%)
  local copies, waits for them, and re-layouts  6.32 us (7%)
  other arithmetic  0.94 us (1%)
    ppermute x24, waiting for transfers between devices, swap(): return lax.ppermute(x, axis, [(i, i ^ bit) for i in range(size)])  41.4 us
    ppermute x24, starting transfers between devices, swap(): return lax.ppermute(x, axis, [(i, i ^ bit) for i in range(size)])  25.1 us
    pallas_call x8, Pallas kernels, down(): pl.pallas_call(down_kernel, grid_spec=pltpu.PrefetchScalarGridSpec(num_sc...  9.31 us
    pallas_call x2, Pallas kernels, front(): pl.pallas_call(functools.partial(front_kernel, pieces, section, experts,...  7.26 us
    unnamed x16, local copies, waits for them, and re-layouts  5.53 us
  transfers between devices with their start and end apart: 24, of which 14 were waited for; matrix products, arithmetic and copies ran while one was open for 2% of the time, Pallas kernels for 8%

profile of v2, /device:TPU:0, one launch (start us, length us, event | category | flops | bytes accessed | tf_op | source)
XLA Modules:
  0.0 93.3 jit_solution(14113691188380720526)
XLA Ops:
  3.1 3.1 %collective-permute-start = (bf16[32,2176]{1,0:T(8,128)(2,1)S(1)}, bf16[32,2176]{1,0:T(8,128)(2,1)S(1)}, u32[]{:S(2)}, u32[]{:S(2)}) collective-permute-start(bf16[32,2176]{1,0:T(8,128)(2,1)S(1)} %get-tuple-element.14.refs_7_.refs_4_), channel_id=1, source_target_pairs={{0,4},{4,0},{8,12},{12,8},{1,5},{5,1},{9,13},{13,9},{2,6},{6,2},{1... | collective-permute-start | bytes 417800 | tf_op jit(solution)/shard_map/ppermute | solution.py:66
  6.2 2.6 %collective-permute-start.2 = (bf16[32,2176]{1,0:T(8,128)(2,1)S(1)}, bf16[32,2176]{1,0:T(8,128)(2,1)S(1)}, u32[]{:S(2)}, u32[]{:S(2)}) collective-permute-start(bf16[32,2176]{1,0:T(8,128)(2,1)S(1)} %get-tuple-element.14.refs_7_.refs_4_), channel_id=1, source_target_pairs={{0,8},{4,12},{8,0},{12,4},{1,9},{5,13},{9,1},{13,5},{2,10},{6,14},... | collective-permute-start | bytes 417800 | tf_op jit(solution)/shard_map/ppermute | solution.py:66
  9.5 2.1 %collective-permute-done.refs_1_.refs_8_.refs_5_ = bf16[32,2176]{1,0:T(8,128)(2,1)S(1)} collective-permute-done((bf16[32,2176]{1,0:T(8,128)(2,1)S(1)}, bf16[32,2176]{1,0:T(8,128)(2,1)S(1)}, u32[]{:S(2)}, u32[]{:S(2)}) %collective-permute-start) | collective-permute-done | bytes 139296 | tf_op jit(solution)/shard_map/ppermute | solution.py:66
  11.6 8.0 %collective-permute-done.2.refs_3_.refs_9_.refs_6_ = bf16[32,2176]{1,0:T(8,128)(2,1)S(1)} collective-permute-done((bf16[32,2176]{1,0:T(8,128)(2,1)S(1)}, bf16[32,2176]{1,0:T(8,128)(2,1)S(1)}, u32[]{:S(2)}, u32[]{:S(2)}) %collective-permute-start.2) | collective-permute-done | bytes 139296 | tf_op jit(solution)/shard_map/ppermute | solution.py:66
  21.2 1.9 %copy-done.1 = bf16[1,4096,384]{2,1,0:T(8,128)(2,1)S(1)} copy-done((bf16[1,4096,384]{2,1,0:T(8,128)(2,1)S(1)}, bf16[1,4096,384]{2,1,0:T(8,128)(2,1)}, u32[]{:S(2)}) %copy-start.1) | copy-done | bytes 3145752
  23.1 1.9 %copy-done.3 = bf16[1,4096,384]{2,1,0:T(8,128)(2,1)S(1)} copy-done((bf16[1,4096,384]{2,1,0:T(8,128)(2,1)S(1)}, bf16[1,4096,384]{2,1,0:T(8,128)(2,1)}, u32[]{:S(2)}) %copy-start.3) | copy-done | bytes 3145752
  25.0 3.5 %front.2.hidden_ref = bf16[128,384]{1,0:T(8,128)(2,1)S(1)} custom-call(s32[3]{0:T(128)S(1)} %pad_add_fusion.place, bf16[32,4096]{1,0:T(8,128)(2,1)S(1)} %copy-done.5, bf16[32,2176]{1,0:T(8,128)(2,1)S(1)} %collective-permute-done.refs_1_.refs_8_.refs_5_, bf16[32,2176]{1,0:T(8,128)(2,1)S(1)} %collective-permute-done.1.refs_2_, ...), custom_call_target="tpu_custom_call" | custom-call | flops 805306368 | bytes 6291456 | tf_op jit(solution)/shard_map/front/pallas_call | solution.py:172
  32.7 1.6 %collective-permute-start.8 = (bf16[128,1024]{1,0:T(8,128)(2,1)S(1)}, bf16[128,1024]{1,0:T(8,128)(2,1)S(1)}, u32[]{:S(2)}, u32[]{:S(2)}) collective-permute-start(bf16[128,1024]{1,0:T(8,128)(2,1)S(1)} %down.11), channel_id=1, source_target_pairs={{0,2},{1,3},{2,0},{3,1},{4,6},{5,7},{6,4},{7,5},{8,10},{9,11},{10,... | collective-permute-start | bytes 786440 | tf_op jit(solution)/shard_map/ppermute | solution.py:66
  35.4 5.8 %collective-permute-done.8.came_ref = bf16[128,1024]{1,0:T(8,128)(2,1)S(1)} collective-permute-done((bf16[128,1024]{1,0:T(8,128)(2,1)S(1)}, bf16[128,1024]{1,0:T(8,128)(2,1)S(1)}, u32[]{:S(2)}, u32[]{:S(2)}) %collective-permute-start.8) | collective-permute-done | bytes 262176 | tf_op jit(solution)/shard_map/ppermute | solution.py:66
  41.3 2.8 %collective-permute-start.10 = (bf16[32,1024]{1,0:T(8,128)(2,1)S(1)}, bf16[32,1024]{1,0:T(8,128)(2,1)S(1)}, u32[]{:S(2)}, u32[]{:S(2)}) collective-permute-start(bf16[32,1024]{1,0:T(8,128)(2,1)S(1)} %get-tuple-element.17), channel_id=1, source_target_pairs={{0,8},{4,12},{8,0},{12,4},{1,9},{5,13},{9,1},{13,5},{2,10},{6,14},... | collective-permute-start | bytes 196616 | tf_op jit(solution)/shard_map/ppermute | solution.py:66
  45.5 3.4 %collective-permute-done.10.refs_1_ = bf16[32,1024]{1,0:T(8,128)(2,1)S(1)} collective-permute-done((bf16[32,1024]{1,0:T(8,128)(2,1)S(1)}, bf16[32,1024]{1,0:T(8,128)(2,1)S(1)}, u32[]{:S(2)}, u32[]{:S(2)}) %collective-permute-start.10) | collective-permute-done | bytes 65568 | tf_op jit(solution)/shard_map/ppermute | solution.py:66
  51.3 2.4 %collective-permute-start.13 = (bf16[32,1024]{1,0:T(8,128)(2,1)S(1)}, bf16[32,1024]{1,0:T(8,128)(2,1)S(1)}, u32[]{:S(2)}, u32[]{:S(2)}) collective-permute-start(bf16[32,1024]{1,0:T(8,128)(2,1)S(1)} %get-tuple-element.19.own_ref), channel_id=1, source_target_pairs={{0,8},{4,12},{8,0},{12,4},{1,9},{5,13},{9,1},{13,5},{2,10},{6,14},... | collective-permute-start | bytes 196616 | tf_op jit(solution)/shard_map/ppermute | solution.py:66
  53.7 1.8 %collective-permute-start.14 = (bf16[32,1024]{1,0:T(8,128)(2,1)S(1)}, bf16[32,1024]{1,0:T(8,128)(2,1)S(1)}, u32[]{:S(2)}, u32[]{:S(2)}) collective-permute-start(bf16[32,1024]{1,0:T(8,128)(2,1)S(1)} %get-tuple-element.19.own_ref), channel_id=1, source_target_pairs={{0,12},{4,8},{8,4},{12,0},{1,13},{5,9},{9,5},{13,1},{2,14},{6,10},... | collective-permute-start | bytes 196616 | tf_op jit(solution)/shard_map/ppermute | solution.py:66
  55.5 2.3 %collective-permute-done.13 = bf16[32,1024]{1,0:T(8,128)(2,1)S(1)} collective-permute-done((bf16[32,1024]{1,0:T(8,128)(2,1)S(1)}, bf16[32,1024]{1,0:T(8,128)(2,1)S(1)}, u32[]{:S(2)}, u32[]{:S(2)}) %collective-permute-start.13) | collective-permute-done | bytes 65568 | tf_op jit(solution)/shard_map/ppermute | solution.py:66
  57.9 1.9 %collective-permute-done.14 = bf16[32,1024]{1,0:T(8,128)(2,1)S(1)} collective-permute-done((bf16[32,1024]{1,0:T(8,128)(2,1)S(1)}, bf16[32,1024]{1,0:T(8,128)(2,1)S(1)}, u32[]{:S(2)}, u32[]{:S(2)}) %collective-permute-start.14) | collective-permute-done | bytes 65568 | tf_op jit(solution)/shard_map/ppermute | solution.py:66
  59.8 1.5 %collective-permute-start.15 = (bf16[128,1024]{1,0:T(8,128)(2,1)S(1)}, bf16[128,1024]{1,0:T(8,128)(2,1)S(1)}, u32[]{:S(2)}, u32[]{:S(2)}) collective-permute-start(bf16[128,1024]{1,0:T(8,128)(2,1)S(1)} %constant_dynamic-update-slice_fusion.refs_0_), channel_id=1, source_target_pairs={{0,2},{1,3},{2,0},{3,1},{4,6},{5,7},{6,4},{7,5},{8,10},{9,11},{10,... | collective-permute-start | bytes 786440 | tf_op jit(solution)/shard_map/ppermute | solution.py:66
  61.3 4.9 %collective-permute-done.15.refs_1_ = bf16[128,1024]{1,0:T(8,128)(2,1)S(1)} collective-permute-done((bf16[128,1024]{1,0:T(8,128)(2,1)S(1)}, bf16[128,1024]{1,0:T(8,128)(2,1)S(1)}, u32[]{:S(2)}, u32[]{:S(2)}) %collective-permute-start.15) | collective-permute-done | bytes 262176 | tf_op jit(solution)/shard_map/ppermute | solution.py:66
  66.2 1.5 %collective-permute-done.17.refs_3_ = bf16[128,1024]{1,0:T(8,128)(2,1)S(1)} collective-permute-done((bf16[128,1024]{1,0:T(8,128)(2,1)S(1)}, bf16[128,1024]{1,0:T(8,128)(2,1)S(1)}, u32[]{:S(2)}, u32[]{:S(2)}) %collective-permute-start.17) | collective-permute-done | bytes 262176 | tf_op jit(solution)/shard_map/ppermute | solution.py:66
  67.7 3.7 %front.3.hidden_ref = bf16[128,384]{1,0:T(8,128)(2,1)S(1)} custom-call(s32[3]{0:T(128)S(1)} %pad_add_fusion.place, bf16[128,1024]{1,0:T(8,128)(2,1)S(1)} %constant_dynamic-update-slice_fusion.refs_0_, bf16[128,1024]{1,0:T(8,128)(2,1)S(1)} %collective-permute-done.15.refs_1_, bf16[128,1024]{1,0:T(8,128)(2,1)S(1)} %collective-permute-done.16.refs_2_, ...), custom_call_target="tpu_custom_call" | custom-call | flops 805306368 | bytes 6291456 | tf_op jit(solution)/shard_map/front/pallas_call | solution.py:172
  75.6 1.6 %collective-permute-start.20 = (bf16[128,1024]{1,0:T(8,128)(2,1)S(1)}, bf16[128,1024]{1,0:T(8,128)(2,1)S(1)}, u32[]{:S(2)}, u32[]{:S(2)}) collective-permute-start(bf16[128,1024]{1,0:T(8,128)(2,1)S(1)} %down.15), channel_id=1, source_target_pairs={{0,2},{1,3},{2,0},{3,1},{4,6},{5,7},{6,4},{7,5},{8,10},{9,11},{10,... | collective-permute-start | bytes 786440 | tf_op jit(solution)/shard_map/ppermute | solution.py:66
  78.3 5.7 %collective-permute-done.20.came_ref = bf16[128,1024]{1,0:T(8,128)(2,1)S(1)} collective-permute-done((bf16[128,1024]{1,0:T(8,128)(2,1)S(1)}, bf16[128,1024]{1,0:T(8,128)(2,1)S(1)}, u32[]{:S(2)}, u32[]{:S(2)}) %collective-permute-start.20) | collective-permute-done | bytes 262176 | tf_op jit(solution)/shard_map/ppermute | solution.py:66
  84.1 2.4 %collective-permute-start.22 = (bf16[32,1024]{1,0:T(8,128)(2,1)S(1)}, bf16[32,1024]{1,0:T(8,128)(2,1)S(1)}, u32[]{:S(2)}, u32[]{:S(2)}) collective-permute-start(bf16[32,1024]{1,0:T(8,128)(2,1)S(1)} %get-tuple-element.22), channel_id=1, source_target_pairs={{0,8},{4,12},{8,0},{12,4},{1,9},{5,13},{9,1},{13,5},{2,10},{6,14},... | collective-permute-start | bytes 196616 | tf_op jit(solution)/shard_map/ppermute | solution.py:66
  86.5 2.0 %collective-permute-start.23 = (bf16[32,1024]{1,0:T(8,128)(2,1)S(1)}, bf16[32,1024]{1,0:T(8,128)(2,1)S(1)}, u32[]{:S(2)}, u32[]{:S(2)}) collective-permute-start(bf16[32,1024]{1,0:T(8,128)(2,1)S(1)} %get-tuple-element.23), channel_id=1, source_target_pairs={{0,12},{4,8},{8,4},{12,0},{1,13},{5,9},{9,5},{13,1},{2,14},{6,10},... | collective-permute-start | bytes 196616 | tf_op jit(solution)/shard_map/ppermute | solution.py:66
  88.5 2.7 %collective-permute-done.22.refs_1_ = bf16[32,1024]{1,0:T(8,128)(2,1)S(1)} collective-permute-done((bf16[32,1024]{1,0:T(8,128)(2,1)S(1)}, bf16[32,1024]{1,0:T(8,128)(2,1)S(1)}, u32[]{:S(2)}, u32[]{:S(2)}) %collective-permute-start.22) | collective-permute-done | bytes 65568 | tf_op jit(solution)/shard_map/ppermute | solution.py:66
  (59 shorter events, 21.4 us)
Async XLA Ops:
  3.1 8.5 %collective-permute-start = (bf16[32,2176]{1,0:T(8,128)(2,1)S(1)}, bf16[32,2176]{1,0:T(8,128)(2,1)S(1)}, u32[]{:S(2)}, u32[]{:S(2)}) collective-permute-start(bf16[32,2176]{1,0:T(8,128)(2,1)S(1)} %get-tuple-element.14.refs_7_.refs_4_), channel_id=1, source_target_pairs={{0,4},{4,0},{8,12},{12,8},{1,5},{5,1},{9,13},{13,9},{2,6},{6,2},{1... | collective-permute-start | bytes 417800 | tf_op jit(solution)/shard_map/ppermute | solution.py:66
  6.2 13.5 %collective-permute-start.2 = (bf16[32,2176]{1,0:T(8,128)(2,1)S(1)}, bf16[32,2176]{1,0:T(8,128)(2,1)S(1)}, u32[]{:S(2)}, u32[]{:S(2)}) collective-permute-start(bf16[32,2176]{1,0:T(8,128)(2,1)S(1)} %get-tuple-element.14.refs_7_.refs_4_), channel_id=1, source_target_pairs={{0,8},{4,12},{8,0},{12,4},{1,9},{5,13},{9,1},{13,5},{2,10},{6,14},... | collective-permute-start | bytes 417800 | tf_op jit(solution)/shard_map/ppermute | solution.py:66
  8.7 10.9 %collective-permute-start.4 = (bf16[32,2176]{1,0:T(8,128)(2,1)S(1)}, bf16[32,2176]{1,0:T(8,128)(2,1)S(1)}, u32[]{:S(2)}, u32[]{:S(2)}) collective-permute-start(bf16[32,2176]{1,0:T(8,128)(2,1)S(1)} %get-tuple-element.14.refs_7_.refs_4_), channel_id=1, source_target_pairs={{0,12},{4,8},{8,4},{12,0},{1,13},{5,9},{9,5},{13,1},{2,14},{6,10},... | collective-permute-start | bytes 417800 | tf_op jit(solution)/shard_map/ppermute | solution.py:66
  11.6 9.4 %collective-permute-start.1 = (bf16[32,2176]{1,0:T(8,128)(2,1)S(1)}, bf16[32,2176]{1,0:T(8,128)(2,1)S(1)}, u32[]{:S(2)}, u32[]{:S(2)}) collective-permute-start(bf16[32,2176]{1,0:T(8,128)(2,1)S(1)} %collective-permute-done.refs_1_.refs_8_.refs_5_), channel_id=1, source_target_pairs={{0,1},{1,0},{2,3},{3,2},{4,5},{5,4},{6,7},{7,6},{8,9},{9,8},{10,11... | collective-permute-start | bytes 417800 | tf_op jit(solution)/shard_map/ppermute | solution.py:66
  19.6 1.4 %collective-permute-start.3 = (bf16[32,2176]{1,0:T(8,128)(2,1)S(1)}, bf16[32,2176]{1,0:T(8,128)(2,1)S(1)}, u32[]{:S(2)}, u32[]{:S(2)}) collective-permute-start(bf16[32,2176]{1,0:T(8,128)(2,1)S(1)} %collective-permute-done.2.refs_3_.refs_9_.refs_6_), channel_id=1, source_target_pairs={{0,1},{1,0},{2,3},{3,2},{4,5},{5,4},{6,7},{7,6},{8,9},{9,8},{10,11... | collective-permute-start | bytes 417800 | tf_op jit(solution)/shard_map/ppermute | solution.py:66
  19.6 1.6 %collective-permute-start.5 = (bf16[32,2176]{1,0:T(8,128)(2,1)S(1)}, bf16[32,2176]{1,0:T(8,128)(2,1)S(1)}, u32[]{:S(2)}, u32[]{:S(2)}) collective-permute-start(bf16[32,2176]{1,0:T(8,128)(2,1)S(1)} %collective-permute-done.4.refs_5_.refs_10_.refs_7_), channel_id=1, source_target_pairs={{0,1},{1,0},{2,3},{3,2},{4,5},{5,4},{6,7},{7,6},{8,9},{9,8},{10,11... | collective-permute-start | bytes 417800 | tf_op jit(solution)/shard_map/ppermute | solution.py:66
  29.7 1.8 %collective-permute-start.7 = (bf16[128,1024]{1,0:T(8,128)(2,1)S(1)}, bf16[128,1024]{1,0:T(8,128)(2,1)S(1)}, u32[]{:S(2)}, u32[]{:S(2)}) collective-permute-start(bf16[128,1024]{1,0:T(8,128)(2,1)S(1)} %down.10), channel_id=1, source_target_pairs={{0,1},{1,0},{2,3},{3,2},{4,5},{5,4},{6,7},{7,6},{8,9},{9,8},{10,11... | collective-permute-start | bytes 786440 | tf_op jit(solution)/shard_map/ppermute | solution.py:66
  31.2 3.0 %collective-permute-start.6 = (bf16[128,1024]{1,0:T(8,128)(2,1)S(1)}, bf16[128,1024]{1,0:T(8,128)(2,1)S(1)}, u32[]{:S(2)}, u32[]{:S(2)}) collective-permute-start(bf16[128,1024]{1,0:T(8,128)(2,1)S(1)} %down.8), channel_id=1, source_target_pairs={{0,1},{1,0},{2,3},{3,2},{4,5},{5,4},{6,7},{7,6},{8,9},{9,8},{10,11... | collective-permute-start | bytes 786440 | tf_op jit(solution)/shard_map/ppermute | solution.py:66
  32.7 8.6 %collective-permute-start.8 = (bf16[128,1024]{1,0:T(8,128)(2,1)S(1)}, bf16[128,1024]{1,0:T(8,128)(2,1)S(1)}, u32[]{:S(2)}, u32[]{:S(2)}) collective-permute-start(bf16[128,1024]{1,0:T(8,128)(2,1)S(1)} %down.11), channel_id=1, source_target_pairs={{0,2},{1,3},{2,0},{3,1},{4,6},{5,7},{6,4},{7,5},{8,10},{9,11},{10,... | collective-permute-start | bytes 786440 | tf_op jit(solution)/shard_map/ppermute | solution.py:66
  41.3 7.6 %collective-permute-start.10 = (bf16[32,1024]{1,0:T(8,128)(2,1)S(1)}, bf16[32,1024]{1,0:T(8,128)(2,1)S(1)}, u32[]{:S(2)}, u32[]{:S(2)}) collective-permute-start(bf16[32,1024]{1,0:T(8,128)(2,1)S(1)} %get-tuple-element.17), channel_id=1, source_target_pairs={{0,8},{4,12},{8,0},{12,4},{1,9},{5,13},{9,1},{13,5},{2,10},{6,14},... | collective-permute-start | bytes 196616 | tf_op jit(solution)/shard_map/ppermute | solution.py:66
  44.2 6.2 %collective-permute-start.11 = (bf16[32,1024]{1,0:T(8,128)(2,1)S(1)}, bf16[32,1024]{1,0:T(8,128)(2,1)S(1)}, u32[]{:S(2)}, u32[]{:S(2)}) collective-permute-start(bf16[32,1024]{1,0:T(8,128)(2,1)S(1)} %get-tuple-element.18), channel_id=1, source_target_pairs={{0,12},{4,8},{8,4},{12,0},{1,13},{5,9},{9,5},{13,1},{2,14},{6,10},... | collective-permute-start | bytes 196616 | tf_op jit(solution)/shard_map/ppermute | solution.py:66
  45.5 5.0 %collective-permute-start.9 = (bf16[32,1024]{1,0:T(8,128)(2,1)S(1)}, bf16[32,1024]{1,0:T(8,128)(2,1)S(1)}, u32[]{:S(2)}, u32[]{:S(2)}) collective-permute-start(bf16[32,1024]{1,0:T(8,128)(2,1)S(1)} %get-tuple-element.16), channel_id=1, source_target_pairs={{0,4},{4,0},{8,12},{12,8},{1,5},{5,1},{9,13},{13,9},{2,6},{6,2},{1... | collective-permute-start | bytes 196616 | tf_op jit(solution)/shard_map/ppermute | solution.py:66
  51.1 4.4 %collective-permute-start.12 = (bf16[32,1024]{1,0:T(8,128)(2,1)S(1)}, bf16[32,1024]{1,0:T(8,128)(2,1)S(1)}, u32[]{:S(2)}, u32[]{:S(2)}) collective-permute-start(bf16[32,1024]{1,0:T(8,128)(2,1)S(1)} %get-tuple-element.19.own_ref), channel_id=1, source_target_pairs={{0,4},{4,0},{8,12},{12,8},{1,5},{5,1},{9,13},{13,9},{2,6},{6,2},{1... | collective-permute-start | bytes 196616 | tf_op jit(solution)/shard_map/ppermute | solution.py:66
  51.3 6.6 %collective-permute-start.13 = (bf16[32,1024]{1,0:T(8,128)(2,1)S(1)}, bf16[32,1024]{1,0:T(8,128)(2,1)S(1)}, u32[]{:S(2)}, u32[]{:S(2)}) collective-permute-start(bf16[32,1024]{1,0:T(8,128)(2,1)S(1)} %get-tuple-element.19.own_ref), channel_id=1, source_target_pairs={{0,8},{4,12},{8,0},{12,4},{1,9},{5,13},{9,1},{13,5},{2,10},{6,14},... | collective-permute-start | bytes 196616 | tf_op jit(solution)/shard_map/ppermute | solution.py:66
  53.7 6.1 %collective-permute-start.14 = (bf16[32,1024]{1,0:T(8,128)(2,1)S(1)}, bf16[32,1024]{1,0:T(8,128)(2,1)S(1)}, u32[]{:S(2)}, u32[]{:S(2)}) collective-permute-start(bf16[32,1024]{1,0:T(8,128)(2,1)S(1)} %get-tuple-element.19.own_ref), channel_id=1, source_target_pairs={{0,12},{4,8},{8,4},{12,0},{1,13},{5,9},{9,5},{13,1},{2,14},{6,10},... | collective-permute-start | bytes 196616 | tf_op jit(solution)/shard_map/ppermute | solution.py:66
  59.8 6.4 %collective-permute-start.15 = (bf16[128,1024]{1,0:T(8,128)(2,1)S(1)}, bf16[128,1024]{1,0:T(8,128)(2,1)S(1)}, u32[]{:S(2)}, u32[]{:S(2)}) collective-permute-start(bf16[128,1024]{1,0:T(8,128)(2,1)S(1)} %constant_dynamic-update-slice_fusion.refs_0_), channel_id=1, source_target_pairs={{0,2},{1,3},{2,0},{3,1},{4,6},{5,7},{6,4},{7,5},{8,10},{9,11},{10,... | collective-permute-start | bytes 786440 | tf_op jit(solution)/shard_map/ppermute | solution.py:66
  61.3 4.9 %collective-permute-start.16 = (bf16[128,1024]{1,0:T(8,128)(2,1)S(1)}, bf16[128,1024]{1,0:T(8,128)(2,1)S(1)}, u32[]{:S(2)}, u32[]{:S(2)}) collective-permute-start(bf16[128,1024]{1,0:T(8,128)(2,1)S(1)} %constant_dynamic-update-slice_fusion.refs_0_), channel_id=1, source_target_pairs={{0,1},{1,0},{2,3},{3,2},{4,5},{5,4},{6,7},{7,6},{8,9},{9,8},{10,11... | collective-permute-start | bytes 786440 | tf_op jit(solution)/shard_map/ppermute | solution.py:66
  66.2 1.5 %collective-permute-start.17 = (bf16[128,1024]{1,0:T(8,128)(2,1)S(1)}, bf16[128,1024]{1,0:T(8,128)(2,1)S(1)}, u32[]{:S(2)}, u32[]{:S(2)}) collective-permute-start(bf16[128,1024]{1,0:T(8,128)(2,1)S(1)} %collective-permute-done.15.refs_1_), channel_id=1, source_target_pairs={{0,1},{1,0},{2,3},{3,2},{4,5},{5,4},{6,7},{7,6},{8,9},{9,8},{10,11... | collective-permute-start | bytes 786440 | tf_op jit(solution)/shard_map/ppermute | solution.py:66
  72.6 1.8 %collective-permute-start.19 = (bf16[128,1024]{1,0:T(8,128)(2,1)S(1)}, bf16[128,1024]{1,0:T(8,128)(2,1)S(1)}, u32[]{:S(2)}, u32[]{:S(2)}) collective-permute-start(bf16[128,1024]{1,0:T(8,128)(2,1)S(1)} %down.14), channel_id=1, source_target_pairs={{0,1},{1,0},{2,3},{3,2},{4,5},{5,4},{6,7},{7,6},{8,9},{9,8},{10,11... | collective-permute-start | bytes 786440 | tf_op jit(solution)/shard_map/ppermute | solution.py:66
  73.9 3.2 %collective-permute-start.18 = (bf16[128,1024]{1,0:T(8,128)(2,1)S(1)}, bf16[128,1024]{1,0:T(8,128)(2,1)S(1)}, u32[]{:S(2)}, u32[]{:S(2)}) collective-permute-start(bf16[128,1024]{1,0:T(8,128)(2,1)S(1)} %down.12), channel_id=1, source_target_pairs={{0,1},{1,0},{2,3},{3,2},{4,5},{5,4},{6,7},{7,6},{8,9},{9,8},{10,11... | collective-permute-start | bytes 786440 | tf_op jit(solution)/shard_map/ppermute | solution.py:66
  75.6 8.4 %collective-permute-start.20 = (bf16[128,1024]{1,0:T(8,128)(2,1)S(1)}, bf16[128,1024]{1,0:T(8,128)(2,1)S(1)}, u32[]{:S(2)}, u32[]{:S(2)}) collective-permute-start(bf16[128,1024]{1,0:T(8,128)(2,1)S(1)} %down.15), channel_id=1, source_target_pairs={{0,2},{1,3},{2,0},{3,1},{4,6},{5,7},{6,4},{7,5},{8,10},{9,11},{10,... | collective-permute-start | bytes 786440 | tf_op jit(solution)/shard_map/ppermute | solution.py:66
  84.0 4.5 %collective-permute-start.21 = (bf16[32,1024]{1,0:T(8,128)(2,1)S(1)}, bf16[32,1024]{1,0:T(8,128)(2,1)S(1)}, u32[]{:S(2)}, u32[]{:S(2)}) collective-permute-start(bf16[32,1024]{1,0:T(8,128)(2,1)S(1)} %get-tuple-element.21), channel_id=1, source_target_pairs={{0,4},{4,0},{8,12},{12,8},{1,5},{5,1},{9,13},{13,9},{2,6},{6,2},{1... | collective-permute-start | bytes 196616 | tf_op jit(solution)/shard_map/ppermute | solution.py:66
  84.1 7.1 %collective-permute-start.22 = (bf16[32,1024]{1,0:T(8,128)(2,1)S(1)}, bf16[32,1024]{1,0:T(8,128)(2,1)S(1)}, u32[]{:S(2)}, u32[]{:S(2)}) collective-permute-start(bf16[32,1024]{1,0:T(8,128)(2,1)S(1)} %get-tuple-element.22), channel_id=1, source_target_pairs={{0,8},{4,12},{8,0},{12,4},{1,9},{5,13},{9,1},{13,5},{2,10},{6,14},... | collective-permute-start | bytes 196616 | tf_op jit(solution)/shard_map/ppermute | solution.py:66
  86.5 6.1 %collective-permute-start.23 = (bf16[32,1024]{1,0:T(8,128)(2,1)S(1)}, bf16[32,1024]{1,0:T(8,128)(2,1)S(1)}, u32[]{:S(2)}, u32[]{:S(2)}) collective-permute-start(bf16[32,1024]{1,0:T(8,128)(2,1)S(1)} %get-tuple-element.23), channel_id=1, source_target_pairs={{0,12},{4,8},{8,4},{12,0},{1,13},{5,9},{9,5},{13,1},{2,14},{6,10},... | collective-permute-start | bytes 196616 | tf_op jit(solution)/shard_map/ppermute | solution.py:66
  (6 other events, 79.5 us)

commit v3 on v0

v3 whole, which is shorter than its diff:
```python
import functools

import jax
import jax.numpy as jnp
from jax import lax
from jax.experimental import pallas as pl
from jax.experimental.pallas import tpu as pltpu
from jax.sharding import PartitionSpec as P


def normalize(x, mod):
    xf = x.astype(jnp.float32)
    scaled = xf * lax.rsqrt(jnp.mean(xf * xf, axis=-1, keepdims=True) + 1e-06)
    return (scaled * (1.0 + mod[0]) + mod[1]).astype(jnp.bfloat16)


def routed_section(x_full, x_cols, mod, ids, router, gate_weight, up_weight, down_weight):
    tok_rows = x_full.shape[0]
    width = x_full.shape[1]
    experts = router.shape[1]
    picks = ids.shape[1]
    n_peers = lax.axis_size("ep")
    quarter = width // lax.axis_size("et")
    slot_count = 3 * tok_rows * picks // (2 * experts)
    normed = normalize(x_full, mod)
    logits = jnp.dot(normed, router, preferred_element_type=jnp.float32)
    chosen = jax.nn.sigmoid(jnp.take_along_axis(logits, ids, axis=1))
    weight = chosen / jnp.sum(chosen, axis=1, keepdims=True)
    flat_e = ids.reshape(-1)
    onehot = (flat_e[:, None] == jnp.arange(experts, dtype=jnp.int32)).astype(jnp.int32)
    counted = jnp.cumsum(onehot, axis=0)
    slot = jnp.sum(onehot * (counted - 1), axis=1)
    repeated = jnp.repeat(normed, picks, axis=0)
    outbox = jnp.zeros((experts, slot_count, width), jnp.bfloat16).at[flat_e, slot].set(repeated)
    arrived = lax.all_to_all(outbox, "ep", split_axis=0, concat_axis=0, tiled=True)
    in_rows = arrived.reshape(n_peers * slot_count, width)
    gate = jnp.dot(in_rows, gate_weight[0], preferred_element_type=jnp.float32)
    upper = jnp.dot(in_rows, up_weight[0], preferred_element_type=jnp.float32)
    hidden = (jax.nn.silu(gate) * upper).astype(jnp.bfloat16)
    partial_out = jnp.dot(hidden, down_weight[0], preferred_element_type=jnp.float32)
    summed = lax.psum_scatter(
        partial_out.astype(jnp.bfloat16), "et", scatter_dimension=1, tiled=True
    )
    returned = lax.all_to_all(
        summed.reshape(n_peers, slot_count, quarter), "ep", split_axis=0, concat_axis=0, tiled=True
    )
    picked = returned[flat_e, slot].astype(jnp.float32).reshape(tok_rows, picks, quarter)
    velocity = jnp.sum(picked * weight[:, :, None], axis=1)
    moved = (x_cols.astype(jnp.float32) - 0.5 * velocity).astype(jnp.bfloat16)
    return (moved, velocity)


def routed_body(tokens, modulation, router, gate_weight, up_weight, down_weight, expert_ids):
    quarter = tokens.shape[1] // lax.axis_size("et")
    column_start = lax.axis_index("et") * quarter
    cols = lax.dynamic_slice_in_dim(tokens, column_start, quarter, 1)
    weights = (router, gate_weight, up_weight, down_weight)
    first, _ = routed_section(tokens, cols, modulation[0], expert_ids[0], *weights)
    full = lax.all_gather(first, "et", axis=1, tiled=True)
    second, velocity = routed_section(full, first, modulation[1], expert_ids[1], *weights)
    return (second, velocity.astype(jnp.bfloat16))


def swap(x, axis, bit):
    size = lax.axis_size(axis)
    return lax.ppermute(x, axis, [(i, i ^ bit) for i in range(size)])


LANES = 128
VMEM_LIMIT = 32 * 1024 * 1024
VMEM = pl.BlockSpec(memory_space=pltpu.VMEM)
SMEM = pl.BlockSpec(memory_space=pltpu.SMEM)
ANY = pl.BlockSpec(memory_space=pl.ANY)


def params():
    return pltpu.CompilerParams(vmem_limit_bytes=VMEM_LIMIT)


def aligned(index, size):
    return pl.ds(pl.multiple_of(index * size, size), size)


def load_kernel(gate_ref, up_ref, down_ref, pair_ref, out_ref, sems):
    hidden = gate_ref.shape[2]
    copies = [
        pltpu.make_async_copy(gate_ref.at[0], pair_ref.at[:, :hidden], sems.at[0]),
        pltpu.make_async_copy(up_ref.at[0], pair_ref.at[:, hidden:], sems.at[1]),
        pltpu.make_async_copy(down_ref.at[0], out_ref, sems.at[2]),
    ]
    for copy in copies:
        copy.start()
    for copy in copies:
        copy.wait()


def load(gate, up, down):
    _, width, hidden = gate.shape
    return pl.pallas_call(
        load_kernel,
        in_specs=[ANY] * 3,
        out_specs=[VMEM] * 2,
        out_shape=[
            pltpu.VMEM((width, 2 * hidden), jnp.bfloat16),
            pltpu.VMEM((hidden, width), jnp.bfloat16),
        ],
        scratch_shapes=[pltpu.SemaphoreType.DMA((3,))],
        compiler_params=params(),
        cost_estimate=pl.CostEstimate(flops=0, bytes_accessed=12 * width * hidden, transcendentals=0),
        name="load",
    )(gate, up, down)


def pack_kernel(experts, place, tokens_ref, ids_ref, out_ref, own_ref):
    quarter = tokens_ref.shape[1] // 4
    own = tokens_ref[:, aligned(place[0], quarter)]
    own_ref[...] = own
    out_ref[:, :quarter] = own
    lane = lax.broadcasted_iota(jnp.int32, (tokens_ref.shape[0], LANES), 1)
    flags = jnp.zeros(lane.shape, jnp.float32)
    for s in range(ids_ref.shape[0]):
        for k in range(ids_ref.shape[2]):
            flags += jnp.where(ids_ref[s][:, k : k + 1] + s * experts == lane, 1.0, 0.0)
    out_ref[:, quarter:] = flags.astype(jnp.bfloat16)


def pack(place, tokens, ids, experts):
    rows, width = tokens.shape
    shapes = [(rows, width // 4 + LANES), (rows, width // 4)]
    return pl.pallas_call(
        functools.partial(pack_kernel, experts),
        in_specs=[SMEM, VMEM, VMEM],
        out_shape=[jax.ShapeDtypeStruct(s, jnp.bfloat16) for s in shapes],
        compiler_params=params(),
        name="pack",
    )(place, tokens, ids)


def front_kernel(pieces, section, experts, n_flags, place, *refs):
    n = len(pieces)
    x_refs, flag_refs = refs[:n], refs[n : n + n_flags]
    mod_ref, router_ref, pair_ref, out_ref, normed_ref = refs[n + n_flags :]
    width = normed_ref.shape[1]
    hidden = out_ref.shape[1]
    for row in sorted({piece[0] for piece in pieces}):
        members = [i for i in range(n) if pieces[i][0] == row]
        rows = pieces[members[0]][1]
        total = jnp.zeros((rows, 1), jnp.float32)
        for i in members:
            xf = x_refs[i][:, : pieces[i][2]].astype(jnp.float32)
            total += jnp.sum(xf * xf, axis=1, keepdims=True)
        scale = lax.rsqrt(total / width + 1e-06)
        for i in members:
            cols = pieces[i][2]
            where = aligned(place[0] ^ pieces[i][3], cols) if cols < width else slice(None)
            xf = x_refs[i][:, :cols].astype(jnp.float32)
            normed_ref[row : row + rows, where] = (
                xf * scale * (1.0 + mod_ref[section, 0:1, where]) + mod_ref[section, 1:2, where]
            ).astype(jnp.bfloat16)
    normed = normed_ref[...]
    both = jnp.dot(normed, pair_ref[...], preferred_element_type=jnp.float32)
    logits = lax.dot_general(
        normed, router_ref[...], (((1,), (1,)), ((), ())), preferred_element_type=jnp.float32
    )
    count = logits.shape[1]
    lane = lax.broadcasted_iota(jnp.int32, logits.shape, 1)
    flags = jnp.concatenate([f[:, f.shape[1] - LANES :] for f in flag_refs], axis=0).astype(jnp.float32)
    flags = flags[:, section * experts : section * experts + count]
    chosen = jnp.where(flags > 0.5, jax.nn.sigmoid(logits), 0.0)
    mine = jnp.where(lane == place[1], chosen, 0.0)
    weight = jnp.sum(mine, axis=1, keepdims=True) / jnp.sum(chosen, axis=1, keepdims=True)
    gate, upper = both[:, :hidden], both[:, hidden:]
    out_ref[...] = (gate / (1.0 + jnp.exp(-gate)) * upper * weight).astype(jnp.bfloat16)


def front(place, xs, pieces, flags, section, mod, router, pair):
    width, hidden = pair.shape[0], pair.shape[1] // 2
    rows = sum(f.shape[0] for f in flags)
    experts = router.shape[0]
    return pl.pallas_call(
        functools.partial(front_kernel, pieces, section, experts, len(flags)),
        in_specs=[SMEM] + [VMEM] * (len(xs) + len(flags) + 3),
        scratch_shapes=[pltpu.VMEM((rows, width), jnp.bfloat16)],
        out_shape=jax.ShapeDtypeStruct((rows, hidden), jnp.bfloat16),
        compiler_params=params(),
        cost_estimate=pl.CostEstimate(
            flops=4 * rows * width * hidden, bytes_accessed=4 * width * hidden, transcendentals=0
        ),
        name="front",
    )(place, *xs, *flags, mod, router, pair)


def down_kernel(flip, n_adds, place, hidden_ref, down_ref, *refs):
    adds, outs = refs[:n_adds], refs[n_adds:]
    quarter = outs[0].shape[1]
    weights = down_ref[:, aligned(place[0] ^ flip, quarter)]
    product = jnp.dot(hidden_ref[...], weights, preferred_element_type=jnp.float32)
    for ref in adds:
        product += ref[...].astype(jnp.float32)
    rows = outs[0].shape[0]
    for k, out in enumerate(outs):
        out[...] = product[k * rows : (k + 1) * rows].astype(out.dtype)


def down(place, hidden, w_down, flip, blocks, adds=(), dtype=jnp.bfloat16):
    units, width = w_down.shape
    rows, quarter = hidden.shape[0], width // 4
    return pl.pallas_call(
        functools.partial(down_kernel, flip, len(adds)),
        in_specs=[SMEM] + [VMEM] * (2 + len(adds)),
        out_shape=[jax.ShapeDtypeStruct((rows // blocks, quarter), dtype)] * blocks,
        compiler_params=params(),
        cost_estimate=pl.CostEstimate(
            flops=2 * rows * units * quarter, bytes_accessed=2 * units * quarter, transcendentals=0
        ),
        name="down",
    )(place, hidden, w_down, *adds)


def add_kernel(keep_ref, came_ref, out_ref):
    out_ref[...] = (keep_ref[...] + came_ref[...].astype(jnp.float32)).astype(out_ref.dtype)


def add(keep, came):
    return pl.pallas_call(
        add_kernel,
        out_shape=jax.ShapeDtypeStruct(keep.shape, jnp.bfloat16),
        compiler_params=params(),
        name="add",
    )(keep, came)


def move_kernel(own_ref, total_ref, *refs):
    came, (next_ref, velocity_ref) = refs[:-2], refs[-2:]
    velocity = total_ref[...]
    for ref in came:
        velocity += ref[...].astype(jnp.float32)
    next_ref[...] = (own_ref[...].astype(jnp.float32) - 0.5 * velocity).astype(jnp.bfloat16)
    velocity_ref[...] = velocity.astype(jnp.bfloat16)


def move(own, total, came):
    return pl.pallas_call(
        move_kernel,
        out_shape=[jax.ShapeDtypeStruct(own.shape, jnp.bfloat16)] * 2,
        compiler_params=params(),
        name="move",
    )(own, total, *came)


def sum_back(place, hidden, w_down, own):
    peers = lax.axis_size("ep")
    far = swap(down(place, hidden, w_down, 3, 1)[0], "et", 1)
    near = swap(down(place, hidden, w_down, 1, 1)[0], "et", 1)
    parts = down(place, hidden, w_down, 2, peers, (far,))
    came = {k: swap(parts[k], "et", 2) for k in reversed(range(peers))}
    keep = down(place, hidden, w_down, 0, peers, (near,), jnp.float32)
    sent = [swap(add(keep[k], came[k]), "ep", k) for k in reversed(range(1, peers))]
    return move(own, keep[0], [came[0], *sent])


def gather(own):
    found = []
    for k in range(lax.axis_size("ep")):
        block = swap(own, "ep", k) if k else own
        side = swap(block, "et", 2)
        found.append([block, side, swap(block, "et", 1), swap(side, "et", 1)])
    return found


FLIPS = (0, 2, 1, 3)


def dense_body(tokens, modulation, router, gate_weight, up_weight, down_weight, expert_ids):
    rows, width = tokens.shape
    quarter = width // 4
    router = router.T
    place = jnp.stack([lax.axis_index("et"), lax.axis_index("ep")]).astype(jnp.int32)

    packed, own = pack(place, tokens, expert_ids, router.shape[0])
    found = gather(packed)
    flags = [blocks[0] for blocks in found]
    xs = [tokens] + sum(found[1:], [])
    pieces = [(0, rows, width, 0)]
    pieces += [(k * rows, rows, quarter, f) for k in range(1, len(found)) for f in FLIPS]
    pair, w_down = load(gate_weight, up_weight, down_weight)
    hidden = front(place, xs, pieces, flags, 0, modulation, router, pair)
    own, _ = sum_back(place, hidden, w_down, own)

    found = gather(own)
    pieces = [(k * rows, rows, quarter, f) for k in range(len(found)) for f in FLIPS]
    hidden = front(place, sum(found, []), pieces, flags, 1, modulation, router, pair)
    return tuple(sum_back(place, hidden, w_down, own))


def solution(mesh):
    in_specs = (
        P(("grp", "ep"), None),
        P(),
        P(),
        P("ep", None, "et"),
        P("ep", None, "et"),
        P("ep", "et", None),
        P(None, ("grp", "ep"), None),
    )
    out_specs = (P(("grp", "ep"), "et"), P(("grp", "ep"), "et"))

    def body(*args):
        experts, picks = args[2].shape[1], args[6].shape[2]
        peers = lax.axis_size("ep")
        fits = lax.axis_size("et") == 4 and peers & (peers - 1) == 0
        chosen = dense_body if fits and experts <= 2 * picks else routed_body
        return chosen(*args)

    return jax.shard_map(body, mesh=mesh, in_specs=in_specs, out_specs=out_specs, check_vma=False)
```

time: 214 us -> 83 us (0.39)
  blocking collectives: 56.6 us -> 0 us
  local copies, waits for them, and re-layouts: 55.3 us -> 7.4 us
  waiting for transfers between devices: 53.6 us -> 20.6 us
  starting transfers between devices: 9.24 us -> 38.8 us
  matrix products: 16.3 us -> 0 us
  Pallas kernels: 0 us -> 14.9 us
  between operations: 14.3 us -> 0.89 us
  other arithmetic: 7.53 us -> 0.07 us
    all_to_all x2 -> x0, blocking collectives: 50.8 us -> none  [one_section(): lax.all_to_all(outbox, 'ep', split_axis=0, concat_axis=0, tiled=True)]
    ppermute x0 -> x45, starting transfers between devices: none -> 38.8 us  [swap(): return lax.ppermute(x, axis, [(i, i ^ bit) for i in range(size)])]
    reduce_scatter x2 -> x0, waiting for transfers between devices: 38.8 us -> none  [one_section(): lax.psum_scatter(partial_out.astype(jnp.bfloat16), 'et', scatter_dimensio...]
    scatter x2 -> x0, local copies, waits for them, and re-layouts: 34.7 us -> none  [one_section(): jnp.zeros((experts, slot_count, width), jnp.bfloat16).at[flat_e, slot]]
    ppermute x0 -> x45, waiting for transfers between devices: none -> 20.6 us  [swap(): return lax.ppermute(x, axis, [(i, i ^ bit) for i in range(size)])]
    dot_general x6 -> x0, matrix products: 16.3 us -> none  [the longest x2 8.96 us: one_section(): jnp.dot(hidden, down_weight[0], preferred_element_type=jnp.float32)]
    pallas_call x0 -> x20, Pallas kernels: none -> 14.9 us  [the longest x8 6.88 us: down(): pl.pallas_call(functools.partial(down_kernel, flip, len(adds)), in_specs=...]
    all_to_all x2 -> x0, waiting for transfers between devices: 14.7 us -> none  [one_section(): lax.all_to_all(summed.reshape(n_peers, slot_count, quarter), 'ep', split_...]
  transfers between devices with their start and end apart: 4 -> 45, of which waited for: 4 -> 20; matrix products, arithmetic and copies ran while one was open for 3% -> 0% of each run, Pallas kernels for 0% -> 7%
where the time goes in v3:
time: 83 us; the launch traced here: 82.7 us
  starting transfers between devices  38.8 us (47%)
  waiting for transfers between devices  20.6 us (25%)
  Pallas kernels  14.9 us (18%)
  local copies, waits for them, and re-layouts  7.4 us (9%)
  between operations  0.89 us (1%)
    ppermute x45, starting transfers between devices, swap(): return lax.ppermute(x, axis, [(i, i ^ bit) for i in range(size)])  38.8 us
    ppermute x45, waiting for transfers between devices, swap(): return lax.ppermute(x, axis, [(i, i ^ bit) for i in range(size)])  20.6 us
    unnamed x15, local copies, waits for them, and re-layouts  7.4 us
    pallas_call x8, Pallas kernels, down(): pl.pallas_call(functools.partial(down_kernel, flip, len(adds)), in_specs=...  6.88 us
    pallas_call x2, Pallas kernels, front(): pl.pallas_call(functools.partial(front_kernel, pieces, section, experts,...  5.01 us
  transfers between devices with their start and end apart: 45, of which 20 were waited for; matrix products, arithmetic and copies ran while one was open for 0% of the time, Pallas kernels for 7%

profile of v3, /device:TPU:0, one launch (start us, length us, event | category | flops | bytes accessed | tf_op | source)
XLA Modules:
  0.0 82.7 jit_solution(7757654736799753949)
XLA Ops:
  3.1 5.1 %collective-permute-start.8 = (bf16[32,1152]{1,0:T(8,128)(2,1)S(1)}, bf16[32,1152]{1,0:T(8,128)(2,1)S(1)}, u32[]{:S(2)}, u32[]{:S(2)}) collective-permute-start(bf16[32,1152]{1,0:T(8,128)(2,1)S(1)} %get-tuple-element.24.refs_13_.refs_16_), channel_id=1, source_target_pairs={{0,12},{4,8},{8,4},{12,0},{1,13},{5,9},{9,5},{13,1},{2,14},{6,10},... | collective-permute-start | bytes 221192 | tf_op jit(solution)/shard_map/ppermute | solution.py:66
  8.8 2.5 %collective-permute-done.8.refs_9_.refs_16_.refs_19_ = bf16[32,1152]{1,0:T(8,128)(2,1)S(1)} collective-permute-done((bf16[32,1152]{1,0:T(8,128)(2,1)S(1)}, bf16[32,1152]{1,0:T(8,128)(2,1)S(1)}, u32[]{:S(2)}, u32[]{:S(2)}) %collective-permute-start.8) | collective-permute-done | bytes 73760 | tf_op jit(solution)/shard_map/ppermute | solution.py:66
  11.3 1.5 %collective-permute-start.9 = (bf16[32,1152]{1,0:T(8,128)(2,1)S(1)}, bf16[32,1152]{1,0:T(8,128)(2,1)S(1)}, u32[]{:S(2)}, u32[]{:S(2)}) collective-permute-start(bf16[32,1152]{1,0:T(8,128)(2,1)S(1)} %collective-permute-done.8.refs_9_.refs_16_.refs_19_), channel_id=1, source_target_pairs={{0,2},{1,3},{2,0},{3,1},{4,6},{5,7},{6,4},{7,5},{8,10},{9,11},{10,... | collective-permute-start | bytes 221192 | tf_op jit(solution)/shard_map/ppermute | solution.py:66
  13.2 1.6 %collective-permute-start.1 = (bf16[32,1152]{1,0:T(8,128)(2,1)S(1)}, bf16[32,1152]{1,0:T(8,128)(2,1)S(1)}, u32[]{:S(2)}, u32[]{:S(2)}) collective-permute-start(bf16[32,1152]{1,0:T(8,128)(2,1)S(1)} %collective-permute-done.refs_1_.refs_14_.refs_17_), channel_id=1, source_target_pairs={{0,2},{1,3},{2,0},{3,1},{4,6},{5,7},{6,4},{7,5},{8,10},{9,11},{10,... | collective-permute-start | bytes 221192 | tf_op jit(solution)/shard_map/ppermute | solution.py:66
  16.2 2.2 %collective-permute-done.1.refs_2_ = bf16[32,1152]{1,0:T(8,128)(2,1)S(1)} collective-permute-done((bf16[32,1152]{1,0:T(8,128)(2,1)S(1)}, bf16[32,1152]{1,0:T(8,128)(2,1)S(1)}, u32[]{:S(2)}, u32[]{:S(2)}) %collective-permute-start.1) | collective-permute-done | bytes 73760 | tf_op jit(solution)/shard_map/ppermute | solution.py:66
  19.7 1.9 %copy-done = bf16[1,4096,384]{2,1,0:T(8,128)(2,1)S(1)} copy-done((bf16[1,4096,384]{2,1,0:T(8,128)(2,1)S(1)}, bf16[1,4096,384]{2,1,0:T(8,128)(2,1)}, u32[]{:S(2)}) %copy-start) | copy-done | bytes 3145752
  21.6 1.9 %copy-done.1 = bf16[1,4096,384]{2,1,0:T(8,128)(2,1)S(1)} copy-done((bf16[1,4096,384]{2,1,0:T(8,128)(2,1)S(1)}, bf16[1,4096,384]{2,1,0:T(8,128)(2,1)}, u32[]{:S(2)}) %copy-start.1) | copy-done | bytes 3145752
  23.5 1.9 %copy-done.2 = bf16[1,384,4096]{2,1,0:T(8,128)(2,1)S(1)} copy-done((bf16[1,384,4096]{2,1,0:T(8,128)(2,1)S(1)}, bf16[1,384,4096]{2,1,0:T(8,128)(2,1)}, u32[]{:S(2)}) %copy-start.2) | copy-done | bytes 3145752
  26.4 2.5 %front.2.hidden_ref = bf16[128,384]{1,0:T(8,128)(2,1)S(1)} custom-call(s32[2]{0:T(128)S(1)} %pad_add_fusion.place, bf16[32,4096]{1,0:T(8,128)(2,1)S(1)} %copy-done.4, bf16[32,1152]{1,0:T(8,128)(2,1)S(1)} %collective-permute-done.refs_1_.refs_14_.refs_17_, bf16[32,1152]{1,0:T(8,128)(2,1)S(1)} %collective-permute-done.1.refs_2_, ...), custom_call_target="tpu_custom_call" | custom-call | flops 805306368 | bytes 6291456 | tf_op jit(solution)/shard_map/front/pallas_call | solution.py:180
  37.2 1.2 %collective-permute-start.20 = (bf16[32,1024]{1,0:T(8,128)(2,1)S(1)}, bf16[32,1024]{1,0:T(8,128)(2,1)S(1)}, u32[]{:S(2)}, u32[]{:S(2)}) collective-permute-start(bf16[32,1024]{1,0:T(8,128)(2,1)S(1)} %add.10), channel_id=1, source_target_pairs={{0,4},{4,0},{8,12},{12,8},{1,5},{5,1},{9,13},{13,9},{2,6},{6,2},{1... | collective-permute-start | bytes 196616 | tf_op jit(solution)/shard_map/ppermute | solution.py:66
  38.6 1.9 %collective-permute-start.18 = (bf16[32,1024]{1,0:T(8,128)(2,1)S(1)}, bf16[32,1024]{1,0:T(8,128)(2,1)S(1)}, u32[]{:S(2)}, u32[]{:S(2)}) collective-permute-start(bf16[32,1024]{1,0:T(8,128)(2,1)S(1)} %add.9), channel_id=1, source_target_pairs={{0,8},{4,12},{8,0},{12,4},{1,9},{5,13},{9,1},{13,5},{2,10},{6,14},... | collective-permute-start | bytes 196616 | tf_op jit(solution)/shard_map/ppermute | solution.py:66
  40.5 2.0 %collective-permute-start.16 = (bf16[32,1024]{1,0:T(8,128)(2,1)S(1)}, bf16[32,1024]{1,0:T(8,128)(2,1)S(1)}, u32[]{:S(2)}, u32[]{:S(2)}) collective-permute-start(bf16[32,1024]{1,0:T(8,128)(2,1)S(1)} %add.8), channel_id=1, source_target_pairs={{0,12},{4,8},{8,4},{12,0},{1,13},{5,9},{9,5},{13,1},{2,14},{6,10},... | collective-permute-start | bytes 196616 | tf_op jit(solution)/shard_map/ppermute | solution.py:66
  42.6 2.8 %collective-permute-done.18.refs_2_ = bf16[32,1024]{1,0:T(8,128)(2,1)S(1)} collective-permute-done((bf16[32,1024]{1,0:T(8,128)(2,1)S(1)}, bf16[32,1024]{1,0:T(8,128)(2,1)S(1)}, u32[]{:S(2)}, u32[]{:S(2)}) %collective-permute-start.18) | collective-permute-done | bytes 65568 | tf_op jit(solution)/shard_map/ppermute | solution.py:66
  45.3 1.4 %collective-permute-done.16.refs_1_ = bf16[32,1024]{1,0:T(8,128)(2,1)S(1)} collective-permute-done((bf16[32,1024]{1,0:T(8,128)(2,1)S(1)}, bf16[32,1024]{1,0:T(8,128)(2,1)S(1)}, u32[]{:S(2)}, u32[]{:S(2)}) %collective-permute-start.16) | collective-permute-done | bytes 65568 | tf_op jit(solution)/shard_map/ppermute | solution.py:66
  47.4 2.6 %collective-permute-start.28 = (bf16[32,1024]{1,0:T(8,128)(2,1)S(1)}, bf16[32,1024]{1,0:T(8,128)(2,1)S(1)}, u32[]{:S(2)}, u32[]{:S(2)}) collective-permute-start(bf16[32,1024]{1,0:T(8,128)(2,1)S(1)} %get-tuple-element.35.refs_0_.own_ref), channel_id=1, source_target_pairs={{0,8},{4,12},{8,0},{12,4},{1,9},{5,13},{9,1},{13,5},{2,10},{6,14},... | collective-permute-start | bytes 196616 | tf_op jit(solution)/shard_map/ppermute | solution.py:66
  50.0 1.8 %collective-permute-start.32 = (bf16[32,1024]{1,0:T(8,128)(2,1)S(1)}, bf16[32,1024]{1,0:T(8,128)(2,1)S(1)}, u32[]{:S(2)}, u32[]{:S(2)}) collective-permute-start(bf16[32,1024]{1,0:T(8,128)(2,1)S(1)} %get-tuple-element.35.refs_0_.own_ref), channel_id=1, source_target_pairs={{0,12},{4,8},{8,4},{12,0},{1,13},{5,9},{9,5},{13,1},{2,14},{6,10},... | collective-permute-start | bytes 196616 | tf_op jit(solution)/shard_map/ppermute | solution.py:66
  56.0 1.3 %collective-permute-start.33 = (bf16[32,1024]{1,0:T(8,128)(2,1)S(1)}, bf16[32,1024]{1,0:T(8,128)(2,1)S(1)}, u32[]{:S(2)}, u32[]{:S(2)}) collective-permute-start(bf16[32,1024]{1,0:T(8,128)(2,1)S(1)} %collective-permute-done.32.refs_12_), channel_id=1, source_target_pairs={{0,2},{1,3},{2,0},{3,1},{4,6},{5,7},{6,4},{7,5},{8,10},{9,11},{10,... | collective-permute-start | bytes 196616 | tf_op jit(solution)/shard_map/ppermute | solution.py:66
  57.9 1.4 %collective-permute-done.29.refs_9_ = bf16[32,1024]{1,0:T(8,128)(2,1)S(1)} collective-permute-done((bf16[32,1024]{1,0:T(8,128)(2,1)S(1)}, bf16[32,1024]{1,0:T(8,128)(2,1)S(1)}, u32[]{:S(2)}, u32[]{:S(2)}) %collective-permute-start.29) | collective-permute-done | bytes 65568 | tf_op jit(solution)/shard_map/ppermute | solution.py:66
  62.1 2.5 %front.3.hidden_ref = bf16[128,384]{1,0:T(8,128)(2,1)S(1)} custom-call(s32[2]{0:T(128)S(1)} %pad_add_fusion.place, bf16[32,1024]{1,0:T(8,128)(2,1)S(1)} %get-tuple-element.35.refs_0_.own_ref, bf16[32,1024]{1,0:T(8,128)(2,1)S(1)} %collective-permute-done.21.refs_1_, bf16[32,1024]{1,0:T(8,128)(2,1)S(1)} %collective-permute-done.22.refs_2_, ...), custom_call_target="tpu_custom_call" | custom-call | flops 805306368 | bytes 6291456 | tf_op jit(solution)/shard_map/front/pallas_call | solution.py:180
  67.9 1.3 %collective-permute-start.43 = (bf16[32,1024]{1,0:T(8,128)(2,1)S(1)}, bf16[32,1024]{1,0:T(8,128)(2,1)S(1)}, u32[]{:S(2)}, u32[]{:S(2)}) collective-permute-start(bf16[32,1024]{1,0:T(8,128)(2,1)S(1)} %get-tuple-element.43), channel_id=1, source_target_pairs={{0,2},{1,3},{2,0},{3,1},{4,6},{5,7},{6,4},{7,5},{8,10},{9,11},{10,... | collective-permute-start | bytes 196616 | tf_op jit(solution)/shard_map/ppermute | solution.py:66
  70.0 1.3 %collective-permute-start.39 = (bf16[32,1024]{1,0:T(8,128)(2,1)S(1)}, bf16[32,1024]{1,0:T(8,128)(2,1)S(1)}, u32[]{:S(2)}, u32[]{:S(2)}) collective-permute-start(bf16[32,1024]{1,0:T(8,128)(2,1)S(1)} %get-tuple-element.39), channel_id=1, source_target_pairs={{0,2},{1,3},{2,0},{3,1},{4,6},{5,7},{6,4},{7,5},{8,10},{9,11},{10,... | collective-permute-start | bytes 196616 | tf_op jit(solution)/shard_map/ppermute | solution.py:66
  74.3 1.5 %collective-permute-start.42 = (bf16[32,1024]{1,0:T(8,128)(2,1)S(1)}, bf16[32,1024]{1,0:T(8,128)(2,1)S(1)}, u32[]{:S(2)}, u32[]{:S(2)}) collective-permute-start(bf16[32,1024]{1,0:T(8,128)(2,1)S(1)} %add.12), channel_id=1, source_target_pairs={{0,8},{4,12},{8,0},{12,4},{1,9},{5,13},{9,1},{13,5},{2,10},{6,14},... | collective-permute-start | bytes 196616 | tf_op jit(solution)/shard_map/ppermute | solution.py:66
  75.8 2.1 %collective-permute-start.40 = (bf16[32,1024]{1,0:T(8,128)(2,1)S(1)}, bf16[32,1024]{1,0:T(8,128)(2,1)S(1)}, u32[]{:S(2)}, u32[]{:S(2)}) collective-permute-start(bf16[32,1024]{1,0:T(8,128)(2,1)S(1)} %add.11), channel_id=1, source_target_pairs={{0,12},{4,8},{8,4},{12,0},{1,13},{5,9},{9,5},{13,1},{2,14},{6,10},... | collective-permute-start | bytes 196616 | tf_op jit(solution)/shard_map/ppermute | solution.py:66
  77.9 3.1 %collective-permute-done.42.refs_2_ = bf16[32,1024]{1,0:T(8,128)(2,1)S(1)} collective-permute-done((bf16[32,1024]{1,0:T(8,128)(2,1)S(1)}, bf16[32,1024]{1,0:T(8,128)(2,1)S(1)}, u32[]{:S(2)}, u32[]{:S(2)}) %collective-permute-start.42) | collective-permute-done | bytes 65568 | tf_op jit(solution)/shard_map/ppermute | solution.py:66
  (102 shorter events, 32.6 us)
Async XLA Ops:
  3.1 8.3 %collective-permute-start.8 = (bf16[32,1152]{1,0:T(8,128)(2,1)S(1)}, bf16[32,1152]{1,0:T(8,128)(2,1)S(1)}, u32[]{:S(2)}, u32[]{:S(2)}) collective-permute-start(bf16[32,1152]{1,0:T(8,128)(2,1)S(1)} %get-tuple-element.24.refs_13_.refs_16_), channel_id=1, source_target_pairs={{0,12},{4,8},{8,4},{12,0},{1,13},{5,9},{9,5},{13,1},{2,14},{6,10},... | collective-permute-start | bytes 221192 | tf_op jit(solution)/shard_map/ppermute | solution.py:66
  8.2 6.7 %collective-permute-start.4 = (bf16[32,1152]{1,0:T(8,128)(2,1)S(1)}, bf16[32,1152]{1,0:T(8,128)(2,1)S(1)}, u32[]{:S(2)}, u32[]{:S(2)}) collective-permute-start(bf16[32,1152]{1,0:T(8,128)(2,1)S(1)} %get-tuple-element.24.refs_13_.refs_16_), channel_id=1, source_target_pairs={{0,8},{4,12},{8,0},{12,4},{1,9},{5,13},{9,1},{13,5},{2,10},{6,14},... | collective-permute-start | bytes 221192 | tf_op jit(solution)/shard_map/ppermute | solution.py:66
  15.6 10.7 %collective-permute-start.2 = (bf16[32,1152]{1,0:T(8,128)(2,1)S(1)}, bf16[32,1152]{1,0:T(8,128)(2,1)S(1)}, u32[]{:S(2)}, u32[]{:S(2)}) collective-permute-start(bf16[32,1152]{1,0:T(8,128)(2,1)S(1)} %collective-permute-done.refs_1_.refs_14_.refs_17_), channel_id=1, source_target_pairs={{0,1},{1,0},{2,3},{3,2},{4,5},{5,4},{6,7},{7,6},{8,9},{9,8},{10,11... | collective-permute-start | bytes 221192 | tf_op jit(solution)/shard_map/ppermute | solution.py:66
  16.2 10.1 %collective-permute-start.6 = (bf16[32,1152]{1,0:T(8,128)(2,1)S(1)}, bf16[32,1152]{1,0:T(8,128)(2,1)S(1)}, u32[]{:S(2)}, u32[]{:S(2)}) collective-permute-start(bf16[32,1152]{1,0:T(8,128)(2,1)S(1)} %collective-permute-done.4.refs_5_.refs_15_.refs_18_), channel_id=1, source_target_pairs={{0,1},{1,0},{2,3},{3,2},{4,5},{5,4},{6,7},{7,6},{8,9},{9,8},{10,11... | collective-permute-start | bytes 221192 | tf_op jit(solution)/shard_map/ppermute | solution.py:66
  18.4 8.0 %collective-permute-start.11 = (bf16[32,1152]{1,0:T(8,128)(2,1)S(1)}, bf16[32,1152]{1,0:T(8,128)(2,1)S(1)}, u32[]{:S(2)}, u32[]{:S(2)}) collective-permute-start(bf16[32,1152]{1,0:T(8,128)(2,1)S(1)} %collective-permute-done.9.refs_10_), channel_id=1, source_target_pairs={{0,1},{1,0},{2,3},{3,2},{4,5},{5,4},{6,7},{7,6},{8,9},{9,8},{10,11... | collective-permute-start | bytes 221192 | tf_op jit(solution)/shard_map/ppermute | solution.py:66
  19.2 7.1 %collective-permute-start.3 = (bf16[32,1152]{1,0:T(8,128)(2,1)S(1)}, bf16[32,1152]{1,0:T(8,128)(2,1)S(1)}, u32[]{:S(2)}, u32[]{:S(2)}) collective-permute-start(bf16[32,1152]{1,0:T(8,128)(2,1)S(1)} %collective-permute-done.1.refs_2_), channel_id=1, source_target_pairs={{0,1},{1,0},{2,3},{3,2},{4,5},{5,4},{6,7},{7,6},{8,9},{9,8},{10,11... | collective-permute-start | bytes 221192 | tf_op jit(solution)/shard_map/ppermute | solution.py:66
  19.2 7.1 %collective-permute-start.7 = (bf16[32,1152]{1,0:T(8,128)(2,1)S(1)}, bf16[32,1152]{1,0:T(8,128)(2,1)S(1)}, u32[]{:S(2)}, u32[]{:S(2)}) collective-permute-start(bf16[32,1152]{1,0:T(8,128)(2,1)S(1)} %collective-permute-done.5.refs_6_), channel_id=1, source_target_pairs={{0,1},{1,0},{2,3},{3,2},{4,5},{5,4},{6,7},{7,6},{8,9},{9,8},{10,11... | collective-permute-start | bytes 221192 | tf_op jit(solution)/shard_map/ppermute | solution.py:66
  30.7 5.7 %collective-permute-start.12 = (bf16[128,1024]{1,0:T(8,128)(2,1)S(1)}, bf16[128,1024]{1,0:T(8,128)(2,1)S(1)}, u32[]{:S(2)}, u32[]{:S(2)}) collective-permute-start(bf16[128,1024]{1,0:T(8,128)(2,1)S(1)} %down.8), channel_id=1, source_target_pairs={{0,1},{1,0},{2,3},{3,2},{4,5},{5,4},{6,7},{7,6},{8,9},{9,8},{10,11... | collective-permute-start | bytes 786440 | tf_op jit(solution)/shard_map/ppermute | solution.py:66
  33.4 5.2 %collective-permute-start.17 = (bf16[32,1024]{1,0:T(8,128)(2,1)S(1)}, bf16[32,1024]{1,0:T(8,128)(2,1)S(1)}, u32[]{:S(2)}, u32[]{:S(2)}) collective-permute-start(bf16[32,1024]{1,0:T(8,128)(2,1)S(1)} %get-tuple-element.32), channel_id=1, source_target_pairs={{0,2},{1,3},{2,0},{3,1},{4,6},{5,7},{6,4},{7,5},{8,10},{9,11},{10,... | collective-permute-start | bytes 196616 | tf_op jit(solution)/shard_map/ppermute | solution.py:66
  34.3 6.2 %collective-permute-start.15 = (bf16[32,1024]{1,0:T(8,128)(2,1)S(1)}, bf16[32,1024]{1,0:T(8,128)(2,1)S(1)}, u32[]{:S(2)}, u32[]{:S(2)}) collective-permute-start(bf16[32,1024]{1,0:T(8,128)(2,1)S(1)} %get-tuple-element.30), channel_id=1, source_target_pairs={{0,2},{1,3},{2,0},{3,1},{4,6},{5,7},{6,4},{7,5},{8,10},{9,11},{10,... | collective-permute-start | bytes 196616 | tf_op jit(solution)/shard_map/ppermute | solution.py:66
  35.4 7.1 %collective-permute-start.14 = (bf16[32,1024]{1,0:T(8,128)(2,1)S(1)}, bf16[32,1024]{1,0:T(8,128)(2,1)S(1)}, u32[]{:S(2)}, u32[]{:S(2)}) collective-permute-start(bf16[32,1024]{1,0:T(8,128)(2,1)S(1)} %get-tuple-element.28), channel_id=1, source_target_pairs={{0,2},{1,3},{2,0},{3,1},{4,6},{5,7},{6,4},{7,5},{8,10},{9,11},{10,... | collective-permute-start | bytes 196616 | tf_op jit(solution)/shard_map/ppermute | solution.py:66
  37.2 5.3 %collective-permute-start.20 = (bf16[32,1024]{1,0:T(8,128)(2,1)S(1)}, bf16[32,1024]{1,0:T(8,128)(2,1)S(1)}, u32[]{:S(2)}, u32[]{:S(2)}) collective-permute-start(bf16[32,1024]{1,0:T(8,128)(2,1)S(1)} %add.10), channel_id=1, source_target_pairs={{0,4},{4,0},{8,12},{12,8},{1,5},{5,1},{9,13},{13,9},{2,6},{6,2},{1... | collective-permute-start | bytes 196616 | tf_op jit(solution)/shard_map/ppermute | solution.py:66
  38.6 6.7 %collective-permute-start.18 = (bf16[32,1024]{1,0:T(8,128)(2,1)S(1)}, bf16[32,1024]{1,0:T(8,128)(2,1)S(1)}, u32[]{:S(2)}, u32[]{:S(2)}) collective-permute-start(bf16[32,1024]{1,0:T(8,128)(2,1)S(1)} %add.9), channel_id=1, source_target_pairs={{0,8},{4,12},{8,0},{12,4},{1,9},{5,13},{9,1},{13,5},{2,10},{6,14},... | collective-permute-start | bytes 196616 | tf_op jit(solution)/shard_map/ppermute | solution.py:66
  40.5 6.2 %collective-permute-start.16 = (bf16[32,1024]{1,0:T(8,128)(2,1)S(1)}, bf16[32,1024]{1,0:T(8,128)(2,1)S(1)}, u32[]{:S(2)}, u32[]{:S(2)}) collective-permute-start(bf16[32,1024]{1,0:T(8,128)(2,1)S(1)} %add.8), channel_id=1, source_target_pairs={{0,12},{4,8},{8,4},{12,0},{1,13},{5,9},{9,5},{13,1},{2,14},{6,10},... | collective-permute-start | bytes 196616 | tf_op jit(solution)/shard_map/ppermute | solution.py:66
  47.4 5.6 %collective-permute-start.24 = (bf16[32,1024]{1,0:T(8,128)(2,1)S(1)}, bf16[32,1024]{1,0:T(8,128)(2,1)S(1)}, u32[]{:S(2)}, u32[]{:S(2)}) collective-permute-start(bf16[32,1024]{1,0:T(8,128)(2,1)S(1)} %get-tuple-element.35.refs_0_.own_ref), channel_id=1, source_target_pairs={{0,4},{4,0},{8,12},{12,8},{1,5},{5,1},{9,13},{13,9},{2,6},{6,2},{1... | collective-permute-start | bytes 196616 | tf_op jit(solution)/shard_map/ppermute | solution.py:66
  47.4 6.4 %collective-permute-start.28 = (bf16[32,1024]{1,0:T(8,128)(2,1)S(1)}, bf16[32,1024]{1,0:T(8,128)(2,1)S(1)}, u32[]{:S(2)}, u32[]{:S(2)}) collective-permute-start(bf16[32,1024]{1,0:T(8,128)(2,1)S(1)} %get-tuple-element.35.refs_0_.own_ref), channel_id=1, source_target_pairs={{0,8},{4,12},{8,0},{12,4},{1,9},{5,13},{9,1},{13,5},{2,10},{6,14},... | collective-permute-start | bytes 196616 | tf_op jit(solution)/shard_map/ppermute | solution.py:66
  50.0 6.1 %collective-permute-start.32 = (bf16[32,1024]{1,0:T(8,128)(2,1)S(1)}, bf16[32,1024]{1,0:T(8,128)(2,1)S(1)}, u32[]{:S(2)}, u32[]{:S(2)}) collective-permute-start(bf16[32,1024]{1,0:T(8,128)(2,1)S(1)} %get-tuple-element.35.refs_0_.own_ref), channel_id=1, source_target_pairs={{0,12},{4,8},{8,4},{12,0},{1,13},{5,9},{9,5},{13,1},{2,14},{6,10},... | collective-permute-start | bytes 196616 | tf_op jit(solution)/shard_map/ppermute | solution.py:66
  51.8 5.5 %collective-permute-start.21 = (bf16[32,1024]{1,0:T(8,128)(2,1)S(1)}, bf16[32,1024]{1,0:T(8,128)(2,1)S(1)}, u32[]{:S(2)}, u32[]{:S(2)}) collective-permute-start(bf16[32,1024]{1,0:T(8,128)(2,1)S(1)} %get-tuple-element.35.refs_0_.own_ref), channel_id=1, source_target_pairs={{0,2},{1,3},{2,0},{3,1},{4,6},{5,7},{6,4},{7,5},{8,10},{9,11},{10,... | collective-permute-start | bytes 196616 | tf_op jit(solution)/shard_map/ppermute | solution.py:66
  53.8 5.5 %collective-permute-start.29 = (bf16[32,1024]{1,0:T(8,128)(2,1)S(1)}, bf16[32,1024]{1,0:T(8,128)(2,1)S(1)}, u32[]{:S(2)}, u32[]{:S(2)}) collective-permute-start(bf16[32,1024]{1,0:T(8,128)(2,1)S(1)} %collective-permute-done.28.refs_8_), channel_id=1, source_target_pairs={{0,2},{1,3},{2,0},{3,1},{4,6},{5,7},{6,4},{7,5},{8,10},{9,11},{10,... | collective-permute-start | bytes 196616 | tf_op jit(solution)/shard_map/ppermute | solution.py:66
  66.6 5.5 %collective-permute-start.36 = (bf16[128,1024]{1,0:T(8,128)(2,1)S(1)}, bf16[128,1024]{1,0:T(8,128)(2,1)S(1)}, u32[]{:S(2)}, u32[]{:S(2)}) collective-permute-start(bf16[128,1024]{1,0:T(8,128)(2,1)S(1)} %down.12), channel_id=1, source_target_pairs={{0,1},{1,0},{2,3},{3,2},{4,5},{5,4},{6,7},{7,6},{8,9},{9,8},{10,11... | collective-permute-start | bytes 786440 | tf_op jit(solution)/shard_map/ppermute | solution.py:66
  70.0 5.7 %collective-permute-start.39 = (bf16[32,1024]{1,0:T(8,128)(2,1)S(1)}, bf16[32,1024]{1,0:T(8,128)(2,1)S(1)}, u32[]{:S(2)}, u32[]{:S(2)}) collective-permute-start(bf16[32,1024]{1,0:T(8,128)(2,1)S(1)} %get-tuple-element.39), channel_id=1, source_target_pairs={{0,2},{1,3},{2,0},{3,1},{4,6},{5,7},{6,4},{7,5},{8,10},{9,11},{10,... | collective-permute-start | bytes 196616 | tf_op jit(solution)/shard_map/ppermute | solution.py:66
  71.3 6.6 %collective-permute-start.38 = (bf16[32,1024]{1,0:T(8,128)(2,1)S(1)}, bf16[32,1024]{1,0:T(8,128)(2,1)S(1)}, u32[]{:S(2)}, u32[]{:S(2)}) collective-permute-start(bf16[32,1024]{1,0:T(8,128)(2,1)S(1)} %get-tuple-element.37), channel_id=1, source_target_pairs={{0,2},{1,3},{2,0},{3,1},{4,6},{5,7},{6,4},{7,5},{8,10},{9,11},{10,... | collective-permute-start | bytes 196616 | tf_op jit(solution)/shard_map/ppermute | solution.py:66
  74.3 6.7 %collective-permute-start.42 = (bf16[32,1024]{1,0:T(8,128)(2,1)S(1)}, bf16[32,1024]{1,0:T(8,128)(2,1)S(1)}, u32[]{:S(2)}, u32[]{:S(2)}) collective-permute-start(bf16[32,1024]{1,0:T(8,128)(2,1)S(1)} %add.12), channel_id=1, source_target_pairs={{0,8},{4,12},{8,0},{12,4},{1,9},{5,13},{9,1},{13,5},{2,10},{6,14},... | collective-permute-start | bytes 196616 | tf_op jit(solution)/shard_map/ppermute | solution.py:66
  75.8 6.2 %collective-permute-start.40 = (bf16[32,1024]{1,0:T(8,128)(2,1)S(1)}, bf16[32,1024]{1,0:T(8,128)(2,1)S(1)}, u32[]{:S(2)}, u32[]{:S(2)}) collective-permute-start(bf16[32,1024]{1,0:T(8,128)(2,1)S(1)} %add.11), channel_id=1, source_target_pairs={{0,12},{4,8},{8,4},{12,0},{1,13},{5,9},{9,5},{13,1},{2,14},{6,10},... | collective-permute-start | bytes 196616 | tf_op jit(solution)/shard_map/ppermute | solution.py:66
  (28 other events, 130.1 us)

commit v4 on v3

--- a/solution.py
+++ b/solution.py
@@ -68,20 +68,21 @@
 
 LANES = 128
 VMEM_LIMIT = 32 * 1024 * 1024
+VMEM_MOST = 52 * 1024 * 1024
+VMEM_ALL = 63 * 1024 * 1024
 VMEM = pl.BlockSpec(memory_space=pltpu.VMEM)
-SMEM = pl.BlockSpec(memory_space=pltpu.SMEM)
 ANY = pl.BlockSpec(memory_space=pl.ANY)
 
 
-def params():
-    return pltpu.CompilerParams(vmem_limit_bytes=VMEM_LIMIT)
+def params(limit=VMEM_LIMIT):
+    return pltpu.CompilerParams(vmem_limit_bytes=limit)
 
 
 def aligned(index, size):
     return pl.ds(pl.multiple_of(index * size, size), size)
 
 
-def load_kernel(gate_ref, up_ref, down_ref, pair_ref, out_ref, sems):
+def load_kernel(gate_ref, up_ref, down_ref, pair_ref, out_ref, done_ref, sems):
     hidden = gate_ref.shape[2]
     copies = [
         pltpu.make_async_copy(gate_ref.at[0], pair_ref.at[:, :hidden], sems.at[0]),
@@ -92,6 +93,7 @@
         copy.start()
     for copy in copies:
         copy.wait()
+    done_ref[...] = jnp.zeros_like(done_ref)
 
 
 def load(gate, up, down):
@@ -99,44 +101,71 @@
     return pl.pallas_call(
         load_kernel,
         in_specs=[ANY] * 3,
-        out_specs=[VMEM] * 2,
+        out_specs=[VMEM] * 3,
         out_shape=[
             pltpu.VMEM((width, 2 * hidden), jnp.bfloat16),
             pltpu.VMEM((hidden, width), jnp.bfloat16),
+            pltpu.VMEM((8, LANES), jnp.float32),
         ],
         scratch_shapes=[pltpu.SemaphoreType.DMA((3,))],
-        compiler_params=params(),
+        compiler_params=params(VMEM_MOST),
         cost_estimate=pl.CostEstimate(flops=0, bytes_accessed=12 * width * hidden, transcendentals=0),
         name="load",
     )(gate, up, down)
 
 
-def pack_kernel(experts, place, tokens_ref, ids_ref, out_ref, own_ref):
-    quarter = tokens_ref.shape[1] // 4
-    own = tokens_ref[:, aligned(place[0], quarter)]
-    own_ref[...] = own
-    out_ref[:, :quarter] = own
-    lane = lax.broadcasted_iota(jnp.int32, (tokens_ref.shape[0], LANES), 1)
+def relay_kernel(block_ref, done_ref, out_ref):
+    out_ref[...] = block_ref[:, : out_ref.shape[1]]
+
+
+def relay(block, cols, done):
+    return pl.pallas_call(
+        relay_kernel,
+        out_shape=jax.ShapeDtypeStruct((block.shape[0], cols), block.dtype),
+        compiler_params=params(),
+        name="relay",
+    )(block, done)
+
+
+def pack_kernel(experts, tokens_ref, ids_ref, wide_ref, out_ref, own_ref, sems):
+    width = tokens_ref.shape[1]
+    half, quarter = width // 2, width // 4
+    where = lax.axis_index("et")
+    copies = [
+        pltpu.make_async_copy(tokens_ref.at[:, aligned(where & 1, half)], wide_ref.at[:, :half], sems.at[0]),
+        pltpu.make_async_copy(tokens_ref.at[:, aligned(where, quarter)], own_ref, sems.at[1]),
+    ]
+    for copy in copies:
+        copy.start()
+    rows = tokens_ref.shape[0]
+    lane = lax.broadcasted_iota(jnp.int32, (LANES, rows), 0)
     flags = jnp.zeros(lane.shape, jnp.float32)
     for s in range(ids_ref.shape[0]):
-        for k in range(ids_ref.shape[2]):
-            flags += jnp.where(ids_ref[s][:, k : k + 1] + s * experts == lane, 1.0, 0.0)
-    out_ref[:, quarter:] = flags.astype(jnp.bfloat16)
-
-
-def pack(place, tokens, ids, experts):
+        for k in range(ids_ref.shape[1]):
+            flags += jnp.where(ids_ref[s][k : k + 1, :] + s * experts == lane, 1.0, 0.0)
+    flags = flags.T.astype(jnp.bfloat16)
+    wide_ref[:, half:] = flags
+    out_ref[:, quarter:] = flags
+    for copy in copies:
+        copy.wait()
+    out_ref[:, :quarter] = own_ref[...]
+
+
+def pack(tokens, ids, experts):
     rows, width = tokens.shape
-    shapes = [(rows, width // 4 + LANES), (rows, width // 4)]
+    shapes = [(rows, width // 2 + LANES), (rows, width // 4 + LANES), (rows, width // 4)]
     return pl.pallas_call(
         functools.partial(pack_kernel, experts),
-        in_specs=[SMEM, VMEM, VMEM],
-        out_shape=[jax.ShapeDtypeStruct(s, jnp.bfloat16) for s in shapes],
-        compiler_params=params(),
+        in_specs=[ANY, VMEM],
+        out_specs=[VMEM] * 3,
+        out_shape=[pltpu.VMEM(s, jnp.bfloat16) for s in shapes],
+        scratch_shapes=[pltpu.SemaphoreType.DMA((2,))],
+        compiler_params=params(VMEM_ALL),
         name="pack",
-    )(place, tokens, ids)
-
-
-def front_kernel(pieces, section, experts, n_flags, place, *refs):
+    )(tokens, ids)
+
+
+def front_kernel(pieces, section, experts, n_flags, *refs):
     n = len(pieces)
     x_refs, flag_refs = refs[:n], refs[n : n + n_flags]
     mod_ref, router_ref, pair_ref, out_ref, normed_ref = refs[n + n_flags :]
@@ -152,7 +181,8 @@
         scale = lax.rsqrt(total / width + 1e-06)
         for i in members:
             cols = pieces[i][2]
-            where = aligned(place[0] ^ pieces[i][3], cols) if cols < width else slice(None)
+            place = (lax.axis_index("et") & (width // cols - 1)) ^ pieces[i][3]
+            where = aligned(place, cols) if cols < width else slice(None)
             xf = x_refs[i][:, :cols].astype(jnp.float32)
             normed_ref[row : row + rows, where] = (
                 xf * scale * (1.0 + mod_ref[section, 0:1, where]) + mod_ref[section, 1:2, where]
@@ -167,19 +197,19 @@
     flags = jnp.concatenate([f[:, f.shape[1] - LANES :] for f in flag_refs], axis=0).astype(jnp.float32)
     flags = flags[:, section * experts : section * experts + count]
     chosen = jnp.where(flags > 0.5, jax.nn.sigmoid(logits), 0.0)
-    mine = jnp.where(lane == place[1], chosen, 0.0)
+    mine = jnp.where(lane == lax.axis_index("ep"), chosen, 0.0)
     weight = jnp.sum(mine, axis=1, keepdims=True) / jnp.sum(chosen, axis=1, keepdims=True)
     gate, upper = both[:, :hidden], both[:, hidden:]
     out_ref[...] = (gate / (1.0 + jnp.exp(-gate)) * upper * weight).astype(jnp.bfloat16)
 
 
-def front(place, xs, pieces, flags, section, mod, router, pair):
+def front(xs, pieces, flags, section, mod, router, pair):
     width, hidden = pair.shape[0], pair.shape[1] // 2
     rows = sum(f.shape[0] for f in flags)
     experts = router.shape[0]
     return pl.pallas_call(
         functools.partial(front_kernel, pieces, section, experts, len(flags)),
-        in_specs=[SMEM] + [VMEM] * (len(xs) + len(flags) + 3),
+        in_specs=[VMEM] * (len(xs) + len(flags) + 3),
         scratch_shapes=[pltpu.VMEM((rows, width), jnp.bfloat16)],
         out_shape=jax.ShapeDtypeStruct((rows, hidden), jnp.bfloat16),
         compiler_params=params(),
@@ -187,13 +217,13 @@
             flops=4 * rows * width * hidden, bytes_accessed=4 * width * hidden, transcendentals=0
         ),
         name="front",
-    )(place, *xs, *flags, mod, router, pair)
-
-
-def down_kernel(flip, n_adds, place, hidden_ref, down_ref, *refs):
+    )(*xs, *flags, mod, router, pair)
+
+
+def down_kernel(flip, n_adds, hidden_ref, down_ref, *refs):
     adds, outs = refs[:n_adds], refs[n_adds:]
     quarter = outs[0].shape[1]
-    weights = down_ref[:, aligned(place[0] ^ flip, quarter)]
+    weights = down_ref[:, aligned(lax.axis_index("et") ^ flip, quarter)]
     product = jnp.dot(hidden_ref[...], weights, preferred_element_type=jnp.float32)
     for ref in adds:
         product += ref[...].astype(jnp.float32)
@@ -202,95 +232,101 @@
         out[...] = product[k * rows : (k + 1) * rows].astype(out.dtype)
 
 
-def down(place, hidden, w_down, flip, blocks, adds=(), dtype=jnp.bfloat16):
+def down(hidden, w_down, flip, blocks, adds=(), dtype=jnp.bfloat16):
     units, width = w_down.shape
     rows, quarter = hidden.shape[0], width // 4
     return pl.pallas_call(
         functools.partial(down_kernel, flip, len(adds)),
-        in_specs=[SMEM] + [VMEM] * (2 + len(adds)),
+        in_specs=[VMEM] * (2 + len(adds)),
         out_shape=[jax.ShapeDtypeStruct((rows // blocks, quarter), dtype)] * blocks,
         compiler_params=params(),
         cost_estimate=pl.CostEstimate(
             flops=2 * rows * units * quarter, bytes_accessed=2 * units * quarter, transcendentals=0
         ),
         name="down",
-    )(place, hidden, w_down, *adds)
-
-
-def add_kernel(keep_ref, came_ref, out_ref):
-    out_ref[...] = (keep_ref[...] + came_ref[...].astype(jnp.float32)).astype(out_ref.dtype)
-
-
-def add(keep, came):
+    )(hidden, w_down, *adds)
+
+
+def add_kernel(keep_ref, came_ref, *outs):
+    for k, out in enumerate(outs):
+        rows = slice(k * out.shape[0], (k + 1) * out.shape[0])
+        out[...] = (keep_ref[rows, :] + came_ref[rows, :].astype(jnp.float32)).astype(out.dtype)
+
+
+def add(keep, came, dtypes):
+    shape = (keep.shape[0] // len(dtypes), keep.shape[1])
     return pl.pallas_call(
         add_kernel,
-        out_shape=jax.ShapeDtypeStruct(keep.shape, jnp.bfloat16),
+        out_shape=[jax.ShapeDtypeStruct(shape, t) for t in dtypes],
         compiler_params=params(),
         name="add",
     )(keep, came)
 
 
-def move_kernel(own_ref, total_ref, *refs):
-    came, (next_ref, velocity_ref) = refs[:-2], refs[-2:]
+def move_kernel(n_outs, own_ref, total_ref, *refs):
+    came, outs = refs[:-n_outs], refs[-n_outs:]
     velocity = total_ref[...]
     for ref in came:
         velocity += ref[...].astype(jnp.float32)
-    next_ref[...] = (own_ref[...].astype(jnp.float32) - 0.5 * velocity).astype(jnp.bfloat16)
-    velocity_ref[...] = velocity.astype(jnp.bfloat16)
-
-
-def move(own, total, came):
-    return pl.pallas_call(
-        move_kernel,
-        out_shape=[jax.ShapeDtypeStruct(own.shape, jnp.bfloat16)] * 2,
+    outs[0][...] = (own_ref[...].astype(jnp.float32) - 0.5 * velocity).astype(jnp.bfloat16)
+    if n_outs > 1:
+        outs[1][...] = velocity.astype(jnp.bfloat16)
+
+
+def move(own, total, came, n_outs):
+    return pl.pallas_call(
+        functools.partial(move_kernel, n_outs),
+        out_shape=[jax.ShapeDtypeStruct(own.shape, jnp.bfloat16)] * n_outs,
         compiler_params=params(),
         name="move",
     )(own, total, *came)
 
 
-def sum_back(place, hidden, w_down, own):
+def sum_back(hidden, w_down, own, n_outs):
     peers = lax.axis_size("ep")
-    far = swap(down(place, hidden, w_down, 3, 1)[0], "et", 1)
-    near = swap(down(place, hidden, w_down, 1, 1)[0], "et", 1)
-    parts = down(place, hidden, w_down, 2, peers, (far,))
-    came = {k: swap(parts[k], "et", 2) for k in reversed(range(peers))}
-    keep = down(place, hidden, w_down, 0, peers, (near,), jnp.float32)
-    sent = [swap(add(keep[k], came[k]), "ep", k) for k in reversed(range(1, peers))]
-    return move(own, keep[0], [came[0], *sent])
-
-
-def gather(own):
-    found = []
-    for k in range(lax.axis_size("ep")):
-        block = swap(own, "ep", k) if k else own
-        side = swap(block, "et", 2)
-        found.append([block, side, swap(block, "et", 1), swap(side, "et", 1)])
-    return found
-
-
-FLIPS = (0, 2, 1, 3)
+    some = peers // 2
+    far = swap(down(hidden, w_down, 3, 1)[0], "et", 1)
+    near = swap(down(hidden, w_down, 1, 1)[0], "et", 1)
+    first, last = down(hidden, w_down, 2, 2, (far,))
+    last, first = swap(last, "et", 2), swap(first, "et", 2)
+    keep_first, keep_last = down(hidden, w_down, 0, 2, (near,), jnp.float32)
+    blocks = add(keep_last, last, [jnp.bfloat16] * (peers - some))
+    total, *others = add(keep_first, first, [jnp.float32] + [jnp.bfloat16] * (some - 1))
+    sent = [swap(b, "ep", k + 1) for k, b in enumerate(others + list(blocks))]
+    return move(own, total, sent, n_outs)
+
+
+QUARTERS = (0, 2, 1, 3)
+
+
+def spread(block):
+    side = swap(block, "et", 2)
+    return [block, side, swap(block, "et", 1), swap(side, "et", 1)]
 
 
 def dense_body(tokens, modulation, router, gate_weight, up_weight, down_weight, expert_ids):
     rows, width = tokens.shape
     quarter = width // 4
     router = router.T
-    place = jnp.stack([lax.axis_index("et"), lax.axis_index("ep")]).astype(jnp.int32)
-
-    packed, own = pack(place, tokens, expert_ids, router.shape[0])
-    found = gather(packed)
-    flags = [blocks[0] for blocks in found]
-    xs = [tokens] + sum(found[1:], [])
-    pieces = [(0, rows, width, 0)]
-    pieces += [(k * rows, rows, quarter, f) for k in range(1, len(found)) for f in FLIPS]
-    pair, w_down = load(gate_weight, up_weight, down_weight)
-    hidden = front(place, xs, pieces, flags, 0, modulation, router, pair)
-    own, _ = sum_back(place, hidden, w_down, own)
-
-    found = gather(own)
-    pieces = [(k * rows, rows, quarter, f) for k in range(len(found)) for f in FLIPS]
-    hidden = front(place, sum(found, []), pieces, flags, 1, modulation, router, pair)
-    return tuple(sum_back(place, hidden, w_down, own))
+    peers = lax.axis_size("ep")
+
+    wide, packed, own = pack(tokens, expert_ids.transpose(0, 2, 1), router.shape[0])
+    pair, w_down, done = load(gate_weight, up_weight, down_weight)
+    flags = [packed, swap(wide, "ep", 1)] + [swap(packed, "ep", k) for k in range(2, peers)]
+    xs = [tokens, flags[1], swap(flags[1], "et", 1)]
+    pieces = [(0, rows, width, 0), (rows, rows, width // 2, 0), (rows, rows, width // 2, 1)]
+    for k in range(2, peers):
+        xs += spread(relay(flags[k], quarter, done))
+        pieces += [(k * rows, rows, quarter, f) for f in QUARTERS]
+    hidden = front(xs, pieces, flags, 0, modulation, router, pair)
+    (own,) = sum_back(hidden, w_down, own, 1)
+
+    xs, pieces = [], []
+    for k in range(peers):
+        xs += spread(swap(own, "ep", k) if k else own)
+        pieces += [(k * rows, rows, quarter, f) for f in QUARTERS]
+    hidden = front(xs, pieces, flags, 1, modulation, router, pair)
+    return tuple(sum_back(hidden, w_down, own, 2))
 
 
 def solution(mesh):

time: 83 us -> 75.5 us (0.910)
  waiting for transfers between devices: 20.6 us -> 28.3 us
  local copies, waits for them, and re-layouts: 7.4 us -> 0.01 us
  starting transfers between devices: 38.8 us -> 33.2 us
  Pallas kernels: 14.9 us -> 13 us
    ppermute x45 -> x39, waiting for transfers between devices: 20.6 us -> 28.3 us  [swap(): return lax.ppermute(x, axis, [(i, i ^ bit) for i in range(size)])]
    unnamed x15 -> x6, local copies, waits for them, and re-layouts: 7.4 us -> 0.01 us
    ppermute x45 -> x39, starting transfers between devices: 38.8 us -> 33.2 us  [swap(): return lax.ppermute(x, axis, [(i, i ^ bit) for i in range(size)])]
    pallas_call x8, Pallas kernels: 6.88 us -> 2.47 us  [down(): pl.pallas_call(functools.partial(down_kernel, flip, len(adds)), in_specs=...]
    pallas_call x10, Pallas kernels: 2.98 us -> 6.28 us  [the longest x1 3.78 us: load(): pl.pallas_call(load_kernel, in_specs=[ANY] * 3, out_specs=[VMEM] * 3, out...]
  transfers between devices with their start and end apart: 45 -> 39, of which waited for: 20 -> 20; matrix products, arithmetic and copies ran while one was open for 0% -> 0% of each run, Pallas kernels for 7% -> 8%
where the time goes in v4:
time: 75.5 us; the launch traced here: 75.3 us
  starting transfers between devices  33.2 us (44%)
  waiting for transfers between devices  28.3 us (37%)
  Pallas kernels  13 us (17%)
  between operations  0.82 us (1%)
    ppermute x39, starting transfers between devices, swap(): return lax.ppermute(x, axis, [(i, i ^ bit) for i in range(size)])  33.2 us
    ppermute x39, waiting for transfers between devices, swap(): return lax.ppermute(x, axis, [(i, i ^ bit) for i in range(size)])  28.3 us
    pallas_call x2, Pallas kernels, front(): pl.pallas_call(functools.partial(front_kernel, pieces, section, experts,...  4.26 us
    pallas_call x1, Pallas kernels, load(): pl.pallas_call(load_kernel, in_specs=[ANY] * 3, out_specs=[VMEM] * 3, out...  3.78 us
    pallas_call x8, Pallas kernels, down(): pl.pallas_call(functools.partial(down_kernel, flip, len(adds)), in_specs=...  2.47 us
    pallas_call x1, Pallas kernels, pack(): pl.pallas_call(functools.partial(pack_kernel, experts), in_specs=[ANY, VM...  1.63 us
  transfers between devices with their start and end apart: 39, of which 20 were waited for; matrix products, arithmetic and copies ran while one was open for 0% of the time, Pallas kernels for 8%

profile of v4, /device:TPU:0, one launch (start us, length us, event | category | flops | bytes accessed | tf_op | source)
XLA Modules:
  0.0 75.3 jit_solution(10939457009295758033)
XLA Ops:
  0.6 1.6 %pack.1 = (bf16[32,2176]{1,0:T(8,128)(2,1)S(1)}, bf16[32,1152]{1,0:T(8,128)(2,1)S(1)}, bf16[32,1024]{1,0:T(8,128)(2,1)S(1)}) custom-call(bf16[32,4096]{1,0:T(8,128)(2,1)} %refs_0_.1, s32[2,2,32]{2,1,0:T(2,128)} %bitcast.4), custom_call_target="tpu_custom_call" | custom-call | tf_op jit(solution)/shard_map/pack/pallas_call | solution.py:157
  2.3 3.1 %collective-permute-start = (bf16[32,2176]{1,0:T(8,128)(2,1)S(1)}, bf16[32,2176]{1,0:T(8,128)(2,1)S(1)}, u32[]{:S(2)}, u32[]{:S(2)}) collective-permute-start(bf16[32,2176]{1,0:T(8,128)(2,1)S(1)} %get-tuple-element.25), channel_id=1, source_target_pairs={{0,4},{4,0},{8,12},{12,8},{1,5},{5,1},{9,13},{13,9},{2,6},{6,2},{1... | collective-permute-start | bytes 417800 | tf_op jit(solution)/shard_map/ppermute | solution.py:66
  5.4 2.6 %collective-permute-start.2 = (bf16[32,1152]{1,0:T(8,128)(2,1)S(1)}, bf16[32,1152]{1,0:T(8,128)(2,1)S(1)}, u32[]{:S(2)}, u32[]{:S(2)}) collective-permute-start(bf16[32,1152]{1,0:T(8,128)(2,1)S(1)} %get-tuple-element.26.refs_11_.refs_16_), channel_id=1, source_target_pairs={{0,8},{4,12},{8,0},{12,4},{1,9},{5,13},{9,1},{13,5},{2,10},{6,14},... | collective-permute-start | bytes 221192 | tf_op jit(solution)/shard_map/ppermute | solution.py:66
  8.0 1.9 %collective-permute-done.refs_1_.refs_12_.refs_17_ = bf16[32,2176]{1,0:T(8,128)(2,1)S(1)} collective-permute-done((bf16[32,2176]{1,0:T(8,128)(2,1)S(1)}, bf16[32,2176]{1,0:T(8,128)(2,1)S(1)}, u32[]{:S(2)}, u32[]{:S(2)}) %collective-permute-start) | collective-permute-done | bytes 139296 | tf_op jit(solution)/shard_map/ppermute | solution.py:66
  9.8 3.8 %load.1 = (bf16[4096,768]{1,0:T(8,128)(2,1)S(1)}, bf16[384,4096]{1,0:T(8,128)(2,1)S(1)}, f32[8,128]{1,0:T(8,128)S(1)}) custom-call(bf16[1,4096,384]{2,1,0:T(8,128)(2,1)} %gate_ref.1, bf16[1,4096,384]{2,1,0:T(8,128)(2,1)} %up_ref.1, bf16[1,384,4096]{2,1,0:T(8,128)(2,1)} %down_ref.1), custom_call_target="tpu_custom_call" | custom-call | bytes 18874368 | tf_op jit(solution)/shard_map/load/pallas_call | solution.py:101
  13.6 1.9 %collective-permute-start.3 = (bf16[32,1024]{1,0:T(8,128)(2,1)S(1)}, bf16[32,1024]{1,0:T(8,128)(2,1)S(1)}, u32[]{:S(2)}, u32[]{:S(2)}) collective-permute-start(bf16[32,1024]{1,0:T(8,128)(2,1)S(1)} %relay.2.refs_3_), channel_id=1, source_target_pairs={{0,2},{1,3},{2,0},{3,1},{4,6},{5,7},{6,4},{7,5},{8,10},{9,11},{10,... | collective-permute-start | bytes 196616 | tf_op jit(solution)/shard_map/ppermute | solution.py:66
  16.5 1.8 %collective-permute-done.3.refs_4_ = bf16[32,1024]{1,0:T(8,128)(2,1)S(1)} collective-permute-done((bf16[32,1024]{1,0:T(8,128)(2,1)S(1)}, bf16[32,1024]{1,0:T(8,128)(2,1)S(1)}, u32[]{:S(2)}, u32[]{:S(2)}) %collective-permute-start.3) | collective-permute-done | bytes 65568 | tf_op jit(solution)/shard_map/ppermute | solution.py:66
  18.3 1.6 %collective-permute-done.7.refs_8_ = bf16[32,1024]{1,0:T(8,128)(2,1)S(1)} collective-permute-done((bf16[32,1024]{1,0:T(8,128)(2,1)S(1)}, bf16[32,1024]{1,0:T(8,128)(2,1)S(1)}, u32[]{:S(2)}, u32[]{:S(2)}) %collective-permute-start.7) | collective-permute-done | bytes 65568 | tf_op jit(solution)/shard_map/ppermute | solution.py:66
  21.1 2.0 %front.2.hidden_ref = bf16[128,384]{1,0:T(8,128)(2,1)S(1)} custom-call(bf16[32,4096]{1,0:T(8,128)(2,1)S(1)} %copy-done, bf16[32,2176]{1,0:T(8,128)(2,1)S(1)} %collective-permute-done.refs_1_.refs_12_.refs_17_, bf16[32,2176]{1,0:T(8,128)(2,1)S(1)} %collective-permute-done.1.refs_2_, bf16[32,1024]{1,0:T(8,128)(2,1)S(1)} %relay.2.refs_3_, ...), custom_call_target="tpu_custom_call" | custom-call | flops 805306368 | bytes 6291456 | tf_op jit(solution)/shard_map/front/pallas_call | solution.py:210
  25.4 1.6 %collective-permute-start.14 = (bf16[64,1024]{1,0:T(8,128)(2,1)S(1)}, bf16[64,1024]{1,0:T(8,128)(2,1)S(1)}, u32[]{:S(2)}, u32[]{:S(2)}) collective-permute-start(bf16[64,1024]{1,0:T(8,128)(2,1)S(1)} %get-tuple-element.35), channel_id=1, source_target_pairs={{0,2},{1,3},{2,0},{3,1},{4,6},{5,7},{6,4},{7,5},{8,10},{9,11},{10,... | collective-permute-start | bytes 393224 | tf_op jit(solution)/shard_map/ppermute | solution.py:66
  27.8 4.0 %collective-permute-done.14.came_ref = bf16[64,1024]{1,0:T(8,128)(2,1)S(1)} collective-permute-done((bf16[64,1024]{1,0:T(8,128)(2,1)S(1)}, bf16[64,1024]{1,0:T(8,128)(2,1)S(1)}, u32[]{:S(2)}, u32[]{:S(2)}) %collective-permute-start.14) | collective-permute-done | bytes 131104 | tf_op jit(solution)/shard_map/ppermute | solution.py:66
  31.8 3.0 %collective-permute-start.15 = (bf16[32,1024]{1,0:T(8,128)(2,1)S(1)}, bf16[32,1024]{1,0:T(8,128)(2,1)S(1)}, u32[]{:S(2)}, u32[]{:S(2)}) collective-permute-start(bf16[32,1024]{1,0:T(8,128)(2,1)S(1)} %get-tuple-element.36), channel_id=1, source_target_pairs={{0,8},{4,12},{8,0},{12,4},{1,9},{5,13},{9,1},{13,5},{2,10},{6,14},... | collective-permute-start | bytes 196616 | tf_op jit(solution)/shard_map/ppermute | solution.py:66
  34.8 1.4 %collective-permute-start.16 = (bf16[32,1024]{1,0:T(8,128)(2,1)S(1)}, bf16[32,1024]{1,0:T(8,128)(2,1)S(1)}, u32[]{:S(2)}, u32[]{:S(2)}) collective-permute-start(bf16[32,1024]{1,0:T(8,128)(2,1)S(1)} %get-tuple-element.37), channel_id=1, source_target_pairs={{0,12},{4,8},{8,4},{12,0},{1,13},{5,9},{9,5},{13,1},{2,14},{6,10},... | collective-permute-start | bytes 196616 | tf_op jit(solution)/shard_map/ppermute | solution.py:66
  37.3 3.7 %collective-permute-done.16.refs_2_ = bf16[32,1024]{1,0:T(8,128)(2,1)S(1)} collective-permute-done((bf16[32,1024]{1,0:T(8,128)(2,1)S(1)}, bf16[32,1024]{1,0:T(8,128)(2,1)S(1)}, u32[]{:S(2)}, u32[]{:S(2)}) %collective-permute-start.16) | collective-permute-done | bytes 65568 | tf_op jit(solution)/shard_map/ppermute | solution.py:66
  41.7 2.3 %collective-permute-start.24 = (bf16[32,1024]{1,0:T(8,128)(2,1)S(1)}, bf16[32,1024]{1,0:T(8,128)(2,1)S(1)}, u32[]{:S(2)}, u32[]{:S(2)}) collective-permute-start(bf16[32,1024]{1,0:T(8,128)(2,1)S(1)} %move.2.refs_0_.own_ref), channel_id=1, source_target_pairs={{0,8},{4,12},{8,0},{12,4},{1,9},{5,13},{9,1},{13,5},{2,10},{6,14},... | collective-permute-start | bytes 196616 | tf_op jit(solution)/shard_map/ppermute | solution.py:66
  44.0 1.7 %collective-permute-start.28 = (bf16[32,1024]{1,0:T(8,128)(2,1)S(1)}, bf16[32,1024]{1,0:T(8,128)(2,1)S(1)}, u32[]{:S(2)}, u32[]{:S(2)}) collective-permute-start(bf16[32,1024]{1,0:T(8,128)(2,1)S(1)} %move.2.refs_0_.own_ref), channel_id=1, source_target_pairs={{0,12},{4,8},{8,4},{12,0},{1,13},{5,9},{9,5},{13,1},{2,14},{6,10},... | collective-permute-start | bytes 196616 | tf_op jit(solution)/shard_map/ppermute | solution.py:66
  45.7 1.5 %collective-permute-start.17 = (bf16[32,1024]{1,0:T(8,128)(2,1)S(1)}, bf16[32,1024]{1,0:T(8,128)(2,1)S(1)}, u32[]{:S(2)}, u32[]{:S(2)}) collective-permute-start(bf16[32,1024]{1,0:T(8,128)(2,1)S(1)} %move.2.refs_0_.own_ref), channel_id=1, source_target_pairs={{0,2},{1,3},{2,0},{3,1},{4,6},{5,7},{6,4},{7,5},{8,10},{9,11},{10,... | collective-permute-start | bytes 196616 | tf_op jit(solution)/shard_map/ppermute | solution.py:66
  50.1 1.6 %collective-permute-start.29 = (bf16[32,1024]{1,0:T(8,128)(2,1)S(1)}, bf16[32,1024]{1,0:T(8,128)(2,1)S(1)}, u32[]{:S(2)}, u32[]{:S(2)}) collective-permute-start(bf16[32,1024]{1,0:T(8,128)(2,1)S(1)} %collective-permute-done.28.refs_12_), channel_id=1, source_target_pairs={{0,2},{1,3},{2,0},{3,1},{4,6},{5,7},{6,4},{7,5},{8,10},{9,11},{10,... | collective-permute-start | bytes 196616 | tf_op jit(solution)/shard_map/ppermute | solution.py:66
  56.3 2.2 %front.3.hidden_ref = bf16[128,384]{1,0:T(8,128)(2,1)S(1)} custom-call(bf16[32,1024]{1,0:T(8,128)(2,1)S(1)} %move.2.refs_0_.own_ref, bf16[32,1024]{1,0:T(8,128)(2,1)S(1)} %collective-permute-done.17.refs_1_, bf16[32,1024]{1,0:T(8,128)(2,1)S(1)} %collective-permute-done.18.refs_2_, bf16[32,1024]{1,0:T(8,128)(2,1)S(1)} %collective-permute-done.19.refs_3_, ...), custom_call_target="tpu_custom_call" | custom-call | flops 805306368 | bytes 6291456 | tf_op jit(solution)/shard_map/front/pallas_call | solution.py:210
  60.8 1.4 %collective-permute-start.36 = (bf16[64,1024]{1,0:T(8,128)(2,1)S(1)}, bf16[64,1024]{1,0:T(8,128)(2,1)S(1)}, u32[]{:S(2)}, u32[]{:S(2)}) collective-permute-start(bf16[64,1024]{1,0:T(8,128)(2,1)S(1)} %get-tuple-element.43), channel_id=1, source_target_pairs={{0,2},{1,3},{2,0},{3,1},{4,6},{5,7},{6,4},{7,5},{8,10},{9,11},{10,... | collective-permute-start | bytes 393224 | tf_op jit(solution)/shard_map/ppermute | solution.py:66
  63.2 4.0 %collective-permute-done.36.came_ref = bf16[64,1024]{1,0:T(8,128)(2,1)S(1)} collective-permute-done((bf16[64,1024]{1,0:T(8,128)(2,1)S(1)}, bf16[64,1024]{1,0:T(8,128)(2,1)S(1)}, u32[]{:S(2)}, u32[]{:S(2)}) %collective-permute-start.36) | collective-permute-done | bytes 131104 | tf_op jit(solution)/shard_map/ppermute | solution.py:66
  67.9 1.7 %collective-permute-start.38 = (bf16[32,1024]{1,0:T(8,128)(2,1)S(1)}, bf16[32,1024]{1,0:T(8,128)(2,1)S(1)}, u32[]{:S(2)}, u32[]{:S(2)}) collective-permute-start(bf16[32,1024]{1,0:T(8,128)(2,1)S(1)} %get-tuple-element.45), channel_id=1, source_target_pairs={{0,12},{4,8},{8,4},{12,0},{1,13},{5,9},{9,5},{13,1},{2,14},{6,10},... | collective-permute-start | bytes 196616 | tf_op jit(solution)/shard_map/ppermute | solution.py:66
  69.6 1.3 %collective-permute-start.35 = (bf16[32,1024]{1,0:T(8,128)(2,1)S(1)}, bf16[32,1024]{1,0:T(8,128)(2,1)S(1)}, u32[]{:S(2)}, u32[]{:S(2)}) collective-permute-start(bf16[32,1024]{1,0:T(8,128)(2,1)S(1)} %get-tuple-element.41), channel_id=1, source_target_pairs={{0,4},{4,0},{8,12},{12,8},{1,5},{5,1},{9,13},{13,9},{2,6},{6,2},{1... | collective-permute-start | bytes 196616 | tf_op jit(solution)/shard_map/ppermute | solution.py:66
  70.9 2.2 %collective-permute-done.37.refs_1_ = bf16[32,1024]{1,0:T(8,128)(2,1)S(1)} collective-permute-done((bf16[32,1024]{1,0:T(8,128)(2,1)S(1)}, bf16[32,1024]{1,0:T(8,128)(2,1)S(1)}, u32[]{:S(2)}, u32[]{:S(2)}) %collective-permute-start.37) | collective-permute-done | bytes 65568 | tf_op jit(solution)/shard_map/ppermute | solution.py:66
  (80 shorter events, 20.7 us)
Async XLA Ops:
  2.3 7.5 %collective-permute-start = (bf16[32,2176]{1,0:T(8,128)(2,1)S(1)}, bf16[32,2176]{1,0:T(8,128)(2,1)S(1)}, u32[]{:S(2)}, u32[]{:S(2)}) collective-permute-start(bf16[32,2176]{1,0:T(8,128)(2,1)S(1)} %get-tuple-element.25), channel_id=1, source_target_pairs={{0,4},{4,0},{8,12},{12,8},{1,5},{5,1},{9,13},{13,9},{2,6},{6,2},{1... | collective-permute-start | bytes 417800 | tf_op jit(solution)/shard_map/ppermute | solution.py:66
  5.4 8.2 %collective-permute-start.2 = (bf16[32,1152]{1,0:T(8,128)(2,1)S(1)}, bf16[32,1152]{1,0:T(8,128)(2,1)S(1)}, u32[]{:S(2)}, u32[]{:S(2)}) collective-permute-start(bf16[32,1152]{1,0:T(8,128)(2,1)S(1)} %get-tuple-element.26.refs_11_.refs_16_), channel_id=1, source_target_pairs={{0,8},{4,12},{8,0},{12,4},{1,9},{5,13},{9,1},{13,5},{2,10},{6,14},... | collective-permute-start | bytes 221192 | tf_op jit(solution)/shard_map/ppermute | solution.py:66
  7.9 7.5 %collective-permute-start.6 = (bf16[32,1152]{1,0:T(8,128)(2,1)S(1)}, bf16[32,1152]{1,0:T(8,128)(2,1)S(1)}, u32[]{:S(2)}, u32[]{:S(2)}) collective-permute-start(bf16[32,1152]{1,0:T(8,128)(2,1)S(1)} %get-tuple-element.26.refs_11_.refs_16_), channel_id=1, source_target_pairs={{0,12},{4,8},{8,4},{12,0},{1,13},{5,9},{9,5},{13,1},{2,14},{6,10},... | collective-permute-start | bytes 221192 | tf_op jit(solution)/shard_map/ppermute | solution.py:66
  9.8 11.3 %collective-permute-start.1 = (bf16[32,2176]{1,0:T(8,128)(2,1)S(1)}, bf16[32,2176]{1,0:T(8,128)(2,1)S(1)}, u32[]{:S(2)}, u32[]{:S(2)}) collective-permute-start(bf16[32,2176]{1,0:T(8,128)(2,1)S(1)} %collective-permute-done.refs_1_.refs_12_.refs_17_), channel_id=1, source_target_pairs={{0,1},{1,0},{2,3},{3,2},{4,5},{5,4},{6,7},{7,6},{8,9},{9,8},{10,11... | collective-permute-start | bytes 417800 | tf_op jit(solution)/shard_map/ppermute | solution.py:66
  13.6 4.6 %collective-permute-start.3 = (bf16[32,1024]{1,0:T(8,128)(2,1)S(1)}, bf16[32,1024]{1,0:T(8,128)(2,1)S(1)}, u32[]{:S(2)}, u32[]{:S(2)}) collective-permute-start(bf16[32,1024]{1,0:T(8,128)(2,1)S(1)} %relay.2.refs_3_), channel_id=1, source_target_pairs={{0,2},{1,3},{2,0},{3,1},{4,6},{5,7},{6,4},{7,5},{8,10},{9,11},{10,... | collective-permute-start | bytes 196616 | tf_op jit(solution)/shard_map/ppermute | solution.py:66
  15.5 4.3 %collective-permute-start.7 = (bf16[32,1024]{1,0:T(8,128)(2,1)S(1)}, bf16[32,1024]{1,0:T(8,128)(2,1)S(1)}, u32[]{:S(2)}, u32[]{:S(2)}) collective-permute-start(bf16[32,1024]{1,0:T(8,128)(2,1)S(1)} %relay.3.refs_7_), channel_id=1, source_target_pairs={{0,2},{1,3},{2,0},{3,1},{4,6},{5,7},{6,4},{7,5},{8,10},{9,11},{10,... | collective-permute-start | bytes 196616 | tf_op jit(solution)/shard_map/ppermute | solution.py:66
  25.4 6.4 %collective-permute-start.14 = (bf16[64,1024]{1,0:T(8,128)(2,1)S(1)}, bf16[64,1024]{1,0:T(8,128)(2,1)S(1)}, u32[]{:S(2)}, u32[]{:S(2)}) collective-permute-start(bf16[64,1024]{1,0:T(8,128)(2,1)S(1)} %get-tuple-element.35), channel_id=1, source_target_pairs={{0,2},{1,3},{2,0},{3,1},{4,6},{5,7},{6,4},{7,5},{8,10},{9,11},{10,... | collective-permute-start | bytes 393224 | tf_op jit(solution)/shard_map/ppermute | solution.py:66
  27.0 9.1 %collective-permute-start.12 = (bf16[64,1024]{1,0:T(8,128)(2,1)S(1)}, bf16[64,1024]{1,0:T(8,128)(2,1)S(1)}, u32[]{:S(2)}, u32[]{:S(2)}) collective-permute-start(bf16[64,1024]{1,0:T(8,128)(2,1)S(1)} %get-tuple-element.31), channel_id=1, source_target_pairs={{0,2},{1,3},{2,0},{3,1},{4,6},{5,7},{6,4},{7,5},{8,10},{9,11},{10,... | collective-permute-start | bytes 393224 | tf_op jit(solution)/shard_map/ppermute | solution.py:66
  31.8 5.5 %collective-permute-start.15 = (bf16[32,1024]{1,0:T(8,128)(2,1)S(1)}, bf16[32,1024]{1,0:T(8,128)(2,1)S(1)}, u32[]{:S(2)}, u32[]{:S(2)}) collective-permute-start(bf16[32,1024]{1,0:T(8,128)(2,1)S(1)} %get-tuple-element.36), channel_id=1, source_target_pairs={{0,8},{4,12},{8,0},{12,4},{1,9},{5,13},{9,1},{13,5},{2,10},{6,14},... | collective-permute-start | bytes 196616 | tf_op jit(solution)/shard_map/ppermute | solution.py:66
  34.8 6.2 %collective-permute-start.16 = (bf16[32,1024]{1,0:T(8,128)(2,1)S(1)}, bf16[32,1024]{1,0:T(8,128)(2,1)S(1)}, u32[]{:S(2)}, u32[]{:S(2)}) collective-permute-start(bf16[32,1024]{1,0:T(8,128)(2,1)S(1)} %get-tuple-element.37), channel_id=1, source_target_pairs={{0,12},{4,8},{8,4},{12,0},{1,13},{5,9},{9,5},{13,1},{2,14},{6,10},... | collective-permute-start | bytes 196616 | tf_op jit(solution)/shard_map/ppermute | solution.py:66
  36.2 5.0 %collective-permute-start.13 = (bf16[32,1024]{1,0:T(8,128)(2,1)S(1)}, bf16[32,1024]{1,0:T(8,128)(2,1)S(1)}, u32[]{:S(2)}, u32[]{:S(2)}) collective-permute-start(bf16[32,1024]{1,0:T(8,128)(2,1)S(1)} %get-tuple-element.33), channel_id=1, source_target_pairs={{0,4},{4,0},{8,12},{12,8},{1,5},{5,1},{9,13},{13,9},{2,6},{6,2},{1... | collective-permute-start | bytes 196616 | tf_op jit(solution)/shard_map/ppermute | solution.py:66
  41.3 6.0 %collective-permute-start.20 = (bf16[32,1024]{1,0:T(8,128)(2,1)S(1)}, bf16[32,1024]{1,0:T(8,128)(2,1)S(1)}, u32[]{:S(2)}, u32[]{:S(2)}) collective-permute-start(bf16[32,1024]{1,0:T(8,128)(2,1)S(1)} %move.2.refs_0_.own_ref), channel_id=1, source_target_pairs={{0,4},{4,0},{8,12},{12,8},{1,5},{5,1},{9,13},{13,9},{2,6},{6,2},{1... | collective-permute-start | bytes 196616 | tf_op jit(solution)/shard_map/ppermute | solution.py:66
  41.7 6.8 %collective-permute-start.24 = (bf16[32,1024]{1,0:T(8,128)(2,1)S(1)}, bf16[32,1024]{1,0:T(8,128)(2,1)S(1)}, u32[]{:S(2)}, u32[]{:S(2)}) collective-permute-start(bf16[32,1024]{1,0:T(8,128)(2,1)S(1)} %move.2.refs_0_.own_ref), channel_id=1, source_target_pairs={{0,8},{4,12},{8,0},{12,4},{1,9},{5,13},{9,1},{13,5},{2,10},{6,14},... | collective-permute-start | bytes 196616 | tf_op jit(solution)/shard_map/ppermute | solution.py:66
  44.0 6.1 %collective-permute-start.28 = (bf16[32,1024]{1,0:T(8,128)(2,1)S(1)}, bf16[32,1024]{1,0:T(8,128)(2,1)S(1)}, u32[]{:S(2)}, u32[]{:S(2)}) collective-permute-start(bf16[32,1024]{1,0:T(8,128)(2,1)S(1)} %move.2.refs_0_.own_ref), channel_id=1, source_target_pairs={{0,12},{4,8},{8,4},{12,0},{1,13},{5,9},{9,5},{13,1},{2,14},{6,10},... | collective-permute-start | bytes 196616 | tf_op jit(solution)/shard_map/ppermute | solution.py:66
  45.7 5.9 %collective-permute-start.17 = (bf16[32,1024]{1,0:T(8,128)(2,1)S(1)}, bf16[32,1024]{1,0:T(8,128)(2,1)S(1)}, u32[]{:S(2)}, u32[]{:S(2)}) collective-permute-start(bf16[32,1024]{1,0:T(8,128)(2,1)S(1)} %move.2.refs_0_.own_ref), channel_id=1, source_target_pairs={{0,2},{1,3},{2,0},{3,1},{4,6},{5,7},{6,4},{7,5},{8,10},{9,11},{10,... | collective-permute-start | bytes 196616 | tf_op jit(solution)/shard_map/ppermute | solution.py:66
  47.2 4.4 %collective-permute-start.18 = (bf16[32,1024]{1,0:T(8,128)(2,1)S(1)}, bf16[32,1024]{1,0:T(8,128)(2,1)S(1)}, u32[]{:S(2)}, u32[]{:S(2)}) collective-permute-start(bf16[32,1024]{1,0:T(8,128)(2,1)S(1)} %move.2.refs_0_.own_ref), channel_id=1, source_target_pairs={{0,1},{1,0},{2,3},{3,2},{4,5},{5,4},{6,7},{7,6},{8,9},{9,8},{10,11... | collective-permute-start | bytes 196616 | tf_op jit(solution)/shard_map/ppermute | solution.py:66
  47.2 4.9 %collective-permute-start.21 = (bf16[32,1024]{1,0:T(8,128)(2,1)S(1)}, bf16[32,1024]{1,0:T(8,128)(2,1)S(1)}, u32[]{:S(2)}, u32[]{:S(2)}) collective-permute-start(bf16[32,1024]{1,0:T(8,128)(2,1)S(1)} %collective-permute-done.20.refs_4_), channel_id=1, source_target_pairs={{0,2},{1,3},{2,0},{3,1},{4,6},{5,7},{6,4},{7,5},{8,10},{9,11},{10,... | collective-permute-start | bytes 196616 | tf_op jit(solution)/shard_map/ppermute | solution.py:66
  48.5 5.0 %collective-permute-start.25 = (bf16[32,1024]{1,0:T(8,128)(2,1)S(1)}, bf16[32,1024]{1,0:T(8,128)(2,1)S(1)}, u32[]{:S(2)}, u32[]{:S(2)}) collective-permute-start(bf16[32,1024]{1,0:T(8,128)(2,1)S(1)} %collective-permute-done.24.refs_8_), channel_id=1, source_target_pairs={{0,2},{1,3},{2,0},{3,1},{4,6},{5,7},{6,4},{7,5},{8,10},{9,11},{10,... | collective-permute-start | bytes 196616 | tf_op jit(solution)/shard_map/ppermute | solution.py:66
  50.1 4.5 %collective-permute-start.29 = (bf16[32,1024]{1,0:T(8,128)(2,1)S(1)}, bf16[32,1024]{1,0:T(8,128)(2,1)S(1)}, u32[]{:S(2)}, u32[]{:S(2)}) collective-permute-start(bf16[32,1024]{1,0:T(8,128)(2,1)S(1)} %collective-permute-done.28.refs_12_), channel_id=1, source_target_pairs={{0,2},{1,3},{2,0},{3,1},{4,6},{5,7},{6,4},{7,5},{8,10},{9,11},{10,... | collective-permute-start | bytes 196616 | tf_op jit(solution)/shard_map/ppermute | solution.py:66
  60.8 6.4 %collective-permute-start.36 = (bf16[64,1024]{1,0:T(8,128)(2,1)S(1)}, bf16[64,1024]{1,0:T(8,128)(2,1)S(1)}, u32[]{:S(2)}, u32[]{:S(2)}) collective-permute-start(bf16[64,1024]{1,0:T(8,128)(2,1)S(1)} %get-tuple-element.43), channel_id=1, source_target_pairs={{0,2},{1,3},{2,0},{3,1},{4,6},{5,7},{6,4},{7,5},{8,10},{9,11},{10,... | collective-permute-start | bytes 393224 | tf_op jit(solution)/shard_map/ppermute | solution.py:66
  62.2 7.3 %collective-permute-start.34 = (bf16[64,1024]{1,0:T(8,128)(2,1)S(1)}, bf16[64,1024]{1,0:T(8,128)(2,1)S(1)}, u32[]{:S(2)}, u32[]{:S(2)}) collective-permute-start(bf16[64,1024]{1,0:T(8,128)(2,1)S(1)} %get-tuple-element.39), channel_id=1, source_target_pairs={{0,2},{1,3},{2,0},{3,1},{4,6},{5,7},{6,4},{7,5},{8,10},{9,11},{10,... | collective-permute-start | bytes 393224 | tf_op jit(solution)/shard_map/ppermute | solution.py:66
  67.3 5.9 %collective-permute-start.37 = (bf16[32,1024]{1,0:T(8,128)(2,1)S(1)}, bf16[32,1024]{1,0:T(8,128)(2,1)S(1)}, u32[]{:S(2)}, u32[]{:S(2)}) collective-permute-start(bf16[32,1024]{1,0:T(8,128)(2,1)S(1)} %get-tuple-element.44), channel_id=1, source_target_pairs={{0,8},{4,12},{8,0},{12,4},{1,9},{5,13},{9,1},{13,5},{2,10},{6,14},... | collective-permute-start | bytes 196616 | tf_op jit(solution)/shard_map/ppermute | solution.py:66
  67.9 6.2 %collective-permute-start.38 = (bf16[32,1024]{1,0:T(8,128)(2,1)S(1)}, bf16[32,1024]{1,0:T(8,128)(2,1)S(1)}, u32[]{:S(2)}, u32[]{:S(2)}) collective-permute-start(bf16[32,1024]{1,0:T(8,128)(2,1)S(1)} %get-tuple-element.45), channel_id=1, source_target_pairs={{0,12},{4,8},{8,4},{12,0},{1,13},{5,9},{9,5},{13,1},{2,14},{6,10},... | collective-permute-start | bytes 196616 | tf_op jit(solution)/shard_map/ppermute | solution.py:66
  69.6 5.0 %collective-permute-start.35 = (bf16[32,1024]{1,0:T(8,128)(2,1)S(1)}, bf16[32,1024]{1,0:T(8,128)(2,1)S(1)}, u32[]{:S(2)}, u32[]{:S(2)}) collective-permute-start(bf16[32,1024]{1,0:T(8,128)(2,1)S(1)} %get-tuple-element.41), channel_id=1, source_target_pairs={{0,4},{4,0},{8,12},{12,8},{1,5},{5,1},{9,13},{13,9},{2,6},{6,2},{1... | collective-permute-start | bytes 196616 | tf_op jit(solution)/shard_map/ppermute | solution.py:66
  (18 other events, 82.8 us)

commit v5 on v4

--- a/solution.py
+++ b/solution.py
@@ -127,66 +127,132 @@
     )(block, done)
 
 
-def pack_kernel(experts, tokens_ref, ids_ref, wide_ref, out_ref, own_ref, sems):
+def choose(ids, expert, slots):
+    picks, rows = ids.shape
+    named = jnp.zeros((1, rows), jnp.float32)
+    for k in range(picks):
+        named += jnp.where(ids[k : k + 1, :] == expert, 1.0, 0.0)
+    named = jnp.broadcast_to(named, (slots, rows))
+    earlier = lax.broadcasted_iota(jnp.int32, (rows, rows), 0) < lax.broadcasted_iota(jnp.int32, (rows, rows), 1)
+    ahead = jnp.dot(
+        named.astype(jnp.bfloat16),
+        jnp.where(earlier, 1.0, 0.0).astype(jnp.bfloat16),
+        preferred_element_type=jnp.float32,
+    )
+    slot = lax.broadcasted_iota(jnp.int32, (slots, rows), 0)
+    return jnp.where((ahead.astype(jnp.int32) == slot) & (named > 0.5), 1.0, 0.0)
+
+
+def select(one_hot, values):
+    one_hot = one_hot.astype(jnp.bfloat16)
+    return jnp.dot(one_hot, values, preferred_element_type=jnp.float32).astype(jnp.bfloat16)
+
+
+def flags_of(ids, section, experts):
+    picks, rows = ids.shape
+    lane = lax.broadcasted_iota(jnp.int32, (LANES, rows), 0)
+    flags = jnp.zeros(lane.shape, jnp.float32)
+    for k in range(picks):
+        flags += jnp.where(ids[k : k + 1, :] + section * experts == lane, 1.0, 0.0)
+    return flags.T.astype(jnp.bfloat16)
+
+
+def chosen_flags(ids, peer, experts, slots):
+    picked = [choose(one, lax.axis_index("ep") ^ peer, slots) for one in ids]
+    parts = [select(p, flags_of(one, s, experts)) for s, (p, one) in enumerate(zip(picked, ids))]
+    return sum(part.astype(jnp.float32) for part in parts).astype(jnp.bfloat16), picked[0]
+
+
+def pack_kernel(experts, tokens_ref, ids_ref, *refs):
+    wide_ref, *out_refs, own_ref, half_ref, held_ref, sems = refs
     width = tokens_ref.shape[1]
     half, quarter = width // 2, width // 4
     where = lax.axis_index("et")
     copies = [
-        pltpu.make_async_copy(tokens_ref.at[:, aligned(where & 1, half)], wide_ref.at[:, :half], sems.at[0]),
-        pltpu.make_async_copy(tokens_ref.at[:, aligned(where, quarter)], own_ref, sems.at[1]),
+        pltpu.make_async_copy(ids_ref, held_ref, sems.at[0]),
+        pltpu.make_async_copy(tokens_ref.at[:, aligned(where & 1, quarter)], half_ref.at[:, :quarter], sems.at[1]),
+        pltpu.make_async_copy(tokens_ref.at[:, aligned(where & 1 | 2, quarter)], half_ref.at[:, quarter:], sems.at[2]),
     ]
     for copy in copies:
         copy.start()
-    rows = tokens_ref.shape[0]
-    lane = lax.broadcasted_iota(jnp.int32, (LANES, rows), 0)
-    flags = jnp.zeros(lane.shape, jnp.float32)
-    for s in range(ids_ref.shape[0]):
-        for k in range(ids_ref.shape[1]):
-            flags += jnp.where(ids_ref[s][k : k + 1, :] + s * experts == lane, 1.0, 0.0)
-    flags = flags.T.astype(jnp.bfloat16)
-    wide_ref[:, half:] = flags
-    out_ref[:, quarter:] = flags
-    for copy in copies:
-        copy.wait()
-    out_ref[:, :quarter] = own_ref[...]
-
-
-def pack(tokens, ids, experts):
+    copies[0].wait()
+    ids = [held_ref[s] for s in range(held_ref.shape[0])]
+    slots = wide_ref.shape[0]
+    made = [chosen_flags(ids, k + 1, experts, slots) for k in range(1 + len(out_refs))]
+    copies[1].wait()
+    copies[2].wait()
+    own_ref[...] = half_ref[:, aligned(where >> 1, quarter)]
+    wide_ref[:, :half] = select(made[0][1], half_ref[...])
+    wide_ref[:, half:] = made[0][0]
+    for (flags, picked), out_ref in zip(made[1:], out_refs):
+        out_ref[:, :quarter] = select(picked, own_ref[...])
+        out_ref[:, quarter:] = flags
+
+
+def pack(tokens, ids, experts, slots):
     rows, width = tokens.shape
-    shapes = [(rows, width // 2 + LANES), (rows, width // 4 + LANES), (rows, width // 4)]
+    far = lax.axis_size("ep") - 2
+    shapes = [(slots, width // 2 + LANES)] + [(slots, width // 4 + LANES)] * far + [(rows, width // 4)]
     return pl.pallas_call(
         functools.partial(pack_kernel, experts),
-        in_specs=[ANY, VMEM],
-        out_specs=[VMEM] * 3,
+        in_specs=[ANY] * 2,
+        out_specs=[VMEM] * len(shapes),
         out_shape=[pltpu.VMEM(s, jnp.bfloat16) for s in shapes],
-        scratch_shapes=[pltpu.SemaphoreType.DMA((2,))],
+        scratch_shapes=[
+            pltpu.VMEM((rows, width // 2), jnp.bfloat16),
+            pltpu.VMEM(ids.shape, jnp.int32),
+            pltpu.SemaphoreType.DMA((3,)),
+        ],
         compiler_params=params(VMEM_ALL),
         name="pack",
     )(tokens, ids)
 
 
-def front_kernel(pieces, section, experts, n_flags, *refs):
-    n = len(pieces)
-    x_refs, flag_refs = refs[:n], refs[n : n + n_flags]
+def own_kernel(experts, tokens_ref, ids_ref, out_ref, flags_ref):
+    ids = [ids_ref[s] for s in range(ids_ref.shape[0])]
+    flags_ref[...], picked = chosen_flags(ids, 0, experts, out_ref.shape[0])
+    out_ref[...] = select(picked, tokens_ref[...])
+
+
+def own_rows(tokens, ids, experts, slots):
+    shapes = [(slots, tokens.shape[1]), (slots, LANES)]
+    return pl.pallas_call(
+        functools.partial(own_kernel, experts),
+        out_shape=[jax.ShapeDtypeStruct(s, jnp.bfloat16) for s in shapes],
+        compiler_params=params(),
+        name="own_rows",
+    )(tokens, ids)
+
+
+def front_kernel(layout, section, experts, n_flags, *refs):
+    n = sum(len(block) for block in layout)
+    x_refs, flag_refs = list(refs[:n]), refs[n : n + n_flags]
     mod_ref, router_ref, pair_ref, out_ref, normed_ref = refs[n + n_flags :]
     width = normed_ref.shape[1]
     hidden = out_ref.shape[1]
-    for row in sorted({piece[0] for piece in pieces}):
-        members = [i for i in range(n) if pieces[i][0] == row]
-        rows = pieces[members[0]][1]
-        total = jnp.zeros((rows, 1), jnp.float32)
-        for i in members:
-            xf = x_refs[i][:, : pieces[i][2]].astype(jnp.float32)
-            total += jnp.sum(xf * xf, axis=1, keepdims=True)
-        scale = lax.rsqrt(total / width + 1e-06)
-        for i in members:
-            cols = pieces[i][2]
-            place = (lax.axis_index("et") & (width // cols - 1)) ^ pieces[i][3]
-            where = aligned(place, cols) if cols < width else slice(None)
-            xf = x_refs[i][:, :cols].astype(jnp.float32)
-            normed_ref[row : row + rows, where] = (
-                xf * scale * (1.0 + mod_ref[section, 0:1, where]) + mod_ref[section, 1:2, where]
-            ).astype(jnp.bfloat16)
+    quarter = width // 4
+    et = lax.axis_index("et")
+    blocks = []
+    for block in layout:
+        blocks.append([(x_refs.pop(0), cols, flip) for cols, flip in block])
+
+    def part(block, flip):
+        for ref, cols, at in block:
+            if cols == quarter and at == flip:
+                return ref[...].astype(jnp.float32)
+            if cols == 2 * quarter and at == flip & 1:
+                return ref[:, aligned((et ^ flip) >> 1, quarter)].astype(jnp.float32)
+            if cols == width:
+                return ref[:, aligned(et ^ flip, quarter)].astype(jnp.float32)
+
+    parts = [jnp.concatenate([part(block, flip) for block in blocks], axis=0) for flip in range(4)]
+    total = sum(jnp.sum(xf * xf, axis=1, keepdims=True) for xf in parts)
+    scale = lax.rsqrt(total / width + 1e-06)
+    for flip, xf in enumerate(parts):
+        where = aligned(et ^ flip, quarter)
+        normed_ref[:, where] = (
+            xf * scale * (1.0 + mod_ref[section, 0:1, where]) + mod_ref[section, 1:2, where]
+        ).astype(jnp.bfloat16)
     normed = normed_ref[...]
     both = jnp.dot(normed, pair_ref[...], preferred_element_type=jnp.float32)
     logits = lax.dot_general(
@@ -194,21 +260,25 @@
     )
     count = logits.shape[1]
     lane = lax.broadcasted_iota(jnp.int32, logits.shape, 1)
-    flags = jnp.concatenate([f[:, f.shape[1] - LANES :] for f in flag_refs], axis=0).astype(jnp.float32)
-    flags = flags[:, section * experts : section * experts + count]
+    flags = [f[:, f.shape[1] - LANES :].astype(jnp.float32) for f in flag_refs]
+    flags = jnp.concatenate(flags, axis=0)[:, section * experts : section * experts + count]
     chosen = jnp.where(flags > 0.5, jax.nn.sigmoid(logits), 0.0)
-    mine = jnp.where(lane == lax.axis_index("ep"), chosen, 0.0)
-    weight = jnp.sum(mine, axis=1, keepdims=True) / jnp.sum(chosen, axis=1, keepdims=True)
+    mine = jnp.sum(jnp.where(lane == lax.axis_index("ep"), chosen, 0.0), axis=1, keepdims=True)
+    used = jnp.max(flags, axis=1, keepdims=True) > 0.5
+    weight = jnp.where(used, mine / jnp.sum(chosen, axis=1, keepdims=True), 0.0)
     gate, upper = both[:, :hidden], both[:, hidden:]
-    out_ref[...] = (gate / (1.0 + jnp.exp(-gate)) * upper * weight).astype(jnp.bfloat16)
-
-
-def front(xs, pieces, flags, section, mod, router, pair):
+    units = jnp.where(used, gate / (1.0 + jnp.exp(-gate)) * upper * weight, 0.0)
+    out_ref[...] = units.astype(jnp.bfloat16)
+
+
+def front(blocks, flags, section, mod, router, pair):
     width, hidden = pair.shape[0], pair.shape[1] // 2
     rows = sum(f.shape[0] for f in flags)
     experts = router.shape[0]
-    return pl.pallas_call(
-        functools.partial(front_kernel, pieces, section, experts, len(flags)),
+    xs = [x for block in blocks for x, _, _ in block]
+    layout = [[piece[1:] for piece in block] for block in blocks]
+    return pl.pallas_call(
+        functools.partial(front_kernel, layout, section, experts, len(flags)),
         in_specs=[VMEM] * (len(xs) + len(flags) + 3),
         scratch_shapes=[pltpu.VMEM((rows, width), jnp.bfloat16)],
         out_shape=jax.ShapeDtypeStruct((rows, hidden), jnp.bfloat16),
@@ -248,41 +318,50 @@
 
 
 def add_kernel(keep_ref, came_ref, *outs):
+    total = keep_ref[...] + came_ref[...].astype(jnp.float32)
+    rows = outs[0].shape[0]
     for k, out in enumerate(outs):
-        rows = slice(k * out.shape[0], (k + 1) * out.shape[0])
-        out[...] = (keep_ref[rows, :] + came_ref[rows, :].astype(jnp.float32)).astype(out.dtype)
-
-
-def add(keep, came, dtypes):
-    shape = (keep.shape[0] // len(dtypes), keep.shape[1])
+        out[...] = total[k * rows : (k + 1) * rows].astype(out.dtype)
+
+
+def add(keep, came, count):
+    shape = (keep.shape[0] // count, keep.shape[1])
     return pl.pallas_call(
         add_kernel,
-        out_shape=[jax.ShapeDtypeStruct(shape, t) for t in dtypes],
+        out_shape=[jax.ShapeDtypeStruct(shape, jnp.bfloat16)] * count,
         compiler_params=params(),
         name="add",
     )(keep, came)
 
 
-def move_kernel(n_outs, own_ref, total_ref, *refs):
-    came, outs = refs[:-n_outs], refs[-n_outs:]
-    velocity = total_ref[...]
-    for ref in came:
-        velocity += ref[...].astype(jnp.float32)
-    outs[0][...] = (own_ref[...].astype(jnp.float32) - 0.5 * velocity).astype(jnp.bfloat16)
-    if n_outs > 1:
+def move_kernel(section, n_came, own_ref, ids_ref, *refs):
+    came, outs = refs[:n_came], refs[n_came:]
+    peer = lax.axis_index("ep")
+    slots = came[0].shape[0]
+    velocity = jnp.zeros(own_ref.shape, jnp.float32)
+    for k, ref in enumerate(came):
+        back = choose(ids_ref[section], peer ^ k, slots).T.astype(jnp.bfloat16)
+        velocity += jnp.dot(back, ref[...], preferred_element_type=jnp.float32)
+    moved = (own_ref[...].astype(jnp.float32) - 0.5 * velocity).astype(jnp.bfloat16)
+    outs[0][...] = moved
+    if len(outs) == 2:
         outs[1][...] = velocity.astype(jnp.bfloat16)
-
-
-def move(own, total, came, n_outs):
-    return pl.pallas_call(
-        functools.partial(move_kernel, n_outs),
-        out_shape=[jax.ShapeDtypeStruct(own.shape, jnp.bfloat16)] * n_outs,
+    else:
+        for k, out in enumerate(outs[1:]):
+            out[...] = select(choose(ids_ref[section + 1], peer ^ k, slots), moved)
+
+
+def move(section, own, ids, came):
+    shapes = [own.shape] + ([own.shape] if section + 1 == ids.shape[0] else [c.shape for c in came])
+    return pl.pallas_call(
+        functools.partial(move_kernel, section, len(came)),
+        out_shape=[jax.ShapeDtypeStruct(s, jnp.bfloat16) for s in shapes],
         compiler_params=params(),
         name="move",
-    )(own, total, *came)
-
-
-def sum_back(hidden, w_down, own, n_outs):
+    )(own, ids, *came)
+
+
+def sum_back(section, hidden, w_down, own, ids):
     peers = lax.axis_size("ep")
     some = peers // 2
     far = swap(down(hidden, w_down, 3, 1)[0], "et", 1)
@@ -290,43 +369,38 @@
     first, last = down(hidden, w_down, 2, 2, (far,))
     last, first = swap(last, "et", 2), swap(first, "et", 2)
     keep_first, keep_last = down(hidden, w_down, 0, 2, (near,), jnp.float32)
-    blocks = add(keep_last, last, [jnp.bfloat16] * (peers - some))
-    total, *others = add(keep_first, first, [jnp.float32] + [jnp.bfloat16] * (some - 1))
-    sent = [swap(b, "ep", k + 1) for k, b in enumerate(others + list(blocks))]
-    return move(own, total, sent, n_outs)
-
-
-QUARTERS = (0, 2, 1, 3)
-
-
-def spread(block):
+    later = add(keep_last, last, peers - some)
+    blocks = add(keep_first, first, some) + later
+    return move(section, own, ids, [swap(b, "ep", k) if k else b for k, b in enumerate(blocks)])
+
+
+def spread(block, quarter):
     side = swap(block, "et", 2)
-    return [block, side, swap(block, "et", 1), swap(side, "et", 1)]
+    near, far = swap(block, "et", 1), swap(side, "et", 1)
+    return [(block, quarter, 0), (side, quarter, 2), (near, quarter, 1), (far, quarter, 3)]
 
 
 def dense_body(tokens, modulation, router, gate_weight, up_weight, down_weight, expert_ids):
     rows, width = tokens.shape
-    quarter = width // 4
+    half, quarter = width // 2, width // 4
     router = router.T
+    experts = router.shape[0]
     peers = lax.axis_size("ep")
-
-    wide, packed, own = pack(tokens, expert_ids.transpose(0, 2, 1), router.shape[0])
+    slots = 3 * rows * expert_ids.shape[2] // (2 * experts)
+    ids = expert_ids.transpose(0, 2, 1)
+
+    wide, *packed, own = pack(tokens, ids, experts, slots)
     pair, w_down, done = load(gate_weight, up_weight, down_weight)
-    flags = [packed, swap(wide, "ep", 1)] + [swap(packed, "ep", k) for k in range(2, peers)]
-    xs = [tokens, flags[1], swap(flags[1], "et", 1)]
-    pieces = [(0, rows, width, 0), (rows, rows, width // 2, 0), (rows, rows, width // 2, 1)]
-    for k in range(2, peers):
-        xs += spread(relay(flags[k], quarter, done))
-        pieces += [(k * rows, rows, quarter, f) for f in QUARTERS]
-    hidden = front(xs, pieces, flags, 0, modulation, router, pair)
-    (own,) = sum_back(hidden, w_down, own, 1)
-
-    xs, pieces = [], []
-    for k in range(peers):
-        xs += spread(swap(own, "ep", k) if k else own)
-        pieces += [(k * rows, rows, quarter, f) for f in QUARTERS]
-    hidden = front(xs, pieces, flags, 1, modulation, router, pair)
-    return tuple(sum_back(hidden, w_down, own, 2))
+    mine, flags = own_rows(tokens, ids, experts, slots)
+    flags = [flags, swap(wide, "ep", 1)] + [swap(p, "ep", k + 2) for k, p in enumerate(packed)]
+    blocks = [[(mine, width, 0)], [(flags[1], half, 0), (swap(flags[1], "et", 1), half, 1)]]
+    blocks += [spread(relay(f, quarter, done), quarter) for f in flags[2:]]
+    hidden = front(blocks, flags, 0, modulation, router, pair)
+    own, *sent = sum_back(0, hidden, w_down, own, ids)
+
+    blocks = [spread(swap(b, "ep", k) if k else b, quarter) for k, b in enumerate(sent)]
+    hidden = front(blocks, flags, 1, modulation, router, pair)
+    return tuple(sum_back(1, hidden, w_down, own, ids))
 
 
 def solution(mesh):

time: 75.5 us -> 71.7 us (0.950)
  waiting for transfers between devices: 28.3 us -> 23.5 us
  Pallas kernels: 13 us -> 14.5 us
    ppermute x39, waiting for transfers between devices: 28.3 us -> 23.5 us  [swap(): return lax.ppermute(x, axis, [(i, i ^ bit) for i in range(size)])]
    pallas_call x9 -> x10, Pallas kernels: 6.75 us -> 8.46 us  [the longest x2 3.81 us: front(): pl.pallas_call(functools.partial(front_kernel, layout, section, experts,...]
where the time goes in v5:
time: 71.7 us; the launch traced here: 71.6 us
  starting transfers between devices  32.7 us (46%)
  waiting for transfers between devices  23.5 us (33%)
  Pallas kernels  14.5 us (20%)
  between operations  0.84 us (1%)
    ppermute x39, starting transfers between devices, swap(): return lax.ppermute(x, axis, [(i, i ^ bit) for i in range(size)])  32.7 us
    ppermute x39, waiting for transfers between devices, swap(): return lax.ppermute(x, axis, [(i, i ^ bit) for i in range(size)])  23.5 us
    pallas_call x2, Pallas kernels, front(): pl.pallas_call(functools.partial(front_kernel, layout, section, experts,...  3.81 us
    pallas_call x1, Pallas kernels, load(): pl.pallas_call(load_kernel, in_specs=[ANY] * 3, out_specs=[VMEM] * 3, out...  3.78 us
    pallas_call x2, Pallas kernels, move(): pl.pallas_call(functools.partial(move_kernel, section, len(came)), out_sh...  2.8 us
    pallas_call x8, Pallas kernels, down(): pl.pallas_call(functools.partial(down_kernel, flip, len(adds)), in_specs=...  2.25 us
  transfers between devices with their start and end apart: 39, of which 20 were waited for; matrix products, arithmetic and copies ran while one was open for 0% of the time, Pallas kernels for 8%

profile of v5, /device:TPU:0, one launch (start us, length us, event | category | flops | bytes accessed | tf_op | source)
XLA Modules:
  0.0 71.6 jit_solution(2354791198739915086)
XLA Ops:
  0.6 1.4 %pack.1 = (bf16[24,2176]{1,0:T(8,128)(2,1)S(1)}, bf16[24,1152]{1,0:T(8,128)(2,1)S(1)}, bf16[24,1152]{1,0:T(8,128)(2,1)S(1)}, bf16[32,1024]{1,0:T(8,128)(2,1)S(1)}) custom-call(bf16[32,4096]{1,0:T(8,128)(2,1)} %tokens_ref.3, s32[2,2,32]{2,1,0:T(2,128)} %bitcast.4), custom_call_target="tpu_custom_call" | custom-call | tf_op jit(solution)/shard_map/pack/pallas_call | solution.py:196
  2.1 3.1 %collective-permute-start = (bf16[24,2176]{1,0:T(8,128)(2,1)S(1)}, bf16[24,2176]{1,0:T(8,128)(2,1)S(1)}, u32[]{:S(2)}, u32[]{:S(2)}) collective-permute-start(bf16[24,2176]{1,0:T(8,128)(2,1)S(1)} %get-tuple-element.34), channel_id=1, source_target_pairs={{0,4},{4,0},{8,12},{12,8},{1,5},{5,1},{9,13},{13,9},{2,6},{6,2},{1... | collective-permute-start | bytes 313352 | tf_op jit(solution)/shard_map/ppermute | solution.py:66
  5.1 2.6 %collective-permute-start.2 = (bf16[24,1152]{1,0:T(8,128)(2,1)S(1)}, bf16[24,1152]{1,0:T(8,128)(2,1)S(1)}, u32[]{:S(2)}, u32[]{:S(2)}) collective-permute-start(bf16[24,1152]{1,0:T(8,128)(2,1)S(1)} %get-tuple-element.35), channel_id=1, source_target_pairs={{0,8},{4,12},{8,0},{12,4},{1,9},{5,13},{9,1},{13,5},{2,10},{6,14},... | collective-permute-start | bytes 165896 | tf_op jit(solution)/shard_map/ppermute | solution.py:66
  8.1 3.8 %load.1 = (bf16[4096,768]{1,0:T(8,128)(2,1)S(1)}, bf16[384,4096]{1,0:T(8,128)(2,1)S(1)}, f32[8,128]{1,0:T(8,128)S(1)}) custom-call(bf16[1,4096,384]{2,1,0:T(8,128)(2,1)} %gate_ref.1, bf16[1,4096,384]{2,1,0:T(8,128)(2,1)} %up_ref.1, bf16[1,384,4096]{2,1,0:T(8,128)(2,1)} %down_ref.1), custom_call_target="tpu_custom_call" | custom-call | bytes 18874368 | tf_op jit(solution)/shard_map/load/pallas_call | solution.py:101
  12.3 1.5 %collective-permute-start.3 = (bf16[24,1024]{1,0:T(8,128)(2,1)S(1)}, bf16[24,1024]{1,0:T(8,128)(2,1)S(1)}, u32[]{:S(2)}, u32[]{:S(2)}) collective-permute-start(bf16[24,1024]{1,0:T(8,128)(2,1)S(1)} %relay.2.refs_3_), channel_id=1, source_target_pairs={{0,2},{1,3},{2,0},{3,1},{4,6},{5,7},{6,4},{7,5},{8,10},{9,11},{10,... | collective-permute-start | bytes 147464 | tf_op jit(solution)/shard_map/ppermute | solution.py:66
  13.8 1.5 %collective-permute-start.7 = (bf16[24,1024]{1,0:T(8,128)(2,1)S(1)}, bf16[24,1024]{1,0:T(8,128)(2,1)S(1)}, u32[]{:S(2)}, u32[]{:S(2)}) collective-permute-start(bf16[24,1024]{1,0:T(8,128)(2,1)S(1)} %relay.3.refs_7_), channel_id=1, source_target_pairs={{0,2},{1,3},{2,0},{3,1},{4,6},{5,7},{6,4},{7,5},{8,10},{9,11},{10,... | collective-permute-start | bytes 147464 | tf_op jit(solution)/shard_map/ppermute | solution.py:66
  16.4 1.6 %collective-permute-done.7.refs_8_ = bf16[24,1024]{1,0:T(8,128)(2,1)S(1)} collective-permute-done((bf16[24,1024]{1,0:T(8,128)(2,1)S(1)}, bf16[24,1024]{1,0:T(8,128)(2,1)S(1)}, u32[]{:S(2)}, u32[]{:S(2)}) %collective-permute-start.7) | collective-permute-done | bytes 49184 | tf_op jit(solution)/shard_map/ppermute | solution.py:66
  19.2 1.8 %front.2.hidden_ref = bf16[96,384]{1,0:T(8,128)(2,1)S(1)} custom-call(bf16[24,4096]{1,0:T(8,128)(2,1)S(1)} %get-tuple-element.33.refs_0_, bf16[24,2176]{1,0:T(8,128)(2,1)S(1)} %collective-permute-done.refs_1_.refs_12_.refs_17_, bf16[24,2176]{1,0:T(8,128)(2,1)S(1)} %collective-permute-done.1.refs_2_, bf16[24,1024]{1,0:T(8,128)(2,1)S(1)} %relay.2.refs_3_, ...), custom_call_target="tpu_custom_call" | custom-call | flops 603979776 | bytes 6291456 | tf_op jit(solution)/shard_map/front/pallas_call | solution.py:280
  23.1 1.5 %collective-permute-start.14 = (bf16[48,1024]{1,0:T(8,128)(2,1)S(1)}, bf16[48,1024]{1,0:T(8,128)(2,1)S(1)}, u32[]{:S(2)}, u32[]{:S(2)}) collective-permute-start(bf16[48,1024]{1,0:T(8,128)(2,1)S(1)} %get-tuple-element.46), channel_id=1, source_target_pairs={{0,2},{1,3},{2,0},{3,1},{4,6},{5,7},{6,4},{7,5},{8,10},{9,11},{10,... | collective-permute-start | bytes 294920 | tf_op jit(solution)/shard_map/ppermute | solution.py:66
  25.5 3.3 %collective-permute-done.14.came_ref = bf16[48,1024]{1,0:T(8,128)(2,1)S(1)} collective-permute-done((bf16[48,1024]{1,0:T(8,128)(2,1)S(1)}, bf16[48,1024]{1,0:T(8,128)(2,1)S(1)}, u32[]{:S(2)}, u32[]{:S(2)}) %collective-permute-start.14) | collective-permute-done | bytes 98336 | tf_op jit(solution)/shard_map/ppermute | solution.py:66
  28.9 3.1 %collective-permute-start.15 = (bf16[24,1024]{1,0:T(8,128)(2,1)S(1)}, bf16[24,1024]{1,0:T(8,128)(2,1)S(1)}, u32[]{:S(2)}, u32[]{:S(2)}) collective-permute-start(bf16[24,1024]{1,0:T(8,128)(2,1)S(1)} %get-tuple-element.47), channel_id=1, source_target_pairs={{0,8},{4,12},{8,0},{12,4},{1,9},{5,13},{9,1},{13,5},{2,10},{6,14},... | collective-permute-start | bytes 147464 | tf_op jit(solution)/shard_map/ppermute | solution.py:66
  34.2 3.6 %collective-permute-done.16.refs_3_ = bf16[24,1024]{1,0:T(8,128)(2,1)S(1)} collective-permute-done((bf16[24,1024]{1,0:T(8,128)(2,1)S(1)}, bf16[24,1024]{1,0:T(8,128)(2,1)S(1)}, u32[]{:S(2)}, u32[]{:S(2)}) %collective-permute-start.16) | collective-permute-done | bytes 49184 | tf_op jit(solution)/shard_map/ppermute | solution.py:66
  37.8 1.4 %move.2 = (bf16[32,1024]{1,0:T(8,128)(2,1)S(1)}, bf16[24,1024]{1,0:T(8,128)(2,1)S(1)}, bf16[24,1024]{1,0:T(8,128)(2,1)S(1)}, bf16[24,1024]{1,0:T(8,128)(2,1)S(1)}, bf16[24,1024]{1,0:T(8,128)(2,1)S(1)}) custom-call(bf16[32,1024]{1,0:T(8,128)(2,1)S(1)} %get-tuple-element.32.own_ref, s32[2,2,32]{2,1,0:T(2,128)S(1)} %bitcast.6, ...), custom_call_target="tpu_custom_call" | custom-call | tf_op jit(solution)/shard_map/move/pallas_call | solution.py:356
  39.3 2.7 %collective-permute-start.24 = (bf16[24,1024]{1,0:T(8,128)(2,1)S(1)}, bf16[24,1024]{1,0:T(8,128)(2,1)S(1)}, u32[]{:S(2)}, u32[]{:S(2)}) collective-permute-start(bf16[24,1024]{1,0:T(8,128)(2,1)S(1)} %get-tuple-element.52), channel_id=1, source_target_pairs={{0,8},{4,12},{8,0},{12,4},{1,9},{5,13},{9,1},{13,5},{2,10},{6,14},... | collective-permute-start | bytes 147464 | tf_op jit(solution)/shard_map/ppermute | solution.py:66
  41.9 1.7 %collective-permute-start.28 = (bf16[24,1024]{1,0:T(8,128)(2,1)S(1)}, bf16[24,1024]{1,0:T(8,128)(2,1)S(1)}, u32[]{:S(2)}, u32[]{:S(2)}) collective-permute-start(bf16[24,1024]{1,0:T(8,128)(2,1)S(1)} %get-tuple-element.53), channel_id=1, source_target_pairs={{0,12},{4,8},{8,4},{12,0},{1,13},{5,9},{9,5},{13,1},{2,14},{6,10},... | collective-permute-start | bytes 147464 | tf_op jit(solution)/shard_map/ppermute | solution.py:66
  50.3 1.7 %collective-permute-done.29.refs_13_ = bf16[24,1024]{1,0:T(8,128)(2,1)S(1)} collective-permute-done((bf16[24,1024]{1,0:T(8,128)(2,1)S(1)}, bf16[24,1024]{1,0:T(8,128)(2,1)S(1)}, u32[]{:S(2)}, u32[]{:S(2)}) %collective-permute-start.29) | collective-permute-done | bytes 49184 | tf_op jit(solution)/shard_map/ppermute | solution.py:66
  53.7 2.0 %front.3.hidden_ref = bf16[96,384]{1,0:T(8,128)(2,1)S(1)} custom-call(bf16[24,1024]{1,0:T(8,128)(2,1)S(1)} %get-tuple-element.50.refs_0_, bf16[24,1024]{1,0:T(8,128)(2,1)S(1)} %collective-permute-done.17.refs_1_, bf16[24,1024]{1,0:T(8,128)(2,1)S(1)} %collective-permute-done.18.refs_2_, bf16[24,1024]{1,0:T(8,128)(2,1)S(1)} %collective-permute-done.19.refs_3_, ...), custom_call_target="tpu_custom_call" | custom-call | flops 603979776 | bytes 6291456 | tf_op jit(solution)/shard_map/front/pallas_call | solution.py:280
  57.7 1.1 %collective-permute-start.36 = (bf16[48,1024]{1,0:T(8,128)(2,1)S(1)}, bf16[48,1024]{1,0:T(8,128)(2,1)S(1)}, u32[]{:S(2)}, u32[]{:S(2)}) collective-permute-start(bf16[48,1024]{1,0:T(8,128)(2,1)S(1)} %get-tuple-element.59), channel_id=1, source_target_pairs={{0,2},{1,3},{2,0},{3,1},{4,6},{5,7},{6,4},{7,5},{8,10},{9,11},{10,... | collective-permute-start | bytes 294920 | tf_op jit(solution)/shard_map/ppermute | solution.py:66
  60.1 3.3 %collective-permute-done.36.came_ref = bf16[48,1024]{1,0:T(8,128)(2,1)S(1)} collective-permute-done((bf16[48,1024]{1,0:T(8,128)(2,1)S(1)}, bf16[48,1024]{1,0:T(8,128)(2,1)S(1)}, u32[]{:S(2)}, u32[]{:S(2)}) %collective-permute-start.36) | collective-permute-done | bytes 98336 | tf_op jit(solution)/shard_map/ppermute | solution.py:66
  63.8 1.6 %collective-permute-start.38 = (bf16[24,1024]{1,0:T(8,128)(2,1)S(1)}, bf16[24,1024]{1,0:T(8,128)(2,1)S(1)}, u32[]{:S(2)}, u32[]{:S(2)}) collective-permute-start(bf16[24,1024]{1,0:T(8,128)(2,1)S(1)} %get-tuple-element.61), channel_id=1, source_target_pairs={{0,12},{4,8},{8,4},{12,0},{1,13},{5,9},{9,5},{13,1},{2,14},{6,10},... | collective-permute-start | bytes 147464 | tf_op jit(solution)/shard_map/ppermute | solution.py:66
  65.4 1.7 %collective-permute-start.35 = (bf16[24,1024]{1,0:T(8,128)(2,1)S(1)}, bf16[24,1024]{1,0:T(8,128)(2,1)S(1)}, u32[]{:S(2)}, u32[]{:S(2)}) collective-permute-start(bf16[24,1024]{1,0:T(8,128)(2,1)S(1)} %get-tuple-element.57), channel_id=1, source_target_pairs={{0,4},{4,0},{8,12},{12,8},{1,5},{5,1},{9,13},{13,9},{2,6},{6,2},{1... | collective-permute-start | bytes 147464 | tf_op jit(solution)/shard_map/ppermute | solution.py:66
  67.1 1.4 %collective-permute-done.37.refs_2_ = bf16[24,1024]{1,0:T(8,128)(2,1)S(1)} collective-permute-done((bf16[24,1024]{1,0:T(8,128)(2,1)S(1)}, bf16[24,1024]{1,0:T(8,128)(2,1)S(1)}, u32[]{:S(2)}, u32[]{:S(2)}) %collective-permute-start.37) | collective-permute-done | bytes 49184 | tf_op jit(solution)/shard_map/ppermute | solution.py:66
  68.5 1.3 %collective-permute-done.38.refs_3_ = bf16[24,1024]{1,0:T(8,128)(2,1)S(1)} collective-permute-done((bf16[24,1024]{1,0:T(8,128)(2,1)S(1)}, bf16[24,1024]{1,0:T(8,128)(2,1)S(1)}, u32[]{:S(2)}, u32[]{:S(2)}) %collective-permute-start.38) | collective-permute-done | bytes 49184 | tf_op jit(solution)/shard_map/ppermute | solution.py:66
  70.1 1.4 %move.3 = (bf16[32,1024]{1,0:T(8,128)(2,1)}, bf16[32,1024]{1,0:T(8,128)(2,1)}) custom-call(bf16[32,1024]{1,0:T(8,128)(2,1)S(1)} %get-tuple-element.49.own_ref, s32[2,2,32]{2,1,0:T(2,128)S(1)} %bitcast.7, bf16[24,1024]{1,0:T(8,128)(2,1)S(1)} %get-tuple-element.56.refs_0_, bf16[24,1024]{1,0:T(8,128)(2,1)S(1)} %collective-permute-done.35.refs_1_, ...), custom_call_target="tpu_custom_call" | custom-call | tf_op jit(solution)/shard_map/move/pallas_call | solution.py:356
  (83 shorter events, 20.8 us)
Async XLA Ops:
  2.1 6.0 %collective-permute-start = (bf16[24,2176]{1,0:T(8,128)(2,1)S(1)}, bf16[24,2176]{1,0:T(8,128)(2,1)S(1)}, u32[]{:S(2)}, u32[]{:S(2)}) collective-permute-start(bf16[24,2176]{1,0:T(8,128)(2,1)S(1)} %get-tuple-element.34), channel_id=1, source_target_pairs={{0,4},{4,0},{8,12},{12,8},{1,5},{5,1},{9,13},{13,9},{2,6},{6,2},{1... | collective-permute-start | bytes 313352 | tf_op jit(solution)/shard_map/ppermute | solution.py:66
  5.1 7.2 %collective-permute-start.2 = (bf16[24,1152]{1,0:T(8,128)(2,1)S(1)}, bf16[24,1152]{1,0:T(8,128)(2,1)S(1)}, u32[]{:S(2)}, u32[]{:S(2)}) collective-permute-start(bf16[24,1152]{1,0:T(8,128)(2,1)S(1)} %get-tuple-element.35), channel_id=1, source_target_pairs={{0,8},{4,12},{8,0},{12,4},{1,9},{5,13},{9,1},{13,5},{2,10},{6,14},... | collective-permute-start | bytes 165896 | tf_op jit(solution)/shard_map/ppermute | solution.py:66
  7.7 6.1 %collective-permute-start.6 = (bf16[24,1152]{1,0:T(8,128)(2,1)S(1)}, bf16[24,1152]{1,0:T(8,128)(2,1)S(1)}, u32[]{:S(2)}, u32[]{:S(2)}) collective-permute-start(bf16[24,1152]{1,0:T(8,128)(2,1)S(1)} %get-tuple-element.37), channel_id=1, source_target_pairs={{0,12},{4,8},{8,4},{12,0},{1,13},{5,9},{9,5},{13,1},{2,14},{6,10},... | collective-permute-start | bytes 165896 | tf_op jit(solution)/shard_map/ppermute | solution.py:66
  8.1 11.1 %collective-permute-start.1 = (bf16[24,2176]{1,0:T(8,128)(2,1)S(1)}, bf16[24,2176]{1,0:T(8,128)(2,1)S(1)}, u32[]{:S(2)}, u32[]{:S(2)}) collective-permute-start(bf16[24,2176]{1,0:T(8,128)(2,1)S(1)} %collective-permute-done.refs_1_.refs_12_.refs_17_), channel_id=1, source_target_pairs={{0,1},{1,0},{2,3},{3,2},{4,5},{5,4},{6,7},{7,6},{8,9},{9,8},{10,11... | collective-permute-start | bytes 313352 | tf_op jit(solution)/shard_map/ppermute | solution.py:66
  12.3 4.1 %collective-permute-start.3 = (bf16[24,1024]{1,0:T(8,128)(2,1)S(1)}, bf16[24,1024]{1,0:T(8,128)(2,1)S(1)}, u32[]{:S(2)}, u32[]{:S(2)}) collective-permute-start(bf16[24,1024]{1,0:T(8,128)(2,1)S(1)} %relay.2.refs_3_), channel_id=1, source_target_pairs={{0,2},{1,3},{2,0},{3,1},{4,6},{5,7},{6,4},{7,5},{8,10},{9,11},{10,... | collective-permute-start | bytes 147464 | tf_op jit(solution)/shard_map/ppermute | solution.py:66
  13.8 4.2 %collective-permute-start.7 = (bf16[24,1024]{1,0:T(8,128)(2,1)S(1)}, bf16[24,1024]{1,0:T(8,128)(2,1)S(1)}, u32[]{:S(2)}, u32[]{:S(2)}) collective-permute-start(bf16[24,1024]{1,0:T(8,128)(2,1)S(1)} %relay.3.refs_7_), channel_id=1, source_target_pairs={{0,2},{1,3},{2,0},{3,1},{4,6},{5,7},{6,4},{7,5},{8,10},{9,11},{10,... | collective-permute-start | bytes 147464 | tf_op jit(solution)/shard_map/ppermute | solution.py:66
  23.1 5.7 %collective-permute-start.14 = (bf16[48,1024]{1,0:T(8,128)(2,1)S(1)}, bf16[48,1024]{1,0:T(8,128)(2,1)S(1)}, u32[]{:S(2)}, u32[]{:S(2)}) collective-permute-start(bf16[48,1024]{1,0:T(8,128)(2,1)S(1)} %get-tuple-element.46), channel_id=1, source_target_pairs={{0,2},{1,3},{2,0},{3,1},{4,6},{5,7},{6,4},{7,5},{8,10},{9,11},{10,... | collective-permute-start | bytes 294920 | tf_op jit(solution)/shard_map/ppermute | solution.py:66
  24.6 8.4 %collective-permute-start.12 = (bf16[48,1024]{1,0:T(8,128)(2,1)S(1)}, bf16[48,1024]{1,0:T(8,128)(2,1)S(1)}, u32[]{:S(2)}, u32[]{:S(2)}) collective-permute-start(bf16[48,1024]{1,0:T(8,128)(2,1)S(1)} %get-tuple-element.42), channel_id=1, source_target_pairs={{0,2},{1,3},{2,0},{3,1},{4,6},{5,7},{6,4},{7,5},{8,10},{9,11},{10,... | collective-permute-start | bytes 294920 | tf_op jit(solution)/shard_map/ppermute | solution.py:66
  28.9 5.3 %collective-permute-start.15 = (bf16[24,1024]{1,0:T(8,128)(2,1)S(1)}, bf16[24,1024]{1,0:T(8,128)(2,1)S(1)}, u32[]{:S(2)}, u32[]{:S(2)}) collective-permute-start(bf16[24,1024]{1,0:T(8,128)(2,1)S(1)} %get-tuple-element.47), channel_id=1, source_target_pairs={{0,8},{4,12},{8,0},{12,4},{1,9},{5,13},{9,1},{13,5},{2,10},{6,14},... | collective-permute-start | bytes 147464 | tf_op jit(solution)/shard_map/ppermute | solution.py:66
  31.9 5.9 %collective-permute-start.16 = (bf16[24,1024]{1,0:T(8,128)(2,1)S(1)}, bf16[24,1024]{1,0:T(8,128)(2,1)S(1)}, u32[]{:S(2)}, u32[]{:S(2)}) collective-permute-start(bf16[24,1024]{1,0:T(8,128)(2,1)S(1)} %get-tuple-element.48), channel_id=1, source_target_pairs={{0,12},{4,8},{8,4},{12,0},{1,13},{5,9},{9,5},{13,1},{2,14},{6,10},... | collective-permute-start | bytes 147464 | tf_op jit(solution)/shard_map/ppermute | solution.py:66
  33.1 4.8 %collective-permute-start.13 = (bf16[24,1024]{1,0:T(8,128)(2,1)S(1)}, bf16[24,1024]{1,0:T(8,128)(2,1)S(1)}, u32[]{:S(2)}, u32[]{:S(2)}) collective-permute-start(bf16[24,1024]{1,0:T(8,128)(2,1)S(1)} %get-tuple-element.44), channel_id=1, source_target_pairs={{0,4},{4,0},{8,12},{12,8},{1,5},{5,1},{9,13},{13,9},{2,6},{6,2},{1... | collective-permute-start | bytes 147464 | tf_op jit(solution)/shard_map/ppermute | solution.py:66
  39.2 5.5 %collective-permute-start.20 = (bf16[24,1024]{1,0:T(8,128)(2,1)S(1)}, bf16[24,1024]{1,0:T(8,128)(2,1)S(1)}, u32[]{:S(2)}, u32[]{:S(2)}) collective-permute-start(bf16[24,1024]{1,0:T(8,128)(2,1)S(1)} %get-tuple-element.51), channel_id=1, source_target_pairs={{0,4},{4,0},{8,12},{12,8},{1,5},{5,1},{9,13},{13,9},{2,6},{6,2},{1... | collective-permute-start | bytes 147464 | tf_op jit(solution)/shard_map/ppermute | solution.py:66
  39.3 6.4 %collective-permute-start.24 = (bf16[24,1024]{1,0:T(8,128)(2,1)S(1)}, bf16[24,1024]{1,0:T(8,128)(2,1)S(1)}, u32[]{:S(2)}, u32[]{:S(2)}) collective-permute-start(bf16[24,1024]{1,0:T(8,128)(2,1)S(1)} %get-tuple-element.52), channel_id=1, source_target_pairs={{0,8},{4,12},{8,0},{12,4},{1,9},{5,13},{9,1},{13,5},{2,10},{6,14},... | collective-permute-start | bytes 147464 | tf_op jit(solution)/shard_map/ppermute | solution.py:66
  41.9 5.9 %collective-permute-start.28 = (bf16[24,1024]{1,0:T(8,128)(2,1)S(1)}, bf16[24,1024]{1,0:T(8,128)(2,1)S(1)}, u32[]{:S(2)}, u32[]{:S(2)}) collective-permute-start(bf16[24,1024]{1,0:T(8,128)(2,1)S(1)} %get-tuple-element.53), channel_id=1, source_target_pairs={{0,12},{4,8},{8,4},{12,0},{1,13},{5,9},{9,5},{13,1},{2,14},{6,10},... | collective-permute-start | bytes 147464 | tf_op jit(solution)/shard_map/ppermute | solution.py:66
  43.6 5.2 %collective-permute-start.17 = (bf16[24,1024]{1,0:T(8,128)(2,1)S(1)}, bf16[24,1024]{1,0:T(8,128)(2,1)S(1)}, u32[]{:S(2)}, u32[]{:S(2)}) collective-permute-start(bf16[24,1024]{1,0:T(8,128)(2,1)S(1)} %get-tuple-element.50.refs_0_), channel_id=1, source_target_pairs={{0,2},{1,3},{2,0},{3,1},{4,6},{5,7},{6,4},{7,5},{8,10},{9,11},{10,... | collective-permute-start | bytes 147464 | tf_op jit(solution)/shard_map/ppermute | solution.py:66
  44.7 4.2 %collective-permute-start.18 = (bf16[24,1024]{1,0:T(8,128)(2,1)S(1)}, bf16[24,1024]{1,0:T(8,128)(2,1)S(1)}, u32[]{:S(2)}, u32[]{:S(2)}) collective-permute-start(bf16[24,1024]{1,0:T(8,128)(2,1)S(1)} %get-tuple-element.50.refs_0_), channel_id=1, source_target_pairs={{0,1},{1,0},{2,3},{3,2},{4,5},{5,4},{6,7},{7,6},{8,9},{9,8},{10,11... | collective-permute-start | bytes 147464 | tf_op jit(solution)/shard_map/ppermute | solution.py:66
  44.7 4.7 %collective-permute-start.21 = (bf16[24,1024]{1,0:T(8,128)(2,1)S(1)}, bf16[24,1024]{1,0:T(8,128)(2,1)S(1)}, u32[]{:S(2)}, u32[]{:S(2)}) collective-permute-start(bf16[24,1024]{1,0:T(8,128)(2,1)S(1)} %collective-permute-done.20.refs_4_), channel_id=1, source_target_pairs={{0,2},{1,3},{2,0},{3,1},{4,6},{5,7},{6,4},{7,5},{8,10},{9,11},{10,... | collective-permute-start | bytes 147464 | tf_op jit(solution)/shard_map/ppermute | solution.py:66
  45.7 4.6 %collective-permute-start.25 = (bf16[24,1024]{1,0:T(8,128)(2,1)S(1)}, bf16[24,1024]{1,0:T(8,128)(2,1)S(1)}, u32[]{:S(2)}, u32[]{:S(2)}) collective-permute-start(bf16[24,1024]{1,0:T(8,128)(2,1)S(1)} %collective-permute-done.24.refs_8_), channel_id=1, source_target_pairs={{0,2},{1,3},{2,0},{3,1},{4,6},{5,7},{6,4},{7,5},{8,10},{9,11},{10,... | collective-permute-start | bytes 147464 | tf_op jit(solution)/shard_map/ppermute | solution.py:66
  47.8 4.1 %collective-permute-start.29 = (bf16[24,1024]{1,0:T(8,128)(2,1)S(1)}, bf16[24,1024]{1,0:T(8,128)(2,1)S(1)}, u32[]{:S(2)}, u32[]{:S(2)}) collective-permute-start(bf16[24,1024]{1,0:T(8,128)(2,1)S(1)} %collective-permute-done.28.refs_12_), channel_id=1, source_target_pairs={{0,2},{1,3},{2,0},{3,1},{4,6},{5,7},{6,4},{7,5},{8,10},{9,11},{10,... | collective-permute-start | bytes 147464 | tf_op jit(solution)/shard_map/ppermute | solution.py:66
  57.7 5.7 %collective-permute-start.36 = (bf16[48,1024]{1,0:T(8,128)(2,1)S(1)}, bf16[48,1024]{1,0:T(8,128)(2,1)S(1)}, u32[]{:S(2)}, u32[]{:S(2)}) collective-permute-start(bf16[48,1024]{1,0:T(8,128)(2,1)S(1)} %get-tuple-element.59), channel_id=1, source_target_pairs={{0,2},{1,3},{2,0},{3,1},{4,6},{5,7},{6,4},{7,5},{8,10},{9,11},{10,... | collective-permute-start | bytes 294920 | tf_op jit(solution)/shard_map/ppermute | solution.py:66
  58.9 6.5 %collective-permute-start.34 = (bf16[48,1024]{1,0:T(8,128)(2,1)S(1)}, bf16[48,1024]{1,0:T(8,128)(2,1)S(1)}, u32[]{:S(2)}, u32[]{:S(2)}) collective-permute-start(bf16[48,1024]{1,0:T(8,128)(2,1)S(1)} %get-tuple-element.55), channel_id=1, source_target_pairs={{0,2},{1,3},{2,0},{3,1},{4,6},{5,7},{6,4},{7,5},{8,10},{9,11},{10,... | collective-permute-start | bytes 294920 | tf_op jit(solution)/shard_map/ppermute | solution.py:66
  63.5 5.1 %collective-permute-start.37 = (bf16[24,1024]{1,0:T(8,128)(2,1)S(1)}, bf16[24,1024]{1,0:T(8,128)(2,1)S(1)}, u32[]{:S(2)}, u32[]{:S(2)}) collective-permute-start(bf16[24,1024]{1,0:T(8,128)(2,1)S(1)} %get-tuple-element.60), channel_id=1, source_target_pairs={{0,8},{4,12},{8,0},{12,4},{1,9},{5,13},{9,1},{13,5},{2,10},{6,14},... | collective-permute-start | bytes 147464 | tf_op jit(solution)/shard_map/ppermute | solution.py:66
  63.8 6.0 %collective-permute-start.38 = (bf16[24,1024]{1,0:T(8,128)(2,1)S(1)}, bf16[24,1024]{1,0:T(8,128)(2,1)S(1)}, u32[]{:S(2)}, u32[]{:S(2)}) collective-permute-start(bf16[24,1024]{1,0:T(8,128)(2,1)S(1)} %get-tuple-element.61), channel_id=1, source_target_pairs={{0,12},{4,8},{8,4},{12,0},{1,13},{5,9},{9,5},{13,1},{2,14},{6,10},... | collective-permute-start | bytes 147464 | tf_op jit(solution)/shard_map/ppermute | solution.py:66
  65.4 4.7 %collective-permute-start.35 = (bf16[24,1024]{1,0:T(8,128)(2,1)S(1)}, bf16[24,1024]{1,0:T(8,128)(2,1)S(1)}, u32[]{:S(2)}, u32[]{:S(2)}) collective-permute-start(bf16[24,1024]{1,0:T(8,128)(2,1)S(1)} %get-tuple-element.57), channel_id=1, source_target_pairs={{0,4},{4,0},{8,12},{12,8},{1,5},{5,1},{9,13},{13,9},{2,6},{6,2},{1... | collective-permute-start | bytes 147464 | tf_op jit(solution)/shard_map/ppermute | solution.py:66
  (19 other events, 78.2 us)

commit v6 on v5

--- a/solution.py
+++ b/solution.py
@@ -127,46 +127,47 @@
     )(block, done)
 
 
-def choose(ids, expert, slots):
-    picks, rows = ids.shape
-    named = jnp.zeros((1, rows), jnp.float32)
-    for k in range(picks):
-        named += jnp.where(ids[k : k + 1, :] == expert, 1.0, 0.0)
-    named = jnp.broadcast_to(named, (slots, rows))
+def choices(ids, peers, slots):
+    rows = ids[0].shape[1]
+    me = lax.axis_index("ep")
+    named = []
+    for one in ids:
+        for k in range(peers):
+            hits = [jnp.where(one[p : p + 1, :] == me ^ k, 1.0, 0.0) for p in range(one.shape[0])]
+            named.append(sum(hits))
     earlier = lax.broadcasted_iota(jnp.int32, (rows, rows), 0) < lax.broadcasted_iota(jnp.int32, (rows, rows), 1)
     ahead = jnp.dot(
-        named.astype(jnp.bfloat16),
+        jnp.concatenate(named, axis=0).astype(jnp.bfloat16),
         jnp.where(earlier, 1.0, 0.0).astype(jnp.bfloat16),
         preferred_element_type=jnp.float32,
-    )
+    ).astype(jnp.int32)
     slot = lax.broadcasted_iota(jnp.int32, (slots, rows), 0)
-    return jnp.where((ahead.astype(jnp.int32) == slot) & (named > 0.5), 1.0, 0.0)
-
-
-def select(one_hot, values):
-    one_hot = one_hot.astype(jnp.bfloat16)
-    return jnp.dot(one_hot, values, preferred_element_type=jnp.float32).astype(jnp.bfloat16)
-
-
-def flags_of(ids, section, experts):
-    picks, rows = ids.shape
-    lane = lax.broadcasted_iota(jnp.int32, (LANES, rows), 0)
-    flags = jnp.zeros(lane.shape, jnp.float32)
-    for k in range(picks):
-        flags += jnp.where(ids[k : k + 1, :] + section * experts == lane, 1.0, 0.0)
-    return flags.T.astype(jnp.bfloat16)
-
-
-def chosen_flags(ids, peer, experts, slots):
-    picked = [choose(one, lax.axis_index("ep") ^ peer, slots) for one in ids]
-    parts = [select(p, flags_of(one, s, experts)) for s, (p, one) in enumerate(zip(picked, ids))]
-    return sum(part.astype(jnp.float32) for part in parts).astype(jnp.bfloat16), picked[0]
+    holds = [jnp.where((ahead[i : i + 1, :] == slot) & (row > 0.5), 1.0, 0.0) for i, row in enumerate(named)]
+    return [jnp.concatenate(holds[s * peers : (s + 1) * peers], axis=0) for s in range(len(ids))]
+
+
+def narrow(x):
+    return x.astype(jnp.bfloat16)
+
+
+def product(x, y):
+    return jnp.dot(narrow(x), narrow(y), preferred_element_type=jnp.float32)
+
+
+def named_experts(ids, held, experts):
+    rows = ids[0].shape[1]
+    flags = []
+    for s, one in enumerate(ids):
+        lane = lax.broadcasted_iota(jnp.int32, (LANES, rows), 0)
+        hits = [jnp.where(one[p : p + 1, :] + s * experts == lane, 1.0, 0.0) for p in range(one.shape[0])]
+        flags.append(product(held[s], sum(hits).T))
+    return sum(flags)
 
 
 def pack_kernel(experts, tokens_ref, ids_ref, *refs):
-    wide_ref, *out_refs, own_ref, half_ref, held_ref, sems = refs
-    width = tokens_ref.shape[1]
-    half, quarter = width // 2, width // 4
+    *out_refs, own_ref, half_ref, held_ref, sems = refs
+    quarter = tokens_ref.shape[1] // 4
+    half = 2 * quarter
     where = lax.axis_index("et")
     copies = [
         pltpu.make_async_copy(ids_ref, held_ref, sems.at[0]),
@@ -177,22 +178,22 @@
         copy.start()
     copies[0].wait()
     ids = [held_ref[s] for s in range(held_ref.shape[0])]
-    slots = wide_ref.shape[0]
-    made = [chosen_flags(ids, k + 1, experts, slots) for k in range(1 + len(out_refs))]
+    slots, peers = out_refs[0].shape[0], 1 + len(out_refs)
+    held = choices(ids, peers, slots)
+    flags = named_experts(ids, held, experts)
     copies[1].wait()
     copies[2].wait()
     own_ref[...] = half_ref[:, aligned(where >> 1, quarter)]
-    wide_ref[:, :half] = select(made[0][1], half_ref[...])
-    wide_ref[:, half:] = made[0][0]
-    for (flags, picked), out_ref in zip(made[1:], out_refs):
-        out_ref[:, :quarter] = select(picked, own_ref[...])
-        out_ref[:, quarter:] = flags
+    picked = product(held[0][slots:], half_ref[...])
+    for k, out_ref in enumerate(out_refs):
+        out_ref[:, :half] = narrow(picked[k * slots : (k + 1) * slots])
+        out_ref[:, half:] = narrow(flags[(k + 1) * slots : (k + 2) * slots])
 
 
 def pack(tokens, ids, experts, slots):
     rows, width = tokens.shape
-    far = lax.axis_size("ep") - 2
-    shapes = [(slots, width // 2 + LANES)] + [(slots, width // 4 + LANES)] * far + [(rows, width // 4)]
+    others = lax.axis_size("ep") - 1
+    shapes = [(slots, width // 2 + LANES)] * others + [(rows, width // 4)]
     return pl.pallas_call(
         functools.partial(pack_kernel, experts),
         in_specs=[ANY] * 2,
@@ -208,14 +209,21 @@
     )(tokens, ids)
 
 
-def own_kernel(experts, tokens_ref, ids_ref, out_ref, flags_ref):
+def own_kernel(experts, tokens_ref, ids_ref, out_ref, flags_ref, *choice_refs):
     ids = [ids_ref[s] for s in range(ids_ref.shape[0])]
-    flags_ref[...], picked = chosen_flags(ids, 0, experts, out_ref.shape[0])
-    out_ref[...] = select(picked, tokens_ref[...])
+    slots = out_ref.shape[0]
+    held = choices(ids, choice_refs[0].shape[0] // slots, slots)
+    flags_ref[...] = narrow(named_experts(ids, held, experts)[:slots])
+    out_ref[...] = narrow(product(held[0][:slots], tokens_ref[...]))
+    for s, one in enumerate(held):
+        choice_refs[2 * s][...] = narrow(one)
+        choice_refs[2 * s + 1][...] = narrow(one.T)
 
 
 def own_rows(tokens, ids, experts, slots):
-    shapes = [(slots, tokens.shape[1]), (slots, LANES)]
+    rows, width = tokens.shape
+    total = lax.axis_size("ep") * slots
+    shapes = [(slots, width), (slots, LANES)] + [(total, rows), (rows, total)] * ids.shape[0]
     return pl.pallas_call(
         functools.partial(own_kernel, experts),
         out_shape=[jax.ShapeDtypeStruct(s, jnp.bfloat16) for s in shapes],
@@ -334,34 +342,32 @@
     )(keep, came)
 
 
-def move_kernel(section, n_came, own_ref, ids_ref, *refs):
+def move_kernel(n_came, last, own_ref, back_ref, pick_ref, *refs):
     came, outs = refs[:n_came], refs[n_came:]
-    peer = lax.axis_index("ep")
-    slots = came[0].shape[0]
-    velocity = jnp.zeros(own_ref.shape, jnp.float32)
-    for k, ref in enumerate(came):
-        back = choose(ids_ref[section], peer ^ k, slots).T.astype(jnp.bfloat16)
-        velocity += jnp.dot(back, ref[...], preferred_element_type=jnp.float32)
-    moved = (own_ref[...].astype(jnp.float32) - 0.5 * velocity).astype(jnp.bfloat16)
+    rows = [ref[...].astype(jnp.float32) for ref in came]
+    velocity = product(back_ref[...], jnp.concatenate(rows, axis=0))
+    moved = narrow(own_ref[...].astype(jnp.float32) - 0.5 * velocity)
     outs[0][...] = moved
-    if len(outs) == 2:
-        outs[1][...] = velocity.astype(jnp.bfloat16)
+    if last:
+        outs[1][...] = narrow(velocity)
     else:
+        slots = came[0].shape[0]
+        picked = product(pick_ref[...], moved)
         for k, out in enumerate(outs[1:]):
-            out[...] = select(choose(ids_ref[section + 1], peer ^ k, slots), moved)
-
-
-def move(section, own, ids, came):
-    shapes = [own.shape] + ([own.shape] if section + 1 == ids.shape[0] else [c.shape for c in came])
-    return pl.pallas_call(
-        functools.partial(move_kernel, section, len(came)),
+            out[...] = narrow(picked[k * slots : (k + 1) * slots])
+
+
+def move(own, back, pick, came, last):
+    shapes = [own.shape] + ([own.shape] if last else [c.shape for c in came])
+    return pl.pallas_call(
+        functools.partial(move_kernel, len(came), last),
         out_shape=[jax.ShapeDtypeStruct(s, jnp.bfloat16) for s in shapes],
         compiler_params=params(),
         name="move",
-    )(own, ids, *came)
-
-
-def sum_back(section, hidden, w_down, own, ids):
+    )(own, back, pick, *came)
+
+
+def sum_back(hidden, w_down, own, back, pick, last_section):
     peers = lax.axis_size("ep")
     some = peers // 2
     far = swap(down(hidden, w_down, 3, 1)[0], "et", 1)
@@ -371,7 +377,8 @@
     keep_first, keep_last = down(hidden, w_down, 0, 2, (near,), jnp.float32)
     later = add(keep_last, last, peers - some)
     blocks = add(keep_first, first, some) + later
-    return move(section, own, ids, [swap(b, "ep", k) if k else b for k, b in enumerate(blocks)])
+    came = [swap(b, "ep", k) if k else b for k, b in enumerate(blocks)]
+    return move(own, back, pick, came, last_section)
 
 
 def spread(block, quarter):
@@ -389,18 +396,21 @@
     slots = 3 * rows * expert_ids.shape[2] // (2 * experts)
     ids = expert_ids.transpose(0, 2, 1)
 
-    wide, *packed, own = pack(tokens, ids, experts, slots)
+    *packed, own = pack(tokens, ids, experts, slots)
     pair, w_down, done = load(gate_weight, up_weight, down_weight)
-    mine, flags = own_rows(tokens, ids, experts, slots)
-    flags = [flags, swap(wide, "ep", 1)] + [swap(p, "ep", k + 2) for k, p in enumerate(packed)]
-    blocks = [[(mine, width, 0)], [(flags[1], half, 0), (swap(flags[1], "et", 1), half, 1)]]
-    blocks += [spread(relay(f, quarter, done), quarter) for f in flags[2:]]
+    mine, flags, *choice = own_rows(tokens, ids, experts, slots)
+    pick, back = choice[2], choice[1::2]
+    flags = [flags] + [swap(p, "ep", k + 1) for k, p in enumerate(packed)]
+    blocks = [[(mine, width, 0)]]
+    for f in flags[1:]:
+        f = relay(f, half, done)
+        blocks.append([(f, half, 0), (swap(f, "et", 1), half, 1)])
     hidden = front(blocks, flags, 0, modulation, router, pair)
-    own, *sent = sum_back(0, hidden, w_down, own, ids)
+    own, *sent = sum_back(hidden, w_down, own, back[0], pick, False)
 
     blocks = [spread(swap(b, "ep", k) if k else b, quarter) for k, b in enumerate(sent)]
     hidden = front(blocks, flags, 1, modulation, router, pair)
-    return tuple(sum_back(1, hidden, w_down, own, ids))
+    return tuple(sum_back(hidden, w_down, own, back[1], pick, True))
 
 
 def solution(mesh):

time: 71.7 us -> 68.3 us (0.953)
  starting transfers between devices: 32.7 us -> 30.1 us
  Pallas kernels: 14.5 us -> 13.1 us
    ppermute x39 -> x35, starting transfers between devices: 32.7 us -> 30.1 us  [swap(): return lax.ppermute(x, axis, [(i, i ^ bit) for i in range(size)])]
    pallas_call x2, Pallas kernels: 2.8 us -> 1.13 us  [move(): pl.pallas_call(functools.partial(move_kernel, len(came), last), out_shape...]
    ppermute x39 -> x35, waiting for transfers between devices: 23.5 us -> 24 us  [swap(): return lax.ppermute(x, axis, [(i, i ^ bit) for i in range(size)])]
  transfers between devices with their start and end apart: 39 -> 35, of which waited for: 20 -> 18; matrix products, arithmetic and copies ran while one was open for 0% -> 0% of each run, Pallas kernels for 8% -> 9%
where the time goes in v6:
time: 68.3 us; the launch traced here: 68.1 us
  starting transfers between devices  30.1 us (44%)
  waiting for transfers between devices  24 us (35%)
  Pallas kernels  13.1 us (19%)
  between operations  0.85 us (1%)
    ppermute x35, starting transfers between devices, swap(): return lax.ppermute(x, axis, [(i, i ^ bit) for i in range(size)])  30.1 us
    ppermute x35, waiting for transfers between devices, swap(): return lax.ppermute(x, axis, [(i, i ^ bit) for i in range(size)])  24 us
    pallas_call x1, Pallas kernels, load(): pl.pallas_call(load_kernel, in_specs=[ANY] * 3, out_specs=[VMEM] * 3, out...  3.82 us
    pallas_call x2, Pallas kernels, front(): pl.pallas_call(functools.partial(front_kernel, layout, section, experts,...  3.81 us
    pallas_call x8, Pallas kernels, down(): pl.pallas_call(functools.partial(down_kernel, flip, len(adds)), in_specs=...  2.25 us
  transfers between devices with their start and end apart: 35, of which 18 were waited for; matrix products, arithmetic and copies ran while one was open for 0% of the time, Pallas kernels for 9%

profile of v6, /device:TPU:0, one launch (start us, length us, event | category | flops | bytes accessed | tf_op | source)
XLA Modules:
  0.0 68.1 jit_solution(18239683563715661062)
XLA Ops:
  0.6 1.2 %pack.1 = (bf16[24,2176]{1,0:T(8,128)(2,1)S(1)}, bf16[24,2176]{1,0:T(8,128)(2,1)S(1)}, bf16[24,2176]{1,0:T(8,128)(2,1)S(1)}, bf16[32,1024]{1,0:T(8,128)(2,1)S(1)}) custom-call(bf16[32,4096]{1,0:T(8,128)(2,1)} %tokens_ref.3, s32[2,2,32]{2,1,0:T(2,128)} %bitcast.4), custom_call_target="tpu_custom_call" | custom-call | tf_op jit(solution)/shard_map/pack/pallas_call | solution.py:197
  1.9 3.1 %collective-permute-start = (bf16[24,2176]{1,0:T(8,128)(2,1)S(1)}, bf16[24,2176]{1,0:T(8,128)(2,1)S(1)}, u32[]{:S(2)}, u32[]{:S(2)}) collective-permute-start(bf16[24,2176]{1,0:T(8,128)(2,1)S(1)} %get-tuple-element.39), channel_id=1, source_target_pairs={{0,4},{4,0},{8,12},{12,8},{1,5},{5,1},{9,13},{13,9},{2,6},{6,2},{1... | collective-permute-start | bytes 313352 | tf_op jit(solution)/shard_map/ppermute | solution.py:66
  4.9 2.6 %collective-permute-start.2 = (bf16[24,2176]{1,0:T(8,128)(2,1)S(1)}, bf16[24,2176]{1,0:T(8,128)(2,1)S(1)}, u32[]{:S(2)}, u32[]{:S(2)}) collective-permute-start(bf16[24,2176]{1,0:T(8,128)(2,1)S(1)} %get-tuple-element.41), channel_id=1, source_target_pairs={{0,8},{4,12},{8,0},{12,4},{1,9},{5,13},{9,1},{13,5},{2,10},{6,14},... | collective-permute-start | bytes 313352 | tf_op jit(solution)/shard_map/ppermute | solution.py:66
  7.6 3.8 %load.1 = (bf16[4096,768]{1,0:T(8,128)(2,1)S(1)}, bf16[384,4096]{1,0:T(8,128)(2,1)S(1)}, f32[8,128]{1,0:T(8,128)S(1)}) custom-call(bf16[1,4096,384]{2,1,0:T(8,128)(2,1)} %gate_ref.1, bf16[1,4096,384]{2,1,0:T(8,128)(2,1)} %up_ref.1, bf16[1,384,4096]{2,1,0:T(8,128)(2,1)} %down_ref.1), custom_call_target="tpu_custom_call" | custom-call | bytes 18874368 | tf_op jit(solution)/shard_map/load/pallas_call | solution.py:101
  11.6 4.3 %collective-permute-done.2.block_ref.refs_9_.refs_18_ = bf16[24,2176]{1,0:T(8,128)(2,1)S(1)} collective-permute-done((bf16[24,2176]{1,0:T(8,128)(2,1)S(1)}, bf16[24,2176]{1,0:T(8,128)(2,1)S(1)}, u32[]{:S(2)}, u32[]{:S(2)}) %collective-permute-start.2) | collective-permute-done | bytes 104480 | tf_op jit(solution)/shard_map/ppermute | solution.py:66
  17.5 1.8 %front.2.hidden_ref = bf16[96,384]{1,0:T(8,128)(2,1)S(1)} custom-call(bf16[24,4096]{1,0:T(8,128)(2,1)S(1)} %get-tuple-element.38.refs_0_, bf16[24,2048]{1,0:T(8,128)(2,1)S(1)} %relay.3.refs_1_, bf16[24,2048]{1,0:T(8,128)(2,1)S(1)} %collective-permute-done.1.refs_2_, bf16[24,2048]{1,0:T(8,128)(2,1)S(1)} %relay.4.refs_3_, ...), custom_call_target="tpu_custom_call" | custom-call | flops 603979776 | bytes 6291456 | tf_op jit(solution)/shard_map/front/pallas_call | solution.py:288
  21.4 1.6 %collective-permute-start.10 = (bf16[48,1024]{1,0:T(8,128)(2,1)S(1)}, bf16[48,1024]{1,0:T(8,128)(2,1)S(1)}, u32[]{:S(2)}, u32[]{:S(2)}) collective-permute-start(bf16[48,1024]{1,0:T(8,128)(2,1)S(1)} %get-tuple-element.51), channel_id=1, source_target_pairs={{0,2},{1,3},{2,0},{3,1},{4,6},{5,7},{6,4},{7,5},{8,10},{9,11},{10,... | collective-permute-start | bytes 294920 | tf_op jit(solution)/shard_map/ppermute | solution.py:66
  23.8 3.3 %collective-permute-done.10.came_ref = bf16[48,1024]{1,0:T(8,128)(2,1)S(1)} collective-permute-done((bf16[48,1024]{1,0:T(8,128)(2,1)S(1)}, bf16[48,1024]{1,0:T(8,128)(2,1)S(1)}, u32[]{:S(2)}, u32[]{:S(2)}) %collective-permute-start.10) | collective-permute-done | bytes 98336 | tf_op jit(solution)/shard_map/ppermute | solution.py:66
  27.1 2.5 %collective-permute-start.11 = (bf16[24,1024]{1,0:T(8,128)(2,1)S(1)}, bf16[24,1024]{1,0:T(8,128)(2,1)S(1)}, u32[]{:S(2)}, u32[]{:S(2)}) collective-permute-start(bf16[24,1024]{1,0:T(8,128)(2,1)S(1)} %get-tuple-element.52), channel_id=1, source_target_pairs={{0,8},{4,12},{8,0},{12,4},{1,9},{5,13},{9,1},{13,5},{2,10},{6,14},... | collective-permute-start | bytes 147464 | tf_op jit(solution)/shard_map/ppermute | solution.py:66
  29.6 1.4 %collective-permute-start.12 = (bf16[24,1024]{1,0:T(8,128)(2,1)S(1)}, bf16[24,1024]{1,0:T(8,128)(2,1)S(1)}, u32[]{:S(2)}, u32[]{:S(2)}) collective-permute-start(bf16[24,1024]{1,0:T(8,128)(2,1)S(1)} %get-tuple-element.53), channel_id=1, source_target_pairs={{0,12},{4,8},{8,4},{12,0},{1,13},{5,9},{9,5},{13,1},{2,14},{6,10},... | collective-permute-start | bytes 147464 | tf_op jit(solution)/shard_map/ppermute | solution.py:66
  31.1 1.1 %collective-permute-done.11.refs_2_ = bf16[24,1024]{1,0:T(8,128)(2,1)S(1)} collective-permute-done((bf16[24,1024]{1,0:T(8,128)(2,1)S(1)}, bf16[24,1024]{1,0:T(8,128)(2,1)S(1)}, u32[]{:S(2)}, u32[]{:S(2)}) %collective-permute-start.11) | collective-permute-done | bytes 49184 | tf_op jit(solution)/shard_map/ppermute | solution.py:66
  32.2 3.4 %collective-permute-done.12.refs_3_ = bf16[24,1024]{1,0:T(8,128)(2,1)S(1)} collective-permute-done((bf16[24,1024]{1,0:T(8,128)(2,1)S(1)}, bf16[24,1024]{1,0:T(8,128)(2,1)S(1)}, u32[]{:S(2)}, u32[]{:S(2)}) %collective-permute-start.12) | collective-permute-done | bytes 49184 | tf_op jit(solution)/shard_map/ppermute | solution.py:66
  36.1 2.5 %collective-permute-start.20 = (bf16[24,1024]{1,0:T(8,128)(2,1)S(1)}, bf16[24,1024]{1,0:T(8,128)(2,1)S(1)}, u32[]{:S(2)}, u32[]{:S(2)}) collective-permute-start(bf16[24,1024]{1,0:T(8,128)(2,1)S(1)} %get-tuple-element.58), channel_id=1, source_target_pairs={{0,8},{4,12},{8,0},{12,4},{1,9},{5,13},{9,1},{13,5},{2,10},{6,14},... | collective-permute-start | bytes 147464 | tf_op jit(solution)/shard_map/ppermute | solution.py:66
  38.6 1.9 %collective-permute-start.24 = (bf16[24,1024]{1,0:T(8,128)(2,1)S(1)}, bf16[24,1024]{1,0:T(8,128)(2,1)S(1)}, u32[]{:S(2)}, u32[]{:S(2)}) collective-permute-start(bf16[24,1024]{1,0:T(8,128)(2,1)S(1)} %get-tuple-element.59), channel_id=1, source_target_pairs={{0,12},{4,8},{8,4},{12,0},{1,13},{5,9},{9,5},{13,1},{2,14},{6,10},... | collective-permute-start | bytes 147464 | tf_op jit(solution)/shard_map/ppermute | solution.py:66
  40.5 1.5 %collective-permute-start.13 = (bf16[24,1024]{1,0:T(8,128)(2,1)S(1)}, bf16[24,1024]{1,0:T(8,128)(2,1)S(1)}, u32[]{:S(2)}, u32[]{:S(2)}) collective-permute-start(bf16[24,1024]{1,0:T(8,128)(2,1)S(1)} %get-tuple-element.56.refs_0_), channel_id=1, source_target_pairs={{0,2},{1,3},{2,0},{3,1},{4,6},{5,7},{6,4},{7,5},{8,10},{9,11},{10,... | collective-permute-start | bytes 147464 | tf_op jit(solution)/shard_map/ppermute | solution.py:66
  42.6 1.5 %collective-permute-start.21 = (bf16[24,1024]{1,0:T(8,128)(2,1)S(1)}, bf16[24,1024]{1,0:T(8,128)(2,1)S(1)}, u32[]{:S(2)}, u32[]{:S(2)}) collective-permute-start(bf16[24,1024]{1,0:T(8,128)(2,1)S(1)} %collective-permute-done.20.refs_8_), channel_id=1, source_target_pairs={{0,2},{1,3},{2,0},{3,1},{4,6},{5,7},{6,4},{7,5},{8,10},{9,11},{10,... | collective-permute-start | bytes 147464 | tf_op jit(solution)/shard_map/ppermute | solution.py:66
  44.5 1.5 %collective-permute-start.25 = (bf16[24,1024]{1,0:T(8,128)(2,1)S(1)}, bf16[24,1024]{1,0:T(8,128)(2,1)S(1)}, u32[]{:S(2)}, u32[]{:S(2)}) collective-permute-start(bf16[24,1024]{1,0:T(8,128)(2,1)S(1)} %collective-permute-done.24.refs_12_), channel_id=1, source_target_pairs={{0,2},{1,3},{2,0},{3,1},{4,6},{5,7},{6,4},{7,5},{8,10},{9,11},{10,... | collective-permute-start | bytes 147464 | tf_op jit(solution)/shard_map/ppermute | solution.py:66
  46.6 1.0 %collective-permute-done.21.refs_9_ = bf16[24,1024]{1,0:T(8,128)(2,1)S(1)} collective-permute-done((bf16[24,1024]{1,0:T(8,128)(2,1)S(1)}, bf16[24,1024]{1,0:T(8,128)(2,1)S(1)}, u32[]{:S(2)}, u32[]{:S(2)}) %collective-permute-start.21) | collective-permute-done | bytes 49184 | tf_op jit(solution)/shard_map/ppermute | solution.py:66
  50.3 2.0 %front.3.hidden_ref = bf16[96,384]{1,0:T(8,128)(2,1)S(1)} custom-call(bf16[24,1024]{1,0:T(8,128)(2,1)S(1)} %get-tuple-element.56.refs_0_, bf16[24,1024]{1,0:T(8,128)(2,1)S(1)} %collective-permute-done.13.refs_1_, bf16[24,1024]{1,0:T(8,128)(2,1)S(1)} %collective-permute-done.14.refs_2_, bf16[24,1024]{1,0:T(8,128)(2,1)S(1)} %collective-permute-done.15.refs_3_, ...), custom_call_target="tpu_custom_call" | custom-call | flops 603979776 | bytes 6291456 | tf_op jit(solution)/shard_map/front/pallas_call | solution.py:288
  54.4 1.6 %collective-permute-start.32 = (bf16[48,1024]{1,0:T(8,128)(2,1)S(1)}, bf16[48,1024]{1,0:T(8,128)(2,1)S(1)}, u32[]{:S(2)}, u32[]{:S(2)}) collective-permute-start(bf16[48,1024]{1,0:T(8,128)(2,1)S(1)} %get-tuple-element.65), channel_id=1, source_target_pairs={{0,2},{1,3},{2,0},{3,1},{4,6},{5,7},{6,4},{7,5},{8,10},{9,11},{10,... | collective-permute-start | bytes 294920 | tf_op jit(solution)/shard_map/ppermute | solution.py:66
  56.8 3.3 %collective-permute-done.32.came_ref = bf16[48,1024]{1,0:T(8,128)(2,1)S(1)} collective-permute-done((bf16[48,1024]{1,0:T(8,128)(2,1)S(1)}, bf16[48,1024]{1,0:T(8,128)(2,1)S(1)}, u32[]{:S(2)}, u32[]{:S(2)}) %collective-permute-start.32) | collective-permute-done | bytes 98336 | tf_op jit(solution)/shard_map/ppermute | solution.py:66
  60.9 1.9 %collective-permute-start.34 = (bf16[24,1024]{1,0:T(8,128)(2,1)S(1)}, bf16[24,1024]{1,0:T(8,128)(2,1)S(1)}, u32[]{:S(2)}, u32[]{:S(2)}) collective-permute-start(bf16[24,1024]{1,0:T(8,128)(2,1)S(1)} %get-tuple-element.67), channel_id=1, source_target_pairs={{0,12},{4,8},{8,4},{12,0},{1,13},{5,9},{9,5},{13,1},{2,14},{6,10},... | collective-permute-start | bytes 147464 | tf_op jit(solution)/shard_map/ppermute | solution.py:66
  63.8 1.8 %collective-permute-done.33.refs_2_ = bf16[24,1024]{1,0:T(8,128)(2,1)S(1)} collective-permute-done((bf16[24,1024]{1,0:T(8,128)(2,1)S(1)}, bf16[24,1024]{1,0:T(8,128)(2,1)S(1)}, u32[]{:S(2)}, u32[]{:S(2)}) %collective-permute-start.33) | collective-permute-done | bytes 49184 | tf_op jit(solution)/shard_map/ppermute | solution.py:66
  65.6 1.3 %collective-permute-done.34.refs_3_ = bf16[24,1024]{1,0:T(8,128)(2,1)S(1)} collective-permute-done((bf16[24,1024]{1,0:T(8,128)(2,1)S(1)}, bf16[24,1024]{1,0:T(8,128)(2,1)S(1)}, u32[]{:S(2)}, u32[]{:S(2)}) %collective-permute-start.34) | collective-permute-done | bytes 49184 | tf_op jit(solution)/shard_map/ppermute | solution.py:66
  (76 shorter events, 15.5 us)
Async XLA Ops:
  1.9 9.6 %collective-permute-start = (bf16[24,2176]{1,0:T(8,128)(2,1)S(1)}, bf16[24,2176]{1,0:T(8,128)(2,1)S(1)}, u32[]{:S(2)}, u32[]{:S(2)}) collective-permute-start(bf16[24,2176]{1,0:T(8,128)(2,1)S(1)} %get-tuple-element.39), channel_id=1, source_target_pairs={{0,4},{4,0},{8,12},{12,8},{1,5},{5,1},{9,13},{13,9},{2,6},{6,2},{1... | collective-permute-start | bytes 313352 | tf_op jit(solution)/shard_map/ppermute | solution.py:66
  4.9 10.9 %collective-permute-start.2 = (bf16[24,2176]{1,0:T(8,128)(2,1)S(1)}, bf16[24,2176]{1,0:T(8,128)(2,1)S(1)}, u32[]{:S(2)}, u32[]{:S(2)}) collective-permute-start(bf16[24,2176]{1,0:T(8,128)(2,1)S(1)} %get-tuple-element.41), channel_id=1, source_target_pairs={{0,8},{4,12},{8,0},{12,4},{1,9},{5,13},{9,1},{13,5},{2,10},{6,14},... | collective-permute-start | bytes 313352 | tf_op jit(solution)/shard_map/ppermute | solution.py:66
  7.5 8.4 %collective-permute-start.4 = (bf16[24,2176]{1,0:T(8,128)(2,1)S(1)}, bf16[24,2176]{1,0:T(8,128)(2,1)S(1)}, u32[]{:S(2)}, u32[]{:S(2)}) collective-permute-start(bf16[24,2176]{1,0:T(8,128)(2,1)S(1)} %get-tuple-element.42), channel_id=1, source_target_pairs={{0,12},{4,8},{8,4},{12,0},{1,13},{5,9},{9,5},{13,1},{2,14},{6,10},... | collective-permute-start | bytes 313352 | tf_op jit(solution)/shard_map/ppermute | solution.py:66
  11.5 5.8 %collective-permute-start.1 = (bf16[24,2048]{1,0:T(8,128)(2,1)S(1)}, bf16[24,2048]{1,0:T(8,128)(2,1)S(1)}, u32[]{:S(2)}, u32[]{:S(2)}) collective-permute-start(bf16[24,2048]{1,0:T(8,128)(2,1)S(1)} %relay.3.refs_1_), channel_id=1, source_target_pairs={{0,1},{1,0},{2,3},{3,2},{4,5},{5,4},{6,7},{7,6},{8,9},{9,8},{10,11... | collective-permute-start | bytes 294920 | tf_op jit(solution)/shard_map/ppermute | solution.py:66
  20.3 3.2 %collective-permute-start.6 = (bf16[96,1024]{1,0:T(8,128)(2,1)S(1)}, bf16[96,1024]{1,0:T(8,128)(2,1)S(1)}, u32[]{:S(2)}, u32[]{:S(2)}) collective-permute-start(bf16[96,1024]{1,0:T(8,128)(2,1)S(1)} %down.8), channel_id=1, source_target_pairs={{0,1},{1,0},{2,3},{3,2},{4,5},{5,4},{6,7},{7,6},{8,9},{9,8},{10,11... | collective-permute-start | bytes 589832 | tf_op jit(solution)/shard_map/ppermute | solution.py:66
  21.4 5.7 %collective-permute-start.10 = (bf16[48,1024]{1,0:T(8,128)(2,1)S(1)}, bf16[48,1024]{1,0:T(8,128)(2,1)S(1)}, u32[]{:S(2)}, u32[]{:S(2)}) collective-permute-start(bf16[48,1024]{1,0:T(8,128)(2,1)S(1)} %get-tuple-element.51), channel_id=1, source_target_pairs={{0,2},{1,3},{2,0},{3,1},{4,6},{5,7},{6,4},{7,5},{8,10},{9,11},{10,... | collective-permute-start | bytes 294920 | tf_op jit(solution)/shard_map/ppermute | solution.py:66
  23.0 8.0 %collective-permute-start.8 = (bf16[48,1024]{1,0:T(8,128)(2,1)S(1)}, bf16[48,1024]{1,0:T(8,128)(2,1)S(1)}, u32[]{:S(2)}, u32[]{:S(2)}) collective-permute-start(bf16[48,1024]{1,0:T(8,128)(2,1)S(1)} %get-tuple-element.47), channel_id=1, source_target_pairs={{0,2},{1,3},{2,0},{3,1},{4,6},{5,7},{6,4},{7,5},{8,10},{9,11},{10,... | collective-permute-start | bytes 294920 | tf_op jit(solution)/shard_map/ppermute | solution.py:66
  27.1 5.1 %collective-permute-start.11 = (bf16[24,1024]{1,0:T(8,128)(2,1)S(1)}, bf16[24,1024]{1,0:T(8,128)(2,1)S(1)}, u32[]{:S(2)}, u32[]{:S(2)}) collective-permute-start(bf16[24,1024]{1,0:T(8,128)(2,1)S(1)} %get-tuple-element.52), channel_id=1, source_target_pairs={{0,8},{4,12},{8,0},{12,4},{1,9},{5,13},{9,1},{13,5},{2,10},{6,14},... | collective-permute-start | bytes 147464 | tf_op jit(solution)/shard_map/ppermute | solution.py:66
  29.6 6.0 %collective-permute-start.12 = (bf16[24,1024]{1,0:T(8,128)(2,1)S(1)}, bf16[24,1024]{1,0:T(8,128)(2,1)S(1)}, u32[]{:S(2)}, u32[]{:S(2)}) collective-permute-start(bf16[24,1024]{1,0:T(8,128)(2,1)S(1)} %get-tuple-element.53), channel_id=1, source_target_pairs={{0,12},{4,8},{8,4},{12,0},{1,13},{5,9},{9,5},{13,1},{2,14},{6,10},... | collective-permute-start | bytes 147464 | tf_op jit(solution)/shard_map/ppermute | solution.py:66
  31.1 4.7 %collective-permute-start.9 = (bf16[24,1024]{1,0:T(8,128)(2,1)S(1)}, bf16[24,1024]{1,0:T(8,128)(2,1)S(1)}, u32[]{:S(2)}, u32[]{:S(2)}) collective-permute-start(bf16[24,1024]{1,0:T(8,128)(2,1)S(1)} %get-tuple-element.49), channel_id=1, source_target_pairs={{0,4},{4,0},{8,12},{12,8},{1,5},{5,1},{9,13},{13,9},{2,6},{6,2},{1... | collective-permute-start | bytes 147464 | tf_op jit(solution)/shard_map/ppermute | solution.py:66
  36.1 5.9 %collective-permute-start.16 = (bf16[24,1024]{1,0:T(8,128)(2,1)S(1)}, bf16[24,1024]{1,0:T(8,128)(2,1)S(1)}, u32[]{:S(2)}, u32[]{:S(2)}) collective-permute-start(bf16[24,1024]{1,0:T(8,128)(2,1)S(1)} %get-tuple-element.57), channel_id=1, source_target_pairs={{0,4},{4,0},{8,12},{12,8},{1,5},{5,1},{9,13},{13,9},{2,6},{6,2},{1... | collective-permute-start | bytes 147464 | tf_op jit(solution)/shard_map/ppermute | solution.py:66
  36.1 6.4 %collective-permute-start.20 = (bf16[24,1024]{1,0:T(8,128)(2,1)S(1)}, bf16[24,1024]{1,0:T(8,128)(2,1)S(1)}, u32[]{:S(2)}, u32[]{:S(2)}) collective-permute-start(bf16[24,1024]{1,0:T(8,128)(2,1)S(1)} %get-tuple-element.58), channel_id=1, source_target_pairs={{0,8},{4,12},{8,0},{12,4},{1,9},{5,13},{9,1},{13,5},{2,10},{6,14},... | collective-permute-start | bytes 147464 | tf_op jit(solution)/shard_map/ppermute | solution.py:66
  38.6 5.9 %collective-permute-start.24 = (bf16[24,1024]{1,0:T(8,128)(2,1)S(1)}, bf16[24,1024]{1,0:T(8,128)(2,1)S(1)}, u32[]{:S(2)}, u32[]{:S(2)}) collective-permute-start(bf16[24,1024]{1,0:T(8,128)(2,1)S(1)} %get-tuple-element.59), channel_id=1, source_target_pairs={{0,12},{4,8},{8,4},{12,0},{1,13},{5,9},{9,5},{13,1},{2,14},{6,10},... | collective-permute-start | bytes 147464 | tf_op jit(solution)/shard_map/ppermute | solution.py:66
  40.5 5.5 %collective-permute-start.13 = (bf16[24,1024]{1,0:T(8,128)(2,1)S(1)}, bf16[24,1024]{1,0:T(8,128)(2,1)S(1)}, u32[]{:S(2)}, u32[]{:S(2)}) collective-permute-start(bf16[24,1024]{1,0:T(8,128)(2,1)S(1)} %get-tuple-element.56.refs_0_), channel_id=1, source_target_pairs={{0,2},{1,3},{2,0},{3,1},{4,6},{5,7},{6,4},{7,5},{8,10},{9,11},{10,... | collective-permute-start | bytes 147464 | tf_op jit(solution)/shard_map/ppermute | solution.py:66
  42.0 4.0 %collective-permute-start.14 = (bf16[24,1024]{1,0:T(8,128)(2,1)S(1)}, bf16[24,1024]{1,0:T(8,128)(2,1)S(1)}, u32[]{:S(2)}, u32[]{:S(2)}) collective-permute-start(bf16[24,1024]{1,0:T(8,128)(2,1)S(1)} %get-tuple-element.56.refs_0_), channel_id=1, source_target_pairs={{0,1},{1,0},{2,3},{3,2},{4,5},{5,4},{6,7},{7,6},{8,9},{9,8},{10,11... | collective-permute-start | bytes 147464 | tf_op jit(solution)/shard_map/ppermute | solution.py:66
  42.0 4.5 %collective-permute-start.17 = (bf16[24,1024]{1,0:T(8,128)(2,1)S(1)}, bf16[24,1024]{1,0:T(8,128)(2,1)S(1)}, u32[]{:S(2)}, u32[]{:S(2)}) collective-permute-start(bf16[24,1024]{1,0:T(8,128)(2,1)S(1)} %collective-permute-done.16.refs_4_), channel_id=1, source_target_pairs={{0,2},{1,3},{2,0},{3,1},{4,6},{5,7},{6,4},{7,5},{8,10},{9,11},{10,... | collective-permute-start | bytes 147464 | tf_op jit(solution)/shard_map/ppermute | solution.py:66
  42.6 5.0 %collective-permute-start.21 = (bf16[24,1024]{1,0:T(8,128)(2,1)S(1)}, bf16[24,1024]{1,0:T(8,128)(2,1)S(1)}, u32[]{:S(2)}, u32[]{:S(2)}) collective-permute-start(bf16[24,1024]{1,0:T(8,128)(2,1)S(1)} %collective-permute-done.20.refs_8_), channel_id=1, source_target_pairs={{0,2},{1,3},{2,0},{3,1},{4,6},{5,7},{6,4},{7,5},{8,10},{9,11},{10,... | collective-permute-start | bytes 147464 | tf_op jit(solution)/shard_map/ppermute | solution.py:66
  44.5 4.1 %collective-permute-start.25 = (bf16[24,1024]{1,0:T(8,128)(2,1)S(1)}, bf16[24,1024]{1,0:T(8,128)(2,1)S(1)}, u32[]{:S(2)}, u32[]{:S(2)}) collective-permute-start(bf16[24,1024]{1,0:T(8,128)(2,1)S(1)} %collective-permute-done.24.refs_12_), channel_id=1, source_target_pairs={{0,2},{1,3},{2,0},{3,1},{4,6},{5,7},{6,4},{7,5},{8,10},{9,11},{10,... | collective-permute-start | bytes 147464 | tf_op jit(solution)/shard_map/ppermute | solution.py:66
  53.1 3.4 %collective-permute-start.28 = (bf16[96,1024]{1,0:T(8,128)(2,1)S(1)}, bf16[96,1024]{1,0:T(8,128)(2,1)S(1)}, u32[]{:S(2)}, u32[]{:S(2)}) collective-permute-start(bf16[96,1024]{1,0:T(8,128)(2,1)S(1)} %down.12), channel_id=1, source_target_pairs={{0,1},{1,0},{2,3},{3,2},{4,5},{5,4},{6,7},{7,6},{8,9},{9,8},{10,11... | collective-permute-start | bytes 589832 | tf_op jit(solution)/shard_map/ppermute | solution.py:66
  54.4 5.7 %collective-permute-start.32 = (bf16[48,1024]{1,0:T(8,128)(2,1)S(1)}, bf16[48,1024]{1,0:T(8,128)(2,1)S(1)}, u32[]{:S(2)}, u32[]{:S(2)}) collective-permute-start(bf16[48,1024]{1,0:T(8,128)(2,1)S(1)} %get-tuple-element.65), channel_id=1, source_target_pairs={{0,2},{1,3},{2,0},{3,1},{4,6},{5,7},{6,4},{7,5},{8,10},{9,11},{10,... | collective-permute-start | bytes 294920 | tf_op jit(solution)/shard_map/ppermute | solution.py:66
  56.0 6.8 %collective-permute-start.30 = (bf16[48,1024]{1,0:T(8,128)(2,1)S(1)}, bf16[48,1024]{1,0:T(8,128)(2,1)S(1)}, u32[]{:S(2)}, u32[]{:S(2)}) collective-permute-start(bf16[48,1024]{1,0:T(8,128)(2,1)S(1)} %get-tuple-element.61), channel_id=1, source_target_pairs={{0,2},{1,3},{2,0},{3,1},{4,6},{5,7},{6,4},{7,5},{8,10},{9,11},{10,... | collective-permute-start | bytes 294920 | tf_op jit(solution)/shard_map/ppermute | solution.py:66
  60.1 5.4 %collective-permute-start.33 = (bf16[24,1024]{1,0:T(8,128)(2,1)S(1)}, bf16[24,1024]{1,0:T(8,128)(2,1)S(1)}, u32[]{:S(2)}, u32[]{:S(2)}) collective-permute-start(bf16[24,1024]{1,0:T(8,128)(2,1)S(1)} %get-tuple-element.66), channel_id=1, source_target_pairs={{0,8},{4,12},{8,0},{12,4},{1,9},{5,13},{9,1},{13,5},{2,10},{6,14},... | collective-permute-start | bytes 147464 | tf_op jit(solution)/shard_map/ppermute | solution.py:66
  60.9 5.9 %collective-permute-start.34 = (bf16[24,1024]{1,0:T(8,128)(2,1)S(1)}, bf16[24,1024]{1,0:T(8,128)(2,1)S(1)}, u32[]{:S(2)}, u32[]{:S(2)}) collective-permute-start(bf16[24,1024]{1,0:T(8,128)(2,1)S(1)} %get-tuple-element.67), channel_id=1, source_target_pairs={{0,12},{4,8},{8,4},{12,0},{1,13},{5,9},{9,5},{13,1},{2,14},{6,10},... | collective-permute-start | bytes 147464 | tf_op jit(solution)/shard_map/ppermute | solution.py:66
  62.8 4.5 %collective-permute-start.31 = (bf16[24,1024]{1,0:T(8,128)(2,1)S(1)}, bf16[24,1024]{1,0:T(8,128)(2,1)S(1)}, u32[]{:S(2)}, u32[]{:S(2)}) collective-permute-start(bf16[24,1024]{1,0:T(8,128)(2,1)S(1)} %get-tuple-element.63), channel_id=1, source_target_pairs={{0,4},{4,0},{8,12},{12,8},{1,5},{5,1},{9,13},{13,9},{2,6},{6,2},{1... | collective-permute-start | bytes 147464 | tf_op jit(solution)/shard_map/ppermute | solution.py:66
  (15 other events, 57.6 us)

commit v7 on v6

--- a/solution.py
+++ b/solution.py
@@ -232,27 +232,27 @@
     )(tokens, ids)
 
 
-def front_kernel(layout, section, experts, n_flags, *refs):
-    n = sum(len(block) for block in layout)
-    x_refs, flag_refs = list(refs[:n]), refs[n : n + n_flags]
-    mod_ref, router_ref, pair_ref, out_ref, normed_ref = refs[n + n_flags :]
+def front_kernel(layout, section, experts, n_x, *refs):
+    x_refs, flag_refs = refs[:n_x], refs[n_x : n_x + len(layout)]
+    mod_ref, router_ref, pair_ref, out_ref, normed_ref = refs[n_x + len(layout) :]
+    slots = flag_refs[0].shape[0]
     width = normed_ref.shape[1]
     hidden = out_ref.shape[1]
     quarter = width // 4
     et = lax.axis_index("et")
-    blocks = []
-    for block in layout:
-        blocks.append([(x_refs.pop(0), cols, flip) for cols, flip in block])
 
     def part(block, flip):
-        for ref, cols, at in block:
-            if cols == quarter and at == flip:
-                return ref[...].astype(jnp.float32)
-            if cols == 2 * quarter and at == flip & 1:
-                return ref[:, aligned((et ^ flip) >> 1, quarter)].astype(jnp.float32)
-            if cols == width:
-                return ref[:, aligned(et ^ flip, quarter)].astype(jnp.float32)
-
+        index, place = block[flip]
+        ref = x_refs[index]
+        if place is None:
+            cols = aligned((et ^ flip) & (ref.shape[1] // quarter - 1), quarter)
+        elif place == "high":
+            cols = aligned((et ^ flip) >> 1, quarter)
+        else:
+            cols = pl.ds(place * quarter, quarter)
+        return ref[:, cols].astype(jnp.float32)[:slots]
+
+    blocks = layout
     parts = [jnp.concatenate([part(block, flip) for block in blocks], axis=0) for flip in range(4)]
     total = sum(jnp.sum(xf * xf, axis=1, keepdims=True) for xf in parts)
     scale = lax.rsqrt(total / width + 1e-06)
@@ -283,10 +283,16 @@
     width, hidden = pair.shape[0], pair.shape[1] // 2
     rows = sum(f.shape[0] for f in flags)
     experts = router.shape[0]
-    xs = [x for block in blocks for x, _, _ in block]
-    layout = [[piece[1:] for piece in block] for block in blocks]
-    return pl.pallas_call(
-        functools.partial(front_kernel, layout, section, experts, len(flags)),
+    xs, layout = [], []
+    for block in blocks:
+        layout.append([])
+        for x, place in block:
+            known = [i for i, other in enumerate(xs) if other is x]
+            layout[-1].append((known[0] if known else len(xs), place))
+            if not known:
+                xs.append(x)
+    return pl.pallas_call(
+        functools.partial(front_kernel, layout, section, experts, len(xs)),
         in_specs=[VMEM] * (len(xs) + len(flags) + 3),
         scratch_shapes=[pltpu.VMEM((rows, width), jnp.bfloat16)],
         out_shape=jax.ShapeDtypeStruct((rows, hidden), jnp.bfloat16),
@@ -300,23 +306,27 @@
 
 def down_kernel(flip, n_adds, hidden_ref, down_ref, *refs):
     adds, outs = refs[:n_adds], refs[n_adds:]
-    quarter = outs[0].shape[1]
+    quarter = down_ref.shape[1] // 4
     weights = down_ref[:, aligned(lax.axis_index("et") ^ flip, quarter)]
     product = jnp.dot(hidden_ref[...], weights, preferred_element_type=jnp.float32)
+    rows = 0
     for ref in adds:
-        product += ref[...].astype(jnp.float32)
-    rows = outs[0].shape[0]
-    for k, out in enumerate(outs):
-        out[...] = product[k * rows : (k + 1) * rows].astype(out.dtype)
-
-
-def down(hidden, w_down, flip, blocks, adds=(), dtype=jnp.bfloat16):
+        if ref.shape[0] == product.shape[0]:
+            product += ref[...].astype(jnp.float32)
+    for out in outs:
+        out[:, :quarter] = product[rows : rows + out.shape[0]].astype(out.dtype)
+        rows += out.shape[0]
+        if out.shape[1] > quarter:
+            out[:, quarter:] = adds[-1][...]
+
+
+def down(hidden, w_down, flip, outs, adds=()):
     units, width = w_down.shape
     rows, quarter = hidden.shape[0], width // 4
     return pl.pallas_call(
         functools.partial(down_kernel, flip, len(adds)),
         in_specs=[VMEM] * (2 + len(adds)),
-        out_shape=[jax.ShapeDtypeStruct((rows // blocks, quarter), dtype)] * blocks,
+        out_shape=[jax.ShapeDtypeStruct((r, quarter * wide), t) for r, wide, t in outs],
         compiler_params=params(),
         cost_estimate=pl.CostEstimate(
             flops=2 * rows * units * quarter, bytes_accessed=2 * units * quarter, transcendentals=0
@@ -342,57 +352,95 @@
     )(keep, came)
 
 
-def move_kernel(n_came, last, own_ref, back_ref, pick_ref, *refs):
+def fold_kernel(back_ref, mine_ref, came_ref, out_ref):
+    cols = mine_ref.shape[1]
+    rows = [mine_ref[...].astype(jnp.float32), came_ref[:, cols:].astype(jnp.float32)]
+    rows = jnp.concatenate(rows, axis=0)
+    out_ref[...] = narrow(product(back_ref[:, : rows.shape[0]], rows))
+
+
+def fold(back, mine, came):
+    return pl.pallas_call(
+        fold_kernel,
+        out_shape=jax.ShapeDtypeStruct((back.shape[0], mine.shape[1]), jnp.bfloat16),
+        compiler_params=params(),
+        name="fold",
+    )(back, mine, came)
+
+
+def move_kernel(n_came, last, own_ref, back_ref, pick_ref, cross_ref, *refs):
     came, outs = refs[:n_came], refs[n_came:]
-    rows = [ref[...].astype(jnp.float32) for ref in came]
-    velocity = product(back_ref[...], jnp.concatenate(rows, axis=0))
+    cols = own_ref.shape[1]
+    rows = [ref[:, :cols].astype(jnp.float32) for ref in came]
+    velocity = product(back_ref[...], jnp.concatenate(rows, axis=0)) + cross_ref[...].astype(jnp.float32)
     moved = narrow(own_ref[...].astype(jnp.float32) - 0.5 * velocity)
     outs[0][...] = moved
     if last:
         outs[1][...] = narrow(velocity)
     else:
-        slots = came[0].shape[0]
-        picked = product(pick_ref[...], moved)
-        for k, out in enumerate(outs[1:]):
-            out[...] = narrow(picked[k * slots : (k + 1) * slots])
-
-
-def move(own, back, pick, came, last):
-    shapes = [own.shape] + ([own.shape] if last else [c.shape for c in came])
+        picked, at = product(pick_ref[...], moved), 0
+        for out in outs[1:]:
+            out[...] = narrow(picked[at : at + out.shape[0]])
+            at += out.shape[0]
+
+
+def move(own, back, pick, cross, came, last):
+    slots = came[0].shape[0]
+    counts = [2] + [1] * (len(came) - 2)
+    shapes = [own.shape] + ([own.shape] if last else [(slots * c, own.shape[1]) for c in counts])
     return pl.pallas_call(
         functools.partial(move_kernel, len(came), last),
         out_shape=[jax.ShapeDtypeStruct(s, jnp.bfloat16) for s in shapes],
         compiler_params=params(),
         name="move",
-    )(own, back, pick, *came)
-
-
-def sum_back(hidden, w_down, own, back, pick, last_section):
+    )(own, back, pick, cross, *came)
+
+
+def sum_back(hidden, w_down, own, back, pick, last):
     peers = lax.axis_size("ep")
-    some = peers // 2
-    far = swap(down(hidden, w_down, 3, 1)[0], "et", 1)
-    near = swap(down(hidden, w_down, 1, 1)[0], "et", 1)
-    first, last = down(hidden, w_down, 2, 2, (far,))
-    last, first = swap(last, "et", 2), swap(first, "et", 2)
-    keep_first, keep_last = down(hidden, w_down, 0, 2, (near,), jnp.float32)
-    later = add(keep_last, last, peers - some)
-    blocks = add(keep_first, first, some) + later
-    came = [swap(b, "ep", k) if k else b for k, b in enumerate(blocks)]
-    return move(own, back, pick, came, last_section)
-
-
-def spread(block, quarter):
+    slots = hidden.shape[0] // peers
+    far_rows = slots * (peers - 2)
+    narrow_type, wide_type = jnp.bfloat16, jnp.float32
+    whole = [(hidden.shape[0], 1, narrow_type)]
+    far = swap(down(hidden, w_down, 3, whole)[0], "et", 1)
+    near = swap(down(hidden, w_down, 1, whole)[0], "et", 1)
+    cuts = [(slots, 1, narrow_type), (slots, 1, narrow_type), (far_rows, 1, narrow_type)]
+    own_cross, next_cross, sent = down(hidden, w_down, 2, cuts, (far,))
+    cuts = [(slots, 1, wide_type), (slots, 2, narrow_type), (far_rows, 1, wide_type)]
+    kept, beside, kept_far = down(hidden, w_down, 0, cuts, (near, next_cross))
+    came = swap(beside, "ep", 1)
+    blocks = add(kept_far, swap(sent, "et", 2), peers - 2)
+    cross = swap(fold(back, own_cross, came), "et", 2)
+    blocks = [kept, came] + [swap(b, "ep", k + 2) for k, b in enumerate(blocks)]
+    return move(own, back, pick, cross, blocks, last)
+
+
+def spread(block, place=0):
     side = swap(block, "et", 2)
     near, far = swap(block, "et", 1), swap(side, "et", 1)
-    return [(block, quarter, 0), (side, quarter, 2), (near, quarter, 1), (far, quarter, 3)]
+    return [(block, place), (near, place), (side, place), (far, place)]
+
+
+def join_kernel(block_ref, side_ref, out_ref):
+    rows, cols = out_ref.shape[0], block_ref.shape[1]
+    out_ref[:, :cols] = narrow(block_ref[...].astype(jnp.float32)[rows:])
+    out_ref[:, cols:] = narrow(side_ref[...].astype(jnp.float32)[rows:])
+
+
+def join(block, side):
+    return pl.pallas_call(
+        join_kernel,
+        out_shape=jax.ShapeDtypeStruct((block.shape[0] // 2, 2 * block.shape[1]), block.dtype),
+        compiler_params=params(),
+        name="join",
+    )(block, side)
 
 
 def dense_body(tokens, modulation, router, gate_weight, up_weight, down_weight, expert_ids):
     rows, width = tokens.shape
-    half, quarter = width // 2, width // 4
+    half = width // 2
     router = router.T
     experts = router.shape[0]
-    peers = lax.axis_size("ep")
     slots = 3 * rows * expert_ids.shape[2] // (2 * experts)
     ids = expert_ids.transpose(0, 2, 1)
 
@@ -401,14 +449,19 @@
     mine, flags, *choice = own_rows(tokens, ids, experts, slots)
     pick, back = choice[2], choice[1::2]
     flags = [flags] + [swap(p, "ep", k + 1) for k, p in enumerate(packed)]
-    blocks = [[(mine, width, 0)]]
+    blocks = [[(mine, None)] * 4]
     for f in flags[1:]:
         f = relay(f, half, done)
-        blocks.append([(f, half, 0), (swap(f, "et", 1), half, 1)])
+        other = swap(f, "et", 1)
+        blocks.append([(f, "high"), (other, "high")] * 2)
     hidden = front(blocks, flags, 0, modulation, router, pair)
-    own, *sent = sum_back(hidden, w_down, own, back[0], pick, False)
-
-    blocks = [spread(swap(b, "ep", k) if k else b, quarter) for k, b in enumerate(sent)]
+    own, near, *far = sum_back(hidden, w_down, own, back[0], pick, False)
+
+    first = spread(near)
+    beside = swap(join(near, first[2][0]), "ep", 1)
+    other = swap(beside, "et", 1)
+    blocks = [first, [(beside, 0), (other, 0), (beside, 1), (other, 1)]]
+    blocks += [spread(swap(b, "ep", k + 2)) for k, b in enumerate(far)]
     hidden = front(blocks, flags, 1, modulation, router, pair)
     return tuple(sum_back(hidden, w_down, own, back[1], pick, True))
 
@@ -428,7 +481,7 @@
     def body(*args):
         experts, picks = args[2].shape[1], args[6].shape[2]
         peers = lax.axis_size("ep")
-        fits = lax.axis_size("et") == 4 and peers & (peers - 1) == 0
+        fits = lax.axis_size("et") == 4 and peers >= 4 and peers & (peers - 1) == 0
         chosen = dense_body if fits and experts <= 2 * picks else routed_body
         return chosen(*args)
 

time: 68.3 us -> 74.8 us (1.095)
  waiting for transfers between devices: 24 us -> 31.7 us
  starting transfers between devices: 30.1 us -> 28.6 us
    ppermute x35 -> x33, waiting for transfers between devices: 24 us -> 31.7 us  [swap(): return lax.ppermute(x, axis, [(i, i ^ bit) for i in range(size)])]
    ppermute x35 -> x33, starting transfers between devices: 30.1 us -> 28.6 us  [swap(): return lax.ppermute(x, axis, [(i, i ^ bit) for i in range(size)])]
  transfers between devices with their start and end apart: 35 -> 33, of which waited for: 18 -> 18; matrix products, arithmetic and copies ran while one was open for 0% -> 0% of each run, Pallas kernels for 9% -> 8%
where the time goes in v7:
time: 74.8 us; the launch traced here: 74.6 us
  waiting for transfers between devices  31.7 us (42%)
  starting transfers between devices  28.6 us (38%)
  Pallas kernels  13.4 us (18%)
  between operations  0.87 us (1%)
    ppermute x33, waiting for transfers between devices, swap(): return lax.ppermute(x, axis, [(i, i ^ bit) for i in range(size)])  31.7 us
    ppermute x33, starting transfers between devices, swap(): return lax.ppermute(x, axis, [(i, i ^ bit) for i in range(size)])  28.6 us
    pallas_call x1, Pallas kernels, load(): pl.pallas_call(load_kernel, in_specs=[ANY] * 3, out_specs=[VMEM] * 3, out...  3.82 us
    pallas_call x2, Pallas kernels, front(): pl.pallas_call(functools.partial(front_kernel, layout, section, experts,...  3.8 us
    pallas_call x8, Pallas kernels, down(): pl.pallas_call(functools.partial(down_kernel, flip, len(adds)), in_specs=...  2.25 us
  transfers between devices with their start and end apart: 33, of which 18 were waited for; matrix products, arithmetic and copies ran while one was open for 0% of the time, Pallas kernels for 8%

profile of v7, /device:TPU:0, one launch (start us, length us, event | category | flops | bytes accessed | tf_op | source)
XLA Modules:
  0.0 74.6 jit_solution(3377353774971595642)
XLA Ops:
  1.9 3.1 %collective-permute-start = (bf16[24,2176]{1,0:T(8,128)(2,1)S(1)}, bf16[24,2176]{1,0:T(8,128)(2,1)S(1)}, u32[]{:S(2)}, u32[]{:S(2)}) collective-permute-start(bf16[24,2176]{1,0:T(8,128)(2,1)S(1)} %get-tuple-element.38), channel_id=1, source_target_pairs={{0,4},{4,0},{8,12},{12,8},{1,5},{5,1},{9,13},{13,9},{2,6},{6,2},{1... | collective-permute-start | bytes 313352 | tf_op jit(solution)/shard_map/ppermute | solution.py:66
  4.9 2.6 %collective-permute-start.2 = (bf16[24,2176]{1,0:T(8,128)(2,1)S(1)}, bf16[24,2176]{1,0:T(8,128)(2,1)S(1)}, u32[]{:S(2)}, u32[]{:S(2)}) collective-permute-start(bf16[24,2176]{1,0:T(8,128)(2,1)S(1)} %get-tuple-element.40), channel_id=1, source_target_pairs={{0,8},{4,12},{8,0},{12,4},{1,9},{5,13},{9,1},{13,5},{2,10},{6,14},... | collective-permute-start | bytes 313352 | tf_op jit(solution)/shard_map/ppermute | solution.py:66
  7.6 3.8 %load.1 = (bf16[4096,768]{1,0:T(8,128)(2,1)S(1)}, bf16[384,4096]{1,0:T(8,128)(2,1)S(1)}, f32[8,128]{1,0:T(8,128)S(1)}) custom-call(bf16[1,4096,384]{2,1,0:T(8,128)(2,1)} %gate_ref.1, bf16[1,4096,384]{2,1,0:T(8,128)(2,1)} %up_ref.1, bf16[1,384,4096]{2,1,0:T(8,128)(2,1)} %down_ref.1), custom_call_target="tpu_custom_call" | custom-call | bytes 18874368 | tf_op jit(solution)/shard_map/load/pallas_call | solution.py:101
  11.6 4.3 %collective-permute-done.2.block_ref.refs_9_.refs_16_ = bf16[24,2176]{1,0:T(8,128)(2,1)S(1)} collective-permute-done((bf16[24,2176]{1,0:T(8,128)(2,1)S(1)}, bf16[24,2176]{1,0:T(8,128)(2,1)S(1)}, u32[]{:S(2)}, u32[]{:S(2)}) %collective-permute-start.2) | collective-permute-done | bytes 104480 | tf_op jit(solution)/shard_map/ppermute | solution.py:66
  17.5 1.8 %front.2.hidden_ref = bf16[96,384]{1,0:T(8,128)(2,1)S(1)} custom-call(bf16[24,4096]{1,0:T(8,128)(2,1)S(1)} %get-tuple-element.37.refs_0_, bf16[24,2048]{1,0:T(8,128)(2,1)S(1)} %relay.3.refs_1_, bf16[24,2048]{1,0:T(8,128)(2,1)S(1)} %collective-permute-done.1.refs_2_, bf16[24,2048]{1,0:T(8,128)(2,1)S(1)} %relay.4.refs_3_, ...), custom_call_target="tpu_custom_call" | custom-call | flops 603979776 | bytes 6291456 | tf_op jit(solution)/shard_map/front/pallas_call | solution.py:294
  22.1 1.3 %collective-permute-start.8 = (bf16[24,2048]{1,0:T(8,128)(2,1)S(1)}, bf16[24,2048]{1,0:T(8,128)(2,1)S(1)}, u32[]{:S(2)}, u32[]{:S(2)}) collective-permute-start(bf16[24,2048]{1,0:T(8,128)(2,1)S(1)} %get-tuple-element.47), channel_id=1, source_target_pairs={{0,4},{4,0},{8,12},{12,8},{1,5},{5,1},{9,13},{13,9},{2,6},{6,2},{1... | collective-permute-start | bytes 294920 | tf_op jit(solution)/shard_map/ppermute | solution.py:66
  23.4 1.5 %collective-permute-start.10 = (bf16[48,1024]{1,0:T(8,128)(2,1)S(1)}, bf16[48,1024]{1,0:T(8,128)(2,1)S(1)}, u32[]{:S(2)}, u32[]{:S(2)}) collective-permute-start(bf16[48,1024]{1,0:T(8,128)(2,1)S(1)} %get-tuple-element.50), channel_id=1, source_target_pairs={{0,2},{1,3},{2,0},{3,1},{4,6},{5,7},{6,4},{7,5},{8,10},{9,11},{10,... | collective-permute-start | bytes 294920 | tf_op jit(solution)/shard_map/ppermute | solution.py:66
  24.9 2.1 %collective-permute-done.8.came_ref.refs_1_ = bf16[24,2048]{1,0:T(8,128)(2,1)S(1)} collective-permute-done((bf16[24,2048]{1,0:T(8,128)(2,1)S(1)}, bf16[24,2048]{1,0:T(8,128)(2,1)S(1)}, u32[]{:S(2)}, u32[]{:S(2)}) %collective-permute-start.8) | collective-permute-done | bytes 98336 | tf_op jit(solution)/shard_map/ppermute | solution.py:66
  27.2 1.6 %collective-permute-start.9 = (bf16[32,1024]{1,0:T(8,128)(2,1)S(1)}, bf16[32,1024]{1,0:T(8,128)(2,1)S(1)}, u32[]{:S(2)}, u32[]{:S(2)}) collective-permute-start(bf16[32,1024]{1,0:T(8,128)(2,1)S(1)} %fold.2), channel_id=1, source_target_pairs={{0,2},{1,3},{2,0},{3,1},{4,6},{5,7},{6,4},{7,5},{8,10},{9,11},{10,... | collective-permute-start | bytes 196616 | tf_op jit(solution)/shard_map/ppermute | solution.py:66
  28.8 2.5 %collective-permute-start.11 = (bf16[24,1024]{1,0:T(8,128)(2,1)S(1)}, bf16[24,1024]{1,0:T(8,128)(2,1)S(1)}, u32[]{:S(2)}, u32[]{:S(2)}) collective-permute-start(bf16[24,1024]{1,0:T(8,128)(2,1)S(1)} %get-tuple-element.51), channel_id=1, source_target_pairs={{0,8},{4,12},{8,0},{12,4},{1,9},{5,13},{9,1},{13,5},{2,10},{6,14},... | collective-permute-start | bytes 147464 | tf_op jit(solution)/shard_map/ppermute | solution.py:66
  31.3 1.4 %collective-permute-start.12 = (bf16[24,1024]{1,0:T(8,128)(2,1)S(1)}, bf16[24,1024]{1,0:T(8,128)(2,1)S(1)}, u32[]{:S(2)}, u32[]{:S(2)}) collective-permute-start(bf16[24,1024]{1,0:T(8,128)(2,1)S(1)} %get-tuple-element.52), channel_id=1, source_target_pairs={{0,12},{4,8},{8,4},{12,0},{1,13},{5,9},{9,5},{13,1},{2,14},{6,10},... | collective-permute-start | bytes 147464 | tf_op jit(solution)/shard_map/ppermute | solution.py:66
  32.6 1.4 %collective-permute-done.11.refs_2_ = bf16[24,1024]{1,0:T(8,128)(2,1)S(1)} collective-permute-done((bf16[24,1024]{1,0:T(8,128)(2,1)S(1)}, bf16[24,1024]{1,0:T(8,128)(2,1)S(1)}, u32[]{:S(2)}, u32[]{:S(2)}) %collective-permute-start.11) | collective-permute-done | bytes 49184 | tf_op jit(solution)/shard_map/ppermute | solution.py:66
  34.0 3.1 %collective-permute-done.12.refs_3_ = bf16[24,1024]{1,0:T(8,128)(2,1)S(1)} collective-permute-done((bf16[24,1024]{1,0:T(8,128)(2,1)S(1)}, bf16[24,1024]{1,0:T(8,128)(2,1)S(1)}, u32[]{:S(2)}, u32[]{:S(2)}) %collective-permute-start.12) | collective-permute-done | bytes 49184 | tf_op jit(solution)/shard_map/ppermute | solution.py:66
  38.1 4.1 %collective-permute-done.14.side_ref.refs_2_ = bf16[48,1024]{1,0:T(8,128)(2,1)S(1)} collective-permute-done((bf16[48,1024]{1,0:T(8,128)(2,1)S(1)}, bf16[48,1024]{1,0:T(8,128)(2,1)S(1)}, u32[]{:S(2)}, u32[]{:S(2)}) %collective-permute-start.14) | collective-permute-done | bytes 98336 | tf_op jit(solution)/shard_map/ppermute | solution.py:66
  42.3 1.9 %collective-permute-start.18 = (bf16[24,1024]{1,0:T(8,128)(2,1)S(1)}, bf16[24,1024]{1,0:T(8,128)(2,1)S(1)}, u32[]{:S(2)}, u32[]{:S(2)}) collective-permute-start(bf16[24,1024]{1,0:T(8,128)(2,1)S(1)} %get-tuple-element.56), channel_id=1, source_target_pairs={{0,8},{4,12},{8,0},{12,4},{1,9},{5,13},{9,1},{13,5},{2,10},{6,14},... | collective-permute-start | bytes 147464 | tf_op jit(solution)/shard_map/ppermute | solution.py:66
  44.2 2.4 %collective-permute-start.22 = (bf16[24,1024]{1,0:T(8,128)(2,1)S(1)}, bf16[24,1024]{1,0:T(8,128)(2,1)S(1)}, u32[]{:S(2)}, u32[]{:S(2)}) collective-permute-start(bf16[24,1024]{1,0:T(8,128)(2,1)S(1)} %get-tuple-element.57), channel_id=1, source_target_pairs={{0,12},{4,8},{8,4},{12,0},{1,13},{5,9},{9,5},{13,1},{2,14},{6,10},... | collective-permute-start | bytes 147464 | tf_op jit(solution)/shard_map/ppermute | solution.py:66
  48.0 2.1 %collective-permute-done.22.refs_10_ = bf16[24,1024]{1,0:T(8,128)(2,1)S(1)} collective-permute-done((bf16[24,1024]{1,0:T(8,128)(2,1)S(1)}, bf16[24,1024]{1,0:T(8,128)(2,1)S(1)}, u32[]{:S(2)}, u32[]{:S(2)}) %collective-permute-start.22) | collective-permute-done | bytes 49184 | tf_op jit(solution)/shard_map/ppermute | solution.py:66
  52.4 1.8 %collective-permute-done.24.refs_12_ = bf16[24,1024]{1,0:T(8,128)(2,1)S(1)} collective-permute-done((bf16[24,1024]{1,0:T(8,128)(2,1)S(1)}, bf16[24,1024]{1,0:T(8,128)(2,1)S(1)}, u32[]{:S(2)}, u32[]{:S(2)}) %collective-permute-start.24) | collective-permute-done | bytes 49184 | tf_op jit(solution)/shard_map/ppermute | solution.py:66
  55.4 2.0 %front.3.hidden_ref = bf16[96,384]{1,0:T(8,128)(2,1)S(1)} custom-call(bf16[48,1024]{1,0:T(8,128)(2,1)S(1)} %get-tuple-element.55.block_ref.refs_0_, bf16[48,1024]{1,0:T(8,128)(2,1)S(1)} %collective-permute-done.13.refs_1_, bf16[48,1024]{1,0:T(8,128)(2,1)S(1)} %collective-permute-done.14.side_ref.refs_2_, ...), custom_call_target="tpu_custom_call" | custom-call | flops 603979776 | bytes 6291456 | tf_op jit(solution)/shard_map/front/pallas_call | solution.py:294
  61.3 3.8 %collective-permute-done.28.came_ref.refs_1_ = bf16[24,2048]{1,0:T(8,128)(2,1)S(1)} collective-permute-done((bf16[24,2048]{1,0:T(8,128)(2,1)S(1)}, bf16[24,2048]{1,0:T(8,128)(2,1)S(1)}, u32[]{:S(2)}, u32[]{:S(2)}) %collective-permute-start.28) | collective-permute-done | bytes 98336 | tf_op jit(solution)/shard_map/ppermute | solution.py:66
  66.0 1.9 %collective-permute-start.31 = (bf16[24,1024]{1,0:T(8,128)(2,1)S(1)}, bf16[24,1024]{1,0:T(8,128)(2,1)S(1)}, u32[]{:S(2)}, u32[]{:S(2)}) collective-permute-start(bf16[24,1024]{1,0:T(8,128)(2,1)S(1)} %get-tuple-element.64), channel_id=1, source_target_pairs={{0,8},{4,12},{8,0},{12,4},{1,9},{5,13},{9,1},{13,5},{2,10},{6,14},... | collective-permute-start | bytes 147464 | tf_op jit(solution)/shard_map/ppermute | solution.py:66
  67.9 1.4 %collective-permute-start.32 = (bf16[24,1024]{1,0:T(8,128)(2,1)S(1)}, bf16[24,1024]{1,0:T(8,128)(2,1)S(1)}, u32[]{:S(2)}, u32[]{:S(2)}) collective-permute-start(bf16[24,1024]{1,0:T(8,128)(2,1)S(1)} %get-tuple-element.65), channel_id=1, source_target_pairs={{0,12},{4,8},{8,4},{12,0},{1,13},{5,9},{9,5},{13,1},{2,14},{6,10},... | collective-permute-start | bytes 147464 | tf_op jit(solution)/shard_map/ppermute | solution.py:66
  69.3 2.8 %collective-permute-done.31.refs_2_ = bf16[24,1024]{1,0:T(8,128)(2,1)S(1)} collective-permute-done((bf16[24,1024]{1,0:T(8,128)(2,1)S(1)}, bf16[24,1024]{1,0:T(8,128)(2,1)S(1)}, u32[]{:S(2)}, u32[]{:S(2)}) %collective-permute-start.31) | collective-permute-done | bytes 49184 | tf_op jit(solution)/shard_map/ppermute | solution.py:66
  72.1 1.7 %collective-permute-done.32.refs_3_ = bf16[24,1024]{1,0:T(8,128)(2,1)S(1)} collective-permute-done((bf16[24,1024]{1,0:T(8,128)(2,1)S(1)}, bf16[24,1024]{1,0:T(8,128)(2,1)S(1)}, u32[]{:S(2)}, u32[]{:S(2)}) %collective-permute-start.32) | collective-permute-done | bytes 49184 | tf_op jit(solution)/shard_map/ppermute | solution.py:66
  (73 shorter events, 17.4 us)
Async XLA Ops:
  1.9 9.6 %collective-permute-start = (bf16[24,2176]{1,0:T(8,128)(2,1)S(1)}, bf16[24,2176]{1,0:T(8,128)(2,1)S(1)}, u32[]{:S(2)}, u32[]{:S(2)}) collective-permute-start(bf16[24,2176]{1,0:T(8,128)(2,1)S(1)} %get-tuple-element.38), channel_id=1, source_target_pairs={{0,4},{4,0},{8,12},{12,8},{1,5},{5,1},{9,13},{13,9},{2,6},{6,2},{1... | collective-permute-start | bytes 313352 | tf_op jit(solution)/shard_map/ppermute | solution.py:66
  4.9 10.9 %collective-permute-start.2 = (bf16[24,2176]{1,0:T(8,128)(2,1)S(1)}, bf16[24,2176]{1,0:T(8,128)(2,1)S(1)}, u32[]{:S(2)}, u32[]{:S(2)}) collective-permute-start(bf16[24,2176]{1,0:T(8,128)(2,1)S(1)} %get-tuple-element.40), channel_id=1, source_target_pairs={{0,8},{4,12},{8,0},{12,4},{1,9},{5,13},{9,1},{13,5},{2,10},{6,14},... | collective-permute-start | bytes 313352 | tf_op jit(solution)/shard_map/ppermute | solution.py:66
  7.5 8.4 %collective-permute-start.4 = (bf16[24,2176]{1,0:T(8,128)(2,1)S(1)}, bf16[24,2176]{1,0:T(8,128)(2,1)S(1)}, u32[]{:S(2)}, u32[]{:S(2)}) collective-permute-start(bf16[24,2176]{1,0:T(8,128)(2,1)S(1)} %get-tuple-element.41), channel_id=1, source_target_pairs={{0,12},{4,8},{8,4},{12,0},{1,13},{5,9},{9,5},{13,1},{2,14},{6,10},... | collective-permute-start | bytes 313352 | tf_op jit(solution)/shard_map/ppermute | solution.py:66
  11.5 5.8 %collective-permute-start.1 = (bf16[24,2048]{1,0:T(8,128)(2,1)S(1)}, bf16[24,2048]{1,0:T(8,128)(2,1)S(1)}, u32[]{:S(2)}, u32[]{:S(2)}) collective-permute-start(bf16[24,2048]{1,0:T(8,128)(2,1)S(1)} %relay.3.refs_1_), channel_id=1, source_target_pairs={{0,1},{1,0},{2,3},{3,2},{4,5},{5,4},{6,7},{7,6},{8,9},{9,8},{10,11... | collective-permute-start | bytes 294920 | tf_op jit(solution)/shard_map/ppermute | solution.py:66
  22.1 4.9 %collective-permute-start.8 = (bf16[24,2048]{1,0:T(8,128)(2,1)S(1)}, bf16[24,2048]{1,0:T(8,128)(2,1)S(1)}, u32[]{:S(2)}, u32[]{:S(2)}) collective-permute-start(bf16[24,2048]{1,0:T(8,128)(2,1)S(1)} %get-tuple-element.47), channel_id=1, source_target_pairs={{0,4},{4,0},{8,12},{12,8},{1,5},{5,1},{9,13},{13,9},{2,6},{6,2},{1... | collective-permute-start | bytes 294920 | tf_op jit(solution)/shard_map/ppermute | solution.py:66
  23.4 5.3 %collective-permute-start.10 = (bf16[48,1024]{1,0:T(8,128)(2,1)S(1)}, bf16[48,1024]{1,0:T(8,128)(2,1)S(1)}, u32[]{:S(2)}, u32[]{:S(2)}) collective-permute-start(bf16[48,1024]{1,0:T(8,128)(2,1)S(1)} %get-tuple-element.50), channel_id=1, source_target_pairs={{0,2},{1,3},{2,0},{3,1},{4,6},{5,7},{6,4},{7,5},{8,10},{9,11},{10,... | collective-permute-start | bytes 294920 | tf_op jit(solution)/shard_map/ppermute | solution.py:66
  27.2 10.0 %collective-permute-start.9 = (bf16[32,1024]{1,0:T(8,128)(2,1)S(1)}, bf16[32,1024]{1,0:T(8,128)(2,1)S(1)}, u32[]{:S(2)}, u32[]{:S(2)}) collective-permute-start(bf16[32,1024]{1,0:T(8,128)(2,1)S(1)} %fold.2), channel_id=1, source_target_pairs={{0,2},{1,3},{2,0},{3,1},{4,6},{5,7},{6,4},{7,5},{8,10},{9,11},{10,... | collective-permute-start | bytes 196616 | tf_op jit(solution)/shard_map/ppermute | solution.py:66
  28.8 5.3 %collective-permute-start.11 = (bf16[24,1024]{1,0:T(8,128)(2,1)S(1)}, bf16[24,1024]{1,0:T(8,128)(2,1)S(1)}, u32[]{:S(2)}, u32[]{:S(2)}) collective-permute-start(bf16[24,1024]{1,0:T(8,128)(2,1)S(1)} %get-tuple-element.51), channel_id=1, source_target_pairs={{0,8},{4,12},{8,0},{12,4},{1,9},{5,13},{9,1},{13,5},{2,10},{6,14},... | collective-permute-start | bytes 147464 | tf_op jit(solution)/shard_map/ppermute | solution.py:66
  31.3 5.9 %collective-permute-start.12 = (bf16[24,1024]{1,0:T(8,128)(2,1)S(1)}, bf16[24,1024]{1,0:T(8,128)(2,1)S(1)}, u32[]{:S(2)}, u32[]{:S(2)}) collective-permute-start(bf16[24,1024]{1,0:T(8,128)(2,1)S(1)} %get-tuple-element.52), channel_id=1, source_target_pairs={{0,12},{4,8},{8,4},{12,0},{1,13},{5,9},{9,5},{13,1},{2,14},{6,10},... | collective-permute-start | bytes 147464 | tf_op jit(solution)/shard_map/ppermute | solution.py:66
  37.5 4.7 %collective-permute-start.14 = (bf16[48,1024]{1,0:T(8,128)(2,1)S(1)}, bf16[48,1024]{1,0:T(8,128)(2,1)S(1)}, u32[]{:S(2)}, u32[]{:S(2)}) collective-permute-start(bf16[48,1024]{1,0:T(8,128)(2,1)S(1)} %get-tuple-element.55.block_ref.refs_0_), channel_id=1, source_target_pairs={{0,2},{1,3},{2,0},{3,1},{4,6},{5,7},{6,4},{7,5},{8,10},{9,11},{10,... | collective-permute-start | bytes 294920 | tf_op jit(solution)/shard_map/ppermute | solution.py:66
  38.1 12.6 %collective-permute-start.13 = (bf16[48,1024]{1,0:T(8,128)(2,1)S(1)}, bf16[48,1024]{1,0:T(8,128)(2,1)S(1)}, u32[]{:S(2)}, u32[]{:S(2)}) collective-permute-start(bf16[48,1024]{1,0:T(8,128)(2,1)S(1)} %get-tuple-element.55.block_ref.refs_0_), channel_id=1, source_target_pairs={{0,1},{1,0},{2,3},{3,2},{4,5},{5,4},{6,7},{7,6},{8,9},{9,8},{10,11... | collective-permute-start | bytes 294920 | tf_op jit(solution)/shard_map/ppermute | solution.py:66
  42.2 8.5 %collective-permute-start.16 = (bf16[24,2048]{1,0:T(8,128)(2,1)S(1)}, bf16[24,2048]{1,0:T(8,128)(2,1)S(1)}, u32[]{:S(2)}, u32[]{:S(2)}) collective-permute-start(bf16[24,2048]{1,0:T(8,128)(2,1)S(1)} %join.1), channel_id=1, source_target_pairs={{0,4},{4,0},{8,12},{12,8},{1,5},{5,1},{9,13},{13,9},{2,6},{6,2},{1... | collective-permute-start | bytes 294920 | tf_op jit(solution)/shard_map/ppermute | solution.py:66
  42.3 5.1 %collective-permute-start.18 = (bf16[24,1024]{1,0:T(8,128)(2,1)S(1)}, bf16[24,1024]{1,0:T(8,128)(2,1)S(1)}, u32[]{:S(2)}, u32[]{:S(2)}) collective-permute-start(bf16[24,1024]{1,0:T(8,128)(2,1)S(1)} %get-tuple-element.56), channel_id=1, source_target_pairs={{0,8},{4,12},{8,0},{12,4},{1,9},{5,13},{9,1},{13,5},{2,10},{6,14},... | collective-permute-start | bytes 147464 | tf_op jit(solution)/shard_map/ppermute | solution.py:66
  44.2 5.9 %collective-permute-start.22 = (bf16[24,1024]{1,0:T(8,128)(2,1)S(1)}, bf16[24,1024]{1,0:T(8,128)(2,1)S(1)}, u32[]{:S(2)}, u32[]{:S(2)}) collective-permute-start(bf16[24,1024]{1,0:T(8,128)(2,1)S(1)} %get-tuple-element.57), channel_id=1, source_target_pairs={{0,12},{4,8},{8,4},{12,0},{1,13},{5,9},{9,5},{13,1},{2,14},{6,10},... | collective-permute-start | bytes 147464 | tf_op jit(solution)/shard_map/ppermute | solution.py:66
  47.4 4.5 %collective-permute-start.20 = (bf16[24,1024]{1,0:T(8,128)(2,1)S(1)}, bf16[24,1024]{1,0:T(8,128)(2,1)S(1)}, u32[]{:S(2)}, u32[]{:S(2)}) collective-permute-start(bf16[24,1024]{1,0:T(8,128)(2,1)S(1)} %collective-permute-done.18.refs_6_), channel_id=1, source_target_pairs={{0,2},{1,3},{2,0},{3,1},{4,6},{5,7},{6,4},{7,5},{8,10},{9,11},{10,... | collective-permute-start | bytes 147464 | tf_op jit(solution)/shard_map/ppermute | solution.py:66
  48.0 3.9 %collective-permute-start.19 = (bf16[24,1024]{1,0:T(8,128)(2,1)S(1)}, bf16[24,1024]{1,0:T(8,128)(2,1)S(1)}, u32[]{:S(2)}, u32[]{:S(2)}) collective-permute-start(bf16[24,1024]{1,0:T(8,128)(2,1)S(1)} %collective-permute-done.18.refs_6_), channel_id=1, source_target_pairs={{0,1},{1,0},{2,3},{3,2},{4,5},{5,4},{6,7},{7,6},{8,9},{9,8},{10,11... | collective-permute-start | bytes 147464 | tf_op jit(solution)/shard_map/ppermute | solution.py:66
  50.1 4.1 %collective-permute-start.24 = (bf16[24,1024]{1,0:T(8,128)(2,1)S(1)}, bf16[24,1024]{1,0:T(8,128)(2,1)S(1)}, u32[]{:S(2)}, u32[]{:S(2)}) collective-permute-start(bf16[24,1024]{1,0:T(8,128)(2,1)S(1)} %collective-permute-done.22.refs_10_), channel_id=1, source_target_pairs={{0,2},{1,3},{2,0},{3,1},{4,6},{5,7},{6,4},{7,5},{8,10},{9,11},{10,... | collective-permute-start | bytes 147464 | tf_op jit(solution)/shard_map/ppermute | solution.py:66
  50.7 4.7 %collective-permute-start.15 = (bf16[48,1024]{1,0:T(8,128)(2,1)S(1)}, bf16[48,1024]{1,0:T(8,128)(2,1)S(1)}, u32[]{:S(2)}, u32[]{:S(2)}) collective-permute-start(bf16[48,1024]{1,0:T(8,128)(2,1)S(1)} %collective-permute-done.14.side_ref.refs_2_), channel_id=1, source_target_pairs={{0,1},{1,0},{2,3},{3,2},{4,5},{5,4},{6,7},{7,6},{8,9},{9,8},{10,11... | collective-permute-start | bytes 294920 | tf_op jit(solution)/shard_map/ppermute | solution.py:66
  50.7 4.7 %collective-permute-start.17 = (bf16[24,2048]{1,0:T(8,128)(2,1)S(1)}, bf16[24,2048]{1,0:T(8,128)(2,1)S(1)}, u32[]{:S(2)}, u32[]{:S(2)}) collective-permute-start(bf16[24,2048]{1,0:T(8,128)(2,1)S(1)} %collective-permute-done.16.refs_4_), channel_id=1, source_target_pairs={{0,1},{1,0},{2,3},{3,2},{4,5},{5,4},{6,7},{7,6},{8,9},{9,8},{10,11... | collective-permute-start | bytes 294920 | tf_op jit(solution)/shard_map/ppermute | solution.py:66
  60.0 5.1 %collective-permute-start.28 = (bf16[24,2048]{1,0:T(8,128)(2,1)S(1)}, bf16[24,2048]{1,0:T(8,128)(2,1)S(1)}, u32[]{:S(2)}, u32[]{:S(2)}) collective-permute-start(bf16[24,2048]{1,0:T(8,128)(2,1)S(1)} %get-tuple-element.60), channel_id=1, source_target_pairs={{0,4},{4,0},{8,12},{12,8},{1,5},{5,1},{9,13},{13,9},{2,6},{6,2},{1... | collective-permute-start | bytes 294920 | tf_op jit(solution)/shard_map/ppermute | solution.py:66
  60.3 5.7 %collective-permute-start.30 = (bf16[48,1024]{1,0:T(8,128)(2,1)S(1)}, bf16[48,1024]{1,0:T(8,128)(2,1)S(1)}, u32[]{:S(2)}, u32[]{:S(2)}) collective-permute-start(bf16[48,1024]{1,0:T(8,128)(2,1)S(1)} %get-tuple-element.63), channel_id=1, source_target_pairs={{0,2},{1,3},{2,0},{3,1},{4,6},{5,7},{6,4},{7,5},{8,10},{9,11},{10,... | collective-permute-start | bytes 294920 | tf_op jit(solution)/shard_map/ppermute | solution.py:66
  65.2 8.6 %collective-permute-start.29 = (bf16[32,1024]{1,0:T(8,128)(2,1)S(1)}, bf16[32,1024]{1,0:T(8,128)(2,1)S(1)}, u32[]{:S(2)}, u32[]{:S(2)}) collective-permute-start(bf16[32,1024]{1,0:T(8,128)(2,1)S(1)} %fold.3), channel_id=1, source_target_pairs={{0,2},{1,3},{2,0},{3,1},{4,6},{5,7},{6,4},{7,5},{8,10},{9,11},{10,... | collective-permute-start | bytes 196616 | tf_op jit(solution)/shard_map/ppermute | solution.py:66
  66.0 6.1 %collective-permute-start.31 = (bf16[24,1024]{1,0:T(8,128)(2,1)S(1)}, bf16[24,1024]{1,0:T(8,128)(2,1)S(1)}, u32[]{:S(2)}, u32[]{:S(2)}) collective-permute-start(bf16[24,1024]{1,0:T(8,128)(2,1)S(1)} %get-tuple-element.64), channel_id=1, source_target_pairs={{0,8},{4,12},{8,0},{12,4},{1,9},{5,13},{9,1},{13,5},{2,10},{6,14},... | collective-permute-start | bytes 147464 | tf_op jit(solution)/shard_map/ppermute | solution.py:66
  67.9 5.9 %collective-permute-start.32 = (bf16[24,1024]{1,0:T(8,128)(2,1)S(1)}, bf16[24,1024]{1,0:T(8,128)(2,1)S(1)}, u32[]{:S(2)}, u32[]{:S(2)}) collective-permute-start(bf16[24,1024]{1,0:T(8,128)(2,1)S(1)} %get-tuple-element.65), channel_id=1, source_target_pairs={{0,12},{4,8},{8,4},{12,0},{1,13},{5,9},{9,5},{13,1},{2,14},{6,10},... | collective-permute-start | bytes 147464 | tf_op jit(solution)/shard_map/ppermute | solution.py:66
  (13 other events, 52.6 us)

commit v8 on v7

--- a/solution.py
+++ b/solution.py
@@ -352,20 +352,20 @@
     )(keep, came)
 
 
-def fold_kernel(back_ref, mine_ref, came_ref, out_ref):
+def fold_kernel(back_ref, mine_ref, came_ref, after_ref, out_ref):
     cols = mine_ref.shape[1]
     rows = [mine_ref[...].astype(jnp.float32), came_ref[:, cols:].astype(jnp.float32)]
     rows = jnp.concatenate(rows, axis=0)
     out_ref[...] = narrow(product(back_ref[:, : rows.shape[0]], rows))
 
 
-def fold(back, mine, came):
+def fold(back, mine, came, after):
     return pl.pallas_call(
         fold_kernel,
         out_shape=jax.ShapeDtypeStruct((back.shape[0], mine.shape[1]), jnp.bfloat16),
         compiler_params=params(),
         name="fold",
-    )(back, mine, came)
+    )(back, mine, came, after)
 
 
 def move_kernel(n_came, last, own_ref, back_ref, pick_ref, cross_ref, *refs):
@@ -386,8 +386,7 @@
 
 def move(own, back, pick, cross, came, last):
     slots = came[0].shape[0]
-    counts = [2] + [1] * (len(came) - 2)
-    shapes = [own.shape] + ([own.shape] if last else [(slots * c, own.shape[1]) for c in counts])
+    shapes = [own.shape] + ([own.shape] if last else [(slots, own.shape[1])] * len(came))
     return pl.pallas_call(
         functools.partial(move_kernel, len(came), last),
         out_shape=[jax.ShapeDtypeStruct(s, jnp.bfloat16) for s in shapes],
@@ -410,7 +409,7 @@
     kept, beside, kept_far = down(hidden, w_down, 0, cuts, (near, next_cross))
     came = swap(beside, "ep", 1)
     blocks = add(kept_far, swap(sent, "et", 2), peers - 2)
-    cross = swap(fold(back, own_cross, came), "et", 2)
+    cross = swap(fold(back, own_cross, came, blocks[-1]), "et", 2)
     blocks = [kept, came] + [swap(b, "ep", k + 2) for k, b in enumerate(blocks)]
     return move(own, back, pick, cross, blocks, last)
 
@@ -419,21 +418,6 @@
     side = swap(block, "et", 2)
     near, far = swap(block, "et", 1), swap(side, "et", 1)
     return [(block, place), (near, place), (side, place), (far, place)]
-
-
-def join_kernel(block_ref, side_ref, out_ref):
-    rows, cols = out_ref.shape[0], block_ref.shape[1]
-    out_ref[:, :cols] = narrow(block_ref[...].astype(jnp.float32)[rows:])
-    out_ref[:, cols:] = narrow(side_ref[...].astype(jnp.float32)[rows:])
-
-
-def join(block, side):
-    return pl.pallas_call(
-        join_kernel,
-        out_shape=jax.ShapeDtypeStruct((block.shape[0] // 2, 2 * block.shape[1]), block.dtype),
-        compiler_params=params(),
-        name="join",
-    )(block, side)
 
 
 def dense_body(tokens, modulation, router, gate_weight, up_weight, down_weight, expert_ids):
@@ -455,13 +439,9 @@
         other = swap(f, "et", 1)
         blocks.append([(f, "high"), (other, "high")] * 2)
     hidden = front(blocks, flags, 0, modulation, router, pair)
-    own, near, *far = sum_back(hidden, w_down, own, back[0], pick, False)
-
-    first = spread(near)
-    beside = swap(join(near, first[2][0]), "ep", 1)
-    other = swap(beside, "et", 1)
-    blocks = [first, [(beside, 0), (other, 0), (beside, 1), (other, 1)]]
-    blocks += [spread(swap(b, "ep", k + 2)) for k, b in enumerate(far)]
+    own, *sent = sum_back(hidden, w_down, own, back[0], pick, False)
+
+    blocks = [spread(swap(b, "ep", k) if k else b) for k, b in enumerate(sent)]
     hidden = front(blocks, flags, 1, modulation, router, pair)
     return tuple(sum_back(hidden, w_down, own, back[1], pick, True))
 

time: 74.8 us -> 71.6 us (0.957)
  waiting for transfers between devices: 31.7 us -> 27 us
  starting transfers between devices: 28.6 us -> 30.1 us
    ppermute x33 -> x35, waiting for transfers between devices: 31.7 us -> 27 us  [swap(): return lax.ppermute(x, axis, [(i, i ^ bit) for i in range(size)])]
    ppermute x33 -> x35, starting transfers between devices: 28.6 us -> 30.1 us  [swap(): return lax.ppermute(x, axis, [(i, i ^ bit) for i in range(size)])]
  transfers between devices with their start and end apart: 33 -> 35, of which waited for: 18 -> 17; matrix products, arithmetic and copies ran while one was open for 0% -> 0% of each run, Pallas kernels for 8% -> 9%
where the time goes in v8:
time: 71.6 us; the launch traced here: 71.4 us
  starting transfers between devices  30.1 us (42%)
  waiting for transfers between devices  27 us (38%)
  Pallas kernels  13.4 us (19%)
  between operations  0.88 us (1%)
    ppermute x35, starting transfers between devices, swap(): return lax.ppermute(x, axis, [(i, i ^ bit) for i in range(size)])  30.1 us
    ppermute x35, waiting for transfers between devices, swap(): return lax.ppermute(x, axis, [(i, i ^ bit) for i in range(size)])  27 us
    pallas_call x1, Pallas kernels, load(): pl.pallas_call(load_kernel, in_specs=[ANY] * 3, out_specs=[VMEM] * 3, out...  3.82 us
    pallas_call x2, Pallas kernels, front(): pl.pallas_call(functools.partial(front_kernel, layout, section, experts,...  3.8 us
    pallas_call x8, Pallas kernels, down(): pl.pallas_call(functools.partial(down_kernel, flip, len(adds)), in_specs=...  2.26 us
  transfers between devices with their start and end apart: 35, of which 17 were waited for; matrix products, arithmetic and copies ran while one was open for 0% of the time, Pallas kernels for 9%

profile of v8, /device:TPU:0, one launch (start us, length us, event | category | flops | bytes accessed | tf_op | source)
XLA Modules:
  0.0 71.4 jit_solution(14325020450829674424)
XLA Ops:
  0.6 1.2 %pack.1 = (bf16[24,2176]{1,0:T(8,128)(2,1)S(1)}, bf16[24,2176]{1,0:T(8,128)(2,1)S(1)}, bf16[24,2176]{1,0:T(8,128)(2,1)S(1)}, bf16[32,1024]{1,0:T(8,128)(2,1)S(1)}) custom-call(bf16[32,4096]{1,0:T(8,128)(2,1)} %tokens_ref.3, s32[2,2,32]{2,1,0:T(2,128)} %bitcast.4), custom_call_target="tpu_custom_call" | custom-call | tf_op jit(solution)/shard_map/pack/pallas_call | solution.py:197
  1.9 3.1 %collective-permute-start = (bf16[24,2176]{1,0:T(8,128)(2,1)S(1)}, bf16[24,2176]{1,0:T(8,128)(2,1)S(1)}, u32[]{:S(2)}, u32[]{:S(2)}) collective-permute-start(bf16[24,2176]{1,0:T(8,128)(2,1)S(1)} %get-tuple-element.39), channel_id=1, source_target_pairs={{0,4},{4,0},{8,12},{12,8},{1,5},{5,1},{9,13},{13,9},{2,6},{6,2},{1... | collective-permute-start | bytes 313352 | tf_op jit(solution)/shard_map/ppermute | solution.py:66
  4.9 2.6 %collective-permute-start.2 = (bf16[24,2176]{1,0:T(8,128)(2,1)S(1)}, bf16[24,2176]{1,0:T(8,128)(2,1)S(1)}, u32[]{:S(2)}, u32[]{:S(2)}) collective-permute-start(bf16[24,2176]{1,0:T(8,128)(2,1)S(1)} %get-tuple-element.41), channel_id=1, source_target_pairs={{0,8},{4,12},{8,0},{12,4},{1,9},{5,13},{9,1},{13,5},{2,10},{6,14},... | collective-permute-start | bytes 313352 | tf_op jit(solution)/shard_map/ppermute | solution.py:66
  7.6 3.8 %load.1 = (bf16[4096,768]{1,0:T(8,128)(2,1)S(1)}, bf16[384,4096]{1,0:T(8,128)(2,1)S(1)}, f32[8,128]{1,0:T(8,128)S(1)}) custom-call(bf16[1,4096,384]{2,1,0:T(8,128)(2,1)} %gate_ref.1, bf16[1,4096,384]{2,1,0:T(8,128)(2,1)} %up_ref.1, bf16[1,384,4096]{2,1,0:T(8,128)(2,1)} %down_ref.1), custom_call_target="tpu_custom_call" | custom-call | bytes 18874368 | tf_op jit(solution)/shard_map/load/pallas_call | solution.py:101
  11.6 4.3 %collective-permute-done.2.block_ref.refs_9_.refs_18_ = bf16[24,2176]{1,0:T(8,128)(2,1)S(1)} collective-permute-done((bf16[24,2176]{1,0:T(8,128)(2,1)S(1)}, bf16[24,2176]{1,0:T(8,128)(2,1)S(1)}, u32[]{:S(2)}, u32[]{:S(2)}) %collective-permute-start.2) | collective-permute-done | bytes 104480 | tf_op jit(solution)/shard_map/ppermute | solution.py:66
  17.5 1.8 %front.2.hidden_ref = bf16[96,384]{1,0:T(8,128)(2,1)S(1)} custom-call(bf16[24,4096]{1,0:T(8,128)(2,1)S(1)} %get-tuple-element.38.refs_0_, bf16[24,2048]{1,0:T(8,128)(2,1)S(1)} %relay.3.refs_1_, bf16[24,2048]{1,0:T(8,128)(2,1)S(1)} %collective-permute-done.1.refs_2_, bf16[24,2048]{1,0:T(8,128)(2,1)S(1)} %relay.4.refs_3_, ...), custom_call_target="tpu_custom_call" | custom-call | flops 603979776 | bytes 6291456 | tf_op jit(solution)/shard_map/front/pallas_call | solution.py:294
  21.4 1.6 %collective-permute-start.9 = (bf16[48,1024]{1,0:T(8,128)(2,1)S(1)}, bf16[48,1024]{1,0:T(8,128)(2,1)S(1)}, u32[]{:S(2)}, u32[]{:S(2)}) collective-permute-start(bf16[48,1024]{1,0:T(8,128)(2,1)S(1)} %get-tuple-element.50), channel_id=1, source_target_pairs={{0,2},{1,3},{2,0},{3,1},{4,6},{5,7},{6,4},{7,5},{8,10},{9,11},{10,... | collective-permute-start | bytes 294920 | tf_op jit(solution)/shard_map/ppermute | solution.py:66
  23.3 1.5 %collective-permute-start.8 = (bf16[24,2048]{1,0:T(8,128)(2,1)S(1)}, bf16[24,2048]{1,0:T(8,128)(2,1)S(1)}, u32[]{:S(2)}, u32[]{:S(2)}) collective-permute-start(bf16[24,2048]{1,0:T(8,128)(2,1)S(1)} %get-tuple-element.48), channel_id=1, source_target_pairs={{0,4},{4,0},{8,12},{12,8},{1,5},{5,1},{9,13},{13,9},{2,6},{6,2},{1... | collective-permute-start | bytes 294920 | tf_op jit(solution)/shard_map/ppermute | solution.py:66
  24.8 1.8 %collective-permute-done.9.came_ref = bf16[48,1024]{1,0:T(8,128)(2,1)S(1)} collective-permute-done((bf16[48,1024]{1,0:T(8,128)(2,1)S(1)}, bf16[48,1024]{1,0:T(8,128)(2,1)S(1)}, u32[]{:S(2)}, u32[]{:S(2)}) %collective-permute-start.9) | collective-permute-done | bytes 98336 | tf_op jit(solution)/shard_map/ppermute | solution.py:66
  26.5 1.5 %collective-permute-done.8.came_ref.refs_1_ = bf16[24,2048]{1,0:T(8,128)(2,1)S(1)} collective-permute-done((bf16[24,2048]{1,0:T(8,128)(2,1)S(1)}, bf16[24,2048]{1,0:T(8,128)(2,1)S(1)}, u32[]{:S(2)}, u32[]{:S(2)}) %collective-permute-start.8) | collective-permute-done | bytes 98336 | tf_op jit(solution)/shard_map/ppermute | solution.py:66
  28.8 2.3 %collective-permute-start.11 = (bf16[24,1024]{1,0:T(8,128)(2,1)S(1)}, bf16[24,1024]{1,0:T(8,128)(2,1)S(1)}, u32[]{:S(2)}, u32[]{:S(2)}) collective-permute-start(bf16[24,1024]{1,0:T(8,128)(2,1)S(1)} %get-tuple-element.53), channel_id=1, source_target_pairs={{0,8},{4,12},{8,0},{12,4},{1,9},{5,13},{9,1},{13,5},{2,10},{6,14},... | collective-permute-start | bytes 147464 | tf_op jit(solution)/shard_map/ppermute | solution.py:66
  31.2 1.4 %collective-permute-start.12 = (bf16[24,1024]{1,0:T(8,128)(2,1)S(1)}, bf16[24,1024]{1,0:T(8,128)(2,1)S(1)}, u32[]{:S(2)}, u32[]{:S(2)}) collective-permute-start(bf16[24,1024]{1,0:T(8,128)(2,1)S(1)} %get-tuple-element.51.after_ref), channel_id=1, source_target_pairs={{0,12},{4,8},{8,4},{12,0},{1,13},{5,9},{9,5},{13,1},{2,14},{6,10},... | collective-permute-start | bytes 147464 | tf_op jit(solution)/shard_map/ppermute | solution.py:66
  32.5 1.3 %collective-permute-done.11.refs_2_ = bf16[24,1024]{1,0:T(8,128)(2,1)S(1)} collective-permute-done((bf16[24,1024]{1,0:T(8,128)(2,1)S(1)}, bf16[24,1024]{1,0:T(8,128)(2,1)S(1)}, u32[]{:S(2)}, u32[]{:S(2)}) %collective-permute-start.11) | collective-permute-done | bytes 49184 | tf_op jit(solution)/shard_map/ppermute | solution.py:66
  33.8 3.2 %collective-permute-done.12.refs_3_ = bf16[24,1024]{1,0:T(8,128)(2,1)S(1)} collective-permute-done((bf16[24,1024]{1,0:T(8,128)(2,1)S(1)}, bf16[24,1024]{1,0:T(8,128)(2,1)S(1)}, u32[]{:S(2)}, u32[]{:S(2)}) %collective-permute-start.12) | collective-permute-done | bytes 49184 | tf_op jit(solution)/shard_map/ppermute | solution.py:66
  37.5 1.9 %collective-permute-start.20 = (bf16[24,1024]{1,0:T(8,128)(2,1)S(1)}, bf16[24,1024]{1,0:T(8,128)(2,1)S(1)}, u32[]{:S(2)}, u32[]{:S(2)}) collective-permute-start(bf16[24,1024]{1,0:T(8,128)(2,1)S(1)} %get-tuple-element.58), channel_id=1, source_target_pairs={{0,8},{4,12},{8,0},{12,4},{1,9},{5,13},{9,1},{13,5},{2,10},{6,14},... | collective-permute-start | bytes 147464 | tf_op jit(solution)/shard_map/ppermute | solution.py:66
  39.4 2.4 %collective-permute-start.24 = (bf16[24,1024]{1,0:T(8,128)(2,1)S(1)}, bf16[24,1024]{1,0:T(8,128)(2,1)S(1)}, u32[]{:S(2)}, u32[]{:S(2)}) collective-permute-start(bf16[24,1024]{1,0:T(8,128)(2,1)S(1)} %get-tuple-element.59), channel_id=1, source_target_pairs={{0,12},{4,8},{8,4},{12,0},{1,13},{5,9},{9,5},{13,1},{2,14},{6,10},... | collective-permute-start | bytes 147464 | tf_op jit(solution)/shard_map/ppermute | solution.py:66
  41.8 1.4 %collective-permute-start.14 = (bf16[24,1024]{1,0:T(8,128)(2,1)S(1)}, bf16[24,1024]{1,0:T(8,128)(2,1)S(1)}, u32[]{:S(2)}, u32[]{:S(2)}) collective-permute-start(bf16[24,1024]{1,0:T(8,128)(2,1)S(1)} %get-tuple-element.56.refs_0_), channel_id=1, source_target_pairs={{0,2},{1,3},{2,0},{3,1},{4,6},{5,7},{6,4},{7,5},{8,10},{9,11},{10,... | collective-permute-start | bytes 147464 | tf_op jit(solution)/shard_map/ppermute | solution.py:66
  45.3 1.4 %collective-permute-start.22 = (bf16[24,1024]{1,0:T(8,128)(2,1)S(1)}, bf16[24,1024]{1,0:T(8,128)(2,1)S(1)}, u32[]{:S(2)}, u32[]{:S(2)}) collective-permute-start(bf16[24,1024]{1,0:T(8,128)(2,1)S(1)} %collective-permute-done.20.refs_8_), channel_id=1, source_target_pairs={{0,2},{1,3},{2,0},{3,1},{4,6},{5,7},{6,4},{7,5},{8,10},{9,11},{10,... | collective-permute-start | bytes 147464 | tf_op jit(solution)/shard_map/ppermute | solution.py:66
  52.1 2.0 %front.3.hidden_ref = bf16[96,384]{1,0:T(8,128)(2,1)S(1)} custom-call(bf16[24,1024]{1,0:T(8,128)(2,1)S(1)} %get-tuple-element.56.refs_0_, bf16[24,1024]{1,0:T(8,128)(2,1)S(1)} %collective-permute-done.13.refs_1_, bf16[24,1024]{1,0:T(8,128)(2,1)S(1)} %collective-permute-done.14.refs_2_, bf16[24,1024]{1,0:T(8,128)(2,1)S(1)} %collective-permute-done.15.refs_3_, ...), custom_call_target="tpu_custom_call" | custom-call | flops 603979776 | bytes 6291456 | tf_op jit(solution)/shard_map/front/pallas_call | solution.py:294
  57.7 3.5 %collective-permute-done.31.came_ref = bf16[48,1024]{1,0:T(8,128)(2,1)S(1)} collective-permute-done((bf16[48,1024]{1,0:T(8,128)(2,1)S(1)}, bf16[48,1024]{1,0:T(8,128)(2,1)S(1)}, u32[]{:S(2)}, u32[]{:S(2)}) %collective-permute-start.31) | collective-permute-done | bytes 98336 | tf_op jit(solution)/shard_map/ppermute | solution.py:66
  63.5 1.2 %collective-permute-start.33 = (bf16[24,1024]{1,0:T(8,128)(2,1)S(1)}, bf16[24,1024]{1,0:T(8,128)(2,1)S(1)}, u32[]{:S(2)}, u32[]{:S(2)}) collective-permute-start(bf16[24,1024]{1,0:T(8,128)(2,1)S(1)} %get-tuple-element.67), channel_id=1, source_target_pairs={{0,8},{4,12},{8,0},{12,4},{1,9},{5,13},{9,1},{13,5},{2,10},{6,14},... | collective-permute-start | bytes 147464 | tf_op jit(solution)/shard_map/ppermute | solution.py:66
  64.7 1.4 %collective-permute-start.34 = (bf16[24,1024]{1,0:T(8,128)(2,1)S(1)}, bf16[24,1024]{1,0:T(8,128)(2,1)S(1)}, u32[]{:S(2)}, u32[]{:S(2)}) collective-permute-start(bf16[24,1024]{1,0:T(8,128)(2,1)S(1)} %get-tuple-element.65.after_ref), channel_id=1, source_target_pairs={{0,12},{4,8},{8,4},{12,0},{1,13},{5,9},{9,5},{13,1},{2,14},{6,10},... | collective-permute-start | bytes 147464 | tf_op jit(solution)/shard_map/ppermute | solution.py:66
  66.1 3.1 %collective-permute-done.33.refs_2_ = bf16[24,1024]{1,0:T(8,128)(2,1)S(1)} collective-permute-done((bf16[24,1024]{1,0:T(8,128)(2,1)S(1)}, bf16[24,1024]{1,0:T(8,128)(2,1)S(1)}, u32[]{:S(2)}, u32[]{:S(2)}) %collective-permute-start.33) | collective-permute-done | bytes 49184 | tf_op jit(solution)/shard_map/ppermute | solution.py:66
  69.2 1.4 %collective-permute-done.34.refs_3_ = bf16[24,1024]{1,0:T(8,128)(2,1)S(1)} collective-permute-done((bf16[24,1024]{1,0:T(8,128)(2,1)S(1)}, bf16[24,1024]{1,0:T(8,128)(2,1)S(1)}, u32[]{:S(2)}, u32[]{:S(2)}) %collective-permute-start.34) | collective-permute-done | bytes 49184 | tf_op jit(solution)/shard_map/ppermute | solution.py:66
  (76 shorter events, 19.3 us)
Async XLA Ops:
  1.9 9.6 %collective-permute-start = (bf16[24,2176]{1,0:T(8,128)(2,1)S(1)}, bf16[24,2176]{1,0:T(8,128)(2,1)S(1)}, u32[]{:S(2)}, u32[]{:S(2)}) collective-permute-start(bf16[24,2176]{1,0:T(8,128)(2,1)S(1)} %get-tuple-element.39), channel_id=1, source_target_pairs={{0,4},{4,0},{8,12},{12,8},{1,5},{5,1},{9,13},{13,9},{2,6},{6,2},{1... | collective-permute-start | bytes 313352 | tf_op jit(solution)/shard_map/ppermute | solution.py:66
  4.9 10.9 %collective-permute-start.2 = (bf16[24,2176]{1,0:T(8,128)(2,1)S(1)}, bf16[24,2176]{1,0:T(8,128)(2,1)S(1)}, u32[]{:S(2)}, u32[]{:S(2)}) collective-permute-start(bf16[24,2176]{1,0:T(8,128)(2,1)S(1)} %get-tuple-element.41), channel_id=1, source_target_pairs={{0,8},{4,12},{8,0},{12,4},{1,9},{5,13},{9,1},{13,5},{2,10},{6,14},... | collective-permute-start | bytes 313352 | tf_op jit(solution)/shard_map/ppermute | solution.py:66
  7.5 8.4 %collective-permute-start.4 = (bf16[24,2176]{1,0:T(8,128)(2,1)S(1)}, bf16[24,2176]{1,0:T(8,128)(2,1)S(1)}, u32[]{:S(2)}, u32[]{:S(2)}) collective-permute-start(bf16[24,2176]{1,0:T(8,128)(2,1)S(1)} %get-tuple-element.42), channel_id=1, source_target_pairs={{0,12},{4,8},{8,4},{12,0},{1,13},{5,9},{9,5},{13,1},{2,14},{6,10},... | collective-permute-start | bytes 313352 | tf_op jit(solution)/shard_map/ppermute | solution.py:66
  11.5 5.8 %collective-permute-start.1 = (bf16[24,2048]{1,0:T(8,128)(2,1)S(1)}, bf16[24,2048]{1,0:T(8,128)(2,1)S(1)}, u32[]{:S(2)}, u32[]{:S(2)}) collective-permute-start(bf16[24,2048]{1,0:T(8,128)(2,1)S(1)} %relay.3.refs_1_), channel_id=1, source_target_pairs={{0,1},{1,0},{2,3},{3,2},{4,5},{5,4},{6,7},{7,6},{8,9},{9,8},{10,11... | collective-permute-start | bytes 294920 | tf_op jit(solution)/shard_map/ppermute | solution.py:66
  21.4 5.1 %collective-permute-start.9 = (bf16[48,1024]{1,0:T(8,128)(2,1)S(1)}, bf16[48,1024]{1,0:T(8,128)(2,1)S(1)}, u32[]{:S(2)}, u32[]{:S(2)}) collective-permute-start(bf16[48,1024]{1,0:T(8,128)(2,1)S(1)} %get-tuple-element.50), channel_id=1, source_target_pairs={{0,2},{1,3},{2,0},{3,1},{4,6},{5,7},{6,4},{7,5},{8,10},{9,11},{10,... | collective-permute-start | bytes 294920 | tf_op jit(solution)/shard_map/ppermute | solution.py:66
  23.3 4.8 %collective-permute-start.8 = (bf16[24,2048]{1,0:T(8,128)(2,1)S(1)}, bf16[24,2048]{1,0:T(8,128)(2,1)S(1)}, u32[]{:S(2)}, u32[]{:S(2)}) collective-permute-start(bf16[24,2048]{1,0:T(8,128)(2,1)S(1)} %get-tuple-element.48), channel_id=1, source_target_pairs={{0,4},{4,0},{8,12},{12,8},{1,5},{5,1},{9,13},{13,9},{2,6},{6,2},{1... | collective-permute-start | bytes 294920 | tf_op jit(solution)/shard_map/ppermute | solution.py:66
  28.2 8.8 %collective-permute-start.10 = (bf16[32,1024]{1,0:T(8,128)(2,1)S(1)}, bf16[32,1024]{1,0:T(8,128)(2,1)S(1)}, u32[]{:S(2)}, u32[]{:S(2)}) collective-permute-start(bf16[32,1024]{1,0:T(8,128)(2,1)S(1)} %fold.2), channel_id=1, source_target_pairs={{0,2},{1,3},{2,0},{3,1},{4,6},{5,7},{6,4},{7,5},{8,10},{9,11},{10,... | collective-permute-start | bytes 196616 | tf_op jit(solution)/shard_map/ppermute | solution.py:66
  28.8 5.0 %collective-permute-start.11 = (bf16[24,1024]{1,0:T(8,128)(2,1)S(1)}, bf16[24,1024]{1,0:T(8,128)(2,1)S(1)}, u32[]{:S(2)}, u32[]{:S(2)}) collective-permute-start(bf16[24,1024]{1,0:T(8,128)(2,1)S(1)} %get-tuple-element.53), channel_id=1, source_target_pairs={{0,8},{4,12},{8,0},{12,4},{1,9},{5,13},{9,1},{13,5},{2,10},{6,14},... | collective-permute-start | bytes 147464 | tf_op jit(solution)/shard_map/ppermute | solution.py:66
  31.2 5.9 %collective-permute-start.12 = (bf16[24,1024]{1,0:T(8,128)(2,1)S(1)}, bf16[24,1024]{1,0:T(8,128)(2,1)S(1)}, u32[]{:S(2)}, u32[]{:S(2)}) collective-permute-start(bf16[24,1024]{1,0:T(8,128)(2,1)S(1)} %get-tuple-element.51.after_ref), channel_id=1, source_target_pairs={{0,12},{4,8},{8,4},{12,0},{1,13},{5,9},{9,5},{13,1},{2,14},{6,10},... | collective-permute-start | bytes 147464 | tf_op jit(solution)/shard_map/ppermute | solution.py:66
  37.4 5.9 %collective-permute-start.16 = (bf16[24,1024]{1,0:T(8,128)(2,1)S(1)}, bf16[24,1024]{1,0:T(8,128)(2,1)S(1)}, u32[]{:S(2)}, u32[]{:S(2)}) collective-permute-start(bf16[24,1024]{1,0:T(8,128)(2,1)S(1)} %get-tuple-element.57), channel_id=1, source_target_pairs={{0,4},{4,0},{8,12},{12,8},{1,5},{5,1},{9,13},{13,9},{2,6},{6,2},{1... | collective-permute-start | bytes 147464 | tf_op jit(solution)/shard_map/ppermute | solution.py:66
  37.5 6.4 %collective-permute-start.20 = (bf16[24,1024]{1,0:T(8,128)(2,1)S(1)}, bf16[24,1024]{1,0:T(8,128)(2,1)S(1)}, u32[]{:S(2)}, u32[]{:S(2)}) collective-permute-start(bf16[24,1024]{1,0:T(8,128)(2,1)S(1)} %get-tuple-element.58), channel_id=1, source_target_pairs={{0,8},{4,12},{8,0},{12,4},{1,9},{5,13},{9,1},{13,5},{2,10},{6,14},... | collective-permute-start | bytes 147464 | tf_op jit(solution)/shard_map/ppermute | solution.py:66
  39.4 5.9 %collective-permute-start.24 = (bf16[24,1024]{1,0:T(8,128)(2,1)S(1)}, bf16[24,1024]{1,0:T(8,128)(2,1)S(1)}, u32[]{:S(2)}, u32[]{:S(2)}) collective-permute-start(bf16[24,1024]{1,0:T(8,128)(2,1)S(1)} %get-tuple-element.59), channel_id=1, source_target_pairs={{0,12},{4,8},{8,4},{12,0},{1,13},{5,9},{9,5},{13,1},{2,14},{6,10},... | collective-permute-start | bytes 147464 | tf_op jit(solution)/shard_map/ppermute | solution.py:66
  41.8 4.9 %collective-permute-start.14 = (bf16[24,1024]{1,0:T(8,128)(2,1)S(1)}, bf16[24,1024]{1,0:T(8,128)(2,1)S(1)}, u32[]{:S(2)}, u32[]{:S(2)}) collective-permute-start(bf16[24,1024]{1,0:T(8,128)(2,1)S(1)} %get-tuple-element.56.refs_0_), channel_id=1, source_target_pairs={{0,2},{1,3},{2,0},{3,1},{4,6},{5,7},{6,4},{7,5},{8,10},{9,11},{10,... | collective-permute-start | bytes 147464 | tf_op jit(solution)/shard_map/ppermute | solution.py:66
  43.3 3.4 %collective-permute-start.13 = (bf16[24,1024]{1,0:T(8,128)(2,1)S(1)}, bf16[24,1024]{1,0:T(8,128)(2,1)S(1)}, u32[]{:S(2)}, u32[]{:S(2)}) collective-permute-start(bf16[24,1024]{1,0:T(8,128)(2,1)S(1)} %get-tuple-element.56.refs_0_), channel_id=1, source_target_pairs={{0,1},{1,0},{2,3},{3,2},{4,5},{5,4},{6,7},{7,6},{8,9},{9,8},{10,11... | collective-permute-start | bytes 147464 | tf_op jit(solution)/shard_map/ppermute | solution.py:66
  43.3 4.5 %collective-permute-start.18 = (bf16[24,1024]{1,0:T(8,128)(2,1)S(1)}, bf16[24,1024]{1,0:T(8,128)(2,1)S(1)}, u32[]{:S(2)}, u32[]{:S(2)}) collective-permute-start(bf16[24,1024]{1,0:T(8,128)(2,1)S(1)} %collective-permute-done.16.refs_4_), channel_id=1, source_target_pairs={{0,2},{1,3},{2,0},{3,1},{4,6},{5,7},{6,4},{7,5},{8,10},{9,11},{10,... | collective-permute-start | bytes 147464 | tf_op jit(solution)/shard_map/ppermute | solution.py:66
  43.9 4.1 %collective-permute-start.17 = (bf16[24,1024]{1,0:T(8,128)(2,1)S(1)}, bf16[24,1024]{1,0:T(8,128)(2,1)S(1)}, u32[]{:S(2)}, u32[]{:S(2)}) collective-permute-start(bf16[24,1024]{1,0:T(8,128)(2,1)S(1)} %collective-permute-done.16.refs_4_), channel_id=1, source_target_pairs={{0,1},{1,0},{2,3},{3,2},{4,5},{5,4},{6,7},{7,6},{8,9},{9,8},{10,11... | collective-permute-start | bytes 147464 | tf_op jit(solution)/shard_map/ppermute | solution.py:66
  45.3 4.1 %collective-permute-start.22 = (bf16[24,1024]{1,0:T(8,128)(2,1)S(1)}, bf16[24,1024]{1,0:T(8,128)(2,1)S(1)}, u32[]{:S(2)}, u32[]{:S(2)}) collective-permute-start(bf16[24,1024]{1,0:T(8,128)(2,1)S(1)} %collective-permute-done.20.refs_8_), channel_id=1, source_target_pairs={{0,2},{1,3},{2,0},{3,1},{4,6},{5,7},{6,4},{7,5},{8,10},{9,11},{10,... | collective-permute-start | bytes 147464 | tf_op jit(solution)/shard_map/ppermute | solution.py:66
  46.7 4.2 %collective-permute-start.26 = (bf16[24,1024]{1,0:T(8,128)(2,1)S(1)}, bf16[24,1024]{1,0:T(8,128)(2,1)S(1)}, u32[]{:S(2)}, u32[]{:S(2)}) collective-permute-start(bf16[24,1024]{1,0:T(8,128)(2,1)S(1)} %collective-permute-done.24.refs_12_), channel_id=1, source_target_pairs={{0,2},{1,3},{2,0},{3,1},{4,6},{5,7},{6,4},{7,5},{8,10},{9,11},{10,... | collective-permute-start | bytes 147464 | tf_op jit(solution)/shard_map/ppermute | solution.py:66
  47.8 3.1 %collective-permute-start.25 = (bf16[24,1024]{1,0:T(8,128)(2,1)S(1)}, bf16[24,1024]{1,0:T(8,128)(2,1)S(1)}, u32[]{:S(2)}, u32[]{:S(2)}) collective-permute-start(bf16[24,1024]{1,0:T(8,128)(2,1)S(1)} %collective-permute-done.24.refs_12_), channel_id=1, source_target_pairs={{0,1},{1,0},{2,3},{3,2},{4,5},{5,4},{6,7},{7,6},{8,9},{9,8},{10,11... | collective-permute-start | bytes 147464 | tf_op jit(solution)/shard_map/ppermute | solution.py:66
  56.2 4.9 %collective-permute-start.31 = (bf16[48,1024]{1,0:T(8,128)(2,1)S(1)}, bf16[48,1024]{1,0:T(8,128)(2,1)S(1)}, u32[]{:S(2)}, u32[]{:S(2)}) collective-permute-start(bf16[48,1024]{1,0:T(8,128)(2,1)S(1)} %get-tuple-element.64), channel_id=1, source_target_pairs={{0,2},{1,3},{2,0},{3,1},{4,6},{5,7},{6,4},{7,5},{8,10},{9,11},{10,... | collective-permute-start | bytes 294920 | tf_op jit(solution)/shard_map/ppermute | solution.py:66
  57.6 4.7 %collective-permute-start.30 = (bf16[24,2048]{1,0:T(8,128)(2,1)S(1)}, bf16[24,2048]{1,0:T(8,128)(2,1)S(1)}, u32[]{:S(2)}, u32[]{:S(2)}) collective-permute-start(bf16[24,2048]{1,0:T(8,128)(2,1)S(1)} %get-tuple-element.62), channel_id=1, source_target_pairs={{0,4},{4,0},{8,12},{12,8},{1,5},{5,1},{9,13},{13,9},{2,6},{6,2},{1... | collective-permute-start | bytes 294920 | tf_op jit(solution)/shard_map/ppermute | solution.py:66
  62.4 8.2 %collective-permute-start.32 = (bf16[32,1024]{1,0:T(8,128)(2,1)S(1)}, bf16[32,1024]{1,0:T(8,128)(2,1)S(1)}, u32[]{:S(2)}, u32[]{:S(2)}) collective-permute-start(bf16[32,1024]{1,0:T(8,128)(2,1)S(1)} %fold.3), channel_id=1, source_target_pairs={{0,2},{1,3},{2,0},{3,1},{4,6},{5,7},{6,4},{7,5},{8,10},{9,11},{10,... | collective-permute-start | bytes 196616 | tf_op jit(solution)/shard_map/ppermute | solution.py:66
  63.5 5.7 %collective-permute-start.33 = (bf16[24,1024]{1,0:T(8,128)(2,1)S(1)}, bf16[24,1024]{1,0:T(8,128)(2,1)S(1)}, u32[]{:S(2)}, u32[]{:S(2)}) collective-permute-start(bf16[24,1024]{1,0:T(8,128)(2,1)S(1)} %get-tuple-element.67), channel_id=1, source_target_pairs={{0,8},{4,12},{8,0},{12,4},{1,9},{5,13},{9,1},{13,5},{2,10},{6,14},... | collective-permute-start | bytes 147464 | tf_op jit(solution)/shard_map/ppermute | solution.py:66
  64.7 5.9 %collective-permute-start.34 = (bf16[24,1024]{1,0:T(8,128)(2,1)S(1)}, bf16[24,1024]{1,0:T(8,128)(2,1)S(1)}, u32[]{:S(2)}, u32[]{:S(2)}) collective-permute-start(bf16[24,1024]{1,0:T(8,128)(2,1)S(1)} %get-tuple-element.65.after_ref), channel_id=1, source_target_pairs={{0,12},{4,8},{8,4},{12,0},{1,13},{5,9},{9,5},{13,1},{2,14},{6,10},... | collective-permute-start | bytes 147464 | tf_op jit(solution)/shard_map/ppermute | solution.py:66
  (15 other events, 58.7 us)

commit v9 on v6

--- a/solution.py
+++ b/solution.py
@@ -232,17 +232,19 @@
     )(tokens, ids)
 
 
-def front_kernel(layout, section, experts, n_flags, *refs):
+def front_kernel(layout, order, section, experts, n_flags, *refs):
     n = sum(len(block) for block in layout)
     x_refs, flag_refs = list(refs[:n]), refs[n : n + n_flags]
+    flag_refs = [flag_refs[order.index(k)] for k in range(n_flags)]
     mod_ref, router_ref, pair_ref, out_ref, normed_ref = refs[n + n_flags :]
     width = normed_ref.shape[1]
     hidden = out_ref.shape[1]
     quarter = width // 4
     et = lax.axis_index("et")
-    blocks = []
-    for block in layout:
-        blocks.append([(x_refs.pop(0), cols, flip) for cols, flip in block])
+    blocks = {}
+    for k in order:
+        blocks[k] = [(x_refs.pop(0), cols, flip) for cols, flip in layout[k]]
+    blocks = [blocks[k] for k in range(len(layout))]
 
     def part(block, flip):
         for ref, cols, at in block:
@@ -279,14 +281,15 @@
     out_ref[...] = units.astype(jnp.bfloat16)
 
 
-def front(blocks, flags, section, mod, router, pair):
+def front(blocks, flags, order, section, mod, router, pair):
     width, hidden = pair.shape[0], pair.shape[1] // 2
     rows = sum(f.shape[0] for f in flags)
     experts = router.shape[0]
-    xs = [x for block in blocks for x, _, _ in block]
+    xs = [x for k in order for x, _, _ in blocks[k]]
+    flags = [flags[k] for k in order]
     layout = [[piece[1:] for piece in block] for block in blocks]
     return pl.pallas_call(
-        functools.partial(front_kernel, layout, section, experts, len(flags)),
+        functools.partial(front_kernel, layout, order, section, experts, len(flags)),
         in_specs=[VMEM] * (len(xs) + len(flags) + 3),
         scratch_shapes=[pltpu.VMEM((rows, width), jnp.bfloat16)],
         out_shape=jax.ShapeDtypeStruct((rows, hidden), jnp.bfloat16),
@@ -372,7 +375,7 @@
     some = peers // 2
     far = swap(down(hidden, w_down, 3, 1)[0], "et", 1)
     near = swap(down(hidden, w_down, 1, 1)[0], "et", 1)
-    first, last = down(hidden, w_down, 2, 2, (far,))
+    first, last = add(down(hidden, w_down, 2, 1, (), jnp.float32)[0], far, 2)
     last, first = swap(last, "et", 2), swap(first, "et", 2)
     keep_first, keep_last = down(hidden, w_down, 0, 2, (near,), jnp.float32)
     later = add(keep_last, last, peers - some)
@@ -400,16 +403,17 @@
     pair, w_down, done = load(gate_weight, up_weight, down_weight)
     mine, flags, *choice = own_rows(tokens, ids, experts, slots)
     pick, back = choice[2], choice[1::2]
-    flags = [flags] + [swap(p, "ep", k + 1) for k, p in enumerate(packed)]
-    blocks = [[(mine, width, 0)]]
-    for f in flags[1:]:
-        f = relay(f, half, done)
-        blocks.append([(f, half, 0), (swap(f, "et", 1), half, 1)])
-    hidden = front(blocks, flags, 0, modulation, router, pair)
+    order = [*range(2, len(packed) + 1), 1]
+    came = {k: swap(packed[k - 1], "ep", k) for k in order}
+    halves = {k: relay(came[k], half, done) for k in order}
+    others = {k: swap(halves[k], "et", 1) for k in order}
+    flags = [flags] + [came[k] for k in sorted(order)]
+    blocks = [[(mine, width, 0)]] + [[(halves[k], half, 0), (others[k], half, 1)] for k in sorted(order)]
+    hidden = front(blocks, flags, order + [0], 0, modulation, router, pair)
     own, *sent = sum_back(hidden, w_down, own, back[0], pick, False)
 
     blocks = [spread(swap(b, "ep", k) if k else b, quarter) for k, b in enumerate(sent)]
-    hidden = front(blocks, flags, 1, modulation, router, pair)
+    hidden = front(blocks, flags, sorted(order + [0]), 1, modulation, router, pair)
     return tuple(sum_back(hidden, w_down, own, back[1], pick, True))
 
 

time: 68.3 us -> 67.7 us (level)
  waiting for transfers between devices: 24 us -> 23 us
    ppermute x35, waiting for transfers between devices: 24 us -> 23 us  [swap(): return lax.ppermute(x, axis, [(i, i ^ bit) for i in range(size)])]
  transfers between devices with their start and end apart: 35 -> 35, of which waited for: 18 -> 17; matrix products, arithmetic and copies ran while one was open for 0% -> 0% of each run, Pallas kernels for 9% -> 10%
where the time goes in v9:
time: 67.7 us; the launch traced here: 67.5 us
  starting transfers between devices  30.6 us (45%)
  waiting for transfers between devices  23 us (34%)
  Pallas kernels  13.2 us (19%)
  between operations  0.83 us (1%)
    ppermute x35, starting transfers between devices, swap(): return lax.ppermute(x, axis, [(i, i ^ bit) for i in range(size)])  30.6 us
    ppermute x35, waiting for transfers between devices, swap(): return lax.ppermute(x, axis, [(i, i ^ bit) for i in range(size)])  23 us
    pallas_call x2, Pallas kernels, front(): pl.pallas_call(functools.partial(front_kernel, layout, order, section, ex...  3.81 us
    pallas_call x1, Pallas kernels, load(): pl.pallas_call(load_kernel, in_specs=[ANY] * 3, out_specs=[VMEM] * 3, out...  3.78 us
    pallas_call x8, Pallas kernels, down(): pl.pallas_call(functools.partial(down_kernel, flip, len(adds)), in_specs=...  2.23 us
  transfers between devices with their start and end apart: 35, of which 17 were waited for; matrix products, arithmetic and copies ran while one was open for 0% of the time, Pallas kernels for 10%

profile of v9, /device:TPU:0, one launch (start us, length us, event | category | flops | bytes accessed | tf_op | source)
XLA Modules:
  0.0 67.5 jit_solution(14466742368869621155)
XLA Ops:
  0.6 1.2 %pack.1 = (bf16[24,2176]{1,0:T(8,128)(2,1)S(1)}, bf16[24,2176]{1,0:T(8,128)(2,1)S(1)}, bf16[24,2176]{1,0:T(8,128)(2,1)S(1)}, bf16[32,1024]{1,0:T(8,128)(2,1)S(1)}) custom-call(bf16[32,4096]{1,0:T(8,128)(2,1)} %tokens_ref.3, s32[2,2,32]{2,1,0:T(2,128)} %bitcast.4), custom_call_target="tpu_custom_call" | custom-call | tf_op jit(solution)/shard_map/pack/pallas_call | solution.py:197
  1.9 4.1 %collective-permute-start = (bf16[24,2176]{1,0:T(8,128)(2,1)S(1)}, bf16[24,2176]{1,0:T(8,128)(2,1)S(1)}, u32[]{:S(2)}, u32[]{:S(2)}) collective-permute-start(bf16[24,2176]{1,0:T(8,128)(2,1)S(1)} %get-tuple-element.38), channel_id=1, source_target_pairs={{0,8},{4,12},{8,0},{12,4},{1,9},{5,13},{9,1},{13,5},{2,10},{6,14},... | collective-permute-start | bytes 313352 | tf_op jit(solution)/shard_map/ppermute | solution.py:66
  6.0 1.3 %collective-permute-start.2 = (bf16[24,2176]{1,0:T(8,128)(2,1)S(1)}, bf16[24,2176]{1,0:T(8,128)(2,1)S(1)}, u32[]{:S(2)}, u32[]{:S(2)}) collective-permute-start(bf16[24,2176]{1,0:T(8,128)(2,1)S(1)} %get-tuple-element.40), channel_id=1, source_target_pairs={{0,12},{4,8},{8,4},{12,0},{1,13},{5,9},{9,5},{13,1},{2,14},{6,10},... | collective-permute-start | bytes 313352 | tf_op jit(solution)/shard_map/ppermute | solution.py:66
  7.6 3.8 %load.1 = (bf16[4096,768]{1,0:T(8,128)(2,1)S(1)}, bf16[384,4096]{1,0:T(8,128)(2,1)S(1)}, f32[8,128]{1,0:T(8,128)S(1)}) custom-call(bf16[1,4096,384]{2,1,0:T(8,128)(2,1)} %gate_ref.1, bf16[1,4096,384]{2,1,0:T(8,128)(2,1)} %up_ref.1, bf16[1,384,4096]{2,1,0:T(8,128)(2,1)} %down_ref.1), custom_call_target="tpu_custom_call" | custom-call | bytes 18874368 | tf_op jit(solution)/shard_map/load/pallas_call | solution.py:101
  11.4 2.8 %collective-permute-done.block_ref.refs_7_.refs_18_ = bf16[24,2176]{1,0:T(8,128)(2,1)S(1)} collective-permute-done((bf16[24,2176]{1,0:T(8,128)(2,1)S(1)}, bf16[24,2176]{1,0:T(8,128)(2,1)S(1)}, u32[]{:S(2)}, u32[]{:S(2)}) %collective-permute-start) | collective-permute-done | bytes 104480 | tf_op jit(solution)/shard_map/ppermute | solution.py:66
  16.3 1.8 %front.2.hidden_ref = bf16[96,384]{1,0:T(8,128)(2,1)S(1)} custom-call(bf16[24,2048]{1,0:T(8,128)(2,1)S(1)} %relay.3.refs_0_, bf16[24,2048]{1,0:T(8,128)(2,1)S(1)} %collective-permute-done.1.refs_1_, bf16[24,2048]{1,0:T(8,128)(2,1)S(1)} %relay.4.refs_2_, bf16[24,2048]{1,0:T(8,128)(2,1)S(1)} %collective-permute-done.3.refs_3_, ...), custom_call_target="tpu_custom_call" | custom-call | flops 603979776 | bytes 6291456 | tf_op jit(solution)/shard_map/front/pallas_call | solution.py:291
  20.0 1.9 %collective-permute-start.10 = (bf16[48,1024]{1,0:T(8,128)(2,1)S(1)}, bf16[48,1024]{1,0:T(8,128)(2,1)S(1)}, u32[]{:S(2)}, u32[]{:S(2)}) collective-permute-start(bf16[48,1024]{1,0:T(8,128)(2,1)S(1)} %get-tuple-element.51), channel_id=1, source_target_pairs={{0,2},{1,3},{2,0},{3,1},{4,6},{5,7},{6,4},{7,5},{8,10},{9,11},{10,... | collective-permute-start | bytes 294920 | tf_op jit(solution)/shard_map/ppermute | solution.py:66
  22.4 3.3 %collective-permute-done.10.came_ref = bf16[48,1024]{1,0:T(8,128)(2,1)S(1)} collective-permute-done((bf16[48,1024]{1,0:T(8,128)(2,1)S(1)}, bf16[48,1024]{1,0:T(8,128)(2,1)S(1)}, u32[]{:S(2)}, u32[]{:S(2)}) %collective-permute-start.10) | collective-permute-done | bytes 98336 | tf_op jit(solution)/shard_map/ppermute | solution.py:66
  25.7 3.7 %collective-permute-start.11 = (bf16[24,1024]{1,0:T(8,128)(2,1)S(1)}, bf16[24,1024]{1,0:T(8,128)(2,1)S(1)}, u32[]{:S(2)}, u32[]{:S(2)}) collective-permute-start(bf16[24,1024]{1,0:T(8,128)(2,1)S(1)} %get-tuple-element.52), channel_id=1, source_target_pairs={{0,8},{4,12},{8,0},{12,4},{1,9},{5,13},{9,1},{13,5},{2,10},{6,14},... | collective-permute-start | bytes 147464 | tf_op jit(solution)/shard_map/ppermute | solution.py:66
  30.1 1.9 %collective-permute-done.11.refs_2_ = bf16[24,1024]{1,0:T(8,128)(2,1)S(1)} collective-permute-done((bf16[24,1024]{1,0:T(8,128)(2,1)S(1)}, bf16[24,1024]{1,0:T(8,128)(2,1)S(1)}, u32[]{:S(2)}, u32[]{:S(2)}) %collective-permute-start.11) | collective-permute-done | bytes 49184 | tf_op jit(solution)/shard_map/ppermute | solution.py:66
  32.0 3.3 %collective-permute-done.12.refs_3_ = bf16[24,1024]{1,0:T(8,128)(2,1)S(1)} collective-permute-done((bf16[24,1024]{1,0:T(8,128)(2,1)S(1)}, bf16[24,1024]{1,0:T(8,128)(2,1)S(1)}, u32[]{:S(2)}, u32[]{:S(2)}) %collective-permute-start.12) | collective-permute-done | bytes 49184 | tf_op jit(solution)/shard_map/ppermute | solution.py:66
  35.7 2.7 %collective-permute-start.20 = (bf16[24,1024]{1,0:T(8,128)(2,1)S(1)}, bf16[24,1024]{1,0:T(8,128)(2,1)S(1)}, u32[]{:S(2)}, u32[]{:S(2)}) collective-permute-start(bf16[24,1024]{1,0:T(8,128)(2,1)S(1)} %get-tuple-element.58), channel_id=1, source_target_pairs={{0,8},{4,12},{8,0},{12,4},{1,9},{5,13},{9,1},{13,5},{2,10},{6,14},... | collective-permute-start | bytes 147464 | tf_op jit(solution)/shard_map/ppermute | solution.py:66
  38.3 1.7 %collective-permute-start.24 = (bf16[24,1024]{1,0:T(8,128)(2,1)S(1)}, bf16[24,1024]{1,0:T(8,128)(2,1)S(1)}, u32[]{:S(2)}, u32[]{:S(2)}) collective-permute-start(bf16[24,1024]{1,0:T(8,128)(2,1)S(1)} %get-tuple-element.59), channel_id=1, source_target_pairs={{0,12},{4,8},{8,4},{12,0},{1,13},{5,9},{9,5},{13,1},{2,14},{6,10},... | collective-permute-start | bytes 147464 | tf_op jit(solution)/shard_map/ppermute | solution.py:66
  40.0 1.5 %collective-permute-start.13 = (bf16[24,1024]{1,0:T(8,128)(2,1)S(1)}, bf16[24,1024]{1,0:T(8,128)(2,1)S(1)}, u32[]{:S(2)}, u32[]{:S(2)}) collective-permute-start(bf16[24,1024]{1,0:T(8,128)(2,1)S(1)} %get-tuple-element.56.refs_0_), channel_id=1, source_target_pairs={{0,2},{1,3},{2,0},{3,1},{4,6},{5,7},{6,4},{7,5},{8,10},{9,11},{10,... | collective-permute-start | bytes 147464 | tf_op jit(solution)/shard_map/ppermute | solution.py:66
  42.3 1.3 %collective-permute-start.21 = (bf16[24,1024]{1,0:T(8,128)(2,1)S(1)}, bf16[24,1024]{1,0:T(8,128)(2,1)S(1)}, u32[]{:S(2)}, u32[]{:S(2)}) collective-permute-start(bf16[24,1024]{1,0:T(8,128)(2,1)S(1)} %collective-permute-done.20.refs_8_), channel_id=1, source_target_pairs={{0,2},{1,3},{2,0},{3,1},{4,6},{5,7},{6,4},{7,5},{8,10},{9,11},{10,... | collective-permute-start | bytes 147464 | tf_op jit(solution)/shard_map/ppermute | solution.py:66
  44.2 1.5 %collective-permute-start.25 = (bf16[24,1024]{1,0:T(8,128)(2,1)S(1)}, bf16[24,1024]{1,0:T(8,128)(2,1)S(1)}, u32[]{:S(2)}, u32[]{:S(2)}) collective-permute-start(bf16[24,1024]{1,0:T(8,128)(2,1)S(1)} %collective-permute-done.24.refs_12_), channel_id=1, source_target_pairs={{0,2},{1,3},{2,0},{3,1},{4,6},{5,7},{6,4},{7,5},{8,10},{9,11},{10,... | collective-permute-start | bytes 147464 | tf_op jit(solution)/shard_map/ppermute | solution.py:66
  47.1 1.2 %collective-permute-done.25.refs_13_ = bf16[24,1024]{1,0:T(8,128)(2,1)S(1)} collective-permute-done((bf16[24,1024]{1,0:T(8,128)(2,1)S(1)}, bf16[24,1024]{1,0:T(8,128)(2,1)S(1)}, u32[]{:S(2)}, u32[]{:S(2)}) %collective-permute-start.25) | collective-permute-done | bytes 49184 | tf_op jit(solution)/shard_map/ppermute | solution.py:66
  50.1 2.0 %front.3.hidden_ref = bf16[96,384]{1,0:T(8,128)(2,1)S(1)} custom-call(bf16[24,1024]{1,0:T(8,128)(2,1)S(1)} %get-tuple-element.56.refs_0_, bf16[24,1024]{1,0:T(8,128)(2,1)S(1)} %collective-permute-done.13.refs_1_, bf16[24,1024]{1,0:T(8,128)(2,1)S(1)} %collective-permute-done.14.refs_2_, bf16[24,1024]{1,0:T(8,128)(2,1)S(1)} %collective-permute-done.15.refs_3_, ...), custom_call_target="tpu_custom_call" | custom-call | flops 603979776 | bytes 6291456 | tf_op jit(solution)/shard_map/front/pallas_call | solution.py:291
  53.9 1.6 %collective-permute-start.32 = (bf16[48,1024]{1,0:T(8,128)(2,1)S(1)}, bf16[48,1024]{1,0:T(8,128)(2,1)S(1)}, u32[]{:S(2)}, u32[]{:S(2)}) collective-permute-start(bf16[48,1024]{1,0:T(8,128)(2,1)S(1)} %get-tuple-element.65), channel_id=1, source_target_pairs={{0,2},{1,3},{2,0},{3,1},{4,6},{5,7},{6,4},{7,5},{8,10},{9,11},{10,... | collective-permute-start | bytes 294920 | tf_op jit(solution)/shard_map/ppermute | solution.py:66
  56.3 3.3 %collective-permute-done.32.came_ref = bf16[48,1024]{1,0:T(8,128)(2,1)S(1)} collective-permute-done((bf16[48,1024]{1,0:T(8,128)(2,1)S(1)}, bf16[48,1024]{1,0:T(8,128)(2,1)S(1)}, u32[]{:S(2)}, u32[]{:S(2)}) %collective-permute-start.32) | collective-permute-done | bytes 98336 | tf_op jit(solution)/shard_map/ppermute | solution.py:66
  60.3 1.7 %collective-permute-start.34 = (bf16[24,1024]{1,0:T(8,128)(2,1)S(1)}, bf16[24,1024]{1,0:T(8,128)(2,1)S(1)}, u32[]{:S(2)}, u32[]{:S(2)}) collective-permute-start(bf16[24,1024]{1,0:T(8,128)(2,1)S(1)} %get-tuple-element.67), channel_id=1, source_target_pairs={{0,12},{4,8},{8,4},{12,0},{1,13},{5,9},{9,5},{13,1},{2,14},{6,10},... | collective-permute-start | bytes 147464 | tf_op jit(solution)/shard_map/ppermute | solution.py:66
  62.1 1.2 %collective-permute-start.31 = (bf16[24,1024]{1,0:T(8,128)(2,1)S(1)}, bf16[24,1024]{1,0:T(8,128)(2,1)S(1)}, u32[]{:S(2)}, u32[]{:S(2)}) collective-permute-start(bf16[24,1024]{1,0:T(8,128)(2,1)S(1)} %get-tuple-element.63), channel_id=1, source_target_pairs={{0,4},{4,0},{8,12},{12,8},{1,5},{5,1},{9,13},{13,9},{2,6},{6,2},{1... | collective-permute-start | bytes 147464 | tf_op jit(solution)/shard_map/ppermute | solution.py:66
  63.3 1.6 %collective-permute-done.33.refs_2_ = bf16[24,1024]{1,0:T(8,128)(2,1)S(1)} collective-permute-done((bf16[24,1024]{1,0:T(8,128)(2,1)S(1)}, bf16[24,1024]{1,0:T(8,128)(2,1)S(1)}, u32[]{:S(2)}, u32[]{:S(2)}) %collective-permute-start.33) | collective-permute-done | bytes 49184 | tf_op jit(solution)/shard_map/ppermute | solution.py:66
  64.9 1.3 %collective-permute-done.34.refs_3_ = bf16[24,1024]{1,0:T(8,128)(2,1)S(1)} collective-permute-done((bf16[24,1024]{1,0:T(8,128)(2,1)S(1)}, bf16[24,1024]{1,0:T(8,128)(2,1)S(1)}, u32[]{:S(2)}, u32[]{:S(2)}) %collective-permute-start.34) | collective-permute-done | bytes 49184 | tf_op jit(solution)/shard_map/ppermute | solution.py:66
  (78 shorter events, 15.0 us)
Async XLA Ops:
  1.9 12.4 %collective-permute-start = (bf16[24,2176]{1,0:T(8,128)(2,1)S(1)}, bf16[24,2176]{1,0:T(8,128)(2,1)S(1)}, u32[]{:S(2)}, u32[]{:S(2)}) collective-permute-start(bf16[24,2176]{1,0:T(8,128)(2,1)S(1)} %get-tuple-element.38), channel_id=1, source_target_pairs={{0,8},{4,12},{8,0},{12,4},{1,9},{5,13},{9,1},{13,5},{2,10},{6,14},... | collective-permute-start | bytes 313352 | tf_op jit(solution)/shard_map/ppermute | solution.py:66
  6.0 8.4 %collective-permute-start.2 = (bf16[24,2176]{1,0:T(8,128)(2,1)S(1)}, bf16[24,2176]{1,0:T(8,128)(2,1)S(1)}, u32[]{:S(2)}, u32[]{:S(2)}) collective-permute-start(bf16[24,2176]{1,0:T(8,128)(2,1)S(1)} %get-tuple-element.40), channel_id=1, source_target_pairs={{0,12},{4,8},{8,4},{12,0},{1,13},{5,9},{9,5},{13,1},{2,14},{6,10},... | collective-permute-start | bytes 313352 | tf_op jit(solution)/shard_map/ppermute | solution.py:66
  7.3 7.6 %collective-permute-start.4 = (bf16[24,2176]{1,0:T(8,128)(2,1)S(1)}, bf16[24,2176]{1,0:T(8,128)(2,1)S(1)}, u32[]{:S(2)}, u32[]{:S(2)}) collective-permute-start(bf16[24,2176]{1,0:T(8,128)(2,1)S(1)} %get-tuple-element.41), channel_id=1, source_target_pairs={{0,4},{4,0},{8,12},{12,8},{1,5},{5,1},{9,13},{13,9},{2,6},{6,2},{1... | collective-permute-start | bytes 313352 | tf_op jit(solution)/shard_map/ppermute | solution.py:66
  18.9 3.1 %collective-permute-start.6 = (bf16[96,1024]{1,0:T(8,128)(2,1)S(1)}, bf16[96,1024]{1,0:T(8,128)(2,1)S(1)}, u32[]{:S(2)}, u32[]{:S(2)}) collective-permute-start(bf16[96,1024]{1,0:T(8,128)(2,1)S(1)} %down.8), channel_id=1, source_target_pairs={{0,1},{1,0},{2,3},{3,2},{4,5},{5,4},{6,7},{7,6},{8,9},{9,8},{10,11... | collective-permute-start | bytes 589832 | tf_op jit(solution)/shard_map/ppermute | solution.py:66
  20.0 5.7 %collective-permute-start.10 = (bf16[48,1024]{1,0:T(8,128)(2,1)S(1)}, bf16[48,1024]{1,0:T(8,128)(2,1)S(1)}, u32[]{:S(2)}, u32[]{:S(2)}) collective-permute-start(bf16[48,1024]{1,0:T(8,128)(2,1)S(1)} %get-tuple-element.51), channel_id=1, source_target_pairs={{0,2},{1,3},{2,0},{3,1},{4,6},{5,7},{6,4},{7,5},{8,10},{9,11},{10,... | collective-permute-start | bytes 294920 | tf_op jit(solution)/shard_map/ppermute | solution.py:66
  21.9 7.9 %collective-permute-start.8 = (bf16[48,1024]{1,0:T(8,128)(2,1)S(1)}, bf16[48,1024]{1,0:T(8,128)(2,1)S(1)}, u32[]{:S(2)}, u32[]{:S(2)}) collective-permute-start(bf16[48,1024]{1,0:T(8,128)(2,1)S(1)} %get-tuple-element.47), channel_id=1, source_target_pairs={{0,2},{1,3},{2,0},{3,1},{4,6},{5,7},{6,4},{7,5},{8,10},{9,11},{10,... | collective-permute-start | bytes 294920 | tf_op jit(solution)/shard_map/ppermute | solution.py:66
  25.7 6.3 %collective-permute-start.11 = (bf16[24,1024]{1,0:T(8,128)(2,1)S(1)}, bf16[24,1024]{1,0:T(8,128)(2,1)S(1)}, u32[]{:S(2)}, u32[]{:S(2)}) collective-permute-start(bf16[24,1024]{1,0:T(8,128)(2,1)S(1)} %get-tuple-element.52), channel_id=1, source_target_pairs={{0,8},{4,12},{8,0},{12,4},{1,9},{5,13},{9,1},{13,5},{2,10},{6,14},... | collective-permute-start | bytes 147464 | tf_op jit(solution)/shard_map/ppermute | solution.py:66
  29.4 5.9 %collective-permute-start.12 = (bf16[24,1024]{1,0:T(8,128)(2,1)S(1)}, bf16[24,1024]{1,0:T(8,128)(2,1)S(1)}, u32[]{:S(2)}, u32[]{:S(2)}) collective-permute-start(bf16[24,1024]{1,0:T(8,128)(2,1)S(1)} %get-tuple-element.53), channel_id=1, source_target_pairs={{0,12},{4,8},{8,4},{12,0},{1,13},{5,9},{9,5},{13,1},{2,14},{6,10},... | collective-permute-start | bytes 147464 | tf_op jit(solution)/shard_map/ppermute | solution.py:66
  29.8 5.5 %collective-permute-start.9 = (bf16[24,1024]{1,0:T(8,128)(2,1)S(1)}, bf16[24,1024]{1,0:T(8,128)(2,1)S(1)}, u32[]{:S(2)}, u32[]{:S(2)}) collective-permute-start(bf16[24,1024]{1,0:T(8,128)(2,1)S(1)} %get-tuple-element.49), channel_id=1, source_target_pairs={{0,4},{4,0},{8,12},{12,8},{1,5},{5,1},{9,13},{13,9},{2,6},{6,2},{1... | collective-permute-start | bytes 147464 | tf_op jit(solution)/shard_map/ppermute | solution.py:66
  35.6 6.0 %collective-permute-start.16 = (bf16[24,1024]{1,0:T(8,128)(2,1)S(1)}, bf16[24,1024]{1,0:T(8,128)(2,1)S(1)}, u32[]{:S(2)}, u32[]{:S(2)}) collective-permute-start(bf16[24,1024]{1,0:T(8,128)(2,1)S(1)} %get-tuple-element.57), channel_id=1, source_target_pairs={{0,4},{4,0},{8,12},{12,8},{1,5},{5,1},{9,13},{13,9},{2,6},{6,2},{1... | collective-permute-start | bytes 147464 | tf_op jit(solution)/shard_map/ppermute | solution.py:66
  35.7 6.6 %collective-permute-start.20 = (bf16[24,1024]{1,0:T(8,128)(2,1)S(1)}, bf16[24,1024]{1,0:T(8,128)(2,1)S(1)}, u32[]{:S(2)}, u32[]{:S(2)}) collective-permute-start(bf16[24,1024]{1,0:T(8,128)(2,1)S(1)} %get-tuple-element.58), channel_id=1, source_target_pairs={{0,8},{4,12},{8,0},{12,4},{1,9},{5,13},{9,1},{13,5},{2,10},{6,14},... | collective-permute-start | bytes 147464 | tf_op jit(solution)/shard_map/ppermute | solution.py:66
  38.3 5.9 %collective-permute-start.24 = (bf16[24,1024]{1,0:T(8,128)(2,1)S(1)}, bf16[24,1024]{1,0:T(8,128)(2,1)S(1)}, u32[]{:S(2)}, u32[]{:S(2)}) collective-permute-start(bf16[24,1024]{1,0:T(8,128)(2,1)S(1)} %get-tuple-element.59), channel_id=1, source_target_pairs={{0,12},{4,8},{8,4},{12,0},{1,13},{5,9},{9,5},{13,1},{2,14},{6,10},... | collective-permute-start | bytes 147464 | tf_op jit(solution)/shard_map/ppermute | solution.py:66
  40.0 5.7 %collective-permute-start.13 = (bf16[24,1024]{1,0:T(8,128)(2,1)S(1)}, bf16[24,1024]{1,0:T(8,128)(2,1)S(1)}, u32[]{:S(2)}, u32[]{:S(2)}) collective-permute-start(bf16[24,1024]{1,0:T(8,128)(2,1)S(1)} %get-tuple-element.56.refs_0_), channel_id=1, source_target_pairs={{0,2},{1,3},{2,0},{3,1},{4,6},{5,7},{6,4},{7,5},{8,10},{9,11},{10,... | collective-permute-start | bytes 147464 | tf_op jit(solution)/shard_map/ppermute | solution.py:66
  41.5 4.2 %collective-permute-start.14 = (bf16[24,1024]{1,0:T(8,128)(2,1)S(1)}, bf16[24,1024]{1,0:T(8,128)(2,1)S(1)}, u32[]{:S(2)}, u32[]{:S(2)}) collective-permute-start(bf16[24,1024]{1,0:T(8,128)(2,1)S(1)} %get-tuple-element.56.refs_0_), channel_id=1, source_target_pairs={{0,1},{1,0},{2,3},{3,2},{4,5},{5,4},{6,7},{7,6},{8,9},{9,8},{10,11... | collective-permute-start | bytes 147464 | tf_op jit(solution)/shard_map/ppermute | solution.py:66
  41.5 4.7 %collective-permute-start.17 = (bf16[24,1024]{1,0:T(8,128)(2,1)S(1)}, bf16[24,1024]{1,0:T(8,128)(2,1)S(1)}, u32[]{:S(2)}, u32[]{:S(2)}) collective-permute-start(bf16[24,1024]{1,0:T(8,128)(2,1)S(1)} %collective-permute-done.16.refs_4_), channel_id=1, source_target_pairs={{0,2},{1,3},{2,0},{3,1},{4,6},{5,7},{6,4},{7,5},{8,10},{9,11},{10,... | collective-permute-start | bytes 147464 | tf_op jit(solution)/shard_map/ppermute | solution.py:66
  42.3 4.8 %collective-permute-start.21 = (bf16[24,1024]{1,0:T(8,128)(2,1)S(1)}, bf16[24,1024]{1,0:T(8,128)(2,1)S(1)}, u32[]{:S(2)}, u32[]{:S(2)}) collective-permute-start(bf16[24,1024]{1,0:T(8,128)(2,1)S(1)} %collective-permute-done.20.refs_8_), channel_id=1, source_target_pairs={{0,2},{1,3},{2,0},{3,1},{4,6},{5,7},{6,4},{7,5},{8,10},{9,11},{10,... | collective-permute-start | bytes 147464 | tf_op jit(solution)/shard_map/ppermute | solution.py:66
  44.2 4.1 %collective-permute-start.25 = (bf16[24,1024]{1,0:T(8,128)(2,1)S(1)}, bf16[24,1024]{1,0:T(8,128)(2,1)S(1)}, u32[]{:S(2)}, u32[]{:S(2)}) collective-permute-start(bf16[24,1024]{1,0:T(8,128)(2,1)S(1)} %collective-permute-done.24.refs_12_), channel_id=1, source_target_pairs={{0,2},{1,3},{2,0},{3,1},{4,6},{5,7},{6,4},{7,5},{8,10},{9,11},{10,... | collective-permute-start | bytes 147464 | tf_op jit(solution)/shard_map/ppermute | solution.py:66
  45.7 3.1 %collective-permute-start.18 = (bf16[24,1024]{1,0:T(8,128)(2,1)S(1)}, bf16[24,1024]{1,0:T(8,128)(2,1)S(1)}, u32[]{:S(2)}, u32[]{:S(2)}) collective-permute-start(bf16[24,1024]{1,0:T(8,128)(2,1)S(1)} %collective-permute-done.16.refs_4_), channel_id=1, source_target_pairs={{0,1},{1,0},{2,3},{3,2},{4,5},{5,4},{6,7},{7,6},{8,9},{9,8},{10,11... | collective-permute-start | bytes 147464 | tf_op jit(solution)/shard_map/ppermute | solution.py:66
  52.9 3.1 %collective-permute-start.28 = (bf16[96,1024]{1,0:T(8,128)(2,1)S(1)}, bf16[96,1024]{1,0:T(8,128)(2,1)S(1)}, u32[]{:S(2)}, u32[]{:S(2)}) collective-permute-start(bf16[96,1024]{1,0:T(8,128)(2,1)S(1)} %down.12), channel_id=1, source_target_pairs={{0,1},{1,0},{2,3},{3,2},{4,5},{5,4},{6,7},{7,6},{8,9},{9,8},{10,11... | collective-permute-start | bytes 589832 | tf_op jit(solution)/shard_map/ppermute | solution.py:66
  53.9 5.7 %collective-permute-start.32 = (bf16[48,1024]{1,0:T(8,128)(2,1)S(1)}, bf16[48,1024]{1,0:T(8,128)(2,1)S(1)}, u32[]{:S(2)}, u32[]{:S(2)}) collective-permute-start(bf16[48,1024]{1,0:T(8,128)(2,1)S(1)} %get-tuple-element.65), channel_id=1, source_target_pairs={{0,2},{1,3},{2,0},{3,1},{4,6},{5,7},{6,4},{7,5},{8,10},{9,11},{10,... | collective-permute-start | bytes 294920 | tf_op jit(solution)/shard_map/ppermute | solution.py:66
  55.5 6.6 %collective-permute-start.30 = (bf16[48,1024]{1,0:T(8,128)(2,1)S(1)}, bf16[48,1024]{1,0:T(8,128)(2,1)S(1)}, u32[]{:S(2)}, u32[]{:S(2)}) collective-permute-start(bf16[48,1024]{1,0:T(8,128)(2,1)S(1)} %get-tuple-element.61), channel_id=1, source_target_pairs={{0,2},{1,3},{2,0},{3,1},{4,6},{5,7},{6,4},{7,5},{8,10},{9,11},{10,... | collective-permute-start | bytes 294920 | tf_op jit(solution)/shard_map/ppermute | solution.py:66
  59.6 5.3 %collective-permute-start.33 = (bf16[24,1024]{1,0:T(8,128)(2,1)S(1)}, bf16[24,1024]{1,0:T(8,128)(2,1)S(1)}, u32[]{:S(2)}, u32[]{:S(2)}) collective-permute-start(bf16[24,1024]{1,0:T(8,128)(2,1)S(1)} %get-tuple-element.66), channel_id=1, source_target_pairs={{0,8},{4,12},{8,0},{12,4},{1,9},{5,13},{9,1},{13,5},{2,10},{6,14},... | collective-permute-start | bytes 147464 | tf_op jit(solution)/shard_map/ppermute | solution.py:66
  60.3 5.9 %collective-permute-start.34 = (bf16[24,1024]{1,0:T(8,128)(2,1)S(1)}, bf16[24,1024]{1,0:T(8,128)(2,1)S(1)}, u32[]{:S(2)}, u32[]{:S(2)}) collective-permute-start(bf16[24,1024]{1,0:T(8,128)(2,1)S(1)} %get-tuple-element.67), channel_id=1, source_target_pairs={{0,12},{4,8},{8,4},{12,0},{1,13},{5,9},{9,5},{13,1},{2,14},{6,10},... | collective-permute-start | bytes 147464 | tf_op jit(solution)/shard_map/ppermute | solution.py:66
  62.1 4.7 %collective-permute-start.31 = (bf16[24,1024]{1,0:T(8,128)(2,1)S(1)}, bf16[24,1024]{1,0:T(8,128)(2,1)S(1)}, u32[]{:S(2)}, u32[]{:S(2)}) collective-permute-start(bf16[24,1024]{1,0:T(8,128)(2,1)S(1)} %get-tuple-element.63), channel_id=1, source_target_pairs={{0,4},{4,0},{8,12},{12,8},{1,5},{5,1},{9,13},{13,9},{2,6},{6,2},{1... | collective-permute-start | bytes 147464 | tf_op jit(solution)/shard_map/ppermute | solution.py:66
  (15 other events, 51.7 us)

commit v10 on v9

--- a/solution.py
+++ b/solution.py
@@ -301,25 +301,35 @@
     )(*xs, *flags, mod, router, pair)
 
 
-def down_kernel(flip, n_adds, hidden_ref, down_ref, *refs):
+def store_blocks(total, groups, outs):
+    rows = total.shape[0] // sum(len(group) for group in groups)
+    for group, out in zip(groups, outs):
+        blocks = [total[k * rows : (k + 1) * rows] for k in group]
+        out[...] = jnp.concatenate(blocks, axis=0).astype(out.dtype)
+
+
+def shapes_of(rows, cols, groups, types):
+    slots = rows // sum(len(group) for group in groups)
+    return [jax.ShapeDtypeStruct((slots * len(group), cols), t) for group, t in zip(groups, types)]
+
+
+def down_kernel(flip, n_adds, groups, hidden_ref, down_ref, *refs):
     adds, outs = refs[:n_adds], refs[n_adds:]
     quarter = outs[0].shape[1]
     weights = down_ref[:, aligned(lax.axis_index("et") ^ flip, quarter)]
-    product = jnp.dot(hidden_ref[...], weights, preferred_element_type=jnp.float32)
+    total = jnp.dot(hidden_ref[...], weights, preferred_element_type=jnp.float32)
     for ref in adds:
-        product += ref[...].astype(jnp.float32)
-    rows = outs[0].shape[0]
-    for k, out in enumerate(outs):
-        out[...] = product[k * rows : (k + 1) * rows].astype(out.dtype)
-
-
-def down(hidden, w_down, flip, blocks, adds=(), dtype=jnp.bfloat16):
+        total += ref[...].astype(jnp.float32)
+    store_blocks(total, groups, outs)
+
+
+def down(hidden, w_down, flip, adds=(), groups=((0,),), types=(jnp.bfloat16,)):
     units, width = w_down.shape
     rows, quarter = hidden.shape[0], width // 4
     return pl.pallas_call(
-        functools.partial(down_kernel, flip, len(adds)),
+        functools.partial(down_kernel, flip, len(adds), groups),
         in_specs=[VMEM] * (2 + len(adds)),
-        out_shape=[jax.ShapeDtypeStruct((rows // blocks, quarter), dtype)] * blocks,
+        out_shape=shapes_of(rows, quarter, groups, types),
         compiler_params=params(),
         cost_estimate=pl.CostEstimate(
             flops=2 * rows * units * quarter, bytes_accessed=2 * units * quarter, transcendentals=0
@@ -328,26 +338,29 @@
     )(hidden, w_down, *adds)
 
 
-def add_kernel(keep_ref, came_ref, *outs):
-    total = keep_ref[...] + came_ref[...].astype(jnp.float32)
-    rows = outs[0].shape[0]
-    for k, out in enumerate(outs):
-        out[...] = total[k * rows : (k + 1) * rows].astype(out.dtype)
-
-
-def add(keep, came, count):
-    shape = (keep.shape[0] // count, keep.shape[1])
-    return pl.pallas_call(
-        add_kernel,
-        out_shape=[jax.ShapeDtypeStruct(shape, jnp.bfloat16)] * count,
+def add_kernel(groups, keep_ref, came_ref, *outs):
+    store_blocks(keep_ref[...] + came_ref[...].astype(jnp.float32), groups, outs)
+
+
+def add(keep, came, groups):
+    return pl.pallas_call(
+        functools.partial(add_kernel, groups),
+        out_shape=shapes_of(*keep.shape, groups, [jnp.bfloat16] * len(groups)),
         compiler_params=params(),
         name="add",
     )(keep, came)
 
 
-def move_kernel(n_came, last, own_ref, back_ref, pick_ref, *refs):
+def diagonal(x, k, flip):
+    n_ep, n_et = lax.axis_size("ep"), lax.axis_size("et")
+    pairs = [(e * n_et + t, (e ^ k) * n_et + (t ^ flip)) for e in range(n_ep) for t in range(n_et)]
+    return lax.ppermute(x, ("ep", "et"), pairs)
+
+
+def move_kernel(n_came, last, own_ref, back_ref, pick_ref, extra_ref, *refs):
     came, outs = refs[:n_came], refs[n_came:]
     rows = [ref[...].astype(jnp.float32) for ref in came]
+    rows[DIRECT] += extra_ref[...].astype(jnp.float32)
     velocity = product(back_ref[...], jnp.concatenate(rows, axis=0))
     moved = narrow(own_ref[...].astype(jnp.float32) - 0.5 * velocity)
     outs[0][...] = moved
@@ -360,28 +373,33 @@
             out[...] = narrow(picked[k * slots : (k + 1) * slots])
 
 
-def move(own, back, pick, came, last):
+def move(own, back, pick, extra, came, last):
     shapes = [own.shape] + ([own.shape] if last else [c.shape for c in came])
     return pl.pallas_call(
         functools.partial(move_kernel, len(came), last),
         out_shape=[jax.ShapeDtypeStruct(s, jnp.bfloat16) for s in shapes],
         compiler_params=params(),
         name="move",
-    )(own, back, pick, *came)
-
-
-def sum_back(hidden, w_down, own, back, pick, last_section):
+    )(own, back, pick, extra, *came)
+
+
+DIRECT = 2
+
+
+def sum_back(hidden, w_down, own, back, pick, last):
     peers = lax.axis_size("ep")
-    some = peers // 2
-    far = swap(down(hidden, w_down, 3, 1)[0], "et", 1)
-    near = swap(down(hidden, w_down, 1, 1)[0], "et", 1)
-    first, last = add(down(hidden, w_down, 2, 1, (), jnp.float32)[0], far, 2)
-    last, first = swap(last, "et", 2), swap(first, "et", 2)
-    keep_first, keep_last = down(hidden, w_down, 0, 2, (near,), jnp.float32)
-    later = add(keep_last, last, peers - some)
-    blocks = add(keep_first, first, some) + later
-    came = [swap(b, "ep", k) if k else b for k, b in enumerate(blocks)]
-    return move(own, back, pick, came, last_section)
+    rest = tuple(k for k in range(peers) if k != DIRECT)
+    groups = (rest, (DIRECT,))
+    (far,), (near,) = down(hidden, w_down, 3), down(hidden, w_down, 1)
+    far, near = swap(far, "et", 1), swap(near, "et", 1)
+    (crossing,) = down(hidden, w_down, 2, types=[jnp.float32])
+    crossing, beside = add(crossing, far, groups)
+    crossed, extra = swap(crossing, "et", 2), diagonal(beside, DIRECT, 2)
+    kept, straight = down(hidden, w_down, 0, (near,), groups, [jnp.float32, jnp.bfloat16])
+    blocks = dict(zip(rest, add(kept, crossed, [(i,) for i in range(len(rest))])))
+    blocks[DIRECT] = straight
+    came = [swap(blocks[k], "ep", k) if k else blocks[k] for k in range(peers)]
+    return move(own, back, pick, extra, came, last)
 
 
 def spread(block, quarter):
@@ -432,7 +450,7 @@
     def body(*args):
         experts, picks = args[2].shape[1], args[6].shape[2]
         peers = lax.axis_size("ep")
-        fits = lax.axis_size("et") == 4 and peers & (peers - 1) == 0
+        fits = lax.axis_size("et") == 4 and peers >= 4 and peers & (peers - 1) == 0
         chosen = dense_body if fits and experts <= 2 * picks else routed_body
         return chosen(*args)
 

time: 67.7 us -> 70.1 us (1.035)
  starting transfers between devices: 30.6 us -> 33.5 us
    ppermute x0 -> x2, starting transfers between devices: none -> 5.5 us  [diagonal(): return lax.ppermute(x, ('ep', 'et'), pairs)]
    ppermute x35 -> x33, starting transfers between devices: 30.6 us -> 28 us  [swap(): return lax.ppermute(x, axis, [(i, i ^ bit) for i in range(size)])]
    ppermute x35 -> x33, waiting for transfers between devices: 23 us -> 22.4 us  [swap(): return lax.ppermute(x, axis, [(i, i ^ bit) for i in range(size)])]
    pallas_call x14 -> x12, Pallas kernels: 2.41 us -> 2.37 us  [the longest x8 2.23 us: down(): pl.pallas_call(functools.partial(down_kernel, flip, len(adds), groups), i...]
  transfers between devices with their start and end apart: 35 -> 35, of which waited for: 17 -> 14; matrix products, arithmetic and copies ran while one was open for 0% -> 0% of each run, Pallas kernels for 10% -> 9%
where the time goes in v10:
time: 70.1 us; the launch traced here: 69.9 us
  starting transfers between devices  33.5 us (48%)
  waiting for transfers between devices  22.4 us (32%)
  Pallas kernels  13.1 us (19%)
  between operations  0.85 us (1%)
    ppermute x33, starting transfers between devices, swap(): return lax.ppermute(x, axis, [(i, i ^ bit) for i in range(size)])  28 us
    ppermute x33, waiting for transfers between devices, swap(): return lax.ppermute(x, axis, [(i, i ^ bit) for i in range(size)])  22.4 us
    ppermute x2, starting transfers between devices, diagonal(): return lax.ppermute(x, ('ep', 'et'), pairs)  5.5 us
    pallas_call x2, Pallas kernels, front(): pl.pallas_call(functools.partial(front_kernel, layout, order, section, ex...  3.81 us
    pallas_call x1, Pallas kernels, load(): pl.pallas_call(load_kernel, in_specs=[ANY] * 3, out_specs=[VMEM] * 3, out...  3.78 us
    pallas_call x8, Pallas kernels, down(): pl.pallas_call(functools.partial(down_kernel, flip, len(adds), groups), i...  2.23 us
  transfers between devices with their start and end apart: 35, of which 14 were waited for; matrix products, arithmetic and copies ran while one was open for 0% of the time, Pallas kernels for 9%

profile of v10, /device:TPU:0, one launch (start us, length us, event | category | flops | bytes accessed | tf_op | source)
XLA Modules:
  0.0 69.9 jit_solution(4185124359034262871)
XLA Ops:
  0.6 1.2 %pack.1 = (bf16[24,2176]{1,0:T(8,128)(2,1)S(1)}, bf16[24,2176]{1,0:T(8,128)(2,1)S(1)}, bf16[24,2176]{1,0:T(8,128)(2,1)S(1)}, bf16[32,1024]{1,0:T(8,128)(2,1)S(1)}) custom-call(bf16[32,4096]{1,0:T(8,128)(2,1)} %tokens_ref.3, s32[2,2,32]{2,1,0:T(2,128)} %bitcast.4), custom_call_target="tpu_custom_call" | custom-call | tf_op jit(solution)/shard_map/pack/pallas_call | solution.py:197
  1.9 4.1 %collective-permute-start = (bf16[24,2176]{1,0:T(8,128)(2,1)S(1)}, bf16[24,2176]{1,0:T(8,128)(2,1)S(1)}, u32[]{:S(2)}, u32[]{:S(2)}) collective-permute-start(bf16[24,2176]{1,0:T(8,128)(2,1)S(1)} %get-tuple-element.36), channel_id=1, source_target_pairs={{0,8},{4,12},{8,0},{12,4},{1,9},{5,13},{9,1},{13,5},{2,10},{6,14},... | collective-permute-start | bytes 313352 | tf_op jit(solution)/shard_map/ppermute | solution.py:66
  6.0 1.3 %collective-permute-start.2 = (bf16[24,2176]{1,0:T(8,128)(2,1)S(1)}, bf16[24,2176]{1,0:T(8,128)(2,1)S(1)}, u32[]{:S(2)}, u32[]{:S(2)}) collective-permute-start(bf16[24,2176]{1,0:T(8,128)(2,1)S(1)} %get-tuple-element.38), channel_id=1, source_target_pairs={{0,12},{4,8},{8,4},{12,0},{1,13},{5,9},{9,5},{13,1},{2,14},{6,10},... | collective-permute-start | bytes 313352 | tf_op jit(solution)/shard_map/ppermute | solution.py:66
  7.6 3.8 %load.1 = (bf16[4096,768]{1,0:T(8,128)(2,1)S(1)}, bf16[384,4096]{1,0:T(8,128)(2,1)S(1)}, f32[8,128]{1,0:T(8,128)S(1)}) custom-call(bf16[1,4096,384]{2,1,0:T(8,128)(2,1)} %gate_ref.1, bf16[1,4096,384]{2,1,0:T(8,128)(2,1)} %up_ref.1, bf16[1,384,4096]{2,1,0:T(8,128)(2,1)} %down_ref.1), custom_call_target="tpu_custom_call" | custom-call | bytes 18874368 | tf_op jit(solution)/shard_map/load/pallas_call | solution.py:101
  11.4 2.8 %collective-permute-done.block_ref.refs_7_.refs_18_ = bf16[24,2176]{1,0:T(8,128)(2,1)S(1)} collective-permute-done((bf16[24,2176]{1,0:T(8,128)(2,1)S(1)}, bf16[24,2176]{1,0:T(8,128)(2,1)S(1)}, u32[]{:S(2)}, u32[]{:S(2)}) %collective-permute-start) | collective-permute-done | bytes 104480 | tf_op jit(solution)/shard_map/ppermute | solution.py:66
  16.3 1.8 %front.2.hidden_ref = bf16[96,384]{1,0:T(8,128)(2,1)S(1)} custom-call(bf16[24,2048]{1,0:T(8,128)(2,1)S(1)} %relay.3.refs_0_, bf16[24,2048]{1,0:T(8,128)(2,1)S(1)} %collective-permute-done.1.refs_1_, bf16[24,2048]{1,0:T(8,128)(2,1)S(1)} %relay.4.refs_2_, bf16[24,2048]{1,0:T(8,128)(2,1)S(1)} %collective-permute-done.3.refs_3_, ...), custom_call_target="tpu_custom_call" | custom-call | flops 603979776 | bytes 6291456 | tf_op jit(solution)/shard_map/front/pallas_call | solution.py:291
  20.0 1.9 %collective-permute-start.9 = (bf16[72,1024]{1,0:T(8,128)(2,1)S(1)}, bf16[72,1024]{1,0:T(8,128)(2,1)S(1)}, u32[]{:S(2)}, u32[]{:S(2)}) collective-permute-start(bf16[72,1024]{1,0:T(8,128)(2,1)S(1)} %get-tuple-element.46), channel_id=1, source_target_pairs={{0,2},{1,3},{2,0},{3,1},{4,6},{5,7},{6,4},{7,5},{8,10},{9,11},{10,... | collective-permute-start | bytes 442376 | tf_op jit(solution)/shard_map/ppermute | solution.py:66
  21.9 3.3 %collective-permute-start.7 = (bf16[24,1024]{1,0:T(8,128)(2,1)S(1)}, bf16[24,1024]{1,0:T(8,128)(2,1)S(1)}, u32[]{:S(2)}, u32[]{:S(2)}) collective-permute-start(bf16[24,1024]{1,0:T(8,128)(2,1)S(1)} %get-tuple-element.44), channel_id=1, source_target_pairs={{0,10},{1,11},{2,8},{3,9},{4,14},{5,15},{6,12},{7,13},{8,2},{9,3},... | collective-permute-start | bytes 147464 | tf_op jit(solution)/shard_map/ppermute | solution.py:357
  26.1 2.3 %collective-permute-start.10 = (bf16[24,1024]{1,0:T(8,128)(2,1)S(1)}, bf16[24,1024]{1,0:T(8,128)(2,1)S(1)}, u32[]{:S(2)}, u32[]{:S(2)}) collective-permute-start(bf16[24,1024]{1,0:T(8,128)(2,1)S(1)} %get-tuple-element.48), channel_id=1, source_target_pairs={{0,4},{4,0},{8,12},{12,8},{1,5},{5,1},{9,13},{13,9},{2,6},{6,2},{1... | collective-permute-start | bytes 147464 | tf_op jit(solution)/shard_map/ppermute | solution.py:66
  28.4 3.3 %collective-permute-start.12 = (bf16[24,1024]{1,0:T(8,128)(2,1)S(1)}, bf16[24,1024]{1,0:T(8,128)(2,1)S(1)}, u32[]{:S(2)}, u32[]{:S(2)}) collective-permute-start(bf16[24,1024]{1,0:T(8,128)(2,1)S(1)} %get-tuple-element.50), channel_id=1, source_target_pairs={{0,12},{4,8},{8,4},{12,0},{1,13},{5,9},{9,5},{13,1},{2,14},{6,10},... | collective-permute-start | bytes 147464 | tf_op jit(solution)/shard_map/ppermute | solution.py:66
  31.7 2.6 %collective-permute-done.12.refs_3_ = bf16[24,1024]{1,0:T(8,128)(2,1)S(1)} collective-permute-done((bf16[24,1024]{1,0:T(8,128)(2,1)S(1)}, bf16[24,1024]{1,0:T(8,128)(2,1)S(1)}, u32[]{:S(2)}, u32[]{:S(2)}) %collective-permute-start.12) | collective-permute-done | bytes 49184 | tf_op jit(solution)/shard_map/ppermute | solution.py:66
  34.6 2.2 %collective-permute-start.13 = (bf16[24,1024]{1,0:T(8,128)(2,1)S(1)}, bf16[24,1024]{1,0:T(8,128)(2,1)S(1)}, u32[]{:S(2)}, u32[]{:S(2)}) collective-permute-start(bf16[24,1024]{1,0:T(8,128)(2,1)S(1)} %get-tuple-element.53.refs_0_), channel_id=1, source_target_pairs={{0,2},{1,3},{2,0},{3,1},{4,6},{5,7},{6,4},{7,5},{8,10},{9,11},{10,... | collective-permute-start | bytes 147464 | tf_op jit(solution)/shard_map/ppermute | solution.py:66
  36.9 4.0 %collective-permute-start.20 = (bf16[24,1024]{1,0:T(8,128)(2,1)S(1)}, bf16[24,1024]{1,0:T(8,128)(2,1)S(1)}, u32[]{:S(2)}, u32[]{:S(2)}) collective-permute-start(bf16[24,1024]{1,0:T(8,128)(2,1)S(1)} %get-tuple-element.55), channel_id=1, source_target_pairs={{0,8},{4,12},{8,0},{12,4},{1,9},{5,13},{9,1},{13,5},{2,10},{6,14},... | collective-permute-start | bytes 147464 | tf_op jit(solution)/shard_map/ppermute | solution.py:66
  41.8 2.6 %collective-permute-done.20.refs_8_ = bf16[24,1024]{1,0:T(8,128)(2,1)S(1)} collective-permute-done((bf16[24,1024]{1,0:T(8,128)(2,1)S(1)}, bf16[24,1024]{1,0:T(8,128)(2,1)S(1)}, u32[]{:S(2)}, u32[]{:S(2)}) %collective-permute-start.20) | collective-permute-done | bytes 49184 | tf_op jit(solution)/shard_map/ppermute | solution.py:66
  44.6 2.2 %collective-permute-done.24.refs_12_ = bf16[24,1024]{1,0:T(8,128)(2,1)S(1)} collective-permute-done((bf16[24,1024]{1,0:T(8,128)(2,1)S(1)}, bf16[24,1024]{1,0:T(8,128)(2,1)S(1)}, u32[]{:S(2)}, u32[]{:S(2)}) %collective-permute-start.24) | collective-permute-done | bytes 49184 | tf_op jit(solution)/shard_map/ppermute | solution.py:66
  47.4 1.4 %collective-permute-done.21.refs_9_ = bf16[24,1024]{1,0:T(8,128)(2,1)S(1)} collective-permute-done((bf16[24,1024]{1,0:T(8,128)(2,1)S(1)}, bf16[24,1024]{1,0:T(8,128)(2,1)S(1)}, u32[]{:S(2)}, u32[]{:S(2)}) %collective-permute-start.21) | collective-permute-done | bytes 49184 | tf_op jit(solution)/shard_map/ppermute | solution.py:66
  48.8 2.0 %collective-permute-done.25.refs_13_ = bf16[24,1024]{1,0:T(8,128)(2,1)S(1)} collective-permute-done((bf16[24,1024]{1,0:T(8,128)(2,1)S(1)}, bf16[24,1024]{1,0:T(8,128)(2,1)S(1)}, u32[]{:S(2)}, u32[]{:S(2)}) %collective-permute-start.25) | collective-permute-done | bytes 49184 | tf_op jit(solution)/shard_map/ppermute | solution.py:66
  52.1 2.0 %front.3.hidden_ref = bf16[96,384]{1,0:T(8,128)(2,1)S(1)} custom-call(bf16[24,1024]{1,0:T(8,128)(2,1)S(1)} %get-tuple-element.53.refs_0_, bf16[24,1024]{1,0:T(8,128)(2,1)S(1)} %collective-permute-done.13.refs_1_, bf16[24,1024]{1,0:T(8,128)(2,1)S(1)} %collective-permute-done.14.refs_2_, bf16[24,1024]{1,0:T(8,128)(2,1)S(1)} %collective-permute-done.15.refs_3_, ...), custom_call_target="tpu_custom_call" | custom-call | flops 603979776 | bytes 6291456 | tf_op jit(solution)/shard_map/front/pallas_call | solution.py:291
  56.0 2.2 %collective-permute-start.29 = (bf16[24,1024]{1,0:T(8,128)(2,1)S(1)}, bf16[24,1024]{1,0:T(8,128)(2,1)S(1)}, u32[]{:S(2)}, u32[]{:S(2)}) collective-permute-start(bf16[24,1024]{1,0:T(8,128)(2,1)S(1)} %get-tuple-element.57), channel_id=1, source_target_pairs={{0,10},{1,11},{2,8},{3,9},{4,14},{5,15},{6,12},{7,13},{8,2},{9,3},... | collective-permute-start | bytes 147464 | tf_op jit(solution)/shard_map/ppermute | solution.py:357
  58.6 2.1 %collective-permute-start.33 = (bf16[24,1024]{1,0:T(8,128)(2,1)S(1)}, bf16[24,1024]{1,0:T(8,128)(2,1)S(1)}, u32[]{:S(2)}, u32[]{:S(2)}) collective-permute-start(bf16[24,1024]{1,0:T(8,128)(2,1)S(1)} %get-tuple-element.62), channel_id=1, source_target_pairs={{0,8},{4,12},{8,0},{12,4},{1,9},{5,13},{9,1},{13,5},{2,10},{6,14},... | collective-permute-start | bytes 147464 | tf_op jit(solution)/shard_map/ppermute | solution.py:66
  60.7 2.2 %collective-permute-done.31.came_ref = bf16[72,1024]{1,0:T(8,128)(2,1)S(1)} collective-permute-done((bf16[72,1024]{1,0:T(8,128)(2,1)S(1)}, bf16[72,1024]{1,0:T(8,128)(2,1)S(1)}, u32[]{:S(2)}, u32[]{:S(2)}) %collective-permute-start.31) | collective-permute-done | bytes 147488 | tf_op jit(solution)/shard_map/ppermute | solution.py:66
  63.0 2.3 %collective-permute-start.34 = (bf16[24,1024]{1,0:T(8,128)(2,1)S(1)}, bf16[24,1024]{1,0:T(8,128)(2,1)S(1)}, u32[]{:S(2)}, u32[]{:S(2)}) collective-permute-start(bf16[24,1024]{1,0:T(8,128)(2,1)S(1)} %get-tuple-element.63), channel_id=1, source_target_pairs={{0,12},{4,8},{8,4},{12,0},{1,13},{5,9},{9,5},{13,1},{2,14},{6,10},... | collective-permute-start | bytes 147464 | tf_op jit(solution)/shard_map/ppermute | solution.py:66
  65.4 2.1 %collective-permute-done.32.refs_1_ = bf16[24,1024]{1,0:T(8,128)(2,1)S(1)} collective-permute-done((bf16[24,1024]{1,0:T(8,128)(2,1)S(1)}, bf16[24,1024]{1,0:T(8,128)(2,1)S(1)}, u32[]{:S(2)}, u32[]{:S(2)}) %collective-permute-start.32) | collective-permute-done | bytes 49184 | tf_op jit(solution)/shard_map/ppermute | solution.py:66
  67.5 1.6 %collective-permute-done.34.refs_3_ = bf16[24,1024]{1,0:T(8,128)(2,1)S(1)} collective-permute-done((bf16[24,1024]{1,0:T(8,128)(2,1)S(1)}, bf16[24,1024]{1,0:T(8,128)(2,1)S(1)}, u32[]{:S(2)}, u32[]{:S(2)}) %collective-permute-start.34) | collective-permute-done | bytes 49184 | tf_op jit(solution)/shard_map/ppermute | solution.py:66
  (76 shorter events, 11.5 us)
Async XLA Ops:
  1.9 12.4 %collective-permute-start = (bf16[24,2176]{1,0:T(8,128)(2,1)S(1)}, bf16[24,2176]{1,0:T(8,128)(2,1)S(1)}, u32[]{:S(2)}, u32[]{:S(2)}) collective-permute-start(bf16[24,2176]{1,0:T(8,128)(2,1)S(1)} %get-tuple-element.36), channel_id=1, source_target_pairs={{0,8},{4,12},{8,0},{12,4},{1,9},{5,13},{9,1},{13,5},{2,10},{6,14},... | collective-permute-start | bytes 313352 | tf_op jit(solution)/shard_map/ppermute | solution.py:66
  6.0 8.4 %collective-permute-start.2 = (bf16[24,2176]{1,0:T(8,128)(2,1)S(1)}, bf16[24,2176]{1,0:T(8,128)(2,1)S(1)}, u32[]{:S(2)}, u32[]{:S(2)}) collective-permute-start(bf16[24,2176]{1,0:T(8,128)(2,1)S(1)} %get-tuple-element.38), channel_id=1, source_target_pairs={{0,12},{4,8},{8,4},{12,0},{1,13},{5,9},{9,5},{13,1},{2,14},{6,10},... | collective-permute-start | bytes 313352 | tf_op jit(solution)/shard_map/ppermute | solution.py:66
  7.3 7.6 %collective-permute-start.4 = (bf16[24,2176]{1,0:T(8,128)(2,1)S(1)}, bf16[24,2176]{1,0:T(8,128)(2,1)S(1)}, u32[]{:S(2)}, u32[]{:S(2)}) collective-permute-start(bf16[24,2176]{1,0:T(8,128)(2,1)S(1)} %get-tuple-element.39), channel_id=1, source_target_pairs={{0,4},{4,0},{8,12},{12,8},{1,5},{5,1},{9,13},{13,9},{2,6},{6,2},{1... | collective-permute-start | bytes 313352 | tf_op jit(solution)/shard_map/ppermute | solution.py:66
  18.9 6.2 %collective-permute-start.8 = (bf16[96,1024]{1,0:T(8,128)(2,1)S(1)}, bf16[96,1024]{1,0:T(8,128)(2,1)S(1)}, u32[]{:S(2)}, u32[]{:S(2)}) collective-permute-start(bf16[96,1024]{1,0:T(8,128)(2,1)S(1)} %down.10), channel_id=1, source_target_pairs={{0,1},{1,0},{2,3},{3,2},{4,5},{5,4},{6,7},{7,6},{8,9},{9,8},{10,11... | collective-permute-start | bytes 589832 | tf_op jit(solution)/shard_map/ppermute | solution.py:66
  20.0 6.1 %collective-permute-start.9 = (bf16[72,1024]{1,0:T(8,128)(2,1)S(1)}, bf16[72,1024]{1,0:T(8,128)(2,1)S(1)}, u32[]{:S(2)}, u32[]{:S(2)}) collective-permute-start(bf16[72,1024]{1,0:T(8,128)(2,1)S(1)} %get-tuple-element.46), channel_id=1, source_target_pairs={{0,2},{1,3},{2,0},{3,1},{4,6},{5,7},{6,4},{7,5},{8,10},{9,11},{10,... | collective-permute-start | bytes 442376 | tf_op jit(solution)/shard_map/ppermute | solution.py:66
  21.9 9.9 %collective-permute-start.7 = (bf16[24,1024]{1,0:T(8,128)(2,1)S(1)}, bf16[24,1024]{1,0:T(8,128)(2,1)S(1)}, u32[]{:S(2)}, u32[]{:S(2)}) collective-permute-start(bf16[24,1024]{1,0:T(8,128)(2,1)S(1)} %get-tuple-element.44), channel_id=1, source_target_pairs={{0,10},{1,11},{2,8},{3,9},{4,14},{5,15},{6,12},{7,13},{8,2},{9,3},... | collective-permute-start | bytes 147464 | tf_op jit(solution)/shard_map/ppermute | solution.py:357
  25.4 6.3 %collective-permute-start.11 = (bf16[24,1024]{1,0:T(8,128)(2,1)S(1)}, bf16[24,1024]{1,0:T(8,128)(2,1)S(1)}, u32[]{:S(2)}, u32[]{:S(2)}) collective-permute-start(bf16[24,1024]{1,0:T(8,128)(2,1)S(1)} %get-tuple-element.49), channel_id=1, source_target_pairs={{0,8},{4,12},{8,0},{12,4},{1,9},{5,13},{9,1},{13,5},{2,10},{6,14},... | collective-permute-start | bytes 147464 | tf_op jit(solution)/shard_map/ppermute | solution.py:66
  26.1 5.7 %collective-permute-start.10 = (bf16[24,1024]{1,0:T(8,128)(2,1)S(1)}, bf16[24,1024]{1,0:T(8,128)(2,1)S(1)}, u32[]{:S(2)}, u32[]{:S(2)}) collective-permute-start(bf16[24,1024]{1,0:T(8,128)(2,1)S(1)} %get-tuple-element.48), channel_id=1, source_target_pairs={{0,4},{4,0},{8,12},{12,8},{1,5},{5,1},{9,13},{13,9},{2,6},{6,2},{1... | collective-permute-start | bytes 147464 | tf_op jit(solution)/shard_map/ppermute | solution.py:66
  28.4 5.9 %collective-permute-start.12 = (bf16[24,1024]{1,0:T(8,128)(2,1)S(1)}, bf16[24,1024]{1,0:T(8,128)(2,1)S(1)}, u32[]{:S(2)}, u32[]{:S(2)}) collective-permute-start(bf16[24,1024]{1,0:T(8,128)(2,1)S(1)} %get-tuple-element.50), channel_id=1, source_target_pairs={{0,12},{4,8},{8,4},{12,0},{1,13},{5,9},{9,5},{13,1},{2,14},{6,10},... | collective-permute-start | bytes 147464 | tf_op jit(solution)/shard_map/ppermute | solution.py:66
  34.6 6.6 %collective-permute-start.13 = (bf16[24,1024]{1,0:T(8,128)(2,1)S(1)}, bf16[24,1024]{1,0:T(8,128)(2,1)S(1)}, u32[]{:S(2)}, u32[]{:S(2)}) collective-permute-start(bf16[24,1024]{1,0:T(8,128)(2,1)S(1)} %get-tuple-element.53.refs_0_), channel_id=1, source_target_pairs={{0,2},{1,3},{2,0},{3,1},{4,6},{5,7},{6,4},{7,5},{8,10},{9,11},{10,... | collective-permute-start | bytes 147464 | tf_op jit(solution)/shard_map/ppermute | solution.py:66
  36.9 4.4 %collective-permute-start.16 = (bf16[24,1024]{1,0:T(8,128)(2,1)S(1)}, bf16[24,1024]{1,0:T(8,128)(2,1)S(1)}, u32[]{:S(2)}, u32[]{:S(2)}) collective-permute-start(bf16[24,1024]{1,0:T(8,128)(2,1)S(1)} %get-tuple-element.54), channel_id=1, source_target_pairs={{0,4},{4,0},{8,12},{12,8},{1,5},{5,1},{9,13},{13,9},{2,6},{6,2},{1... | collective-permute-start | bytes 147464 | tf_op jit(solution)/shard_map/ppermute | solution.py:66
  36.9 4.5 %collective-permute-start.14 = (bf16[24,1024]{1,0:T(8,128)(2,1)S(1)}, bf16[24,1024]{1,0:T(8,128)(2,1)S(1)}, u32[]{:S(2)}, u32[]{:S(2)}) collective-permute-start(bf16[24,1024]{1,0:T(8,128)(2,1)S(1)} %get-tuple-element.53.refs_0_), channel_id=1, source_target_pairs={{0,1},{1,0},{2,3},{3,2},{4,5},{5,4},{6,7},{7,6},{8,9},{9,8},{10,11... | collective-permute-start | bytes 147464 | tf_op jit(solution)/shard_map/ppermute | solution.py:66
  36.9 7.6 %collective-permute-start.20 = (bf16[24,1024]{1,0:T(8,128)(2,1)S(1)}, bf16[24,1024]{1,0:T(8,128)(2,1)S(1)}, u32[]{:S(2)}, u32[]{:S(2)}) collective-permute-start(bf16[24,1024]{1,0:T(8,128)(2,1)S(1)} %get-tuple-element.55), channel_id=1, source_target_pairs={{0,8},{4,12},{8,0},{12,4},{1,9},{5,13},{9,1},{13,5},{2,10},{6,14},... | collective-permute-start | bytes 147464 | tf_op jit(solution)/shard_map/ppermute | solution.py:66
  40.8 5.9 %collective-permute-start.24 = (bf16[24,1024]{1,0:T(8,128)(2,1)S(1)}, bf16[24,1024]{1,0:T(8,128)(2,1)S(1)}, u32[]{:S(2)}, u32[]{:S(2)}) collective-permute-start(bf16[24,1024]{1,0:T(8,128)(2,1)S(1)} %get-tuple-element.56), channel_id=1, source_target_pairs={{0,12},{4,8},{8,4},{12,0},{1,13},{5,9},{9,5},{13,1},{2,14},{6,10},... | collective-permute-start | bytes 147464 | tf_op jit(solution)/shard_map/ppermute | solution.py:66
  41.2 5.6 %collective-permute-start.15 = (bf16[24,1024]{1,0:T(8,128)(2,1)S(1)}, bf16[24,1024]{1,0:T(8,128)(2,1)S(1)}, u32[]{:S(2)}, u32[]{:S(2)}) collective-permute-start(bf16[24,1024]{1,0:T(8,128)(2,1)S(1)} %collective-permute-done.13.refs_1_), channel_id=1, source_target_pairs={{0,1},{1,0},{2,3},{3,2},{4,5},{5,4},{6,7},{7,6},{8,9},{9,8},{10,11... | collective-permute-start | bytes 147464 | tf_op jit(solution)/shard_map/ppermute | solution.py:66
  41.3 5.6 %collective-permute-start.17 = (bf16[24,1024]{1,0:T(8,128)(2,1)S(1)}, bf16[24,1024]{1,0:T(8,128)(2,1)S(1)}, u32[]{:S(2)}, u32[]{:S(2)}) collective-permute-start(bf16[24,1024]{1,0:T(8,128)(2,1)S(1)} %collective-permute-done.16.refs_4_), channel_id=1, source_target_pairs={{0,2},{1,3},{2,0},{3,1},{4,6},{5,7},{6,4},{7,5},{8,10},{9,11},{10,... | collective-permute-start | bytes 147464 | tf_op jit(solution)/shard_map/ppermute | solution.py:66
  41.4 5.9 %collective-permute-start.18 = (bf16[24,1024]{1,0:T(8,128)(2,1)S(1)}, bf16[24,1024]{1,0:T(8,128)(2,1)S(1)}, u32[]{:S(2)}, u32[]{:S(2)}) collective-permute-start(bf16[24,1024]{1,0:T(8,128)(2,1)S(1)} %collective-permute-done.16.refs_4_), channel_id=1, source_target_pairs={{0,1},{1,0},{2,3},{3,2},{4,5},{5,4},{6,7},{7,6},{8,9},{9,8},{10,11... | collective-permute-start | bytes 147464 | tf_op jit(solution)/shard_map/ppermute | solution.py:66
  44.5 4.3 %collective-permute-start.21 = (bf16[24,1024]{1,0:T(8,128)(2,1)S(1)}, bf16[24,1024]{1,0:T(8,128)(2,1)S(1)}, u32[]{:S(2)}, u32[]{:S(2)}) collective-permute-start(bf16[24,1024]{1,0:T(8,128)(2,1)S(1)} %collective-permute-done.20.refs_8_), channel_id=1, source_target_pairs={{0,2},{1,3},{2,0},{3,1},{4,6},{5,7},{6,4},{7,5},{8,10},{9,11},{10,... | collective-permute-start | bytes 147464 | tf_op jit(solution)/shard_map/ppermute | solution.py:66
  46.7 4.1 %collective-permute-start.25 = (bf16[24,1024]{1,0:T(8,128)(2,1)S(1)}, bf16[24,1024]{1,0:T(8,128)(2,1)S(1)}, u32[]{:S(2)}, u32[]{:S(2)}) collective-permute-start(bf16[24,1024]{1,0:T(8,128)(2,1)S(1)} %collective-permute-done.24.refs_12_), channel_id=1, source_target_pairs={{0,2},{1,3},{2,0},{3,1},{4,6},{5,7},{6,4},{7,5},{8,10},{9,11},{10,... | collective-permute-start | bytes 147464 | tf_op jit(solution)/shard_map/ppermute | solution.py:66
  55.9 7.0 %collective-permute-start.31 = (bf16[72,1024]{1,0:T(8,128)(2,1)S(1)}, bf16[72,1024]{1,0:T(8,128)(2,1)S(1)}, u32[]{:S(2)}, u32[]{:S(2)}) collective-permute-start(bf16[72,1024]{1,0:T(8,128)(2,1)S(1)} %get-tuple-element.59), channel_id=1, source_target_pairs={{0,2},{1,3},{2,0},{3,1},{4,6},{5,7},{6,4},{7,5},{8,10},{9,11},{10,... | collective-permute-start | bytes 442376 | tf_op jit(solution)/shard_map/ppermute | solution.py:66
  56.0 9.3 %collective-permute-start.29 = (bf16[24,1024]{1,0:T(8,128)(2,1)S(1)}, bf16[24,1024]{1,0:T(8,128)(2,1)S(1)}, u32[]{:S(2)}, u32[]{:S(2)}) collective-permute-start(bf16[24,1024]{1,0:T(8,128)(2,1)S(1)} %get-tuple-element.57), channel_id=1, source_target_pairs={{0,10},{1,11},{2,8},{3,9},{4,14},{5,15},{6,12},{7,13},{8,2},{9,3},... | collective-permute-start | bytes 147464 | tf_op jit(solution)/shard_map/ppermute | solution.py:357
  58.6 6.8 %collective-permute-start.33 = (bf16[24,1024]{1,0:T(8,128)(2,1)S(1)}, bf16[24,1024]{1,0:T(8,128)(2,1)S(1)}, u32[]{:S(2)}, u32[]{:S(2)}) collective-permute-start(bf16[24,1024]{1,0:T(8,128)(2,1)S(1)} %get-tuple-element.62), channel_id=1, source_target_pairs={{0,8},{4,12},{8,0},{12,4},{1,9},{5,13},{9,1},{13,5},{2,10},{6,14},... | collective-permute-start | bytes 147464 | tf_op jit(solution)/shard_map/ppermute | solution.py:66
  63.0 4.5 %collective-permute-start.32 = (bf16[24,1024]{1,0:T(8,128)(2,1)S(1)}, bf16[24,1024]{1,0:T(8,128)(2,1)S(1)}, u32[]{:S(2)}, u32[]{:S(2)}) collective-permute-start(bf16[24,1024]{1,0:T(8,128)(2,1)S(1)} %get-tuple-element.61), channel_id=1, source_target_pairs={{0,4},{4,0},{8,12},{12,8},{1,5},{5,1},{9,13},{13,9},{2,6},{6,2},{1... | collective-permute-start | bytes 147464 | tf_op jit(solution)/shard_map/ppermute | solution.py:66
  63.0 6.1 %collective-permute-start.34 = (bf16[24,1024]{1,0:T(8,128)(2,1)S(1)}, bf16[24,1024]{1,0:T(8,128)(2,1)S(1)}, u32[]{:S(2)}, u32[]{:S(2)}) collective-permute-start(bf16[24,1024]{1,0:T(8,128)(2,1)S(1)} %get-tuple-element.63), channel_id=1, source_target_pairs={{0,12},{4,8},{8,4},{12,0},{1,13},{5,9},{9,5},{13,1},{2,14},{6,10},... | collective-permute-start | bytes 147464 | tf_op jit(solution)/shard_map/ppermute | solution.py:66
  (15 other events, 59.0 us)

commit v11 on v9

--- a/solution.py
+++ b/solution.py
@@ -413,7 +413,7 @@
     own, *sent = sum_back(hidden, w_down, own, back[0], pick, False)
 
     blocks = [spread(swap(b, "ep", k) if k else b, quarter) for k, b in enumerate(sent)]
-    hidden = front(blocks, flags, sorted(order + [0]), 1, modulation, router, pair)
+    hidden = front(blocks, flags, order + [0], 1, modulation, router, pair)
     return tuple(sum_back(hidden, w_down, own, back[1], pick, True))
 
 

time: 67.7 us -> 67.5 us (level)
  starting transfers between devices: 30.6 us -> 29.6 us
  waiting for transfers between devices: 23 us -> 23.7 us
    ppermute x35, starting transfers between devices: 30.6 us -> 29.6 us  [swap(): return lax.ppermute(x, axis, [(i, i ^ bit) for i in range(size)])]
    ppermute x35, waiting for transfers between devices: 23 us -> 23.7 us  [swap(): return lax.ppermute(x, axis, [(i, i ^ bit) for i in range(size)])]
  transfers between devices with their start and end apart: 35 -> 35, of which waited for: 17 -> 19; matrix products, arithmetic and copies ran while one was open for 0% -> 0% of each run, Pallas kernels for 10% -> 10%
where the time goes in v11:
time: 67.5 us; the launch traced here: 67.3 us
  starting transfers between devices  29.6 us (44%)
  waiting for transfers between devices  23.7 us (35%)
  Pallas kernels  13.2 us (20%)
  between operations  0.82 us (1%)
    ppermute x35, starting transfers between devices, swap(): return lax.ppermute(x, axis, [(i, i ^ bit) for i in range(size)])  29.6 us
    ppermute x35, waiting for transfers between devices, swap(): return lax.ppermute(x, axis, [(i, i ^ bit) for i in range(size)])  23.7 us
    pallas_call x2, Pallas kernels, front(): pl.pallas_call(functools.partial(front_kernel, layout, order, section, ex...  3.8 us
    pallas_call x1, Pallas kernels, load(): pl.pallas_call(load_kernel, in_specs=[ANY] * 3, out_specs=[VMEM] * 3, out...  3.78 us
    pallas_call x8, Pallas kernels, down(): pl.pallas_call(functools.partial(down_kernel, flip, len(adds)), in_specs=...  2.24 us
  transfers between devices with their start and end apart: 35, of which 19 were waited for; matrix products, arithmetic and copies ran while one was open for 0% of the time, Pallas kernels for 10%

profile of v11, /device:TPU:0, one launch (start us, length us, event | category | flops | bytes accessed | tf_op | source)
XLA Modules:
  0.0 67.3 jit_solution(9037979573470556618)
XLA Ops:
  0.6 1.2 %pack.1 = (bf16[24,2176]{1,0:T(8,128)(2,1)S(1)}, bf16[24,2176]{1,0:T(8,128)(2,1)S(1)}, bf16[24,2176]{1,0:T(8,128)(2,1)S(1)}, bf16[32,1024]{1,0:T(8,128)(2,1)S(1)}) custom-call(bf16[32,4096]{1,0:T(8,128)(2,1)} %tokens_ref.3, s32[2,2,32]{2,1,0:T(2,128)} %bitcast.4), custom_call_target="tpu_custom_call" | custom-call | tf_op jit(solution)/shard_map/pack/pallas_call | solution.py:197
  1.9 4.1 %collective-permute-start = (bf16[24,2176]{1,0:T(8,128)(2,1)S(1)}, bf16[24,2176]{1,0:T(8,128)(2,1)S(1)}, u32[]{:S(2)}, u32[]{:S(2)}) collective-permute-start(bf16[24,2176]{1,0:T(8,128)(2,1)S(1)} %get-tuple-element.38), channel_id=1, source_target_pairs={{0,8},{4,12},{8,0},{12,4},{1,9},{5,13},{9,1},{13,5},{2,10},{6,14},... | collective-permute-start | bytes 313352 | tf_op jit(solution)/shard_map/ppermute | solution.py:66
  6.0 1.3 %collective-permute-start.2 = (bf16[24,2176]{1,0:T(8,128)(2,1)S(1)}, bf16[24,2176]{1,0:T(8,128)(2,1)S(1)}, u32[]{:S(2)}, u32[]{:S(2)}) collective-permute-start(bf16[24,2176]{1,0:T(8,128)(2,1)S(1)} %get-tuple-element.40), channel_id=1, source_target_pairs={{0,12},{4,8},{8,4},{12,0},{1,13},{5,9},{9,5},{13,1},{2,14},{6,10},... | collective-permute-start | bytes 313352 | tf_op jit(solution)/shard_map/ppermute | solution.py:66
  7.6 3.8 %load.1 = (bf16[4096,768]{1,0:T(8,128)(2,1)S(1)}, bf16[384,4096]{1,0:T(8,128)(2,1)S(1)}, f32[8,128]{1,0:T(8,128)S(1)}) custom-call(bf16[1,4096,384]{2,1,0:T(8,128)(2,1)} %gate_ref.1, bf16[1,4096,384]{2,1,0:T(8,128)(2,1)} %up_ref.1, bf16[1,384,4096]{2,1,0:T(8,128)(2,1)} %down_ref.1), custom_call_target="tpu_custom_call" | custom-call | bytes 18874368 | tf_op jit(solution)/shard_map/load/pallas_call | solution.py:101
  11.4 2.8 %collective-permute-done.block_ref.refs_7_.refs_16_ = bf16[24,2176]{1,0:T(8,128)(2,1)S(1)} collective-permute-done((bf16[24,2176]{1,0:T(8,128)(2,1)S(1)}, bf16[24,2176]{1,0:T(8,128)(2,1)S(1)}, u32[]{:S(2)}, u32[]{:S(2)}) %collective-permute-start) | collective-permute-done | bytes 104480 | tf_op jit(solution)/shard_map/ppermute | solution.py:66
  16.3 1.8 %front.2.hidden_ref = bf16[96,384]{1,0:T(8,128)(2,1)S(1)} custom-call(bf16[24,2048]{1,0:T(8,128)(2,1)S(1)} %relay.3.refs_0_, bf16[24,2048]{1,0:T(8,128)(2,1)S(1)} %collective-permute-done.1.refs_1_, bf16[24,2048]{1,0:T(8,128)(2,1)S(1)} %relay.4.refs_2_, bf16[24,2048]{1,0:T(8,128)(2,1)S(1)} %collective-permute-done.3.refs_3_, ...), custom_call_target="tpu_custom_call" | custom-call | flops 603979776 | bytes 6291456 | tf_op jit(solution)/shard_map/front/pallas_call | solution.py:291
  20.0 1.9 %collective-permute-start.10 = (bf16[48,1024]{1,0:T(8,128)(2,1)S(1)}, bf16[48,1024]{1,0:T(8,128)(2,1)S(1)}, u32[]{:S(2)}, u32[]{:S(2)}) collective-permute-start(bf16[48,1024]{1,0:T(8,128)(2,1)S(1)} %get-tuple-element.51), channel_id=1, source_target_pairs={{0,2},{1,3},{2,0},{3,1},{4,6},{5,7},{6,4},{7,5},{8,10},{9,11},{10,... | collective-permute-start | bytes 294920 | tf_op jit(solution)/shard_map/ppermute | solution.py:66
  22.4 3.3 %collective-permute-done.10.came_ref = bf16[48,1024]{1,0:T(8,128)(2,1)S(1)} collective-permute-done((bf16[48,1024]{1,0:T(8,128)(2,1)S(1)}, bf16[48,1024]{1,0:T(8,128)(2,1)S(1)}, u32[]{:S(2)}, u32[]{:S(2)}) %collective-permute-start.10) | collective-permute-done | bytes 98336 | tf_op jit(solution)/shard_map/ppermute | solution.py:66
  25.7 3.7 %collective-permute-start.11 = (bf16[24,1024]{1,0:T(8,128)(2,1)S(1)}, bf16[24,1024]{1,0:T(8,128)(2,1)S(1)}, u32[]{:S(2)}, u32[]{:S(2)}) collective-permute-start(bf16[24,1024]{1,0:T(8,128)(2,1)S(1)} %get-tuple-element.52), channel_id=1, source_target_pairs={{0,8},{4,12},{8,0},{12,4},{1,9},{5,13},{9,1},{13,5},{2,10},{6,14},... | collective-permute-start | bytes 147464 | tf_op jit(solution)/shard_map/ppermute | solution.py:66
  30.1 1.9 %collective-permute-done.11.refs_2_ = bf16[24,1024]{1,0:T(8,128)(2,1)S(1)} collective-permute-done((bf16[24,1024]{1,0:T(8,128)(2,1)S(1)}, bf16[24,1024]{1,0:T(8,128)(2,1)S(1)}, u32[]{:S(2)}, u32[]{:S(2)}) %collective-permute-start.11) | collective-permute-done | bytes 49184 | tf_op jit(solution)/shard_map/ppermute | solution.py:66
  32.0 3.3 %collective-permute-done.12.refs_3_ = bf16[24,1024]{1,0:T(8,128)(2,1)S(1)} collective-permute-done((bf16[24,1024]{1,0:T(8,128)(2,1)S(1)}, bf16[24,1024]{1,0:T(8,128)(2,1)S(1)}, u32[]{:S(2)}, u32[]{:S(2)}) %collective-permute-start.12) | collective-permute-done | bytes 49184 | tf_op jit(solution)/shard_map/ppermute | solution.py:66
  37.9 1.3 %collective-permute-start.21 = (bf16[24,1024]{1,0:T(8,128)(2,1)S(1)}, bf16[24,1024]{1,0:T(8,128)(2,1)S(1)}, u32[]{:S(2)}, u32[]{:S(2)}) collective-permute-start(bf16[24,1024]{1,0:T(8,128)(2,1)S(1)} %get-tuple-element.58), channel_id=1, source_target_pairs={{0,4},{4,0},{8,12},{12,8},{1,5},{5,1},{9,13},{13,9},{2,6},{6,2},{1... | collective-permute-start | bytes 147464 | tf_op jit(solution)/shard_map/ppermute | solution.py:66
  39.1 1.5 %collective-permute-start.25 = (bf16[24,1024]{1,0:T(8,128)(2,1)S(1)}, bf16[24,1024]{1,0:T(8,128)(2,1)S(1)}, u32[]{:S(2)}, u32[]{:S(2)}) collective-permute-start(bf16[24,1024]{1,0:T(8,128)(2,1)S(1)} %get-tuple-element.59.refs_12_), channel_id=1, source_target_pairs={{0,2},{1,3},{2,0},{3,1},{4,6},{5,7},{6,4},{7,5},{8,10},{9,11},{10,... | collective-permute-start | bytes 147464 | tf_op jit(solution)/shard_map/ppermute | solution.py:66
  40.7 1.5 %collective-permute-start.14 = (bf16[24,1024]{1,0:T(8,128)(2,1)S(1)}, bf16[24,1024]{1,0:T(8,128)(2,1)S(1)}, u32[]{:S(2)}, u32[]{:S(2)}) collective-permute-start(bf16[24,1024]{1,0:T(8,128)(2,1)S(1)} %collective-permute-done.13.refs_0_), channel_id=1, source_target_pairs={{0,2},{1,3},{2,0},{3,1},{4,6},{5,7},{6,4},{7,5},{8,10},{9,11},{10,... | collective-permute-start | bytes 147464 | tf_op jit(solution)/shard_map/ppermute | solution.py:66
  42.6 1.5 %collective-permute-start.18 = (bf16[24,1024]{1,0:T(8,128)(2,1)S(1)}, bf16[24,1024]{1,0:T(8,128)(2,1)S(1)}, u32[]{:S(2)}, u32[]{:S(2)}) collective-permute-start(bf16[24,1024]{1,0:T(8,128)(2,1)S(1)} %collective-permute-done.17.refs_4_), channel_id=1, source_target_pairs={{0,2},{1,3},{2,0},{3,1},{4,6},{5,7},{6,4},{7,5},{8,10},{9,11},{10,... | collective-permute-start | bytes 147464 | tf_op jit(solution)/shard_map/ppermute | solution.py:66
  45.3 1.4 %collective-permute-done.18.refs_5_ = bf16[24,1024]{1,0:T(8,128)(2,1)S(1)} collective-permute-done((bf16[24,1024]{1,0:T(8,128)(2,1)S(1)}, bf16[24,1024]{1,0:T(8,128)(2,1)S(1)}, u32[]{:S(2)}, u32[]{:S(2)}) %collective-permute-start.18) | collective-permute-done | bytes 49184 | tf_op jit(solution)/shard_map/ppermute | solution.py:66
  46.7 1.5 %collective-permute-done.22.refs_9_ = bf16[24,1024]{1,0:T(8,128)(2,1)S(1)} collective-permute-done((bf16[24,1024]{1,0:T(8,128)(2,1)S(1)}, bf16[24,1024]{1,0:T(8,128)(2,1)S(1)}, u32[]{:S(2)}, u32[]{:S(2)}) %collective-permute-start.22) | collective-permute-done | bytes 49184 | tf_op jit(solution)/shard_map/ppermute | solution.py:66
  50.0 2.0 %front.3.hidden_ref = bf16[96,384]{1,0:T(8,128)(2,1)S(1)} custom-call(bf16[24,1024]{1,0:T(8,128)(2,1)S(1)} %collective-permute-done.13.refs_0_, bf16[24,1024]{1,0:T(8,128)(2,1)S(1)} %collective-permute-done.14.refs_1_, bf16[24,1024]{1,0:T(8,128)(2,1)S(1)} %collective-permute-done.15.refs_2_, bf16[24,1024]{1,0:T(8,128)(2,1)S(1)} %collective-permute-done.16.refs_3_, ...), custom_call_target="tpu_custom_call" | custom-call | flops 603979776 | bytes 6291456 | tf_op jit(solution)/shard_map/front/pallas_call | solution.py:291
  54.4 1.5 %collective-permute-start.30 = (bf16[48,1024]{1,0:T(8,128)(2,1)S(1)}, bf16[48,1024]{1,0:T(8,128)(2,1)S(1)}, u32[]{:S(2)}, u32[]{:S(2)}) collective-permute-start(bf16[48,1024]{1,0:T(8,128)(2,1)S(1)} %get-tuple-element.61), channel_id=1, source_target_pairs={{0,2},{1,3},{2,0},{3,1},{4,6},{5,7},{6,4},{7,5},{8,10},{9,11},{10,... | collective-permute-start | bytes 294920 | tf_op jit(solution)/shard_map/ppermute | solution.py:66
  56.2 3.3 %collective-permute-done.32.came_ref = bf16[48,1024]{1,0:T(8,128)(2,1)S(1)} collective-permute-done((bf16[48,1024]{1,0:T(8,128)(2,1)S(1)}, bf16[48,1024]{1,0:T(8,128)(2,1)S(1)}, u32[]{:S(2)}, u32[]{:S(2)}) %collective-permute-start.32) | collective-permute-done | bytes 98336 | tf_op jit(solution)/shard_map/ppermute | solution.py:66
  60.3 1.5 %collective-permute-start.34 = (bf16[24,1024]{1,0:T(8,128)(2,1)S(1)}, bf16[24,1024]{1,0:T(8,128)(2,1)S(1)}, u32[]{:S(2)}, u32[]{:S(2)}) collective-permute-start(bf16[24,1024]{1,0:T(8,128)(2,1)S(1)} %get-tuple-element.67), channel_id=1, source_target_pairs={{0,12},{4,8},{8,4},{12,0},{1,13},{5,9},{9,5},{13,1},{2,14},{6,10},... | collective-permute-start | bytes 147464 | tf_op jit(solution)/shard_map/ppermute | solution.py:66
  61.8 1.4 %collective-permute-start.31 = (bf16[24,1024]{1,0:T(8,128)(2,1)S(1)}, bf16[24,1024]{1,0:T(8,128)(2,1)S(1)}, u32[]{:S(2)}, u32[]{:S(2)}) collective-permute-start(bf16[24,1024]{1,0:T(8,128)(2,1)S(1)} %get-tuple-element.63), channel_id=1, source_target_pairs={{0,4},{4,0},{8,12},{12,8},{1,5},{5,1},{9,13},{13,9},{2,6},{6,2},{1... | collective-permute-start | bytes 147464 | tf_op jit(solution)/shard_map/ppermute | solution.py:66
  63.2 1.5 %collective-permute-done.33.refs_2_ = bf16[24,1024]{1,0:T(8,128)(2,1)S(1)} collective-permute-done((bf16[24,1024]{1,0:T(8,128)(2,1)S(1)}, bf16[24,1024]{1,0:T(8,128)(2,1)S(1)}, u32[]{:S(2)}, u32[]{:S(2)}) %collective-permute-start.33) | collective-permute-done | bytes 49184 | tf_op jit(solution)/shard_map/ppermute | solution.py:66
  64.7 1.6 %collective-permute-done.34.refs_3_ = bf16[24,1024]{1,0:T(8,128)(2,1)S(1)} collective-permute-done((bf16[24,1024]{1,0:T(8,128)(2,1)S(1)}, bf16[24,1024]{1,0:T(8,128)(2,1)S(1)}, u32[]{:S(2)}, u32[]{:S(2)}) %collective-permute-start.34) | collective-permute-done | bytes 49184 | tf_op jit(solution)/shard_map/ppermute | solution.py:66
  (78 shorter events, 15.9 us)
Async XLA Ops:
  1.9 12.4 %collective-permute-start = (bf16[24,2176]{1,0:T(8,128)(2,1)S(1)}, bf16[24,2176]{1,0:T(8,128)(2,1)S(1)}, u32[]{:S(2)}, u32[]{:S(2)}) collective-permute-start(bf16[24,2176]{1,0:T(8,128)(2,1)S(1)} %get-tuple-element.38), channel_id=1, source_target_pairs={{0,8},{4,12},{8,0},{12,4},{1,9},{5,13},{9,1},{13,5},{2,10},{6,14},... | collective-permute-start | bytes 313352 | tf_op jit(solution)/shard_map/ppermute | solution.py:66
  6.0 8.4 %collective-permute-start.2 = (bf16[24,2176]{1,0:T(8,128)(2,1)S(1)}, bf16[24,2176]{1,0:T(8,128)(2,1)S(1)}, u32[]{:S(2)}, u32[]{:S(2)}) collective-permute-start(bf16[24,2176]{1,0:T(8,128)(2,1)S(1)} %get-tuple-element.40), channel_id=1, source_target_pairs={{0,12},{4,8},{8,4},{12,0},{1,13},{5,9},{9,5},{13,1},{2,14},{6,10},... | collective-permute-start | bytes 313352 | tf_op jit(solution)/shard_map/ppermute | solution.py:66
  7.3 7.6 %collective-permute-start.4 = (bf16[24,2176]{1,0:T(8,128)(2,1)S(1)}, bf16[24,2176]{1,0:T(8,128)(2,1)S(1)}, u32[]{:S(2)}, u32[]{:S(2)}) collective-permute-start(bf16[24,2176]{1,0:T(8,128)(2,1)S(1)} %get-tuple-element.41), channel_id=1, source_target_pairs={{0,4},{4,0},{8,12},{12,8},{1,5},{5,1},{9,13},{13,9},{2,6},{6,2},{1... | collective-permute-start | bytes 313352 | tf_op jit(solution)/shard_map/ppermute | solution.py:66
  20.0 5.7 %collective-permute-start.10 = (bf16[48,1024]{1,0:T(8,128)(2,1)S(1)}, bf16[48,1024]{1,0:T(8,128)(2,1)S(1)}, u32[]{:S(2)}, u32[]{:S(2)}) collective-permute-start(bf16[48,1024]{1,0:T(8,128)(2,1)S(1)} %get-tuple-element.51), channel_id=1, source_target_pairs={{0,2},{1,3},{2,0},{3,1},{4,6},{5,7},{6,4},{7,5},{8,10},{9,11},{10,... | collective-permute-start | bytes 294920 | tf_op jit(solution)/shard_map/ppermute | solution.py:66
  21.9 7.9 %collective-permute-start.8 = (bf16[48,1024]{1,0:T(8,128)(2,1)S(1)}, bf16[48,1024]{1,0:T(8,128)(2,1)S(1)}, u32[]{:S(2)}, u32[]{:S(2)}) collective-permute-start(bf16[48,1024]{1,0:T(8,128)(2,1)S(1)} %get-tuple-element.47), channel_id=1, source_target_pairs={{0,2},{1,3},{2,0},{3,1},{4,6},{5,7},{6,4},{7,5},{8,10},{9,11},{10,... | collective-permute-start | bytes 294920 | tf_op jit(solution)/shard_map/ppermute | solution.py:66
  25.7 6.3 %collective-permute-start.11 = (bf16[24,1024]{1,0:T(8,128)(2,1)S(1)}, bf16[24,1024]{1,0:T(8,128)(2,1)S(1)}, u32[]{:S(2)}, u32[]{:S(2)}) collective-permute-start(bf16[24,1024]{1,0:T(8,128)(2,1)S(1)} %get-tuple-element.52), channel_id=1, source_target_pairs={{0,8},{4,12},{8,0},{12,4},{1,9},{5,13},{9,1},{13,5},{2,10},{6,14},... | collective-permute-start | bytes 147464 | tf_op jit(solution)/shard_map/ppermute | solution.py:66
  29.4 5.9 %collective-permute-start.12 = (bf16[24,1024]{1,0:T(8,128)(2,1)S(1)}, bf16[24,1024]{1,0:T(8,128)(2,1)S(1)}, u32[]{:S(2)}, u32[]{:S(2)}) collective-permute-start(bf16[24,1024]{1,0:T(8,128)(2,1)S(1)} %get-tuple-element.53), channel_id=1, source_target_pairs={{0,12},{4,8},{8,4},{12,0},{1,13},{5,9},{9,5},{13,1},{2,14},{6,10},... | collective-permute-start | bytes 147464 | tf_op jit(solution)/shard_map/ppermute | solution.py:66
  29.8 5.5 %collective-permute-start.9 = (bf16[24,1024]{1,0:T(8,128)(2,1)S(1)}, bf16[24,1024]{1,0:T(8,128)(2,1)S(1)}, u32[]{:S(2)}, u32[]{:S(2)}) collective-permute-start(bf16[24,1024]{1,0:T(8,128)(2,1)S(1)} %get-tuple-element.49), channel_id=1, source_target_pairs={{0,4},{4,0},{8,12},{12,8},{1,5},{5,1},{9,13},{13,9},{2,6},{6,2},{1... | collective-permute-start | bytes 147464 | tf_op jit(solution)/shard_map/ppermute | solution.py:66
  35.6 5.2 %collective-permute-start.13 = (bf16[24,1024]{1,0:T(8,128)(2,1)S(1)}, bf16[24,1024]{1,0:T(8,128)(2,1)S(1)}, u32[]{:S(2)}, u32[]{:S(2)}) collective-permute-start(bf16[24,1024]{1,0:T(8,128)(2,1)S(1)} %get-tuple-element.56), channel_id=1, source_target_pairs={{0,8},{4,12},{8,0},{12,4},{1,9},{5,13},{9,1},{13,5},{2,10},{6,14},... | collective-permute-start | bytes 147464 | tf_op jit(solution)/shard_map/ppermute | solution.py:66
  36.7 5.9 %collective-permute-start.17 = (bf16[24,1024]{1,0:T(8,128)(2,1)S(1)}, bf16[24,1024]{1,0:T(8,128)(2,1)S(1)}, u32[]{:S(2)}, u32[]{:S(2)}) collective-permute-start(bf16[24,1024]{1,0:T(8,128)(2,1)S(1)} %get-tuple-element.57), channel_id=1, source_target_pairs={{0,12},{4,8},{8,4},{12,0},{1,13},{5,9},{9,5},{13,1},{2,14},{6,10},... | collective-permute-start | bytes 147464 | tf_op jit(solution)/shard_map/ppermute | solution.py:66
  37.9 6.3 %collective-permute-start.21 = (bf16[24,1024]{1,0:T(8,128)(2,1)S(1)}, bf16[24,1024]{1,0:T(8,128)(2,1)S(1)}, u32[]{:S(2)}, u32[]{:S(2)}) collective-permute-start(bf16[24,1024]{1,0:T(8,128)(2,1)S(1)} %get-tuple-element.58), channel_id=1, source_target_pairs={{0,4},{4,0},{8,12},{12,8},{1,5},{5,1},{9,13},{13,9},{2,6},{6,2},{1... | collective-permute-start | bytes 147464 | tf_op jit(solution)/shard_map/ppermute | solution.py:66
  39.1 5.5 %collective-permute-start.25 = (bf16[24,1024]{1,0:T(8,128)(2,1)S(1)}, bf16[24,1024]{1,0:T(8,128)(2,1)S(1)}, u32[]{:S(2)}, u32[]{:S(2)}) collective-permute-start(bf16[24,1024]{1,0:T(8,128)(2,1)S(1)} %get-tuple-element.59.refs_12_), channel_id=1, source_target_pairs={{0,2},{1,3},{2,0},{3,1},{4,6},{5,7},{6,4},{7,5},{8,10},{9,11},{10,... | collective-permute-start | bytes 147464 | tf_op jit(solution)/shard_map/ppermute | solution.py:66
  40.6 4.0 %collective-permute-start.26 = (bf16[24,1024]{1,0:T(8,128)(2,1)S(1)}, bf16[24,1024]{1,0:T(8,128)(2,1)S(1)}, u32[]{:S(2)}, u32[]{:S(2)}) collective-permute-start(bf16[24,1024]{1,0:T(8,128)(2,1)S(1)} %get-tuple-element.59.refs_12_), channel_id=1, source_target_pairs={{0,1},{1,0},{2,3},{3,2},{4,5},{5,4},{6,7},{7,6},{8,9},{9,8},{10,11... | collective-permute-start | bytes 147464 | tf_op jit(solution)/shard_map/ppermute | solution.py:66
  40.7 4.5 %collective-permute-start.14 = (bf16[24,1024]{1,0:T(8,128)(2,1)S(1)}, bf16[24,1024]{1,0:T(8,128)(2,1)S(1)}, u32[]{:S(2)}, u32[]{:S(2)}) collective-permute-start(bf16[24,1024]{1,0:T(8,128)(2,1)S(1)} %collective-permute-done.13.refs_0_), channel_id=1, source_target_pairs={{0,2},{1,3},{2,0},{3,1},{4,6},{5,7},{6,4},{7,5},{8,10},{9,11},{10,... | collective-permute-start | bytes 147464 | tf_op jit(solution)/shard_map/ppermute | solution.py:66
  42.6 4.1 %collective-permute-start.18 = (bf16[24,1024]{1,0:T(8,128)(2,1)S(1)}, bf16[24,1024]{1,0:T(8,128)(2,1)S(1)}, u32[]{:S(2)}, u32[]{:S(2)}) collective-permute-start(bf16[24,1024]{1,0:T(8,128)(2,1)S(1)} %collective-permute-done.17.refs_4_), channel_id=1, source_target_pairs={{0,2},{1,3},{2,0},{3,1},{4,6},{5,7},{6,4},{7,5},{8,10},{9,11},{10,... | collective-permute-start | bytes 147464 | tf_op jit(solution)/shard_map/ppermute | solution.py:66
  44.1 4.1 %collective-permute-start.22 = (bf16[24,1024]{1,0:T(8,128)(2,1)S(1)}, bf16[24,1024]{1,0:T(8,128)(2,1)S(1)}, u32[]{:S(2)}, u32[]{:S(2)}) collective-permute-start(bf16[24,1024]{1,0:T(8,128)(2,1)S(1)} %collective-permute-done.21.refs_8_), channel_id=1, source_target_pairs={{0,2},{1,3},{2,0},{3,1},{4,6},{5,7},{6,4},{7,5},{8,10},{9,11},{10,... | collective-permute-start | bytes 147464 | tf_op jit(solution)/shard_map/ppermute | solution.py:66
  44.7 3.6 %collective-permute-start.15 = (bf16[24,1024]{1,0:T(8,128)(2,1)S(1)}, bf16[24,1024]{1,0:T(8,128)(2,1)S(1)}, u32[]{:S(2)}, u32[]{:S(2)}) collective-permute-start(bf16[24,1024]{1,0:T(8,128)(2,1)S(1)} %collective-permute-done.13.refs_0_), channel_id=1, source_target_pairs={{0,1},{1,0},{2,3},{3,2},{4,5},{5,4},{6,7},{7,6},{8,9},{9,8},{10,11... | collective-permute-start | bytes 147464 | tf_op jit(solution)/shard_map/ppermute | solution.py:66
  44.7 4.1 %collective-permute-start.19 = (bf16[24,1024]{1,0:T(8,128)(2,1)S(1)}, bf16[24,1024]{1,0:T(8,128)(2,1)S(1)}, u32[]{:S(2)}, u32[]{:S(2)}) collective-permute-start(bf16[24,1024]{1,0:T(8,128)(2,1)S(1)} %collective-permute-done.17.refs_4_), channel_id=1, source_target_pairs={{0,1},{1,0},{2,3},{3,2},{4,5},{5,4},{6,7},{7,6},{8,9},{9,8},{10,11... | collective-permute-start | bytes 147464 | tf_op jit(solution)/shard_map/ppermute | solution.py:66
  45.3 3.5 %collective-permute-start.23 = (bf16[24,1024]{1,0:T(8,128)(2,1)S(1)}, bf16[24,1024]{1,0:T(8,128)(2,1)S(1)}, u32[]{:S(2)}, u32[]{:S(2)}) collective-permute-start(bf16[24,1024]{1,0:T(8,128)(2,1)S(1)} %collective-permute-done.21.refs_8_), channel_id=1, source_target_pairs={{0,1},{1,0},{2,3},{3,2},{4,5},{5,4},{6,7},{7,6},{8,9},{9,8},{10,11... | collective-permute-start | bytes 147464 | tf_op jit(solution)/shard_map/ppermute | solution.py:66
  53.8 5.7 %collective-permute-start.32 = (bf16[48,1024]{1,0:T(8,128)(2,1)S(1)}, bf16[48,1024]{1,0:T(8,128)(2,1)S(1)}, u32[]{:S(2)}, u32[]{:S(2)}) collective-permute-start(bf16[48,1024]{1,0:T(8,128)(2,1)S(1)} %get-tuple-element.65), channel_id=1, source_target_pairs={{0,2},{1,3},{2,0},{3,1},{4,6},{5,7},{6,4},{7,5},{8,10},{9,11},{10,... | collective-permute-start | bytes 294920 | tf_op jit(solution)/shard_map/ppermute | solution.py:66
  54.4 7.4 %collective-permute-start.30 = (bf16[48,1024]{1,0:T(8,128)(2,1)S(1)}, bf16[48,1024]{1,0:T(8,128)(2,1)S(1)}, u32[]{:S(2)}, u32[]{:S(2)}) collective-permute-start(bf16[48,1024]{1,0:T(8,128)(2,1)S(1)} %get-tuple-element.61), channel_id=1, source_target_pairs={{0,2},{1,3},{2,0},{3,1},{4,6},{5,7},{6,4},{7,5},{8,10},{9,11},{10,... | collective-permute-start | bytes 294920 | tf_op jit(solution)/shard_map/ppermute | solution.py:66
  59.5 5.2 %collective-permute-start.33 = (bf16[24,1024]{1,0:T(8,128)(2,1)S(1)}, bf16[24,1024]{1,0:T(8,128)(2,1)S(1)}, u32[]{:S(2)}, u32[]{:S(2)}) collective-permute-start(bf16[24,1024]{1,0:T(8,128)(2,1)S(1)} %get-tuple-element.66), channel_id=1, source_target_pairs={{0,8},{4,12},{8,0},{12,4},{1,9},{5,13},{9,1},{13,5},{2,10},{6,14},... | collective-permute-start | bytes 147464 | tf_op jit(solution)/shard_map/ppermute | solution.py:66
  60.3 6.0 %collective-permute-start.34 = (bf16[24,1024]{1,0:T(8,128)(2,1)S(1)}, bf16[24,1024]{1,0:T(8,128)(2,1)S(1)}, u32[]{:S(2)}, u32[]{:S(2)}) collective-permute-start(bf16[24,1024]{1,0:T(8,128)(2,1)S(1)} %get-tuple-element.67), channel_id=1, source_target_pairs={{0,12},{4,8},{8,4},{12,0},{1,13},{5,9},{9,5},{13,1},{2,14},{6,10},... | collective-permute-start | bytes 147464 | tf_op jit(solution)/shard_map/ppermute | solution.py:66
  61.8 4.7 %collective-permute-start.31 = (bf16[24,1024]{1,0:T(8,128)(2,1)S(1)}, bf16[24,1024]{1,0:T(8,128)(2,1)S(1)}, u32[]{:S(2)}, u32[]{:S(2)}) collective-permute-start(bf16[24,1024]{1,0:T(8,128)(2,1)S(1)} %get-tuple-element.63), channel_id=1, source_target_pairs={{0,4},{4,0},{8,12},{12,8},{1,5},{5,1},{9,13},{13,9},{2,6},{6,2},{1... | collective-permute-start | bytes 147464 | tf_op jit(solution)/shard_map/ppermute | solution.py:66
  (15 other events, 53.0 us)

commit v12 on v11

--- a/solution.py
+++ b/solution.py
@@ -209,7 +209,7 @@
     )(tokens, ids)
 
 
-def own_kernel(experts, tokens_ref, ids_ref, out_ref, flags_ref, *choice_refs):
+def own_kernel(experts, tokens_ref, ids_ref, done_ref, out_ref, flags_ref, *choice_refs):
     ids = [ids_ref[s] for s in range(ids_ref.shape[0])]
     slots = out_ref.shape[0]
     held = choices(ids, choice_refs[0].shape[0] // slots, slots)
@@ -220,7 +220,7 @@
         choice_refs[2 * s + 1][...] = narrow(one.T)
 
 
-def own_rows(tokens, ids, experts, slots):
+def own_rows(tokens, ids, experts, slots, done):
     rows, width = tokens.shape
     total = lax.axis_size("ep") * slots
     shapes = [(slots, width), (slots, LANES)] + [(total, rows), (rows, total)] * ids.shape[0]
@@ -229,22 +229,19 @@
         out_shape=[jax.ShapeDtypeStruct(s, jnp.bfloat16) for s in shapes],
         compiler_params=params(),
         name="own_rows",
-    )(tokens, ids)
-
-
-def front_kernel(layout, order, section, experts, n_flags, *refs):
+    )(tokens, ids, done)
+
+
+def front_kernel(layout, order, flips, section, experts, *refs):
     n = sum(len(block) for block in layout)
-    x_refs, flag_refs = list(refs[:n]), refs[n : n + n_flags]
-    flag_refs = [flag_refs[order.index(k)] for k in range(n_flags)]
-    mod_ref, router_ref, pair_ref, out_ref, normed_ref = refs[n + n_flags :]
-    width = normed_ref.shape[1]
-    hidden = out_ref.shape[1]
+    x_refs = list(refs[:n])
+    mod_ref, router_ref, pair_ref, *rest = refs[n:]
+    width = pair_ref.shape[0]
     quarter = width // 4
     et = lax.axis_index("et")
     blocks = {}
     for k in order:
         blocks[k] = [(x_refs.pop(0), cols, flip) for cols, flip in layout[k]]
-    blocks = [blocks[k] for k in range(len(layout))]
 
     def part(block, flip):
         for ref, cols, at in block:
@@ -255,50 +252,72 @@
             if cols == width:
                 return ref[:, aligned(et ^ flip, quarter)].astype(jnp.float32)
 
-    parts = [jnp.concatenate([part(block, flip) for block in blocks], axis=0) for flip in range(4)]
-    total = sum(jnp.sum(xf * xf, axis=1, keepdims=True) for xf in parts)
-    scale = lax.rsqrt(total / width + 1e-06)
-    for flip, xf in enumerate(parts):
+    units, logits, squares = 0.0, 0.0, 0.0
+    for flip in flips:
+        xf = jnp.concatenate([part(blocks[k], flip) for k in range(len(layout))], axis=0)
+        squares += jnp.sum(xf * xf, axis=1, keepdims=True)
         where = aligned(et ^ flip, quarter)
-        normed_ref[:, where] = (
-            xf * scale * (1.0 + mod_ref[section, 0:1, where]) + mod_ref[section, 1:2, where]
-        ).astype(jnp.bfloat16)
-    normed = normed_ref[...]
-    both = jnp.dot(normed, pair_ref[...], preferred_element_type=jnp.float32)
-    logits = lax.dot_general(
-        normed, router_ref[...], (((1,), (1,)), ((), ())), preferred_element_type=jnp.float32
-    )
+        shift = mod_ref[section, 1:2, where]
+        head = narrow(shift).astype(jnp.float32)
+        blank = jnp.zeros((6, quarter), jnp.float32)
+        lhs = [xf * (1.0 + mod_ref[section, 0:1, where]), head, shift - head, blank]
+        lhs = narrow(jnp.concatenate(lhs, axis=0))
+        units += jnp.dot(lhs, pair_ref[where, :], preferred_element_type=jnp.float32)
+        logits += lax.dot_general(
+            lhs, router_ref[:, where], (((1,), (1,)), ((), ())), preferred_element_type=jnp.float32
+        )
+    if len(rest) == 3:
+        rest[0][...], rest[1][...], rest[2][...] = units, logits, squares
+        return
+    *flag_refs, units_ref, logits_ref, squares_ref, out_ref = rest
+    rows, hidden = out_ref.shape
+    scale = lax.rsqrt((squares + squares_ref[...]) / width + 1e-06)
+
+    def scaled(x):
+        return x[:rows] * scale + (x[rows : rows + 1] + x[rows + 1 : rows + 2])
+
+    units, logits = scaled(units + units_ref[...]), scaled(logits + logits_ref[...])
     count = logits.shape[1]
     lane = lax.broadcasted_iota(jnp.int32, logits.shape, 1)
-    flags = [f[:, f.shape[1] - LANES :].astype(jnp.float32) for f in flag_refs]
+    flags = [flag_refs[order.index(k)] for k in range(len(layout))]
+    flags = [f[:, f.shape[1] - LANES :].astype(jnp.float32) for f in flags]
     flags = jnp.concatenate(flags, axis=0)[:, section * experts : section * experts + count]
     chosen = jnp.where(flags > 0.5, jax.nn.sigmoid(logits), 0.0)
     mine = jnp.sum(jnp.where(lane == lax.axis_index("ep"), chosen, 0.0), axis=1, keepdims=True)
     used = jnp.max(flags, axis=1, keepdims=True) > 0.5
     weight = jnp.where(used, mine / jnp.sum(chosen, axis=1, keepdims=True), 0.0)
-    gate, upper = both[:, :hidden], both[:, hidden:]
-    units = jnp.where(used, gate / (1.0 + jnp.exp(-gate)) * upper * weight, 0.0)
-    out_ref[...] = units.astype(jnp.bfloat16)
-
-
-def front(blocks, flags, order, section, mod, router, pair):
-    width, hidden = pair.shape[0], pair.shape[1] // 2
-    rows = sum(f.shape[0] for f in flags)
-    experts = router.shape[0]
+    gate, upper = units[:, :hidden], units[:, hidden:]
+    out = jnp.where(used, gate / (1.0 + jnp.exp(-gate)) * upper * weight, 0.0)
+    out_ref[...] = narrow(out)
+
+
+def half_front(blocks, flips, extra, shapes, order, section, mod, router, pair):
     xs = [x for k in order for x, _, _ in blocks[k]]
-    flags = [flags[k] for k in order]
     layout = [[piece[1:] for piece in block] for block in blocks]
-    return pl.pallas_call(
-        functools.partial(front_kernel, layout, order, section, experts, len(flags)),
-        in_specs=[VMEM] * (len(xs) + len(flags) + 3),
-        scratch_shapes=[pltpu.VMEM((rows, width), jnp.bfloat16)],
-        out_shape=jax.ShapeDtypeStruct((rows, hidden), jnp.bfloat16),
+    rows, (width, units) = shapes[0].shape[0], pair.shape
+    return pl.pallas_call(
+        functools.partial(front_kernel, layout, order, flips, section, router.shape[0]),
+        in_specs=[VMEM] * (len(xs) + 3 + len(extra)),
+        out_shape=shapes,
         compiler_params=params(),
         cost_estimate=pl.CostEstimate(
-            flops=4 * rows * width * hidden, bytes_accessed=4 * width * hidden, transcendentals=0
+            flops=rows * width * units, bytes_accessed=width * units, transcendentals=0
         ),
         name="front",
-    )(*xs, *flags, mod, router, pair)
+    )(*xs, mod, router, pair, *extra)
+
+
+def front(blocks, flags, order, section, mod, router, pair):
+    rows = sum(f.shape[0] for f in flags)
+    units, experts = pair.shape[1], router.shape[0]
+    width = pair.shape[0]
+    common = (order, section, mod, router, pair)
+    here = [[p for p in block if p[1] == width or p[2] & 1 == 0] for block in blocks]
+    there = [[p for p in block if p[1] == width or p[2] & 1] for block in blocks]
+    shapes = [jax.ShapeDtypeStruct(s, jnp.float32) for s in ((rows + 8, units), (rows + 8, experts), (rows, 1))]
+    sums = half_front(here, (0, 2), [], shapes, *common)
+    shapes = [jax.ShapeDtypeStruct((rows, units // 2), jnp.bfloat16)]
+    return half_front(there, (1, 3), [flags[k] for k in order] + list(sums), shapes, *common)[0]
 
 
 def down_kernel(flip, n_adds, hidden_ref, down_ref, *refs):
@@ -401,11 +420,11 @@
 
     *packed, own = pack(tokens, ids, experts, slots)
     pair, w_down, done = load(gate_weight, up_weight, down_weight)
-    mine, flags, *choice = own_rows(tokens, ids, experts, slots)
+    mine, flags, *choice = own_rows(tokens, ids, experts, slots, done)
     pick, back = choice[2], choice[1::2]
     order = [*range(2, len(packed) + 1), 1]
     came = {k: swap(packed[k - 1], "ep", k) for k in order}
-    halves = {k: relay(came[k], half, done) for k in order}
+    halves = {k: relay(came[k], half, flags) for k in order}
     others = {k: swap(halves[k], "et", 1) for k in order}
     flags = [flags] + [came[k] for k in sorted(order)]
     blocks = [[(mine, width, 0)]] + [[(halves[k], half, 0), (others[k], half, 1)] for k in sorted(order)]

time: 67.5 us -> 65.5 us (0.970)
  waiting for transfers between devices: 23.7 us -> 22.2 us
    ppermute x35, waiting for transfers between devices: 23.7 us -> 22.2 us  [swap(): return lax.ppermute(x, axis, [(i, i ^ bit) for i in range(size)])]
    pallas_call x2 -> x4, Pallas kernels: 3.8 us -> 3.34 us  [half_front(): pl.pallas_call(functools.partial(front_kernel, layout, order, flips, sect...]
  transfers between devices with their start and end apart: 35 -> 35, of which waited for: 19 -> 18; matrix products, arithmetic and copies ran while one was open for 0% -> 0% of each run, Pallas kernels for 10% -> 12%
where the time goes in v12:
time: 65.5 us; the launch traced here: 65.4 us
  starting transfers between devices  29.6 us (45%)
  waiting for transfers between devices  22.2 us (34%)
  Pallas kernels  12.7 us (19%)
  between operations  0.88 us (1%)
    ppermute x35, starting transfers between devices, swap(): return lax.ppermute(x, axis, [(i, i ^ bit) for i in range(size)])  29.6 us
    ppermute x35, waiting for transfers between devices, swap(): return lax.ppermute(x, axis, [(i, i ^ bit) for i in range(size)])  22.2 us
    pallas_call x1, Pallas kernels, load(): pl.pallas_call(load_kernel, in_specs=[ANY] * 3, out_specs=[VMEM] * 3, out...  3.78 us
    pallas_call x4, Pallas kernels, half_front(): pl.pallas_call(functools.partial(front_kernel, layout, order, flips, sect...  3.34 us
    pallas_call x8, Pallas kernels, down(): pl.pallas_call(functools.partial(down_kernel, flip, len(adds)), in_specs=...  2.24 us
  transfers between devices with their start and end apart: 35, of which 18 were waited for; matrix products, arithmetic and copies ran while one was open for 0% of the time, Pallas kernels for 12%

profile of v12, /device:TPU:0, one launch (start us, length us, event | category | flops | bytes accessed | tf_op | source)
XLA Modules:
  0.0 65.4 jit_solution(11375208660847769421)
XLA Ops:
  0.6 1.2 %pack.1 = (bf16[24,2176]{1,0:T(8,128)(2,1)S(1)}, bf16[24,2176]{1,0:T(8,128)(2,1)S(1)}, bf16[24,2176]{1,0:T(8,128)(2,1)S(1)}, bf16[32,1024]{1,0:T(8,128)(2,1)S(1)}) custom-call(bf16[32,4096]{1,0:T(8,128)(2,1)} %tokens_ref.3, s32[2,2,32]{2,1,0:T(2,128)} %bitcast.6), custom_call_target="tpu_custom_call" | custom-call | tf_op jit(solution)/shard_map/pack/pallas_call | solution.py:197
  1.9 4.1 %collective-permute-start = (bf16[24,2176]{1,0:T(8,128)(2,1)S(1)}, bf16[24,2176]{1,0:T(8,128)(2,1)S(1)}, u32[]{:S(2)}, u32[]{:S(2)}) collective-permute-start(bf16[24,2176]{1,0:T(8,128)(2,1)S(1)} %get-tuple-element.45), channel_id=1, source_target_pairs={{0,8},{4,12},{8,0},{12,4},{1,9},{5,13},{9,1},{13,5},{2,10},{6,14},... | collective-permute-start | bytes 313352 | tf_op jit(solution)/shard_map/ppermute | solution.py:66
  6.0 1.3 %collective-permute-start.2 = (bf16[24,2176]{1,0:T(8,128)(2,1)S(1)}, bf16[24,2176]{1,0:T(8,128)(2,1)S(1)}, u32[]{:S(2)}, u32[]{:S(2)}) collective-permute-start(bf16[24,2176]{1,0:T(8,128)(2,1)S(1)} %get-tuple-element.47), channel_id=1, source_target_pairs={{0,12},{4,8},{8,4},{12,0},{1,13},{5,9},{9,5},{13,1},{2,14},{6,10},... | collective-permute-start | bytes 313352 | tf_op jit(solution)/shard_map/ppermute | solution.py:66
  7.6 3.8 %load.1 = (bf16[4096,768]{1,0:T(8,128)(2,1)S(1)}, bf16[384,4096]{1,0:T(8,128)(2,1)S(1)}, f32[8,128]{1,0:T(8,128)S(1)}) custom-call(bf16[1,4096,384]{2,1,0:T(8,128)(2,1)} %gate_ref.1, bf16[1,4096,384]{2,1,0:T(8,128)(2,1)} %up_ref.1, bf16[1,384,4096]{2,1,0:T(8,128)(2,1)} %down_ref.1), custom_call_target="tpu_custom_call" | custom-call | bytes 18874368 | tf_op jit(solution)/shard_map/load/pallas_call | solution.py:101
  12.2 2.0 %collective-permute-done.block_ref.refs_7_.refs_11_ = bf16[24,2176]{1,0:T(8,128)(2,1)S(1)} collective-permute-done((bf16[24,2176]{1,0:T(8,128)(2,1)S(1)}, bf16[24,2176]{1,0:T(8,128)(2,1)S(1)}, u32[]{:S(2)}, u32[]{:S(2)}) %collective-permute-start) | collective-permute-done | bytes 104480 | tf_op jit(solution)/shard_map/ppermute | solution.py:66
  19.0 1.9 %collective-permute-start.10 = (bf16[48,1024]{1,0:T(8,128)(2,1)S(1)}, bf16[48,1024]{1,0:T(8,128)(2,1)S(1)}, u32[]{:S(2)}, u32[]{:S(2)}) collective-permute-start(bf16[48,1024]{1,0:T(8,128)(2,1)S(1)} %get-tuple-element.60), channel_id=1, source_target_pairs={{0,2},{1,3},{2,0},{3,1},{4,6},{5,7},{6,4},{7,5},{8,10},{9,11},{10,... | collective-permute-start | bytes 294920 | tf_op jit(solution)/shard_map/ppermute | solution.py:66
  21.4 3.3 %collective-permute-done.10.came_ref = bf16[48,1024]{1,0:T(8,128)(2,1)S(1)} collective-permute-done((bf16[48,1024]{1,0:T(8,128)(2,1)S(1)}, bf16[48,1024]{1,0:T(8,128)(2,1)S(1)}, u32[]{:S(2)}, u32[]{:S(2)}) %collective-permute-start.10) | collective-permute-done | bytes 98336 | tf_op jit(solution)/shard_map/ppermute | solution.py:66
  24.7 3.7 %collective-permute-start.11 = (bf16[24,1024]{1,0:T(8,128)(2,1)S(1)}, bf16[24,1024]{1,0:T(8,128)(2,1)S(1)}, u32[]{:S(2)}, u32[]{:S(2)}) collective-permute-start(bf16[24,1024]{1,0:T(8,128)(2,1)S(1)} %get-tuple-element.61), channel_id=1, source_target_pairs={{0,8},{4,12},{8,0},{12,4},{1,9},{5,13},{9,1},{13,5},{2,10},{6,14},... | collective-permute-start | bytes 147464 | tf_op jit(solution)/shard_map/ppermute | solution.py:66
  29.1 1.9 %collective-permute-done.11.refs_2_ = bf16[24,1024]{1,0:T(8,128)(2,1)S(1)} collective-permute-done((bf16[24,1024]{1,0:T(8,128)(2,1)S(1)}, bf16[24,1024]{1,0:T(8,128)(2,1)S(1)}, u32[]{:S(2)}, u32[]{:S(2)}) %collective-permute-start.11) | collective-permute-done | bytes 49184 | tf_op jit(solution)/shard_map/ppermute | solution.py:66
  31.0 3.3 %collective-permute-done.12.refs_3_ = bf16[24,1024]{1,0:T(8,128)(2,1)S(1)} collective-permute-done((bf16[24,1024]{1,0:T(8,128)(2,1)S(1)}, bf16[24,1024]{1,0:T(8,128)(2,1)S(1)}, u32[]{:S(2)}, u32[]{:S(2)}) %collective-permute-start.12) | collective-permute-done | bytes 49184 | tf_op jit(solution)/shard_map/ppermute | solution.py:66
  34.6 1.2 %collective-permute-start.13 = (bf16[24,1024]{1,0:T(8,128)(2,1)S(1)}, bf16[24,1024]{1,0:T(8,128)(2,1)S(1)}, u32[]{:S(2)}, u32[]{:S(2)}) collective-permute-start(bf16[24,1024]{1,0:T(8,128)(2,1)S(1)} %get-tuple-element.65), channel_id=1, source_target_pairs={{0,8},{4,12},{8,0},{12,4},{1,9},{5,13},{9,1},{13,5},{2,10},{6,14},... | collective-permute-start | bytes 147464 | tf_op jit(solution)/shard_map/ppermute | solution.py:66
  35.8 1.1 %collective-permute-start.17 = (bf16[24,1024]{1,0:T(8,128)(2,1)S(1)}, bf16[24,1024]{1,0:T(8,128)(2,1)S(1)}, u32[]{:S(2)}, u32[]{:S(2)}) collective-permute-start(bf16[24,1024]{1,0:T(8,128)(2,1)S(1)} %get-tuple-element.66), channel_id=1, source_target_pairs={{0,12},{4,8},{8,4},{12,0},{1,13},{5,9},{9,5},{13,1},{2,14},{6,10},... | collective-permute-start | bytes 147464 | tf_op jit(solution)/shard_map/ppermute | solution.py:66
  36.9 1.3 %collective-permute-start.21 = (bf16[24,1024]{1,0:T(8,128)(2,1)S(1)}, bf16[24,1024]{1,0:T(8,128)(2,1)S(1)}, u32[]{:S(2)}, u32[]{:S(2)}) collective-permute-start(bf16[24,1024]{1,0:T(8,128)(2,1)S(1)} %get-tuple-element.67), channel_id=1, source_target_pairs={{0,4},{4,0},{8,12},{12,8},{1,5},{5,1},{9,13},{13,9},{2,6},{6,2},{1... | collective-permute-start | bytes 147464 | tf_op jit(solution)/shard_map/ppermute | solution.py:66
  38.2 1.5 %collective-permute-start.26 = (bf16[24,1024]{1,0:T(8,128)(2,1)S(1)}, bf16[24,1024]{1,0:T(8,128)(2,1)S(1)}, u32[]{:S(2)}, u32[]{:S(2)}) collective-permute-start(bf16[24,1024]{1,0:T(8,128)(2,1)S(1)} %get-tuple-element.68.refs_6_), channel_id=1, source_target_pairs={{0,2},{1,3},{2,0},{3,1},{4,6},{5,7},{6,4},{7,5},{8,10},{9,11},{10,... | collective-permute-start | bytes 147464 | tf_op jit(solution)/shard_map/ppermute | solution.py:66
  39.8 1.5 %collective-permute-start.15 = (bf16[24,1024]{1,0:T(8,128)(2,1)S(1)}, bf16[24,1024]{1,0:T(8,128)(2,1)S(1)}, u32[]{:S(2)}, u32[]{:S(2)}) collective-permute-start(bf16[24,1024]{1,0:T(8,128)(2,1)S(1)} %collective-permute-done.13.refs_0_), channel_id=1, source_target_pairs={{0,2},{1,3},{2,0},{3,1},{4,6},{5,7},{6,4},{7,5},{8,10},{9,11},{10,... | collective-permute-start | bytes 147464 | tf_op jit(solution)/shard_map/ppermute | solution.py:66
  41.7 1.5 %collective-permute-start.19 = (bf16[24,1024]{1,0:T(8,128)(2,1)S(1)}, bf16[24,1024]{1,0:T(8,128)(2,1)S(1)}, u32[]{:S(2)}, u32[]{:S(2)}) collective-permute-start(bf16[24,1024]{1,0:T(8,128)(2,1)S(1)} %collective-permute-done.17.refs_2_), channel_id=1, source_target_pairs={{0,2},{1,3},{2,0},{3,1},{4,6},{5,7},{6,4},{7,5},{8,10},{9,11},{10,... | collective-permute-start | bytes 147464 | tf_op jit(solution)/shard_map/ppermute | solution.py:66
  44.4 1.4 %collective-permute-done.19.refs_3_ = bf16[24,1024]{1,0:T(8,128)(2,1)S(1)} collective-permute-done((bf16[24,1024]{1,0:T(8,128)(2,1)S(1)}, bf16[24,1024]{1,0:T(8,128)(2,1)S(1)}, u32[]{:S(2)}, u32[]{:S(2)}) %collective-permute-start.19) | collective-permute-done | bytes 49184 | tf_op jit(solution)/shard_map/ppermute | solution.py:66
  45.8 1.5 %collective-permute-done.23.refs_5_ = bf16[24,1024]{1,0:T(8,128)(2,1)S(1)} collective-permute-done((bf16[24,1024]{1,0:T(8,128)(2,1)S(1)}, bf16[24,1024]{1,0:T(8,128)(2,1)S(1)}, u32[]{:S(2)}, u32[]{:S(2)}) %collective-permute-start.23) | collective-permute-done | bytes 49184 | tf_op jit(solution)/shard_map/ppermute | solution.py:66
  52.5 1.5 %collective-permute-start.30 = (bf16[48,1024]{1,0:T(8,128)(2,1)S(1)}, bf16[48,1024]{1,0:T(8,128)(2,1)S(1)}, u32[]{:S(2)}, u32[]{:S(2)}) collective-permute-start(bf16[48,1024]{1,0:T(8,128)(2,1)S(1)} %get-tuple-element.73), channel_id=1, source_target_pairs={{0,2},{1,3},{2,0},{3,1},{4,6},{5,7},{6,4},{7,5},{8,10},{9,11},{10,... | collective-permute-start | bytes 294920 | tf_op jit(solution)/shard_map/ppermute | solution.py:66
  54.2 3.3 %collective-permute-done.32.came_ref = bf16[48,1024]{1,0:T(8,128)(2,1)S(1)} collective-permute-done((bf16[48,1024]{1,0:T(8,128)(2,1)S(1)}, bf16[48,1024]{1,0:T(8,128)(2,1)S(1)}, u32[]{:S(2)}, u32[]{:S(2)}) %collective-permute-start.32) | collective-permute-done | bytes 98336 | tf_op jit(solution)/shard_map/ppermute | solution.py:66
  58.3 1.5 %collective-permute-start.34 = (bf16[24,1024]{1,0:T(8,128)(2,1)S(1)}, bf16[24,1024]{1,0:T(8,128)(2,1)S(1)}, u32[]{:S(2)}, u32[]{:S(2)}) collective-permute-start(bf16[24,1024]{1,0:T(8,128)(2,1)S(1)} %get-tuple-element.79), channel_id=1, source_target_pairs={{0,12},{4,8},{8,4},{12,0},{1,13},{5,9},{9,5},{13,1},{2,14},{6,10},... | collective-permute-start | bytes 147464 | tf_op jit(solution)/shard_map/ppermute | solution.py:66
  59.9 1.4 %collective-permute-start.31 = (bf16[24,1024]{1,0:T(8,128)(2,1)S(1)}, bf16[24,1024]{1,0:T(8,128)(2,1)S(1)}, u32[]{:S(2)}, u32[]{:S(2)}) collective-permute-start(bf16[24,1024]{1,0:T(8,128)(2,1)S(1)} %get-tuple-element.75), channel_id=1, source_target_pairs={{0,4},{4,0},{8,12},{12,8},{1,5},{5,1},{9,13},{13,9},{2,6},{6,2},{1... | collective-permute-start | bytes 147464 | tf_op jit(solution)/shard_map/ppermute | solution.py:66
  61.2 1.5 %collective-permute-done.33.refs_2_ = bf16[24,1024]{1,0:T(8,128)(2,1)S(1)} collective-permute-done((bf16[24,1024]{1,0:T(8,128)(2,1)S(1)}, bf16[24,1024]{1,0:T(8,128)(2,1)S(1)}, u32[]{:S(2)}, u32[]{:S(2)}) %collective-permute-start.33) | collective-permute-done | bytes 49184 | tf_op jit(solution)/shard_map/ppermute | solution.py:66
  62.8 1.5 %collective-permute-done.34.refs_3_ = bf16[24,1024]{1,0:T(8,128)(2,1)S(1)} collective-permute-done((bf16[24,1024]{1,0:T(8,128)(2,1)S(1)}, bf16[24,1024]{1,0:T(8,128)(2,1)S(1)}, u32[]{:S(2)}, u32[]{:S(2)}) %collective-permute-start.34) | collective-permute-done | bytes 49184 | tf_op jit(solution)/shard_map/ppermute | solution.py:66
  (80 shorter events, 16.4 us)
Async XLA Ops:
  1.9 12.4 %collective-permute-start = (bf16[24,2176]{1,0:T(8,128)(2,1)S(1)}, bf16[24,2176]{1,0:T(8,128)(2,1)S(1)}, u32[]{:S(2)}, u32[]{:S(2)}) collective-permute-start(bf16[24,2176]{1,0:T(8,128)(2,1)S(1)} %get-tuple-element.45), channel_id=1, source_target_pairs={{0,8},{4,12},{8,0},{12,4},{1,9},{5,13},{9,1},{13,5},{2,10},{6,14},... | collective-permute-start | bytes 313352 | tf_op jit(solution)/shard_map/ppermute | solution.py:66
  6.0 8.4 %collective-permute-start.2 = (bf16[24,2176]{1,0:T(8,128)(2,1)S(1)}, bf16[24,2176]{1,0:T(8,128)(2,1)S(1)}, u32[]{:S(2)}, u32[]{:S(2)}) collective-permute-start(bf16[24,2176]{1,0:T(8,128)(2,1)S(1)} %get-tuple-element.47), channel_id=1, source_target_pairs={{0,12},{4,8},{8,4},{12,0},{1,13},{5,9},{9,5},{13,1},{2,14},{6,10},... | collective-permute-start | bytes 313352 | tf_op jit(solution)/shard_map/ppermute | solution.py:66
  7.3 7.6 %collective-permute-start.4 = (bf16[24,2176]{1,0:T(8,128)(2,1)S(1)}, bf16[24,2176]{1,0:T(8,128)(2,1)S(1)}, u32[]{:S(2)}, u32[]{:S(2)}) collective-permute-start(bf16[24,2176]{1,0:T(8,128)(2,1)S(1)} %get-tuple-element.48), channel_id=1, source_target_pairs={{0,4},{4,0},{8,12},{12,8},{1,5},{5,1},{9,13},{13,9},{2,6},{6,2},{1... | collective-permute-start | bytes 313352 | tf_op jit(solution)/shard_map/ppermute | solution.py:66
  19.0 5.7 %collective-permute-start.10 = (bf16[48,1024]{1,0:T(8,128)(2,1)S(1)}, bf16[48,1024]{1,0:T(8,128)(2,1)S(1)}, u32[]{:S(2)}, u32[]{:S(2)}) collective-permute-start(bf16[48,1024]{1,0:T(8,128)(2,1)S(1)} %get-tuple-element.60), channel_id=1, source_target_pairs={{0,2},{1,3},{2,0},{3,1},{4,6},{5,7},{6,4},{7,5},{8,10},{9,11},{10,... | collective-permute-start | bytes 294920 | tf_op jit(solution)/shard_map/ppermute | solution.py:66
  20.9 7.9 %collective-permute-start.8 = (bf16[48,1024]{1,0:T(8,128)(2,1)S(1)}, bf16[48,1024]{1,0:T(8,128)(2,1)S(1)}, u32[]{:S(2)}, u32[]{:S(2)}) collective-permute-start(bf16[48,1024]{1,0:T(8,128)(2,1)S(1)} %get-tuple-element.56), channel_id=1, source_target_pairs={{0,2},{1,3},{2,0},{3,1},{4,6},{5,7},{6,4},{7,5},{8,10},{9,11},{10,... | collective-permute-start | bytes 294920 | tf_op jit(solution)/shard_map/ppermute | solution.py:66
  24.7 6.3 %collective-permute-start.11 = (bf16[24,1024]{1,0:T(8,128)(2,1)S(1)}, bf16[24,1024]{1,0:T(8,128)(2,1)S(1)}, u32[]{:S(2)}, u32[]{:S(2)}) collective-permute-start(bf16[24,1024]{1,0:T(8,128)(2,1)S(1)} %get-tuple-element.61), channel_id=1, source_target_pairs={{0,8},{4,12},{8,0},{12,4},{1,9},{5,13},{9,1},{13,5},{2,10},{6,14},... | collective-permute-start | bytes 147464 | tf_op jit(solution)/shard_map/ppermute | solution.py:66
  28.4 5.9 %collective-permute-start.12 = (bf16[24,1024]{1,0:T(8,128)(2,1)S(1)}, bf16[24,1024]{1,0:T(8,128)(2,1)S(1)}, u32[]{:S(2)}, u32[]{:S(2)}) collective-permute-start(bf16[24,1024]{1,0:T(8,128)(2,1)S(1)} %get-tuple-element.62), channel_id=1, source_target_pairs={{0,12},{4,8},{8,4},{12,0},{1,13},{5,9},{9,5},{13,1},{2,14},{6,10},... | collective-permute-start | bytes 147464 | tf_op jit(solution)/shard_map/ppermute | solution.py:66
  28.8 5.5 %collective-permute-start.9 = (bf16[24,1024]{1,0:T(8,128)(2,1)S(1)}, bf16[24,1024]{1,0:T(8,128)(2,1)S(1)}, u32[]{:S(2)}, u32[]{:S(2)}) collective-permute-start(bf16[24,1024]{1,0:T(8,128)(2,1)S(1)} %get-tuple-element.58), channel_id=1, source_target_pairs={{0,4},{4,0},{8,12},{12,8},{1,5},{5,1},{9,13},{13,9},{2,6},{6,2},{1... | collective-permute-start | bytes 147464 | tf_op jit(solution)/shard_map/ppermute | solution.py:66
  34.6 5.2 %collective-permute-start.13 = (bf16[24,1024]{1,0:T(8,128)(2,1)S(1)}, bf16[24,1024]{1,0:T(8,128)(2,1)S(1)}, u32[]{:S(2)}, u32[]{:S(2)}) collective-permute-start(bf16[24,1024]{1,0:T(8,128)(2,1)S(1)} %get-tuple-element.65), channel_id=1, source_target_pairs={{0,8},{4,12},{8,0},{12,4},{1,9},{5,13},{9,1},{13,5},{2,10},{6,14},... | collective-permute-start | bytes 147464 | tf_op jit(solution)/shard_map/ppermute | solution.py:66
  35.8 5.9 %collective-permute-start.17 = (bf16[24,1024]{1,0:T(8,128)(2,1)S(1)}, bf16[24,1024]{1,0:T(8,128)(2,1)S(1)}, u32[]{:S(2)}, u32[]{:S(2)}) collective-permute-start(bf16[24,1024]{1,0:T(8,128)(2,1)S(1)} %get-tuple-element.66), channel_id=1, source_target_pairs={{0,12},{4,8},{8,4},{12,0},{1,13},{5,9},{9,5},{13,1},{2,14},{6,10},... | collective-permute-start | bytes 147464 | tf_op jit(solution)/shard_map/ppermute | solution.py:66
  36.9 6.3 %collective-permute-start.21 = (bf16[24,1024]{1,0:T(8,128)(2,1)S(1)}, bf16[24,1024]{1,0:T(8,128)(2,1)S(1)}, u32[]{:S(2)}, u32[]{:S(2)}) collective-permute-start(bf16[24,1024]{1,0:T(8,128)(2,1)S(1)} %get-tuple-element.67), channel_id=1, source_target_pairs={{0,4},{4,0},{8,12},{12,8},{1,5},{5,1},{9,13},{13,9},{2,6},{6,2},{1... | collective-permute-start | bytes 147464 | tf_op jit(solution)/shard_map/ppermute | solution.py:66
  38.2 5.5 %collective-permute-start.26 = (bf16[24,1024]{1,0:T(8,128)(2,1)S(1)}, bf16[24,1024]{1,0:T(8,128)(2,1)S(1)}, u32[]{:S(2)}, u32[]{:S(2)}) collective-permute-start(bf16[24,1024]{1,0:T(8,128)(2,1)S(1)} %get-tuple-element.68.refs_6_), channel_id=1, source_target_pairs={{0,2},{1,3},{2,0},{3,1},{4,6},{5,7},{6,4},{7,5},{8,10},{9,11},{10,... | collective-permute-start | bytes 147464 | tf_op jit(solution)/shard_map/ppermute | solution.py:66
  39.7 4.0 %collective-permute-start.25 = (bf16[24,1024]{1,0:T(8,128)(2,1)S(1)}, bf16[24,1024]{1,0:T(8,128)(2,1)S(1)}, u32[]{:S(2)}, u32[]{:S(2)}) collective-permute-start(bf16[24,1024]{1,0:T(8,128)(2,1)S(1)} %get-tuple-element.68.refs_6_), channel_id=1, source_target_pairs={{0,1},{1,0},{2,3},{3,2},{4,5},{5,4},{6,7},{7,6},{8,9},{9,8},{10,11... | collective-permute-start | bytes 147464 | tf_op jit(solution)/shard_map/ppermute | solution.py:66
  39.8 4.6 %collective-permute-start.15 = (bf16[24,1024]{1,0:T(8,128)(2,1)S(1)}, bf16[24,1024]{1,0:T(8,128)(2,1)S(1)}, u32[]{:S(2)}, u32[]{:S(2)}) collective-permute-start(bf16[24,1024]{1,0:T(8,128)(2,1)S(1)} %collective-permute-done.13.refs_0_), channel_id=1, source_target_pairs={{0,2},{1,3},{2,0},{3,1},{4,6},{5,7},{6,4},{7,5},{8,10},{9,11},{10,... | collective-permute-start | bytes 147464 | tf_op jit(solution)/shard_map/ppermute | solution.py:66
  41.7 4.1 %collective-permute-start.19 = (bf16[24,1024]{1,0:T(8,128)(2,1)S(1)}, bf16[24,1024]{1,0:T(8,128)(2,1)S(1)}, u32[]{:S(2)}, u32[]{:S(2)}) collective-permute-start(bf16[24,1024]{1,0:T(8,128)(2,1)S(1)} %collective-permute-done.17.refs_2_), channel_id=1, source_target_pairs={{0,2},{1,3},{2,0},{3,1},{4,6},{5,7},{6,4},{7,5},{8,10},{9,11},{10,... | collective-permute-start | bytes 147464 | tf_op jit(solution)/shard_map/ppermute | solution.py:66
  43.1 4.1 %collective-permute-start.23 = (bf16[24,1024]{1,0:T(8,128)(2,1)S(1)}, bf16[24,1024]{1,0:T(8,128)(2,1)S(1)}, u32[]{:S(2)}, u32[]{:S(2)}) collective-permute-start(bf16[24,1024]{1,0:T(8,128)(2,1)S(1)} %collective-permute-done.21.refs_4_), channel_id=1, source_target_pairs={{0,2},{1,3},{2,0},{3,1},{4,6},{5,7},{6,4},{7,5},{8,10},{9,11},{10,... | collective-permute-start | bytes 147464 | tf_op jit(solution)/shard_map/ppermute | solution.py:66
  43.7 3.5 %collective-permute-start.14 = (bf16[24,1024]{1,0:T(8,128)(2,1)S(1)}, bf16[24,1024]{1,0:T(8,128)(2,1)S(1)}, u32[]{:S(2)}, u32[]{:S(2)}) collective-permute-start(bf16[24,1024]{1,0:T(8,128)(2,1)S(1)} %collective-permute-done.13.refs_0_), channel_id=1, source_target_pairs={{0,1},{1,0},{2,3},{3,2},{4,5},{5,4},{6,7},{7,6},{8,9},{9,8},{10,11... | collective-permute-start | bytes 147464 | tf_op jit(solution)/shard_map/ppermute | solution.py:66
  43.7 4.0 %collective-permute-start.18 = (bf16[24,1024]{1,0:T(8,128)(2,1)S(1)}, bf16[24,1024]{1,0:T(8,128)(2,1)S(1)}, u32[]{:S(2)}, u32[]{:S(2)}) collective-permute-start(bf16[24,1024]{1,0:T(8,128)(2,1)S(1)} %collective-permute-done.17.refs_2_), channel_id=1, source_target_pairs={{0,1},{1,0},{2,3},{3,2},{4,5},{5,4},{6,7},{7,6},{8,9},{9,8},{10,11... | collective-permute-start | bytes 147464 | tf_op jit(solution)/shard_map/ppermute | solution.py:66
  44.4 4.2 %collective-permute-start.22 = (bf16[24,1024]{1,0:T(8,128)(2,1)S(1)}, bf16[24,1024]{1,0:T(8,128)(2,1)S(1)}, u32[]{:S(2)}, u32[]{:S(2)}) collective-permute-start(bf16[24,1024]{1,0:T(8,128)(2,1)S(1)} %collective-permute-done.21.refs_4_), channel_id=1, source_target_pairs={{0,1},{1,0},{2,3},{3,2},{4,5},{5,4},{6,7},{7,6},{8,9},{9,8},{10,11... | collective-permute-start | bytes 147464 | tf_op jit(solution)/shard_map/ppermute | solution.py:66
  51.9 5.7 %collective-permute-start.32 = (bf16[48,1024]{1,0:T(8,128)(2,1)S(1)}, bf16[48,1024]{1,0:T(8,128)(2,1)S(1)}, u32[]{:S(2)}, u32[]{:S(2)}) collective-permute-start(bf16[48,1024]{1,0:T(8,128)(2,1)S(1)} %get-tuple-element.77), channel_id=1, source_target_pairs={{0,2},{1,3},{2,0},{3,1},{4,6},{5,7},{6,4},{7,5},{8,10},{9,11},{10,... | collective-permute-start | bytes 294920 | tf_op jit(solution)/shard_map/ppermute | solution.py:66
  52.5 7.3 %collective-permute-start.30 = (bf16[48,1024]{1,0:T(8,128)(2,1)S(1)}, bf16[48,1024]{1,0:T(8,128)(2,1)S(1)}, u32[]{:S(2)}, u32[]{:S(2)}) collective-permute-start(bf16[48,1024]{1,0:T(8,128)(2,1)S(1)} %get-tuple-element.73), channel_id=1, source_target_pairs={{0,2},{1,3},{2,0},{3,1},{4,6},{5,7},{6,4},{7,5},{8,10},{9,11},{10,... | collective-permute-start | bytes 294920 | tf_op jit(solution)/shard_map/ppermute | solution.py:66
  57.6 5.2 %collective-permute-start.33 = (bf16[24,1024]{1,0:T(8,128)(2,1)S(1)}, bf16[24,1024]{1,0:T(8,128)(2,1)S(1)}, u32[]{:S(2)}, u32[]{:S(2)}) collective-permute-start(bf16[24,1024]{1,0:T(8,128)(2,1)S(1)} %get-tuple-element.78), channel_id=1, source_target_pairs={{0,8},{4,12},{8,0},{12,4},{1,9},{5,13},{9,1},{13,5},{2,10},{6,14},... | collective-permute-start | bytes 147464 | tf_op jit(solution)/shard_map/ppermute | solution.py:66
  58.3 6.0 %collective-permute-start.34 = (bf16[24,1024]{1,0:T(8,128)(2,1)S(1)}, bf16[24,1024]{1,0:T(8,128)(2,1)S(1)}, u32[]{:S(2)}, u32[]{:S(2)}) collective-permute-start(bf16[24,1024]{1,0:T(8,128)(2,1)S(1)} %get-tuple-element.79), channel_id=1, source_target_pairs={{0,12},{4,8},{8,4},{12,0},{1,13},{5,9},{9,5},{13,1},{2,14},{6,10},... | collective-permute-start | bytes 147464 | tf_op jit(solution)/shard_map/ppermute | solution.py:66
  59.9 4.7 %collective-permute-start.31 = (bf16[24,1024]{1,0:T(8,128)(2,1)S(1)}, bf16[24,1024]{1,0:T(8,128)(2,1)S(1)}, u32[]{:S(2)}, u32[]{:S(2)}) collective-permute-start(bf16[24,1024]{1,0:T(8,128)(2,1)S(1)} %get-tuple-element.75), channel_id=1, source_target_pairs={{0,4},{4,0},{8,12},{12,8},{1,5},{5,1},{9,13},{13,9},{2,6},{6,2},{1... | collective-permute-start | bytes 147464 | tf_op jit(solution)/shard_map/ppermute | solution.py:66
  (15 other events, 44.1 us)

commit v13 on v12

--- a/solution.py
+++ b/solution.py
@@ -69,6 +69,7 @@
 LANES = 128
 VMEM_LIMIT = 32 * 1024 * 1024
 VMEM_MOST = 52 * 1024 * 1024
+VMEM_REST = 48 * 1024 * 1024
 VMEM_ALL = 63 * 1024 * 1024
 VMEM = pl.BlockSpec(memory_space=pltpu.VMEM)
 ANY = pl.BlockSpec(memory_space=pl.ANY)
@@ -82,13 +83,13 @@
     return pl.ds(pl.multiple_of(index * size, size), size)
 
 
-def load_kernel(gate_ref, up_ref, down_ref, pair_ref, out_ref, done_ref, sems):
-    hidden = gate_ref.shape[2]
-    copies = [
-        pltpu.make_async_copy(gate_ref.at[0], pair_ref.at[:, :hidden], sems.at[0]),
-        pltpu.make_async_copy(up_ref.at[0], pair_ref.at[:, hidden:], sems.at[1]),
-        pltpu.make_async_copy(down_ref.at[0], out_ref, sems.at[2]),
-    ]
+def load_kernel(n, *refs):
+    in_refs, (out_ref, done_ref, sems) = refs[:n], refs[-3:]
+    cols = out_ref.shape[1] // n
+    copies = []
+    for i, ref in enumerate(in_refs):
+        to = out_ref.at[:, i * cols : (i + 1) * cols]
+        copies.append(pltpu.make_async_copy(ref.at[0], to, sems.at[i]))
     for copy in copies:
         copy.start()
     for copy in copies:
@@ -96,22 +97,19 @@
     done_ref[...] = jnp.zeros_like(done_ref)
 
 
-def load(gate, up, down):
-    _, width, hidden = gate.shape
-    return pl.pallas_call(
-        load_kernel,
-        in_specs=[ANY] * 3,
-        out_specs=[VMEM] * 3,
-        out_shape=[
-            pltpu.VMEM((width, 2 * hidden), jnp.bfloat16),
-            pltpu.VMEM((hidden, width), jnp.bfloat16),
-            pltpu.VMEM((8, LANES), jnp.float32),
-        ],
-        scratch_shapes=[pltpu.SemaphoreType.DMA((3,))],
-        compiler_params=params(VMEM_MOST),
-        cost_estimate=pl.CostEstimate(flops=0, bytes_accessed=12 * width * hidden, transcendentals=0),
+def load(*weights, after=()):
+    _, rows, cols = weights[0].shape
+    n = len(weights)
+    return pl.pallas_call(
+        functools.partial(load_kernel, n),
+        in_specs=[ANY] * n + [VMEM] * len(after),
+        out_specs=[VMEM] * 2,
+        out_shape=[pltpu.VMEM((rows, n * cols), jnp.bfloat16), pltpu.VMEM((8, LANES), jnp.float32)],
+        scratch_shapes=[pltpu.SemaphoreType.DMA((n,))],
+        compiler_params=params(VMEM_MOST if n > 1 else VMEM_REST),
+        cost_estimate=pl.CostEstimate(flops=0, bytes_accessed=4 * n * rows * cols, transcendentals=0),
         name="load",
-    )(gate, up, down)
+    )(*weights, *after)
 
 
 def relay_kernel(block_ref, done_ref, out_ref):
@@ -162,6 +160,9 @@
         hits = [jnp.where(one[p : p + 1, :] + s * experts == lane, 1.0, 0.0) for p in range(one.shape[0])]
         flags.append(product(held[s], sum(hits).T))
     return sum(flags)
+
+
+CROSSING = 3
 
 
 def pack_kernel(experts, tokens_ref, ids_ref, *refs):
@@ -186,14 +187,18 @@
     own_ref[...] = half_ref[:, aligned(where >> 1, quarter)]
     picked = product(held[0][slots:], half_ref[...])
     for k, out_ref in enumerate(out_refs):
-        out_ref[:, :half] = narrow(picked[k * slots : (k + 1) * slots])
-        out_ref[:, half:] = narrow(flags[(k + 1) * slots : (k + 2) * slots])
+        cols = out_ref.shape[1] - LANES
+        part = picked[k * slots : (k + 1) * slots]
+        if cols < half:
+            part = product(held[0][(k + 1) * slots : (k + 2) * slots], own_ref[...])
+        out_ref[:, :cols] = narrow(part)
+        out_ref[:, cols:] = narrow(flags[(k + 1) * slots : (k + 2) * slots])
 
 
 def pack(tokens, ids, experts, slots):
     rows, width = tokens.shape
-    others = lax.axis_size("ep") - 1
-    shapes = [(slots, width // 2 + LANES)] * others + [(rows, width // 4)]
+    parts = [4 if k == CROSSING else 2 for k in range(1, lax.axis_size("ep"))]
+    shapes = [(slots, width // part + LANES) for part in parts] + [(rows, width // 4)]
     return pl.pallas_call(
         functools.partial(pack_kernel, experts),
         in_specs=[ANY] * 2,
@@ -419,20 +424,25 @@
     ids = expert_ids.transpose(0, 2, 1)
 
     *packed, own = pack(tokens, ids, experts, slots)
-    pair, w_down, done = load(gate_weight, up_weight, down_weight)
-    mine, flags, *choice = own_rows(tokens, ids, experts, slots, done)
+    pair, pair_done = load(gate_weight, up_weight)
+    order = [*range(1, len(packed) + 1)]
+    came = {k: swap(packed[k - 1], "ep", k) for k in order}
+    crossing = relay(came[CROSSING], quarter, pair_done)
+    w_down, down_done = load(down_weight, after=(crossing,))
+    mine, flags, *choice = own_rows(tokens, ids, experts, slots, down_done)
     pick, back = choice[2], choice[1::2]
-    order = [*range(2, len(packed) + 1), 1]
-    came = {k: swap(packed[k - 1], "ep", k) for k in order}
-    halves = {k: relay(came[k], half, flags) for k in order}
-    others = {k: swap(halves[k], "et", 1) for k in order}
+    pieces = {0: [(mine, width, 0)], CROSSING: spread(crossing, quarter)}
+    for k in order:
+        if k != CROSSING:
+            f = relay(came[k], half, flags)
+            pieces[k] = [(f, half, 0), (swap(f, "et", 1), half, 1)]
     flags = [flags] + [came[k] for k in sorted(order)]
-    blocks = [[(mine, width, 0)]] + [[(halves[k], half, 0), (others[k], half, 1)] for k in sorted(order)]
+    blocks = [pieces[k] for k in sorted(pieces)]
     hidden = front(blocks, flags, order + [0], 0, modulation, router, pair)
     own, *sent = sum_back(hidden, w_down, own, back[0], pick, False)
 
     blocks = [spread(swap(b, "ep", k) if k else b, quarter) for k, b in enumerate(sent)]
-    hidden = front(blocks, flags, order + [0], 1, modulation, router, pair)
+    hidden = front(blocks, flags, order[1:] + [1, 0], 1, modulation, router, pair)
     return tuple(sum_back(hidden, w_down, own, back[1], pick, True))
 
 
@@ -451,7 +461,7 @@
     def body(*args):
         experts, picks = args[2].shape[1], args[6].shape[2]
         peers = lax.axis_size("ep")
-        fits = lax.axis_size("et") == 4 and peers & (peers - 1) == 0
+        fits = lax.axis_size("et") == 4 and peers >= 4 and peers & (peers - 1) == 0
         chosen = dense_body if fits and experts <= 2 * picks else routed_body
         return chosen(*args)
 

time: 65.5 us -> 67.4 us (1.029)
  waiting for transfers between devices: 22.2 us -> 23.8 us
  Pallas kernels: 12.7 us -> 13.7 us
  starting transfers between devices: 29.6 us -> 28.8 us
    ppermute x35 -> x37, waiting for transfers between devices: 22.2 us -> 23.8 us  [swap(): return lax.ppermute(x, axis, [(i, i ^ bit) for i in range(size)])]
    pallas_call x1 -> x2, Pallas kernels: 3.78 us -> 4.76 us  [load(): pl.pallas_call(functools.partial(load_kernel, n), in_specs=[ANY] * n + [V...]
    ppermute x35 -> x37, starting transfers between devices: 29.6 us -> 28.8 us  [swap(): return lax.ppermute(x, axis, [(i, i ^ bit) for i in range(size)])]
  transfers between devices with their start and end apart: 35 -> 37, of which waited for: 18 -> 17; matrix products, arithmetic and copies ran while one was open for 0% -> 0% of each run, Pallas kernels for 12% -> 13%
where the time goes in v13:
time: 67.4 us; the launch traced here: 67.2 us
  starting transfers between devices  28.8 us (43%)
  waiting for transfers between devices  23.8 us (35%)
  Pallas kernels  13.7 us (20%)
  between operations  0.91 us (1%)
    ppermute x37, starting transfers between devices, swap(): return lax.ppermute(x, axis, [(i, i ^ bit) for i in range(size)])  28.8 us
    ppermute x37, waiting for transfers between devices, swap(): return lax.ppermute(x, axis, [(i, i ^ bit) for i in range(size)])  23.8 us
    pallas_call x2, Pallas kernels, load(): pl.pallas_call(functools.partial(load_kernel, n), in_specs=[ANY] * n + [V...  4.76 us
    pallas_call x4, Pallas kernels, half_front(): pl.pallas_call(functools.partial(front_kernel, layout, order, flips, sect...  3.31 us
    pallas_call x8, Pallas kernels, down(): pl.pallas_call(functools.partial(down_kernel, flip, len(adds)), in_specs=...  2.24 us
  transfers between devices with their start and end apart: 37, of which 17 were waited for; matrix products, arithmetic and copies ran while one was open for 0% of the time, Pallas kernels for 13%

profile of v13, /device:TPU:0, one launch (start us, length us, event | category | flops | bytes accessed | tf_op | source)
XLA Modules:
  0.0 67.2 jit_solution(11602523982124914688)
XLA Ops:
  0.6 1.2 %pack.1 = (bf16[24,2176]{1,0:T(8,128)(2,1)S(1)}, bf16[24,2176]{1,0:T(8,128)(2,1)S(1)}, bf16[24,1152]{1,0:T(8,128)(2,1)S(1)}, bf16[32,1024]{1,0:T(8,128)(2,1)S(1)}) custom-call(bf16[32,4096]{1,0:T(8,128)(2,1)} %tokens_ref.3, s32[2,2,32]{2,1,0:T(2,128)} %bitcast.6), custom_call_target="tpu_custom_call" | custom-call | tf_op jit(solution)/shard_map/pack/pallas_call | solution.py:202
  1.9 4.1 %collective-permute-start.3 = (bf16[24,2176]{1,0:T(8,128)(2,1)S(1)}, bf16[24,2176]{1,0:T(8,128)(2,1)S(1)}, u32[]{:S(2)}, u32[]{:S(2)}) collective-permute-start(bf16[24,2176]{1,0:T(8,128)(2,1)S(1)} %get-tuple-element.50), channel_id=1, source_target_pairs={{0,8},{4,12},{8,0},{12,4},{1,9},{5,13},{9,1},{13,5},{2,10},{6,14},... | collective-permute-start | bytes 313352 | tf_op jit(solution)/shard_map/ppermute | solution.py:66
  6.0 1.6 %collective-permute-start.1 = (bf16[24,2176]{1,0:T(8,128)(2,1)S(1)}, bf16[24,2176]{1,0:T(8,128)(2,1)S(1)}, u32[]{:S(2)}, u32[]{:S(2)}) collective-permute-start(bf16[24,2176]{1,0:T(8,128)(2,1)S(1)} %get-tuple-element.48), channel_id=1, source_target_pairs={{0,4},{4,0},{8,12},{12,8},{1,5},{5,1},{9,13},{13,9},{2,6},{6,2},{1... | collective-permute-start | bytes 313352 | tf_op jit(solution)/shard_map/ppermute | solution.py:66
  7.5 2.9 %load.2 = (bf16[4096,768]{1,0:T(8,128)(2,1)S(1)}, f32[8,128]{1,0:T(8,128)S(1)}) custom-call(bf16[1,4096,384]{2,1,0:T(8,128)(2,1)} %refs_0_.2, bf16[1,4096,384]{2,1,0:T(8,128)(2,1)} %refs_1_.1), custom_call_target="tpu_custom_call" | custom-call | bytes 12582912 | tf_op jit(solution)/shard_map/load/pallas_call | solution.py:103
  10.5 3.0 %collective-permute-done.block_ref.refs_10_.refs_12_ = bf16[24,1152]{1,0:T(8,128)(2,1)S(1)} collective-permute-done((bf16[24,1152]{1,0:T(8,128)(2,1)S(1)}, bf16[24,1152]{1,0:T(8,128)(2,1)S(1)}, u32[]{:S(2)}, u32[]{:S(2)}) %collective-permute-start) | collective-permute-done | bytes 55328 | tf_op jit(solution)/shard_map/ppermute | solution.py:66
  13.5 1.5 %collective-permute-start.6 = (bf16[24,1024]{1,0:T(8,128)(2,1)S(1)}, bf16[24,1024]{1,0:T(8,128)(2,1)S(1)}, u32[]{:S(2)}, u32[]{:S(2)}) collective-permute-start(bf16[24,1024]{1,0:T(8,128)(2,1)S(1)} %relay.3.refs_1_.refs_2_), channel_id=1, source_target_pairs={{0,2},{1,3},{2,0},{3,1},{4,6},{5,7},{6,4},{7,5},{8,10},{9,11},{10,... | collective-permute-start | bytes 147464 | tf_op jit(solution)/shard_map/ppermute | solution.py:66
  15.1 1.9 %load.3 = (bf16[384,4096]{1,0:T(8,128)(2,1)S(1)}, f32[8,128]{1,0:T(8,128)S(1)}) custom-call(bf16[1,384,4096]{2,1,0:T(8,128)(2,1)} %refs_0_.3, bf16[24,1024]{1,0:T(8,128)(2,1)S(1)} %relay.3.refs_1_.refs_2_), custom_call_target="tpu_custom_call" | custom-call | bytes 6291456 | tf_op jit(solution)/shard_map/load/pallas_call | solution.py:103
  23.2 1.5 %collective-permute-start.10 = (bf16[48,1024]{1,0:T(8,128)(2,1)S(1)}, bf16[48,1024]{1,0:T(8,128)(2,1)S(1)}, u32[]{:S(2)}, u32[]{:S(2)}) collective-permute-start(bf16[48,1024]{1,0:T(8,128)(2,1)S(1)} %get-tuple-element.58), channel_id=1, source_target_pairs={{0,2},{1,3},{2,0},{3,1},{4,6},{5,7},{6,4},{7,5},{8,10},{9,11},{10,... | collective-permute-start | bytes 294920 | tf_op jit(solution)/shard_map/ppermute | solution.py:66
  25.0 3.3 %collective-permute-done.12.came_ref = bf16[48,1024]{1,0:T(8,128)(2,1)S(1)} collective-permute-done((bf16[48,1024]{1,0:T(8,128)(2,1)S(1)}, bf16[48,1024]{1,0:T(8,128)(2,1)S(1)}, u32[]{:S(2)}, u32[]{:S(2)}) %collective-permute-start.12) | collective-permute-done | bytes 98336 | tf_op jit(solution)/shard_map/ppermute | solution.py:66
  28.3 2.7 %collective-permute-start.13 = (bf16[24,1024]{1,0:T(8,128)(2,1)S(1)}, bf16[24,1024]{1,0:T(8,128)(2,1)S(1)}, u32[]{:S(2)}, u32[]{:S(2)}) collective-permute-start(bf16[24,1024]{1,0:T(8,128)(2,1)S(1)} %get-tuple-element.63), channel_id=1, source_target_pairs={{0,8},{4,12},{8,0},{12,4},{1,9},{5,13},{9,1},{13,5},{2,10},{6,14},... | collective-permute-start | bytes 147464 | tf_op jit(solution)/shard_map/ppermute | solution.py:66
  31.9 1.9 %collective-permute-done.13.refs_2_ = bf16[24,1024]{1,0:T(8,128)(2,1)S(1)} collective-permute-done((bf16[24,1024]{1,0:T(8,128)(2,1)S(1)}, bf16[24,1024]{1,0:T(8,128)(2,1)S(1)}, u32[]{:S(2)}, u32[]{:S(2)}) %collective-permute-start.13) | collective-permute-done | bytes 49184 | tf_op jit(solution)/shard_map/ppermute | solution.py:66
  33.9 3.0 %collective-permute-done.14.refs_3_ = bf16[24,1024]{1,0:T(8,128)(2,1)S(1)} collective-permute-done((bf16[24,1024]{1,0:T(8,128)(2,1)S(1)}, bf16[24,1024]{1,0:T(8,128)(2,1)S(1)}, u32[]{:S(2)}, u32[]{:S(2)}) %collective-permute-start.14) | collective-permute-done | bytes 49184 | tf_op jit(solution)/shard_map/ppermute | solution.py:66
  37.2 1.1 %collective-permute-start.15 = (bf16[24,1024]{1,0:T(8,128)(2,1)S(1)}, bf16[24,1024]{1,0:T(8,128)(2,1)S(1)}, u32[]{:S(2)}, u32[]{:S(2)}) collective-permute-start(bf16[24,1024]{1,0:T(8,128)(2,1)S(1)} %get-tuple-element.67), channel_id=1, source_target_pairs={{0,8},{4,12},{8,0},{12,4},{1,9},{5,13},{9,1},{13,5},{2,10},{6,14},... | collective-permute-start | bytes 147464 | tf_op jit(solution)/shard_map/ppermute | solution.py:66
  39.4 1.3 %collective-permute-start.23 = (bf16[24,1024]{1,0:T(8,128)(2,1)S(1)}, bf16[24,1024]{1,0:T(8,128)(2,1)S(1)}, u32[]{:S(2)}, u32[]{:S(2)}) collective-permute-start(bf16[24,1024]{1,0:T(8,128)(2,1)S(1)} %get-tuple-element.69), channel_id=1, source_target_pairs={{0,4},{4,0},{8,12},{12,8},{1,5},{5,1},{9,13},{13,9},{2,6},{6,2},{1... | collective-permute-start | bytes 147464 | tf_op jit(solution)/shard_map/ppermute | solution.py:66
  42.8 1.3 %collective-permute-done.19.refs_2_ = bf16[24,1024]{1,0:T(8,128)(2,1)S(1)} collective-permute-done((bf16[24,1024]{1,0:T(8,128)(2,1)S(1)}, bf16[24,1024]{1,0:T(8,128)(2,1)S(1)}, u32[]{:S(2)}, u32[]{:S(2)}) %collective-permute-start.19) | collective-permute-done | bytes 49184 | tf_op jit(solution)/shard_map/ppermute | solution.py:66
  44.7 1.5 %collective-permute-start.25 = (bf16[24,1024]{1,0:T(8,128)(2,1)S(1)}, bf16[24,1024]{1,0:T(8,128)(2,1)S(1)}, u32[]{:S(2)}, u32[]{:S(2)}) collective-permute-start(bf16[24,1024]{1,0:T(8,128)(2,1)S(1)} %collective-permute-done.23.refs_4_), channel_id=1, source_target_pairs={{0,2},{1,3},{2,0},{3,1},{4,6},{5,7},{6,4},{7,5},{8,10},{9,11},{10,... | collective-permute-start | bytes 147464 | tf_op jit(solution)/shard_map/ppermute | solution.py:66
  46.9 1.4 %collective-permute-done.21.refs_3_ = bf16[24,1024]{1,0:T(8,128)(2,1)S(1)} collective-permute-done((bf16[24,1024]{1,0:T(8,128)(2,1)S(1)}, bf16[24,1024]{1,0:T(8,128)(2,1)S(1)}, u32[]{:S(2)}, u32[]{:S(2)}) %collective-permute-start.21) | collective-permute-done | bytes 49184 | tf_op jit(solution)/shard_map/ppermute | solution.py:66
  53.4 1.5 %collective-permute-start.34 = (bf16[48,1024]{1,0:T(8,128)(2,1)S(1)}, bf16[48,1024]{1,0:T(8,128)(2,1)S(1)}, u32[]{:S(2)}, u32[]{:S(2)}) collective-permute-start(bf16[48,1024]{1,0:T(8,128)(2,1)S(1)} %get-tuple-element.79), channel_id=1, source_target_pairs={{0,2},{1,3},{2,0},{3,1},{4,6},{5,7},{6,4},{7,5},{8,10},{9,11},{10,... | collective-permute-start | bytes 294920 | tf_op jit(solution)/shard_map/ppermute | solution.py:66
  55.8 3.3 %collective-permute-done.34.came_ref = bf16[48,1024]{1,0:T(8,128)(2,1)S(1)} collective-permute-done((bf16[48,1024]{1,0:T(8,128)(2,1)S(1)}, bf16[48,1024]{1,0:T(8,128)(2,1)S(1)}, u32[]{:S(2)}, u32[]{:S(2)}) %collective-permute-start.34) | collective-permute-done | bytes 98336 | tf_op jit(solution)/shard_map/ppermute | solution.py:66
  59.2 1.2 %collective-permute-start.35 = (bf16[24,1024]{1,0:T(8,128)(2,1)S(1)}, bf16[24,1024]{1,0:T(8,128)(2,1)S(1)}, u32[]{:S(2)}, u32[]{:S(2)}) collective-permute-start(bf16[24,1024]{1,0:T(8,128)(2,1)S(1)} %get-tuple-element.80), channel_id=1, source_target_pairs={{0,8},{4,12},{8,0},{12,4},{1,9},{5,13},{9,1},{13,5},{2,10},{6,14},... | collective-permute-start | bytes 147464 | tf_op jit(solution)/shard_map/ppermute | solution.py:66
  60.4 1.3 %collective-permute-start.36 = (bf16[24,1024]{1,0:T(8,128)(2,1)S(1)}, bf16[24,1024]{1,0:T(8,128)(2,1)S(1)}, u32[]{:S(2)}, u32[]{:S(2)}) collective-permute-start(bf16[24,1024]{1,0:T(8,128)(2,1)S(1)} %get-tuple-element.81), channel_id=1, source_target_pairs={{0,12},{4,8},{8,4},{12,0},{1,13},{5,9},{9,5},{13,1},{2,14},{6,10},... | collective-permute-start | bytes 147464 | tf_op jit(solution)/shard_map/ppermute | solution.py:66
  61.7 1.1 %collective-permute-start.33 = (bf16[24,1024]{1,0:T(8,128)(2,1)S(1)}, bf16[24,1024]{1,0:T(8,128)(2,1)S(1)}, u32[]{:S(2)}, u32[]{:S(2)}) collective-permute-start(bf16[24,1024]{1,0:T(8,128)(2,1)S(1)} %get-tuple-element.77), channel_id=1, source_target_pairs={{0,4},{4,0},{8,12},{12,8},{1,5},{5,1},{9,13},{13,9},{2,6},{6,2},{1... | collective-permute-start | bytes 147464 | tf_op jit(solution)/shard_map/ppermute | solution.py:66
  62.8 1.8 %collective-permute-done.35.refs_2_ = bf16[24,1024]{1,0:T(8,128)(2,1)S(1)} collective-permute-done((bf16[24,1024]{1,0:T(8,128)(2,1)S(1)}, bf16[24,1024]{1,0:T(8,128)(2,1)S(1)}, u32[]{:S(2)}, u32[]{:S(2)}) %collective-permute-start.35) | collective-permute-done | bytes 49184 | tf_op jit(solution)/shard_map/ppermute | solution.py:66
  64.6 1.8 %collective-permute-done.36.refs_3_ = bf16[24,1024]{1,0:T(8,128)(2,1)S(1)} collective-permute-done((bf16[24,1024]{1,0:T(8,128)(2,1)S(1)}, bf16[24,1024]{1,0:T(8,128)(2,1)S(1)}, u32[]{:S(2)}, u32[]{:S(2)}) %collective-permute-start.36) | collective-permute-done | bytes 49184 | tf_op jit(solution)/shard_map/ppermute | solution.py:66
  (85 shorter events, 19.1 us)
Async XLA Ops:
  1.9 15.9 %collective-permute-start.3 = (bf16[24,2176]{1,0:T(8,128)(2,1)S(1)}, bf16[24,2176]{1,0:T(8,128)(2,1)S(1)}, u32[]{:S(2)}, u32[]{:S(2)}) collective-permute-start(bf16[24,2176]{1,0:T(8,128)(2,1)S(1)} %get-tuple-element.50), channel_id=1, source_target_pairs={{0,8},{4,12},{8,0},{12,4},{1,9},{5,13},{9,1},{13,5},{2,10},{6,14},... | collective-permute-start | bytes 313352 | tf_op jit(solution)/shard_map/ppermute | solution.py:66
  6.0 11.9 %collective-permute-start.1 = (bf16[24,2176]{1,0:T(8,128)(2,1)S(1)}, bf16[24,2176]{1,0:T(8,128)(2,1)S(1)}, u32[]{:S(2)}, u32[]{:S(2)}) collective-permute-start(bf16[24,2176]{1,0:T(8,128)(2,1)S(1)} %get-tuple-element.48), channel_id=1, source_target_pairs={{0,4},{4,0},{8,12},{12,8},{1,5},{5,1},{9,13},{13,9},{2,6},{6,2},{1... | collective-permute-start | bytes 313352 | tf_op jit(solution)/shard_map/ppermute | solution.py:66
  7.5 6.0 %collective-permute-start = (bf16[24,1152]{1,0:T(8,128)(2,1)S(1)}, bf16[24,1152]{1,0:T(8,128)(2,1)S(1)}, u32[]{:S(2)}, u32[]{:S(2)}) collective-permute-start(bf16[24,1152]{1,0:T(8,128)(2,1)S(1)} %get-tuple-element.43), channel_id=1, source_target_pairs={{0,12},{4,8},{8,4},{12,0},{1,13},{5,9},{9,5},{13,1},{2,14},{6,10},... | collective-permute-start | bytes 165896 | tf_op jit(solution)/shard_map/ppermute | solution.py:66
  13.5 5.0 %collective-permute-start.6 = (bf16[24,1024]{1,0:T(8,128)(2,1)S(1)}, bf16[24,1024]{1,0:T(8,128)(2,1)S(1)}, u32[]{:S(2)}, u32[]{:S(2)}) collective-permute-start(bf16[24,1024]{1,0:T(8,128)(2,1)S(1)} %relay.3.refs_1_.refs_2_), channel_id=1, source_target_pairs={{0,2},{1,3},{2,0},{3,1},{4,6},{5,7},{6,4},{7,5},{8,10},{9,11},{10,... | collective-permute-start | bytes 147464 | tf_op jit(solution)/shard_map/ppermute | solution.py:66
  22.6 5.7 %collective-permute-start.12 = (bf16[48,1024]{1,0:T(8,128)(2,1)S(1)}, bf16[48,1024]{1,0:T(8,128)(2,1)S(1)}, u32[]{:S(2)}, u32[]{:S(2)}) collective-permute-start(bf16[48,1024]{1,0:T(8,128)(2,1)S(1)} %get-tuple-element.62), channel_id=1, source_target_pairs={{0,2},{1,3},{2,0},{3,1},{4,6},{5,7},{6,4},{7,5},{8,10},{9,11},{10,... | collective-permute-start | bytes 294920 | tf_op jit(solution)/shard_map/ppermute | solution.py:66
  23.2 8.2 %collective-permute-start.10 = (bf16[48,1024]{1,0:T(8,128)(2,1)S(1)}, bf16[48,1024]{1,0:T(8,128)(2,1)S(1)}, u32[]{:S(2)}, u32[]{:S(2)}) collective-permute-start(bf16[48,1024]{1,0:T(8,128)(2,1)S(1)} %get-tuple-element.58), channel_id=1, source_target_pairs={{0,2},{1,3},{2,0},{3,1},{4,6},{5,7},{6,4},{7,5},{8,10},{9,11},{10,... | collective-permute-start | bytes 294920 | tf_op jit(solution)/shard_map/ppermute | solution.py:66
  28.3 5.6 %collective-permute-start.13 = (bf16[24,1024]{1,0:T(8,128)(2,1)S(1)}, bf16[24,1024]{1,0:T(8,128)(2,1)S(1)}, u32[]{:S(2)}, u32[]{:S(2)}) collective-permute-start(bf16[24,1024]{1,0:T(8,128)(2,1)S(1)} %get-tuple-element.63), channel_id=1, source_target_pairs={{0,8},{4,12},{8,0},{12,4},{1,9},{5,13},{9,1},{13,5},{2,10},{6,14},... | collective-permute-start | bytes 147464 | tf_op jit(solution)/shard_map/ppermute | solution.py:66
  30.9 5.9 %collective-permute-start.14 = (bf16[24,1024]{1,0:T(8,128)(2,1)S(1)}, bf16[24,1024]{1,0:T(8,128)(2,1)S(1)}, u32[]{:S(2)}, u32[]{:S(2)}) collective-permute-start(bf16[24,1024]{1,0:T(8,128)(2,1)S(1)} %get-tuple-element.64), channel_id=1, source_target_pairs={{0,12},{4,8},{8,4},{12,0},{1,13},{5,9},{9,5},{13,1},{2,14},{6,10},... | collective-permute-start | bytes 147464 | tf_op jit(solution)/shard_map/ppermute | solution.py:66
  31.4 5.4 %collective-permute-start.11 = (bf16[24,1024]{1,0:T(8,128)(2,1)S(1)}, bf16[24,1024]{1,0:T(8,128)(2,1)S(1)}, u32[]{:S(2)}, u32[]{:S(2)}) collective-permute-start(bf16[24,1024]{1,0:T(8,128)(2,1)S(1)} %get-tuple-element.60), channel_id=1, source_target_pairs={{0,4},{4,0},{8,12},{12,8},{1,5},{5,1},{9,13},{13,9},{2,6},{6,2},{1... | collective-permute-start | bytes 147464 | tf_op jit(solution)/shard_map/ppermute | solution.py:66
  37.2 5.1 %collective-permute-start.15 = (bf16[24,1024]{1,0:T(8,128)(2,1)S(1)}, bf16[24,1024]{1,0:T(8,128)(2,1)S(1)}, u32[]{:S(2)}, u32[]{:S(2)}) collective-permute-start(bf16[24,1024]{1,0:T(8,128)(2,1)S(1)} %get-tuple-element.67), channel_id=1, source_target_pairs={{0,8},{4,12},{8,0},{12,4},{1,9},{5,13},{9,1},{13,5},{2,10},{6,14},... | collective-permute-start | bytes 147464 | tf_op jit(solution)/shard_map/ppermute | solution.py:66
  38.3 5.9 %collective-permute-start.19 = (bf16[24,1024]{1,0:T(8,128)(2,1)S(1)}, bf16[24,1024]{1,0:T(8,128)(2,1)S(1)}, u32[]{:S(2)}, u32[]{:S(2)}) collective-permute-start(bf16[24,1024]{1,0:T(8,128)(2,1)S(1)} %get-tuple-element.68), channel_id=1, source_target_pairs={{0,12},{4,8},{8,4},{12,0},{1,13},{5,9},{9,5},{13,1},{2,14},{6,10},... | collective-permute-start | bytes 147464 | tf_op jit(solution)/shard_map/ppermute | solution.py:66
  39.4 5.3 %collective-permute-start.23 = (bf16[24,1024]{1,0:T(8,128)(2,1)S(1)}, bf16[24,1024]{1,0:T(8,128)(2,1)S(1)}, u32[]{:S(2)}, u32[]{:S(2)}) collective-permute-start(bf16[24,1024]{1,0:T(8,128)(2,1)S(1)} %get-tuple-element.69), channel_id=1, source_target_pairs={{0,4},{4,0},{8,12},{12,8},{1,5},{5,1},{9,13},{13,9},{2,6},{6,2},{1... | collective-permute-start | bytes 147464 | tf_op jit(solution)/shard_map/ppermute | solution.py:66
  40.7 5.5 %collective-permute-start.28 = (bf16[24,1024]{1,0:T(8,128)(2,1)S(1)}, bf16[24,1024]{1,0:T(8,128)(2,1)S(1)}, u32[]{:S(2)}, u32[]{:S(2)}) collective-permute-start(bf16[24,1024]{1,0:T(8,128)(2,1)S(1)} %get-tuple-element.70.refs_6_), channel_id=1, source_target_pairs={{0,2},{1,3},{2,0},{3,1},{4,6},{5,7},{6,4},{7,5},{8,10},{9,11},{10,... | collective-permute-start | bytes 147464 | tf_op jit(solution)/shard_map/ppermute | solution.py:66
  41.2 5.0 %collective-permute-start.27 = (bf16[24,1024]{1,0:T(8,128)(2,1)S(1)}, bf16[24,1024]{1,0:T(8,128)(2,1)S(1)}, u32[]{:S(2)}, u32[]{:S(2)}) collective-permute-start(bf16[24,1024]{1,0:T(8,128)(2,1)S(1)} %get-tuple-element.70.refs_6_), channel_id=1, source_target_pairs={{0,1},{1,0},{2,3},{3,2},{4,5},{5,4},{6,7},{7,6},{8,9},{9,8},{10,11... | collective-permute-start | bytes 147464 | tf_op jit(solution)/shard_map/ppermute | solution.py:66
  42.3 4.6 %collective-permute-start.17 = (bf16[24,1024]{1,0:T(8,128)(2,1)S(1)}, bf16[24,1024]{1,0:T(8,128)(2,1)S(1)}, u32[]{:S(2)}, u32[]{:S(2)}) collective-permute-start(bf16[24,1024]{1,0:T(8,128)(2,1)S(1)} %collective-permute-done.15.refs_0_), channel_id=1, source_target_pairs={{0,2},{1,3},{2,0},{3,1},{4,6},{5,7},{6,4},{7,5},{8,10},{9,11},{10,... | collective-permute-start | bytes 147464 | tf_op jit(solution)/shard_map/ppermute | solution.py:66
  44.2 4.1 %collective-permute-start.21 = (bf16[24,1024]{1,0:T(8,128)(2,1)S(1)}, bf16[24,1024]{1,0:T(8,128)(2,1)S(1)}, u32[]{:S(2)}, u32[]{:S(2)}) collective-permute-start(bf16[24,1024]{1,0:T(8,128)(2,1)S(1)} %collective-permute-done.19.refs_2_), channel_id=1, source_target_pairs={{0,2},{1,3},{2,0},{3,1},{4,6},{5,7},{6,4},{7,5},{8,10},{9,11},{10,... | collective-permute-start | bytes 147464 | tf_op jit(solution)/shard_map/ppermute | solution.py:66
  44.7 4.1 %collective-permute-start.25 = (bf16[24,1024]{1,0:T(8,128)(2,1)S(1)}, bf16[24,1024]{1,0:T(8,128)(2,1)S(1)}, u32[]{:S(2)}, u32[]{:S(2)}) collective-permute-start(bf16[24,1024]{1,0:T(8,128)(2,1)S(1)} %collective-permute-done.23.refs_4_), channel_id=1, source_target_pairs={{0,2},{1,3},{2,0},{3,1},{4,6},{5,7},{6,4},{7,5},{8,10},{9,11},{10,... | collective-permute-start | bytes 147464 | tf_op jit(solution)/shard_map/ppermute | solution.py:66
  46.9 3.2 %collective-permute-start.24 = (bf16[24,1024]{1,0:T(8,128)(2,1)S(1)}, bf16[24,1024]{1,0:T(8,128)(2,1)S(1)}, u32[]{:S(2)}, u32[]{:S(2)}) collective-permute-start(bf16[24,1024]{1,0:T(8,128)(2,1)S(1)} %collective-permute-done.23.refs_4_), channel_id=1, source_target_pairs={{0,1},{1,0},{2,3},{3,2},{4,5},{5,4},{6,7},{7,6},{8,9},{9,8},{10,11... | collective-permute-start | bytes 147464 | tf_op jit(solution)/shard_map/ppermute | solution.py:66
  52.4 3.1 %collective-permute-start.30 = (bf16[96,1024]{1,0:T(8,128)(2,1)S(1)}, bf16[96,1024]{1,0:T(8,128)(2,1)S(1)}, u32[]{:S(2)}, u32[]{:S(2)}) collective-permute-start(bf16[96,1024]{1,0:T(8,128)(2,1)S(1)} %down.12), channel_id=1, source_target_pairs={{0,1},{1,0},{2,3},{3,2},{4,5},{5,4},{6,7},{7,6},{8,9},{9,8},{10,11... | collective-permute-start | bytes 589832 | tf_op jit(solution)/shard_map/ppermute | solution.py:66
  53.4 5.7 %collective-permute-start.34 = (bf16[48,1024]{1,0:T(8,128)(2,1)S(1)}, bf16[48,1024]{1,0:T(8,128)(2,1)S(1)}, u32[]{:S(2)}, u32[]{:S(2)}) collective-permute-start(bf16[48,1024]{1,0:T(8,128)(2,1)S(1)} %get-tuple-element.79), channel_id=1, source_target_pairs={{0,2},{1,3},{2,0},{3,1},{4,6},{5,7},{6,4},{7,5},{8,10},{9,11},{10,... | collective-permute-start | bytes 294920 | tf_op jit(solution)/shard_map/ppermute | solution.py:66
  55.0 6.7 %collective-permute-start.32 = (bf16[48,1024]{1,0:T(8,128)(2,1)S(1)}, bf16[48,1024]{1,0:T(8,128)(2,1)S(1)}, u32[]{:S(2)}, u32[]{:S(2)}) collective-permute-start(bf16[48,1024]{1,0:T(8,128)(2,1)S(1)} %get-tuple-element.75), channel_id=1, source_target_pairs={{0,2},{1,3},{2,0},{3,1},{4,6},{5,7},{6,4},{7,5},{8,10},{9,11},{10,... | collective-permute-start | bytes 294920 | tf_op jit(solution)/shard_map/ppermute | solution.py:66
  59.2 5.4 %collective-permute-start.35 = (bf16[24,1024]{1,0:T(8,128)(2,1)S(1)}, bf16[24,1024]{1,0:T(8,128)(2,1)S(1)}, u32[]{:S(2)}, u32[]{:S(2)}) collective-permute-start(bf16[24,1024]{1,0:T(8,128)(2,1)S(1)} %get-tuple-element.80), channel_id=1, source_target_pairs={{0,8},{4,12},{8,0},{12,4},{1,9},{5,13},{9,1},{13,5},{2,10},{6,14},... | collective-permute-start | bytes 147464 | tf_op jit(solution)/shard_map/ppermute | solution.py:66
  60.4 6.0 %collective-permute-start.36 = (bf16[24,1024]{1,0:T(8,128)(2,1)S(1)}, bf16[24,1024]{1,0:T(8,128)(2,1)S(1)}, u32[]{:S(2)}, u32[]{:S(2)}) collective-permute-start(bf16[24,1024]{1,0:T(8,128)(2,1)S(1)} %get-tuple-element.81), channel_id=1, source_target_pairs={{0,12},{4,8},{8,4},{12,0},{1,13},{5,9},{9,5},{13,1},{2,14},{6,10},... | collective-permute-start | bytes 147464 | tf_op jit(solution)/shard_map/ppermute | solution.py:66
  61.7 4.7 %collective-permute-start.33 = (bf16[24,1024]{1,0:T(8,128)(2,1)S(1)}, bf16[24,1024]{1,0:T(8,128)(2,1)S(1)}, u32[]{:S(2)}, u32[]{:S(2)}) collective-permute-start(bf16[24,1024]{1,0:T(8,128)(2,1)S(1)} %get-tuple-element.77), channel_id=1, source_target_pairs={{0,4},{4,0},{8,12},{12,8},{1,5},{5,1},{9,13},{13,9},{2,6},{6,2},{1... | collective-permute-start | bytes 147464 | tf_op jit(solution)/shard_map/ppermute | solution.py:66
  (17 other events, 54.2 us)

commit v14 on v12

--- a/solution.py
+++ b/solution.py
@@ -320,25 +320,35 @@
     return half_front(there, (1, 3), [flags[k] for k in order] + list(sums), shapes, *common)[0]
 
 
-def down_kernel(flip, n_adds, hidden_ref, down_ref, *refs):
+def store_blocks(total, groups, outs):
+    rows = total.shape[0] // sum(len(group) for group in groups)
+    for group, out in zip(groups, outs):
+        blocks = [total[k * rows : (k + 1) * rows] for k in group]
+        out[...] = jnp.concatenate(blocks, axis=0).astype(out.dtype)
+
+
+def shapes_of(rows, cols, groups, types):
+    slots = rows // sum(len(group) for group in groups)
+    return [jax.ShapeDtypeStruct((slots * len(group), cols), t) for group, t in zip(groups, types)]
+
+
+def down_kernel(flip, n_adds, groups, hidden_ref, down_ref, *refs):
     adds, outs = refs[:n_adds], refs[n_adds:]
     quarter = outs[0].shape[1]
     weights = down_ref[:, aligned(lax.axis_index("et") ^ flip, quarter)]
-    product = jnp.dot(hidden_ref[...], weights, preferred_element_type=jnp.float32)
+    total = jnp.dot(hidden_ref[...], weights, preferred_element_type=jnp.float32)
     for ref in adds:
-        product += ref[...].astype(jnp.float32)
-    rows = outs[0].shape[0]
-    for k, out in enumerate(outs):
-        out[...] = product[k * rows : (k + 1) * rows].astype(out.dtype)
-
-
-def down(hidden, w_down, flip, blocks, adds=(), dtype=jnp.bfloat16):
+        total += ref[...].astype(jnp.float32)
+    store_blocks(total, groups, outs)
+
+
+def down(hidden, w_down, flip, adds=(), groups=((0,),), types=(jnp.bfloat16,)):
     units, width = w_down.shape
     rows, quarter = hidden.shape[0], width // 4
     return pl.pallas_call(
-        functools.partial(down_kernel, flip, len(adds)),
+        functools.partial(down_kernel, flip, len(adds), groups),
         in_specs=[VMEM] * (2 + len(adds)),
-        out_shape=[jax.ShapeDtypeStruct((rows // blocks, quarter), dtype)] * blocks,
+        out_shape=shapes_of(rows, quarter, groups, types),
         compiler_params=params(),
         cost_estimate=pl.CostEstimate(
             flops=2 * rows * units * quarter, bytes_accessed=2 * units * quarter, transcendentals=0
@@ -347,26 +357,29 @@
     )(hidden, w_down, *adds)
 
 
-def add_kernel(keep_ref, came_ref, *outs):
-    total = keep_ref[...] + came_ref[...].astype(jnp.float32)
-    rows = outs[0].shape[0]
-    for k, out in enumerate(outs):
-        out[...] = total[k * rows : (k + 1) * rows].astype(out.dtype)
-
-
-def add(keep, came, count):
-    shape = (keep.shape[0] // count, keep.shape[1])
-    return pl.pallas_call(
-        add_kernel,
-        out_shape=[jax.ShapeDtypeStruct(shape, jnp.bfloat16)] * count,
+def add_kernel(groups, keep_ref, came_ref, *outs):
+    store_blocks(keep_ref[...] + came_ref[...].astype(jnp.float32), groups, outs)
+
+
+def add(keep, came, groups):
+    return pl.pallas_call(
+        functools.partial(add_kernel, groups),
+        out_shape=shapes_of(*keep.shape, groups, [jnp.bfloat16] * len(groups)),
         compiler_params=params(),
         name="add",
     )(keep, came)
 
 
-def move_kernel(n_came, last, own_ref, back_ref, pick_ref, *refs):
-    came, outs = refs[:n_came], refs[n_came:]
-    rows = [ref[...].astype(jnp.float32) for ref in came]
+def diagonal(x, k, flip):
+    n_ep, n_et = lax.axis_size("ep"), lax.axis_size("et")
+    pairs = [(e * n_et + t, (e ^ k) * n_et + (t ^ flip)) for e in range(n_ep) for t in range(n_et)]
+    return lax.ppermute(x, ("ep", "et"), pairs)
+
+
+def move_kernel(order, last, own_ref, back_ref, pick_ref, extra_ref, *refs):
+    came, outs = refs[: len(order)], refs[len(order) :]
+    rows = [came[order.index(k)][...].astype(jnp.float32) for k in range(len(order))]
+    rows[DIRECT] += extra_ref[...].astype(jnp.float32)
     velocity = product(back_ref[...], jnp.concatenate(rows, axis=0))
     moved = narrow(own_ref[...].astype(jnp.float32) - 0.5 * velocity)
     outs[0][...] = moved
@@ -379,28 +392,34 @@
             out[...] = narrow(picked[k * slots : (k + 1) * slots])
 
 
-def move(own, back, pick, came, last):
+def move(own, back, pick, extra, came, order, last):
     shapes = [own.shape] + ([own.shape] if last else [c.shape for c in came])
     return pl.pallas_call(
-        functools.partial(move_kernel, len(came), last),
+        functools.partial(move_kernel, order, last),
         out_shape=[jax.ShapeDtypeStruct(s, jnp.bfloat16) for s in shapes],
         compiler_params=params(),
         name="move",
-    )(own, back, pick, *came)
-
-
-def sum_back(hidden, w_down, own, back, pick, last_section):
+    )(own, back, pick, extra, *[came[k] for k in order])
+
+
+DIRECT = 2
+
+
+def sum_back(hidden, w_down, own, back, pick, last):
     peers = lax.axis_size("ep")
-    some = peers // 2
-    far = swap(down(hidden, w_down, 3, 1)[0], "et", 1)
-    near = swap(down(hidden, w_down, 1, 1)[0], "et", 1)
-    first, last = add(down(hidden, w_down, 2, 1, (), jnp.float32)[0], far, 2)
-    last, first = swap(last, "et", 2), swap(first, "et", 2)
-    keep_first, keep_last = down(hidden, w_down, 0, 2, (near,), jnp.float32)
-    later = add(keep_last, last, peers - some)
-    blocks = add(keep_first, first, some) + later
-    came = [swap(b, "ep", k) if k else b for k, b in enumerate(blocks)]
-    return move(own, back, pick, came, last_section)
+    rest = tuple(k for k in range(peers) if k != DIRECT)
+    groups = (rest, (DIRECT,))
+    (far,), (near,) = down(hidden, w_down, 3), down(hidden, w_down, 1)
+    far, near = swap(far, "et", 1), swap(near, "et", 1)
+    (crossing,) = down(hidden, w_down, 2, types=[jnp.float32])
+    crossing, beside = add(crossing, far, groups)
+    crossed, extra = swap(crossing, "et", 2), diagonal(beside, DIRECT, 2)
+    kept, straight = down(hidden, w_down, 0, (near,), groups, [jnp.float32, jnp.bfloat16])
+    blocks = dict(zip(rest, add(kept, crossed, [(i,) for i in range(len(rest))])))
+    blocks[DIRECT] = straight
+    came = [swap(blocks[k], "ep", k) if k else blocks[k] for k in range(peers)]
+    order = [*range(2, peers), 1, 0]
+    return move(own, back, pick, extra, came, order, last)
 
 
 def spread(block, quarter):
@@ -451,7 +470,7 @@
     def body(*args):
         experts, picks = args[2].shape[1], args[6].shape[2]
         peers = lax.axis_size("ep")
-        fits = lax.axis_size("et") == 4 and peers & (peers - 1) == 0
+        fits = lax.axis_size("et") == 4 and peers >= 4 and peers & (peers - 1) == 0
         chosen = dense_body if fits and experts <= 2 * picks else routed_body
         return chosen(*args)
 

time: 65.5 us -> 63.7 us (0.973)
  waiting for transfers between devices: 22.2 us -> 15.7 us
  starting transfers between devices: 29.6 us -> 34.3 us
    ppermute x35 -> x33, waiting for transfers between devices: 22.2 us -> 12.3 us  [swap(): return lax.ppermute(x, axis, [(i, i ^ bit) for i in range(size)])]
    ppermute x0 -> x2, waiting for transfers between devices: none -> 3.38 us  [diagonal(): return lax.ppermute(x, ('ep', 'et'), pairs)]
    ppermute x0 -> x2, starting transfers between devices: none -> 2.83 us  [diagonal(): return lax.ppermute(x, ('ep', 'et'), pairs)]
    ppermute x35 -> x33, starting transfers between devices: 29.6 us -> 31.4 us  [swap(): return lax.ppermute(x, axis, [(i, i ^ bit) for i in range(size)])]
    pallas_call x16 -> x14, Pallas kernels: 3.56 us -> 3.52 us  [the longest x8 2.24 us: down(): pl.pallas_call(functools.partial(down_kernel, flip, len(adds), groups), i...]
where the time goes in v14:
time: 63.7 us; the launch traced here: 63.5 us
  starting transfers between devices  34.3 us (54%)
  waiting for transfers between devices  15.7 us (25%)
  Pallas kernels  12.7 us (20%)
  between operations  0.87 us (1%)
    ppermute x33, starting transfers between devices, swap(): return lax.ppermute(x, axis, [(i, i ^ bit) for i in range(size)])  31.4 us
    ppermute x33, waiting for transfers between devices, swap(): return lax.ppermute(x, axis, [(i, i ^ bit) for i in range(size)])  12.3 us
    pallas_call x1, Pallas kernels, load(): pl.pallas_call(load_kernel, in_specs=[ANY] * 3, out_specs=[VMEM] * 3, out...  3.78 us
    ppermute x2, waiting for transfers between devices, diagonal(): return lax.ppermute(x, ('ep', 'et'), pairs)  3.38 us
    pallas_call x4, Pallas kernels, half_front(): pl.pallas_call(functools.partial(front_kernel, layout, order, flips, sect...  3.34 us
    ppermute x2, starting transfers between devices, diagonal(): return lax.ppermute(x, ('ep', 'et'), pairs)  2.83 us
    pallas_call x8, Pallas kernels, down(): pl.pallas_call(functools.partial(down_kernel, flip, len(adds), groups), i...  2.24 us
  transfers between devices with their start and end apart: 35, of which 18 were waited for; matrix products, arithmetic and copies ran while one was open for 0% of the time, Pallas kernels for 12%

profile of v14, /device:TPU:0, one launch (start us, length us, event | category | flops | bytes accessed | tf_op | source)
XLA Modules:
  0.0 63.5 jit_solution(17245665515278097388)
XLA Ops:
  0.6 1.2 %pack.1 = (bf16[24,2176]{1,0:T(8,128)(2,1)S(1)}, bf16[24,2176]{1,0:T(8,128)(2,1)S(1)}, bf16[24,2176]{1,0:T(8,128)(2,1)S(1)}, bf16[32,1024]{1,0:T(8,128)(2,1)S(1)}) custom-call(bf16[32,4096]{1,0:T(8,128)(2,1)} %tokens_ref.3, s32[2,2,32]{2,1,0:T(2,128)} %bitcast.6), custom_call_target="tpu_custom_call" | custom-call | tf_op jit(solution)/shard_map/pack/pallas_call | solution.py:197
  1.9 4.1 %collective-permute-start = (bf16[24,2176]{1,0:T(8,128)(2,1)S(1)}, bf16[24,2176]{1,0:T(8,128)(2,1)S(1)}, u32[]{:S(2)}, u32[]{:S(2)}) collective-permute-start(bf16[24,2176]{1,0:T(8,128)(2,1)S(1)} %get-tuple-element.43), channel_id=1, source_target_pairs={{0,8},{4,12},{8,0},{12,4},{1,9},{5,13},{9,1},{13,5},{2,10},{6,14},... | collective-permute-start | bytes 313352 | tf_op jit(solution)/shard_map/ppermute | solution.py:66
  6.0 1.3 %collective-permute-start.2 = (bf16[24,2176]{1,0:T(8,128)(2,1)S(1)}, bf16[24,2176]{1,0:T(8,128)(2,1)S(1)}, u32[]{:S(2)}, u32[]{:S(2)}) collective-permute-start(bf16[24,2176]{1,0:T(8,128)(2,1)S(1)} %get-tuple-element.45), channel_id=1, source_target_pairs={{0,12},{4,8},{8,4},{12,0},{1,13},{5,9},{9,5},{13,1},{2,14},{6,10},... | collective-permute-start | bytes 313352 | tf_op jit(solution)/shard_map/ppermute | solution.py:66
  7.6 3.8 %load.1 = (bf16[4096,768]{1,0:T(8,128)(2,1)S(1)}, bf16[384,4096]{1,0:T(8,128)(2,1)S(1)}, f32[8,128]{1,0:T(8,128)S(1)}) custom-call(bf16[1,4096,384]{2,1,0:T(8,128)(2,1)} %gate_ref.1, bf16[1,4096,384]{2,1,0:T(8,128)(2,1)} %up_ref.1, bf16[1,384,4096]{2,1,0:T(8,128)(2,1)} %down_ref.1), custom_call_target="tpu_custom_call" | custom-call | bytes 18874368 | tf_op jit(solution)/shard_map/load/pallas_call | solution.py:101
  12.2 2.0 %collective-permute-done.block_ref.refs_7_.refs_11_ = bf16[24,2176]{1,0:T(8,128)(2,1)S(1)} collective-permute-done((bf16[24,2176]{1,0:T(8,128)(2,1)S(1)}, bf16[24,2176]{1,0:T(8,128)(2,1)S(1)}, u32[]{:S(2)}, u32[]{:S(2)}) %collective-permute-start) | collective-permute-done | bytes 104480 | tf_op jit(solution)/shard_map/ppermute | solution.py:66
  19.0 1.9 %collective-permute-start.10 = (bf16[72,1024]{1,0:T(8,128)(2,1)S(1)}, bf16[72,1024]{1,0:T(8,128)(2,1)S(1)}, u32[]{:S(2)}, u32[]{:S(2)}) collective-permute-start(bf16[72,1024]{1,0:T(8,128)(2,1)S(1)} %get-tuple-element.56), channel_id=1, source_target_pairs={{0,2},{1,3},{2,0},{3,1},{4,6},{5,7},{6,4},{7,5},{8,10},{9,11},{10,... | collective-permute-start | bytes 442376 | tf_op jit(solution)/shard_map/ppermute | solution.py:66
  21.2 3.3 %collective-permute-start.9 = (bf16[24,1024]{1,0:T(8,128)(2,1)S(1)}, bf16[24,1024]{1,0:T(8,128)(2,1)S(1)}, u32[]{:S(2)}, u32[]{:S(2)}) collective-permute-start(bf16[24,1024]{1,0:T(8,128)(2,1)S(1)} %get-tuple-element.54), channel_id=1, source_target_pairs={{0,8},{4,12},{8,0},{12,4},{1,9},{5,13},{9,1},{13,5},{2,10},{6,14},... | collective-permute-start | bytes 147464 | tf_op jit(solution)/shard_map/ppermute | solution.py:66
  25.1 3.2 %collective-permute-start.11 = (bf16[24,1024]{1,0:T(8,128)(2,1)S(1)}, bf16[24,1024]{1,0:T(8,128)(2,1)S(1)}, u32[]{:S(2)}, u32[]{:S(2)}) collective-permute-start(bf16[24,1024]{1,0:T(8,128)(2,1)S(1)} %get-tuple-element.57), channel_id=1, source_target_pairs={{0,12},{4,8},{8,4},{12,0},{1,13},{5,9},{9,5},{13,1},{2,14},{6,10},... | collective-permute-start | bytes 147464 | tf_op jit(solution)/shard_map/ppermute | solution.py:66
  28.3 1.1 %collective-permute-start.12 = (bf16[24,1024]{1,0:T(8,128)(2,1)S(1)}, bf16[24,1024]{1,0:T(8,128)(2,1)S(1)}, u32[]{:S(2)}, u32[]{:S(2)}) collective-permute-start(bf16[24,1024]{1,0:T(8,128)(2,1)S(1)} %get-tuple-element.58), channel_id=1, source_target_pairs={{0,4},{4,0},{8,12},{12,8},{1,5},{5,1},{9,13},{13,9},{2,6},{6,2},{1... | collective-permute-start | bytes 147464 | tf_op jit(solution)/shard_map/ppermute | solution.py:66
  29.5 2.2 %collective-permute-done.7.extra_ref = bf16[24,1024]{1,0:T(8,128)(2,1)S(1)} collective-permute-done((bf16[24,1024]{1,0:T(8,128)(2,1)S(1)}, bf16[24,1024]{1,0:T(8,128)(2,1)S(1)}, u32[]{:S(2)}, u32[]{:S(2)}) %collective-permute-start.7) | collective-permute-done | bytes 49184 | tf_op jit(solution)/shard_map/ppermute | solution.py:376
  32.8 1.1 %collective-permute-start.13 = (bf16[24,1024]{1,0:T(8,128)(2,1)S(1)}, bf16[24,1024]{1,0:T(8,128)(2,1)S(1)}, u32[]{:S(2)}, u32[]{:S(2)}) collective-permute-start(bf16[24,1024]{1,0:T(8,128)(2,1)S(1)} %get-tuple-element.62), channel_id=1, source_target_pairs={{0,8},{4,12},{8,0},{12,4},{1,9},{5,13},{9,1},{13,5},{2,10},{6,14},... | collective-permute-start | bytes 147464 | tf_op jit(solution)/shard_map/ppermute | solution.py:66
  33.9 2.4 %collective-permute-start.17 = (bf16[24,1024]{1,0:T(8,128)(2,1)S(1)}, bf16[24,1024]{1,0:T(8,128)(2,1)S(1)}, u32[]{:S(2)}, u32[]{:S(2)}) collective-permute-start(bf16[24,1024]{1,0:T(8,128)(2,1)S(1)} %get-tuple-element.63), channel_id=1, source_target_pairs={{0,12},{4,8},{8,4},{12,0},{1,13},{5,9},{9,5},{13,1},{2,14},{6,10},... | collective-permute-start | bytes 147464 | tf_op jit(solution)/shard_map/ppermute | solution.py:66
  36.3 1.5 %collective-permute-start.26 = (bf16[24,1024]{1,0:T(8,128)(2,1)S(1)}, bf16[24,1024]{1,0:T(8,128)(2,1)S(1)}, u32[]{:S(2)}, u32[]{:S(2)}) collective-permute-start(bf16[24,1024]{1,0:T(8,128)(2,1)S(1)} %get-tuple-element.65.refs_6_), channel_id=1, source_target_pairs={{0,2},{1,3},{2,0},{3,1},{4,6},{5,7},{6,4},{7,5},{8,10},{9,11},{10,... | collective-permute-start | bytes 147464 | tf_op jit(solution)/shard_map/ppermute | solution.py:66
  37.9 1.5 %collective-permute-start.15 = (bf16[24,1024]{1,0:T(8,128)(2,1)S(1)}, bf16[24,1024]{1,0:T(8,128)(2,1)S(1)}, u32[]{:S(2)}, u32[]{:S(2)}) collective-permute-start(bf16[24,1024]{1,0:T(8,128)(2,1)S(1)} %collective-permute-done.13.refs_0_), channel_id=1, source_target_pairs={{0,2},{1,3},{2,0},{3,1},{4,6},{5,7},{6,4},{7,5},{8,10},{9,11},{10,... | collective-permute-start | bytes 147464 | tf_op jit(solution)/shard_map/ppermute | solution.py:66
  39.8 1.5 %collective-permute-start.19 = (bf16[24,1024]{1,0:T(8,128)(2,1)S(1)}, bf16[24,1024]{1,0:T(8,128)(2,1)S(1)}, u32[]{:S(2)}, u32[]{:S(2)}) collective-permute-start(bf16[24,1024]{1,0:T(8,128)(2,1)S(1)} %collective-permute-done.17.refs_2_), channel_id=1, source_target_pairs={{0,2},{1,3},{2,0},{3,1},{4,6},{5,7},{6,4},{7,5},{8,10},{9,11},{10,... | collective-permute-start | bytes 147464 | tf_op jit(solution)/shard_map/ppermute | solution.py:66
  42.5 1.4 %collective-permute-done.19.refs_3_ = bf16[24,1024]{1,0:T(8,128)(2,1)S(1)} collective-permute-done((bf16[24,1024]{1,0:T(8,128)(2,1)S(1)}, bf16[24,1024]{1,0:T(8,128)(2,1)S(1)}, u32[]{:S(2)}, u32[]{:S(2)}) %collective-permute-start.19) | collective-permute-done | bytes 49184 | tf_op jit(solution)/shard_map/ppermute | solution.py:66
  43.9 1.5 %collective-permute-done.23.refs_5_ = bf16[24,1024]{1,0:T(8,128)(2,1)S(1)} collective-permute-done((bf16[24,1024]{1,0:T(8,128)(2,1)S(1)}, bf16[24,1024]{1,0:T(8,128)(2,1)S(1)}, u32[]{:S(2)}, u32[]{:S(2)}) %collective-permute-start.23) | collective-permute-done | bytes 49184 | tf_op jit(solution)/shard_map/ppermute | solution.py:66
  47.1 1.0 %front.7.hidden_ref = bf16[96,384]{1,0:T(8,128)(2,1)S(1)} custom-call(bf16[24,1024]{1,0:T(8,128)(2,1)S(1)} %collective-permute-done.14.refs_0_, bf16[24,1024]{1,0:T(8,128)(2,1)S(1)} %collective-permute-done.16.refs_1_, bf16[24,1024]{1,0:T(8,128)(2,1)S(1)} %collective-permute-done.18.refs_2_, bf16[24,1024]{1,0:T(8,128)(2,1)S(1)} %collective-permute-done.20.refs_3_, ...), custom_call_target="tpu_custom_call" | custom-call | flops 301989888 | bytes 3145728 | tf_op jit(solution)/shard_map/front/pallas_call | solution.py:298
  51.0 1.1 %collective-permute-start.31 = (bf16[24,1024]{1,0:T(8,128)(2,1)S(1)}, bf16[24,1024]{1,0:T(8,128)(2,1)S(1)}, u32[]{:S(2)}, u32[]{:S(2)}) collective-permute-start(bf16[24,1024]{1,0:T(8,128)(2,1)S(1)} %get-tuple-element.70), channel_id=1, source_target_pairs={{0,8},{4,12},{8,0},{12,4},{1,9},{5,13},{9,1},{13,5},{2,10},{6,14},... | collective-permute-start | bytes 147464 | tf_op jit(solution)/shard_map/ppermute | solution.py:66
  52.1 2.7 %collective-permute-start.29 = (bf16[24,1024]{1,0:T(8,128)(2,1)S(1)}, bf16[24,1024]{1,0:T(8,128)(2,1)S(1)}, u32[]{:S(2)}, u32[]{:S(2)}) collective-permute-start(bf16[24,1024]{1,0:T(8,128)(2,1)S(1)} %get-tuple-element.69), channel_id=1, source_target_pairs={{0,10},{1,11},{2,8},{3,9},{4,14},{5,15},{6,12},{7,13},{8,2},{9,3},... | collective-permute-start | bytes 147464 | tf_op jit(solution)/shard_map/ppermute | solution.py:376
  54.8 1.2 %collective-permute-done.32.came_ref = bf16[72,1024]{1,0:T(8,128)(2,1)S(1)} collective-permute-done((bf16[72,1024]{1,0:T(8,128)(2,1)S(1)}, bf16[72,1024]{1,0:T(8,128)(2,1)S(1)}, u32[]{:S(2)}, u32[]{:S(2)}) %collective-permute-start.32) | collective-permute-done | bytes 147488 | tf_op jit(solution)/shard_map/ppermute | solution.py:66
  56.0 2.6 %collective-permute-start.33 = (bf16[24,1024]{1,0:T(8,128)(2,1)S(1)}, bf16[24,1024]{1,0:T(8,128)(2,1)S(1)}, u32[]{:S(2)}, u32[]{:S(2)}) collective-permute-start(bf16[24,1024]{1,0:T(8,128)(2,1)S(1)} %get-tuple-element.73), channel_id=1, source_target_pairs={{0,12},{4,8},{8,4},{12,0},{1,13},{5,9},{9,5},{13,1},{2,14},{6,10},... | collective-permute-start | bytes 147464 | tf_op jit(solution)/shard_map/ppermute | solution.py:66
  58.6 1.2 %collective-permute-done.29.extra_ref = bf16[24,1024]{1,0:T(8,128)(2,1)S(1)} collective-permute-done((bf16[24,1024]{1,0:T(8,128)(2,1)S(1)}, bf16[24,1024]{1,0:T(8,128)(2,1)S(1)}, u32[]{:S(2)}, u32[]{:S(2)}) %collective-permute-start.29) | collective-permute-done | bytes 49184 | tf_op jit(solution)/shard_map/ppermute | solution.py:376
  59.8 2.2 %collective-permute-done.33.refs_1_ = bf16[24,1024]{1,0:T(8,128)(2,1)S(1)} collective-permute-done((bf16[24,1024]{1,0:T(8,128)(2,1)S(1)}, bf16[24,1024]{1,0:T(8,128)(2,1)S(1)}, u32[]{:S(2)}, u32[]{:S(2)}) %collective-permute-start.33) | collective-permute-done | bytes 49184 | tf_op jit(solution)/shard_map/ppermute | solution.py:66
  (78 shorter events, 15.5 us)
Async XLA Ops:
  1.9 12.4 %collective-permute-start = (bf16[24,2176]{1,0:T(8,128)(2,1)S(1)}, bf16[24,2176]{1,0:T(8,128)(2,1)S(1)}, u32[]{:S(2)}, u32[]{:S(2)}) collective-permute-start(bf16[24,2176]{1,0:T(8,128)(2,1)S(1)} %get-tuple-element.43), channel_id=1, source_target_pairs={{0,8},{4,12},{8,0},{12,4},{1,9},{5,13},{9,1},{13,5},{2,10},{6,14},... | collective-permute-start | bytes 313352 | tf_op jit(solution)/shard_map/ppermute | solution.py:66
  6.0 8.4 %collective-permute-start.2 = (bf16[24,2176]{1,0:T(8,128)(2,1)S(1)}, bf16[24,2176]{1,0:T(8,128)(2,1)S(1)}, u32[]{:S(2)}, u32[]{:S(2)}) collective-permute-start(bf16[24,2176]{1,0:T(8,128)(2,1)S(1)} %get-tuple-element.45), channel_id=1, source_target_pairs={{0,12},{4,8},{8,4},{12,0},{1,13},{5,9},{9,5},{13,1},{2,14},{6,10},... | collective-permute-start | bytes 313352 | tf_op jit(solution)/shard_map/ppermute | solution.py:66
  7.3 7.6 %collective-permute-start.4 = (bf16[24,2176]{1,0:T(8,128)(2,1)S(1)}, bf16[24,2176]{1,0:T(8,128)(2,1)S(1)}, u32[]{:S(2)}, u32[]{:S(2)}) collective-permute-start(bf16[24,2176]{1,0:T(8,128)(2,1)S(1)} %get-tuple-element.46), channel_id=1, source_target_pairs={{0,4},{4,0},{8,12},{12,8},{1,5},{5,1},{9,13},{13,9},{2,6},{6,2},{1... | collective-permute-start | bytes 313352 | tf_op jit(solution)/shard_map/ppermute | solution.py:66
  19.0 6.1 %collective-permute-start.10 = (bf16[72,1024]{1,0:T(8,128)(2,1)S(1)}, bf16[72,1024]{1,0:T(8,128)(2,1)S(1)}, u32[]{:S(2)}, u32[]{:S(2)}) collective-permute-start(bf16[72,1024]{1,0:T(8,128)(2,1)S(1)} %get-tuple-element.56), channel_id=1, source_target_pairs={{0,2},{1,3},{2,0},{3,1},{4,6},{5,7},{6,4},{7,5},{8,10},{9,11},{10,... | collective-permute-start | bytes 442376 | tf_op jit(solution)/shard_map/ppermute | solution.py:66
  21.2 8.3 %collective-permute-start.9 = (bf16[24,1024]{1,0:T(8,128)(2,1)S(1)}, bf16[24,1024]{1,0:T(8,128)(2,1)S(1)}, u32[]{:S(2)}, u32[]{:S(2)}) collective-permute-start(bf16[24,1024]{1,0:T(8,128)(2,1)S(1)} %get-tuple-element.54), channel_id=1, source_target_pairs={{0,8},{4,12},{8,0},{12,4},{1,9},{5,13},{9,1},{13,5},{2,10},{6,14},... | collective-permute-start | bytes 147464 | tf_op jit(solution)/shard_map/ppermute | solution.py:66
  24.5 7.1 %collective-permute-start.7 = (bf16[24,1024]{1,0:T(8,128)(2,1)S(1)}, bf16[24,1024]{1,0:T(8,128)(2,1)S(1)}, u32[]{:S(2)}, u32[]{:S(2)}) collective-permute-start(bf16[24,1024]{1,0:T(8,128)(2,1)S(1)} %get-tuple-element.53), channel_id=1, source_target_pairs={{0,10},{1,11},{2,8},{3,9},{4,14},{5,15},{6,12},{7,13},{8,2},{9,3},... | collective-permute-start | bytes 147464 | tf_op jit(solution)/shard_map/ppermute | solution.py:376
  25.1 6.5 %collective-permute-start.11 = (bf16[24,1024]{1,0:T(8,128)(2,1)S(1)}, bf16[24,1024]{1,0:T(8,128)(2,1)S(1)}, u32[]{:S(2)}, u32[]{:S(2)}) collective-permute-start(bf16[24,1024]{1,0:T(8,128)(2,1)S(1)} %get-tuple-element.57), channel_id=1, source_target_pairs={{0,12},{4,8},{8,4},{12,0},{1,13},{5,9},{9,5},{13,1},{2,14},{6,10},... | collective-permute-start | bytes 147464 | tf_op jit(solution)/shard_map/ppermute | solution.py:66
  28.3 4.1 %collective-permute-start.12 = (bf16[24,1024]{1,0:T(8,128)(2,1)S(1)}, bf16[24,1024]{1,0:T(8,128)(2,1)S(1)}, u32[]{:S(2)}, u32[]{:S(2)}) collective-permute-start(bf16[24,1024]{1,0:T(8,128)(2,1)S(1)} %get-tuple-element.58), channel_id=1, source_target_pairs={{0,4},{4,0},{8,12},{12,8},{1,5},{5,1},{9,13},{13,9},{2,6},{6,2},{1... | collective-permute-start | bytes 147464 | tf_op jit(solution)/shard_map/ppermute | solution.py:66
  32.8 5.1 %collective-permute-start.13 = (bf16[24,1024]{1,0:T(8,128)(2,1)S(1)}, bf16[24,1024]{1,0:T(8,128)(2,1)S(1)}, u32[]{:S(2)}, u32[]{:S(2)}) collective-permute-start(bf16[24,1024]{1,0:T(8,128)(2,1)S(1)} %get-tuple-element.62), channel_id=1, source_target_pairs={{0,8},{4,12},{8,0},{12,4},{1,9},{5,13},{9,1},{13,5},{2,10},{6,14},... | collective-permute-start | bytes 147464 | tf_op jit(solution)/shard_map/ppermute | solution.py:66
  33.9 5.9 %collective-permute-start.17 = (bf16[24,1024]{1,0:T(8,128)(2,1)S(1)}, bf16[24,1024]{1,0:T(8,128)(2,1)S(1)}, u32[]{:S(2)}, u32[]{:S(2)}) collective-permute-start(bf16[24,1024]{1,0:T(8,128)(2,1)S(1)} %get-tuple-element.63), channel_id=1, source_target_pairs={{0,12},{4,8},{8,4},{12,0},{1,13},{5,9},{9,5},{13,1},{2,14},{6,10},... | collective-permute-start | bytes 147464 | tf_op jit(solution)/shard_map/ppermute | solution.py:66
  36.3 5.0 %collective-permute-start.21 = (bf16[24,1024]{1,0:T(8,128)(2,1)S(1)}, bf16[24,1024]{1,0:T(8,128)(2,1)S(1)}, u32[]{:S(2)}, u32[]{:S(2)}) collective-permute-start(bf16[24,1024]{1,0:T(8,128)(2,1)S(1)} %get-tuple-element.64), channel_id=1, source_target_pairs={{0,4},{4,0},{8,12},{12,8},{1,5},{5,1},{9,13},{13,9},{2,6},{6,2},{1... | collective-permute-start | bytes 147464 | tf_op jit(solution)/shard_map/ppermute | solution.py:66
  36.3 5.6 %collective-permute-start.26 = (bf16[24,1024]{1,0:T(8,128)(2,1)S(1)}, bf16[24,1024]{1,0:T(8,128)(2,1)S(1)}, u32[]{:S(2)}, u32[]{:S(2)}) collective-permute-start(bf16[24,1024]{1,0:T(8,128)(2,1)S(1)} %get-tuple-element.65.refs_6_), channel_id=1, source_target_pairs={{0,2},{1,3},{2,0},{3,1},{4,6},{5,7},{6,4},{7,5},{8,10},{9,11},{10,... | collective-permute-start | bytes 147464 | tf_op jit(solution)/shard_map/ppermute | solution.py:66
  37.8 4.1 %collective-permute-start.25 = (bf16[24,1024]{1,0:T(8,128)(2,1)S(1)}, bf16[24,1024]{1,0:T(8,128)(2,1)S(1)}, u32[]{:S(2)}, u32[]{:S(2)}) collective-permute-start(bf16[24,1024]{1,0:T(8,128)(2,1)S(1)} %get-tuple-element.65.refs_6_), channel_id=1, source_target_pairs={{0,1},{1,0},{2,3},{3,2},{4,5},{5,4},{6,7},{7,6},{8,9},{9,8},{10,11... | collective-permute-start | bytes 147464 | tf_op jit(solution)/shard_map/ppermute | solution.py:66
  37.9 4.5 %collective-permute-start.15 = (bf16[24,1024]{1,0:T(8,128)(2,1)S(1)}, bf16[24,1024]{1,0:T(8,128)(2,1)S(1)}, u32[]{:S(2)}, u32[]{:S(2)}) collective-permute-start(bf16[24,1024]{1,0:T(8,128)(2,1)S(1)} %collective-permute-done.13.refs_0_), channel_id=1, source_target_pairs={{0,2},{1,3},{2,0},{3,1},{4,6},{5,7},{6,4},{7,5},{8,10},{9,11},{10,... | collective-permute-start | bytes 147464 | tf_op jit(solution)/shard_map/ppermute | solution.py:66
  39.8 4.1 %collective-permute-start.19 = (bf16[24,1024]{1,0:T(8,128)(2,1)S(1)}, bf16[24,1024]{1,0:T(8,128)(2,1)S(1)}, u32[]{:S(2)}, u32[]{:S(2)}) collective-permute-start(bf16[24,1024]{1,0:T(8,128)(2,1)S(1)} %collective-permute-done.17.refs_2_), channel_id=1, source_target_pairs={{0,2},{1,3},{2,0},{3,1},{4,6},{5,7},{6,4},{7,5},{8,10},{9,11},{10,... | collective-permute-start | bytes 147464 | tf_op jit(solution)/shard_map/ppermute | solution.py:66
  41.3 4.1 %collective-permute-start.23 = (bf16[24,1024]{1,0:T(8,128)(2,1)S(1)}, bf16[24,1024]{1,0:T(8,128)(2,1)S(1)}, u32[]{:S(2)}, u32[]{:S(2)}) collective-permute-start(bf16[24,1024]{1,0:T(8,128)(2,1)S(1)} %collective-permute-done.21.refs_4_), channel_id=1, source_target_pairs={{0,2},{1,3},{2,0},{3,1},{4,6},{5,7},{6,4},{7,5},{8,10},{9,11},{10,... | collective-permute-start | bytes 147464 | tf_op jit(solution)/shard_map/ppermute | solution.py:66
  41.9 3.5 %collective-permute-start.14 = (bf16[24,1024]{1,0:T(8,128)(2,1)S(1)}, bf16[24,1024]{1,0:T(8,128)(2,1)S(1)}, u32[]{:S(2)}, u32[]{:S(2)}) collective-permute-start(bf16[24,1024]{1,0:T(8,128)(2,1)S(1)} %collective-permute-done.13.refs_0_), channel_id=1, source_target_pairs={{0,1},{1,0},{2,3},{3,2},{4,5},{5,4},{6,7},{7,6},{8,9},{9,8},{10,11... | collective-permute-start | bytes 147464 | tf_op jit(solution)/shard_map/ppermute | solution.py:66
  41.9 4.0 %collective-permute-start.18 = (bf16[24,1024]{1,0:T(8,128)(2,1)S(1)}, bf16[24,1024]{1,0:T(8,128)(2,1)S(1)}, u32[]{:S(2)}, u32[]{:S(2)}) collective-permute-start(bf16[24,1024]{1,0:T(8,128)(2,1)S(1)} %collective-permute-done.17.refs_2_), channel_id=1, source_target_pairs={{0,1},{1,0},{2,3},{3,2},{4,5},{5,4},{6,7},{7,6},{8,9},{9,8},{10,11... | collective-permute-start | bytes 147464 | tf_op jit(solution)/shard_map/ppermute | solution.py:66
  42.4 4.3 %collective-permute-start.22 = (bf16[24,1024]{1,0:T(8,128)(2,1)S(1)}, bf16[24,1024]{1,0:T(8,128)(2,1)S(1)}, u32[]{:S(2)}, u32[]{:S(2)}) collective-permute-start(bf16[24,1024]{1,0:T(8,128)(2,1)S(1)} %collective-permute-done.21.refs_4_), channel_id=1, source_target_pairs={{0,1},{1,0},{2,3},{3,2},{4,5},{5,4},{6,7},{7,6},{8,9},{9,8},{10,11... | collective-permute-start | bytes 147464 | tf_op jit(solution)/shard_map/ppermute | solution.py:66
  50.0 6.0 %collective-permute-start.32 = (bf16[72,1024]{1,0:T(8,128)(2,1)S(1)}, bf16[72,1024]{1,0:T(8,128)(2,1)S(1)}, u32[]{:S(2)}, u32[]{:S(2)}) collective-permute-start(bf16[72,1024]{1,0:T(8,128)(2,1)S(1)} %get-tuple-element.72), channel_id=1, source_target_pairs={{0,2},{1,3},{2,0},{3,1},{4,6},{5,7},{6,4},{7,5},{8,10},{9,11},{10,... | collective-permute-start | bytes 442376 | tf_op jit(solution)/shard_map/ppermute | solution.py:66
  51.0 7.6 %collective-permute-start.31 = (bf16[24,1024]{1,0:T(8,128)(2,1)S(1)}, bf16[24,1024]{1,0:T(8,128)(2,1)S(1)}, u32[]{:S(2)}, u32[]{:S(2)}) collective-permute-start(bf16[24,1024]{1,0:T(8,128)(2,1)S(1)} %get-tuple-element.70), channel_id=1, source_target_pairs={{0,8},{4,12},{8,0},{12,4},{1,9},{5,13},{9,1},{13,5},{2,10},{6,14},... | collective-permute-start | bytes 147464 | tf_op jit(solution)/shard_map/ppermute | solution.py:66
  52.1 7.7 %collective-permute-start.29 = (bf16[24,1024]{1,0:T(8,128)(2,1)S(1)}, bf16[24,1024]{1,0:T(8,128)(2,1)S(1)}, u32[]{:S(2)}, u32[]{:S(2)}) collective-permute-start(bf16[24,1024]{1,0:T(8,128)(2,1)S(1)} %get-tuple-element.69), channel_id=1, source_target_pairs={{0,10},{1,11},{2,8},{3,9},{4,14},{5,15},{6,12},{7,13},{8,2},{9,3},... | collective-permute-start | bytes 147464 | tf_op jit(solution)/shard_map/ppermute | solution.py:376
  56.0 6.0 %collective-permute-start.33 = (bf16[24,1024]{1,0:T(8,128)(2,1)S(1)}, bf16[24,1024]{1,0:T(8,128)(2,1)S(1)}, u32[]{:S(2)}, u32[]{:S(2)}) collective-permute-start(bf16[24,1024]{1,0:T(8,128)(2,1)S(1)} %get-tuple-element.73), channel_id=1, source_target_pairs={{0,12},{4,8},{8,4},{12,0},{1,13},{5,9},{9,5},{13,1},{2,14},{6,10},... | collective-permute-start | bytes 147464 | tf_op jit(solution)/shard_map/ppermute | solution.py:66
  58.6 4.1 %collective-permute-start.34 = (bf16[24,1024]{1,0:T(8,128)(2,1)S(1)}, bf16[24,1024]{1,0:T(8,128)(2,1)S(1)}, u32[]{:S(2)}, u32[]{:S(2)}) collective-permute-start(bf16[24,1024]{1,0:T(8,128)(2,1)S(1)} %get-tuple-element.74), channel_id=1, source_target_pairs={{0,4},{4,0},{8,12},{12,8},{1,5},{5,1},{9,13},{13,9},{2,6},{6,2},{1... | collective-permute-start | bytes 147464 | tf_op jit(solution)/shard_map/ppermute | solution.py:66
  (15 other events, 42.5 us)

commit v15 on v14

--- a/solution.py
+++ b/solution.py
@@ -422,8 +422,8 @@
     return move(own, back, pick, extra, came, order, last)
 
 
-def spread(block, quarter):
-    side = swap(block, "et", 2)
+def spread(block, quarter, side=None):
+    side = swap(block, "et", 2) if side is None else side
     near, far = swap(block, "et", 1), swap(side, "et", 1)
     return [(block, quarter, 0), (side, quarter, 2), (near, quarter, 1), (far, quarter, 3)]
 
@@ -450,7 +450,8 @@
     hidden = front(blocks, flags, order + [0], 0, modulation, router, pair)
     own, *sent = sum_back(hidden, w_down, own, back[0], pick, False)
 
-    blocks = [spread(swap(b, "ep", k) if k else b, quarter) for k, b in enumerate(sent)]
+    sides = {1: diagonal(sent[1], 1, 2)}
+    blocks = [spread(swap(b, "ep", k) if k else b, quarter, sides.get(k)) for k, b in enumerate(sent)]
     hidden = front(blocks, flags, order + [0], 1, modulation, router, pair)
     return tuple(sum_back(hidden, w_down, own, back[1], pick, True))
 

time: 63.7 us -> 63.7 us (level)
    ppermute x2 -> x3, starting transfers between devices: 2.83 us -> 5.92 us  [diagonal(): return lax.ppermute(x, ('ep', 'et'), pairs)]
    ppermute x33 -> x32, starting transfers between devices: 31.4 us -> 28.7 us  [swap(): return lax.ppermute(x, axis, [(i, i ^ bit) for i in range(size)])]
    ppermute x33 -> x32, waiting for transfers between devices: 12.3 us -> 11.8 us  [swap(): return lax.ppermute(x, axis, [(i, i ^ bit) for i in range(size)])]
    ppermute x2 -> x3, waiting for transfers between devices: 3.38 us -> 3.51 us  [diagonal(): return lax.ppermute(x, ('ep', 'et'), pairs)]
  transfers between devices with their start and end apart: 35 -> 35, of which waited for: 18 -> 17; matrix products, arithmetic and copies ran while one was open for 0% -> 0% of each run, Pallas kernels for 12% -> 12%
where the time goes in v15:
time: 63.7 us; the launch traced here: 63.5 us
  starting transfers between devices  34.6 us (54%)
  waiting for transfers between devices  15.3 us (24%)
  Pallas kernels  12.7 us (20%)
  between operations  0.87 us (1%)
    ppermute x32, starting transfers between devices, swap(): return lax.ppermute(x, axis, [(i, i ^ bit) for i in range(size)])  28.7 us
    ppermute x32, waiting for transfers between devices, swap(): return lax.ppermute(x, axis, [(i, i ^ bit) for i in range(size)])  11.8 us
    ppermute x3, starting transfers between devices, diagonal(): return lax.ppermute(x, ('ep', 'et'), pairs)  5.92 us
    pallas_call x1, Pallas kernels, load(): pl.pallas_call(load_kernel, in_specs=[ANY] * 3, out_specs=[VMEM] * 3, out...  3.78 us
    ppermute x3, waiting for transfers between devices, diagonal(): return lax.ppermute(x, ('ep', 'et'), pairs)  3.51 us
    pallas_call x4, Pallas kernels, half_front(): pl.pallas_call(functools.partial(front_kernel, layout, order, flips, sect...  3.35 us
    pallas_call x8, Pallas kernels, down(): pl.pallas_call(functools.partial(down_kernel, flip, len(adds), groups), i...  2.23 us
  transfers between devices with their start and end apart: 35, of which 17 were waited for; matrix products, arithmetic and copies ran while one was open for 0% of the time, Pallas kernels for 12%

profile of v15, /device:TPU:0, one launch (start us, length us, event | category | flops | bytes accessed | tf_op | source)
XLA Modules:
  0.0 63.5 jit_solution(7291435613842189471)
XLA Ops:
  0.6 1.2 %pack.1 = (bf16[24,2176]{1,0:T(8,128)(2,1)S(1)}, bf16[24,2176]{1,0:T(8,128)(2,1)S(1)}, bf16[24,2176]{1,0:T(8,128)(2,1)S(1)}, bf16[32,1024]{1,0:T(8,128)(2,1)S(1)}) custom-call(bf16[32,4096]{1,0:T(8,128)(2,1)} %tokens_ref.3, s32[2,2,32]{2,1,0:T(2,128)} %bitcast.6), custom_call_target="tpu_custom_call" | custom-call | tf_op jit(solution)/shard_map/pack/pallas_call | solution.py:197
  1.9 4.1 %collective-permute-start = (bf16[24,2176]{1,0:T(8,128)(2,1)S(1)}, bf16[24,2176]{1,0:T(8,128)(2,1)S(1)}, u32[]{:S(2)}, u32[]{:S(2)}) collective-permute-start(bf16[24,2176]{1,0:T(8,128)(2,1)S(1)} %get-tuple-element.43), channel_id=1, source_target_pairs={{0,8},{4,12},{8,0},{12,4},{1,9},{5,13},{9,1},{13,5},{2,10},{6,14},... | collective-permute-start | bytes 313352 | tf_op jit(solution)/shard_map/ppermute | solution.py:66
  6.0 1.3 %collective-permute-start.2 = (bf16[24,2176]{1,0:T(8,128)(2,1)S(1)}, bf16[24,2176]{1,0:T(8,128)(2,1)S(1)}, u32[]{:S(2)}, u32[]{:S(2)}) collective-permute-start(bf16[24,2176]{1,0:T(8,128)(2,1)S(1)} %get-tuple-element.45), channel_id=1, source_target_pairs={{0,12},{4,8},{8,4},{12,0},{1,13},{5,9},{9,5},{13,1},{2,14},{6,10},... | collective-permute-start | bytes 313352 | tf_op jit(solution)/shard_map/ppermute | solution.py:66
  7.6 3.8 %load.1 = (bf16[4096,768]{1,0:T(8,128)(2,1)S(1)}, bf16[384,4096]{1,0:T(8,128)(2,1)S(1)}, f32[8,128]{1,0:T(8,128)S(1)}) custom-call(bf16[1,4096,384]{2,1,0:T(8,128)(2,1)} %gate_ref.1, bf16[1,4096,384]{2,1,0:T(8,128)(2,1)} %up_ref.1, bf16[1,384,4096]{2,1,0:T(8,128)(2,1)} %down_ref.1), custom_call_target="tpu_custom_call" | custom-call | bytes 18874368 | tf_op jit(solution)/shard_map/load/pallas_call | solution.py:101
  12.2 2.0 %collective-permute-done.block_ref.refs_7_.refs_11_ = bf16[24,2176]{1,0:T(8,128)(2,1)S(1)} collective-permute-done((bf16[24,2176]{1,0:T(8,128)(2,1)S(1)}, bf16[24,2176]{1,0:T(8,128)(2,1)S(1)}, u32[]{:S(2)}, u32[]{:S(2)}) %collective-permute-start) | collective-permute-done | bytes 104480 | tf_op jit(solution)/shard_map/ppermute | solution.py:66
  16.3 0.9 %front.5.hidden_ref = bf16[96,384]{1,0:T(8,128)(2,1)S(1)} custom-call(bf16[24,2048]{1,0:T(8,128)(2,1)S(1)} %collective-permute-done.1.refs_0_, bf16[24,2048]{1,0:T(8,128)(2,1)S(1)} %collective-permute-done.3.refs_1_, bf16[24,2048]{1,0:T(8,128)(2,1)S(1)} %collective-permute-done.5.refs_2_, bf16[24,4096]{1,0:T(8,128)(2,1)S(1)} %get-tuple-element.47.refs_3_, ...), custom_call_target="tpu_custom_call" | custom-call | flops 301989888 | bytes 3145728 | tf_op jit(solution)/shard_map/front/pallas_call | solution.py:298
  19.0 1.9 %collective-permute-start.10 = (bf16[72,1024]{1,0:T(8,128)(2,1)S(1)}, bf16[72,1024]{1,0:T(8,128)(2,1)S(1)}, u32[]{:S(2)}, u32[]{:S(2)}) collective-permute-start(bf16[72,1024]{1,0:T(8,128)(2,1)S(1)} %get-tuple-element.56), channel_id=1, source_target_pairs={{0,2},{1,3},{2,0},{3,1},{4,6},{5,7},{6,4},{7,5},{8,10},{9,11},{10,... | collective-permute-start | bytes 442376 | tf_op jit(solution)/shard_map/ppermute | solution.py:66
  21.2 3.3 %collective-permute-start.9 = (bf16[24,1024]{1,0:T(8,128)(2,1)S(1)}, bf16[24,1024]{1,0:T(8,128)(2,1)S(1)}, u32[]{:S(2)}, u32[]{:S(2)}) collective-permute-start(bf16[24,1024]{1,0:T(8,128)(2,1)S(1)} %get-tuple-element.54), channel_id=1, source_target_pairs={{0,8},{4,12},{8,0},{12,4},{1,9},{5,13},{9,1},{13,5},{2,10},{6,14},... | collective-permute-start | bytes 147464 | tf_op jit(solution)/shard_map/ppermute | solution.py:66
  25.1 3.2 %collective-permute-start.11 = (bf16[24,1024]{1,0:T(8,128)(2,1)S(1)}, bf16[24,1024]{1,0:T(8,128)(2,1)S(1)}, u32[]{:S(2)}, u32[]{:S(2)}) collective-permute-start(bf16[24,1024]{1,0:T(8,128)(2,1)S(1)} %get-tuple-element.57), channel_id=1, source_target_pairs={{0,12},{4,8},{8,4},{12,0},{1,13},{5,9},{9,5},{13,1},{2,14},{6,10},... | collective-permute-start | bytes 147464 | tf_op jit(solution)/shard_map/ppermute | solution.py:66
  28.3 1.1 %collective-permute-start.12 = (bf16[24,1024]{1,0:T(8,128)(2,1)S(1)}, bf16[24,1024]{1,0:T(8,128)(2,1)S(1)}, u32[]{:S(2)}, u32[]{:S(2)}) collective-permute-start(bf16[24,1024]{1,0:T(8,128)(2,1)S(1)} %get-tuple-element.58), channel_id=1, source_target_pairs={{0,4},{4,0},{8,12},{12,8},{1,5},{5,1},{9,13},{13,9},{2,6},{6,2},{1... | collective-permute-start | bytes 147464 | tf_op jit(solution)/shard_map/ppermute | solution.py:66
  29.5 2.2 %collective-permute-done.7.extra_ref = bf16[24,1024]{1,0:T(8,128)(2,1)S(1)} collective-permute-done((bf16[24,1024]{1,0:T(8,128)(2,1)S(1)}, bf16[24,1024]{1,0:T(8,128)(2,1)S(1)}, u32[]{:S(2)}, u32[]{:S(2)}) %collective-permute-start.7) | collective-permute-done | bytes 49184 | tf_op jit(solution)/shard_map/ppermute | solution.py:376
  32.8 1.1 %collective-permute-start.13 = (bf16[24,1024]{1,0:T(8,128)(2,1)S(1)}, bf16[24,1024]{1,0:T(8,128)(2,1)S(1)}, u32[]{:S(2)}, u32[]{:S(2)}) collective-permute-start(bf16[24,1024]{1,0:T(8,128)(2,1)S(1)} %get-tuple-element.62), channel_id=1, source_target_pairs={{0,8},{4,12},{8,0},{12,4},{1,9},{5,13},{9,1},{13,5},{2,10},{6,14},... | collective-permute-start | bytes 147464 | tf_op jit(solution)/shard_map/ppermute | solution.py:66
  33.9 2.4 %collective-permute-start.17 = (bf16[24,1024]{1,0:T(8,128)(2,1)S(1)}, bf16[24,1024]{1,0:T(8,128)(2,1)S(1)}, u32[]{:S(2)}, u32[]{:S(2)}) collective-permute-start(bf16[24,1024]{1,0:T(8,128)(2,1)S(1)} %get-tuple-element.63), channel_id=1, source_target_pairs={{0,12},{4,8},{8,4},{12,0},{1,13},{5,9},{9,5},{13,1},{2,14},{6,10},... | collective-permute-start | bytes 147464 | tf_op jit(solution)/shard_map/ppermute | solution.py:66
  36.3 3.0 %collective-permute-start.23 = (bf16[24,1024]{1,0:T(8,128)(2,1)S(1)}, bf16[24,1024]{1,0:T(8,128)(2,1)S(1)}, u32[]{:S(2)}, u32[]{:S(2)}) collective-permute-start(bf16[24,1024]{1,0:T(8,128)(2,1)S(1)} %get-tuple-element.64), channel_id=1, source_target_pairs={{0,6},{1,7},{2,4},{3,5},{4,2},{5,3},{6,0},{7,1},{8,14},{9,15},{10,... | collective-permute-start | bytes 147464 | tf_op jit(solution)/shard_map/ppermute | solution.py:376
  39.9 1.5 %collective-permute-start.15 = (bf16[24,1024]{1,0:T(8,128)(2,1)S(1)}, bf16[24,1024]{1,0:T(8,128)(2,1)S(1)}, u32[]{:S(2)}, u32[]{:S(2)}) collective-permute-start(bf16[24,1024]{1,0:T(8,128)(2,1)S(1)} %collective-permute-done.13.refs_0_), channel_id=1, source_target_pairs={{0,2},{1,3},{2,0},{3,1},{4,6},{5,7},{6,4},{7,5},{8,10},{9,11},{10,... | collective-permute-start | bytes 147464 | tf_op jit(solution)/shard_map/ppermute | solution.py:66
  41.9 1.9 %collective-permute-done.26.refs_7_ = bf16[24,1024]{1,0:T(8,128)(2,1)S(1)} collective-permute-done((bf16[24,1024]{1,0:T(8,128)(2,1)S(1)}, bf16[24,1024]{1,0:T(8,128)(2,1)S(1)}, u32[]{:S(2)}, u32[]{:S(2)}) %collective-permute-start.26) | collective-permute-done | bytes 49184 | tf_op jit(solution)/shard_map/ppermute | solution.py:66
  47.2 1.0 %front.7.hidden_ref = bf16[96,384]{1,0:T(8,128)(2,1)S(1)} custom-call(bf16[24,1024]{1,0:T(8,128)(2,1)S(1)} %collective-permute-done.14.refs_0_, bf16[24,1024]{1,0:T(8,128)(2,1)S(1)} %collective-permute-done.16.refs_1_, bf16[24,1024]{1,0:T(8,128)(2,1)S(1)} %collective-permute-done.18.refs_2_, bf16[24,1024]{1,0:T(8,128)(2,1)S(1)} %collective-permute-done.20.refs_3_, ...), custom_call_target="tpu_custom_call" | custom-call | flops 301989888 | bytes 3145728 | tf_op jit(solution)/shard_map/front/pallas_call | solution.py:298
  50.1 1.1 %collective-permute-start.32 = (bf16[72,1024]{1,0:T(8,128)(2,1)S(1)}, bf16[72,1024]{1,0:T(8,128)(2,1)S(1)}, u32[]{:S(2)}, u32[]{:S(2)}) collective-permute-start(bf16[72,1024]{1,0:T(8,128)(2,1)S(1)} %get-tuple-element.72), channel_id=1, source_target_pairs={{0,2},{1,3},{2,0},{3,1},{4,6},{5,7},{6,4},{7,5},{8,10},{9,11},{10,... | collective-permute-start | bytes 442376 | tf_op jit(solution)/shard_map/ppermute | solution.py:66
  52.0 2.9 %collective-permute-start.29 = (bf16[24,1024]{1,0:T(8,128)(2,1)S(1)}, bf16[24,1024]{1,0:T(8,128)(2,1)S(1)}, u32[]{:S(2)}, u32[]{:S(2)}) collective-permute-start(bf16[24,1024]{1,0:T(8,128)(2,1)S(1)} %get-tuple-element.69), channel_id=1, source_target_pairs={{0,10},{1,11},{2,8},{3,9},{4,14},{5,15},{6,12},{7,13},{8,2},{9,3},... | collective-permute-start | bytes 147464 | tf_op jit(solution)/shard_map/ppermute | solution.py:376
  54.9 1.2 %collective-permute-done.32.came_ref = bf16[72,1024]{1,0:T(8,128)(2,1)S(1)} collective-permute-done((bf16[72,1024]{1,0:T(8,128)(2,1)S(1)}, bf16[72,1024]{1,0:T(8,128)(2,1)S(1)}, u32[]{:S(2)}, u32[]{:S(2)}) %collective-permute-start.32) | collective-permute-done | bytes 147488 | tf_op jit(solution)/shard_map/ppermute | solution.py:66
  56.1 2.5 %collective-permute-start.33 = (bf16[24,1024]{1,0:T(8,128)(2,1)S(1)}, bf16[24,1024]{1,0:T(8,128)(2,1)S(1)}, u32[]{:S(2)}, u32[]{:S(2)}) collective-permute-start(bf16[24,1024]{1,0:T(8,128)(2,1)S(1)} %get-tuple-element.73), channel_id=1, source_target_pairs={{0,12},{4,8},{8,4},{12,0},{1,13},{5,9},{9,5},{13,1},{2,14},{6,10},... | collective-permute-start | bytes 147464 | tf_op jit(solution)/shard_map/ppermute | solution.py:66
  58.6 1.3 %collective-permute-done.29.extra_ref = bf16[24,1024]{1,0:T(8,128)(2,1)S(1)} collective-permute-done((bf16[24,1024]{1,0:T(8,128)(2,1)S(1)}, bf16[24,1024]{1,0:T(8,128)(2,1)S(1)}, u32[]{:S(2)}, u32[]{:S(2)}) %collective-permute-start.29) | collective-permute-done | bytes 49184 | tf_op jit(solution)/shard_map/ppermute | solution.py:376
  59.9 2.1 %collective-permute-done.33.refs_1_ = bf16[24,1024]{1,0:T(8,128)(2,1)S(1)} collective-permute-done((bf16[24,1024]{1,0:T(8,128)(2,1)S(1)}, bf16[24,1024]{1,0:T(8,128)(2,1)S(1)}, u32[]{:S(2)}, u32[]{:S(2)}) %collective-permute-start.33) | collective-permute-done | bytes 49184 | tf_op jit(solution)/shard_map/ppermute | solution.py:66
  62.7 0.8 %move.3 = (bf16[32,1024]{1,0:T(8,128)(2,1)}, bf16[32,1024]{1,0:T(8,128)(2,1)}) custom-call(bf16[32,1024]{1,0:T(8,128)(2,1)S(1)} %get-tuple-element.60.own_ref, bf16[32,96]{1,0:T(8,128)(2,1)S(1)} %get-tuple-element.61.back_ref, bf16[96,32]{1,0:T(8,128)(2,1)S(1)} %get-tuple-element.42.pick_ref, bf16[24,1024]{1,0:T(8,128)(2,1)S(1)} %collective-permute-done.29.extra_ref, ...), custom_call_target="tpu_custom_call" | custom-call | tf_op jit(solution)/shard_map/move/pallas_call | solution.py:397
  (78 shorter events, 14.7 us)
Async XLA Ops:
  1.9 12.4 %collective-permute-start = (bf16[24,2176]{1,0:T(8,128)(2,1)S(1)}, bf16[24,2176]{1,0:T(8,128)(2,1)S(1)}, u32[]{:S(2)}, u32[]{:S(2)}) collective-permute-start(bf16[24,2176]{1,0:T(8,128)(2,1)S(1)} %get-tuple-element.43), channel_id=1, source_target_pairs={{0,8},{4,12},{8,0},{12,4},{1,9},{5,13},{9,1},{13,5},{2,10},{6,14},... | collective-permute-start | bytes 313352 | tf_op jit(solution)/shard_map/ppermute | solution.py:66
  6.0 8.4 %collective-permute-start.2 = (bf16[24,2176]{1,0:T(8,128)(2,1)S(1)}, bf16[24,2176]{1,0:T(8,128)(2,1)S(1)}, u32[]{:S(2)}, u32[]{:S(2)}) collective-permute-start(bf16[24,2176]{1,0:T(8,128)(2,1)S(1)} %get-tuple-element.45), channel_id=1, source_target_pairs={{0,12},{4,8},{8,4},{12,0},{1,13},{5,9},{9,5},{13,1},{2,14},{6,10},... | collective-permute-start | bytes 313352 | tf_op jit(solution)/shard_map/ppermute | solution.py:66
  7.3 7.6 %collective-permute-start.4 = (bf16[24,2176]{1,0:T(8,128)(2,1)S(1)}, bf16[24,2176]{1,0:T(8,128)(2,1)S(1)}, u32[]{:S(2)}, u32[]{:S(2)}) collective-permute-start(bf16[24,2176]{1,0:T(8,128)(2,1)S(1)} %get-tuple-element.46), channel_id=1, source_target_pairs={{0,4},{4,0},{8,12},{12,8},{1,5},{5,1},{9,13},{13,9},{2,6},{6,2},{1... | collective-permute-start | bytes 313352 | tf_op jit(solution)/shard_map/ppermute | solution.py:66
  18.0 3.0 %collective-permute-start.8 = (bf16[96,1024]{1,0:T(8,128)(2,1)S(1)}, bf16[96,1024]{1,0:T(8,128)(2,1)S(1)}, u32[]{:S(2)}, u32[]{:S(2)}) collective-permute-start(bf16[96,1024]{1,0:T(8,128)(2,1)S(1)} %down.10), channel_id=1, source_target_pairs={{0,1},{1,0},{2,3},{3,2},{4,5},{5,4},{6,7},{7,6},{8,9},{9,8},{10,11... | collective-permute-start | bytes 589832 | tf_op jit(solution)/shard_map/ppermute | solution.py:66
  19.0 6.1 %collective-permute-start.10 = (bf16[72,1024]{1,0:T(8,128)(2,1)S(1)}, bf16[72,1024]{1,0:T(8,128)(2,1)S(1)}, u32[]{:S(2)}, u32[]{:S(2)}) collective-permute-start(bf16[72,1024]{1,0:T(8,128)(2,1)S(1)} %get-tuple-element.56), channel_id=1, source_target_pairs={{0,2},{1,3},{2,0},{3,1},{4,6},{5,7},{6,4},{7,5},{8,10},{9,11},{10,... | collective-permute-start | bytes 442376 | tf_op jit(solution)/shard_map/ppermute | solution.py:66
  21.2 8.3 %collective-permute-start.9 = (bf16[24,1024]{1,0:T(8,128)(2,1)S(1)}, bf16[24,1024]{1,0:T(8,128)(2,1)S(1)}, u32[]{:S(2)}, u32[]{:S(2)}) collective-permute-start(bf16[24,1024]{1,0:T(8,128)(2,1)S(1)} %get-tuple-element.54), channel_id=1, source_target_pairs={{0,8},{4,12},{8,0},{12,4},{1,9},{5,13},{9,1},{13,5},{2,10},{6,14},... | collective-permute-start | bytes 147464 | tf_op jit(solution)/shard_map/ppermute | solution.py:66
  24.5 7.1 %collective-permute-start.7 = (bf16[24,1024]{1,0:T(8,128)(2,1)S(1)}, bf16[24,1024]{1,0:T(8,128)(2,1)S(1)}, u32[]{:S(2)}, u32[]{:S(2)}) collective-permute-start(bf16[24,1024]{1,0:T(8,128)(2,1)S(1)} %get-tuple-element.53), channel_id=1, source_target_pairs={{0,10},{1,11},{2,8},{3,9},{4,14},{5,15},{6,12},{7,13},{8,2},{9,3},... | collective-permute-start | bytes 147464 | tf_op jit(solution)/shard_map/ppermute | solution.py:376
  25.1 6.5 %collective-permute-start.11 = (bf16[24,1024]{1,0:T(8,128)(2,1)S(1)}, bf16[24,1024]{1,0:T(8,128)(2,1)S(1)}, u32[]{:S(2)}, u32[]{:S(2)}) collective-permute-start(bf16[24,1024]{1,0:T(8,128)(2,1)S(1)} %get-tuple-element.57), channel_id=1, source_target_pairs={{0,12},{4,8},{8,4},{12,0},{1,13},{5,9},{9,5},{13,1},{2,14},{6,10},... | collective-permute-start | bytes 147464 | tf_op jit(solution)/shard_map/ppermute | solution.py:66
  28.3 4.1 %collective-permute-start.12 = (bf16[24,1024]{1,0:T(8,128)(2,1)S(1)}, bf16[24,1024]{1,0:T(8,128)(2,1)S(1)}, u32[]{:S(2)}, u32[]{:S(2)}) collective-permute-start(bf16[24,1024]{1,0:T(8,128)(2,1)S(1)} %get-tuple-element.58), channel_id=1, source_target_pairs={{0,4},{4,0},{8,12},{12,8},{1,5},{5,1},{9,13},{13,9},{2,6},{6,2},{1... | collective-permute-start | bytes 147464 | tf_op jit(solution)/shard_map/ppermute | solution.py:66
  32.8 7.0 %collective-permute-start.13 = (bf16[24,1024]{1,0:T(8,128)(2,1)S(1)}, bf16[24,1024]{1,0:T(8,128)(2,1)S(1)}, u32[]{:S(2)}, u32[]{:S(2)}) collective-permute-start(bf16[24,1024]{1,0:T(8,128)(2,1)S(1)} %get-tuple-element.62), channel_id=1, source_target_pairs={{0,8},{4,12},{8,0},{12,4},{1,9},{5,13},{9,1},{13,5},{2,10},{6,14},... | collective-permute-start | bytes 147464 | tf_op jit(solution)/shard_map/ppermute | solution.py:66
  33.9 6.0 %collective-permute-start.17 = (bf16[24,1024]{1,0:T(8,128)(2,1)S(1)}, bf16[24,1024]{1,0:T(8,128)(2,1)S(1)}, u32[]{:S(2)}, u32[]{:S(2)}) collective-permute-start(bf16[24,1024]{1,0:T(8,128)(2,1)S(1)} %get-tuple-element.63), channel_id=1, source_target_pairs={{0,12},{4,8},{8,4},{12,0},{1,13},{5,9},{9,5},{13,1},{2,14},{6,10},... | collective-permute-start | bytes 147464 | tf_op jit(solution)/shard_map/ppermute | solution.py:66
  36.3 5.1 %collective-permute-start.21 = (bf16[24,1024]{1,0:T(8,128)(2,1)S(1)}, bf16[24,1024]{1,0:T(8,128)(2,1)S(1)}, u32[]{:S(2)}, u32[]{:S(2)}) collective-permute-start(bf16[24,1024]{1,0:T(8,128)(2,1)S(1)} %get-tuple-element.64), channel_id=1, source_target_pairs={{0,4},{4,0},{8,12},{12,8},{1,5},{5,1},{9,13},{13,9},{2,6},{6,2},{1... | collective-permute-start | bytes 147464 | tf_op jit(solution)/shard_map/ppermute | solution.py:66
  36.3 5.6 %collective-permute-start.23 = (bf16[24,1024]{1,0:T(8,128)(2,1)S(1)}, bf16[24,1024]{1,0:T(8,128)(2,1)S(1)}, u32[]{:S(2)}, u32[]{:S(2)}) collective-permute-start(bf16[24,1024]{1,0:T(8,128)(2,1)S(1)} %get-tuple-element.64), channel_id=1, source_target_pairs={{0,6},{1,7},{2,4},{3,5},{4,2},{5,3},{6,0},{7,1},{8,14},{9,15},{10,... | collective-permute-start | bytes 147464 | tf_op jit(solution)/shard_map/ppermute | solution.py:376
  39.3 4.5 %collective-permute-start.26 = (bf16[24,1024]{1,0:T(8,128)(2,1)S(1)}, bf16[24,1024]{1,0:T(8,128)(2,1)S(1)}, u32[]{:S(2)}, u32[]{:S(2)}) collective-permute-start(bf16[24,1024]{1,0:T(8,128)(2,1)S(1)} %get-tuple-element.65.refs_6_), channel_id=1, source_target_pairs={{0,2},{1,3},{2,0},{3,1},{4,6},{5,7},{6,4},{7,5},{8,10},{9,11},{10,... | collective-permute-start | bytes 147464 | tf_op jit(solution)/shard_map/ppermute | solution.py:66
  39.8 4.0 %collective-permute-start.25 = (bf16[24,1024]{1,0:T(8,128)(2,1)S(1)}, bf16[24,1024]{1,0:T(8,128)(2,1)S(1)}, u32[]{:S(2)}, u32[]{:S(2)}) collective-permute-start(bf16[24,1024]{1,0:T(8,128)(2,1)S(1)} %get-tuple-element.65.refs_6_), channel_id=1, source_target_pairs={{0,1},{1,0},{2,3},{3,2},{4,5},{5,4},{6,7},{7,6},{8,9},{9,8},{10,11... | collective-permute-start | bytes 147464 | tf_op jit(solution)/shard_map/ppermute | solution.py:66
  39.9 4.8 %collective-permute-start.15 = (bf16[24,1024]{1,0:T(8,128)(2,1)S(1)}, bf16[24,1024]{1,0:T(8,128)(2,1)S(1)}, u32[]{:S(2)}, u32[]{:S(2)}) collective-permute-start(bf16[24,1024]{1,0:T(8,128)(2,1)S(1)} %collective-permute-done.13.refs_0_), channel_id=1, source_target_pairs={{0,2},{1,3},{2,0},{3,1},{4,6},{5,7},{6,4},{7,5},{8,10},{9,11},{10,... | collective-permute-start | bytes 147464 | tf_op jit(solution)/shard_map/ppermute | solution.py:66
  41.4 4.1 %collective-permute-start.19 = (bf16[24,1024]{1,0:T(8,128)(2,1)S(1)}, bf16[24,1024]{1,0:T(8,128)(2,1)S(1)}, u32[]{:S(2)}, u32[]{:S(2)}) collective-permute-start(bf16[24,1024]{1,0:T(8,128)(2,1)S(1)} %collective-permute-done.17.refs_2_), channel_id=1, source_target_pairs={{0,2},{1,3},{2,0},{3,1},{4,6},{5,7},{6,4},{7,5},{8,10},{9,11},{10,... | collective-permute-start | bytes 147464 | tf_op jit(solution)/shard_map/ppermute | solution.py:66
  41.9 3.6 %collective-permute-start.14 = (bf16[24,1024]{1,0:T(8,128)(2,1)S(1)}, bf16[24,1024]{1,0:T(8,128)(2,1)S(1)}, u32[]{:S(2)}, u32[]{:S(2)}) collective-permute-start(bf16[24,1024]{1,0:T(8,128)(2,1)S(1)} %collective-permute-done.13.refs_0_), channel_id=1, source_target_pairs={{0,1},{1,0},{2,3},{3,2},{4,5},{5,4},{6,7},{7,6},{8,9},{9,8},{10,11... | collective-permute-start | bytes 147464 | tf_op jit(solution)/shard_map/ppermute | solution.py:66
  43.8 3.0 %collective-permute-start.22 = (bf16[24,1024]{1,0:T(8,128)(2,1)S(1)}, bf16[24,1024]{1,0:T(8,128)(2,1)S(1)}, u32[]{:S(2)}, u32[]{:S(2)}) collective-permute-start(bf16[24,1024]{1,0:T(8,128)(2,1)S(1)} %collective-permute-done.21.refs_4_), channel_id=1, source_target_pairs={{0,1},{1,0},{2,3},{3,2},{4,5},{5,4},{6,7},{7,6},{8,9},{9,8},{10,11... | collective-permute-start | bytes 147464 | tf_op jit(solution)/shard_map/ppermute | solution.py:66
  50.1 6.0 %collective-permute-start.32 = (bf16[72,1024]{1,0:T(8,128)(2,1)S(1)}, bf16[72,1024]{1,0:T(8,128)(2,1)S(1)}, u32[]{:S(2)}, u32[]{:S(2)}) collective-permute-start(bf16[72,1024]{1,0:T(8,128)(2,1)S(1)} %get-tuple-element.72), channel_id=1, source_target_pairs={{0,2},{1,3},{2,0},{3,1},{4,6},{5,7},{6,4},{7,5},{8,10},{9,11},{10,... | collective-permute-start | bytes 442376 | tf_op jit(solution)/shard_map/ppermute | solution.py:66
  51.5 7.1 %collective-permute-start.31 = (bf16[24,1024]{1,0:T(8,128)(2,1)S(1)}, bf16[24,1024]{1,0:T(8,128)(2,1)S(1)}, u32[]{:S(2)}, u32[]{:S(2)}) collective-permute-start(bf16[24,1024]{1,0:T(8,128)(2,1)S(1)} %get-tuple-element.70), channel_id=1, source_target_pairs={{0,8},{4,12},{8,0},{12,4},{1,9},{5,13},{9,1},{13,5},{2,10},{6,14},... | collective-permute-start | bytes 147464 | tf_op jit(solution)/shard_map/ppermute | solution.py:66
  52.0 7.9 %collective-permute-start.29 = (bf16[24,1024]{1,0:T(8,128)(2,1)S(1)}, bf16[24,1024]{1,0:T(8,128)(2,1)S(1)}, u32[]{:S(2)}, u32[]{:S(2)}) collective-permute-start(bf16[24,1024]{1,0:T(8,128)(2,1)S(1)} %get-tuple-element.69), channel_id=1, source_target_pairs={{0,10},{1,11},{2,8},{3,9},{4,14},{5,15},{6,12},{7,13},{8,2},{9,3},... | collective-permute-start | bytes 147464 | tf_op jit(solution)/shard_map/ppermute | solution.py:376
  56.1 6.0 %collective-permute-start.33 = (bf16[24,1024]{1,0:T(8,128)(2,1)S(1)}, bf16[24,1024]{1,0:T(8,128)(2,1)S(1)}, u32[]{:S(2)}, u32[]{:S(2)}) collective-permute-start(bf16[24,1024]{1,0:T(8,128)(2,1)S(1)} %get-tuple-element.73), channel_id=1, source_target_pairs={{0,12},{4,8},{8,4},{12,0},{1,13},{5,9},{9,5},{13,1},{2,14},{6,10},... | collective-permute-start | bytes 147464 | tf_op jit(solution)/shard_map/ppermute | solution.py:66
  58.6 4.1 %collective-permute-start.34 = (bf16[24,1024]{1,0:T(8,128)(2,1)S(1)}, bf16[24,1024]{1,0:T(8,128)(2,1)S(1)}, u32[]{:S(2)}, u32[]{:S(2)}) collective-permute-start(bf16[24,1024]{1,0:T(8,128)(2,1)S(1)} %get-tuple-element.74), channel_id=1, source_target_pairs={{0,4},{4,0},{8,12},{12,8},{1,5},{5,1},{9,13},{13,9},{2,6},{6,2},{1... | collective-permute-start | bytes 147464 | tf_op jit(solution)/shard_map/ppermute | solution.py:66
  (15 other events, 41.5 us)

commit v16 on v14

--- a/solution.py
+++ b/solution.py
@@ -402,7 +402,7 @@
     )(own, back, pick, extra, *[came[k] for k in order])
 
 
-DIRECT = 2
+DIRECT = 3
 
 
 def sum_back(hidden, w_down, own, back, pick, last):

time: 63.7 us -> 63.1 us (level)
  waiting for transfers between devices: 15.7 us -> 14.4 us
    ppermute x33, waiting for transfers between devices: 12.3 us -> 10.5 us  [swap(): return lax.ppermute(x, axis, [(i, i ^ bit) for i in range(size)])]
  transfers between devices with their start and end apart: 35 -> 35, of which waited for: 18 -> 17; matrix products, arithmetic and copies ran while one was open for 0% -> 0% of each run, Pallas kernels for 12% -> 13%
where the time goes in v16:
time: 63.1 us; the launch traced here: 62.9 us
  starting transfers between devices  34.9 us (55%)
  waiting for transfers between devices  14.4 us (23%)
  Pallas kernels  12.7 us (20%)
  between operations  0.87 us (1%)
    ppermute x33, starting transfers between devices, swap(): return lax.ppermute(x, axis, [(i, i ^ bit) for i in range(size)])  31.5 us
    ppermute x33, waiting for transfers between devices, swap(): return lax.ppermute(x, axis, [(i, i ^ bit) for i in range(size)])  10.5 us
    ppermute x2, waiting for transfers between devices, diagonal(): return lax.ppermute(x, ('ep', 'et'), pairs)  3.97 us
    pallas_call x1, Pallas kernels, load(): pl.pallas_call(load_kernel, in_specs=[ANY] * 3, out_specs=[VMEM] * 3, out...  3.78 us
    ppermute x2, starting transfers between devices, diagonal(): return lax.ppermute(x, ('ep', 'et'), pairs)  3.43 us
    pallas_call x4, Pallas kernels, half_front(): pl.pallas_call(functools.partial(front_kernel, layout, order, flips, sect...  3.34 us
    pallas_call x8, Pallas kernels, down(): pl.pallas_call(functools.partial(down_kernel, flip, len(adds), groups), i...  2.23 us
  transfers between devices with their start and end apart: 35, of which 17 were waited for; matrix products, arithmetic and copies ran while one was open for 0% of the time, Pallas kernels for 13%

profile of v16, /device:TPU:0, one launch (start us, length us, event | category | flops | bytes accessed | tf_op | source)
XLA Modules:
  0.0 62.9 jit_solution(15639052279607334446)
XLA Ops:
  0.6 1.2 %pack.1 = (bf16[24,2176]{1,0:T(8,128)(2,1)S(1)}, bf16[24,2176]{1,0:T(8,128)(2,1)S(1)}, bf16[24,2176]{1,0:T(8,128)(2,1)S(1)}, bf16[32,1024]{1,0:T(8,128)(2,1)S(1)}) custom-call(bf16[32,4096]{1,0:T(8,128)(2,1)} %tokens_ref.3, s32[2,2,32]{2,1,0:T(2,128)} %bitcast.6), custom_call_target="tpu_custom_call" | custom-call | tf_op jit(solution)/shard_map/pack/pallas_call | solution.py:197
  1.9 4.1 %collective-permute-start = (bf16[24,2176]{1,0:T(8,128)(2,1)S(1)}, bf16[24,2176]{1,0:T(8,128)(2,1)S(1)}, u32[]{:S(2)}, u32[]{:S(2)}) collective-permute-start(bf16[24,2176]{1,0:T(8,128)(2,1)S(1)} %get-tuple-element.43), channel_id=1, source_target_pairs={{0,8},{4,12},{8,0},{12,4},{1,9},{5,13},{9,1},{13,5},{2,10},{6,14},... | collective-permute-start | bytes 313352 | tf_op jit(solution)/shard_map/ppermute | solution.py:66
  6.0 1.3 %collective-permute-start.2 = (bf16[24,2176]{1,0:T(8,128)(2,1)S(1)}, bf16[24,2176]{1,0:T(8,128)(2,1)S(1)}, u32[]{:S(2)}, u32[]{:S(2)}) collective-permute-start(bf16[24,2176]{1,0:T(8,128)(2,1)S(1)} %get-tuple-element.45), channel_id=1, source_target_pairs={{0,12},{4,8},{8,4},{12,0},{1,13},{5,9},{9,5},{13,1},{2,14},{6,10},... | collective-permute-start | bytes 313352 | tf_op jit(solution)/shard_map/ppermute | solution.py:66
  7.6 3.8 %load.1 = (bf16[4096,768]{1,0:T(8,128)(2,1)S(1)}, bf16[384,4096]{1,0:T(8,128)(2,1)S(1)}, f32[8,128]{1,0:T(8,128)S(1)}) custom-call(bf16[1,4096,384]{2,1,0:T(8,128)(2,1)} %gate_ref.1, bf16[1,4096,384]{2,1,0:T(8,128)(2,1)} %up_ref.1, bf16[1,384,4096]{2,1,0:T(8,128)(2,1)} %down_ref.1), custom_call_target="tpu_custom_call" | custom-call | bytes 18874368 | tf_op jit(solution)/shard_map/load/pallas_call | solution.py:101
  12.2 2.0 %collective-permute-done.block_ref.refs_7_.refs_11_ = bf16[24,2176]{1,0:T(8,128)(2,1)S(1)} collective-permute-done((bf16[24,2176]{1,0:T(8,128)(2,1)S(1)}, bf16[24,2176]{1,0:T(8,128)(2,1)S(1)}, u32[]{:S(2)}, u32[]{:S(2)}) %collective-permute-start) | collective-permute-done | bytes 104480 | tf_op jit(solution)/shard_map/ppermute | solution.py:66
  19.0 1.9 %collective-permute-start.9 = (bf16[72,1024]{1,0:T(8,128)(2,1)S(1)}, bf16[72,1024]{1,0:T(8,128)(2,1)S(1)}, u32[]{:S(2)}, u32[]{:S(2)}) collective-permute-start(bf16[72,1024]{1,0:T(8,128)(2,1)S(1)} %get-tuple-element.55), channel_id=1, source_target_pairs={{0,2},{1,3},{2,0},{3,1},{4,6},{5,7},{6,4},{7,5},{8,10},{9,11},{10,... | collective-permute-start | bytes 442376 | tf_op jit(solution)/shard_map/ppermute | solution.py:66
  21.2 3.0 %collective-permute-start.11 = (bf16[24,1024]{1,0:T(8,128)(2,1)S(1)}, bf16[24,1024]{1,0:T(8,128)(2,1)S(1)}, u32[]{:S(2)}, u32[]{:S(2)}) collective-permute-start(bf16[24,1024]{1,0:T(8,128)(2,1)S(1)} %get-tuple-element.57), channel_id=1, source_target_pairs={{0,12},{4,8},{8,4},{12,0},{1,13},{5,9},{9,5},{13,1},{2,14},{6,10},... | collective-permute-start | bytes 147464 | tf_op jit(solution)/shard_map/ppermute | solution.py:66
  25.1 3.9 %collective-permute-start.10 = (bf16[24,1024]{1,0:T(8,128)(2,1)S(1)}, bf16[24,1024]{1,0:T(8,128)(2,1)S(1)}, u32[]{:S(2)}, u32[]{:S(2)}) collective-permute-start(bf16[24,1024]{1,0:T(8,128)(2,1)S(1)} %get-tuple-element.56), channel_id=1, source_target_pairs={{0,8},{4,12},{8,0},{12,4},{1,9},{5,13},{9,1},{13,5},{2,10},{6,14},... | collective-permute-start | bytes 147464 | tf_op jit(solution)/shard_map/ppermute | solution.py:66
  29.0 2.5 %collective-permute-done.7.extra_ref = bf16[24,1024]{1,0:T(8,128)(2,1)S(1)} collective-permute-done((bf16[24,1024]{1,0:T(8,128)(2,1)S(1)}, bf16[24,1024]{1,0:T(8,128)(2,1)S(1)}, u32[]{:S(2)}, u32[]{:S(2)}) %collective-permute-start.7) | collective-permute-done | bytes 49184 | tf_op jit(solution)/shard_map/ppermute | solution.py:376
  31.9 1.2 %collective-permute-done.12.refs_2_ = bf16[24,1024]{1,0:T(8,128)(2,1)S(1)} collective-permute-done((bf16[24,1024]{1,0:T(8,128)(2,1)S(1)}, bf16[24,1024]{1,0:T(8,128)(2,1)S(1)}, u32[]{:S(2)}, u32[]{:S(2)}) %collective-permute-start.12) | collective-permute-done | bytes 49184 | tf_op jit(solution)/shard_map/ppermute | solution.py:66
  33.4 1.0 %collective-permute-start.13 = (bf16[24,1024]{1,0:T(8,128)(2,1)S(1)}, bf16[24,1024]{1,0:T(8,128)(2,1)S(1)}, u32[]{:S(2)}, u32[]{:S(2)}) collective-permute-start(bf16[24,1024]{1,0:T(8,128)(2,1)S(1)} %get-tuple-element.62), channel_id=1, source_target_pairs={{0,8},{4,12},{8,0},{12,4},{1,9},{5,13},{9,1},{13,5},{2,10},{6,14},... | collective-permute-start | bytes 147464 | tf_op jit(solution)/shard_map/ppermute | solution.py:66
  34.4 2.0 %collective-permute-start.17 = (bf16[24,1024]{1,0:T(8,128)(2,1)S(1)}, bf16[24,1024]{1,0:T(8,128)(2,1)S(1)}, u32[]{:S(2)}, u32[]{:S(2)}) collective-permute-start(bf16[24,1024]{1,0:T(8,128)(2,1)S(1)} %get-tuple-element.63), channel_id=1, source_target_pairs={{0,12},{4,8},{8,4},{12,0},{1,13},{5,9},{9,5},{13,1},{2,14},{6,10},... | collective-permute-start | bytes 147464 | tf_op jit(solution)/shard_map/ppermute | solution.py:66
  37.0 1.4 %collective-permute-start.26 = (bf16[24,1024]{1,0:T(8,128)(2,1)S(1)}, bf16[24,1024]{1,0:T(8,128)(2,1)S(1)}, u32[]{:S(2)}, u32[]{:S(2)}) collective-permute-start(bf16[24,1024]{1,0:T(8,128)(2,1)S(1)} %get-tuple-element.65.refs_6_), channel_id=1, source_target_pairs={{0,2},{1,3},{2,0},{3,1},{4,6},{5,7},{6,4},{7,5},{8,10},{9,11},{10,... | collective-permute-start | bytes 147464 | tf_op jit(solution)/shard_map/ppermute | solution.py:66
  39.0 1.4 %collective-permute-start.15 = (bf16[24,1024]{1,0:T(8,128)(2,1)S(1)}, bf16[24,1024]{1,0:T(8,128)(2,1)S(1)}, u32[]{:S(2)}, u32[]{:S(2)}) collective-permute-start(bf16[24,1024]{1,0:T(8,128)(2,1)S(1)} %collective-permute-done.13.refs_0_), channel_id=1, source_target_pairs={{0,2},{1,3},{2,0},{3,1},{4,6},{5,7},{6,4},{7,5},{8,10},{9,11},{10,... | collective-permute-start | bytes 147464 | tf_op jit(solution)/shard_map/ppermute | solution.py:66
  40.4 1.3 %collective-permute-start.19 = (bf16[24,1024]{1,0:T(8,128)(2,1)S(1)}, bf16[24,1024]{1,0:T(8,128)(2,1)S(1)}, u32[]{:S(2)}, u32[]{:S(2)}) collective-permute-start(bf16[24,1024]{1,0:T(8,128)(2,1)S(1)} %collective-permute-done.17.refs_2_), channel_id=1, source_target_pairs={{0,2},{1,3},{2,0},{3,1},{4,6},{5,7},{6,4},{7,5},{8,10},{9,11},{10,... | collective-permute-start | bytes 147464 | tf_op jit(solution)/shard_map/ppermute | solution.py:66
  43.3 1.2 %collective-permute-done.19.refs_3_ = bf16[24,1024]{1,0:T(8,128)(2,1)S(1)} collective-permute-done((bf16[24,1024]{1,0:T(8,128)(2,1)S(1)}, bf16[24,1024]{1,0:T(8,128)(2,1)S(1)}, u32[]{:S(2)}, u32[]{:S(2)}) %collective-permute-start.19) | collective-permute-done | bytes 49184 | tf_op jit(solution)/shard_map/ppermute | solution.py:66
  44.5 1.3 %collective-permute-done.23.refs_5_ = bf16[24,1024]{1,0:T(8,128)(2,1)S(1)} collective-permute-done((bf16[24,1024]{1,0:T(8,128)(2,1)S(1)}, bf16[24,1024]{1,0:T(8,128)(2,1)S(1)}, u32[]{:S(2)}, u32[]{:S(2)}) %collective-permute-start.23) | collective-permute-done | bytes 49184 | tf_op jit(solution)/shard_map/ppermute | solution.py:66
  47.6 1.0 %front.7.hidden_ref = bf16[96,384]{1,0:T(8,128)(2,1)S(1)} custom-call(bf16[24,1024]{1,0:T(8,128)(2,1)S(1)} %collective-permute-done.14.refs_0_, bf16[24,1024]{1,0:T(8,128)(2,1)S(1)} %collective-permute-done.16.refs_1_, bf16[24,1024]{1,0:T(8,128)(2,1)S(1)} %collective-permute-done.18.refs_2_, bf16[24,1024]{1,0:T(8,128)(2,1)S(1)} %collective-permute-done.20.refs_3_, ...), custom_call_target="tpu_custom_call" | custom-call | flops 301989888 | bytes 3145728 | tf_op jit(solution)/shard_map/front/pallas_call | solution.py:298
  51.5 2.0 %collective-permute-start.33 = (bf16[24,1024]{1,0:T(8,128)(2,1)S(1)}, bf16[24,1024]{1,0:T(8,128)(2,1)S(1)}, u32[]{:S(2)}, u32[]{:S(2)}) collective-permute-start(bf16[24,1024]{1,0:T(8,128)(2,1)S(1)} %get-tuple-element.73), channel_id=1, source_target_pairs={{0,12},{4,8},{8,4},{12,0},{1,13},{5,9},{9,5},{13,1},{2,14},{6,10},... | collective-permute-start | bytes 147464 | tf_op jit(solution)/shard_map/ppermute | solution.py:66
  53.5 2.7 %collective-permute-start.29 = (bf16[24,1024]{1,0:T(8,128)(2,1)S(1)}, bf16[24,1024]{1,0:T(8,128)(2,1)S(1)}, u32[]{:S(2)}, u32[]{:S(2)}) collective-permute-start(bf16[24,1024]{1,0:T(8,128)(2,1)S(1)} %get-tuple-element.69), channel_id=1, source_target_pairs={{0,14},{1,15},{2,12},{3,13},{4,10},{5,11},{6,8},{7,9},{8,6},{9,7},... | collective-permute-start | bytes 147464 | tf_op jit(solution)/shard_map/ppermute | solution.py:376
  56.5 1.1 %collective-permute-start.32 = (bf16[24,1024]{1,0:T(8,128)(2,1)S(1)}, bf16[24,1024]{1,0:T(8,128)(2,1)S(1)}, u32[]{:S(2)}, u32[]{:S(2)}) collective-permute-start(bf16[24,1024]{1,0:T(8,128)(2,1)S(1)} %get-tuple-element.72), channel_id=1, source_target_pairs={{0,8},{4,12},{8,0},{12,4},{1,9},{5,13},{9,1},{13,5},{2,10},{6,14},... | collective-permute-start | bytes 147464 | tf_op jit(solution)/shard_map/ppermute | solution.py:66
  57.6 1.5 %collective-permute-start.34 = (bf16[24,1024]{1,0:T(8,128)(2,1)S(1)}, bf16[24,1024]{1,0:T(8,128)(2,1)S(1)}, u32[]{:S(2)}, u32[]{:S(2)}) collective-permute-start(bf16[24,1024]{1,0:T(8,128)(2,1)S(1)} %get-tuple-element.74), channel_id=1, source_target_pairs={{0,4},{4,0},{8,12},{12,8},{1,5},{5,1},{9,13},{13,9},{2,6},{6,2},{1... | collective-permute-start | bytes 147464 | tf_op jit(solution)/shard_map/ppermute | solution.py:66
  59.1 1.5 %collective-permute-done.29.extra_ref = bf16[24,1024]{1,0:T(8,128)(2,1)S(1)} collective-permute-done((bf16[24,1024]{1,0:T(8,128)(2,1)S(1)}, bf16[24,1024]{1,0:T(8,128)(2,1)S(1)}, u32[]{:S(2)}, u32[]{:S(2)}) %collective-permute-start.29) | collective-permute-done | bytes 49184 | tf_op jit(solution)/shard_map/ppermute | solution.py:376
  60.6 1.4 %collective-permute-done.32.refs_0_ = bf16[24,1024]{1,0:T(8,128)(2,1)S(1)} collective-permute-done((bf16[24,1024]{1,0:T(8,128)(2,1)S(1)}, bf16[24,1024]{1,0:T(8,128)(2,1)S(1)}, u32[]{:S(2)}, u32[]{:S(2)}) %collective-permute-start.32) | collective-permute-done | bytes 49184 | tf_op jit(solution)/shard_map/ppermute | solution.py:66
  (78 shorter events, 16.2 us)
Async XLA Ops:
  1.9 12.4 %collective-permute-start = (bf16[24,2176]{1,0:T(8,128)(2,1)S(1)}, bf16[24,2176]{1,0:T(8,128)(2,1)S(1)}, u32[]{:S(2)}, u32[]{:S(2)}) collective-permute-start(bf16[24,2176]{1,0:T(8,128)(2,1)S(1)} %get-tuple-element.43), channel_id=1, source_target_pairs={{0,8},{4,12},{8,0},{12,4},{1,9},{5,13},{9,1},{13,5},{2,10},{6,14},... | collective-permute-start | bytes 313352 | tf_op jit(solution)/shard_map/ppermute | solution.py:66
  6.0 8.4 %collective-permute-start.2 = (bf16[24,2176]{1,0:T(8,128)(2,1)S(1)}, bf16[24,2176]{1,0:T(8,128)(2,1)S(1)}, u32[]{:S(2)}, u32[]{:S(2)}) collective-permute-start(bf16[24,2176]{1,0:T(8,128)(2,1)S(1)} %get-tuple-element.45), channel_id=1, source_target_pairs={{0,12},{4,8},{8,4},{12,0},{1,13},{5,9},{9,5},{13,1},{2,14},{6,10},... | collective-permute-start | bytes 313352 | tf_op jit(solution)/shard_map/ppermute | solution.py:66
  7.3 7.6 %collective-permute-start.4 = (bf16[24,2176]{1,0:T(8,128)(2,1)S(1)}, bf16[24,2176]{1,0:T(8,128)(2,1)S(1)}, u32[]{:S(2)}, u32[]{:S(2)}) collective-permute-start(bf16[24,2176]{1,0:T(8,128)(2,1)S(1)} %get-tuple-element.46), channel_id=1, source_target_pairs={{0,4},{4,0},{8,12},{12,8},{1,5},{5,1},{9,13},{13,9},{2,6},{6,2},{1... | collective-permute-start | bytes 313352 | tf_op jit(solution)/shard_map/ppermute | solution.py:66
  19.0 6.1 %collective-permute-start.9 = (bf16[72,1024]{1,0:T(8,128)(2,1)S(1)}, bf16[72,1024]{1,0:T(8,128)(2,1)S(1)}, u32[]{:S(2)}, u32[]{:S(2)}) collective-permute-start(bf16[72,1024]{1,0:T(8,128)(2,1)S(1)} %get-tuple-element.55), channel_id=1, source_target_pairs={{0,2},{1,3},{2,0},{3,1},{4,6},{5,7},{6,4},{7,5},{8,10},{9,11},{10,... | collective-permute-start | bytes 442376 | tf_op jit(solution)/shard_map/ppermute | solution.py:66
  21.2 7.8 %collective-permute-start.11 = (bf16[24,1024]{1,0:T(8,128)(2,1)S(1)}, bf16[24,1024]{1,0:T(8,128)(2,1)S(1)}, u32[]{:S(2)}, u32[]{:S(2)}) collective-permute-start(bf16[24,1024]{1,0:T(8,128)(2,1)S(1)} %get-tuple-element.57), channel_id=1, source_target_pairs={{0,12},{4,8},{8,4},{12,0},{1,13},{5,9},{9,5},{13,1},{2,14},{6,10},... | collective-permute-start | bytes 147464 | tf_op jit(solution)/shard_map/ppermute | solution.py:66
  24.2 7.3 %collective-permute-start.7 = (bf16[24,1024]{1,0:T(8,128)(2,1)S(1)}, bf16[24,1024]{1,0:T(8,128)(2,1)S(1)}, u32[]{:S(2)}, u32[]{:S(2)}) collective-permute-start(bf16[24,1024]{1,0:T(8,128)(2,1)S(1)} %get-tuple-element.53), channel_id=1, source_target_pairs={{0,14},{1,15},{2,12},{3,13},{4,10},{5,11},{6,8},{7,9},{8,6},{9,7},... | collective-permute-start | bytes 147464 | tf_op jit(solution)/shard_map/ppermute | solution.py:376
  25.1 6.8 %collective-permute-start.10 = (bf16[24,1024]{1,0:T(8,128)(2,1)S(1)}, bf16[24,1024]{1,0:T(8,128)(2,1)S(1)}, u32[]{:S(2)}, u32[]{:S(2)}) collective-permute-start(bf16[24,1024]{1,0:T(8,128)(2,1)S(1)} %get-tuple-element.56), channel_id=1, source_target_pairs={{0,8},{4,12},{8,0},{12,4},{1,9},{5,13},{9,1},{13,5},{2,10},{6,14},... | collective-permute-start | bytes 147464 | tf_op jit(solution)/shard_map/ppermute | solution.py:66
  29.0 4.1 %collective-permute-start.12 = (bf16[24,1024]{1,0:T(8,128)(2,1)S(1)}, bf16[24,1024]{1,0:T(8,128)(2,1)S(1)}, u32[]{:S(2)}, u32[]{:S(2)}) collective-permute-start(bf16[24,1024]{1,0:T(8,128)(2,1)S(1)} %get-tuple-element.58), channel_id=1, source_target_pairs={{0,4},{4,0},{8,12},{12,8},{1,5},{5,1},{9,13},{13,9},{2,6},{6,2},{1... | collective-permute-start | bytes 147464 | tf_op jit(solution)/shard_map/ppermute | solution.py:66
  33.4 5.5 %collective-permute-start.13 = (bf16[24,1024]{1,0:T(8,128)(2,1)S(1)}, bf16[24,1024]{1,0:T(8,128)(2,1)S(1)}, u32[]{:S(2)}, u32[]{:S(2)}) collective-permute-start(bf16[24,1024]{1,0:T(8,128)(2,1)S(1)} %get-tuple-element.62), channel_id=1, source_target_pairs={{0,8},{4,12},{8,0},{12,4},{1,9},{5,13},{9,1},{13,5},{2,10},{6,14},... | collective-permute-start | bytes 147464 | tf_op jit(solution)/shard_map/ppermute | solution.py:66
  34.4 6.0 %collective-permute-start.17 = (bf16[24,1024]{1,0:T(8,128)(2,1)S(1)}, bf16[24,1024]{1,0:T(8,128)(2,1)S(1)}, u32[]{:S(2)}, u32[]{:S(2)}) collective-permute-start(bf16[24,1024]{1,0:T(8,128)(2,1)S(1)} %get-tuple-element.63), channel_id=1, source_target_pairs={{0,12},{4,8},{8,4},{12,0},{1,13},{5,9},{9,5},{13,1},{2,14},{6,10},... | collective-permute-start | bytes 147464 | tf_op jit(solution)/shard_map/ppermute | solution.py:66
  36.4 5.4 %collective-permute-start.21 = (bf16[24,1024]{1,0:T(8,128)(2,1)S(1)}, bf16[24,1024]{1,0:T(8,128)(2,1)S(1)}, u32[]{:S(2)}, u32[]{:S(2)}) collective-permute-start(bf16[24,1024]{1,0:T(8,128)(2,1)S(1)} %get-tuple-element.64), channel_id=1, source_target_pairs={{0,4},{4,0},{8,12},{12,8},{1,5},{5,1},{9,13},{13,9},{2,6},{6,2},{1... | collective-permute-start | bytes 147464 | tf_op jit(solution)/shard_map/ppermute | solution.py:66
  37.0 5.5 %collective-permute-start.26 = (bf16[24,1024]{1,0:T(8,128)(2,1)S(1)}, bf16[24,1024]{1,0:T(8,128)(2,1)S(1)}, u32[]{:S(2)}, u32[]{:S(2)}) collective-permute-start(bf16[24,1024]{1,0:T(8,128)(2,1)S(1)} %get-tuple-element.65.refs_6_), channel_id=1, source_target_pairs={{0,2},{1,3},{2,0},{3,1},{4,6},{5,7},{6,4},{7,5},{8,10},{9,11},{10,... | collective-permute-start | bytes 147464 | tf_op jit(solution)/shard_map/ppermute | solution.py:66
  38.4 4.0 %collective-permute-start.25 = (bf16[24,1024]{1,0:T(8,128)(2,1)S(1)}, bf16[24,1024]{1,0:T(8,128)(2,1)S(1)}, u32[]{:S(2)}, u32[]{:S(2)}) collective-permute-start(bf16[24,1024]{1,0:T(8,128)(2,1)S(1)} %get-tuple-element.65.refs_6_), channel_id=1, source_target_pairs={{0,1},{1,0},{2,3},{3,2},{4,5},{5,4},{6,7},{7,6},{8,9},{9,8},{10,11... | collective-permute-start | bytes 147464 | tf_op jit(solution)/shard_map/ppermute | solution.py:66
  39.0 4.3 %collective-permute-start.15 = (bf16[24,1024]{1,0:T(8,128)(2,1)S(1)}, bf16[24,1024]{1,0:T(8,128)(2,1)S(1)}, u32[]{:S(2)}, u32[]{:S(2)}) collective-permute-start(bf16[24,1024]{1,0:T(8,128)(2,1)S(1)} %collective-permute-done.13.refs_0_), channel_id=1, source_target_pairs={{0,2},{1,3},{2,0},{3,1},{4,6},{5,7},{6,4},{7,5},{8,10},{9,11},{10,... | collective-permute-start | bytes 147464 | tf_op jit(solution)/shard_map/ppermute | solution.py:66
  40.4 4.1 %collective-permute-start.19 = (bf16[24,1024]{1,0:T(8,128)(2,1)S(1)}, bf16[24,1024]{1,0:T(8,128)(2,1)S(1)}, u32[]{:S(2)}, u32[]{:S(2)}) collective-permute-start(bf16[24,1024]{1,0:T(8,128)(2,1)S(1)} %collective-permute-done.17.refs_2_), channel_id=1, source_target_pairs={{0,2},{1,3},{2,0},{3,1},{4,6},{5,7},{6,4},{7,5},{8,10},{9,11},{10,... | collective-permute-start | bytes 147464 | tf_op jit(solution)/shard_map/ppermute | solution.py:66
  41.8 4.1 %collective-permute-start.23 = (bf16[24,1024]{1,0:T(8,128)(2,1)S(1)}, bf16[24,1024]{1,0:T(8,128)(2,1)S(1)}, u32[]{:S(2)}, u32[]{:S(2)}) collective-permute-start(bf16[24,1024]{1,0:T(8,128)(2,1)S(1)} %collective-permute-done.21.refs_4_), channel_id=1, source_target_pairs={{0,2},{1,3},{2,0},{3,1},{4,6},{5,7},{6,4},{7,5},{8,10},{9,11},{10,... | collective-permute-start | bytes 147464 | tf_op jit(solution)/shard_map/ppermute | solution.py:66
  42.5 3.4 %collective-permute-start.14 = (bf16[24,1024]{1,0:T(8,128)(2,1)S(1)}, bf16[24,1024]{1,0:T(8,128)(2,1)S(1)}, u32[]{:S(2)}, u32[]{:S(2)}) collective-permute-start(bf16[24,1024]{1,0:T(8,128)(2,1)S(1)} %collective-permute-done.13.refs_0_), channel_id=1, source_target_pairs={{0,1},{1,0},{2,3},{3,2},{4,5},{5,4},{6,7},{7,6},{8,9},{9,8},{10,11... | collective-permute-start | bytes 147464 | tf_op jit(solution)/shard_map/ppermute | solution.py:66
  42.5 3.9 %collective-permute-start.18 = (bf16[24,1024]{1,0:T(8,128)(2,1)S(1)}, bf16[24,1024]{1,0:T(8,128)(2,1)S(1)}, u32[]{:S(2)}, u32[]{:S(2)}) collective-permute-start(bf16[24,1024]{1,0:T(8,128)(2,1)S(1)} %collective-permute-done.17.refs_2_), channel_id=1, source_target_pairs={{0,1},{1,0},{2,3},{3,2},{4,5},{5,4},{6,7},{7,6},{8,9},{9,8},{10,11... | collective-permute-start | bytes 147464 | tf_op jit(solution)/shard_map/ppermute | solution.py:66
  43.3 3.9 %collective-permute-start.22 = (bf16[24,1024]{1,0:T(8,128)(2,1)S(1)}, bf16[24,1024]{1,0:T(8,128)(2,1)S(1)}, u32[]{:S(2)}, u32[]{:S(2)}) collective-permute-start(bf16[24,1024]{1,0:T(8,128)(2,1)S(1)} %collective-permute-done.21.refs_4_), channel_id=1, source_target_pairs={{0,1},{1,0},{2,3},{3,2},{4,5},{5,4},{6,7},{7,6},{8,9},{9,8},{10,11... | collective-permute-start | bytes 147464 | tf_op jit(solution)/shard_map/ppermute | solution.py:66
  50.5 6.0 %collective-permute-start.31 = (bf16[72,1024]{1,0:T(8,128)(2,1)S(1)}, bf16[72,1024]{1,0:T(8,128)(2,1)S(1)}, u32[]{:S(2)}, u32[]{:S(2)}) collective-permute-start(bf16[72,1024]{1,0:T(8,128)(2,1)S(1)} %get-tuple-element.71), channel_id=1, source_target_pairs={{0,2},{1,3},{2,0},{3,1},{4,6},{5,7},{6,4},{7,5},{8,10},{9,11},{10,... | collective-permute-start | bytes 442376 | tf_op jit(solution)/shard_map/ppermute | solution.py:66
  51.5 7.6 %collective-permute-start.33 = (bf16[24,1024]{1,0:T(8,128)(2,1)S(1)}, bf16[24,1024]{1,0:T(8,128)(2,1)S(1)}, u32[]{:S(2)}, u32[]{:S(2)}) collective-permute-start(bf16[24,1024]{1,0:T(8,128)(2,1)S(1)} %get-tuple-element.73), channel_id=1, source_target_pairs={{0,12},{4,8},{8,4},{12,0},{1,13},{5,9},{9,5},{13,1},{2,14},{6,10},... | collective-permute-start | bytes 147464 | tf_op jit(solution)/shard_map/ppermute | solution.py:66
  53.5 7.1 %collective-permute-start.29 = (bf16[24,1024]{1,0:T(8,128)(2,1)S(1)}, bf16[24,1024]{1,0:T(8,128)(2,1)S(1)}, u32[]{:S(2)}, u32[]{:S(2)}) collective-permute-start(bf16[24,1024]{1,0:T(8,128)(2,1)S(1)} %get-tuple-element.69), channel_id=1, source_target_pairs={{0,14},{1,15},{2,12},{3,13},{4,10},{5,11},{6,8},{7,9},{8,6},{9,7},... | collective-permute-start | bytes 147464 | tf_op jit(solution)/shard_map/ppermute | solution.py:376
  56.5 5.6 %collective-permute-start.32 = (bf16[24,1024]{1,0:T(8,128)(2,1)S(1)}, bf16[24,1024]{1,0:T(8,128)(2,1)S(1)}, u32[]{:S(2)}, u32[]{:S(2)}) collective-permute-start(bf16[24,1024]{1,0:T(8,128)(2,1)S(1)} %get-tuple-element.72), channel_id=1, source_target_pairs={{0,8},{4,12},{8,0},{12,4},{1,9},{5,13},{9,1},{13,5},{2,10},{6,14},... | collective-permute-start | bytes 147464 | tf_op jit(solution)/shard_map/ppermute | solution.py:66
  57.6 4.5 %collective-permute-start.34 = (bf16[24,1024]{1,0:T(8,128)(2,1)S(1)}, bf16[24,1024]{1,0:T(8,128)(2,1)S(1)}, u32[]{:S(2)}, u32[]{:S(2)}) collective-permute-start(bf16[24,1024]{1,0:T(8,128)(2,1)S(1)} %get-tuple-element.74), channel_id=1, source_target_pairs={{0,4},{4,0},{8,12},{12,8},{1,5},{5,1},{9,13},{13,9},{2,6},{6,2},{1... | collective-permute-start | bytes 147464 | tf_op jit(solution)/shard_map/ppermute | solution.py:66
  (15 other events, 42.4 us)

commit v17 on v15

--- a/solution.py
+++ b/solution.py
@@ -402,7 +402,7 @@
     )(own, back, pick, extra, *[came[k] for k in order])
 
 
-DIRECT = 2
+DIRECT = 3
 
 
 def sum_back(hidden, w_down, own, back, pick, last):
@@ -450,7 +450,7 @@
     hidden = front(blocks, flags, order + [0], 0, modulation, router, pair)
     own, *sent = sum_back(hidden, w_down, own, back[0], pick, False)
 
-    sides = {1: diagonal(sent[1], 1, 2)}
+    sides = {DIRECT: diagonal(sent[DIRECT], DIRECT, 2)}
     blocks = [spread(swap(b, "ep", k) if k else b, quarter, sides.get(k)) for k, b in enumerate(sent)]
     hidden = front(blocks, flags, order + [0], 1, modulation, router, pair)
     return tuple(sum_back(hidden, w_down, own, back[1], pick, True))

time: 63.7 us -> 63.6 us (level)
  waiting for transfers between devices: 15.3 us -> 13.4 us
  starting transfers between devices: 34.6 us -> 36.4 us
    ppermute x32, waiting for transfers between devices: 11.8 us -> 6.97 us  [swap(): return lax.ppermute(x, axis, [(i, i ^ bit) for i in range(size)])]
    ppermute x32, starting transfers between devices: 28.7 us -> 32.2 us  [swap(): return lax.ppermute(x, axis, [(i, i ^ bit) for i in range(size)])]
    ppermute x3, waiting for transfers between devices: 3.51 us -> 6.43 us  [diagonal(): return lax.ppermute(x, ('ep', 'et'), pairs)]
    ppermute x3, starting transfers between devices: 5.92 us -> 4.2 us  [diagonal(): return lax.ppermute(x, ('ep', 'et'), pairs)]
where the time goes in v17:
time: 63.6 us; the launch traced here: 63.4 us
  starting transfers between devices  36.4 us (57%)
  waiting for transfers between devices  13.4 us (21%)
  Pallas kernels  12.7 us (20%)
  between operations  0.87 us (1%)
    ppermute x32, starting transfers between devices, swap(): return lax.ppermute(x, axis, [(i, i ^ bit) for i in range(size)])  32.2 us
    ppermute x32, waiting for transfers between devices, swap(): return lax.ppermute(x, axis, [(i, i ^ bit) for i in range(size)])  6.97 us
    ppermute x3, waiting for transfers between devices, diagonal(): return lax.ppermute(x, ('ep', 'et'), pairs)  6.43 us
    ppermute x3, starting transfers between devices, diagonal(): return lax.ppermute(x, ('ep', 'et'), pairs)  4.2 us
    pallas_call x1, Pallas kernels, load(): pl.pallas_call(load_kernel, in_specs=[ANY] * 3, out_specs=[VMEM] * 3, out...  3.78 us
    pallas_call x4, Pallas kernels, half_front(): pl.pallas_call(functools.partial(front_kernel, layout, order, flips, sect...  3.34 us
    pallas_call x8, Pallas kernels, down(): pl.pallas_call(functools.partial(down_kernel, flip, len(adds), groups), i...  2.24 us
  transfers between devices with their start and end apart: 35, of which 17 were waited for; matrix products, arithmetic and copies ran while one was open for 0% of the time, Pallas kernels for 12%

profile of v17, /device:TPU:0, one launch (start us, length us, event | category | flops | bytes accessed | tf_op | source)
XLA Modules:
  0.0 63.4 jit_solution(13612893753159035898)
XLA Ops:
  0.6 1.2 %pack.1 = (bf16[24,2176]{1,0:T(8,128)(2,1)S(1)}, bf16[24,2176]{1,0:T(8,128)(2,1)S(1)}, bf16[24,2176]{1,0:T(8,128)(2,1)S(1)}, bf16[32,1024]{1,0:T(8,128)(2,1)S(1)}) custom-call(bf16[32,4096]{1,0:T(8,128)(2,1)} %tokens_ref.3, s32[2,2,32]{2,1,0:T(2,128)} %bitcast.6), custom_call_target="tpu_custom_call" | custom-call | tf_op jit(solution)/shard_map/pack/pallas_call | solution.py:197
  1.9 4.1 %collective-permute-start = (bf16[24,2176]{1,0:T(8,128)(2,1)S(1)}, bf16[24,2176]{1,0:T(8,128)(2,1)S(1)}, u32[]{:S(2)}, u32[]{:S(2)}) collective-permute-start(bf16[24,2176]{1,0:T(8,128)(2,1)S(1)} %get-tuple-element.43), channel_id=1, source_target_pairs={{0,8},{4,12},{8,0},{12,4},{1,9},{5,13},{9,1},{13,5},{2,10},{6,14},... | collective-permute-start | bytes 313352 | tf_op jit(solution)/shard_map/ppermute | solution.py:66
  6.0 1.3 %collective-permute-start.2 = (bf16[24,2176]{1,0:T(8,128)(2,1)S(1)}, bf16[24,2176]{1,0:T(8,128)(2,1)S(1)}, u32[]{:S(2)}, u32[]{:S(2)}) collective-permute-start(bf16[24,2176]{1,0:T(8,128)(2,1)S(1)} %get-tuple-element.45), channel_id=1, source_target_pairs={{0,12},{4,8},{8,4},{12,0},{1,13},{5,9},{9,5},{13,1},{2,14},{6,10},... | collective-permute-start | bytes 313352 | tf_op jit(solution)/shard_map/ppermute | solution.py:66
  7.6 3.8 %load.1 = (bf16[4096,768]{1,0:T(8,128)(2,1)S(1)}, bf16[384,4096]{1,0:T(8,128)(2,1)S(1)}, f32[8,128]{1,0:T(8,128)S(1)}) custom-call(bf16[1,4096,384]{2,1,0:T(8,128)(2,1)} %gate_ref.1, bf16[1,4096,384]{2,1,0:T(8,128)(2,1)} %up_ref.1, bf16[1,384,4096]{2,1,0:T(8,128)(2,1)} %down_ref.1), custom_call_target="tpu_custom_call" | custom-call | bytes 18874368 | tf_op jit(solution)/shard_map/load/pallas_call | solution.py:101
  12.2 2.0 %collective-permute-done.block_ref.refs_7_.refs_11_ = bf16[24,2176]{1,0:T(8,128)(2,1)S(1)} collective-permute-done((bf16[24,2176]{1,0:T(8,128)(2,1)S(1)}, bf16[24,2176]{1,0:T(8,128)(2,1)S(1)}, u32[]{:S(2)}, u32[]{:S(2)}) %collective-permute-start) | collective-permute-done | bytes 104480 | tf_op jit(solution)/shard_map/ppermute | solution.py:66
  16.3 0.9 %front.5.hidden_ref = bf16[96,384]{1,0:T(8,128)(2,1)S(1)} custom-call(bf16[24,2048]{1,0:T(8,128)(2,1)S(1)} %collective-permute-done.1.refs_0_, bf16[24,2048]{1,0:T(8,128)(2,1)S(1)} %collective-permute-done.3.refs_1_, bf16[24,2048]{1,0:T(8,128)(2,1)S(1)} %collective-permute-done.5.refs_2_, bf16[24,4096]{1,0:T(8,128)(2,1)S(1)} %get-tuple-element.47.refs_3_, ...), custom_call_target="tpu_custom_call" | custom-call | flops 301989888 | bytes 3145728 | tf_op jit(solution)/shard_map/front/pallas_call | solution.py:298
  19.0 1.9 %collective-permute-start.9 = (bf16[72,1024]{1,0:T(8,128)(2,1)S(1)}, bf16[72,1024]{1,0:T(8,128)(2,1)S(1)}, u32[]{:S(2)}, u32[]{:S(2)}) collective-permute-start(bf16[72,1024]{1,0:T(8,128)(2,1)S(1)} %get-tuple-element.55), channel_id=1, source_target_pairs={{0,2},{1,3},{2,0},{3,1},{4,6},{5,7},{6,4},{7,5},{8,10},{9,11},{10,... | collective-permute-start | bytes 442376 | tf_op jit(solution)/shard_map/ppermute | solution.py:66
  21.2 3.0 %collective-permute-start.11 = (bf16[24,1024]{1,0:T(8,128)(2,1)S(1)}, bf16[24,1024]{1,0:T(8,128)(2,1)S(1)}, u32[]{:S(2)}, u32[]{:S(2)}) collective-permute-start(bf16[24,1024]{1,0:T(8,128)(2,1)S(1)} %get-tuple-element.57), channel_id=1, source_target_pairs={{0,12},{4,8},{8,4},{12,0},{1,13},{5,9},{9,5},{13,1},{2,14},{6,10},... | collective-permute-start | bytes 147464 | tf_op jit(solution)/shard_map/ppermute | solution.py:66
  25.1 3.9 %collective-permute-start.10 = (bf16[24,1024]{1,0:T(8,128)(2,1)S(1)}, bf16[24,1024]{1,0:T(8,128)(2,1)S(1)}, u32[]{:S(2)}, u32[]{:S(2)}) collective-permute-start(bf16[24,1024]{1,0:T(8,128)(2,1)S(1)} %get-tuple-element.56), channel_id=1, source_target_pairs={{0,8},{4,12},{8,0},{12,4},{1,9},{5,13},{9,1},{13,5},{2,10},{6,14},... | collective-permute-start | bytes 147464 | tf_op jit(solution)/shard_map/ppermute | solution.py:66
  29.0 2.5 %collective-permute-done.7.extra_ref = bf16[24,1024]{1,0:T(8,128)(2,1)S(1)} collective-permute-done((bf16[24,1024]{1,0:T(8,128)(2,1)S(1)}, bf16[24,1024]{1,0:T(8,128)(2,1)S(1)}, u32[]{:S(2)}, u32[]{:S(2)}) %collective-permute-start.7) | collective-permute-done | bytes 49184 | tf_op jit(solution)/shard_map/ppermute | solution.py:376
  31.9 1.2 %collective-permute-done.12.refs_2_ = bf16[24,1024]{1,0:T(8,128)(2,1)S(1)} collective-permute-done((bf16[24,1024]{1,0:T(8,128)(2,1)S(1)}, bf16[24,1024]{1,0:T(8,128)(2,1)S(1)}, u32[]{:S(2)}, u32[]{:S(2)}) %collective-permute-start.12) | collective-permute-done | bytes 49184 | tf_op jit(solution)/shard_map/ppermute | solution.py:66
  33.4 1.0 %collective-permute-start.13 = (bf16[24,1024]{1,0:T(8,128)(2,1)S(1)}, bf16[24,1024]{1,0:T(8,128)(2,1)S(1)}, u32[]{:S(2)}, u32[]{:S(2)}) collective-permute-start(bf16[24,1024]{1,0:T(8,128)(2,1)S(1)} %get-tuple-element.62), channel_id=1, source_target_pairs={{0,8},{4,12},{8,0},{12,4},{1,9},{5,13},{9,1},{13,5},{2,10},{6,14},... | collective-permute-start | bytes 147464 | tf_op jit(solution)/shard_map/ppermute | solution.py:66
  34.9 3.0 %collective-permute-start.17 = (bf16[24,1024]{1,0:T(8,128)(2,1)S(1)}, bf16[24,1024]{1,0:T(8,128)(2,1)S(1)}, u32[]{:S(2)}, u32[]{:S(2)}) collective-permute-start(bf16[24,1024]{1,0:T(8,128)(2,1)S(1)} %get-tuple-element.63), channel_id=1, source_target_pairs={{0,12},{4,8},{8,4},{12,0},{1,13},{5,9},{9,5},{13,1},{2,14},{6,10},... | collective-permute-start | bytes 147464 | tf_op jit(solution)/shard_map/ppermute | solution.py:66
  37.9 1.7 %collective-permute-start.19 = (bf16[24,1024]{1,0:T(8,128)(2,1)S(1)}, bf16[24,1024]{1,0:T(8,128)(2,1)S(1)}, u32[]{:S(2)}, u32[]{:S(2)}) collective-permute-start(bf16[24,1024]{1,0:T(8,128)(2,1)S(1)} %get-tuple-element.63), channel_id=1, source_target_pairs={{0,14},{1,15},{2,12},{3,13},{4,10},{5,11},{6,8},{7,9},{8,6},{9,7},... | collective-permute-start | bytes 147464 | tf_op jit(solution)/shard_map/ppermute | solution.py:376
  40.2 1.5 %collective-permute-start.15 = (bf16[24,1024]{1,0:T(8,128)(2,1)S(1)}, bf16[24,1024]{1,0:T(8,128)(2,1)S(1)}, u32[]{:S(2)}, u32[]{:S(2)}) collective-permute-start(bf16[24,1024]{1,0:T(8,128)(2,1)S(1)} %collective-permute-done.13.refs_0_), channel_id=1, source_target_pairs={{0,2},{1,3},{2,0},{3,1},{4,6},{5,7},{6,4},{7,5},{8,10},{9,11},{10,... | collective-permute-start | bytes 147464 | tf_op jit(solution)/shard_map/ppermute | solution.py:66
  41.7 1.1 %collective-permute-start.23 = (bf16[24,1024]{1,0:T(8,128)(2,1)S(1)}, bf16[24,1024]{1,0:T(8,128)(2,1)S(1)}, u32[]{:S(2)}, u32[]{:S(2)}) collective-permute-start(bf16[24,1024]{1,0:T(8,128)(2,1)S(1)} %collective-permute-done.21.refs_4_), channel_id=1, source_target_pairs={{0,2},{1,3},{2,0},{3,1},{4,6},{5,7},{6,4},{7,5},{8,10},{9,11},{10,... | collective-permute-start | bytes 147464 | tf_op jit(solution)/shard_map/ppermute | solution.py:66
  42.7 2.0 %collective-permute-done.19.refs_3_ = bf16[24,1024]{1,0:T(8,128)(2,1)S(1)} collective-permute-done((bf16[24,1024]{1,0:T(8,128)(2,1)S(1)}, bf16[24,1024]{1,0:T(8,128)(2,1)S(1)}, u32[]{:S(2)}, u32[]{:S(2)}) %collective-permute-start.19) | collective-permute-done | bytes 49184 | tf_op jit(solution)/shard_map/ppermute | solution.py:376
  48.1 1.0 %front.7.hidden_ref = bf16[96,384]{1,0:T(8,128)(2,1)S(1)} custom-call(bf16[24,1024]{1,0:T(8,128)(2,1)S(1)} %collective-permute-done.14.refs_0_, bf16[24,1024]{1,0:T(8,128)(2,1)S(1)} %collective-permute-done.16.refs_1_, bf16[24,1024]{1,0:T(8,128)(2,1)S(1)} %collective-permute-done.18.refs_2_, bf16[24,1024]{1,0:T(8,128)(2,1)S(1)} %collective-permute-done.20.refs_3_, ...), custom_call_target="tpu_custom_call" | custom-call | flops 301989888 | bytes 3145728 | tf_op jit(solution)/shard_map/front/pallas_call | solution.py:298
  50.9 1.1 %collective-permute-start.31 = (bf16[72,1024]{1,0:T(8,128)(2,1)S(1)}, bf16[72,1024]{1,0:T(8,128)(2,1)S(1)}, u32[]{:S(2)}, u32[]{:S(2)}) collective-permute-start(bf16[72,1024]{1,0:T(8,128)(2,1)S(1)} %get-tuple-element.71), channel_id=1, source_target_pairs={{0,2},{1,3},{2,0},{3,1},{4,6},{5,7},{6,4},{7,5},{8,10},{9,11},{10,... | collective-permute-start | bytes 442376 | tf_op jit(solution)/shard_map/ppermute | solution.py:66
  52.3 2.5 %collective-permute-start.33 = (bf16[24,1024]{1,0:T(8,128)(2,1)S(1)}, bf16[24,1024]{1,0:T(8,128)(2,1)S(1)}, u32[]{:S(2)}, u32[]{:S(2)}) collective-permute-start(bf16[24,1024]{1,0:T(8,128)(2,1)S(1)} %get-tuple-element.73), channel_id=1, source_target_pairs={{0,12},{4,8},{8,4},{12,0},{1,13},{5,9},{9,5},{13,1},{2,14},{6,10},... | collective-permute-start | bytes 147464 | tf_op jit(solution)/shard_map/ppermute | solution.py:66
  54.9 1.8 %collective-permute-start.29 = (bf16[24,1024]{1,0:T(8,128)(2,1)S(1)}, bf16[24,1024]{1,0:T(8,128)(2,1)S(1)}, u32[]{:S(2)}, u32[]{:S(2)}) collective-permute-start(bf16[24,1024]{1,0:T(8,128)(2,1)S(1)} %get-tuple-element.69), channel_id=1, source_target_pairs={{0,14},{1,15},{2,12},{3,13},{4,10},{5,11},{6,8},{7,9},{8,6},{9,7},... | collective-permute-start | bytes 147464 | tf_op jit(solution)/shard_map/ppermute | solution.py:376
  57.1 2.9 %collective-permute-start.34 = (bf16[24,1024]{1,0:T(8,128)(2,1)S(1)}, bf16[24,1024]{1,0:T(8,128)(2,1)S(1)}, u32[]{:S(2)}, u32[]{:S(2)}) collective-permute-start(bf16[24,1024]{1,0:T(8,128)(2,1)S(1)} %get-tuple-element.74), channel_id=1, source_target_pairs={{0,4},{4,0},{8,12},{12,8},{1,5},{5,1},{9,13},{13,9},{2,6},{6,2},{1... | collective-permute-start | bytes 147464 | tf_op jit(solution)/shard_map/ppermute | solution.py:66
  60.1 1.9 %collective-permute-done.29.extra_ref = bf16[24,1024]{1,0:T(8,128)(2,1)S(1)} collective-permute-done((bf16[24,1024]{1,0:T(8,128)(2,1)S(1)}, bf16[24,1024]{1,0:T(8,128)(2,1)S(1)}, u32[]{:S(2)}, u32[]{:S(2)}) %collective-permute-start.29) | collective-permute-done | bytes 49184 | tf_op jit(solution)/shard_map/ppermute | solution.py:376
  62.6 0.8 %move.3 = (bf16[32,1024]{1,0:T(8,128)(2,1)}, bf16[32,1024]{1,0:T(8,128)(2,1)}) custom-call(bf16[32,1024]{1,0:T(8,128)(2,1)S(1)} %get-tuple-element.60.own_ref, bf16[32,96]{1,0:T(8,128)(2,1)S(1)} %get-tuple-element.61.back_ref, bf16[96,32]{1,0:T(8,128)(2,1)S(1)} %get-tuple-element.42.pick_ref, bf16[24,1024]{1,0:T(8,128)(2,1)S(1)} %collective-permute-done.29.extra_ref, ...), custom_call_target="tpu_custom_call" | custom-call | tf_op jit(solution)/shard_map/move/pallas_call | solution.py:397
  (78 shorter events, 14.4 us)
Async XLA Ops:
  1.9 12.4 %collective-permute-start = (bf16[24,2176]{1,0:T(8,128)(2,1)S(1)}, bf16[24,2176]{1,0:T(8,128)(2,1)S(1)}, u32[]{:S(2)}, u32[]{:S(2)}) collective-permute-start(bf16[24,2176]{1,0:T(8,128)(2,1)S(1)} %get-tuple-element.43), channel_id=1, source_target_pairs={{0,8},{4,12},{8,0},{12,4},{1,9},{5,13},{9,1},{13,5},{2,10},{6,14},... | collective-permute-start | bytes 313352 | tf_op jit(solution)/shard_map/ppermute | solution.py:66
  6.0 8.4 %collective-permute-start.2 = (bf16[24,2176]{1,0:T(8,128)(2,1)S(1)}, bf16[24,2176]{1,0:T(8,128)(2,1)S(1)}, u32[]{:S(2)}, u32[]{:S(2)}) collective-permute-start(bf16[24,2176]{1,0:T(8,128)(2,1)S(1)} %get-tuple-element.45), channel_id=1, source_target_pairs={{0,12},{4,8},{8,4},{12,0},{1,13},{5,9},{9,5},{13,1},{2,14},{6,10},... | collective-permute-start | bytes 313352 | tf_op jit(solution)/shard_map/ppermute | solution.py:66
  7.3 7.6 %collective-permute-start.4 = (bf16[24,2176]{1,0:T(8,128)(2,1)S(1)}, bf16[24,2176]{1,0:T(8,128)(2,1)S(1)}, u32[]{:S(2)}, u32[]{:S(2)}) collective-permute-start(bf16[24,2176]{1,0:T(8,128)(2,1)S(1)} %get-tuple-element.46), channel_id=1, source_target_pairs={{0,4},{4,0},{8,12},{12,8},{1,5},{5,1},{9,13},{13,9},{2,6},{6,2},{1... | collective-permute-start | bytes 313352 | tf_op jit(solution)/shard_map/ppermute | solution.py:66
  18.0 3.0 %collective-permute-start.8 = (bf16[96,1024]{1,0:T(8,128)(2,1)S(1)}, bf16[96,1024]{1,0:T(8,128)(2,1)S(1)}, u32[]{:S(2)}, u32[]{:S(2)}) collective-permute-start(bf16[96,1024]{1,0:T(8,128)(2,1)S(1)} %down.10), channel_id=1, source_target_pairs={{0,1},{1,0},{2,3},{3,2},{4,5},{5,4},{6,7},{7,6},{8,9},{9,8},{10,11... | collective-permute-start | bytes 589832 | tf_op jit(solution)/shard_map/ppermute | solution.py:66
  19.0 6.1 %collective-permute-start.9 = (bf16[72,1024]{1,0:T(8,128)(2,1)S(1)}, bf16[72,1024]{1,0:T(8,128)(2,1)S(1)}, u32[]{:S(2)}, u32[]{:S(2)}) collective-permute-start(bf16[72,1024]{1,0:T(8,128)(2,1)S(1)} %get-tuple-element.55), channel_id=1, source_target_pairs={{0,2},{1,3},{2,0},{3,1},{4,6},{5,7},{6,4},{7,5},{8,10},{9,11},{10,... | collective-permute-start | bytes 442376 | tf_op jit(solution)/shard_map/ppermute | solution.py:66
  21.2 7.8 %collective-permute-start.11 = (bf16[24,1024]{1,0:T(8,128)(2,1)S(1)}, bf16[24,1024]{1,0:T(8,128)(2,1)S(1)}, u32[]{:S(2)}, u32[]{:S(2)}) collective-permute-start(bf16[24,1024]{1,0:T(8,128)(2,1)S(1)} %get-tuple-element.57), channel_id=1, source_target_pairs={{0,12},{4,8},{8,4},{12,0},{1,13},{5,9},{9,5},{13,1},{2,14},{6,10},... | collective-permute-start | bytes 147464 | tf_op jit(solution)/shard_map/ppermute | solution.py:66
  24.2 7.3 %collective-permute-start.7 = (bf16[24,1024]{1,0:T(8,128)(2,1)S(1)}, bf16[24,1024]{1,0:T(8,128)(2,1)S(1)}, u32[]{:S(2)}, u32[]{:S(2)}) collective-permute-start(bf16[24,1024]{1,0:T(8,128)(2,1)S(1)} %get-tuple-element.53), channel_id=1, source_target_pairs={{0,14},{1,15},{2,12},{3,13},{4,10},{5,11},{6,8},{7,9},{8,6},{9,7},... | collective-permute-start | bytes 147464 | tf_op jit(solution)/shard_map/ppermute | solution.py:376
  25.1 6.8 %collective-permute-start.10 = (bf16[24,1024]{1,0:T(8,128)(2,1)S(1)}, bf16[24,1024]{1,0:T(8,128)(2,1)S(1)}, u32[]{:S(2)}, u32[]{:S(2)}) collective-permute-start(bf16[24,1024]{1,0:T(8,128)(2,1)S(1)} %get-tuple-element.56), channel_id=1, source_target_pairs={{0,8},{4,12},{8,0},{12,4},{1,9},{5,13},{9,1},{13,5},{2,10},{6,14},... | collective-permute-start | bytes 147464 | tf_op jit(solution)/shard_map/ppermute | solution.py:66
  29.0 4.1 %collective-permute-start.12 = (bf16[24,1024]{1,0:T(8,128)(2,1)S(1)}, bf16[24,1024]{1,0:T(8,128)(2,1)S(1)}, u32[]{:S(2)}, u32[]{:S(2)}) collective-permute-start(bf16[24,1024]{1,0:T(8,128)(2,1)S(1)} %get-tuple-element.58), channel_id=1, source_target_pairs={{0,4},{4,0},{8,12},{12,8},{1,5},{5,1},{9,13},{13,9},{2,6},{6,2},{1... | collective-permute-start | bytes 147464 | tf_op jit(solution)/shard_map/ppermute | solution.py:66
  33.4 6.7 %collective-permute-start.13 = (bf16[24,1024]{1,0:T(8,128)(2,1)S(1)}, bf16[24,1024]{1,0:T(8,128)(2,1)S(1)}, u32[]{:S(2)}, u32[]{:S(2)}) collective-permute-start(bf16[24,1024]{1,0:T(8,128)(2,1)S(1)} %get-tuple-element.62), channel_id=1, source_target_pairs={{0,8},{4,12},{8,0},{12,4},{1,9},{5,13},{9,1},{13,5},{2,10},{6,14},... | collective-permute-start | bytes 147464 | tf_op jit(solution)/shard_map/ppermute | solution.py:66
  34.4 5.8 %collective-permute-start.21 = (bf16[24,1024]{1,0:T(8,128)(2,1)S(1)}, bf16[24,1024]{1,0:T(8,128)(2,1)S(1)}, u32[]{:S(2)}, u32[]{:S(2)}) collective-permute-start(bf16[24,1024]{1,0:T(8,128)(2,1)S(1)} %get-tuple-element.64), channel_id=1, source_target_pairs={{0,4},{4,0},{8,12},{12,8},{1,5},{5,1},{9,13},{13,9},{2,6},{6,2},{1... | collective-permute-start | bytes 147464 | tf_op jit(solution)/shard_map/ppermute | solution.py:66
  34.9 6.8 %collective-permute-start.17 = (bf16[24,1024]{1,0:T(8,128)(2,1)S(1)}, bf16[24,1024]{1,0:T(8,128)(2,1)S(1)}, u32[]{:S(2)}, u32[]{:S(2)}) collective-permute-start(bf16[24,1024]{1,0:T(8,128)(2,1)S(1)} %get-tuple-element.63), channel_id=1, source_target_pairs={{0,12},{4,8},{8,4},{12,0},{1,13},{5,9},{9,5},{13,1},{2,14},{6,10},... | collective-permute-start | bytes 147464 | tf_op jit(solution)/shard_map/ppermute | solution.py:66
  37.9 6.9 %collective-permute-start.19 = (bf16[24,1024]{1,0:T(8,128)(2,1)S(1)}, bf16[24,1024]{1,0:T(8,128)(2,1)S(1)}, u32[]{:S(2)}, u32[]{:S(2)}) collective-permute-start(bf16[24,1024]{1,0:T(8,128)(2,1)S(1)} %get-tuple-element.63), channel_id=1, source_target_pairs={{0,14},{1,15},{2,12},{3,13},{4,10},{5,11},{6,8},{7,9},{8,6},{9,7},... | collective-permute-start | bytes 147464 | tf_op jit(solution)/shard_map/ppermute | solution.py:376
  39.6 5.2 %collective-permute-start.26 = (bf16[24,1024]{1,0:T(8,128)(2,1)S(1)}, bf16[24,1024]{1,0:T(8,128)(2,1)S(1)}, u32[]{:S(2)}, u32[]{:S(2)}) collective-permute-start(bf16[24,1024]{1,0:T(8,128)(2,1)S(1)} %get-tuple-element.65.refs_6_), channel_id=1, source_target_pairs={{0,2},{1,3},{2,0},{3,1},{4,6},{5,7},{6,4},{7,5},{8,10},{9,11},{10,... | collective-permute-start | bytes 147464 | tf_op jit(solution)/shard_map/ppermute | solution.py:66
  40.2 5.1 %collective-permute-start.25 = (bf16[24,1024]{1,0:T(8,128)(2,1)S(1)}, bf16[24,1024]{1,0:T(8,128)(2,1)S(1)}, u32[]{:S(2)}, u32[]{:S(2)}) collective-permute-start(bf16[24,1024]{1,0:T(8,128)(2,1)S(1)} %get-tuple-element.65.refs_6_), channel_id=1, source_target_pairs={{0,1},{1,0},{2,3},{3,2},{4,5},{5,4},{6,7},{7,6},{8,9},{9,8},{10,11... | collective-permute-start | bytes 147464 | tf_op jit(solution)/shard_map/ppermute | solution.py:66
  40.2 5.5 %collective-permute-start.15 = (bf16[24,1024]{1,0:T(8,128)(2,1)S(1)}, bf16[24,1024]{1,0:T(8,128)(2,1)S(1)}, u32[]{:S(2)}, u32[]{:S(2)}) collective-permute-start(bf16[24,1024]{1,0:T(8,128)(2,1)S(1)} %collective-permute-done.13.refs_0_), channel_id=1, source_target_pairs={{0,2},{1,3},{2,0},{3,1},{4,6},{5,7},{6,4},{7,5},{8,10},{9,11},{10,... | collective-permute-start | bytes 147464 | tf_op jit(solution)/shard_map/ppermute | solution.py:66
  41.7 4.6 %collective-permute-start.23 = (bf16[24,1024]{1,0:T(8,128)(2,1)S(1)}, bf16[24,1024]{1,0:T(8,128)(2,1)S(1)}, u32[]{:S(2)}, u32[]{:S(2)}) collective-permute-start(bf16[24,1024]{1,0:T(8,128)(2,1)S(1)} %collective-permute-done.21.refs_4_), channel_id=1, source_target_pairs={{0,2},{1,3},{2,0},{3,1},{4,6},{5,7},{6,4},{7,5},{8,10},{9,11},{10,... | collective-permute-start | bytes 147464 | tf_op jit(solution)/shard_map/ppermute | solution.py:66
  45.3 2.3 %collective-permute-start.22 = (bf16[24,1024]{1,0:T(8,128)(2,1)S(1)}, bf16[24,1024]{1,0:T(8,128)(2,1)S(1)}, u32[]{:S(2)}, u32[]{:S(2)}) collective-permute-start(bf16[24,1024]{1,0:T(8,128)(2,1)S(1)} %collective-permute-done.21.refs_4_), channel_id=1, source_target_pairs={{0,1},{1,0},{2,3},{3,2},{4,5},{5,4},{6,7},{7,6},{8,9},{9,8},{10,11... | collective-permute-start | bytes 147464 | tf_op jit(solution)/shard_map/ppermute | solution.py:66
  49.9 2.2 %collective-permute-start.30 = (bf16[96,1024]{1,0:T(8,128)(2,1)S(1)}, bf16[96,1024]{1,0:T(8,128)(2,1)S(1)}, u32[]{:S(2)}, u32[]{:S(2)}) collective-permute-start(bf16[96,1024]{1,0:T(8,128)(2,1)S(1)} %down.14), channel_id=1, source_target_pairs={{0,1},{1,0},{2,3},{3,2},{4,5},{5,4},{6,7},{7,6},{8,9},{9,8},{10,11... | collective-permute-start | bytes 589832 | tf_op jit(solution)/shard_map/ppermute | solution.py:66
  50.9 6.0 %collective-permute-start.31 = (bf16[72,1024]{1,0:T(8,128)(2,1)S(1)}, bf16[72,1024]{1,0:T(8,128)(2,1)S(1)}, u32[]{:S(2)}, u32[]{:S(2)}) collective-permute-start(bf16[72,1024]{1,0:T(8,128)(2,1)S(1)} %get-tuple-element.71), channel_id=1, source_target_pairs={{0,2},{1,3},{2,0},{3,1},{4,6},{5,7},{6,4},{7,5},{8,10},{9,11},{10,... | collective-permute-start | bytes 442376 | tf_op jit(solution)/shard_map/ppermute | solution.py:66
  52.3 7.7 %collective-permute-start.33 = (bf16[24,1024]{1,0:T(8,128)(2,1)S(1)}, bf16[24,1024]{1,0:T(8,128)(2,1)S(1)}, u32[]{:S(2)}, u32[]{:S(2)}) collective-permute-start(bf16[24,1024]{1,0:T(8,128)(2,1)S(1)} %get-tuple-element.73), channel_id=1, source_target_pairs={{0,12},{4,8},{8,4},{12,0},{1,13},{5,9},{9,5},{13,1},{2,14},{6,10},... | collective-permute-start | bytes 147464 | tf_op jit(solution)/shard_map/ppermute | solution.py:66
  54.9 7.1 %collective-permute-start.29 = (bf16[24,1024]{1,0:T(8,128)(2,1)S(1)}, bf16[24,1024]{1,0:T(8,128)(2,1)S(1)}, u32[]{:S(2)}, u32[]{:S(2)}) collective-permute-start(bf16[24,1024]{1,0:T(8,128)(2,1)S(1)} %get-tuple-element.69), channel_id=1, source_target_pairs={{0,14},{1,15},{2,12},{3,13},{4,10},{5,11},{6,8},{7,9},{8,6},{9,7},... | collective-permute-start | bytes 147464 | tf_op jit(solution)/shard_map/ppermute | solution.py:376
  56.9 5.6 %collective-permute-start.32 = (bf16[24,1024]{1,0:T(8,128)(2,1)S(1)}, bf16[24,1024]{1,0:T(8,128)(2,1)S(1)}, u32[]{:S(2)}, u32[]{:S(2)}) collective-permute-start(bf16[24,1024]{1,0:T(8,128)(2,1)S(1)} %get-tuple-element.72), channel_id=1, source_target_pairs={{0,8},{4,12},{8,0},{12,4},{1,9},{5,13},{9,1},{13,5},{2,10},{6,14},... | collective-permute-start | bytes 147464 | tf_op jit(solution)/shard_map/ppermute | solution.py:66
  57.1 5.5 %collective-permute-start.34 = (bf16[24,1024]{1,0:T(8,128)(2,1)S(1)}, bf16[24,1024]{1,0:T(8,128)(2,1)S(1)}, u32[]{:S(2)}, u32[]{:S(2)}) collective-permute-start(bf16[24,1024]{1,0:T(8,128)(2,1)S(1)} %get-tuple-element.74), channel_id=1, source_target_pairs={{0,4},{4,0},{8,12},{12,8},{1,5},{5,1},{9,13},{13,9},{2,6},{6,2},{1... | collective-permute-start | bytes 147464 | tf_op jit(solution)/shard_map/ppermute | solution.py:66
  (15 other events, 40.5 us)

commit v18 on v16

--- a/solution.py
+++ b/solution.py
@@ -418,7 +418,7 @@
     blocks = dict(zip(rest, add(kept, crossed, [(i,) for i in range(len(rest))])))
     blocks[DIRECT] = straight
     came = [swap(blocks[k], "ep", k) if k else blocks[k] for k in range(peers)]
-    order = [*range(2, peers), 1, 0]
+    order = [*range(1, peers), 0]
     return move(own, back, pick, extra, came, order, last)
 
 

time: 63.1 us -> 64.3 us (1.019)
  waiting for transfers between devices: 14.4 us -> 15.1 us
    ppermute x33, waiting for transfers between devices: 10.5 us -> 11.9 us  [swap(): return lax.ppermute(x, axis, [(i, i ^ bit) for i in range(size)])]
    ppermute x2, waiting for transfers between devices: 3.97 us -> 3.2 us  [diagonal(): return lax.ppermute(x, ('ep', 'et'), pairs)]
  transfers between devices with their start and end apart: 35 -> 35, of which waited for: 17 -> 17; matrix products, arithmetic and copies ran while one was open for 0% -> 0% of each run, Pallas kernels for 13% -> 12%
where the time goes in v18:
time: 64.3 us; the launch traced here: 64.2 us
  starting transfers between devices  35.5 us (55%)
  waiting for transfers between devices  15.1 us (23%)
  Pallas kernels  12.7 us (20%)
  between operations  0.87 us (1%)
    ppermute x33, starting transfers between devices, swap(): return lax.ppermute(x, axis, [(i, i ^ bit) for i in range(size)])  31.9 us
    ppermute x33, waiting for transfers between devices, swap(): return lax.ppermute(x, axis, [(i, i ^ bit) for i in range(size)])  11.9 us
    pallas_call x1, Pallas kernels, load(): pl.pallas_call(load_kernel, in_specs=[ANY] * 3, out_specs=[VMEM] * 3, out...  3.78 us
    ppermute x2, starting transfers between devices, diagonal(): return lax.ppermute(x, ('ep', 'et'), pairs)  3.55 us
    pallas_call x4, Pallas kernels, half_front(): pl.pallas_call(functools.partial(front_kernel, layout, order, flips, sect...  3.33 us
    ppermute x2, waiting for transfers between devices, diagonal(): return lax.ppermute(x, ('ep', 'et'), pairs)  3.2 us
    pallas_call x8, Pallas kernels, down(): pl.pallas_call(functools.partial(down_kernel, flip, len(adds), groups), i...  2.24 us
  transfers between devices with their start and end apart: 35, of which 17 were waited for; matrix products, arithmetic and copies ran while one was open for 0% of the time, Pallas kernels for 12%

profile of v18, /device:TPU:0, one launch (start us, length us, event | category | flops | bytes accessed | tf_op | source)
XLA Modules:
  0.0 64.2 jit_solution(14438741496597199269)
XLA Ops:
  0.6 1.2 %pack.1 = (bf16[24,2176]{1,0:T(8,128)(2,1)S(1)}, bf16[24,2176]{1,0:T(8,128)(2,1)S(1)}, bf16[24,2176]{1,0:T(8,128)(2,1)S(1)}, bf16[32,1024]{1,0:T(8,128)(2,1)S(1)}) custom-call(bf16[32,4096]{1,0:T(8,128)(2,1)} %tokens_ref.3, s32[2,2,32]{2,1,0:T(2,128)} %bitcast.6), custom_call_target="tpu_custom_call" | custom-call | tf_op jit(solution)/shard_map/pack/pallas_call | solution.py:197
  1.9 4.1 %collective-permute-start = (bf16[24,2176]{1,0:T(8,128)(2,1)S(1)}, bf16[24,2176]{1,0:T(8,128)(2,1)S(1)}, u32[]{:S(2)}, u32[]{:S(2)}) collective-permute-start(bf16[24,2176]{1,0:T(8,128)(2,1)S(1)} %get-tuple-element.43), channel_id=1, source_target_pairs={{0,8},{4,12},{8,0},{12,4},{1,9},{5,13},{9,1},{13,5},{2,10},{6,14},... | collective-permute-start | bytes 313352 | tf_op jit(solution)/shard_map/ppermute | solution.py:66
  6.0 1.3 %collective-permute-start.2 = (bf16[24,2176]{1,0:T(8,128)(2,1)S(1)}, bf16[24,2176]{1,0:T(8,128)(2,1)S(1)}, u32[]{:S(2)}, u32[]{:S(2)}) collective-permute-start(bf16[24,2176]{1,0:T(8,128)(2,1)S(1)} %get-tuple-element.45), channel_id=1, source_target_pairs={{0,12},{4,8},{8,4},{12,0},{1,13},{5,9},{9,5},{13,1},{2,14},{6,10},... | collective-permute-start | bytes 313352 | tf_op jit(solution)/shard_map/ppermute | solution.py:66
  7.6 3.8 %load.1 = (bf16[4096,768]{1,0:T(8,128)(2,1)S(1)}, bf16[384,4096]{1,0:T(8,128)(2,1)S(1)}, f32[8,128]{1,0:T(8,128)S(1)}) custom-call(bf16[1,4096,384]{2,1,0:T(8,128)(2,1)} %gate_ref.1, bf16[1,4096,384]{2,1,0:T(8,128)(2,1)} %up_ref.1, bf16[1,384,4096]{2,1,0:T(8,128)(2,1)} %down_ref.1), custom_call_target="tpu_custom_call" | custom-call | bytes 18874368 | tf_op jit(solution)/shard_map/load/pallas_call | solution.py:101
  12.2 2.0 %collective-permute-done.block_ref.refs_7_.refs_11_ = bf16[24,2176]{1,0:T(8,128)(2,1)S(1)} collective-permute-done((bf16[24,2176]{1,0:T(8,128)(2,1)S(1)}, bf16[24,2176]{1,0:T(8,128)(2,1)S(1)}, u32[]{:S(2)}, u32[]{:S(2)}) %collective-permute-start) | collective-permute-done | bytes 104480 | tf_op jit(solution)/shard_map/ppermute | solution.py:66
  19.0 1.9 %collective-permute-start.9 = (bf16[72,1024]{1,0:T(8,128)(2,1)S(1)}, bf16[72,1024]{1,0:T(8,128)(2,1)S(1)}, u32[]{:S(2)}, u32[]{:S(2)}) collective-permute-start(bf16[72,1024]{1,0:T(8,128)(2,1)S(1)} %get-tuple-element.55), channel_id=1, source_target_pairs={{0,2},{1,3},{2,0},{3,1},{4,6},{5,7},{6,4},{7,5},{8,10},{9,11},{10,... | collective-permute-start | bytes 442376 | tf_op jit(solution)/shard_map/ppermute | solution.py:66
  21.2 3.0 %collective-permute-start.12 = (bf16[24,1024]{1,0:T(8,128)(2,1)S(1)}, bf16[24,1024]{1,0:T(8,128)(2,1)S(1)}, u32[]{:S(2)}, u32[]{:S(2)}) collective-permute-start(bf16[24,1024]{1,0:T(8,128)(2,1)S(1)} %get-tuple-element.58), channel_id=1, source_target_pairs={{0,12},{4,8},{8,4},{12,0},{1,13},{5,9},{9,5},{13,1},{2,14},{6,10},... | collective-permute-start | bytes 147464 | tf_op jit(solution)/shard_map/ppermute | solution.py:66
  25.1 1.8 %collective-permute-start.10 = (bf16[24,1024]{1,0:T(8,128)(2,1)S(1)}, bf16[24,1024]{1,0:T(8,128)(2,1)S(1)}, u32[]{:S(2)}, u32[]{:S(2)}) collective-permute-start(bf16[24,1024]{1,0:T(8,128)(2,1)S(1)} %get-tuple-element.56), channel_id=1, source_target_pairs={{0,4},{4,0},{8,12},{12,8},{1,5},{5,1},{9,13},{13,9},{2,6},{6,2},{1... | collective-permute-start | bytes 147464 | tf_op jit(solution)/shard_map/ppermute | solution.py:66
  26.9 2.2 %collective-permute-start.11 = (bf16[24,1024]{1,0:T(8,128)(2,1)S(1)}, bf16[24,1024]{1,0:T(8,128)(2,1)S(1)}, u32[]{:S(2)}, u32[]{:S(2)}) collective-permute-start(bf16[24,1024]{1,0:T(8,128)(2,1)S(1)} %get-tuple-element.57), channel_id=1, source_target_pairs={{0,8},{4,12},{8,0},{12,4},{1,9},{5,13},{9,1},{13,5},{2,10},{6,14},... | collective-permute-start | bytes 147464 | tf_op jit(solution)/shard_map/ppermute | solution.py:66
  29.1 1.9 %collective-permute-done.7.extra_ref = bf16[24,1024]{1,0:T(8,128)(2,1)S(1)} collective-permute-done((bf16[24,1024]{1,0:T(8,128)(2,1)S(1)}, bf16[24,1024]{1,0:T(8,128)(2,1)S(1)}, u32[]{:S(2)}, u32[]{:S(2)}) %collective-permute-start.7) | collective-permute-done | bytes 49184 | tf_op jit(solution)/shard_map/ppermute | solution.py:376
  31.0 1.0 %collective-permute-done.11.refs_1_ = bf16[24,1024]{1,0:T(8,128)(2,1)S(1)} collective-permute-done((bf16[24,1024]{1,0:T(8,128)(2,1)S(1)}, bf16[24,1024]{1,0:T(8,128)(2,1)S(1)}, u32[]{:S(2)}, u32[]{:S(2)}) %collective-permute-start.11) | collective-permute-done | bytes 49184 | tf_op jit(solution)/shard_map/ppermute | solution.py:66
  32.4 2.1 %collective-permute-start.13 = (bf16[24,1024]{1,0:T(8,128)(2,1)S(1)}, bf16[24,1024]{1,0:T(8,128)(2,1)S(1)}, u32[]{:S(2)}, u32[]{:S(2)}) collective-permute-start(bf16[24,1024]{1,0:T(8,128)(2,1)S(1)} %get-tuple-element.62), channel_id=1, source_target_pairs={{0,8},{4,12},{8,0},{12,4},{1,9},{5,13},{9,1},{13,5},{2,10},{6,14},... | collective-permute-start | bytes 147464 | tf_op jit(solution)/shard_map/ppermute | solution.py:66
  34.5 1.9 %collective-permute-start.17 = (bf16[24,1024]{1,0:T(8,128)(2,1)S(1)}, bf16[24,1024]{1,0:T(8,128)(2,1)S(1)}, u32[]{:S(2)}, u32[]{:S(2)}) collective-permute-start(bf16[24,1024]{1,0:T(8,128)(2,1)S(1)} %get-tuple-element.63), channel_id=1, source_target_pairs={{0,12},{4,8},{8,4},{12,0},{1,13},{5,9},{9,5},{13,1},{2,14},{6,10},... | collective-permute-start | bytes 147464 | tf_op jit(solution)/shard_map/ppermute | solution.py:66
  36.5 1.4 %collective-permute-start.26 = (bf16[24,1024]{1,0:T(8,128)(2,1)S(1)}, bf16[24,1024]{1,0:T(8,128)(2,1)S(1)}, u32[]{:S(2)}, u32[]{:S(2)}) collective-permute-start(bf16[24,1024]{1,0:T(8,128)(2,1)S(1)} %get-tuple-element.65.refs_6_), channel_id=1, source_target_pairs={{0,2},{1,3},{2,0},{3,1},{4,6},{5,7},{6,4},{7,5},{8,10},{9,11},{10,... | collective-permute-start | bytes 147464 | tf_op jit(solution)/shard_map/ppermute | solution.py:66
  38.2 1.6 %collective-permute-start.15 = (bf16[24,1024]{1,0:T(8,128)(2,1)S(1)}, bf16[24,1024]{1,0:T(8,128)(2,1)S(1)}, u32[]{:S(2)}, u32[]{:S(2)}) collective-permute-start(bf16[24,1024]{1,0:T(8,128)(2,1)S(1)} %collective-permute-done.13.refs_0_), channel_id=1, source_target_pairs={{0,2},{1,3},{2,0},{3,1},{4,6},{5,7},{6,4},{7,5},{8,10},{9,11},{10,... | collective-permute-start | bytes 147464 | tf_op jit(solution)/shard_map/ppermute | solution.py:66
  40.5 1.4 %collective-permute-start.19 = (bf16[24,1024]{1,0:T(8,128)(2,1)S(1)}, bf16[24,1024]{1,0:T(8,128)(2,1)S(1)}, u32[]{:S(2)}, u32[]{:S(2)}) collective-permute-start(bf16[24,1024]{1,0:T(8,128)(2,1)S(1)} %collective-permute-done.17.refs_2_), channel_id=1, source_target_pairs={{0,2},{1,3},{2,0},{3,1},{4,6},{5,7},{6,4},{7,5},{8,10},{9,11},{10,... | collective-permute-start | bytes 147464 | tf_op jit(solution)/shard_map/ppermute | solution.py:66
  43.1 1.5 %collective-permute-done.19.refs_3_ = bf16[24,1024]{1,0:T(8,128)(2,1)S(1)} collective-permute-done((bf16[24,1024]{1,0:T(8,128)(2,1)S(1)}, bf16[24,1024]{1,0:T(8,128)(2,1)S(1)}, u32[]{:S(2)}, u32[]{:S(2)}) %collective-permute-start.19) | collective-permute-done | bytes 49184 | tf_op jit(solution)/shard_map/ppermute | solution.py:66
  44.6 1.4 %collective-permute-done.23.refs_5_ = bf16[24,1024]{1,0:T(8,128)(2,1)S(1)} collective-permute-done((bf16[24,1024]{1,0:T(8,128)(2,1)S(1)}, bf16[24,1024]{1,0:T(8,128)(2,1)S(1)}, u32[]{:S(2)}, u32[]{:S(2)}) %collective-permute-start.23) | collective-permute-done | bytes 49184 | tf_op jit(solution)/shard_map/ppermute | solution.py:66
  51.6 1.9 %collective-permute-start.34 = (bf16[24,1024]{1,0:T(8,128)(2,1)S(1)}, bf16[24,1024]{1,0:T(8,128)(2,1)S(1)}, u32[]{:S(2)}, u32[]{:S(2)}) collective-permute-start(bf16[24,1024]{1,0:T(8,128)(2,1)S(1)} %get-tuple-element.74), channel_id=1, source_target_pairs={{0,12},{4,8},{8,4},{12,0},{1,13},{5,9},{9,5},{13,1},{2,14},{6,10},... | collective-permute-start | bytes 147464 | tf_op jit(solution)/shard_map/ppermute | solution.py:66
  53.6 2.8 %collective-permute-start.29 = (bf16[24,1024]{1,0:T(8,128)(2,1)S(1)}, bf16[24,1024]{1,0:T(8,128)(2,1)S(1)}, u32[]{:S(2)}, u32[]{:S(2)}) collective-permute-start(bf16[24,1024]{1,0:T(8,128)(2,1)S(1)} %get-tuple-element.69), channel_id=1, source_target_pairs={{0,14},{1,15},{2,12},{3,13},{4,10},{5,11},{6,8},{7,9},{8,6},{9,7},... | collective-permute-start | bytes 147464 | tf_op jit(solution)/shard_map/ppermute | solution.py:376
  56.7 1.2 %collective-permute-start.32 = (bf16[24,1024]{1,0:T(8,128)(2,1)S(1)}, bf16[24,1024]{1,0:T(8,128)(2,1)S(1)}, u32[]{:S(2)}, u32[]{:S(2)}) collective-permute-start(bf16[24,1024]{1,0:T(8,128)(2,1)S(1)} %get-tuple-element.72), channel_id=1, source_target_pairs={{0,4},{4,0},{8,12},{12,8},{1,5},{5,1},{9,13},{13,9},{2,6},{6,2},{1... | collective-permute-start | bytes 147464 | tf_op jit(solution)/shard_map/ppermute | solution.py:66
  57.8 1.3 %collective-permute-start.33 = (bf16[24,1024]{1,0:T(8,128)(2,1)S(1)}, bf16[24,1024]{1,0:T(8,128)(2,1)S(1)}, u32[]{:S(2)}, u32[]{:S(2)}) collective-permute-start(bf16[24,1024]{1,0:T(8,128)(2,1)S(1)} %get-tuple-element.73), channel_id=1, source_target_pairs={{0,8},{4,12},{8,0},{12,4},{1,9},{5,13},{9,1},{13,5},{2,10},{6,14},... | collective-permute-start | bytes 147464 | tf_op jit(solution)/shard_map/ppermute | solution.py:66
  59.1 1.3 %collective-permute-done.29.extra_ref = bf16[24,1024]{1,0:T(8,128)(2,1)S(1)} collective-permute-done((bf16[24,1024]{1,0:T(8,128)(2,1)S(1)}, bf16[24,1024]{1,0:T(8,128)(2,1)S(1)}, u32[]{:S(2)}, u32[]{:S(2)}) %collective-permute-start.29) | collective-permute-done | bytes 49184 | tf_op jit(solution)/shard_map/ppermute | solution.py:376
  61.3 2.0 %collective-permute-done.33.refs_1_ = bf16[24,1024]{1,0:T(8,128)(2,1)S(1)} collective-permute-done((bf16[24,1024]{1,0:T(8,128)(2,1)S(1)}, bf16[24,1024]{1,0:T(8,128)(2,1)S(1)}, u32[]{:S(2)}, u32[]{:S(2)}) %collective-permute-start.33) | collective-permute-done | bytes 49184 | tf_op jit(solution)/shard_map/ppermute | solution.py:66
  (78 shorter events, 17.2 us)
Async XLA Ops:
  1.9 12.4 %collective-permute-start = (bf16[24,2176]{1,0:T(8,128)(2,1)S(1)}, bf16[24,2176]{1,0:T(8,128)(2,1)S(1)}, u32[]{:S(2)}, u32[]{:S(2)}) collective-permute-start(bf16[24,2176]{1,0:T(8,128)(2,1)S(1)} %get-tuple-element.43), channel_id=1, source_target_pairs={{0,8},{4,12},{8,0},{12,4},{1,9},{5,13},{9,1},{13,5},{2,10},{6,14},... | collective-permute-start | bytes 313352 | tf_op jit(solution)/shard_map/ppermute | solution.py:66
  6.0 8.4 %collective-permute-start.2 = (bf16[24,2176]{1,0:T(8,128)(2,1)S(1)}, bf16[24,2176]{1,0:T(8,128)(2,1)S(1)}, u32[]{:S(2)}, u32[]{:S(2)}) collective-permute-start(bf16[24,2176]{1,0:T(8,128)(2,1)S(1)} %get-tuple-element.45), channel_id=1, source_target_pairs={{0,12},{4,8},{8,4},{12,0},{1,13},{5,9},{9,5},{13,1},{2,14},{6,10},... | collective-permute-start | bytes 313352 | tf_op jit(solution)/shard_map/ppermute | solution.py:66
  7.3 7.6 %collective-permute-start.4 = (bf16[24,2176]{1,0:T(8,128)(2,1)S(1)}, bf16[24,2176]{1,0:T(8,128)(2,1)S(1)}, u32[]{:S(2)}, u32[]{:S(2)}) collective-permute-start(bf16[24,2176]{1,0:T(8,128)(2,1)S(1)} %get-tuple-element.46), channel_id=1, source_target_pairs={{0,4},{4,0},{8,12},{12,8},{1,5},{5,1},{9,13},{13,9},{2,6},{6,2},{1... | collective-permute-start | bytes 313352 | tf_op jit(solution)/shard_map/ppermute | solution.py:66
  19.0 6.1 %collective-permute-start.9 = (bf16[72,1024]{1,0:T(8,128)(2,1)S(1)}, bf16[72,1024]{1,0:T(8,128)(2,1)S(1)}, u32[]{:S(2)}, u32[]{:S(2)}) collective-permute-start(bf16[72,1024]{1,0:T(8,128)(2,1)S(1)} %get-tuple-element.55), channel_id=1, source_target_pairs={{0,2},{1,3},{2,0},{3,1},{4,6},{5,7},{6,4},{7,5},{8,10},{9,11},{10,... | collective-permute-start | bytes 442376 | tf_op jit(solution)/shard_map/ppermute | solution.py:66
  21.2 7.9 %collective-permute-start.12 = (bf16[24,1024]{1,0:T(8,128)(2,1)S(1)}, bf16[24,1024]{1,0:T(8,128)(2,1)S(1)}, u32[]{:S(2)}, u32[]{:S(2)}) collective-permute-start(bf16[24,1024]{1,0:T(8,128)(2,1)S(1)} %get-tuple-element.58), channel_id=1, source_target_pairs={{0,12},{4,8},{8,4},{12,0},{1,13},{5,9},{9,5},{13,1},{2,14},{6,10},... | collective-permute-start | bytes 147464 | tf_op jit(solution)/shard_map/ppermute | solution.py:66
  24.2 6.8 %collective-permute-start.7 = (bf16[24,1024]{1,0:T(8,128)(2,1)S(1)}, bf16[24,1024]{1,0:T(8,128)(2,1)S(1)}, u32[]{:S(2)}, u32[]{:S(2)}) collective-permute-start(bf16[24,1024]{1,0:T(8,128)(2,1)S(1)} %get-tuple-element.53), channel_id=1, source_target_pairs={{0,14},{1,15},{2,12},{3,13},{4,10},{5,11},{6,8},{7,9},{8,6},{9,7},... | collective-permute-start | bytes 147464 | tf_op jit(solution)/shard_map/ppermute | solution.py:376
  25.1 5.9 %collective-permute-start.10 = (bf16[24,1024]{1,0:T(8,128)(2,1)S(1)}, bf16[24,1024]{1,0:T(8,128)(2,1)S(1)}, u32[]{:S(2)}, u32[]{:S(2)}) collective-permute-start(bf16[24,1024]{1,0:T(8,128)(2,1)S(1)} %get-tuple-element.56), channel_id=1, source_target_pairs={{0,4},{4,0},{8,12},{12,8},{1,5},{5,1},{9,13},{13,9},{2,6},{6,2},{1... | collective-permute-start | bytes 147464 | tf_op jit(solution)/shard_map/ppermute | solution.py:66
  26.9 5.1 %collective-permute-start.11 = (bf16[24,1024]{1,0:T(8,128)(2,1)S(1)}, bf16[24,1024]{1,0:T(8,128)(2,1)S(1)}, u32[]{:S(2)}, u32[]{:S(2)}) collective-permute-start(bf16[24,1024]{1,0:T(8,128)(2,1)S(1)} %get-tuple-element.57), channel_id=1, source_target_pairs={{0,8},{4,12},{8,0},{12,4},{1,9},{5,13},{9,1},{13,5},{2,10},{6,14},... | collective-permute-start | bytes 147464 | tf_op jit(solution)/shard_map/ppermute | solution.py:66
  32.4 5.8 %collective-permute-start.13 = (bf16[24,1024]{1,0:T(8,128)(2,1)S(1)}, bf16[24,1024]{1,0:T(8,128)(2,1)S(1)}, u32[]{:S(2)}, u32[]{:S(2)}) collective-permute-start(bf16[24,1024]{1,0:T(8,128)(2,1)S(1)} %get-tuple-element.62), channel_id=1, source_target_pairs={{0,8},{4,12},{8,0},{12,4},{1,9},{5,13},{9,1},{13,5},{2,10},{6,14},... | collective-permute-start | bytes 147464 | tf_op jit(solution)/shard_map/ppermute | solution.py:66
  34.5 6.0 %collective-permute-start.17 = (bf16[24,1024]{1,0:T(8,128)(2,1)S(1)}, bf16[24,1024]{1,0:T(8,128)(2,1)S(1)}, u32[]{:S(2)}, u32[]{:S(2)}) collective-permute-start(bf16[24,1024]{1,0:T(8,128)(2,1)S(1)} %get-tuple-element.63), channel_id=1, source_target_pairs={{0,12},{4,8},{8,4},{12,0},{1,13},{5,9},{9,5},{13,1},{2,14},{6,10},... | collective-permute-start | bytes 147464 | tf_op jit(solution)/shard_map/ppermute | solution.py:66
  36.4 5.6 %collective-permute-start.21 = (bf16[24,1024]{1,0:T(8,128)(2,1)S(1)}, bf16[24,1024]{1,0:T(8,128)(2,1)S(1)}, u32[]{:S(2)}, u32[]{:S(2)}) collective-permute-start(bf16[24,1024]{1,0:T(8,128)(2,1)S(1)} %get-tuple-element.64), channel_id=1, source_target_pairs={{0,4},{4,0},{8,12},{12,8},{1,5},{5,1},{9,13},{13,9},{2,6},{6,2},{1... | collective-permute-start | bytes 147464 | tf_op jit(solution)/shard_map/ppermute | solution.py:66
  36.5 6.1 %collective-permute-start.26 = (bf16[24,1024]{1,0:T(8,128)(2,1)S(1)}, bf16[24,1024]{1,0:T(8,128)(2,1)S(1)}, u32[]{:S(2)}, u32[]{:S(2)}) collective-permute-start(bf16[24,1024]{1,0:T(8,128)(2,1)S(1)} %get-tuple-element.65.refs_6_), channel_id=1, source_target_pairs={{0,2},{1,3},{2,0},{3,1},{4,6},{5,7},{6,4},{7,5},{8,10},{9,11},{10,... | collective-permute-start | bytes 147464 | tf_op jit(solution)/shard_map/ppermute | solution.py:66
  37.9 4.7 %collective-permute-start.25 = (bf16[24,1024]{1,0:T(8,128)(2,1)S(1)}, bf16[24,1024]{1,0:T(8,128)(2,1)S(1)}, u32[]{:S(2)}, u32[]{:S(2)}) collective-permute-start(bf16[24,1024]{1,0:T(8,128)(2,1)S(1)} %get-tuple-element.65.refs_6_), channel_id=1, source_target_pairs={{0,1},{1,0},{2,3},{3,2},{4,5},{5,4},{6,7},{7,6},{8,9},{9,8},{10,11... | collective-permute-start | bytes 147464 | tf_op jit(solution)/shard_map/ppermute | solution.py:66
  38.2 4.9 %collective-permute-start.15 = (bf16[24,1024]{1,0:T(8,128)(2,1)S(1)}, bf16[24,1024]{1,0:T(8,128)(2,1)S(1)}, u32[]{:S(2)}, u32[]{:S(2)}) collective-permute-start(bf16[24,1024]{1,0:T(8,128)(2,1)S(1)} %collective-permute-done.13.refs_0_), channel_id=1, source_target_pairs={{0,2},{1,3},{2,0},{3,1},{4,6},{5,7},{6,4},{7,5},{8,10},{9,11},{10,... | collective-permute-start | bytes 147464 | tf_op jit(solution)/shard_map/ppermute | solution.py:66
  40.5 4.1 %collective-permute-start.19 = (bf16[24,1024]{1,0:T(8,128)(2,1)S(1)}, bf16[24,1024]{1,0:T(8,128)(2,1)S(1)}, u32[]{:S(2)}, u32[]{:S(2)}) collective-permute-start(bf16[24,1024]{1,0:T(8,128)(2,1)S(1)} %collective-permute-done.17.refs_2_), channel_id=1, source_target_pairs={{0,2},{1,3},{2,0},{3,1},{4,6},{5,7},{6,4},{7,5},{8,10},{9,11},{10,... | collective-permute-start | bytes 147464 | tf_op jit(solution)/shard_map/ppermute | solution.py:66
  42.0 4.1 %collective-permute-start.23 = (bf16[24,1024]{1,0:T(8,128)(2,1)S(1)}, bf16[24,1024]{1,0:T(8,128)(2,1)S(1)}, u32[]{:S(2)}, u32[]{:S(2)}) collective-permute-start(bf16[24,1024]{1,0:T(8,128)(2,1)S(1)} %collective-permute-done.21.refs_4_), channel_id=1, source_target_pairs={{0,2},{1,3},{2,0},{3,1},{4,6},{5,7},{6,4},{7,5},{8,10},{9,11},{10,... | collective-permute-start | bytes 147464 | tf_op jit(solution)/shard_map/ppermute | solution.py:66
  42.6 3.5 %collective-permute-start.14 = (bf16[24,1024]{1,0:T(8,128)(2,1)S(1)}, bf16[24,1024]{1,0:T(8,128)(2,1)S(1)}, u32[]{:S(2)}, u32[]{:S(2)}) collective-permute-start(bf16[24,1024]{1,0:T(8,128)(2,1)S(1)} %collective-permute-done.13.refs_0_), channel_id=1, source_target_pairs={{0,1},{1,0},{2,3},{3,2},{4,5},{5,4},{6,7},{7,6},{8,9},{9,8},{10,11... | collective-permute-start | bytes 147464 | tf_op jit(solution)/shard_map/ppermute | solution.py:66
  42.6 4.0 %collective-permute-start.18 = (bf16[24,1024]{1,0:T(8,128)(2,1)S(1)}, bf16[24,1024]{1,0:T(8,128)(2,1)S(1)}, u32[]{:S(2)}, u32[]{:S(2)}) collective-permute-start(bf16[24,1024]{1,0:T(8,128)(2,1)S(1)} %collective-permute-done.17.refs_2_), channel_id=1, source_target_pairs={{0,1},{1,0},{2,3},{3,2},{4,5},{5,4},{6,7},{7,6},{8,9},{9,8},{10,11... | collective-permute-start | bytes 147464 | tf_op jit(solution)/shard_map/ppermute | solution.py:66
  43.1 4.3 %collective-permute-start.22 = (bf16[24,1024]{1,0:T(8,128)(2,1)S(1)}, bf16[24,1024]{1,0:T(8,128)(2,1)S(1)}, u32[]{:S(2)}, u32[]{:S(2)}) collective-permute-start(bf16[24,1024]{1,0:T(8,128)(2,1)S(1)} %collective-permute-done.21.refs_4_), channel_id=1, source_target_pairs={{0,1},{1,0},{2,3},{3,2},{4,5},{5,4},{6,7},{7,6},{8,9},{9,8},{10,11... | collective-permute-start | bytes 147464 | tf_op jit(solution)/shard_map/ppermute | solution.py:66
  50.7 6.0 %collective-permute-start.31 = (bf16[72,1024]{1,0:T(8,128)(2,1)S(1)}, bf16[72,1024]{1,0:T(8,128)(2,1)S(1)}, u32[]{:S(2)}, u32[]{:S(2)}) collective-permute-start(bf16[72,1024]{1,0:T(8,128)(2,1)S(1)} %get-tuple-element.71), channel_id=1, source_target_pairs={{0,2},{1,3},{2,0},{3,1},{4,6},{5,7},{6,4},{7,5},{8,10},{9,11},{10,... | collective-permute-start | bytes 442376 | tf_op jit(solution)/shard_map/ppermute | solution.py:66
  51.6 7.5 %collective-permute-start.34 = (bf16[24,1024]{1,0:T(8,128)(2,1)S(1)}, bf16[24,1024]{1,0:T(8,128)(2,1)S(1)}, u32[]{:S(2)}, u32[]{:S(2)}) collective-permute-start(bf16[24,1024]{1,0:T(8,128)(2,1)S(1)} %get-tuple-element.74), channel_id=1, source_target_pairs={{0,12},{4,8},{8,4},{12,0},{1,13},{5,9},{9,5},{13,1},{2,14},{6,10},... | collective-permute-start | bytes 147464 | tf_op jit(solution)/shard_map/ppermute | solution.py:66
  53.6 6.8 %collective-permute-start.29 = (bf16[24,1024]{1,0:T(8,128)(2,1)S(1)}, bf16[24,1024]{1,0:T(8,128)(2,1)S(1)}, u32[]{:S(2)}, u32[]{:S(2)}) collective-permute-start(bf16[24,1024]{1,0:T(8,128)(2,1)S(1)} %get-tuple-element.69), channel_id=1, source_target_pairs={{0,14},{1,15},{2,12},{3,13},{4,10},{5,11},{6,8},{7,9},{8,6},{9,7},... | collective-permute-start | bytes 147464 | tf_op jit(solution)/shard_map/ppermute | solution.py:376
  56.7 4.6 %collective-permute-start.32 = (bf16[24,1024]{1,0:T(8,128)(2,1)S(1)}, bf16[24,1024]{1,0:T(8,128)(2,1)S(1)}, u32[]{:S(2)}, u32[]{:S(2)}) collective-permute-start(bf16[24,1024]{1,0:T(8,128)(2,1)S(1)} %get-tuple-element.72), channel_id=1, source_target_pairs={{0,4},{4,0},{8,12},{12,8},{1,5},{5,1},{9,13},{13,9},{2,6},{6,2},{1... | collective-permute-start | bytes 147464 | tf_op jit(solution)/shard_map/ppermute | solution.py:66
  57.8 5.5 %collective-permute-start.33 = (bf16[24,1024]{1,0:T(8,128)(2,1)S(1)}, bf16[24,1024]{1,0:T(8,128)(2,1)S(1)}, u32[]{:S(2)}, u32[]{:S(2)}) collective-permute-start(bf16[24,1024]{1,0:T(8,128)(2,1)S(1)} %get-tuple-element.73), channel_id=1, source_target_pairs={{0,8},{4,12},{8,0},{12,4},{1,9},{5,13},{9,1},{13,5},{2,10},{6,14},... | collective-permute-start | bytes 147464 | tf_op jit(solution)/shard_map/ppermute | solution.py:66
  (15 other events, 42.4 us)

commit v19 on v16

--- a/solution.py
+++ b/solution.py
@@ -160,7 +160,10 @@
     for s, one in enumerate(ids):
         lane = lax.broadcasted_iota(jnp.int32, (LANES, rows), 0)
         hits = [jnp.where(one[p : p + 1, :] + s * experts == lane, 1.0, 0.0) for p in range(one.shape[0])]
-        flags.append(product(held[s], sum(hits).T))
+        over_rows = (((1,), (1,)), ((), ()))
+        flags.append(
+            lax.dot_general(narrow(held[s]), narrow(sum(hits)), over_rows, preferred_element_type=jnp.float32)
+        )
     return sum(flags)
 
 

time: 63.1 us -> 63.1 us (level)
  transfers between devices with their start and end apart: 35 -> 35, of which waited for: 17 -> 17; matrix products, arithmetic and copies ran while one was open for 0% -> 0% of each run, Pallas kernels for 13% -> 12%
where the time goes in v19:
time: 63.1 us; the launch traced here: 62.9 us
  starting transfers between devices  34.9 us (55%)
  waiting for transfers between devices  14.5 us (23%)
  Pallas kernels  12.7 us (20%)
  between operations  0.87 us (1%)
    ppermute x33, starting transfers between devices, swap(): return lax.ppermute(x, axis, [(i, i ^ bit) for i in range(size)])  31.4 us
    ppermute x33, waiting for transfers between devices, swap(): return lax.ppermute(x, axis, [(i, i ^ bit) for i in range(size)])  10.5 us
    ppermute x2, waiting for transfers between devices, diagonal(): return lax.ppermute(x, ('ep', 'et'), pairs)  3.99 us
    pallas_call x1, Pallas kernels, load(): pl.pallas_call(load_kernel, in_specs=[ANY] * 3, out_specs=[VMEM] * 3, out...  3.78 us
    ppermute x2, starting transfers between devices, diagonal(): return lax.ppermute(x, ('ep', 'et'), pairs)  3.44 us
    pallas_call x4, Pallas kernels, half_front(): pl.pallas_call(functools.partial(front_kernel, layout, order, flips, sect...  3.34 us
    pallas_call x8, Pallas kernels, down(): pl.pallas_call(functools.partial(down_kernel, flip, len(adds), groups), i...  2.23 us
    pallas_call x1, Pallas kernels, pack(): pl.pallas_call(functools.partial(pack_kernel, experts), in_specs=[ANY] *...  1.26 us
  transfers between devices with their start and end apart: 35, of which 17 were waited for; matrix products, arithmetic and copies ran while one was open for 0% of the time, Pallas kernels for 12%

profile of v19, /device:TPU:0, one launch (start us, length us, event | category | flops | bytes accessed | tf_op | source)
XLA Modules:
  0.0 62.9 jit_solution(8860846901086428092)
XLA Ops:
  0.6 1.3 %pack.1 = (bf16[24,2176]{1,0:T(8,128)(2,1)S(1)}, bf16[24,2176]{1,0:T(8,128)(2,1)S(1)}, bf16[24,2176]{1,0:T(8,128)(2,1)S(1)}, bf16[32,1024]{1,0:T(8,128)(2,1)S(1)}) custom-call(bf16[32,4096]{1,0:T(8,128)(2,1)} %tokens_ref.3, s32[2,2,32]{2,1,0:T(2,128)} %bitcast.6), custom_call_target="tpu_custom_call" | custom-call | tf_op jit(solution)/shard_map/pack/pallas_call | solution.py:200
  1.9 4.1 %collective-permute-start = (bf16[24,2176]{1,0:T(8,128)(2,1)S(1)}, bf16[24,2176]{1,0:T(8,128)(2,1)S(1)}, u32[]{:S(2)}, u32[]{:S(2)}) collective-permute-start(bf16[24,2176]{1,0:T(8,128)(2,1)S(1)} %get-tuple-element.43), channel_id=1, source_target_pairs={{0,8},{4,12},{8,0},{12,4},{1,9},{5,13},{9,1},{13,5},{2,10},{6,14},... | collective-permute-start | bytes 313352 | tf_op jit(solution)/shard_map/ppermute | solution.py:66
  6.0 1.3 %collective-permute-start.2 = (bf16[24,2176]{1,0:T(8,128)(2,1)S(1)}, bf16[24,2176]{1,0:T(8,128)(2,1)S(1)}, u32[]{:S(2)}, u32[]{:S(2)}) collective-permute-start(bf16[24,2176]{1,0:T(8,128)(2,1)S(1)} %get-tuple-element.45), channel_id=1, source_target_pairs={{0,12},{4,8},{8,4},{12,0},{1,13},{5,9},{9,5},{13,1},{2,14},{6,10},... | collective-permute-start | bytes 313352 | tf_op jit(solution)/shard_map/ppermute | solution.py:66
  7.7 3.8 %load.1 = (bf16[4096,768]{1,0:T(8,128)(2,1)S(1)}, bf16[384,4096]{1,0:T(8,128)(2,1)S(1)}, f32[8,128]{1,0:T(8,128)S(1)}) custom-call(bf16[1,4096,384]{2,1,0:T(8,128)(2,1)} %gate_ref.1, bf16[1,4096,384]{2,1,0:T(8,128)(2,1)} %up_ref.1, bf16[1,384,4096]{2,1,0:T(8,128)(2,1)} %down_ref.1), custom_call_target="tpu_custom_call" | custom-call | bytes 18874368 | tf_op jit(solution)/shard_map/load/pallas_call | solution.py:101
  12.2 2.0 %collective-permute-done.block_ref.refs_7_.refs_11_ = bf16[24,2176]{1,0:T(8,128)(2,1)S(1)} collective-permute-done((bf16[24,2176]{1,0:T(8,128)(2,1)S(1)}, bf16[24,2176]{1,0:T(8,128)(2,1)S(1)}, u32[]{:S(2)}, u32[]{:S(2)}) %collective-permute-start) | collective-permute-done | bytes 104480 | tf_op jit(solution)/shard_map/ppermute | solution.py:66
  19.1 1.9 %collective-permute-start.9 = (bf16[72,1024]{1,0:T(8,128)(2,1)S(1)}, bf16[72,1024]{1,0:T(8,128)(2,1)S(1)}, u32[]{:S(2)}, u32[]{:S(2)}) collective-permute-start(bf16[72,1024]{1,0:T(8,128)(2,1)S(1)} %get-tuple-element.55), channel_id=1, source_target_pairs={{0,2},{1,3},{2,0},{3,1},{4,6},{5,7},{6,4},{7,5},{8,10},{9,11},{10,... | collective-permute-start | bytes 442376 | tf_op jit(solution)/shard_map/ppermute | solution.py:66
  21.2 3.0 %collective-permute-start.11 = (bf16[24,1024]{1,0:T(8,128)(2,1)S(1)}, bf16[24,1024]{1,0:T(8,128)(2,1)S(1)}, u32[]{:S(2)}, u32[]{:S(2)}) collective-permute-start(bf16[24,1024]{1,0:T(8,128)(2,1)S(1)} %get-tuple-element.57), channel_id=1, source_target_pairs={{0,12},{4,8},{8,4},{12,0},{1,13},{5,9},{9,5},{13,1},{2,14},{6,10},... | collective-permute-start | bytes 147464 | tf_op jit(solution)/shard_map/ppermute | solution.py:66
  25.2 3.9 %collective-permute-start.10 = (bf16[24,1024]{1,0:T(8,128)(2,1)S(1)}, bf16[24,1024]{1,0:T(8,128)(2,1)S(1)}, u32[]{:S(2)}, u32[]{:S(2)}) collective-permute-start(bf16[24,1024]{1,0:T(8,128)(2,1)S(1)} %get-tuple-element.56), channel_id=1, source_target_pairs={{0,8},{4,12},{8,0},{12,4},{1,9},{5,13},{9,1},{13,5},{2,10},{6,14},... | collective-permute-start | bytes 147464 | tf_op jit(solution)/shard_map/ppermute | solution.py:66
  29.1 2.5 %collective-permute-done.7.extra_ref = bf16[24,1024]{1,0:T(8,128)(2,1)S(1)} collective-permute-done((bf16[24,1024]{1,0:T(8,128)(2,1)S(1)}, bf16[24,1024]{1,0:T(8,128)(2,1)S(1)}, u32[]{:S(2)}, u32[]{:S(2)}) %collective-permute-start.7) | collective-permute-done | bytes 49184 | tf_op jit(solution)/shard_map/ppermute | solution.py:379
  32.0 1.2 %collective-permute-done.12.refs_2_ = bf16[24,1024]{1,0:T(8,128)(2,1)S(1)} collective-permute-done((bf16[24,1024]{1,0:T(8,128)(2,1)S(1)}, bf16[24,1024]{1,0:T(8,128)(2,1)S(1)}, u32[]{:S(2)}, u32[]{:S(2)}) %collective-permute-start.12) | collective-permute-done | bytes 49184 | tf_op jit(solution)/shard_map/ppermute | solution.py:66
  33.5 1.0 %collective-permute-start.13 = (bf16[24,1024]{1,0:T(8,128)(2,1)S(1)}, bf16[24,1024]{1,0:T(8,128)(2,1)S(1)}, u32[]{:S(2)}, u32[]{:S(2)}) collective-permute-start(bf16[24,1024]{1,0:T(8,128)(2,1)S(1)} %get-tuple-element.62), channel_id=1, source_target_pairs={{0,8},{4,12},{8,0},{12,4},{1,9},{5,13},{9,1},{13,5},{2,10},{6,14},... | collective-permute-start | bytes 147464 | tf_op jit(solution)/shard_map/ppermute | solution.py:66
  34.4 2.0 %collective-permute-start.17 = (bf16[24,1024]{1,0:T(8,128)(2,1)S(1)}, bf16[24,1024]{1,0:T(8,128)(2,1)S(1)}, u32[]{:S(2)}, u32[]{:S(2)}) collective-permute-start(bf16[24,1024]{1,0:T(8,128)(2,1)S(1)} %get-tuple-element.63), channel_id=1, source_target_pairs={{0,12},{4,8},{8,4},{12,0},{1,13},{5,9},{9,5},{13,1},{2,14},{6,10},... | collective-permute-start | bytes 147464 | tf_op jit(solution)/shard_map/ppermute | solution.py:66
  37.0 1.4 %collective-permute-start.26 = (bf16[24,1024]{1,0:T(8,128)(2,1)S(1)}, bf16[24,1024]{1,0:T(8,128)(2,1)S(1)}, u32[]{:S(2)}, u32[]{:S(2)}) collective-permute-start(bf16[24,1024]{1,0:T(8,128)(2,1)S(1)} %get-tuple-element.65.refs_6_), channel_id=1, source_target_pairs={{0,2},{1,3},{2,0},{3,1},{4,6},{5,7},{6,4},{7,5},{8,10},{9,11},{10,... | collective-permute-start | bytes 147464 | tf_op jit(solution)/shard_map/ppermute | solution.py:66
  39.0 1.4 %collective-permute-start.15 = (bf16[24,1024]{1,0:T(8,128)(2,1)S(1)}, bf16[24,1024]{1,0:T(8,128)(2,1)S(1)}, u32[]{:S(2)}, u32[]{:S(2)}) collective-permute-start(bf16[24,1024]{1,0:T(8,128)(2,1)S(1)} %collective-permute-done.13.refs_0_), channel_id=1, source_target_pairs={{0,2},{1,3},{2,0},{3,1},{4,6},{5,7},{6,4},{7,5},{8,10},{9,11},{10,... | collective-permute-start | bytes 147464 | tf_op jit(solution)/shard_map/ppermute | solution.py:66
  40.5 1.3 %collective-permute-start.19 = (bf16[24,1024]{1,0:T(8,128)(2,1)S(1)}, bf16[24,1024]{1,0:T(8,128)(2,1)S(1)}, u32[]{:S(2)}, u32[]{:S(2)}) collective-permute-start(bf16[24,1024]{1,0:T(8,128)(2,1)S(1)} %collective-permute-done.17.refs_2_), channel_id=1, source_target_pairs={{0,2},{1,3},{2,0},{3,1},{4,6},{5,7},{6,4},{7,5},{8,10},{9,11},{10,... | collective-permute-start | bytes 147464 | tf_op jit(solution)/shard_map/ppermute | solution.py:66
  43.3 1.2 %collective-permute-done.19.refs_3_ = bf16[24,1024]{1,0:T(8,128)(2,1)S(1)} collective-permute-done((bf16[24,1024]{1,0:T(8,128)(2,1)S(1)}, bf16[24,1024]{1,0:T(8,128)(2,1)S(1)}, u32[]{:S(2)}, u32[]{:S(2)}) %collective-permute-start.19) | collective-permute-done | bytes 49184 | tf_op jit(solution)/shard_map/ppermute | solution.py:66
  44.6 1.3 %collective-permute-done.23.refs_5_ = bf16[24,1024]{1,0:T(8,128)(2,1)S(1)} collective-permute-done((bf16[24,1024]{1,0:T(8,128)(2,1)S(1)}, bf16[24,1024]{1,0:T(8,128)(2,1)S(1)}, u32[]{:S(2)}, u32[]{:S(2)}) %collective-permute-start.23) | collective-permute-done | bytes 49184 | tf_op jit(solution)/shard_map/ppermute | solution.py:66
  47.6 1.0 %front.7.hidden_ref = bf16[96,384]{1,0:T(8,128)(2,1)S(1)} custom-call(bf16[24,1024]{1,0:T(8,128)(2,1)S(1)} %collective-permute-done.14.refs_0_, bf16[24,1024]{1,0:T(8,128)(2,1)S(1)} %collective-permute-done.16.refs_1_, bf16[24,1024]{1,0:T(8,128)(2,1)S(1)} %collective-permute-done.18.refs_2_, bf16[24,1024]{1,0:T(8,128)(2,1)S(1)} %collective-permute-done.20.refs_3_, ...), custom_call_target="tpu_custom_call" | custom-call | flops 301989888 | bytes 3145728 | tf_op jit(solution)/shard_map/front/pallas_call | solution.py:301
  51.6 2.0 %collective-permute-start.33 = (bf16[24,1024]{1,0:T(8,128)(2,1)S(1)}, bf16[24,1024]{1,0:T(8,128)(2,1)S(1)}, u32[]{:S(2)}, u32[]{:S(2)}) collective-permute-start(bf16[24,1024]{1,0:T(8,128)(2,1)S(1)} %get-tuple-element.73), channel_id=1, source_target_pairs={{0,12},{4,8},{8,4},{12,0},{1,13},{5,9},{9,5},{13,1},{2,14},{6,10},... | collective-permute-start | bytes 147464 | tf_op jit(solution)/shard_map/ppermute | solution.py:66
  53.5 2.7 %collective-permute-start.29 = (bf16[24,1024]{1,0:T(8,128)(2,1)S(1)}, bf16[24,1024]{1,0:T(8,128)(2,1)S(1)}, u32[]{:S(2)}, u32[]{:S(2)}) collective-permute-start(bf16[24,1024]{1,0:T(8,128)(2,1)S(1)} %get-tuple-element.69), channel_id=1, source_target_pairs={{0,14},{1,15},{2,12},{3,13},{4,10},{5,11},{6,8},{7,9},{8,6},{9,7},... | collective-permute-start | bytes 147464 | tf_op jit(solution)/shard_map/ppermute | solution.py:379
  56.5 1.1 %collective-permute-start.32 = (bf16[24,1024]{1,0:T(8,128)(2,1)S(1)}, bf16[24,1024]{1,0:T(8,128)(2,1)S(1)}, u32[]{:S(2)}, u32[]{:S(2)}) collective-permute-start(bf16[24,1024]{1,0:T(8,128)(2,1)S(1)} %get-tuple-element.72), channel_id=1, source_target_pairs={{0,8},{4,12},{8,0},{12,4},{1,9},{5,13},{9,1},{13,5},{2,10},{6,14},... | collective-permute-start | bytes 147464 | tf_op jit(solution)/shard_map/ppermute | solution.py:66
  57.6 1.5 %collective-permute-start.34 = (bf16[24,1024]{1,0:T(8,128)(2,1)S(1)}, bf16[24,1024]{1,0:T(8,128)(2,1)S(1)}, u32[]{:S(2)}, u32[]{:S(2)}) collective-permute-start(bf16[24,1024]{1,0:T(8,128)(2,1)S(1)} %get-tuple-element.74), channel_id=1, source_target_pairs={{0,4},{4,0},{8,12},{12,8},{1,5},{5,1},{9,13},{13,9},{2,6},{6,2},{1... | collective-permute-start | bytes 147464 | tf_op jit(solution)/shard_map/ppermute | solution.py:66
  59.2 1.5 %collective-permute-done.29.extra_ref = bf16[24,1024]{1,0:T(8,128)(2,1)S(1)} collective-permute-done((bf16[24,1024]{1,0:T(8,128)(2,1)S(1)}, bf16[24,1024]{1,0:T(8,128)(2,1)S(1)}, u32[]{:S(2)}, u32[]{:S(2)}) %collective-permute-start.29) | collective-permute-done | bytes 49184 | tf_op jit(solution)/shard_map/ppermute | solution.py:379
  60.7 1.4 %collective-permute-done.32.refs_0_ = bf16[24,1024]{1,0:T(8,128)(2,1)S(1)} collective-permute-done((bf16[24,1024]{1,0:T(8,128)(2,1)S(1)}, bf16[24,1024]{1,0:T(8,128)(2,1)S(1)}, u32[]{:S(2)}, u32[]{:S(2)}) %collective-permute-start.32) | collective-permute-done | bytes 49184 | tf_op jit(solution)/shard_map/ppermute | solution.py:66
  (78 shorter events, 16.1 us)
Async XLA Ops:
  1.9 12.4 %collective-permute-start = (bf16[24,2176]{1,0:T(8,128)(2,1)S(1)}, bf16[24,2176]{1,0:T(8,128)(2,1)S(1)}, u32[]{:S(2)}, u32[]{:S(2)}) collective-permute-start(bf16[24,2176]{1,0:T(8,128)(2,1)S(1)} %get-tuple-element.43), channel_id=1, source_target_pairs={{0,8},{4,12},{8,0},{12,4},{1,9},{5,13},{9,1},{13,5},{2,10},{6,14},... | collective-permute-start | bytes 313352 | tf_op jit(solution)/shard_map/ppermute | solution.py:66
  6.0 8.4 %collective-permute-start.2 = (bf16[24,2176]{1,0:T(8,128)(2,1)S(1)}, bf16[24,2176]{1,0:T(8,128)(2,1)S(1)}, u32[]{:S(2)}, u32[]{:S(2)}) collective-permute-start(bf16[24,2176]{1,0:T(8,128)(2,1)S(1)} %get-tuple-element.45), channel_id=1, source_target_pairs={{0,12},{4,8},{8,4},{12,0},{1,13},{5,9},{9,5},{13,1},{2,14},{6,10},... | collective-permute-start | bytes 313352 | tf_op jit(solution)/shard_map/ppermute | solution.py:66
  7.4 7.6 %collective-permute-start.4 = (bf16[24,2176]{1,0:T(8,128)(2,1)S(1)}, bf16[24,2176]{1,0:T(8,128)(2,1)S(1)}, u32[]{:S(2)}, u32[]{:S(2)}) collective-permute-start(bf16[24,2176]{1,0:T(8,128)(2,1)S(1)} %get-tuple-element.46), channel_id=1, source_target_pairs={{0,4},{4,0},{8,12},{12,8},{1,5},{5,1},{9,13},{13,9},{2,6},{6,2},{1... | collective-permute-start | bytes 313352 | tf_op jit(solution)/shard_map/ppermute | solution.py:66
  19.1 6.1 %collective-permute-start.9 = (bf16[72,1024]{1,0:T(8,128)(2,1)S(1)}, bf16[72,1024]{1,0:T(8,128)(2,1)S(1)}, u32[]{:S(2)}, u32[]{:S(2)}) collective-permute-start(bf16[72,1024]{1,0:T(8,128)(2,1)S(1)} %get-tuple-element.55), channel_id=1, source_target_pairs={{0,2},{1,3},{2,0},{3,1},{4,6},{5,7},{6,4},{7,5},{8,10},{9,11},{10,... | collective-permute-start | bytes 442376 | tf_op jit(solution)/shard_map/ppermute | solution.py:66
  21.2 7.8 %collective-permute-start.11 = (bf16[24,1024]{1,0:T(8,128)(2,1)S(1)}, bf16[24,1024]{1,0:T(8,128)(2,1)S(1)}, u32[]{:S(2)}, u32[]{:S(2)}) collective-permute-start(bf16[24,1024]{1,0:T(8,128)(2,1)S(1)} %get-tuple-element.57), channel_id=1, source_target_pairs={{0,12},{4,8},{8,4},{12,0},{1,13},{5,9},{9,5},{13,1},{2,14},{6,10},... | collective-permute-start | bytes 147464 | tf_op jit(solution)/shard_map/ppermute | solution.py:66
  24.2 7.3 %collective-permute-start.7 = (bf16[24,1024]{1,0:T(8,128)(2,1)S(1)}, bf16[24,1024]{1,0:T(8,128)(2,1)S(1)}, u32[]{:S(2)}, u32[]{:S(2)}) collective-permute-start(bf16[24,1024]{1,0:T(8,128)(2,1)S(1)} %get-tuple-element.53), channel_id=1, source_target_pairs={{0,14},{1,15},{2,12},{3,13},{4,10},{5,11},{6,8},{7,9},{8,6},{9,7},... | collective-permute-start | bytes 147464 | tf_op jit(solution)/shard_map/ppermute | solution.py:379
  25.2 6.8 %collective-permute-start.10 = (bf16[24,1024]{1,0:T(8,128)(2,1)S(1)}, bf16[24,1024]{1,0:T(8,128)(2,1)S(1)}, u32[]{:S(2)}, u32[]{:S(2)}) collective-permute-start(bf16[24,1024]{1,0:T(8,128)(2,1)S(1)} %get-tuple-element.56), channel_id=1, source_target_pairs={{0,8},{4,12},{8,0},{12,4},{1,9},{5,13},{9,1},{13,5},{2,10},{6,14},... | collective-permute-start | bytes 147464 | tf_op jit(solution)/shard_map/ppermute | solution.py:66
  29.1 4.1 %collective-permute-start.12 = (bf16[24,1024]{1,0:T(8,128)(2,1)S(1)}, bf16[24,1024]{1,0:T(8,128)(2,1)S(1)}, u32[]{:S(2)}, u32[]{:S(2)}) collective-permute-start(bf16[24,1024]{1,0:T(8,128)(2,1)S(1)} %get-tuple-element.58), channel_id=1, source_target_pairs={{0,4},{4,0},{8,12},{12,8},{1,5},{5,1},{9,13},{13,9},{2,6},{6,2},{1... | collective-permute-start | bytes 147464 | tf_op jit(solution)/shard_map/ppermute | solution.py:66
  33.5 5.5 %collective-permute-start.13 = (bf16[24,1024]{1,0:T(8,128)(2,1)S(1)}, bf16[24,1024]{1,0:T(8,128)(2,1)S(1)}, u32[]{:S(2)}, u32[]{:S(2)}) collective-permute-start(bf16[24,1024]{1,0:T(8,128)(2,1)S(1)} %get-tuple-element.62), channel_id=1, source_target_pairs={{0,8},{4,12},{8,0},{12,4},{1,9},{5,13},{9,1},{13,5},{2,10},{6,14},... | collective-permute-start | bytes 147464 | tf_op jit(solution)/shard_map/ppermute | solution.py:66
  34.4 6.0 %collective-permute-start.17 = (bf16[24,1024]{1,0:T(8,128)(2,1)S(1)}, bf16[24,1024]{1,0:T(8,128)(2,1)S(1)}, u32[]{:S(2)}, u32[]{:S(2)}) collective-permute-start(bf16[24,1024]{1,0:T(8,128)(2,1)S(1)} %get-tuple-element.63), channel_id=1, source_target_pairs={{0,12},{4,8},{8,4},{12,0},{1,13},{5,9},{9,5},{13,1},{2,14},{6,10},... | collective-permute-start | bytes 147464 | tf_op jit(solution)/shard_map/ppermute | solution.py:66
  36.4 5.4 %collective-permute-start.21 = (bf16[24,1024]{1,0:T(8,128)(2,1)S(1)}, bf16[24,1024]{1,0:T(8,128)(2,1)S(1)}, u32[]{:S(2)}, u32[]{:S(2)}) collective-permute-start(bf16[24,1024]{1,0:T(8,128)(2,1)S(1)} %get-tuple-element.64), channel_id=1, source_target_pairs={{0,4},{4,0},{8,12},{12,8},{1,5},{5,1},{9,13},{13,9},{2,6},{6,2},{1... | collective-permute-start | bytes 147464 | tf_op jit(solution)/shard_map/ppermute | solution.py:66
  37.0 5.5 %collective-permute-start.26 = (bf16[24,1024]{1,0:T(8,128)(2,1)S(1)}, bf16[24,1024]{1,0:T(8,128)(2,1)S(1)}, u32[]{:S(2)}, u32[]{:S(2)}) collective-permute-start(bf16[24,1024]{1,0:T(8,128)(2,1)S(1)} %get-tuple-element.65.refs_6_), channel_id=1, source_target_pairs={{0,2},{1,3},{2,0},{3,1},{4,6},{5,7},{6,4},{7,5},{8,10},{9,11},{10,... | collective-permute-start | bytes 147464 | tf_op jit(solution)/shard_map/ppermute | solution.py:66
  38.5 4.0 %collective-permute-start.25 = (bf16[24,1024]{1,0:T(8,128)(2,1)S(1)}, bf16[24,1024]{1,0:T(8,128)(2,1)S(1)}, u32[]{:S(2)}, u32[]{:S(2)}) collective-permute-start(bf16[24,1024]{1,0:T(8,128)(2,1)S(1)} %get-tuple-element.65.refs_6_), channel_id=1, source_target_pairs={{0,1},{1,0},{2,3},{3,2},{4,5},{5,4},{6,7},{7,6},{8,9},{9,8},{10,11... | collective-permute-start | bytes 147464 | tf_op jit(solution)/shard_map/ppermute | solution.py:66
  39.0 4.3 %collective-permute-start.15 = (bf16[24,1024]{1,0:T(8,128)(2,1)S(1)}, bf16[24,1024]{1,0:T(8,128)(2,1)S(1)}, u32[]{:S(2)}, u32[]{:S(2)}) collective-permute-start(bf16[24,1024]{1,0:T(8,128)(2,1)S(1)} %collective-permute-done.13.refs_0_), channel_id=1, source_target_pairs={{0,2},{1,3},{2,0},{3,1},{4,6},{5,7},{6,4},{7,5},{8,10},{9,11},{10,... | collective-permute-start | bytes 147464 | tf_op jit(solution)/shard_map/ppermute | solution.py:66
  40.5 4.1 %collective-permute-start.19 = (bf16[24,1024]{1,0:T(8,128)(2,1)S(1)}, bf16[24,1024]{1,0:T(8,128)(2,1)S(1)}, u32[]{:S(2)}, u32[]{:S(2)}) collective-permute-start(bf16[24,1024]{1,0:T(8,128)(2,1)S(1)} %collective-permute-done.17.refs_2_), channel_id=1, source_target_pairs={{0,2},{1,3},{2,0},{3,1},{4,6},{5,7},{6,4},{7,5},{8,10},{9,11},{10,... | collective-permute-start | bytes 147464 | tf_op jit(solution)/shard_map/ppermute | solution.py:66
  41.8 4.1 %collective-permute-start.23 = (bf16[24,1024]{1,0:T(8,128)(2,1)S(1)}, bf16[24,1024]{1,0:T(8,128)(2,1)S(1)}, u32[]{:S(2)}, u32[]{:S(2)}) collective-permute-start(bf16[24,1024]{1,0:T(8,128)(2,1)S(1)} %collective-permute-done.21.refs_4_), channel_id=1, source_target_pairs={{0,2},{1,3},{2,0},{3,1},{4,6},{5,7},{6,4},{7,5},{8,10},{9,11},{10,... | collective-permute-start | bytes 147464 | tf_op jit(solution)/shard_map/ppermute | solution.py:66
  42.5 3.4 %collective-permute-start.14 = (bf16[24,1024]{1,0:T(8,128)(2,1)S(1)}, bf16[24,1024]{1,0:T(8,128)(2,1)S(1)}, u32[]{:S(2)}, u32[]{:S(2)}) collective-permute-start(bf16[24,1024]{1,0:T(8,128)(2,1)S(1)} %collective-permute-done.13.refs_0_), channel_id=1, source_target_pairs={{0,1},{1,0},{2,3},{3,2},{4,5},{5,4},{6,7},{7,6},{8,9},{9,8},{10,11... | collective-permute-start | bytes 147464 | tf_op jit(solution)/shard_map/ppermute | solution.py:66
  42.5 3.9 %collective-permute-start.18 = (bf16[24,1024]{1,0:T(8,128)(2,1)S(1)}, bf16[24,1024]{1,0:T(8,128)(2,1)S(1)}, u32[]{:S(2)}, u32[]{:S(2)}) collective-permute-start(bf16[24,1024]{1,0:T(8,128)(2,1)S(1)} %collective-permute-done.17.refs_2_), channel_id=1, source_target_pairs={{0,1},{1,0},{2,3},{3,2},{4,5},{5,4},{6,7},{7,6},{8,9},{9,8},{10,11... | collective-permute-start | bytes 147464 | tf_op jit(solution)/shard_map/ppermute | solution.py:66
  43.3 3.9 %collective-permute-start.22 = (bf16[24,1024]{1,0:T(8,128)(2,1)S(1)}, bf16[24,1024]{1,0:T(8,128)(2,1)S(1)}, u32[]{:S(2)}, u32[]{:S(2)}) collective-permute-start(bf16[24,1024]{1,0:T(8,128)(2,1)S(1)} %collective-permute-done.21.refs_4_), channel_id=1, source_target_pairs={{0,1},{1,0},{2,3},{3,2},{4,5},{5,4},{6,7},{7,6},{8,9},{9,8},{10,11... | collective-permute-start | bytes 147464 | tf_op jit(solution)/shard_map/ppermute | solution.py:66
  50.5 6.0 %collective-permute-start.31 = (bf16[72,1024]{1,0:T(8,128)(2,1)S(1)}, bf16[72,1024]{1,0:T(8,128)(2,1)S(1)}, u32[]{:S(2)}, u32[]{:S(2)}) collective-permute-start(bf16[72,1024]{1,0:T(8,128)(2,1)S(1)} %get-tuple-element.71), channel_id=1, source_target_pairs={{0,2},{1,3},{2,0},{3,1},{4,6},{5,7},{6,4},{7,5},{8,10},{9,11},{10,... | collective-permute-start | bytes 442376 | tf_op jit(solution)/shard_map/ppermute | solution.py:66
  51.6 7.6 %collective-permute-start.33 = (bf16[24,1024]{1,0:T(8,128)(2,1)S(1)}, bf16[24,1024]{1,0:T(8,128)(2,1)S(1)}, u32[]{:S(2)}, u32[]{:S(2)}) collective-permute-start(bf16[24,1024]{1,0:T(8,128)(2,1)S(1)} %get-tuple-element.73), channel_id=1, source_target_pairs={{0,12},{4,8},{8,4},{12,0},{1,13},{5,9},{9,5},{13,1},{2,14},{6,10},... | collective-permute-start | bytes 147464 | tf_op jit(solution)/shard_map/ppermute | solution.py:66
  53.5 7.1 %collective-permute-start.29 = (bf16[24,1024]{1,0:T(8,128)(2,1)S(1)}, bf16[24,1024]{1,0:T(8,128)(2,1)S(1)}, u32[]{:S(2)}, u32[]{:S(2)}) collective-permute-start(bf16[24,1024]{1,0:T(8,128)(2,1)S(1)} %get-tuple-element.69), channel_id=1, source_target_pairs={{0,14},{1,15},{2,12},{3,13},{4,10},{5,11},{6,8},{7,9},{8,6},{9,7},... | collective-permute-start | bytes 147464 | tf_op jit(solution)/shard_map/ppermute | solution.py:379
  56.5 5.6 %collective-permute-start.32 = (bf16[24,1024]{1,0:T(8,128)(2,1)S(1)}, bf16[24,1024]{1,0:T(8,128)(2,1)S(1)}, u32[]{:S(2)}, u32[]{:S(2)}) collective-permute-start(bf16[24,1024]{1,0:T(8,128)(2,1)S(1)} %get-tuple-element.72), channel_id=1, source_target_pairs={{0,8},{4,12},{8,0},{12,4},{1,9},{5,13},{9,1},{13,5},{2,10},{6,14},... | collective-permute-start | bytes 147464 | tf_op jit(solution)/shard_map/ppermute | solution.py:66
  57.6 4.5 %collective-permute-start.34 = (bf16[24,1024]{1,0:T(8,128)(2,1)S(1)}, bf16[24,1024]{1,0:T(8,128)(2,1)S(1)}, u32[]{:S(2)}, u32[]{:S(2)}) collective-permute-start(bf16[24,1024]{1,0:T(8,128)(2,1)S(1)} %get-tuple-element.74), channel_id=1, source_target_pairs={{0,4},{4,0},{8,12},{12,8},{1,5},{5,1},{9,13},{13,9},{2,6},{6,2},{1... | collective-permute-start | bytes 147464 | tf_op jit(solution)/shard_map/ppermute | solution.py:66
  (15 other events, 42.4 us)

commit v20 on v16

--- a/solution.py
+++ b/solution.py
@@ -451,7 +451,7 @@
     own, *sent = sum_back(hidden, w_down, own, back[0], pick, False)
 
     blocks = [spread(swap(b, "ep", k) if k else b, quarter) for k, b in enumerate(sent)]
-    hidden = front(blocks, flags, order + [0], 1, modulation, router, pair)
+    hidden = front(blocks, flags, [order[0], 1, *order[1:-1], 0], 1, modulation, router, pair)
     return tuple(sum_back(hidden, w_down, own, back[1], pick, True))
 
 

time: 63.1 us -> 63 us (level)
  waiting for transfers between devices: 14.4 us -> 13.4 us
  starting transfers between devices: 34.9 us -> 35.8 us
    ppermute x33, starting transfers between devices: 31.5 us -> 33.5 us  [swap(): return lax.ppermute(x, axis, [(i, i ^ bit) for i in range(size)])]
    ppermute x33, waiting for transfers between devices: 10.5 us -> 8.62 us  [swap(): return lax.ppermute(x, axis, [(i, i ^ bit) for i in range(size)])]
    ppermute x2, starting transfers between devices: 3.43 us -> 2.32 us  [diagonal(): return lax.ppermute(x, ('ep', 'et'), pairs)]
    ppermute x2, waiting for transfers between devices: 3.97 us -> 4.79 us  [diagonal(): return lax.ppermute(x, ('ep', 'et'), pairs)]
  transfers between devices with their start and end apart: 35 -> 35, of which waited for: 17 -> 18; matrix products, arithmetic and copies ran while one was open for 0% -> 0% of each run, Pallas kernels for 13% -> 13%
where the time goes in v20:
time: 63 us; the launch traced here: 62.8 us
  starting transfers between devices  35.8 us (57%)
  waiting for transfers between devices  13.4 us (21%)
  Pallas kernels  12.7 us (20%)
  between operations  0.87 us (1%)
    ppermute x33, starting transfers between devices, swap(): return lax.ppermute(x, axis, [(i, i ^ bit) for i in range(size)])  33.5 us
    ppermute x33, waiting for transfers between devices, swap(): return lax.ppermute(x, axis, [(i, i ^ bit) for i in range(size)])  8.62 us
    ppermute x2, waiting for transfers between devices, diagonal(): return lax.ppermute(x, ('ep', 'et'), pairs)  4.79 us
    pallas_call x1, Pallas kernels, load(): pl.pallas_call(load_kernel, in_specs=[ANY] * 3, out_specs=[VMEM] * 3, out...  3.78 us
    pallas_call x4, Pallas kernels, half_front(): pl.pallas_call(functools.partial(front_kernel, layout, order, flips, sect...  3.34 us
    ppermute x2, starting transfers between devices, diagonal(): return lax.ppermute(x, ('ep', 'et'), pairs)  2.32 us
    pallas_call x8, Pallas kernels, down(): pl.pallas_call(functools.partial(down_kernel, flip, len(adds), groups), i...  2.24 us
  transfers between devices with their start and end apart: 35, of which 18 were waited for; matrix products, arithmetic and copies ran while one was open for 0% of the time, Pallas kernels for 13%

profile of v20, /device:TPU:0, one launch (start us, length us, event | category | flops | bytes accessed | tf_op | source)
XLA Modules:
  0.0 62.8 jit_solution(12611006946367889238)
XLA Ops:
  0.6 1.2 %pack.1 = (bf16[24,2176]{1,0:T(8,128)(2,1)S(1)}, bf16[24,2176]{1,0:T(8,128)(2,1)S(1)}, bf16[24,2176]{1,0:T(8,128)(2,1)S(1)}, bf16[32,1024]{1,0:T(8,128)(2,1)S(1)}) custom-call(bf16[32,4096]{1,0:T(8,128)(2,1)} %tokens_ref.3, s32[2,2,32]{2,1,0:T(2,128)} %bitcast.6), custom_call_target="tpu_custom_call" | custom-call | tf_op jit(solution)/shard_map/pack/pallas_call | solution.py:197
  1.9 4.1 %collective-permute-start = (bf16[24,2176]{1,0:T(8,128)(2,1)S(1)}, bf16[24,2176]{1,0:T(8,128)(2,1)S(1)}, u32[]{:S(2)}, u32[]{:S(2)}) collective-permute-start(bf16[24,2176]{1,0:T(8,128)(2,1)S(1)} %get-tuple-element.43), channel_id=1, source_target_pairs={{0,8},{4,12},{8,0},{12,4},{1,9},{5,13},{9,1},{13,5},{2,10},{6,14},... | collective-permute-start | bytes 313352 | tf_op jit(solution)/shard_map/ppermute | solution.py:66
  6.0 1.3 %collective-permute-start.2 = (bf16[24,2176]{1,0:T(8,128)(2,1)S(1)}, bf16[24,2176]{1,0:T(8,128)(2,1)S(1)}, u32[]{:S(2)}, u32[]{:S(2)}) collective-permute-start(bf16[24,2176]{1,0:T(8,128)(2,1)S(1)} %get-tuple-element.45), channel_id=1, source_target_pairs={{0,12},{4,8},{8,4},{12,0},{1,13},{5,9},{9,5},{13,1},{2,14},{6,10},... | collective-permute-start | bytes 313352 | tf_op jit(solution)/shard_map/ppermute | solution.py:66
  7.6 3.8 %load.1 = (bf16[4096,768]{1,0:T(8,128)(2,1)S(1)}, bf16[384,4096]{1,0:T(8,128)(2,1)S(1)}, f32[8,128]{1,0:T(8,128)S(1)}) custom-call(bf16[1,4096,384]{2,1,0:T(8,128)(2,1)} %gate_ref.1, bf16[1,4096,384]{2,1,0:T(8,128)(2,1)} %up_ref.1, bf16[1,384,4096]{2,1,0:T(8,128)(2,1)} %down_ref.1), custom_call_target="tpu_custom_call" | custom-call | bytes 18874368 | tf_op jit(solution)/shard_map/load/pallas_call | solution.py:101
  12.2 2.0 %collective-permute-done.block_ref.refs_7_.refs_11_ = bf16[24,2176]{1,0:T(8,128)(2,1)S(1)} collective-permute-done((bf16[24,2176]{1,0:T(8,128)(2,1)S(1)}, bf16[24,2176]{1,0:T(8,128)(2,1)S(1)}, u32[]{:S(2)}, u32[]{:S(2)}) %collective-permute-start) | collective-permute-done | bytes 104480 | tf_op jit(solution)/shard_map/ppermute | solution.py:66
  16.3 0.9 %front.5.hidden_ref = bf16[96,384]{1,0:T(8,128)(2,1)S(1)} custom-call(bf16[24,2048]{1,0:T(8,128)(2,1)S(1)} %collective-permute-done.1.refs_0_, bf16[24,2048]{1,0:T(8,128)(2,1)S(1)} %collective-permute-done.3.refs_1_, bf16[24,2048]{1,0:T(8,128)(2,1)S(1)} %collective-permute-done.5.refs_2_, bf16[24,4096]{1,0:T(8,128)(2,1)S(1)} %get-tuple-element.47.refs_3_, ...), custom_call_target="tpu_custom_call" | custom-call | flops 301989888 | bytes 3145728 | tf_op jit(solution)/shard_map/front/pallas_call | solution.py:298
  19.0 1.9 %collective-permute-start.9 = (bf16[72,1024]{1,0:T(8,128)(2,1)S(1)}, bf16[72,1024]{1,0:T(8,128)(2,1)S(1)}, u32[]{:S(2)}, u32[]{:S(2)}) collective-permute-start(bf16[72,1024]{1,0:T(8,128)(2,1)S(1)} %get-tuple-element.55), channel_id=1, source_target_pairs={{0,2},{1,3},{2,0},{3,1},{4,6},{5,7},{6,4},{7,5},{8,10},{9,11},{10,... | collective-permute-start | bytes 442376 | tf_op jit(solution)/shard_map/ppermute | solution.py:66
  21.2 3.0 %collective-permute-start.11 = (bf16[24,1024]{1,0:T(8,128)(2,1)S(1)}, bf16[24,1024]{1,0:T(8,128)(2,1)S(1)}, u32[]{:S(2)}, u32[]{:S(2)}) collective-permute-start(bf16[24,1024]{1,0:T(8,128)(2,1)S(1)} %get-tuple-element.57), channel_id=1, source_target_pairs={{0,12},{4,8},{8,4},{12,0},{1,13},{5,9},{9,5},{13,1},{2,14},{6,10},... | collective-permute-start | bytes 147464 | tf_op jit(solution)/shard_map/ppermute | solution.py:66
  25.1 3.9 %collective-permute-start.10 = (bf16[24,1024]{1,0:T(8,128)(2,1)S(1)}, bf16[24,1024]{1,0:T(8,128)(2,1)S(1)}, u32[]{:S(2)}, u32[]{:S(2)}) collective-permute-start(bf16[24,1024]{1,0:T(8,128)(2,1)S(1)} %get-tuple-element.56), channel_id=1, source_target_pairs={{0,8},{4,12},{8,0},{12,4},{1,9},{5,13},{9,1},{13,5},{2,10},{6,14},... | collective-permute-start | bytes 147464 | tf_op jit(solution)/shard_map/ppermute | solution.py:66
  29.0 2.5 %collective-permute-done.7.extra_ref = bf16[24,1024]{1,0:T(8,128)(2,1)S(1)} collective-permute-done((bf16[24,1024]{1,0:T(8,128)(2,1)S(1)}, bf16[24,1024]{1,0:T(8,128)(2,1)S(1)}, u32[]{:S(2)}, u32[]{:S(2)}) %collective-permute-start.7) | collective-permute-done | bytes 49184 | tf_op jit(solution)/shard_map/ppermute | solution.py:376
  31.9 1.2 %collective-permute-done.12.refs_2_ = bf16[24,1024]{1,0:T(8,128)(2,1)S(1)} collective-permute-done((bf16[24,1024]{1,0:T(8,128)(2,1)S(1)}, bf16[24,1024]{1,0:T(8,128)(2,1)S(1)}, u32[]{:S(2)}, u32[]{:S(2)}) %collective-permute-start.12) | collective-permute-done | bytes 49184 | tf_op jit(solution)/shard_map/ppermute | solution.py:66
  33.4 1.0 %collective-permute-start.13 = (bf16[24,1024]{1,0:T(8,128)(2,1)S(1)}, bf16[24,1024]{1,0:T(8,128)(2,1)S(1)}, u32[]{:S(2)}, u32[]{:S(2)}) collective-permute-start(bf16[24,1024]{1,0:T(8,128)(2,1)S(1)} %get-tuple-element.62), channel_id=1, source_target_pairs={{0,8},{4,12},{8,0},{12,4},{1,9},{5,13},{9,1},{13,5},{2,10},{6,14},... | collective-permute-start | bytes 147464 | tf_op jit(solution)/shard_map/ppermute | solution.py:66
  34.9 3.0 %collective-permute-start.21 = (bf16[24,1024]{1,0:T(8,128)(2,1)S(1)}, bf16[24,1024]{1,0:T(8,128)(2,1)S(1)}, u32[]{:S(2)}, u32[]{:S(2)}) collective-permute-start(bf16[24,1024]{1,0:T(8,128)(2,1)S(1)} %get-tuple-element.64), channel_id=1, source_target_pairs={{0,12},{4,8},{8,4},{12,0},{1,13},{5,9},{9,5},{13,1},{2,14},{6,10},... | collective-permute-start | bytes 147464 | tf_op jit(solution)/shard_map/ppermute | solution.py:66
  37.9 1.4 %collective-permute-start.26 = (bf16[24,1024]{1,0:T(8,128)(2,1)S(1)}, bf16[24,1024]{1,0:T(8,128)(2,1)S(1)}, u32[]{:S(2)}, u32[]{:S(2)}) collective-permute-start(bf16[24,1024]{1,0:T(8,128)(2,1)S(1)} %get-tuple-element.65.refs_6_), channel_id=1, source_target_pairs={{0,2},{1,3},{2,0},{3,1},{4,6},{5,7},{6,4},{7,5},{8,10},{9,11},{10,... | collective-permute-start | bytes 147464 | tf_op jit(solution)/shard_map/ppermute | solution.py:66
  39.3 1.2 %collective-permute-start.15 = (bf16[24,1024]{1,0:T(8,128)(2,1)S(1)}, bf16[24,1024]{1,0:T(8,128)(2,1)S(1)}, u32[]{:S(2)}, u32[]{:S(2)}) collective-permute-start(bf16[24,1024]{1,0:T(8,128)(2,1)S(1)} %collective-permute-done.13.refs_0_), channel_id=1, source_target_pairs={{0,2},{1,3},{2,0},{3,1},{4,6},{5,7},{6,4},{7,5},{8,10},{9,11},{10,... | collective-permute-start | bytes 147464 | tf_op jit(solution)/shard_map/ppermute | solution.py:66
  40.5 0.8 %collective-permute-start.19 = (bf16[24,1024]{1,0:T(8,128)(2,1)S(1)}, bf16[24,1024]{1,0:T(8,128)(2,1)S(1)}, u32[]{:S(2)}, u32[]{:S(2)}) collective-permute-start(bf16[24,1024]{1,0:T(8,128)(2,1)S(1)} %collective-permute-done.17.refs_2_), channel_id=1, source_target_pairs={{0,2},{1,3},{2,0},{3,1},{4,6},{5,7},{6,4},{7,5},{8,10},{9,11},{10,... | collective-permute-start | bytes 147464 | tf_op jit(solution)/shard_map/ppermute | solution.py:66
  41.4 1.2 %collective-permute-start.23 = (bf16[24,1024]{1,0:T(8,128)(2,1)S(1)}, bf16[24,1024]{1,0:T(8,128)(2,1)S(1)}, u32[]{:S(2)}, u32[]{:S(2)}) collective-permute-start(bf16[24,1024]{1,0:T(8,128)(2,1)S(1)} %collective-permute-done.21.refs_4_), channel_id=1, source_target_pairs={{0,2},{1,3},{2,0},{3,1},{4,6},{5,7},{6,4},{7,5},{8,10},{9,11},{10,... | collective-permute-start | bytes 147464 | tf_op jit(solution)/shard_map/ppermute | solution.py:66
  43.9 1.2 %collective-permute-done.19.refs_3_ = bf16[24,1024]{1,0:T(8,128)(2,1)S(1)} collective-permute-done((bf16[24,1024]{1,0:T(8,128)(2,1)S(1)}, bf16[24,1024]{1,0:T(8,128)(2,1)S(1)}, u32[]{:S(2)}, u32[]{:S(2)}) %collective-permute-start.19) | collective-permute-done | bytes 49184 | tf_op jit(solution)/shard_map/ppermute | solution.py:66
  47.3 1.0 %front.7.hidden_ref = bf16[96,384]{1,0:T(8,128)(2,1)S(1)} custom-call(bf16[24,1024]{1,0:T(8,128)(2,1)S(1)} %collective-permute-done.14.refs_0_, bf16[24,1024]{1,0:T(8,128)(2,1)S(1)} %collective-permute-done.16.refs_1_, bf16[24,1024]{1,0:T(8,128)(2,1)S(1)} %collective-permute-done.18.refs_2_, bf16[24,1024]{1,0:T(8,128)(2,1)S(1)} %collective-permute-done.20.refs_3_, ...), custom_call_target="tpu_custom_call" | custom-call | flops 301989888 | bytes 3145728 | tf_op jit(solution)/shard_map/front/pallas_call | solution.py:298
  50.2 1.2 %collective-permute-start.31 = (bf16[72,1024]{1,0:T(8,128)(2,1)S(1)}, bf16[72,1024]{1,0:T(8,128)(2,1)S(1)}, u32[]{:S(2)}, u32[]{:S(2)}) collective-permute-start(bf16[72,1024]{1,0:T(8,128)(2,1)S(1)} %get-tuple-element.71), channel_id=1, source_target_pairs={{0,2},{1,3},{2,0},{3,1},{4,6},{5,7},{6,4},{7,5},{8,10},{9,11},{10,... | collective-permute-start | bytes 442376 | tf_op jit(solution)/shard_map/ppermute | solution.py:66
  51.7 2.6 %collective-permute-start.33 = (bf16[24,1024]{1,0:T(8,128)(2,1)S(1)}, bf16[24,1024]{1,0:T(8,128)(2,1)S(1)}, u32[]{:S(2)}, u32[]{:S(2)}) collective-permute-start(bf16[24,1024]{1,0:T(8,128)(2,1)S(1)} %get-tuple-element.73), channel_id=1, source_target_pairs={{0,12},{4,8},{8,4},{12,0},{1,13},{5,9},{9,5},{13,1},{2,14},{6,10},... | collective-permute-start | bytes 147464 | tf_op jit(solution)/shard_map/ppermute | solution.py:66
  54.3 1.6 %collective-permute-start.29 = (bf16[24,1024]{1,0:T(8,128)(2,1)S(1)}, bf16[24,1024]{1,0:T(8,128)(2,1)S(1)}, u32[]{:S(2)}, u32[]{:S(2)}) collective-permute-start(bf16[24,1024]{1,0:T(8,128)(2,1)S(1)} %get-tuple-element.69), channel_id=1, source_target_pairs={{0,14},{1,15},{2,12},{3,13},{4,10},{5,11},{6,8},{7,9},{8,6},{9,7},... | collective-permute-start | bytes 147464 | tf_op jit(solution)/shard_map/ppermute | solution.py:376
  57.1 2.1 %collective-permute-start.34 = (bf16[24,1024]{1,0:T(8,128)(2,1)S(1)}, bf16[24,1024]{1,0:T(8,128)(2,1)S(1)}, u32[]{:S(2)}, u32[]{:S(2)}) collective-permute-start(bf16[24,1024]{1,0:T(8,128)(2,1)S(1)} %get-tuple-element.74), channel_id=1, source_target_pairs={{0,4},{4,0},{8,12},{12,8},{1,5},{5,1},{9,13},{13,9},{2,6},{6,2},{1... | collective-permute-start | bytes 147464 | tf_op jit(solution)/shard_map/ppermute | solution.py:66
  59.1 2.3 %collective-permute-done.29.extra_ref = bf16[24,1024]{1,0:T(8,128)(2,1)S(1)} collective-permute-done((bf16[24,1024]{1,0:T(8,128)(2,1)S(1)}, bf16[24,1024]{1,0:T(8,128)(2,1)S(1)}, u32[]{:S(2)}, u32[]{:S(2)}) %collective-permute-start.29) | collective-permute-done | bytes 49184 | tf_op jit(solution)/shard_map/ppermute | solution.py:376
  (78 shorter events, 15.5 us)
Async XLA Ops:
  1.9 12.4 %collective-permute-start = (bf16[24,2176]{1,0:T(8,128)(2,1)S(1)}, bf16[24,2176]{1,0:T(8,128)(2,1)S(1)}, u32[]{:S(2)}, u32[]{:S(2)}) collective-permute-start(bf16[24,2176]{1,0:T(8,128)(2,1)S(1)} %get-tuple-element.43), channel_id=1, source_target_pairs={{0,8},{4,12},{8,0},{12,4},{1,9},{5,13},{9,1},{13,5},{2,10},{6,14},... | collective-permute-start | bytes 313352 | tf_op jit(solution)/shard_map/ppermute | solution.py:66
  6.0 8.4 %collective-permute-start.2 = (bf16[24,2176]{1,0:T(8,128)(2,1)S(1)}, bf16[24,2176]{1,0:T(8,128)(2,1)S(1)}, u32[]{:S(2)}, u32[]{:S(2)}) collective-permute-start(bf16[24,2176]{1,0:T(8,128)(2,1)S(1)} %get-tuple-element.45), channel_id=1, source_target_pairs={{0,12},{4,8},{8,4},{12,0},{1,13},{5,9},{9,5},{13,1},{2,14},{6,10},... | collective-permute-start | bytes 313352 | tf_op jit(solution)/shard_map/ppermute | solution.py:66
  7.3 7.6 %collective-permute-start.4 = (bf16[24,2176]{1,0:T(8,128)(2,1)S(1)}, bf16[24,2176]{1,0:T(8,128)(2,1)S(1)}, u32[]{:S(2)}, u32[]{:S(2)}) collective-permute-start(bf16[24,2176]{1,0:T(8,128)(2,1)S(1)} %get-tuple-element.46), channel_id=1, source_target_pairs={{0,4},{4,0},{8,12},{12,8},{1,5},{5,1},{9,13},{13,9},{2,6},{6,2},{1... | collective-permute-start | bytes 313352 | tf_op jit(solution)/shard_map/ppermute | solution.py:66
  19.0 6.1 %collective-permute-start.9 = (bf16[72,1024]{1,0:T(8,128)(2,1)S(1)}, bf16[72,1024]{1,0:T(8,128)(2,1)S(1)}, u32[]{:S(2)}, u32[]{:S(2)}) collective-permute-start(bf16[72,1024]{1,0:T(8,128)(2,1)S(1)} %get-tuple-element.55), channel_id=1, source_target_pairs={{0,2},{1,3},{2,0},{3,1},{4,6},{5,7},{6,4},{7,5},{8,10},{9,11},{10,... | collective-permute-start | bytes 442376 | tf_op jit(solution)/shard_map/ppermute | solution.py:66
  21.2 7.8 %collective-permute-start.11 = (bf16[24,1024]{1,0:T(8,128)(2,1)S(1)}, bf16[24,1024]{1,0:T(8,128)(2,1)S(1)}, u32[]{:S(2)}, u32[]{:S(2)}) collective-permute-start(bf16[24,1024]{1,0:T(8,128)(2,1)S(1)} %get-tuple-element.57), channel_id=1, source_target_pairs={{0,12},{4,8},{8,4},{12,0},{1,13},{5,9},{9,5},{13,1},{2,14},{6,10},... | collective-permute-start | bytes 147464 | tf_op jit(solution)/shard_map/ppermute | solution.py:66
  24.2 7.3 %collective-permute-start.7 = (bf16[24,1024]{1,0:T(8,128)(2,1)S(1)}, bf16[24,1024]{1,0:T(8,128)(2,1)S(1)}, u32[]{:S(2)}, u32[]{:S(2)}) collective-permute-start(bf16[24,1024]{1,0:T(8,128)(2,1)S(1)} %get-tuple-element.53), channel_id=1, source_target_pairs={{0,14},{1,15},{2,12},{3,13},{4,10},{5,11},{6,8},{7,9},{8,6},{9,7},... | collective-permute-start | bytes 147464 | tf_op jit(solution)/shard_map/ppermute | solution.py:376
  25.1 6.8 %collective-permute-start.10 = (bf16[24,1024]{1,0:T(8,128)(2,1)S(1)}, bf16[24,1024]{1,0:T(8,128)(2,1)S(1)}, u32[]{:S(2)}, u32[]{:S(2)}) collective-permute-start(bf16[24,1024]{1,0:T(8,128)(2,1)S(1)} %get-tuple-element.56), channel_id=1, source_target_pairs={{0,8},{4,12},{8,0},{12,4},{1,9},{5,13},{9,1},{13,5},{2,10},{6,14},... | collective-permute-start | bytes 147464 | tf_op jit(solution)/shard_map/ppermute | solution.py:66
  29.0 4.1 %collective-permute-start.12 = (bf16[24,1024]{1,0:T(8,128)(2,1)S(1)}, bf16[24,1024]{1,0:T(8,128)(2,1)S(1)}, u32[]{:S(2)}, u32[]{:S(2)}) collective-permute-start(bf16[24,1024]{1,0:T(8,128)(2,1)S(1)} %get-tuple-element.58), channel_id=1, source_target_pairs={{0,4},{4,0},{8,12},{12,8},{1,5},{5,1},{9,13},{13,9},{2,6},{6,2},{1... | collective-permute-start | bytes 147464 | tf_op jit(solution)/shard_map/ppermute | solution.py:66
  33.4 5.9 %collective-permute-start.13 = (bf16[24,1024]{1,0:T(8,128)(2,1)S(1)}, bf16[24,1024]{1,0:T(8,128)(2,1)S(1)}, u32[]{:S(2)}, u32[]{:S(2)}) collective-permute-start(bf16[24,1024]{1,0:T(8,128)(2,1)S(1)} %get-tuple-element.62), channel_id=1, source_target_pairs={{0,8},{4,12},{8,0},{12,4},{1,9},{5,13},{9,1},{13,5},{2,10},{6,14},... | collective-permute-start | bytes 147464 | tf_op jit(solution)/shard_map/ppermute | solution.py:66
  34.4 6.1 %collective-permute-start.17 = (bf16[24,1024]{1,0:T(8,128)(2,1)S(1)}, bf16[24,1024]{1,0:T(8,128)(2,1)S(1)}, u32[]{:S(2)}, u32[]{:S(2)}) collective-permute-start(bf16[24,1024]{1,0:T(8,128)(2,1)S(1)} %get-tuple-element.63), channel_id=1, source_target_pairs={{0,4},{4,0},{8,12},{12,8},{1,5},{5,1},{9,13},{13,9},{2,6},{6,2},{1... | collective-permute-start | bytes 147464 | tf_op jit(solution)/shard_map/ppermute | solution.py:66
  34.9 6.5 %collective-permute-start.21 = (bf16[24,1024]{1,0:T(8,128)(2,1)S(1)}, bf16[24,1024]{1,0:T(8,128)(2,1)S(1)}, u32[]{:S(2)}, u32[]{:S(2)}) collective-permute-start(bf16[24,1024]{1,0:T(8,128)(2,1)S(1)} %get-tuple-element.64), channel_id=1, source_target_pairs={{0,12},{4,8},{8,4},{12,0},{1,13},{5,9},{9,5},{13,1},{2,14},{6,10},... | collective-permute-start | bytes 147464 | tf_op jit(solution)/shard_map/ppermute | solution.py:66
  37.9 4.7 %collective-permute-start.26 = (bf16[24,1024]{1,0:T(8,128)(2,1)S(1)}, bf16[24,1024]{1,0:T(8,128)(2,1)S(1)}, u32[]{:S(2)}, u32[]{:S(2)}) collective-permute-start(bf16[24,1024]{1,0:T(8,128)(2,1)S(1)} %get-tuple-element.65.refs_6_), channel_id=1, source_target_pairs={{0,2},{1,3},{2,0},{3,1},{4,6},{5,7},{6,4},{7,5},{8,10},{9,11},{10,... | collective-permute-start | bytes 147464 | tf_op jit(solution)/shard_map/ppermute | solution.py:66
  39.3 3.2 %collective-permute-start.25 = (bf16[24,1024]{1,0:T(8,128)(2,1)S(1)}, bf16[24,1024]{1,0:T(8,128)(2,1)S(1)}, u32[]{:S(2)}, u32[]{:S(2)}) collective-permute-start(bf16[24,1024]{1,0:T(8,128)(2,1)S(1)} %get-tuple-element.65.refs_6_), channel_id=1, source_target_pairs={{0,1},{1,0},{2,3},{3,2},{4,5},{5,4},{6,7},{7,6},{8,9},{9,8},{10,11... | collective-permute-start | bytes 147464 | tf_op jit(solution)/shard_map/ppermute | solution.py:66
  39.3 4.5 %collective-permute-start.15 = (bf16[24,1024]{1,0:T(8,128)(2,1)S(1)}, bf16[24,1024]{1,0:T(8,128)(2,1)S(1)}, u32[]{:S(2)}, u32[]{:S(2)}) collective-permute-start(bf16[24,1024]{1,0:T(8,128)(2,1)S(1)} %collective-permute-done.13.refs_0_), channel_id=1, source_target_pairs={{0,2},{1,3},{2,0},{3,1},{4,6},{5,7},{6,4},{7,5},{8,10},{9,11},{10,... | collective-permute-start | bytes 147464 | tf_op jit(solution)/shard_map/ppermute | solution.py:66
  40.5 4.5 %collective-permute-start.19 = (bf16[24,1024]{1,0:T(8,128)(2,1)S(1)}, bf16[24,1024]{1,0:T(8,128)(2,1)S(1)}, u32[]{:S(2)}, u32[]{:S(2)}) collective-permute-start(bf16[24,1024]{1,0:T(8,128)(2,1)S(1)} %collective-permute-done.17.refs_2_), channel_id=1, source_target_pairs={{0,2},{1,3},{2,0},{3,1},{4,6},{5,7},{6,4},{7,5},{8,10},{9,11},{10,... | collective-permute-start | bytes 147464 | tf_op jit(solution)/shard_map/ppermute | solution.py:66
  41.4 4.2 %collective-permute-start.23 = (bf16[24,1024]{1,0:T(8,128)(2,1)S(1)}, bf16[24,1024]{1,0:T(8,128)(2,1)S(1)}, u32[]{:S(2)}, u32[]{:S(2)}) collective-permute-start(bf16[24,1024]{1,0:T(8,128)(2,1)S(1)} %collective-permute-done.21.refs_4_), channel_id=1, source_target_pairs={{0,2},{1,3},{2,0},{3,1},{4,6},{5,7},{6,4},{7,5},{8,10},{9,11},{10,... | collective-permute-start | bytes 147464 | tf_op jit(solution)/shard_map/ppermute | solution.py:66
  42.6 3.0 %collective-permute-start.14 = (bf16[24,1024]{1,0:T(8,128)(2,1)S(1)}, bf16[24,1024]{1,0:T(8,128)(2,1)S(1)}, u32[]{:S(2)}, u32[]{:S(2)}) collective-permute-start(bf16[24,1024]{1,0:T(8,128)(2,1)S(1)} %collective-permute-done.13.refs_0_), channel_id=1, source_target_pairs={{0,1},{1,0},{2,3},{3,2},{4,5},{5,4},{6,7},{7,6},{8,9},{9,8},{10,11... | collective-permute-start | bytes 147464 | tf_op jit(solution)/shard_map/ppermute | solution.py:66
  42.6 3.5 %collective-permute-start.18 = (bf16[24,1024]{1,0:T(8,128)(2,1)S(1)}, bf16[24,1024]{1,0:T(8,128)(2,1)S(1)}, u32[]{:S(2)}, u32[]{:S(2)}) collective-permute-start(bf16[24,1024]{1,0:T(8,128)(2,1)S(1)} %collective-permute-done.17.refs_2_), channel_id=1, source_target_pairs={{0,1},{1,0},{2,3},{3,2},{4,5},{5,4},{6,7},{7,6},{8,9},{9,8},{10,11... | collective-permute-start | bytes 147464 | tf_op jit(solution)/shard_map/ppermute | solution.py:66
  43.9 3.0 %collective-permute-start.22 = (bf16[24,1024]{1,0:T(8,128)(2,1)S(1)}, bf16[24,1024]{1,0:T(8,128)(2,1)S(1)}, u32[]{:S(2)}, u32[]{:S(2)}) collective-permute-start(bf16[24,1024]{1,0:T(8,128)(2,1)S(1)} %collective-permute-done.21.refs_4_), channel_id=1, source_target_pairs={{0,1},{1,0},{2,3},{3,2},{4,5},{5,4},{6,7},{7,6},{8,9},{9,8},{10,11... | collective-permute-start | bytes 147464 | tf_op jit(solution)/shard_map/ppermute | solution.py:66
  50.2 6.0 %collective-permute-start.31 = (bf16[72,1024]{1,0:T(8,128)(2,1)S(1)}, bf16[72,1024]{1,0:T(8,128)(2,1)S(1)}, u32[]{:S(2)}, u32[]{:S(2)}) collective-permute-start(bf16[72,1024]{1,0:T(8,128)(2,1)S(1)} %get-tuple-element.71), channel_id=1, source_target_pairs={{0,2},{1,3},{2,0},{3,1},{4,6},{5,7},{6,4},{7,5},{8,10},{9,11},{10,... | collective-permute-start | bytes 442376 | tf_op jit(solution)/shard_map/ppermute | solution.py:66
  51.7 7.4 %collective-permute-start.33 = (bf16[24,1024]{1,0:T(8,128)(2,1)S(1)}, bf16[24,1024]{1,0:T(8,128)(2,1)S(1)}, u32[]{:S(2)}, u32[]{:S(2)}) collective-permute-start(bf16[24,1024]{1,0:T(8,128)(2,1)S(1)} %get-tuple-element.73), channel_id=1, source_target_pairs={{0,12},{4,8},{8,4},{12,0},{1,13},{5,9},{9,5},{13,1},{2,14},{6,10},... | collective-permute-start | bytes 147464 | tf_op jit(solution)/shard_map/ppermute | solution.py:66
  54.3 7.1 %collective-permute-start.29 = (bf16[24,1024]{1,0:T(8,128)(2,1)S(1)}, bf16[24,1024]{1,0:T(8,128)(2,1)S(1)}, u32[]{:S(2)}, u32[]{:S(2)}) collective-permute-start(bf16[24,1024]{1,0:T(8,128)(2,1)S(1)} %get-tuple-element.69), channel_id=1, source_target_pairs={{0,14},{1,15},{2,12},{3,13},{4,10},{5,11},{6,8},{7,9},{8,6},{9,7},... | collective-permute-start | bytes 147464 | tf_op jit(solution)/shard_map/ppermute | solution.py:376
  56.2 5.6 %collective-permute-start.32 = (bf16[24,1024]{1,0:T(8,128)(2,1)S(1)}, bf16[24,1024]{1,0:T(8,128)(2,1)S(1)}, u32[]{:S(2)}, u32[]{:S(2)}) collective-permute-start(bf16[24,1024]{1,0:T(8,128)(2,1)S(1)} %get-tuple-element.72), channel_id=1, source_target_pairs={{0,8},{4,12},{8,0},{12,4},{1,9},{5,13},{9,1},{13,5},{2,10},{6,14},... | collective-permute-start | bytes 147464 | tf_op jit(solution)/shard_map/ppermute | solution.py:66
  57.1 4.9 %collective-permute-start.34 = (bf16[24,1024]{1,0:T(8,128)(2,1)S(1)}, bf16[24,1024]{1,0:T(8,128)(2,1)S(1)}, u32[]{:S(2)}, u32[]{:S(2)}) collective-permute-start(bf16[24,1024]{1,0:T(8,128)(2,1)S(1)} %get-tuple-element.74), channel_id=1, source_target_pairs={{0,4},{4,0},{8,12},{12,8},{1,5},{5,1},{9,13},{13,9},{2,6},{6,2},{1... | collective-permute-start | bytes 147464 | tf_op jit(solution)/shard_map/ppermute | solution.py:66
  (15 other events, 42.0 us)
